TPU v7x, 32 devices: a whole 2x2x4 slice. The times are simulated.
32 devices in a mesh: tm: 8 (over y, x, core), sky: 4 (over z).
Axes of the slice: x: 2, y: 2, z: 4, core: 2. Of those that a mesh axis runs over, the one named last changes fastest.
Arguments:
- residuals: bfloat16 [32, 512, 1024], P('tm', None, 'sky')
- seg_counts: int32 [32], P('tm'), may hold values from 256 to 512, as said below
- attitude: bfloat16 [32, 512, 512], P('tm', 'sky')
- sched_seg: int32 [256, 256], P(('tm', 'sky')), may hold values from 0 to 31, as said below
- sched_slot: int32 [256, 256], P(('tm', 'sky')), may hold values from 0 to 511, as said below
- periods: int32 [1024], replicated, may hold values from 16 to 16383
Outputs:
- cleaned: float32 [32, 512, 1024], P('tm', None, 'sky')
- log_evidence: float32 [256, 128], P(('tm', 'sky'))
Inputs may be any that keep to these rules, and one draw needn't show every extreme that they name: `seg_counts`: every segment has between 256 and 512 observed slots; some segment has all 512. `sched_seg`: in each aligned block of 8 rows (the plans of one device) at most 512 entries fall in the segments of one index of tm, and in every block some index receives exactly 512. `sched_slot`: each slot is below the observed count of its segment.
All inputs are finite; a program needn't handle non-finite values.
Results may differ from a plain program's by a relative error of at most 0.035.
Values may be sent and summed in bfloat16 or wider, within the bound.
No kernel may reach another device: no remote copies, remote signals or barrier semaphores. Data moves between devices by JAX's collectives and lax.ppermute only.
A program may use at most 128 MiB of HBM per device.

v0:
```python
import jax
import jax.numpy as jnp
from jax import lax
from jax.sharding import PartitionSpec as P

SRC_GROUP = 128
ITERS = 2


TWO_PI = 6.283185307179586
BETA = 2.0
RIDGE = 1.0


def make_basis(times, periods):
    period_float = periods.astype(jnp.float32)
    phase = (times[..., None] % periods).astype(jnp.float32) * (TWO_PI / period_float)
    return jnp.concatenate([jnp.cos(phase), jnp.sin(phase)], axis=-1).astype(jnp.bfloat16)


def fit_groups(basis, observed, norm_cos, norm_sin, nper):
    corr = jnp.einsum("fio,fic->foc", basis, observed, preferred_element_type=jnp.float32)
    cosine = corr[:, :nper]
    sine = corr[:, nper:]
    amp_c = cosine / norm_cos[:, :, None]
    amp_s = sine / norm_sin[:, :, None]
    power = cosine * amp_c + sine * amp_s
    logits = BETA * power
    highest = jnp.max(logits, axis=1)
    expo = jnp.exp(logits - highest[:, None, :])
    total = jnp.sum(expo, axis=1)
    share = expo / total[:, None, :]
    coeff = jnp.concatenate([share * amp_c, share * amp_s], axis=1).astype(jnp.bfloat16)
    model = jnp.einsum("fio,foc->fic", basis, coeff, preferred_element_type=jnp.float32)
    return (model, highest + jnp.log(total))


def on_device(residuals, seg_counts, attitude, sched_seg, sched_slot, periods):
    tm_count = lax.axis_size("tm")
    sched_dev, obs = sched_seg.shape
    seg_dev, slots, width = residuals.shape
    nper = periods.shape[0]
    column_blocks = width // SRC_GROUP
    capacity = 2 * sched_dev * obs // tm_count
    requests = sched_dev * obs
    seg_flat = sched_seg.reshape(-1)
    slot_flat = sched_slot.reshape(-1)
    block_of = jnp.repeat(jnp.arange(sched_dev, dtype=jnp.int32) % column_blocks, obs)
    target = seg_flat // seg_dev
    local_row = (seg_flat % seg_dev * slots + slot_flat) * column_blocks + block_of
    onehot = (target[:, None] == jnp.arange(tm_count, dtype=jnp.int32)[None, :]).astype(jnp.int32)
    position = jnp.sum(jnp.cumsum(onehot, axis=0) * onehot, axis=1) - 1
    empty_row = seg_dev * slots * column_blocks
    wanted = (
        jnp.full((tm_count, capacity), empty_row, jnp.int32).at[target, position].set(local_row)
    )
    asked = lax.all_to_all(wanted, "tm", split_axis=0, concat_axis=0, tiled=True)
    basis = make_basis(sched_seg * slots + sched_slot, periods)
    squares = basis.astype(jnp.float32) ** 2
    norm_cos = jnp.sum(squares[:, :, :nper], axis=1) + RIDGE
    norm_sin = jnp.sum(squares[:, :, nper:], axis=1) + RIDGE
    valid = jnp.arange(slots, dtype=jnp.int32)[None, :] < seg_counts[:, None]
    current = residuals.astype(jnp.float32)
    evidence = jnp.zeros((sched_dev, SRC_GROUP), jnp.float32)
    for iteration in range(ITERS):
        masked = jnp.where(valid[:, :, None], current, 0.0).astype(jnp.bfloat16)
        white = jnp.einsum(
            "sij,sjc->sic",
            lax.all_gather(attitude, "sky", axis=1, tiled=True),
            masked,
            preferred_element_type=jnp.float32,
        ).astype(jnp.bfloat16)
        flat = white.reshape(-1, SRC_GROUP)
        picked = jnp.take(flat, asked, axis=0, mode="fill", fill_value=0)
        arrived = lax.all_to_all(picked, "tm", split_axis=0, concat_axis=0, tiled=True)
        observed = arrived[target, position].reshape(sched_dev, obs, SRC_GROUP)
        model, evidence = fit_groups(basis, observed, norm_cos, norm_sin, nper)
        outgoing = (
            jnp.zeros((tm_count, capacity, SRC_GROUP), jnp.float32)
            .at[target, position]
            .set(model.reshape(requests, SRC_GROUP))
        )
        returned = lax.all_to_all(outgoing, "tm", split_axis=0, concat_axis=0, tiled=True)
        placed = (
            jnp.zeros((empty_row, SRC_GROUP), jnp.float32)
            .at[asked.reshape(-1)]
            .add(returned.reshape(-1, SRC_GROUP), mode="drop")
        )
        current = current - placed.reshape(seg_dev, slots, width)
    return (current, evidence)


def solution(mesh):
    in_specs = (
        P("tm", None, "sky"),
        P("tm"),
        P("tm", "sky", None),
        P(("tm", "sky"), None),
        P(("tm", "sky"), None),
        P(),
    )
    out_specs = (P("tm", None, "sky"), P(("tm", "sky"), None))
    return jax.shard_map(
        on_device, mesh=mesh, in_specs=in_specs, out_specs=out_specs, check_vma=False
    )
```

profile of v0, /device:TPU:1, one launch (start us, length us, event | category | flops | bytes accessed | tf_op | source)
XLA Modules:
  0.0 447.7 jit_solution(15605732289935617949)
XLA Ops:
  7.2 0.7 all-gather.2.cloned.1.call-update
  7.9 0.7 reshape.255
  8.6 0.7 copy.29
  9.3 2.3 reduce-window.6
  12.3 0.7 copy.32
  13.0 0.7 copy.30
  13.8 0.7 multiply_reduce_fusion
  14.6 0.8 and_reduce_fusion
  15.4 8.6 %scatter_custom_fusion.2 = s32[4096]{0:T(1024)} fusion(s32[2048]{0:T(1024)S(1)} %broadcast_select_fusion.2, s32[2048]{0:T(1024)S(1)} %get-tuple-element.16, s32[]{:T(128)} %constant.75.clone.1), kind=kCustom, calls=%fused_computation.113 | custom fusion | bytes 16388
  24.0 5.2 %all-to-all-start = ((s32[8,1,512]{2,1,0:T(1,128)}), s32[8,1,512]{2,1,0:T(1,128)S(1)}, u32[]{:S(2)}, u32[]{:S(2)}) async-start(s32[8,1,512]{2,1,0:T(1,128)} %bitcast.3), calls=%async_computation | async-start | bytes 32768 | tf_op jit(solution)/shard_map/all_to_all | solution.py:57
  29.2 0.7 broadcast_compare_fusion
  29.9 0.7 convert_divide_fusion
  30.6 0.7 compare_select_fusion.7
  31.3 0.7 multiply_add_fusion
  32.0 112.5 %fusion.6 = (bf16[8,256,1024]{1,2,0:T(8,128)(2,1)}, bf16[8,256,1024]{1,2,0:T(8,128)(2,1)}) fusion(f32[1024]{0:T(1024)S(1)} %convert_divide_fusion, s32[1024]{0:T(1024)S(1)} %compare_select_fusion.7, s32[8,256]{1,0:T(8,128)S(1)} %multiply_add_fusion, pred[1024]{0:T(1024)(128)(4,1)S(1)} %broadcast_compare_fusion), kind=kLoop, calls=%fused_computation.20 | loop fusion | flops 23068672 | bytes 8406016 | tf_op jit(solution)/shard_map/convert.4
  144.6 2.7 fusion.23
  148.3 12.1 %gather_fusion.2 = bf16[4096,128]{1,0:T(8,128)(2,1)S(1)} fusion(bf16[4096,128]{1,0:T(8,128)(2,1)S(1)} %reshape.260, s32[4096]{0:T(1024)S(1)} %broadcast_clamp_fusion), kind=kCustom, calls=%fused_computation.clone | custom fusion | bytes 2113536 | tf_op jit(solution)/shard_map/jit(_take)/gather | solution.py:74
  160.5 1.5 broadcast_select_fusion.1
  162.0 4.5 %all-to-all-start.1 = ((bf16[8,512,128]{2,1,0:T(8,128)(2,1)}), bf16[8,512,128]{2,1,0:T(8,128)(2,1)S(1)}, u32[]{:S(2)}, u32[]{:S(2)}) async-start(bf16[8,512,128]{2,1,0:T(8,128)(2,1)} %broadcast_select_fusion.1), calls=%async_computation.1 | async-start | bytes 2097152 | tf_op jit(solution)/shard_map/all_to_all | solution.py:75
  166.5 10.8 %convert_multiply_fusion = f32[8,256,2048]{1,2,0:T(8,128)} fusion(bf16[8,256,1024]{1,2,0:T(8,128)(2,1)} %get-tuple-element.15, bf16[8,256,1024]{1,2,0:T(8,128)(2,1)} %get-tuple-element.14), kind=kLoop, calls=%fused_computation.15 | loop fusion | flops 20971520 | bytes 25165824 | tf_op jit(solution)/shard_map/integer_pow | solution.py:59
  177.2 7.0 %slice_reduce_fusion.1 = (f32[8,1024]{1,0:T(8,128)S(1)}, f32[8,1024]{1,0:T(8,128)S(1)}) fusion(f32[8,256,2048]{1,2,0:T(8,128)} %convert_multiply_fusion), kind=kLoop, calls=%fused_computation.23 | loop fusion | flops 4177920 | bytes 16842752 | tf_op jit(solution)/shard_map/reduce_sum | solution.py:60
  184.3 11.1 %gather_fusion = bf16[2048,128]{1,0:T(8,128)(2,1)S(1)} fusion(bf16[8,512,128]{2,1,0:T(8,128)(2,1)S(1)} %all-to-all-done.1, s32[2048]{0:T(1024)S(1)} %bitcast.59), kind=kCustom, calls=%fused_computation.2 | custom fusion | bytes 1064960 | tf_op jit(solution)/shard_map/gather | solution.py:76
  195.4 9.0 %fusion.58 = f32[8,2048,128]{2,1,0:T(8,128)} fusion(bf16[8,256,128]{2,1,0:T(8,128)(2,1)S(1)} %bitcast.66, bf16[8,256,1024]{1,2,0:T(8,128)(2,1)} %get-tuple-element.15, bf16[8,256,1024]{1,2,0:T(8,128)(2,1)} %get-tuple-element.14), kind=kOutput, calls=%fused_computation.136 | convolution fusion | flops 1090519040 | bytes 17301504 | tf_op jit(solution)/shard_map/fio,fic->foc/dot_general | solution.py:22
  204.5 10.1 %multiply_convert_fusion.3 = (bf16[8,1024,128]{2,1,0:T(8,128)(2,1)}, bf16[8,1024,128]{2,1,0:T(8,128)(2,1)}) fusion(f32[8,1024]{1,0:T(8,128)S(1)} %get-tuple-element.21, f32[8,2048,128]{2,1,0:T(8,128)} %fusion.58, f32[8,1024]{1,0:T(8,128)S(1)} %get-tuple-element.20), kind=kOutput, calls=%fused_computation.40 | output fusion | flops 14684158 | bytes 21102592 | tf_op jit(solution)/shard_map/div | solution.py:32
  214.5 6.2 %fusion.10 = f32[8,256,128]{2,1,0:T(8,128)S(1)} fusion(bf16[8,1024,128]{2,1,0:T(8,128)(2,1)} %get-tuple-element.13, bf16[8,1024,128]{2,1,0:T(8,128)(2,1)} %get-tuple-element.12, bf16[8,256,1024]{1,2,0:T(8,128)(2,1)} %get-tuple-element.15, bf16[8,256,1024]{1,2,0:T(8,128)(2,1)} %get-tuple-element.14), kind=kOutput, calls=%fused_computation.27 | convolution fusion | flops 1098907648 | bytes 13631488 | tf_op jit(solution)/shard_map/fio,foc->fic/dot_general | solution.py:34
  220.7 7.0 %scatter_custom_fusion.3 = f32[4096,128]{1,0:T(8,128)} fusion(s32[2048]{0:T(1024)S(1)} %broadcast_select_fusion.2, f32[2048,128]{1,0:T(8,128)S(1)} %bitcast.82, f32[]{:T(128)} %constant.74.clone.1), kind=kCustom, calls=%fused_computation.63 | custom fusion | bytes 2097156
  227.7 4.2 all-to-all-start.2
  231.9 23.2 %all-to-all-done.2 = f32[8,512,128]{2,1,0:T(8,128)S(1)} async-done(((f32[8,512,128]{2,1,0:T(8,128)}), f32[8,512,128]{2,1,0:T(8,128)S(1)}, u32[]{:S(2)}, u32[]{:S(2)}) %all-to-all-start.2) | async-done | bytes 2097184 | tf_op jit(solution)/shard_map/all_to_all | solution.py:83
  255.1 32.7 %scatter_custom_fusion = f32[4096,128]{1,0:T(8,128)} fusion(s32[4096]{0:T(1024)S(1)} %bitcast.79, f32[4096,128]{1,0:T(8,128)S(1)} %bitcast.64, f32[]{:T(128)} %constant.74.clone.1), kind=kCustom, calls=%fused_computation.67 | custom fusion | flops 524288 | bytes 2097156 | tf_op jit(solution)/shard_map/scatter-add | solution.py:87
  287.8 1.9 reshape.264
  289.7 3.7 fusion.24
  293.5 2.3 copy.22
  295.7 1.4 reshape.265
  297.2 15.0 %gather_fusion.3 = bf16[4096,128]{1,0:T(8,128)(2,1)} fusion(bf16[4096,128]{1,0:T(8,128)(2,1)S(1)} %reshape.265, s32[4096]{0:T(1024)S(1)} %broadcast_clamp_fusion), kind=kCustom, calls=%fused_computation.1.clone | custom fusion | bytes 2113536 | tf_op jit(solution)/shard_map/jit(_take)/gather | solution.py:74
  312.2 1.8 broadcast_select_fusion
  314.0 19.9 %all_to_all.32 = bf16[8,512,128]{2,1,0:T(8,128)(2,1)S(1)} all-to-all(bf16[8,512,128]{2,1,0:T(8,128)(2,1)S(1)} %broadcast_select_fusion), channel_id=1, replica_groups=mesh['tm'=8,'sky'=4] {'tm'}, dimensions={0} | all-to-all | bytes 2097152 | tf_op jit(solution)/shard_map/all_to_all | solution.py:75
  333.9 20.5 %gather_fusion.1 = bf16[2048,128]{1,0:T(8,128)(2,1)} fusion(bf16[8,512,128]{2,1,0:T(8,128)(2,1)S(1)} %all_to_all.32, s32[2048]{0:T(1024)S(1)} %bitcast.60), kind=kCustom, calls=%fused_computation.3 | custom fusion | bytes 1064960 | tf_op jit(solution)/shard_map/gather | solution.py:76
  354.4 5.8 %fusion.57 = f32[8,2048,128]{2,1,0:T(8,128)S(1)} fusion(bf16[8,256,128]{2,1,0:T(8,128)(2,1)} %bitcast.65, bf16[8,256,1024]{1,2,0:T(8,128)(2,1)} %get-tuple-element.15, bf16[8,256,1024]{1,2,0:T(8,128)(2,1)} %get-tuple-element.14), kind=kOutput, calls=%fused_computation.135 | convolution fusion | flops 1090519040 | bytes 17301504 | tf_op jit(solution)/shard_map/fio,fic->foc/dot_general | solution.py:22
  360.3 3.0 fusion.59
  363.8 4.7 %multiply_convert_fusion.1 = (bf16[8,1024,128]{2,1,0:T(8,128)(2,1)}, bf16[8,1024,128]{2,1,0:T(8,128)(2,1)}) fusion(f32[8,1024]{1,0:T(8,128)S(1)} %get-tuple-element.21, f32[8,2048,128]{2,1,0:T(8,128)S(1)} %fusion.57, f32[8,128]{1,0:T(8,128)S(1)} %fusion.19, f32[8,1024,128]{2,1,0:T(8,128)S(1)} %get-tuple-element.6, f32[8,128]{1,0:T(8,128)S(1)} %get-tuple-element.5, ...), kind=kLoop, calls=%fused_computation.36 | loop fusion | flops 8388608 | bytes 16850944 | tf_op jit(solution)/shard_map/convert
  368.5 6.1 %fusion.14 = f32[8,256,128]{2,1,0:T(8,128)S(1)} fusion(bf16[8,1024,128]{2,1,0:T(8,128)(2,1)} %get-tuple-element.11, bf16[8,1024,128]{2,1,0:T(8,128)(2,1)} %get-tuple-element.10, bf16[8,256,1024]{1,2,0:T(8,128)(2,1)} %get-tuple-element.15, bf16[8,256,1024]{1,2,0:T(8,128)(2,1)} %get-tuple-element.14), kind=kOutput, calls=%fused_computation.31 | convolution fusion | flops 1098907648 | bytes 13631488 | tf_op jit(solution)/shard_map/fio,foc->fic/dot_general | solution.py:34
  374.6 7.0 %scatter_custom_fusion.4 = f32[4096,128]{1,0:T(8,128)} fusion(s32[2048]{0:T(1024)S(1)} %broadcast_select_fusion.2, f32[2048,128]{1,0:T(8,128)S(1)} %bitcast.81, f32[]{:T(128)} %constant.74.clone.1), kind=kCustom, calls=%fused_computation.61 | custom fusion | bytes 2097156
  381.6 5.5 %all-to-all-start.4 = ((f32[8,512,128]{2,1,0:T(8,128)}), f32[8,512,128]{2,1,0:T(8,128)}, u32[]{:S(2)}, u32[]{:S(2)}) async-start(f32[8,512,128]{2,1,0:T(8,128)} %bitcast.61), calls=%async_computation.4 | async-start | bytes 4194304 | tf_op jit(solution)/shard_map/all_to_all | solution.py:83
  387.2 0.6 log_add_fusion
  387.8 22.5 %all-to-all-done.4 = f32[8,512,128]{2,1,0:T(8,128)} async-done(((f32[8,512,128]{2,1,0:T(8,128)}), f32[8,512,128]{2,1,0:T(8,128)}, u32[]{:S(2)}, u32[]{:S(2)}) %all-to-all-start.4) | async-done | bytes 2097184 | tf_op jit(solution)/shard_map/all_to_all | solution.py:83
  410.3 24.1 %scatter_custom_fusion.1 = f32[4096,128]{1,0:T(8,128)} fusion(s32[4096]{0:T(1024)S(1)} %bitcast.80, f32[4096,128]{1,0:T(8,128)} %bitcast.18, f32[]{:T(128)} %constant.74.clone.1), kind=kCustom, calls=%fused_computation.65 | custom fusion | flops 524288 | bytes 2097664 | tf_op jit(solution)/shard_map/scatter-add | solution.py:87
  434.4 2.9 reshape.269
  437.3 3.4 fusion.22
  (33 shorter events, 2.5 us)
Async XLA Ops:
  7.2 137.5 %all-gather.2.cloned.1.call-start = ((), (), s32[]{:S(2)}) async-start(), calls=%async_computation.5 | async-start | bytes 2621440 | tf_op jit(solution)/shard_map/all_gather | solution.py:69
  24.0 120.6 %all-to-all-start = ((s32[8,1,512]{2,1,0:T(1,128)}), s32[8,1,512]{2,1,0:T(1,128)S(1)}, u32[]{:S(2)}, u32[]{:S(2)}) async-start(s32[8,1,512]{2,1,0:T(1,128)} %bitcast.3), calls=%async_computation | async-start | bytes 32768 | tf_op jit(solution)/shard_map/all_to_all | solution.py:57
  32.0 112.5 %copy-start.2 = (s32[4]{0:T(128)S(1)}, s32[4]{0:T(128)}, u32[]{:S(2)}) copy-start(s32[4]{0:T(128)} %param.9) | copy-start | bytes 52
  32.0 112.6 %copy-start = (bf16[4,512,256]{2,1,0:T(8,128)(2,1)S(1)}, bf16[4,512,256]{2,1,0:T(8,128)(2,1)}, u32[]{:S(2)}) copy-start(bf16[4,512,256]{2,1,0:T(8,128)(2,1)} %param.8) | copy-start | bytes 3145732
  162.0 22.3 %all-to-all-start.1 = ((bf16[8,512,128]{2,1,0:T(8,128)(2,1)}), bf16[8,512,128]{2,1,0:T(8,128)(2,1)S(1)}, u32[]{:S(2)}, u32[]{:S(2)}) async-start(bf16[8,512,128]{2,1,0:T(8,128)(2,1)} %broadcast_select_fusion.1), calls=%async_computation.1 | async-start | bytes 2097152 | tf_op jit(solution)/shard_map/all_to_all | solution.py:75
  227.7 27.4 %all-to-all-start.2 = ((f32[8,512,128]{2,1,0:T(8,128)}), f32[8,512,128]{2,1,0:T(8,128)S(1)}, u32[]{:S(2)}, u32[]{:S(2)}) async-start(f32[8,512,128]{2,1,0:T(8,128)} %bitcast.11), calls=%async_computation.2 | async-start | bytes 4194304 | tf_op jit(solution)/shard_map/all_to_all | solution.py:83
  381.6 28.7 %all-to-all-start.4 = ((f32[8,512,128]{2,1,0:T(8,128)}), f32[8,512,128]{2,1,0:T(8,128)}, u32[]{:S(2)}, u32[]{:S(2)}) async-start(f32[8,512,128]{2,1,0:T(8,128)} %bitcast.61), calls=%async_computation.4 | async-start | bytes 4194304 | tf_op jit(solution)/shard_map/all_to_all | solution.py:83
  387.2 50.1 %copy-start.1 = (bf16[4,512,256]{2,1,0:T(8,128)(2,1)S(1)}, bf16[4,512,256]{2,1,0:T(8,128)(2,1)}, u32[]{:S(2)}) copy-start(bf16[4,512,256]{2,1,0:T(8,128)(2,1)} %param.8) | copy-start | bytes 3145732
Sparse Core Ops, SparseCore 0:
  9.6 47.9 all-gather.1
where the time goes:
time: 456 us; the launch traced here: 448 us
  other arithmetic  220 us (48%)
  local copies, waits for them, and re-layouts  94 us (21%)
  waiting for transfers between devices  46.4 us (10%)
  matrix products  33.6 us (7%)
  blocking collectives  19.9 us (4%)
  starting transfers between devices  19.5 us (4%)
  between operations  14.5 us (3%)
    another operation x4, other arithmetic  120 us
    scatter-add x2, other arithmetic, on_device(): placed = jnp.zeros((empty_row, SRC_GROUP), jnp.float32).at[asked.reshape(...  56.8 us
    all_to_all x2, waiting for transfers between devices, on_device(): lax.all_to_all(outgoing, 'tm', split_axis=0, concat_axis=0, tiled=True)  45.7 us
    gather x2, local copies, waits for them, and re-layouts, on_device(): observed = arrived[target, position].reshape(sched_dev, obs, SRC_GROUP)  31.7 us
    gather x2, local copies, waits for them, and re-layouts, on_device(): picked = jnp.take(flat, asked, axis=0, mode='fill', fill_value=0)  27.2 us
    unnamed x15, local copies, waits for them, and re-layouts  24.8 us
    all_to_all x1, blocking collectives, on_device(): lax.all_to_all(picked, 'tm', split_axis=0, concat_axis=0, tiled=True)  19.9 us
    dot_general x2, matrix products, fit_groups(): jnp.einsum('fio,fic->foc', basis, observed, preferred_element_type=jnp.fl...  14.9 us
  transfers between devices with their start and end apart: 5, of which 2 were waited for; matrix products, arithmetic and copies ran while one was open for 33% of the time, Pallas kernels for 0%

commit v1 on v0

v1 whole, which is shorter than its diff:
```python
import functools

import jax
import jax.numpy as jnp
from jax import lax
from jax.experimental import pallas as pl
from jax.experimental.pallas import tpu as pltpu
from jax.sharding import PartitionSpec as P

SRC_GROUP = 128
ITERS = 2
STREAMS = 8
BETA = 2.0
RIDGE = 1.0
VMEM_LIMIT = 60 * 1024 * 1024

COS_POLY = (1.0, -19.73920440673828, 64.9391098022461, -85.4500503540039, 60.16689682006836,
            -25.96480369567871, 6.52468729019165)
SIN_POLY = (6.283185005187988, -41.34158706665039, 81.59986114501953, -76.61351013183594,
            41.33811950683594, -12.463061332702637)

VMEM = pl.BlockSpec(memory_space=pltpu.VMEM)
SMEM = pl.BlockSpec(memory_space=pltpu.SMEM)


def horner(poly, v):
    acc = jnp.full_like(v, poly[-1])
    for term in poly[-2::-1]:
        acc = acc * v + term
    return acc


def basis_kernel(time_ref, period_ref, inverse_ref, basis_ref, norm_ref):
    obs = time_ref.shape[0]
    nper = period_ref.shape[1]
    rows = 32
    for chunk in range(nper // 128):
        lanes = pl.ds(chunk * 128, 128)
        sines = pl.ds(nper + chunk * 128, 128)
        period = period_ref[:, lanes]
        inverse = inverse_ref[:, lanes]

        def step(index, sums):
            at = pl.ds(pl.multiple_of(index * rows, rows), rows)
            time = time_ref[at, :]
            turns = jnp.round(time * inverse)
            part = (time - turns * period) * inverse
            square = part * part
            cosine = horner(COS_POLY, square).astype(jnp.bfloat16)
            sine = (horner(SIN_POLY, square) * part).astype(jnp.bfloat16)
            basis_ref[0, at, lanes] = cosine
            basis_ref[0, at, sines] = sine
            cosine = cosine.astype(jnp.float32)
            sine = sine.astype(jnp.float32)
            return (
                sums[0] + jnp.sum((cosine * cosine).reshape(rows // 8, 8, 128), axis=0),
                sums[1] + jnp.sum((sine * sine).reshape(rows // 8, 8, 128), axis=0),
            )

        zero = jnp.zeros((8, 128), jnp.float32)
        total_c, total_s = lax.fori_loop(0, obs // rows, step, (zero, zero))
        norm_ref[0, :, lanes] = 1.0 / (jnp.sum(total_c, axis=0, keepdims=True) + RIDGE)
        norm_ref[0, :, sines] = 1.0 / (jnp.sum(total_s, axis=0, keepdims=True) + RIDGE)


def make_basis(times, periods):
    sched_dev, obs = times.shape
    nper = periods.shape[0]
    wide = jnp.broadcast_to(
        times.astype(jnp.float32).reshape(-1, 1), (sched_dev * obs, SRC_GROUP)
    )
    period = periods.astype(jnp.float32)[None, :]
    return pl.pallas_call(
        basis_kernel,
        grid=(sched_dev,),
        in_specs=[
            pl.BlockSpec((obs, SRC_GROUP), lambda j: (j, 0)),
            pl.BlockSpec((1, nper), lambda j: (0, 0)),
            pl.BlockSpec((1, nper), lambda j: (0, 0)),
        ],
        out_specs=[
            pl.BlockSpec((1, obs, 2 * nper), lambda j: (j, 0, 0)),
            pl.BlockSpec((1, 1, 2 * nper), lambda j: (j, 0, 0)),
        ],
        out_shape=[
            jax.ShapeDtypeStruct((sched_dev, obs, 2 * nper), jnp.bfloat16),
            jax.ShapeDtypeStruct((sched_dev, 1, 2 * nper), jnp.float32),
        ],
        compiler_params=pltpu.CompilerParams(vmem_limit_bytes=VMEM_LIMIT),
        cost_estimate=pl.CostEstimate(
            flops=sched_dev * obs * nper * 300, bytes_accessed=sched_dev * obs * nper * 4, transcendentals=0
        ),
    )(wide, period, 1.0 / period)


def copy_rows(count, out_ref, out_at, in_ref, in_at, unroll=8):
    def step(index, carry):
        for lane in range(unroll):
            row = index * unroll + lane
            out_ref[pl.ds(out_at(row), 1), :] = in_ref[pl.ds(in_at(row), 1), :]
        return carry

    lax.fori_loop(0, count // unroll, step, 0)


def fit_kernel(place_ref, arrived_ref, basis_ref, norm_ref, out_ref, score_ref,
               rows_ref, obs_ref, corr_ref, coeff_ref, model_ref, back_ref):
    plan = pl.program_id(0)
    plans = pl.num_programs(0)
    obs, width = obs_ref.shape
    nper = basis_ref.shape[2] // 2

    @pl.when(plan == 0)
    def _():
        rows_ref[...] = arrived_ref[...].astype(jnp.float32)

    first = plan * obs
    copy_rows(obs, obs_ref, lambda row: row, rows_ref, lambda row: place_ref[first + row])
    corr_ref[...] = lax.dot_general(
        obs_ref[...].astype(jnp.bfloat16), basis_ref[0], (((0,), (0,)), ((), ())),
        preferred_element_type=jnp.float32,
    )
    group = 16
    for start in range(0, width, group):
        at = pl.ds(start, group)
        power = []
        for chunk in range(nper // 128):
            lanes = pl.ds(chunk * 128, 128)
            sines = pl.ds(nper + chunk * 128, 128)
            cosine = corr_ref[at, lanes]
            sine = corr_ref[at, sines]
            power.append(
                cosine * (cosine * norm_ref[0, :, lanes]) + sine * (sine * norm_ref[0, :, sines])
            )
        highest = functools.reduce(jnp.maximum, power)
        highest = jnp.max(highest, axis=1, keepdims=True)
        expo = [jnp.exp(BETA * (value - highest)) for value in power]
        total = jnp.sum(functools.reduce(jnp.add, expo), axis=1, keepdims=True)
        scale = 1.0 / total
        for chunk in range(nper // 128):
            lanes = pl.ds(chunk * 128, 128)
            sines = pl.ds(nper + chunk * 128, 128)
            share = expo[chunk] * scale
            coeff_ref[at, lanes] = (share * (corr_ref[at, lanes] * norm_ref[0, :, lanes])).astype(jnp.bfloat16)
            coeff_ref[at, sines] = (share * (corr_ref[at, sines] * norm_ref[0, :, sines])).astype(jnp.bfloat16)
        score_ref[0, at, :] = BETA * highest + jnp.log(total)
    model_ref[...] = lax.dot_general(
        basis_ref[0], coeff_ref[...], (((1,), (1,)), ((), ())), preferred_element_type=jnp.float32
    )
    copy_rows(obs, back_ref, lambda row: place_ref[first + row], model_ref, lambda row: row)

    @pl.when(plan == plans - 1)
    def _():
        out_ref[...] = back_ref[...].astype(jnp.bfloat16)


def fit_plans(place, arrived, basis, norms):
    sched_dev, obs, twice = basis.shape
    slots, width = arrived.shape
    work = sched_dev * obs * twice * width
    return pl.pallas_call(
        fit_kernel,
        grid=(sched_dev,),
        in_specs=[
            SMEM,
            VMEM,
            pl.BlockSpec((1, obs, twice), lambda j: (j, 0, 0)),
            pl.BlockSpec((1, 1, twice), lambda j: (j, 0, 0)),
        ],
        out_specs=[VMEM, pl.BlockSpec((1, width, 1), lambda j: (j, 0, 0))],
        out_shape=[
            jax.ShapeDtypeStruct((slots, width), jnp.bfloat16),
            jax.ShapeDtypeStruct((sched_dev, width, 1), jnp.float32),
        ],
        scratch_shapes=[
            pltpu.VMEM((slots, width), jnp.float32),
            pltpu.VMEM((obs, width), jnp.float32),
            pltpu.VMEM((width, twice), jnp.float32),
            pltpu.VMEM((width, twice), jnp.bfloat16),
            pltpu.VMEM((obs, width), jnp.float32),
            pltpu.VMEM((slots, width), jnp.float32),
        ],
        compiler_params=pltpu.CompilerParams(vmem_limit_bytes=VMEM_LIMIT),
        cost_estimate=pl.CostEstimate(flops=4 * work, bytes_accessed=2 * basis.size, transcendentals=0),
    )(place, arrived, basis, norms)


def whiten_and_pick(asked_ref, count_ref, attitude_ref, load, picked_ref, white_ref, gather_ref):
    segs, slots, _ = attitude_ref.shape
    requests, width = picked_ref.shape
    blocks = white_ref.shape[0] // (segs * slots)
    row = lax.broadcasted_iota(jnp.int32, (slots, width * blocks), 0)
    for seg in range(segs):
        masked = jnp.where(row < count_ref[seg], load(seg).astype(jnp.float32), 0.0).astype(jnp.bfloat16)
        white = jnp.dot(attitude_ref[seg], masked, preferred_element_type=jnp.float32)
        for block in range(blocks):
            white_ref[pl.ds((block * segs + seg) * slots, slots), :] = white[:, block * width:(block + 1) * width]
    copy_rows(requests, gather_ref, lambda row: row, white_ref, lambda row: asked_ref[row])
    picked_ref[...] = gather_ref[...].astype(jnp.bfloat16)


def pick_kernel(asked_ref, count_ref, attitude_ref, residual_ref, picked_ref, white_ref, gather_ref):
    whiten_and_pick(
        asked_ref, count_ref, attitude_ref, lambda seg: residual_ref[seg], picked_ref, white_ref, gather_ref
    )


def place_rows(asked_ref, returned_ref, current_ref, out_ref, rows_ref, sums):
    segs, slots, _ = current_ref.shape
    requests, width = returned_ref.shape
    blocks = current_ref.shape[2] // width
    part = requests // len(sums)
    rows_ref[...] = returned_ref[...].astype(jnp.float32)
    for total in sums:
        total[...] = jnp.zeros_like(total)

    def step(index, carry):
        rows = [stream * part + index for stream in range(len(sums))]
        places = [asked_ref[row] for row in rows]
        values = [
            total[pl.ds(place, 1), :] + rows_ref[pl.ds(row, 1), :]
            for total, place, row in zip(sums, places, rows)
        ]
        for total, place, value in zip(sums, places, values):
            total[pl.ds(place, 1), :] = value
        return carry

    lax.fori_loop(0, part, step, 0, unroll=2)
    for seg in range(segs):
        for block in range(blocks):
            at = pl.ds((block * segs + seg) * slots, slots)
            lanes = slice(block * width, (block + 1) * width)
            placed = functools.reduce(jnp.add, [total[at, :] for total in sums])
            out_ref[seg, :, lanes] = current_ref[seg, :, lanes].astype(jnp.float32) - placed


def place_pick_kernel(asked_ref, count_ref, attitude_ref, returned_ref, current_ref, out_ref, picked_ref,
                      white_ref, gather_ref, rows_ref, *sums):
    place_rows(asked_ref, returned_ref, current_ref, out_ref, rows_ref, sums)
    whiten_and_pick(
        asked_ref, count_ref, attitude_ref, lambda seg: out_ref[seg], picked_ref, white_ref, gather_ref
    )


def place_kernel(asked_ref, returned_ref, current_ref, out_ref, rows_ref, *sums):
    place_rows(asked_ref, returned_ref, current_ref, out_ref, rows_ref, sums)


def on_device(residuals, seg_counts, attitude, sched_seg, sched_slot, periods):
    tm_count = lax.axis_size("tm")
    sched_dev, obs = sched_seg.shape
    seg_dev, slots, width = residuals.shape
    column_blocks = width // SRC_GROUP
    capacity = 2 * sched_dev * obs // tm_count
    requests = tm_count * capacity
    whole = lax.all_gather(attitude, "sky", axis=1, tiled=True)

    seg_flat = sched_seg.reshape(-1)
    slot_flat = sched_slot.reshape(-1)
    block_of = jnp.repeat(jnp.arange(sched_dev, dtype=jnp.int32) % column_blocks, obs)
    target = seg_flat // seg_dev
    local_row = (block_of * seg_dev + seg_flat % seg_dev) * slots + slot_flat
    onehot = (target[:, None] == jnp.arange(tm_count, dtype=jnp.int32)[None, :]).astype(jnp.int32)
    position = jnp.sum(jnp.cumsum(onehot, axis=0) * onehot, axis=1) - 1
    place = target * capacity + position
    rows = seg_dev * slots * column_blocks
    wanted = jnp.full((requests,), rows, jnp.int32).at[place].set(local_row, unique_indices=True)
    asked = lax.all_to_all(
        wanted.reshape(tm_count, capacity), "tm", split_axis=0, concat_axis=0, tiled=True
    ).reshape(-1)
    basis, norms = make_basis(sched_seg * slots + sched_slot, periods)

    def exchange(values):
        shaped = values.reshape(tm_count, capacity, SRC_GROUP)
        return lax.all_to_all(shaped, "tm", split_axis=0, concat_axis=0, tiled=True).reshape(
            requests, SRC_GROUP
        )

    table = pltpu.VMEM((rows + 8, SRC_GROUP), jnp.float32)
    list_rows = pltpu.VMEM((requests, SRC_GROUP), jnp.float32)
    picked_shape = jax.ShapeDtypeStruct((requests, SRC_GROUP), jnp.bfloat16)
    current_shape = jax.ShapeDtypeStruct(residuals.shape, jnp.float32)
    params = pltpu.CompilerParams(vmem_limit_bytes=VMEM_LIMIT)
    white_flops = 2 * seg_dev * slots * slots * width

    current = residuals
    for iteration in range(ITERS):
        if iteration == 0:
            picked = pl.pallas_call(
                pick_kernel,
                in_specs=[SMEM, SMEM, VMEM, VMEM],
                out_specs=VMEM,
                out_shape=picked_shape,
                scratch_shapes=[table, list_rows],
                compiler_params=params,
                cost_estimate=pl.CostEstimate(flops=white_flops, bytes_accessed=8 << 20, transcendentals=0),
            )(asked, seg_counts, whole, current)
        else:
            current, picked = pl.pallas_call(
                place_pick_kernel,
                in_specs=[SMEM, SMEM, VMEM, VMEM, VMEM],
                out_specs=[VMEM, VMEM],
                out_shape=[current_shape, picked_shape],
                scratch_shapes=[table, list_rows, list_rows] + [table] * STREAMS,
                compiler_params=params,
                cost_estimate=pl.CostEstimate(flops=white_flops, bytes_accessed=16 << 20, transcendentals=0),
            )(asked, seg_counts, whole, returned, current)
        model, score = fit_plans(place, exchange(picked), basis, norms)
        returned = exchange(model)
    current = pl.pallas_call(
        place_kernel,
        in_specs=[SMEM, VMEM, VMEM],
        out_specs=VMEM,
        out_shape=current_shape,
        scratch_shapes=[list_rows] + [table] * STREAMS,
        compiler_params=params,
        cost_estimate=pl.CostEstimate(flops=1 << 20, bytes_accessed=16 << 20, transcendentals=0),
    )(asked, returned, current)
    return (current, score.reshape(sched_dev, SRC_GROUP))


def solution(mesh):
    in_specs = (
        P("tm", None, "sky"),
        P("tm"),
        P("tm", "sky", None),
        P(("tm", "sky"), None),
        P(("tm", "sky"), None),
        P(),
    )
    out_specs = (P("tm", None, "sky"), P(("tm", "sky"), None))
    return jax.shard_map(
        on_device, mesh=mesh, in_specs=in_specs, out_specs=out_specs, check_vma=False
    )
```

time: 456 us -> 223 us (0.49)
  other arithmetic: 220 us -> 5.27 us
  Pallas kernels: 0 us -> 91 us
  local copies, waits for them, and re-layouts: 94 us -> 14.5 us
  matrix products: 33.6 us -> 0 us
  blocking collectives: 19.9 us -> 47.4 us
  starting transfers between devices: 19.5 us -> 9.49 us
  waiting for transfers between devices: 46.4 us -> 37.5 us
    another operation x4 -> x2, other arithmetic: 120 us -> 2.45 us
    pallas_call x0 -> x6, Pallas kernels: none -> 91 us  [the longest x2 36.3 us: fit_plans(): pl.pallas_call(fit_kernel, grid=(sched_dev,), in_specs=[SMEM, VMEM, pl.Bl...]
    gather x4 -> x0, local copies, waits for them, and re-layouts: 58.8 us -> none  [the longest x2 31.7 us: on_device(): observed = arrived[target, position].reshape(sched_dev, obs, SRC_GROUP)]
    scatter-add x2 -> x0, other arithmetic: 56.8 us -> none  [on_device(): placed = jnp.zeros((empty_row, SRC_GROUP), jnp.float32).at[asked.reshape(...]
    all_to_all x4 -> x2, waiting for transfers between devices: 45.7 us -> 11.1 us  [exchange(): lax.all_to_all(shaped, 'tm', split_axis=0, concat_axis=0, tiled=True)]
    dot_general x6 -> x0, matrix products: 33.6 us -> none  [the longest x2 14.9 us: fit_groups(): jnp.einsum('fio,fic->foc', basis, observed, preferred_element_type=jnp.fl...]
    all_to_all x1 -> x3, blocking collectives: 19.9 us -> 47.4 us  [the longest x2 37.9 us: exchange(): lax.all_to_all(shaped, 'tm', split_axis=0, concat_axis=0, tiled=True)]
    all_gather x1, waiting for transfers between devices: 0.02 us -> 25.7 us  [on_device(): whole = lax.all_gather(attitude, 'sky', axis=1, tiled=True)]
  transfers between devices with their start and end apart: 5 -> 3, of which waited for: 2 -> 2; matrix products, arithmetic and copies ran while one was open for 33% -> 8% of each run, Pallas kernels for 0% -> 9%
where the time goes in v1:
time: 223 us; the launch traced here: 219 us
  Pallas kernels  91 us (41%)
  blocking collectives  47.4 us (21%)
  waiting for transfers between devices  37.5 us (17%)
  local copies, waits for them, and re-layouts  14.5 us (7%)
  between operations  14.1 us (6%)
  starting transfers between devices  9.49 us (4%)
  other arithmetic  5.27 us (2%)
    all_to_all x2, blocking collectives, exchange(): lax.all_to_all(shaped, 'tm', split_axis=0, concat_axis=0, tiled=True)  37.9 us
    pallas_call x2, Pallas kernels, fit_plans(): pl.pallas_call(fit_kernel, grid=(sched_dev,), in_specs=[SMEM, VMEM, pl.Bl...  36.3 us
    all_gather x1, waiting for transfers between devices, on_device(): whole = lax.all_gather(attitude, 'sky', axis=1, tiled=True)  25.7 us
    pallas_call x1, Pallas kernels, make_basis(): pl.pallas_call(basis_kernel, grid=(sched_dev,), in_specs=[pl.BlockSpec((o...  18.8 us
    pallas_call x1, Pallas kernels, on_device(): pl.pallas_call(place_pick_kernel, in_specs=[SMEM, SMEM, VMEM, VMEM, VMEM]...  16.6 us
    all_to_all x2, waiting for transfers between devices, exchange(): lax.all_to_all(shaped, 'tm', split_axis=0, concat_axis=0, tiled=True)  11.1 us
    pallas_call x1, Pallas kernels, on_device(): pl.pallas_call(place_kernel, in_specs=[SMEM, VMEM, VMEM], out_specs=VMEM,...  9.99 us
    all_to_all x2, starting transfers between devices, exchange(): lax.all_to_all(shaped, 'tm', split_axis=0, concat_axis=0, tiled=True)  9.46 us
  transfers between devices with their start and end apart: 3, of which 2 were waited for; matrix products, arithmetic and copies ran while one was open for 8% of the time, Pallas kernels for 9%

profile of v1, /device:TPU:1, one launch (start us, length us, event | category | flops | bytes accessed | tf_op | source)
XLA Modules:
  0.0 219.2 jit_solution(3964844737859723272)
XLA Ops:
  7.2 0.0 all-gather.2.cloned.1.call-start
  7.2 0.7 all-gather.2.cloned.1.call-update
  7.9 0.1 broadcast_bitcast_fusion
  8.0 0.7 reshape.180
  8.7 0.7 copy.8
  9.4 0.7 copy.9
  10.1 0.7 copy.12
  10.8 2.3 %reduce-window.6 = s32[8,16,128]{2,1,0:T(8,128)S(1)} reduce-window(s32[8,16,128]{2,1,0:T(8,128)S(1)} %fusion.2, s32[]{:T(128)} %constant.51.clone.1), window={size=1x1x128 pad=0_0x0_0x127_0}, to_apply=%region_0.1 | reduce-window | flops 2080768 | bytes 131076 | tf_op jit(solution)/shard_map/reduce-window
  13.1 0.3 slice_reduce_fusion
  13.4 0.2 reduce-window.9
  13.6 0.1 add_bitcast_fusion
  13.7 0.6 multiply_add_fusion
  14.3 0.1 compare_select_fusion
  14.4 8.1 %scatter_custom_fusion = s32[4096]{0:T(1024)S(1)} fusion(s32[2048]{0:T(1024)S(1)} %bitcast.67, s32[2048]{0:T(1024)S(1)} %get-tuple-element.17, s32[]{:T(128)} %constant.49.clone.1), kind=kCustom, calls=%fused_computation.31 | custom fusion | bytes 16388 | tf_op jit(solution)/shard_map/scatter | solution.py:267
  22.4 9.4 %all_to_all.29 = s32[8,1,512]{2,1,0:T(1,128)} all-to-all(s32[8,1,512]{2,1,0:T(1,128)S(1)} %bitcast.59), channel_id=1, replica_groups=mesh['tm'=8,'sky'=4] {'tm'}, dimensions={0} | all-to-all | bytes 32768 | tf_op jit(solution)/shard_map/all_to_all | solution.py:268
  31.9 25.7 %all-gather.2.cloned.1.call-done.attitude_ref = bf16[4,512,512]{2,1,0:T(8,128)(2,1)} async-done(((bf16[4,128,512]{2,1,0:T(8,128)(2,1)}), bf16[4,512,512]{2,1,0:T(8,128)(2,1)}) %all-gather.2.cloned.1.call-update) | async-done | bytes 2097168 | tf_op jit(solution)/shard_map/all_gather | solution.py:256
  57.6 9.3 %shard_map.77 = bf16[4096,128]{1,0:T(8,128)(2,1)} custom-call(s32[4096]{0:T(1024)} %bitcast.52, s32[4]{0:T(128)} %count_ref.3, bf16[4,512,512]{2,1,0:T(8,128)(2,1)} %all-gather.2.cloned.1.call-done.attitude_ref, bf16[4,512,256]{2,1,0:T(8,128)(2,1)} %current_ref.1), custom_call_target="tpu_custom_call" | custom-call | flops 536870912 | bytes 8388608 | tf_op jit(solution)/shard_map/pallas_call | solution.py:289
  66.9 0.0 copy-start.5
  66.9 0.0 copy-start.3
  66.9 0.0 copy-start.4
  66.9 4.5 %all-to-all-start.1 = ((bf16[8,512,128]{2,1,0:T(8,128)(2,1)}), bf16[8,512,128]{2,1,0:T(8,128)(2,1)S(1)}, u32[]{:S(2)}, u32[]{:S(2)}) async-start(bf16[8,512,128]{2,1,0:T(8,128)(2,1)} %bitcast.44), calls=%async_computation.1 | async-start | bytes 2097152 | tf_op jit(solution)/shard_map/all_to_all | solution.py:275
  71.4 0.0 copy-done.5
  71.4 0.6 convert_element_type.13
  72.0 0.0 copy-done.3
  72.0 0.0 copy-done.4
  72.0 0.6 broadcast_divide_fusion
  72.6 1.3 broadcast_in_dim.22.time_ref
  73.9 18.8 %shard_map.78 = (bf16[8,256,2048]{2,1,0:T(8,128)(2,1)}, f32[8,1,2048]{2,1,0:T(1,128)}) custom-call(f32[2048,128]{1,0:T(8,128)} %broadcast_in_dim.22.time_ref, f32[1,1024]{1,0:T(1,128)} %bitcast.68, f32[1,1024]{1,0:T(1,128)} %bitcast.69), custom_call_target="tpu_custom_call" | custom-call | flops 629145600 | bytes 8388608 | tf_op jit(solution)/shard_map/pallas_call | solution.py:73
  92.7 0.0 all-to-all-done.1
  92.7 0.0 copy-start.1
  92.7 1.0 copy-done.1
  93.7 18.2 %shard_map.79 = (bf16[4096,128]{1,0:T(8,128)(2,1)}, f32[8,128,1]{2,1,0:T(8,128)}) custom-call(s32[2048]{0:T(1024)} %get-tuple-element.16.place_ref, bf16[4096,128]{1,0:T(8,128)(2,1)} %bitcast.47, bf16[8,256,2048]{2,1,0:T(8,128)(2,1)} %get-tuple-element.9.basis_ref, f32[8,1,2048]{2,1,0:T(1,128)} %get-tuple-element.10.norm_ref), custom_call_target="tpu_custom_call" | custom-call | flops 2147483648 | bytes 8388608 | tf_op jit(solution)/shard_map/pallas_call | solution.py:161
  111.9 18.3 %all_to_all.30 = bf16[8,512,128]{2,1,0:T(8,128)(2,1)} all-to-all(bf16[8,512,128]{2,1,0:T(8,128)(2,1)} %bitcast.51), channel_id=1, replica_groups=mesh['tm'=8,'sky'=4] {'tm'}, dimensions={0} | all-to-all | bytes 2097152 | tf_op jit(solution)/shard_map/all_to_all | solution.py:275
  130.2 16.6 %shard_map.80 = (f32[4,512,256]{2,1,0:T(8,128)}, bf16[4096,128]{1,0:T(8,128)(2,1)}) custom-call(s32[4096]{0:T(1024)} %bitcast.53, s32[4]{0:T(128)} %count_ref.3, bf16[4,512,512]{2,1,0:T(8,128)(2,1)} %all-gather.2.cloned.1.call-done.attitude_ref, bf16[4096,128]{1,0:T(8,128)(2,1)} %bitcast.46, bf16[4,512,256]{2,1,0:T(8,128)(2,1)} %current_ref.1), custom_call_target="tpu_custom_call" | custom-call | flops 536870912 | bytes 16777216 | tf_op jit(solution)/shard_map/pallas_call | solution.py:299
  146.8 19.6 %all_to_all.31 = bf16[8,512,128]{2,1,0:T(8,128)(2,1)} all-to-all(bf16[8,512,128]{2,1,0:T(8,128)(2,1)} %bitcast.50), channel_id=1, replica_groups=mesh['tm'=8,'sky'=4] {'tm'}, dimensions={0} | all-to-all | bytes 2097152 | tf_op jit(solution)/shard_map/all_to_all | solution.py:275
  166.4 18.2 %shard_map.81 = (bf16[4096,128]{1,0:T(8,128)(2,1)}, f32[8,128,1]{2,1,0:T(8,128)}) custom-call(s32[2048]{0:T(1024)} %get-tuple-element.16.place_ref, bf16[4096,128]{1,0:T(8,128)(2,1)} %bitcast.48, bf16[8,256,2048]{2,1,0:T(8,128)(2,1)} %get-tuple-element.9.basis_ref, f32[8,1,2048]{2,1,0:T(1,128)} %get-tuple-element.10.norm_ref), custom_call_target="tpu_custom_call" | custom-call | flops 2147483648 | bytes 8388608 | tf_op jit(solution)/shard_map/pallas_call | solution.py:161
  184.5 0.0 copy-start.2
  184.5 4.9 %all-to-all-start.4 = ((bf16[8,512,128]{2,1,0:T(8,128)(2,1)}), bf16[8,512,128]{2,1,0:T(8,128)(2,1)S(1)}, u32[]{:S(2)}, u32[]{:S(2)}) async-start(bf16[8,512,128]{2,1,0:T(8,128)(2,1)} %bitcast.49), calls=%async_computation.4 | async-start | bytes 2097152 | tf_op jit(solution)/shard_map/all_to_all | solution.py:275
  189.5 0.0 copy-done.2
  189.5 0.8 reduce.1
  190.3 11.1 %all-to-all-done.4 = bf16[8,512,128]{2,1,0:T(8,128)(2,1)S(1)} async-done(((bf16[8,512,128]{2,1,0:T(8,128)(2,1)}), bf16[8,512,128]{2,1,0:T(8,128)(2,1)S(1)}, u32[]{:S(2)}, u32[]{:S(2)}) %all-to-all-start.4) | async-done | bytes 1048608 | tf_op jit(solution)/shard_map/all_to_all | solution.py:275
  201.4 0.0 copy-start
  201.4 1.0 copy-done
  202.3 10.0 %shard_map.82 = f32[4,512,256]{2,1,0:T(8,128)} custom-call(s32[4096]{0:T(1024)} %bitcast.54, bf16[4096,128]{1,0:T(8,128)(2,1)} %bitcast.45, f32[4,512,256]{2,1,0:T(8,128)} %get-tuple-element.14.current_ref), custom_call_target="tpu_custom_call" | custom-call | flops 1048576 | bytes 16777216 | tf_op jit(solution)/shard_map/pallas_call | solution.py:310
  (8 shorter events, 0.1 us)
Async XLA Ops:
  7.2 50.4 %all-gather.2.cloned.1.call-start = ((), (), s32[]{:S(2)}) async-start(), calls=%async_computation.5 | async-start | bytes 2621440 | tf_op jit(solution)/shard_map/all_gather | solution.py:256
  66.9 4.5 %copy-start.5 = (s32[1024]{0:T(1024)S(1)}, s32[1024]{0:T(1024)}, u32[]{:S(2)}) copy-start(s32[1024]{0:T(1024)} %param.11) | copy-start | bytes 12292
  66.9 5.1 %copy-start.3 = (s32[8,256]{1,0:T(8,128)S(1)}, s32[8,256]{1,0:T(8,128)}, u32[]{:S(2)}) copy-start(s32[8,256]{1,0:T(8,128)} %param.9) | copy-start | bytes 24580
  66.9 5.1 %copy-start.4 = (s32[8,256]{1,0:T(8,128)S(1)}, s32[8,256]{1,0:T(8,128)}, u32[]{:S(2)}) copy-start(s32[8,256]{1,0:T(8,128)} %param.10) | copy-start | bytes 24580
  66.9 25.8 %all-to-all-start.1 = ((bf16[8,512,128]{2,1,0:T(8,128)(2,1)}), bf16[8,512,128]{2,1,0:T(8,128)(2,1)S(1)}, u32[]{:S(2)}, u32[]{:S(2)}) async-start(bf16[8,512,128]{2,1,0:T(8,128)(2,1)} %bitcast.44), calls=%async_computation.1 | async-start | bytes 2097152 | tf_op jit(solution)/shard_map/all_to_all | solution.py:275
  92.7 1.0 copy-start.1
  184.5 4.9 %copy-start.2 = (f32[8,128,1]{2,1,0:T(8,128)S(1)}, f32[8,128,1]{2,1,0:T(8,128)}, u32[]{:S(2)}) copy-start(f32[8,128,1]{2,1,0:T(8,128)} %get-tuple-element.15) | copy-start | bytes 12292
  184.5 16.8 %all-to-all-start.4 = ((bf16[8,512,128]{2,1,0:T(8,128)(2,1)}), bf16[8,512,128]{2,1,0:T(8,128)(2,1)S(1)}, u32[]{:S(2)}, u32[]{:S(2)}) async-start(bf16[8,512,128]{2,1,0:T(8,128)(2,1)} %bitcast.49), calls=%async_computation.4 | async-start | bytes 2097152 | tf_op jit(solution)/shard_map/all_to_all | solution.py:275
  201.4 1.0 copy-start
Sparse Core Ops, SparseCore 0:
  9.6 47.9 all-gather.1

commit v2 on v1

v2 whole, which is shorter than its diff:
```python
import functools

import jax
import jax.numpy as jnp
from jax import lax
from jax.experimental import pallas as pl
from jax.experimental.pallas import tpu as pltpu
from jax.sharding import PartitionSpec as P

SRC_GROUP = 128
ITERS = 2
STREAMS = 4
STEP = 16
BETA = 2.0
RIDGE = 1.0
VMEM_LIMIT = 60 * 1024 * 1024

COS_POLY = (1.0, -19.73920440673828, 64.9391098022461, -85.4500503540039, 60.16689682006836,
            -25.96480369567871, 6.52468729019165)
SIN_POLY = (6.283185005187988, -41.34158706665039, 81.59986114501953, -76.61351013183594,
            41.33811950683594, -12.463061332702637)

VMEM = pl.BlockSpec(memory_space=pltpu.VMEM)
SMEM = pl.BlockSpec(memory_space=pltpu.SMEM)


def horner(poly, v):
    acc = jnp.full_like(v, poly[-1])
    for term in poly[-2::-1]:
        acc = acc * v + term
    return acc


def basis_kernel(time_ref, period_ref, inverse_ref, basis_ref, norm_ref):
    obs = time_ref.shape[0]
    nper = period_ref.shape[1]
    rows = 32
    for chunk in range(nper // 128):
        lanes = pl.ds(chunk * 128, 128)
        sines = pl.ds(nper + chunk * 128, 128)
        period = period_ref[:, lanes]
        inverse = inverse_ref[:, lanes]

        def step(index, sums):
            at = pl.ds(pl.multiple_of(index * rows, rows), rows)
            time = time_ref[at, :]
            turns = jnp.round(time * inverse)
            part = (time - turns * period) * inverse
            square = part * part
            cosine = horner(COS_POLY, square).astype(jnp.bfloat16)
            sine = (horner(SIN_POLY, square) * part).astype(jnp.bfloat16)
            basis_ref[0, at, lanes] = cosine
            basis_ref[0, at, sines] = sine
            cosine = cosine.astype(jnp.float32)
            sine = sine.astype(jnp.float32)
            return (
                sums[0] + jnp.sum((cosine * cosine).reshape(rows // 8, 8, 128), axis=0),
                sums[1] + jnp.sum((sine * sine).reshape(rows // 8, 8, 128), axis=0),
            )

        zero = jnp.zeros((8, 128), jnp.float32)
        total_c, total_s = lax.fori_loop(0, obs // rows, step, (zero, zero))
        norm_ref[0, :, lanes] = 1.0 / (jnp.sum(total_c, axis=0, keepdims=True) + RIDGE)
        norm_ref[0, :, sines] = 1.0 / (jnp.sum(total_s, axis=0, keepdims=True) + RIDGE)


def make_basis(times, periods):
    sched_dev, obs = times.shape
    nper = periods.shape[0]
    wide = jnp.broadcast_to(
        times.astype(jnp.float32).reshape(-1, 1), (sched_dev * obs, SRC_GROUP)
    )
    period = periods.astype(jnp.float32)[None, :]
    return pl.pallas_call(
        basis_kernel,
        grid=(sched_dev,),
        in_specs=[
            pl.BlockSpec((obs, SRC_GROUP), lambda j: (j, 0)),
            pl.BlockSpec((1, nper), lambda j: (0, 0)),
            pl.BlockSpec((1, nper), lambda j: (0, 0)),
        ],
        out_specs=[
            pl.BlockSpec((1, obs, 2 * nper), lambda j: (j, 0, 0)),
            pl.BlockSpec((1, 1, 2 * nper), lambda j: (j, 0, 0)),
        ],
        out_shape=[
            jax.ShapeDtypeStruct((sched_dev, obs, 2 * nper), jnp.bfloat16),
            jax.ShapeDtypeStruct((sched_dev, 1, 2 * nper), jnp.float32),
        ],
        compiler_params=pltpu.CompilerParams(vmem_limit_bytes=VMEM_LIMIT),
        cost_estimate=pl.CostEstimate(
            flops=sched_dev * obs * nper * 300, bytes_accessed=sched_dev * obs * nper * 4, transcendentals=0
        ),
    )(wide, period, 1.0 / period)


def fit_kernel(tm_count, cnt_ref, src_ref, dst_ref, *refs):
    arrived = refs[:tm_count]
    basis_ref, norm_ref = refs[tm_count:tm_count + 2]
    outs = refs[tm_count + 2:2 * tm_count + 2]
    score_ref, rows_ref, obs_ref, corr_ref, coeff_ref, model_ref, back_ref = refs[2 * tm_count + 2:]
    plan = pl.program_id(0)
    plans = pl.num_programs(0)
    capacity, width = arrived[0].shape
    obs = basis_ref.shape[1]
    nper = basis_ref.shape[2] // 2
    spaced = capacity + STEP

    @pl.when(plan == 0)
    def _():
        for owner in range(tm_count):
            rows_ref[pl.ds(owner * spaced, capacity), :] = arrived[owner][...].astype(jnp.float32)

    def ranges(move):
        for owner in range(tm_count):
            first = owner * spaced + src_ref[plan, owner]
            target = dst_ref[plan, owner]

            def step(index, carry):
                move(first + index * STEP, target + index * STEP)
                return carry

            lax.fori_loop(0, (cnt_ref[plan, owner] + STEP - 1) // STEP, step, 0)

    def collect(first, target):
        obs_ref[pl.ds(target, STEP), :] = rows_ref[pl.ds(first, STEP), :]

    def put_back(first, target):
        back_ref[pl.ds(first, STEP), :] = model_ref[pl.ds(target, STEP), :]

    ranges(collect)
    corr_ref[...] = lax.dot_general(
        obs_ref[:obs, :].astype(jnp.bfloat16), basis_ref[0], (((0,), (0,)), ((), ())),
        preferred_element_type=jnp.float32,
    )
    group = 16
    for start in range(0, width, group):
        at = pl.ds(start, group)
        power = []
        for chunk in range(nper // 128):
            lanes = pl.ds(chunk * 128, 128)
            sines = pl.ds(nper + chunk * 128, 128)
            cosine = corr_ref[at, lanes]
            sine = corr_ref[at, sines]
            power.append(
                cosine * (cosine * norm_ref[0, :, lanes]) + sine * (sine * norm_ref[0, :, sines])
            )
        highest = functools.reduce(jnp.maximum, power)
        highest = jnp.max(highest, axis=1, keepdims=True)
        expo = [jnp.exp(BETA * (value - highest)) for value in power]
        total = jnp.sum(functools.reduce(jnp.add, expo), axis=1, keepdims=True)
        scale = 1.0 / total
        for chunk in range(nper // 128):
            lanes = pl.ds(chunk * 128, 128)
            sines = pl.ds(nper + chunk * 128, 128)
            share = expo[chunk] * scale
            coeff_ref[at, lanes] = (share * (corr_ref[at, lanes] * norm_ref[0, :, lanes])).astype(jnp.bfloat16)
            coeff_ref[at, sines] = (share * (corr_ref[at, sines] * norm_ref[0, :, sines])).astype(jnp.bfloat16)
        score_ref[0, at, :] = BETA * highest + jnp.log(total)
    model_ref[:obs, :] = lax.dot_general(
        basis_ref[0], coeff_ref[...], (((1,), (1,)), ((), ())), preferred_element_type=jnp.float32
    )
    ranges(put_back)

    @pl.when(plan == plans - 1)
    def _():
        for owner in range(tm_count):
            outs[owner][...] = back_ref[pl.ds(owner * spaced, capacity), :].astype(jnp.bfloat16)


def fit_plans(tables, arrived, basis, norms):
    tm_count = len(arrived)
    sched_dev, obs, twice = basis.shape
    capacity, width = arrived[0].shape
    work = sched_dev * obs * twice * width
    spaced = tm_count * (capacity + STEP)
    *models, score = pl.pallas_call(
        functools.partial(fit_kernel, tm_count),
        grid=(sched_dev,),
        in_specs=[SMEM, SMEM, SMEM] + [VMEM] * tm_count + [
            pl.BlockSpec((1, obs, twice), lambda j: (j, 0, 0)),
            pl.BlockSpec((1, 1, twice), lambda j: (j, 0, 0)),
        ],
        out_specs=[VMEM] * tm_count + [pl.BlockSpec((1, width, 1), lambda j: (j, 0, 0))],
        out_shape=[jax.ShapeDtypeStruct((capacity, width), jnp.bfloat16)] * tm_count
        + [jax.ShapeDtypeStruct((sched_dev, width, 1), jnp.float32)],
        scratch_shapes=[
            pltpu.VMEM((spaced, width), jnp.float32),
            pltpu.VMEM((obs + STEP, width), jnp.float32),
            pltpu.VMEM((width, twice), jnp.float32),
            pltpu.VMEM((width, twice), jnp.bfloat16),
            pltpu.VMEM((obs + STEP, width), jnp.float32),
            pltpu.VMEM((spaced, width), jnp.float32),
        ],
        compiler_params=pltpu.CompilerParams(vmem_limit_bytes=VMEM_LIMIT),
        cost_estimate=pl.CostEstimate(flops=4 * work, bytes_accessed=2 * basis.size, transcendentals=0),
    )(*tables, *arrived, basis, norms)
    return models, score


def load_attitude(where_ref, own_ref, passed, whole_ref, sems):
    sky = where_ref[0]
    count = len(passed) // 2 + 1
    rows = own_ref.shape[1]
    copies = [(True, sky, own_ref)]
    for hop in range(1, count):
        copies.append((sky >= hop, sky - hop, passed[2 * hop - 2]))
        copies.append((sky + hop < count, sky + hop, passed[2 * hop - 1]))

    def each(act):
        for index, (valid, quarter, ref) in enumerate(copies):
            def run(index=index, quarter=quarter, ref=ref):
                at = pl.ds(pl.multiple_of(quarter * rows, rows), rows)
                act(pltpu.make_async_copy(ref, whole_ref.at[:, at, :], sems.at[index]))

            if valid is True:
                run()
            else:
                pl.when(valid)(run)

    each(lambda copy: copy.start())
    return lambda: each(lambda copy: copy.wait())


def whiten_and_pick(asked_ref, cnt_ref, count_ref, whole_ref, load, picked, white_ref, gather_ref):
    segs, slots, _ = whole_ref.shape
    capacity, width = picked[0].shape
    blocks = white_ref.shape[0] // (segs * slots)
    row = lax.broadcasted_iota(jnp.int32, (slots, width * blocks), 0)
    for seg in range(segs):
        masked = jnp.where(row < count_ref[seg], load(seg).astype(jnp.float32), 0.0).astype(jnp.bfloat16)
        white = jnp.dot(whole_ref[seg], masked, preferred_element_type=jnp.float32)
        for block in range(blocks):
            white_ref[pl.ds((block * segs + seg) * slots, slots), :] = white[:, block * width:(block + 1) * width]
    for owner, out_ref in enumerate(picked):
        def step(index, carry):
            at = owner * capacity + index * 8
            for lane in range(8):
                gather_ref[pl.ds(at + lane, 1), :] = white_ref[pl.ds(asked_ref[at + lane], 1), :]
            return carry

        lax.fori_loop(0, (cnt_ref[owner] + 7) // 8, step, 0)
        out_ref[...] = gather_ref[pl.ds(owner * capacity, capacity), :].astype(jnp.bfloat16)


def place_rows(asked_ref, cnt_ref, returned, current_ref, out_ref, rows_ref, sums):
    segs, slots, _ = current_ref.shape
    capacity, width = returned[0].shape
    blocks = current_ref.shape[2] // width
    streams = len(sums)
    for total in sums:
        total[...] = jnp.zeros_like(total)
    for owner, ref in enumerate(returned):
        rows_ref[pl.ds(owner * capacity, capacity), :] = ref[...].astype(jnp.float32)

        def step(index, carry):
            first = owner * capacity + index * 8
            for start in range(0, 8, streams):
                rows = [first + start + lane for lane in range(streams)]
                places = [asked_ref[row] for row in rows]
                values = [
                    total[pl.ds(place, 1), :] + rows_ref[pl.ds(row, 1), :]
                    for total, place, row in zip(sums, places, rows)
                ]
                for total, place, value in zip(sums, places, values):
                    total[pl.ds(place, 1), :] = value
            return carry

        lax.fori_loop(0, (cnt_ref[owner] + 7) // 8, step, 0)
    for seg in range(segs):
        for block in range(blocks):
            at = pl.ds((block * segs + seg) * slots, slots)
            lanes = slice(block * width, (block + 1) * width)
            placed = functools.reduce(jnp.add, [total[at, :] for total in sums])
            out_ref[seg, :, lanes] = current_ref[seg, :, lanes].astype(jnp.float32) - placed


def owner_kernel(tm_count, passed_count, placing, picking, *refs):
    refs = list(refs)

    def take(count):
        taken = refs[:count]
        del refs[:count]
        return taken

    asked_ref, cnt_ref, count_ref, where_ref = take(4)
    (current_ref,) = take(1)
    attitude = take(passed_count + 1) if picking else None
    returned = take(tm_count) if placing else None
    out_ref = take(1)[0] if placing else None
    picked = take(tm_count) if picking else None
    wait = None
    if picking:
        whole_ref, sems, white_ref = take(3)
        wait = load_attitude(where_ref, attitude[0], attitude[1:], whole_ref, sems)
    (rows_ref,) = take(1)
    if placing:
        place_rows(asked_ref, cnt_ref, returned, current_ref, out_ref, rows_ref, refs)
    if picking:
        wait()
        source = out_ref if placing else current_ref
        whiten_and_pick(
            asked_ref, cnt_ref, count_ref, whole_ref, lambda seg: source[seg], picked, white_ref, rows_ref
        )


def owner_step(scalars, current, attitude, returned):
    asked, cnt, seg_counts, where = scalars
    seg_dev, slots, width = current.shape
    placing, picking = returned is not None, attitude is not None
    tm_count = cnt.shape[0]
    capacity = asked.shape[0] // tm_count
    table = pltpu.VMEM((seg_dev * slots * width // SRC_GROUP + 8, SRC_GROUP), jnp.float32)
    in_specs = [SMEM] * 4 + [VMEM]
    args = [asked, cnt, seg_counts, where, current]
    out_shape = []
    scratch = []
    if picking:
        in_specs += [pl.BlockSpec(memory_space=pl.ANY)] * len(attitude)
        args += attitude
        scratch += [
            pltpu.VMEM((seg_dev, slots, slots), jnp.bfloat16),
            pltpu.SemaphoreType.DMA((len(attitude),)),
            table,
        ]
    scratch.append(pltpu.VMEM((tm_count * capacity, SRC_GROUP), jnp.float32))
    if placing:
        in_specs += [VMEM] * tm_count
        args += returned
        out_shape.append(jax.ShapeDtypeStruct(current.shape, jnp.float32))
        scratch += [table] * STREAMS
    if picking:
        out_shape += [jax.ShapeDtypeStruct((capacity, SRC_GROUP), jnp.bfloat16)] * tm_count
    passed = len(attitude) - 1 if picking else 0
    out = pl.pallas_call(
        functools.partial(owner_kernel, tm_count, passed, placing, picking),
        in_specs=in_specs,
        out_specs=[VMEM] * len(out_shape),
        out_shape=out_shape,
        scratch_shapes=scratch,
        compiler_params=pltpu.CompilerParams(vmem_limit_bytes=VMEM_LIMIT),
        cost_estimate=pl.CostEstimate(
            flops=2 * seg_dev * slots * slots * width, bytes_accessed=16 << 20, transcendentals=0
        ),
    )(*args)
    if placing:
        return out[0], list(out[1:])
    return current, list(out)


def make_lists(sched_seg, sched_slot, seg_dev, slots, column_blocks, tm_count, capacity):
    sched_dev, obs = sched_seg.shape
    partner = (sched_seg // seg_dev) ^ lax.axis_index("tm")
    block_of = (jnp.arange(sched_dev, dtype=jnp.int32) % column_blocks)[:, None]
    local_row = (block_of * seg_dev + sched_seg % seg_dev) * slots + sched_slot
    hot = (partner[:, :, None] == jnp.arange(tm_count, dtype=jnp.int32)).astype(jnp.int32)
    cnt = jnp.sum(hot, axis=1)
    plans = jnp.arange(sched_dev)
    before = (plans[None, :] < plans[:, None]).astype(jnp.int32)
    src = jnp.sum(before[:, :, None] * cnt[None, :, :], axis=1)
    owners = jnp.arange(tm_count)
    ahead = (owners[None, :] < owners[:, None]).astype(jnp.int32)
    dst = jnp.sum(ahead[None, :, :] * cnt[:, None, :], axis=2)
    entry = jnp.arange(obs)
    rank = jnp.sum(
        ((partner[:, None, :] == partner[:, :, None]) & (entry[None, :] < entry[:, None])).astype(jnp.int32),
        axis=2,
    )
    place = partner * capacity + jnp.sum(hot * src[:, None, :], axis=2) + rank
    order = jnp.sum(hot * dst[:, None, :], axis=2) + rank
    time = sched_seg * slots + sched_slot
    times = jnp.sum(jnp.where(order[:, None, :] == entry[None, :, None], time[:, None, :], 0), axis=2)
    rows = seg_dev * slots * column_blocks
    wanted = rows + jnp.sum(
        jnp.where(
            place.reshape(1, -1) == jnp.arange(tm_count * capacity, dtype=jnp.int32)[:, None],
            local_row.reshape(1, -1) - rows,
            0,
        ),
        axis=1,
    )
    return (cnt, src, dst), times, wanted


def exchange(blocks):
    count = len(blocks)
    return [blocks[0]] + [
        lax.ppermute(blocks[step], "tm", [(i, i ^ step) for i in range(count)]) for step in range(1, count)
    ]


def pass_along(shard):
    count = lax.axis_size("sky")
    right = left = shard
    passed = []
    for hop in range(1, count):
        right = lax.ppermute(right, "sky", [(i, i + 1) for i in range(hop - 1, count - 1)])
        left = lax.ppermute(left, "sky", [(i, i - 1) for i in range(1, count - hop + 1)])
        passed += [right, left]
    return [shard] + passed


def on_device(residuals, seg_counts, attitude, sched_seg, sched_slot, periods):
    tm_count = lax.axis_size("tm")
    sched_dev, obs = sched_seg.shape
    seg_dev, slots, width = residuals.shape
    column_blocks = width // SRC_GROUP
    capacity = 2 * sched_dev * obs // tm_count
    pieces = pass_along(attitude)
    tables, times, wanted = make_lists(
        sched_seg, sched_slot, seg_dev, slots, column_blocks, tm_count, capacity
    )
    wanted = wanted.reshape(tm_count, capacity)
    asked = jnp.concatenate(exchange([wanted[owner] for owner in range(tm_count)]))
    cnt = jnp.sum((asked.reshape(tm_count, capacity) < seg_dev * slots * column_blocks).astype(jnp.int32), axis=1)
    basis, norms = make_basis(times, periods)
    scalars = (asked, cnt, seg_counts, lax.axis_index("sky").reshape(1))

    current, returned = residuals, None
    for iteration in range(ITERS):
        current, picked = owner_step(scalars, current, pieces, returned)
        models, score = fit_plans(tables, exchange(picked), basis, norms)
        returned = exchange(models)
    current, _ = owner_step(scalars, current, None, returned)
    return (current, score.reshape(sched_dev, SRC_GROUP))


def solution(mesh):
    in_specs = (
        P("tm", None, "sky"),
        P("tm"),
        P("tm", "sky", None),
        P(("tm", "sky"), None),
        P(("tm", "sky"), None),
        P(),
    )
    out_specs = (P("tm", None, "sky"), P(("tm", "sky"), None))
    return jax.shard_map(
        on_device, mesh=mesh, in_specs=in_specs, out_specs=out_specs, check_vma=False
    )
```

time: 223 us -> 191 us (0.86); the launches traced: 219 us -> 189 us
  blocking collectives: 47.4 us -> 0 us
  starting transfers between devices: 9.49 us -> 53.6 us
  Pallas kernels: 91 us -> 75.5 us
  between operations: 14.1 us -> 1.3 us
  local copies, waits for them, and re-layouts: 14.5 us -> 5.27 us
  waiting for transfers between devices: 37.5 us -> 44 us
  other arithmetic: 5.27 us -> 9.74 us
    ppermute x0 -> x41, starting transfers between devices: none -> 53.6 us  [the longest x35 43.6 us: exchange(): lax.ppermute(blocks[step], 'tm', [(i, i ^ step) for i in range(count)])]
    all_to_all x3 -> x0, blocking collectives: 47.4 us -> none  [the longest x2 37.9 us: exchange(): lax.all_to_all(shaped, 'tm', split_axis=0, concat_axis=0, tiled=True)]
    ppermute x0 -> x41, waiting for transfers between devices: none -> 44 us  [the longest x35 28.8 us: exchange(): lax.ppermute(blocks[step], 'tm', [(i, i ^ step) for i in range(count)])]
    all_gather x1 -> x0, waiting for transfers between devices: 25.7 us -> none  [on_device(): whole = lax.all_gather(attitude, 'sky', axis=1, tiled=True)]
    pallas_call x5, Pallas kernels: 72.2 us -> 56.7 us  [the longest x2 29.7 us: fit_plans(): pl.pallas_call(functools.partial(fit_kernel, tm_count), grid=(sched_dev,)...]
    all_to_all x2 -> x0, waiting for transfers between devices: 11.1 us -> none  [exchange(): lax.all_to_all(shaped, 'tm', split_axis=0, concat_axis=0, tiled=True)]
    all_to_all x2 -> x0, starting transfers between devices: 9.46 us -> none  [exchange(): lax.all_to_all(shaped, 'tm', split_axis=0, concat_axis=0, tiled=True)]
    scatter x1 -> x0, local copies, waits for them, and re-layouts: 8.06 us -> none  [on_device(): jnp.full((requests,), rows, jnp.int32).at[place]]
  transfers between devices with their start and end apart: 3 -> 41, of which waited for: 2 -> 13; matrix products, arithmetic and copies ran while one was open for 8% -> 6% of each run, Pallas kernels for 9% -> 10%
where the time goes in v2:
time: 191 us; the launch traced here: 189 us
  Pallas kernels  75.5 us (40%)
  starting transfers between devices  53.6 us (28%)
  waiting for transfers between devices  44 us (23%)
  other arithmetic  9.74 us (5%)
  local copies, waits for them, and re-layouts  5.27 us (3%)
    ppermute x35, starting transfers between devices, exchange(): lax.ppermute(blocks[step], 'tm', [(i, i ^ step) for i in range(count)])  43.6 us
    pallas_call x2, Pallas kernels, fit_plans(): pl.pallas_call(functools.partial(fit_kernel, tm_count), grid=(sched_dev,)...  29.7 us
    ppermute x35, waiting for transfers between devices, exchange(): lax.ppermute(blocks[step], 'tm', [(i, i ^ step) for i in range(count)])  28.8 us
    pallas_call x3, Pallas kernels, owner_step(): pl.pallas_call(functools.partial(owner_kernel, tm_count, passed, placing,...  27 us
    pallas_call x1, Pallas kernels, make_basis(): pl.pallas_call(basis_kernel, grid=(sched_dev,), in_specs=[pl.BlockSpec((o...  18.8 us
    ppermute x3, waiting for transfers between devices, pass_along(): lax.ppermute(left, 'sky', [(i, i - 1) for i in range(1, count - hop + 1)])  15.2 us
    ppermute x3, starting transfers between devices, pass_along(): lax.ppermute(right, 'sky', [(i, i + 1) for i in range(hop - 1, count - 1)])  6.08 us
    unnamed x87, local copies, waits for them, and re-layouts  3.95 us
  transfers between devices with their start and end apart: 41, of which 13 were waited for; matrix products, arithmetic and copies ran while one was open for 6% of the time, Pallas kernels for 10%

profile of v2, /device:TPU:1, one launch (start us, length us, event | category | flops | bytes accessed | tf_op | source)
XLA Modules:
  0.0 189.4 jit_solution(9822608322296850917)
XLA Ops:
  0.6 1.3 collective-permute-start.8
  1.9 4.7 %collective-permute-start.7 = (bf16[4,128,512]{2,1,0:T(8,128)(2,1)}, bf16[4,128,512]{2,1,0:T(8,128)(2,1)S(1)}, u32[]{:S(2)}, u32[]{:S(2)}) collective-permute-start(bf16[4,128,512]{2,1,0:T(8,128)(2,1)} %refs_5_.3), channel_id=1, source_target_pairs={{0,1},{1,2},{2,3},{4,5},{5,6},{6,7},{8,9},{9,10},{10,11},{12,13},{... | collective-permute-start | bytes 1572872 | tf_op jit(solution)/shard_map/ppermute | solution.py:397
  6.7 0.8 multiply_add_fusion
  7.7 0.8 convert_reduce_fusion
  8.9 3.4 %select_reduce_fusion = s32[4096]{0:T(1024)S(1)} fusion(s32[2048]{0:T(1024)S(1)} %bitcast.13, s32[2048]{0:T(1024)S(1)} %bitcast.14), kind=kLoop, calls=%fused_computation | loop fusion | flops 25161728 | bytes 32768 | tf_op jit(solution)/shard_map/reduce_sum | solution.py:374
  12.4 3.5 %collective-permute-start.6 = (s32[512]{0:T(512)S(1)}, s32[512]{0:T(512)S(1)}, u32[]{:S(2)}, u32[]{:S(2)}) collective-permute-start(s32[512]{0:T(512)S(1)} %get-tuple-element.80), channel_id=1, source_target_pairs={{0,28},{4,24},{8,20},{12,16},{16,12},{20,8},{24,4},{28,0},{1,29},{... | collective-permute-start | bytes 6152 | tf_op jit(solution)/shard_map/ppermute | solution.py:388
  16.5 1.3 collective-permute-start.10
  19.0 1.1 collective-permute-start.1
  20.1 1.4 collective-permute-done.1
  21.5 3.6 %collective-permute-start.2 = (s32[512]{0:T(512)S(1)}, s32[512]{0:T(512)S(1)}, u32[]{:S(2)}, u32[]{:S(2)}) collective-permute-start(s32[512]{0:T(512)S(1)} %get-tuple-element.84), channel_id=1, source_target_pairs={{0,12},{4,8},{8,4},{12,0},{16,28},{20,24},{24,20},{28,16},{1,13},{... | collective-permute-start | bytes 6152 | tf_op jit(solution)/shard_map/ppermute | solution.py:388
  25.1 1.6 collective-permute-done.2
  26.7 1.2 collective-permute-start.3
  27.9 1.5 collective-permute-done.3
  29.4 2.3 %collective-permute-start.4 = (s32[512]{0:T(512)S(1)}, s32[512]{0:T(512)S(1)}, u32[]{:S(2)}, u32[]{:S(2)}) collective-permute-start(s32[512]{0:T(512)S(1)} %get-tuple-element.82), channel_id=1, source_target_pairs={{0,20},{4,16},{8,28},{12,24},{16,4},{20,0},{24,12},{28,8},{1,21},{... | collective-permute-start | bytes 6152 | tf_op jit(solution)/shard_map/ppermute | solution.py:388
  31.7 1.3 collective-permute-start.12
  33.9 0.7 reduce_sum.86.refs_1_
  34.6 15.0 %collective-permute-done.12.refs_11_ = bf16[4,128,512]{2,1,0:T(8,128)(2,1)S(1)} collective-permute-done((bf16[4,128,512]{2,1,0:T(8,128)(2,1)S(1)}, bf16[4,128,512]{2,1,0:T(8,128)(2,1)S(1)}, u32[]{:S(2)}, u32[]{:S(2)}) %collective-permute-start.12) | collective-permute-done | bytes 524320 | tf_op jit(solution)/shard_map/ppermute | solution.py:398
  49.7 0.7 copy-done.4
  50.6 7.5 %shard_map.77 = (bf16[512,128]{1,0:T(8,128)(2,1)}, bf16[512,128]{1,0:T(8,128)(2,1)}, bf16[512,128]{1,0:T(8,128)(2,1)}, bf16[512,128]{1,0:T(8,128)(2,1)}, bf16[51...) custom-call(s32[4096]{0:T(1024)} %copy-done.6, ...), custom_call_target="tpu_custom_call" | custom-call | flops 536870912 | bytes 16777216 | tf_op jit(solution)/shard_map/pallas_call | solution.py:335
  58.2 1.5 collective-permute-start.14
  60.3 1.8 collective-permute-start.16
  62.2 2.0 %collective-permute-start.18 = (bf16[512,128]{1,0:T(8,128)(2,1)}, bf16[512,128]{1,0:T(8,128)(2,1)S(1)}, u32[]{:S(2)}, u32[]{:S(2)}) collective-permute-start(bf16[512,128]{1,0:T(8,128)(2,1)} %get-tuple-element.44), channel_id=1, source_target_pairs={{0,24},{4,28},{8,16},{12,20},{16,8},{20,12},{24,0},{28,4},{1,25},{... | collective-permute-start | bytes 393224 | tf_op jit(solution)/shard_map/ppermute | solution.py:388
  64.2 3.0 %collective-permute-start.19 = (bf16[512,128]{1,0:T(8,128)(2,1)}, bf16[512,128]{1,0:T(8,128)(2,1)S(1)}, u32[]{:S(2)}, u32[]{:S(2)}) collective-permute-start(bf16[512,128]{1,0:T(8,128)(2,1)} %get-tuple-element.45), channel_id=1, source_target_pairs={{0,28},{4,24},{8,20},{12,16},{16,12},{20,8},{24,4},{28,0},{1,29},{... | collective-permute-start | bytes 393224 | tf_op jit(solution)/shard_map/ppermute | solution.py:388
  68.3 1.3 broadcast_in_dim.24.time_ref
  69.6 18.8 %shard_map.78 = (bf16[8,256,2048]{2,1,0:T(8,128)(2,1)}, f32[8,1,2048]{2,1,0:T(1,128)}) custom-call(f32[2048,128]{1,0:T(8,128)} %broadcast_in_dim.24.time_ref, f32[1,1024]{1,0:T(1,128)} %bitcast.16, f32[1,1024]{1,0:T(1,128)} %bitcast.15), custom_call_target="tpu_custom_call" | custom-call | flops 629145600 | bytes 8388608 | tf_op jit(solution)/shard_map/pallas_call | solution.py:74
  89.3 14.8 %shard_map.79 = (bf16[512,128]{1,0:T(8,128)(2,1)}, bf16[512,128]{1,0:T(8,128)(2,1)}, bf16[512,128]{1,0:T(8,128)(2,1)}, bf16[512,128]{1,0:T(8,128)(2,1)}, bf16[51...) custom-call(s32[8,8]{1,0:T(8,128)} %copy-done.35, ...), custom_call_target="tpu_custom_call" | custom-call | flops 2147483648 | bytes 8388608 | tf_op jit(solution)/shard_map/pallas_call | solution.py:177
  104.2 1.0 collective-permute-start.21
  105.3 1.1 collective-permute-start.22
  107.0 0.8 collective-permute-start.24
  107.8 0.8 collective-permute-start.25
  109.1 2.2 %collective-permute-start.26 = (bf16[512,128]{1,0:T(8,128)(2,1)}, bf16[512,128]{1,0:T(8,128)(2,1)S(1)}, u32[]{:S(2)}, u32[]{:S(2)}) collective-permute-start(bf16[512,128]{1,0:T(8,128)(2,1)} %get-tuple-element.55), channel_id=1, source_target_pairs={{0,28},{4,24},{8,20},{12,16},{16,12},{20,8},{24,4},{28,0},{1,29},{... | collective-permute-start | bytes 393224 | tf_op jit(solution)/shard_map/ppermute | solution.py:388
  111.4 2.3 %collective-permute-done.22.refs_15_ = bf16[512,128]{1,0:T(8,128)(2,1)S(1)} collective-permute-done((bf16[512,128]{1,0:T(8,128)(2,1)}, bf16[512,128]{1,0:T(8,128)(2,1)S(1)}, u32[]{:S(2)}, u32[]{:S(2)}) %collective-permute-start.22) | collective-permute-done | bytes 131104 | tf_op jit(solution)/shard_map/ppermute | solution.py:388
  113.7 6.5 %collective-permute-done.24.refs_17_ = bf16[512,128]{1,0:T(8,128)(2,1)S(1)} collective-permute-done((bf16[512,128]{1,0:T(8,128)(2,1)}, bf16[512,128]{1,0:T(8,128)(2,1)S(1)}, u32[]{:S(2)}, u32[]{:S(2)}) %collective-permute-start.24) | collective-permute-done | bytes 131104 | tf_op jit(solution)/shard_map/ppermute | solution.py:388
  121.0 11.7 %shard_map.80 = (f32[4,512,256]{2,1,0:T(8,128)}, bf16[512,128]{1,0:T(8,128)(2,1)}, bf16[512,128]{1,0:T(8,128)(2,1)}, bf16[512,128]{1,0:T(8,128)(2,1)}, bf16[512,...) custom-call(s32[4096]{0:T(1024)} %copy-done.6, ...), custom_call_target="tpu_custom_call" | custom-call | flops 536870912 | bytes 16777216 | tf_op jit(solution)/shard_map/pallas_call | solution.py:335
  132.9 1.8 collective-permute-start.28
  135.0 1.7 collective-permute-start.30
  137.0 1.3 collective-permute-start.32
  138.4 2.6 %collective-permute-start.33 = (bf16[512,128]{1,0:T(8,128)(2,1)}, bf16[512,128]{1,0:T(8,128)(2,1)S(1)}, u32[]{:S(2)}, u32[]{:S(2)}) collective-permute-start(bf16[512,128]{1,0:T(8,128)(2,1)} %get-tuple-element.64), channel_id=1, source_target_pairs={{0,28},{4,24},{8,20},{12,16},{16,12},{20,8},{24,4},{28,0},{1,29},{... | collective-permute-start | bytes 393224 | tf_op jit(solution)/shard_map/ppermute | solution.py:388
  141.0 1.3 collective-permute-done.29.refs_3_
  142.3 6.8 %collective-permute-done.31.refs_5_ = bf16[512,128]{1,0:T(8,128)(2,1)S(1)} collective-permute-done((bf16[512,128]{1,0:T(8,128)(2,1)}, bf16[512,128]{1,0:T(8,128)(2,1)S(1)}, u32[]{:S(2)}, u32[]{:S(2)}) %collective-permute-start.31) | collective-permute-done | bytes 131104 | tf_op jit(solution)/shard_map/ppermute | solution.py:388
  149.9 14.9 %shard_map.81 = (bf16[512,128]{1,0:T(8,128)(2,1)}, bf16[512,128]{1,0:T(8,128)(2,1)}, bf16[512,128]{1,0:T(8,128)(2,1)}, bf16[512,128]{1,0:T(8,128)(2,1)}, bf16[51...) custom-call(s32[8,8]{1,0:T(8,128)} %copy-done.35, ...), custom_call_target="tpu_custom_call" | custom-call | flops 2147483648 | bytes 8388608 | tf_op jit(solution)/shard_map/pallas_call | solution.py:177
  164.9 1.9 collective-permute-start.35
  167.0 1.5 collective-permute-start.37
  168.8 1.1 collective-permute-start.39
  170.6 2.3 %collective-permute-start.40 = (bf16[512,128]{1,0:T(8,128)(2,1)}, bf16[512,128]{1,0:T(8,128)(2,1)S(1)}, u32[]{:S(2)}, u32[]{:S(2)}) collective-permute-start(bf16[512,128]{1,0:T(8,128)(2,1)} %get-tuple-element.72), channel_id=1, source_target_pairs={{0,28},{4,24},{8,20},{12,16},{16,12},{20,8},{24,4},{28,0},{1,29},{... | collective-permute-start | bytes 393224 | tf_op jit(solution)/shard_map/ppermute | solution.py:388
  172.9 1.8 reduce
  174.8 6.1 %collective-permute-done.38.refs_10_ = bf16[512,128]{1,0:T(8,128)(2,1)S(1)} collective-permute-done((bf16[512,128]{1,0:T(8,128)(2,1)}, bf16[512,128]{1,0:T(8,128)(2,1)S(1)}, u32[]{:S(2)}, u32[]{:S(2)}) %collective-permute-start.38) | collective-permute-done | bytes 131104 | tf_op jit(solution)/shard_map/ppermute | solution.py:388
  181.6 7.8 %shard_map.82 = f32[4,512,256]{2,1,0:T(8,128)} custom-call(s32[4096]{0:T(1024)} %copy-done.6, s32[8]{0:T(128)} %reduce_sum.86.refs_1_, s32[4]{0:T(128)} %refs_2_.5, s32[1]{0:T(128)} %bitcast.refs_3_, f32[4,512,256]{2,1,0:T(8,128)} %get-tuple-element.56.refs_4_, bf16[512,128]{1,0:T(8,128)(2,1)} %get-tuple-element.65.refs_5_, bf16[512,128]{1,0:T(8,128)(2,1)} %copy-done.24, ...), custom_call_target="tpu_custom_call" | custom-call | flops 536870912 | bytes 16777216 | tf_op jit(solution)/shard_map/pallas_call | solution.py:335
  (150 shorter events, 11.7 us)
Async XLA Ops:
  0.6 15.9 %collective-permute-start.8 = (bf16[4,128,512]{2,1,0:T(8,128)(2,1)}, bf16[4,128,512]{2,1,0:T(8,128)(2,1)S(1)}, u32[]{:S(2)}, u32[]{:S(2)}) collective-permute-start(bf16[4,128,512]{2,1,0:T(8,128)(2,1)} %refs_5_.3), channel_id=1, source_target_pairs={{1,0},{2,1},{3,2},{5,4},{6,5},{7,6},{9,8},{10,9},{11,10},{13,12},{... | collective-permute-start | bytes 1572872 | tf_op jit(solution)/shard_map/ppermute | solution.py:398
  1.9 15.9 %collective-permute-start.7 = (bf16[4,128,512]{2,1,0:T(8,128)(2,1)}, bf16[4,128,512]{2,1,0:T(8,128)(2,1)S(1)}, u32[]{:S(2)}, u32[]{:S(2)}) collective-permute-start(bf16[4,128,512]{2,1,0:T(8,128)(2,1)} %refs_5_.3), channel_id=1, source_target_pairs={{0,1},{1,2},{2,3},{4,5},{5,6},{6,7},{8,9},{9,10},{10,11},{12,13},{... | collective-permute-start | bytes 1572872 | tf_op jit(solution)/shard_map/ppermute | solution.py:397
  7.7 50.4 %copy-start.35 = (s32[8,8]{1,0:T(8,128)}, s32[8,8]{1,0:T(8,128)S(1)}, u32[]{:S(2)}) copy-start(s32[8,8]{1,0:T(8,128)S(1)} %convert_reduce_fusion.1.cnt_ref) | copy-start | bytes 772
  8.8 49.3 %copy-start.36 = (s32[8,8]{1,0:T(8,128)}, s32[8,8]{1,0:T(8,128)S(1)}, u32[]{:S(2)}) copy-start(s32[8,8]{1,0:T(8,128)S(1)} %get-tuple-element.76.dst_ref) | copy-start | bytes 772
  8.8 49.3 %copy-start.37 = (s32[8,8]{1,0:T(8,128)}, s32[8,8]{1,0:T(8,128)S(1)}, u32[]{:S(2)}) copy-start(s32[8,8]{1,0:T(8,128)S(1)} %get-tuple-element.77.src_ref) | copy-start | bytes 772
  12.4 21.5 %collective-permute-start.6 = (s32[512]{0:T(512)S(1)}, s32[512]{0:T(512)S(1)}, u32[]{:S(2)}, u32[]{:S(2)}) collective-permute-start(s32[512]{0:T(512)S(1)} %get-tuple-element.80), channel_id=1, source_target_pairs={{0,28},{4,24},{8,20},{12,16},{16,12},{20,8},{24,4},{28,0},{1,29},{... | collective-permute-start | bytes 6152 | tf_op jit(solution)/shard_map/ppermute | solution.py:388
  15.9 17.9 %collective-permute-start.5 = (s32[512]{0:T(512)S(1)}, s32[512]{0:T(512)S(1)}, u32[]{:S(2)}, u32[]{:S(2)}) collective-permute-start(s32[512]{0:T(512)S(1)} %get-tuple-element.81), channel_id=1, source_target_pairs={{0,24},{4,28},{8,16},{12,20},{16,8},{20,12},{24,0},{28,4},{1,25},{... | collective-permute-start | bytes 6152 | tf_op jit(solution)/shard_map/ppermute | solution.py:388
  15.9 3.1 %collective-permute-start = (s32[512]{0:T(512)S(1)}, s32[512]{0:T(512)S(1)}, u32[]{:S(2)}, u32[]{:S(2)}) collective-permute-start(s32[512]{0:T(512)S(1)} %get-tuple-element.86), channel_id=1, source_target_pairs={{0,4},{4,0},{8,12},{12,8},{16,20},{20,16},{24,28},{28,24},{1,5},{5... | collective-permute-start | bytes 6152 | tf_op jit(solution)/shard_map/ppermute | solution.py:388
  16.5 33.1 %copy-start = (bf16[4,128,512]{2,1,0:T(8,128)(2,1)}, bf16[4,128,512]{2,1,0:T(8,128)(2,1)S(1)}, u32[]{:S(2)}) copy-start(bf16[4,128,512]{2,1,0:T(8,128)(2,1)S(1)} %collective-permute-done.8.refs_7_) | copy-start | bytes 1572868
  16.5 15.2 %collective-permute-start.10 = (bf16[4,128,512]{2,1,0:T(8,128)(2,1)S(1)}, bf16[4,128,512]{2,1,0:T(8,128)(2,1)S(1)}, u32[]{:S(2)}, u32[]{:S(2)}) collective-permute-start(bf16[4,128,512]{2,1,0:T(8,128)(2,1)S(1)} %collective-permute-done.8.refs_7_), channel_id=1, source_target_pairs={{1,0},{2,1},{5,4},{6,5},{9,8},{10,9},{13,12},{14,13},{17,16},{18,1... | collective-permute-start | bytes 1572872 | tf_op jit(solution)/shard_map/ppermute | solution.py:398
  17.8 31.8 %copy-start.1 = (bf16[4,128,512]{2,1,0:T(8,128)(2,1)}, bf16[4,128,512]{2,1,0:T(8,128)(2,1)S(1)}, u32[]{:S(2)}) copy-start(bf16[4,128,512]{2,1,0:T(8,128)(2,1)S(1)} %collective-permute-done.7.refs_6_) | copy-start | bytes 1572868
  17.8 15.2 %collective-permute-start.9 = (bf16[4,128,512]{2,1,0:T(8,128)(2,1)S(1)}, bf16[4,128,512]{2,1,0:T(8,128)(2,1)S(1)}, u32[]{:S(2)}, u32[]{:S(2)}) collective-permute-start(bf16[4,128,512]{2,1,0:T(8,128)(2,1)S(1)} %collective-permute-done.7.refs_6_), channel_id=1, source_target_pairs={{1,2},{2,3},{5,6},{6,7},{9,10},{10,11},{13,14},{14,15},{17,18},{18... | collective-permute-start | bytes 1572872 | tf_op jit(solution)/shard_map/ppermute | solution.py:397
  19.0 2.5 %collective-permute-start.1 = (s32[512]{0:T(512)S(1)}, s32[512]{0:T(512)S(1)}, u32[]{:S(2)}, u32[]{:S(2)}) collective-permute-start(s32[512]{0:T(512)S(1)} %get-tuple-element.85), channel_id=1, source_target_pairs={{0,8},{4,12},{8,0},{12,4},{16,24},{20,28},{24,16},{28,20},{1,9},{5... | collective-permute-start | bytes 6152 | tf_op jit(solution)/shard_map/ppermute | solution.py:388
  21.5 5.2 %collective-permute-start.2 = (s32[512]{0:T(512)S(1)}, s32[512]{0:T(512)S(1)}, u32[]{:S(2)}, u32[]{:S(2)}) collective-permute-start(s32[512]{0:T(512)S(1)} %get-tuple-element.84), channel_id=1, source_target_pairs={{0,12},{4,8},{8,4},{12,0},{16,28},{20,24},{24,20},{28,16},{1,13},{... | collective-permute-start | bytes 6152 | tf_op jit(solution)/shard_map/ppermute | solution.py:388
  26.7 2.7 %collective-permute-start.3 = (s32[512]{0:T(512)S(1)}, s32[512]{0:T(512)S(1)}, u32[]{:S(2)}, u32[]{:S(2)}) collective-permute-start(s32[512]{0:T(512)S(1)} %get-tuple-element.83), channel_id=1, source_target_pairs={{0,16},{4,20},{8,24},{12,28},{16,0},{20,4},{24,8},{28,12},{1,17},{... | collective-permute-start | bytes 6152 | tf_op jit(solution)/shard_map/ppermute | solution.py:388
  29.4 4.4 %collective-permute-start.4 = (s32[512]{0:T(512)S(1)}, s32[512]{0:T(512)S(1)}, u32[]{:S(2)}, u32[]{:S(2)}) collective-permute-start(s32[512]{0:T(512)S(1)} %get-tuple-element.82), channel_id=1, source_target_pairs={{0,20},{4,16},{8,28},{12,24},{16,4},{20,0},{24,12},{28,8},{1,21},{... | collective-permute-start | bytes 6152 | tf_op jit(solution)/shard_map/ppermute | solution.py:388
  31.7 17.9 %collective-permute-start.12 = (bf16[4,128,512]{2,1,0:T(8,128)(2,1)S(1)}, bf16[4,128,512]{2,1,0:T(8,128)(2,1)S(1)}, u32[]{:S(2)}, u32[]{:S(2)}) collective-permute-start(bf16[4,128,512]{2,1,0:T(8,128)(2,1)S(1)} %collective-permute-done.10.refs_9_), channel_id=1, source_target_pairs={{1,0},{5,4},{9,8},{13,12},{17,16},{21,20},{25,24},{29,28}} | collective-permute-start | bytes 1572872 | tf_op jit(solution)/shard_map/ppermute | solution.py:398
  33.1 16.5 %collective-permute-start.11 = (bf16[4,128,512]{2,1,0:T(8,128)(2,1)S(1)}, bf16[4,128,512]{2,1,0:T(8,128)(2,1)S(1)}, u32[]{:S(2)}, u32[]{:S(2)}) collective-permute-start(bf16[4,128,512]{2,1,0:T(8,128)(2,1)S(1)} %collective-permute-done.9.refs_8_), channel_id=1, source_target_pairs={{2,3},{6,7},{10,11},{14,15},{18,19},{22,23},{26,27},{30,31}} | collective-permute-start | bytes 1572872 | tf_op jit(solution)/shard_map/ppermute | solution.py:397
  58.1 4.1 %collective-permute-start.13 = (bf16[512,128]{1,0:T(8,128)(2,1)}, bf16[512,128]{1,0:T(8,128)(2,1)S(1)}, u32[]{:S(2)}, u32[]{:S(2)}) collective-permute-start(bf16[512,128]{1,0:T(8,128)(2,1)} %get-tuple-element.39), channel_id=1, source_target_pairs={{0,4},{4,0},{8,12},{12,8},{16,20},{20,16},{24,28},{28,24},{1,5},{5... | collective-permute-start | bytes 393224 | tf_op jit(solution)/shard_map/ppermute | solution.py:388
  58.2 6.0 %collective-permute-start.14 = (bf16[512,128]{1,0:T(8,128)(2,1)}, bf16[512,128]{1,0:T(8,128)(2,1)S(1)}, u32[]{:S(2)}, u32[]{:S(2)}) collective-permute-start(bf16[512,128]{1,0:T(8,128)(2,1)} %get-tuple-element.40), channel_id=1, source_target_pairs={{0,8},{4,12},{8,0},{12,4},{16,24},{20,28},{24,16},{28,20},{1,9},{5... | collective-permute-start | bytes 393224 | tf_op jit(solution)/shard_map/ppermute | solution.py:388
  59.7 28.8 %collective-permute-start.15 = (bf16[512,128]{1,0:T(8,128)(2,1)}, bf16[512,128]{1,0:T(8,128)(2,1)S(1)}, u32[]{:S(2)}, u32[]{:S(2)}) collective-permute-start(bf16[512,128]{1,0:T(8,128)(2,1)} %get-tuple-element.41), channel_id=1, source_target_pairs={{0,12},{4,8},{8,4},{12,0},{16,28},{20,24},{24,20},{28,16},{1,13},{... | collective-permute-start | bytes 393224 | tf_op jit(solution)/shard_map/ppermute | solution.py:388
  60.3 28.2 %collective-permute-start.16 = (bf16[512,128]{1,0:T(8,128)(2,1)}, bf16[512,128]{1,0:T(8,128)(2,1)S(1)}, u32[]{:S(2)}, u32[]{:S(2)}) collective-permute-start(bf16[512,128]{1,0:T(8,128)(2,1)} %get-tuple-element.42), channel_id=1, source_target_pairs={{0,16},{4,20},{8,24},{12,28},{16,0},{20,4},{24,8},{28,12},{1,17},{... | collective-permute-start | bytes 393224 | tf_op jit(solution)/shard_map/ppermute | solution.py:388
  62.1 26.4 %collective-permute-start.17 = (bf16[512,128]{1,0:T(8,128)(2,1)}, bf16[512,128]{1,0:T(8,128)(2,1)S(1)}, u32[]{:S(2)}, u32[]{:S(2)}) collective-permute-start(bf16[512,128]{1,0:T(8,128)(2,1)} %get-tuple-element.43), channel_id=1, source_target_pairs={{0,20},{4,16},{8,28},{12,24},{16,4},{20,0},{24,12},{28,8},{1,21},{... | collective-permute-start | bytes 393224 | tf_op jit(solution)/shard_map/ppermute | solution.py:388
  62.2 26.4 %copy-start.7 = (bf16[512,128]{1,0:T(8,128)(2,1)}, bf16[512,128]{1,0:T(8,128)(2,1)S(1)}, u32[]{:S(2)}) copy-start(bf16[512,128]{1,0:T(8,128)(2,1)S(1)} %collective-permute-done.13.refs_1_) | copy-start | bytes 393220
  62.2 26.3 %collective-permute-start.18 = (bf16[512,128]{1,0:T(8,128)(2,1)}, bf16[512,128]{1,0:T(8,128)(2,1)S(1)}, u32[]{:S(2)}, u32[]{:S(2)}) collective-permute-start(bf16[512,128]{1,0:T(8,128)(2,1)} %get-tuple-element.44), channel_id=1, source_target_pairs={{0,24},{4,28},{8,16},{12,20},{16,8},{20,12},{24,0},{28,4},{1,25},{... | collective-permute-start | bytes 393224 | tf_op jit(solution)/shard_map/ppermute | solution.py:388
  64.2 24.4 %copy-start.8 = (bf16[512,128]{1,0:T(8,128)(2,1)}, bf16[512,128]{1,0:T(8,128)(2,1)S(1)}, u32[]{:S(2)}) copy-start(bf16[512,128]{1,0:T(8,128)(2,1)S(1)} %collective-permute-done.14.refs_2_) | copy-start | bytes 393220
  64.2 24.4 %collective-permute-start.19 = (bf16[512,128]{1,0:T(8,128)(2,1)}, bf16[512,128]{1,0:T(8,128)(2,1)S(1)}, u32[]{:S(2)}, u32[]{:S(2)}) collective-permute-start(bf16[512,128]{1,0:T(8,128)(2,1)} %get-tuple-element.45), channel_id=1, source_target_pairs={{0,28},{4,24},{8,20},{12,16},{16,12},{20,8},{24,4},{28,0},{1,29},{... | collective-permute-start | bytes 393224 | tf_op jit(solution)/shard_map/ppermute | solution.py:388
  104.1 3.6 %collective-permute-start.20 = (bf16[512,128]{1,0:T(8,128)(2,1)}, bf16[512,128]{1,0:T(8,128)(2,1)S(1)}, u32[]{:S(2)}, u32[]{:S(2)}) collective-permute-start(bf16[512,128]{1,0:T(8,128)(2,1)} %get-tuple-element.49), channel_id=1, source_target_pairs={{0,4},{4,0},{8,12},{12,8},{16,20},{20,16},{24,28},{28,24},{1,5},{5... | collective-permute-start | bytes 393224 | tf_op jit(solution)/shard_map/ppermute | solution.py:388
  104.2 4.9 %collective-permute-start.21 = (bf16[512,128]{1,0:T(8,128)(2,1)}, bf16[512,128]{1,0:T(8,128)(2,1)S(1)}, u32[]{:S(2)}, u32[]{:S(2)}) collective-permute-start(bf16[512,128]{1,0:T(8,128)(2,1)} %get-tuple-element.50), channel_id=1, source_target_pairs={{0,8},{4,12},{8,0},{12,4},{16,24},{20,28},{24,16},{28,20},{1,9},{5... | collective-permute-start | bytes 393224 | tf_op jit(solution)/shard_map/ppermute | solution.py:388
  105.3 8.4 %collective-permute-start.22 = (bf16[512,128]{1,0:T(8,128)(2,1)}, bf16[512,128]{1,0:T(8,128)(2,1)S(1)}, u32[]{:S(2)}, u32[]{:S(2)}) collective-permute-start(bf16[512,128]{1,0:T(8,128)(2,1)} %get-tuple-element.51), channel_id=1, source_target_pairs={{0,12},{4,8},{8,4},{12,0},{16,28},{20,24},{24,20},{28,16},{1,13},{... | collective-permute-start | bytes 393224 | tf_op jit(solution)/shard_map/ppermute | solution.py:388
  106.4 7.3 %collective-permute-start.23 = (bf16[512,128]{1,0:T(8,128)(2,1)}, bf16[512,128]{1,0:T(8,128)(2,1)S(1)}, u32[]{:S(2)}, u32[]{:S(2)}) collective-permute-start(bf16[512,128]{1,0:T(8,128)(2,1)} %get-tuple-element.52), channel_id=1, source_target_pairs={{0,16},{4,20},{8,24},{12,28},{16,0},{20,4},{24,8},{28,12},{1,17},{... | collective-permute-start | bytes 393224 | tf_op jit(solution)/shard_map/ppermute | solution.py:388
  107.0 13.2 %collective-permute-start.24 = (bf16[512,128]{1,0:T(8,128)(2,1)}, bf16[512,128]{1,0:T(8,128)(2,1)S(1)}, u32[]{:S(2)}, u32[]{:S(2)}) collective-permute-start(bf16[512,128]{1,0:T(8,128)(2,1)} %get-tuple-element.53), channel_id=1, source_target_pairs={{0,20},{4,16},{8,28},{12,24},{16,4},{20,0},{24,12},{28,8},{1,21},{... | collective-permute-start | bytes 393224 | tf_op jit(solution)/shard_map/ppermute | solution.py:388
  107.8 12.5 %collective-permute-start.25 = (bf16[512,128]{1,0:T(8,128)(2,1)}, bf16[512,128]{1,0:T(8,128)(2,1)S(1)}, u32[]{:S(2)}, u32[]{:S(2)}) collective-permute-start(bf16[512,128]{1,0:T(8,128)(2,1)} %get-tuple-element.54), channel_id=1, source_target_pairs={{0,24},{4,28},{8,16},{12,20},{16,8},{20,12},{24,0},{28,4},{1,25},{... | collective-permute-start | bytes 393224 | tf_op jit(solution)/shard_map/ppermute | solution.py:388
  109.1 11.1 %collective-permute-start.26 = (bf16[512,128]{1,0:T(8,128)(2,1)}, bf16[512,128]{1,0:T(8,128)(2,1)S(1)}, u32[]{:S(2)}, u32[]{:S(2)}) collective-permute-start(bf16[512,128]{1,0:T(8,128)(2,1)} %get-tuple-element.55), channel_id=1, source_target_pairs={{0,28},{4,24},{8,20},{12,16},{16,12},{20,8},{24,4},{28,0},{1,29},{... | collective-permute-start | bytes 393224 | tf_op jit(solution)/shard_map/ppermute | solution.py:388
  132.8 4.2 %collective-permute-start.27 = (bf16[512,128]{1,0:T(8,128)(2,1)}, bf16[512,128]{1,0:T(8,128)(2,1)S(1)}, u32[]{:S(2)}, u32[]{:S(2)}) collective-permute-start(bf16[512,128]{1,0:T(8,128)(2,1)} %get-tuple-element.58), channel_id=1, source_target_pairs={{0,4},{4,0},{8,12},{12,8},{16,20},{20,16},{24,28},{28,24},{1,5},{5... | collective-permute-start | bytes 393224 | tf_op jit(solution)/shard_map/ppermute | solution.py:388
  132.9 5.5 %collective-permute-start.28 = (bf16[512,128]{1,0:T(8,128)(2,1)}, bf16[512,128]{1,0:T(8,128)(2,1)S(1)}, u32[]{:S(2)}, u32[]{:S(2)}) collective-permute-start(bf16[512,128]{1,0:T(8,128)(2,1)} %get-tuple-element.59), channel_id=1, source_target_pairs={{0,8},{4,12},{8,0},{12,4},{16,24},{20,28},{24,16},{28,20},{1,9},{5... | collective-permute-start | bytes 393224 | tf_op jit(solution)/shard_map/ppermute | solution.py:388
  134.7 7.6 %collective-permute-start.29 = (bf16[512,128]{1,0:T(8,128)(2,1)}, bf16[512,128]{1,0:T(8,128)(2,1)S(1)}, u32[]{:S(2)}, u32[]{:S(2)}) collective-permute-start(bf16[512,128]{1,0:T(8,128)(2,1)} %get-tuple-element.60), channel_id=1, source_target_pairs={{0,12},{4,8},{8,4},{12,0},{16,28},{20,24},{24,20},{28,16},{1,13},{... | collective-permute-start | bytes 393224 | tf_op jit(solution)/shard_map/ppermute | solution.py:388
  135.0 7.3 %collective-permute-start.30 = (bf16[512,128]{1,0:T(8,128)(2,1)}, bf16[512,128]{1,0:T(8,128)(2,1)S(1)}, u32[]{:S(2)}, u32[]{:S(2)}) collective-permute-start(bf16[512,128]{1,0:T(8,128)(2,1)} %get-tuple-element.61), channel_id=1, source_target_pairs={{0,16},{4,20},{8,24},{12,28},{16,0},{20,4},{24,8},{28,12},{1,17},{... | collective-permute-start | bytes 393224 | tf_op jit(solution)/shard_map/ppermute | solution.py:388
  136.7 12.4 %collective-permute-start.31 = (bf16[512,128]{1,0:T(8,128)(2,1)}, bf16[512,128]{1,0:T(8,128)(2,1)S(1)}, u32[]{:S(2)}, u32[]{:S(2)}) collective-permute-start(bf16[512,128]{1,0:T(8,128)(2,1)} %get-tuple-element.62), channel_id=1, source_target_pairs={{0,20},{4,16},{8,28},{12,24},{16,4},{20,0},{24,12},{28,8},{1,21},{... | collective-permute-start | bytes 393224 | tf_op jit(solution)/shard_map/ppermute | solution.py:388
  137.0 12.1 %collective-permute-start.32 = (bf16[512,128]{1,0:T(8,128)(2,1)}, bf16[512,128]{1,0:T(8,128)(2,1)S(1)}, u32[]{:S(2)}, u32[]{:S(2)}) collective-permute-start(bf16[512,128]{1,0:T(8,128)(2,1)} %get-tuple-element.63), channel_id=1, source_target_pairs={{0,24},{4,28},{8,16},{12,20},{16,8},{20,12},{24,0},{28,4},{1,25},{... | collective-permute-start | bytes 393224 | tf_op jit(solution)/shard_map/ppermute | solution.py:388
  138.4 10.8 %collective-permute-start.33 = (bf16[512,128]{1,0:T(8,128)(2,1)}, bf16[512,128]{1,0:T(8,128)(2,1)S(1)}, u32[]{:S(2)}, u32[]{:S(2)}) collective-permute-start(bf16[512,128]{1,0:T(8,128)(2,1)} %get-tuple-element.64), channel_id=1, source_target_pairs={{0,28},{4,24},{8,20},{12,16},{16,12},{20,8},{24,4},{28,0},{1,29},{... | collective-permute-start | bytes 393224 | tf_op jit(solution)/shard_map/ppermute | solution.py:388
  164.8 4.1 %collective-permute-start.34 = (bf16[512,128]{1,0:T(8,128)(2,1)}, bf16[512,128]{1,0:T(8,128)(2,1)S(1)}, u32[]{:S(2)}, u32[]{:S(2)}) collective-permute-start(bf16[512,128]{1,0:T(8,128)(2,1)} %get-tuple-element.66), channel_id=1, source_target_pairs={{0,4},{4,0},{8,12},{12,8},{16,20},{20,16},{24,28},{28,24},{1,5},{5... | collective-permute-start | bytes 393224 | tf_op jit(solution)/shard_map/ppermute | solution.py:388
  164.9 5.7 %collective-permute-start.35 = (bf16[512,128]{1,0:T(8,128)(2,1)}, bf16[512,128]{1,0:T(8,128)(2,1)S(1)}, u32[]{:S(2)}, u32[]{:S(2)}) collective-permute-start(bf16[512,128]{1,0:T(8,128)(2,1)} %get-tuple-element.67), channel_id=1, source_target_pairs={{0,8},{4,12},{8,0},{12,4},{16,24},{20,28},{24,16},{28,20},{1,9},{5... | collective-permute-start | bytes 393224 | tf_op jit(solution)/shard_map/ppermute | solution.py:388
  166.7 8.0 %collective-permute-start.36 = (bf16[512,128]{1,0:T(8,128)(2,1)}, bf16[512,128]{1,0:T(8,128)(2,1)S(1)}, u32[]{:S(2)}, u32[]{:S(2)}) collective-permute-start(bf16[512,128]{1,0:T(8,128)(2,1)} %get-tuple-element.68), channel_id=1, source_target_pairs={{0,12},{4,8},{8,4},{12,0},{16,28},{20,24},{24,20},{28,16},{1,13},{... | collective-permute-start | bytes 393224 | tf_op jit(solution)/shard_map/ppermute | solution.py:388
  167.0 7.8 %collective-permute-start.37 = (bf16[512,128]{1,0:T(8,128)(2,1)}, bf16[512,128]{1,0:T(8,128)(2,1)S(1)}, u32[]{:S(2)}, u32[]{:S(2)}) collective-permute-start(bf16[512,128]{1,0:T(8,128)(2,1)} %get-tuple-element.69), channel_id=1, source_target_pairs={{0,16},{4,20},{8,24},{12,28},{16,0},{20,4},{24,8},{28,12},{1,17},{... | collective-permute-start | bytes 393224 | tf_op jit(solution)/shard_map/ppermute | solution.py:388
  168.5 12.4 %collective-permute-start.38 = (bf16[512,128]{1,0:T(8,128)(2,1)}, bf16[512,128]{1,0:T(8,128)(2,1)S(1)}, u32[]{:S(2)}, u32[]{:S(2)}) collective-permute-start(bf16[512,128]{1,0:T(8,128)(2,1)} %get-tuple-element.70), channel_id=1, source_target_pairs={{0,20},{4,16},{8,28},{12,24},{16,4},{20,0},{24,12},{28,8},{1,21},{... | collective-permute-start | bytes 393224 | tf_op jit(solution)/shard_map/ppermute | solution.py:388
  168.8 12.0 %collective-permute-start.39 = (bf16[512,128]{1,0:T(8,128)(2,1)}, bf16[512,128]{1,0:T(8,128)(2,1)S(1)}, u32[]{:S(2)}, u32[]{:S(2)}) collective-permute-start(bf16[512,128]{1,0:T(8,128)(2,1)} %get-tuple-element.71), channel_id=1, source_target_pairs={{0,24},{4,28},{8,16},{12,20},{16,8},{20,12},{24,0},{28,4},{1,25},{... | collective-permute-start | bytes 393224 | tf_op jit(solution)/shard_map/ppermute | solution.py:388
  170.6 10.3 %collective-permute-start.40 = (bf16[512,128]{1,0:T(8,128)(2,1)}, bf16[512,128]{1,0:T(8,128)(2,1)S(1)}, u32[]{:S(2)}, u32[]{:S(2)}) collective-permute-start(bf16[512,128]{1,0:T(8,128)(2,1)} %get-tuple-element.72), channel_id=1, source_target_pairs={{0,28},{4,24},{8,20},{12,16},{16,12},{20,8},{24,4},{28,0},{1,29},{... | collective-permute-start | bytes 393224 | tf_op jit(solution)/shard_map/ppermute | solution.py:388
  (32 other events, 186.8 us)

commit v3 on v2

v3 whole, which is shorter than its diff:
```python
import functools

import jax
import jax.numpy as jnp
from jax import lax
from jax.experimental import pallas as pl
from jax.experimental.pallas import tpu as pltpu
from jax.sharding import PartitionSpec as P

SRC_GROUP = 128
ITERS = 2
STREAMS = 4
STEP = 16
BETA = 2.0
RIDGE = 1.0
VMEM_LIMIT = 36 * 1024 * 1024
BASIS_CALLS = 4
CHUNKS = 2
UNROLL = 16

COS_POLY = (1.0, -19.73920440673828, 64.9391098022461, -85.4500503540039, 60.16689682006836,
            -25.96480369567871, 6.52468729019165)
SIN_POLY = (6.283185005187988, -41.34158706665039, 81.59986114501953, -76.61351013183594,
            41.33811950683594, -12.463061332702637)

VMEM = pl.BlockSpec(memory_space=pltpu.VMEM)
SMEM = pl.BlockSpec(memory_space=pltpu.SMEM)


def horner(poly, v):
    acc = jnp.full_like(v, poly[-1])
    for term in poly[-2::-1]:
        acc = acc * v + term
    return acc


def basis_kernel(time_ref, period_ref, inverse_ref, basis_ref, norm_ref):
    obs = time_ref.shape[0]
    nper = period_ref.shape[1]
    rows = 32
    for chunk in range(nper // 128):
        lanes = pl.ds(chunk * 128, 128)
        sines = pl.ds(nper + chunk * 128, 128)
        period = period_ref[:, lanes]
        inverse = inverse_ref[:, lanes]

        def step(index, sums):
            at = pl.ds(pl.multiple_of(index * rows, rows), rows)
            time = time_ref[at, :]
            turns = jnp.round(time * inverse)
            part = (time - turns * period) * inverse
            square = part * part
            cosine = horner(COS_POLY, square).astype(jnp.bfloat16)
            sine = (horner(SIN_POLY, square) * part).astype(jnp.bfloat16)
            basis_ref[0, at, lanes] = cosine
            basis_ref[0, at, sines] = sine
            cosine = cosine.astype(jnp.float32)
            sine = sine.astype(jnp.float32)
            return (
                sums[0] + jnp.sum((cosine * cosine).reshape(rows // 8, 8, 128), axis=0),
                sums[1] + jnp.sum((sine * sine).reshape(rows // 8, 8, 128), axis=0),
            )

        zero = jnp.zeros((8, 128), jnp.float32)
        total_c, total_s = lax.fori_loop(0, obs // rows, step, (zero, zero))
        norm_ref[0, :, lanes] = 1.0 / (jnp.sum(total_c, axis=0, keepdims=True) + RIDGE)
        norm_ref[0, :, sines] = 1.0 / (jnp.sum(total_s, axis=0, keepdims=True) + RIDGE)


def make_basis(times, periods):
    sched_dev, obs = times.shape
    nper = periods.shape[0]
    wide = jnp.broadcast_to(
        times.astype(jnp.float32).reshape(-1, 1), (sched_dev * obs, SRC_GROUP)
    )
    period = periods.astype(jnp.float32)[None, :]
    return pl.pallas_call(
        basis_kernel,
        grid=(sched_dev,),
        in_specs=[
            pl.BlockSpec((obs, SRC_GROUP), lambda j: (j, 0)),
            pl.BlockSpec((1, nper), lambda j: (0, 0)),
            pl.BlockSpec((1, nper), lambda j: (0, 0)),
        ],
        out_specs=[
            pl.BlockSpec((1, obs, 2 * nper), lambda j: (j, 0, 0)),
            pl.BlockSpec((1, 1, 2 * nper), lambda j: (j, 0, 0)),
        ],
        out_shape=[
            jax.ShapeDtypeStruct((sched_dev, obs, 2 * nper), jnp.bfloat16),
            jax.ShapeDtypeStruct((sched_dev, 1, 2 * nper), jnp.float32),
        ],
        compiler_params=pltpu.CompilerParams(vmem_limit_bytes=VMEM_LIMIT),
        cost_estimate=pl.CostEstimate(
            flops=sched_dev * obs * nper * 10000, bytes_accessed=sched_dev * obs * nper * 4, transcendentals=0
        ),
    )(wide, period, 1.0 / period)


def fit_kernel(tm_count, src_ref, dst_ref, *refs):
    refs = list(refs)

    def take(count):
        taken = refs[:count]
        del refs[:count]
        return taken

    arrived = take(tm_count)
    parts = take(BASIS_CALLS)
    (norm_ref,) = take(1)
    outs = take(tm_count)
    score_ref, basis_ref, sems, rows_ref, back_ref = take(5)
    slots = [take(4), take(4)]
    plans, obs, twice = basis_ref.shape
    nper = twice // 2
    capacity, width = arrived[0].shape
    spaced = capacity + STEP
    steps = src_ref.shape[1]
    each = plans // len(parts)

    def basis_copy(plan):
        return pltpu.make_async_copy(parts[plan // each].at[plan % each], basis_ref.at[plan], sems.at[plan])

    for plan in range(plans):
        basis_copy(plan).start()
    for owner in range(tm_count):
        rows_ref[pl.ds(owner * spaced, capacity), :] = arrived[owner][...].astype(jnp.float32)

    def correlate(plan, obs_ref, corr_ref):
        for step in range(steps):
            obs_ref[pl.ds(dst_ref[plan, step], STEP), :] = rows_ref[pl.ds(src_ref[plan, step], STEP), :]
        corr_ref[...] = lax.dot_general(
            obs_ref[:obs, :].astype(jnp.bfloat16), basis_ref[plan], (((0,), (0,)), ((), ())),
            preferred_element_type=jnp.float32,
        )

    def finish(plan, corr_ref, coeff_ref, model_ref):
        group = 16
        for start in range(0, width, group):
            at = pl.ds(start, group)
            power = []
            for chunk in range(nper // 128):
                lanes = pl.ds(chunk * 128, 128)
                sines = pl.ds(nper + chunk * 128, 128)
                cosine = corr_ref[at, lanes]
                sine = corr_ref[at, sines]
                power.append(
                    cosine * (cosine * norm_ref[plan, :, lanes]) + sine * (sine * norm_ref[plan, :, sines])
                )
            highest = functools.reduce(jnp.maximum, power)
            highest = jnp.max(highest, axis=1, keepdims=True)
            expo = [jnp.exp(BETA * (value - highest)) for value in power]
            total = jnp.sum(functools.reduce(jnp.add, expo), axis=1, keepdims=True)
            scale = 1.0 / total
            for chunk in range(nper // 128):
                lanes = pl.ds(chunk * 128, 128)
                sines = pl.ds(nper + chunk * 128, 128)
                share = expo[chunk] * scale
                coeff_ref[at, lanes] = (share * (corr_ref[at, lanes] * norm_ref[plan, :, lanes])).astype(jnp.bfloat16)
                coeff_ref[at, sines] = (share * (corr_ref[at, sines] * norm_ref[plan, :, sines])).astype(jnp.bfloat16)
            score_ref[plan, at, :] = BETA * highest + jnp.log(total)
        model_ref[:obs, :] = lax.dot_general(
            basis_ref[plan], coeff_ref[...], (((1,), (1,)), ((), ())), preferred_element_type=jnp.float32
        )
        for step in range(steps):
            back_ref[pl.ds(src_ref[plan, step], STEP), :] = model_ref[pl.ds(dst_ref[plan, step], STEP), :]

    basis_copy(0).wait()
    correlate(0, slots[0][0], slots[0][1])

    def pair(index, carry):
        plan = index * 2
        for ahead in (1, 2):
            for known in range(ahead, plans, 2):
                pl.when(plan + ahead == known)(basis_copy(known).wait)
        correlate(plan + 1, slots[1][0], slots[1][1])
        finish(plan, *slots[0][1:])
        correlate(jnp.minimum(plan + 2, plans - 1), slots[0][0], slots[0][1])
        finish(plan + 1, *slots[1][1:])
        return carry

    lax.fori_loop(0, plans // 2, pair, 0)
    for owner in range(tm_count):
        outs[owner][...] = back_ref[pl.ds(owner * spaced, capacity), :].astype(jnp.bfloat16)


def fit_plans(tables, arrived, parts, norms):
    tm_count = len(arrived)
    each, obs, twice = parts[0].shape
    sched_dev = each * len(parts)
    capacity, width = arrived[0].shape
    work = sched_dev * obs * twice * width
    spaced = tm_count * (capacity + STEP) + STEP
    slot = [
        pltpu.VMEM((obs + STEP, width), jnp.float32),
        pltpu.VMEM((width, twice), jnp.float32),
        pltpu.VMEM((width, twice), jnp.bfloat16),
        pltpu.VMEM((obs + STEP, width), jnp.float32),
    ]
    *models, score = pl.pallas_call(
        functools.partial(fit_kernel, tm_count),
        in_specs=[SMEM, SMEM] + [VMEM] * tm_count + [pl.BlockSpec(memory_space=pl.ANY)] * len(parts) + [VMEM],
        out_specs=[VMEM] * (tm_count + 1),
        out_shape=[jax.ShapeDtypeStruct((capacity, width), jnp.bfloat16)] * tm_count
        + [jax.ShapeDtypeStruct((sched_dev, width, 1), jnp.float32)],
        scratch_shapes=[
            pltpu.VMEM((sched_dev, obs, twice), jnp.bfloat16),
            pltpu.SemaphoreType.DMA((sched_dev,)),
            pltpu.VMEM((spaced, width), jnp.float32),
            pltpu.VMEM((spaced, width), jnp.float32),
        ] + slot + slot,
        compiler_params=pltpu.CompilerParams(vmem_limit_bytes=VMEM_LIMIT),
        cost_estimate=pl.CostEstimate(flops=20 * work, bytes_accessed=sched_dev * obs * twice * 2, transcendentals=0),
    )(*tables, *arrived, *parts, norms)
    return models, score


def load_attitude(sky, own_ref, chunks, whole_ref, sems):
    rows = own_ref.shape[1]
    copies = [(None, sky, slice(None), own_ref)]
    for index, passed in enumerate(chunks):
        count = len(passed) // 2 + 1
        segs = passed[0].shape[0]
        held = pl.ds(index * segs, segs)
        for hop in range(1, count):
            copies.append((sky >= hop, sky - hop, held, passed[2 * hop - 2]))
            copies.append((sky + hop < count, sky + hop, held, passed[2 * hop - 1]))

    def each(act):
        for index, (valid, quarter, held, ref) in enumerate(copies):
            def run(index=index, quarter=quarter, held=held, ref=ref):
                at = pl.ds(pl.multiple_of(quarter * rows, rows), rows)
                act(pltpu.make_async_copy(ref, whole_ref.at[held, at, :], sems.at[index]))

            if valid is None:
                run()
            else:
                pl.when(valid)(run)

    each(lambda copy: copy.start())
    return lambda: each(lambda copy: copy.wait())


def whiten_and_pick(me, asked_ref, cnt_ref, count_ref, whole_ref, load, picked, white_ref, gather_ref):
    segs, slots, _ = whole_ref.shape
    capacity, width = picked[0].shape
    blocks = white_ref.shape[0] // (segs * slots)
    row = lax.broadcasted_iota(jnp.int32, (slots, width * blocks), 0)
    for seg in range(segs):
        masked = jnp.where(row < count_ref[seg], load(seg).astype(jnp.float32), 0.0).astype(jnp.bfloat16)
        white = jnp.dot(whole_ref[seg], masked, preferred_element_type=jnp.float32)
        for block in range(blocks):
            white_ref[pl.ds((block * segs + seg) * slots, slots), :] = white[:, block * width:(block + 1) * width]
    for owner, out_ref in enumerate(picked):
        asker = owner ^ me

        def step(index, carry):
            first = index * UNROLL
            for lane in range(UNROLL):
                gather_ref[pl.ds(owner * capacity + first + lane, 1), :] = white_ref[
                    pl.ds(asked_ref[asker * capacity + first + lane], 1), :
                ]
            return carry

        lax.fori_loop(0, (cnt_ref[asker] + UNROLL - 1) // UNROLL, step, 0)
        out_ref[...] = gather_ref[pl.ds(owner * capacity, capacity), :].astype(jnp.bfloat16)


def place_rows(me, asked_ref, cnt_ref, returned, current_ref, out_ref, rows_ref, sums):
    segs, slots, _ = current_ref.shape
    capacity, width = returned[0].shape
    blocks = current_ref.shape[2] // width
    streams = len(sums)
    for total in sums:
        total[...] = jnp.zeros_like(total)
    for owner, ref in enumerate(returned):
        rows_ref[pl.ds(owner * capacity, capacity), :] = ref[...].astype(jnp.float32)

        asker = owner ^ me

        def step(index, carry):
            first = index * UNROLL
            for start in range(0, UNROLL, streams):
                lanes = [first + start + lane for lane in range(streams)]
                places = [asked_ref[asker * capacity + lane] for lane in lanes]
                values = [
                    total[pl.ds(place, 1), :] + rows_ref[pl.ds(owner * capacity + lane, 1), :]
                    for total, place, lane in zip(sums, places, lanes)
                ]
                for total, place, value in zip(sums, places, values):
                    total[pl.ds(place, 1), :] = value
            return carry

        lax.fori_loop(0, (cnt_ref[asker] + UNROLL - 1) // UNROLL, step, 0)
    for seg in range(segs):
        for block in range(blocks):
            at = pl.ds((block * segs + seg) * slots, slots)
            lanes = slice(block * width, (block + 1) * width)
            placed = functools.reduce(jnp.add, [total[at, :] for total in sums])
            out_ref[seg, :, lanes] = current_ref[seg, :, lanes].astype(jnp.float32) - placed


def owner_kernel(tm_count, chunk_counts, placing, *refs):
    refs = list(refs)

    def take(count):
        taken = refs[:count]
        del refs[:count]
        return taken

    asked_ref, cnt_ref, count_ref, where_ref, _, current_ref = take(6)
    me, sky = where_ref[0], where_ref[1]
    picking = chunk_counts is not None
    if picking:
        (own_ref,) = take(1)
        chunks = [take(count) for count in chunk_counts]
    returned = take(tm_count) if placing else None
    out_ref = take(1)[0] if placing else None
    picked = take(tm_count) if picking else None
    if picking:
        whole_ref, sems, white_ref = take(3)
        wait = load_attitude(sky, own_ref, chunks, whole_ref, sems)
    (rows_ref,) = take(1)
    if placing:
        place_rows(me, asked_ref, cnt_ref, returned, current_ref, out_ref, rows_ref, refs)
    if picking:
        wait()
        source = out_ref if placing else current_ref
        whiten_and_pick(
            me, asked_ref, cnt_ref, count_ref, whole_ref, lambda seg: source[seg], picked, white_ref, rows_ref
        )


def owner_step(scalars, norms, current, attitude, returned):
    asked, cnt, seg_counts, where = scalars
    seg_dev, slots, width = current.shape
    placing, picking = returned is not None, attitude is not None
    tm_count = cnt.shape[0]
    capacity = asked.shape[0] // tm_count
    table = pltpu.VMEM((seg_dev * slots * width // SRC_GROUP + 8, SRC_GROUP), jnp.float32)
    anywhere = pl.BlockSpec(memory_space=pl.ANY)
    in_specs = [SMEM] * 4 + [anywhere, VMEM]
    args = [asked, cnt, seg_counts, where, norms, current]
    out_shape = []
    scratch = []
    counts = None
    if picking:
        own, chunks = attitude
        counts = [len(chunk) for chunk in chunks]
        args += [own] + [piece for chunk in chunks for piece in chunk]
        in_specs += [anywhere] * (1 + sum(counts))
        scratch += [
            pltpu.VMEM((seg_dev, slots, slots), jnp.bfloat16),
            pltpu.SemaphoreType.DMA((1 + sum(counts),)),
            table,
        ]
    scratch.append(pltpu.VMEM((tm_count * capacity, SRC_GROUP), jnp.float32))
    if placing:
        in_specs += [VMEM] * tm_count
        args += returned
        out_shape.append(jax.ShapeDtypeStruct(current.shape, jnp.float32))
        scratch += [table] * STREAMS
    if picking:
        out_shape += [jax.ShapeDtypeStruct((capacity, SRC_GROUP), jnp.bfloat16)] * tm_count
    out = pl.pallas_call(
        functools.partial(owner_kernel, tm_count, counts, placing),
        in_specs=in_specs,
        out_specs=[VMEM] * len(out_shape),
        out_shape=out_shape,
        scratch_shapes=scratch,
        compiler_params=pltpu.CompilerParams(vmem_limit_bytes=VMEM_LIMIT),
        cost_estimate=pl.CostEstimate(
            flops=16 * seg_dev * slots * slots * width, bytes_accessed=16 << 20, transcendentals=0
        ),
    )(*args)
    if placing:
        return out[0], list(out[1:])
    return current, list(out)


def make_lists(sched_seg, sched_slot, seg_dev, slots, column_blocks, tm_count, capacity):
    sched_dev, obs = sched_seg.shape
    me = lax.axis_index("tm")
    owner = sched_seg // seg_dev
    partner = owner ^ me
    block_of = (jnp.arange(sched_dev, dtype=jnp.int32) % column_blocks)[:, None]
    local_row = (block_of * seg_dev + sched_seg % seg_dev) * slots + sched_slot
    hot = (partner[:, :, None] == jnp.arange(tm_count, dtype=jnp.int32)).astype(jnp.int32)
    cnt = jnp.sum(hot, axis=1)
    plans = jnp.arange(sched_dev)
    before = (plans[None, :] < plans[:, None]).astype(jnp.int32)
    src = jnp.sum(before[:, :, None] * cnt[None, :, :], axis=1)
    owners = jnp.arange(tm_count)
    ahead = (owners[None, :] < owners[:, None]).astype(jnp.int32)
    dst = jnp.sum(ahead[None, :, :] * cnt[:, None, :], axis=2)
    entry = jnp.arange(obs)
    rank = jnp.sum(
        ((partner[:, None, :] == partner[:, :, None]) & (entry[None, :] < entry[:, None])).astype(jnp.int32),
        axis=2,
    )
    place = owner * capacity + jnp.sum(hot * src[:, None, :], axis=2) + rank
    order = jnp.sum(hot * dst[:, None, :], axis=2) + rank
    time = sched_seg * slots + sched_slot
    times = jnp.sum(jnp.where(order[:, None, :] == entry[None, :, None], time[:, None, :], 0), axis=2)
    rows = seg_dev * slots * column_blocks
    wanted = rows + jnp.sum(
        jnp.where(
            place.reshape(1, -1) == jnp.arange(tm_count * capacity, dtype=jnp.int32)[:, None],
            local_row.reshape(1, -1) - rows,
            0,
        ),
        axis=1,
    )
    step_count = (cnt + STEP - 1) // STEP
    step_first = jnp.sum(ahead[None, :, :] * step_count[:, None, :], axis=2)
    step = jnp.arange(obs // STEP + tm_count)[None, :, None] - step_first[:, None, :]
    inside = (step >= 0) & (step < step_count[:, None, :])
    spaced = capacity + STEP
    end = tm_count * spaced
    step_src = end + jnp.sum(
        jnp.where(inside, owners * spaced - end + src[:, None, :] + step * STEP, 0), axis=2
    )
    step_dst = obs + jnp.sum(jnp.where(inside, dst[:, None, :] + step * STEP - obs, 0), axis=2)
    return (step_src, step_dst), times, wanted


def exchange(blocks):
    count = len(blocks)
    out = list(blocks)
    for step in sorted(range(1, count), key=lambda step: -bin(step // 2).count("1")):
        out[step] = lax.ppermute(blocks[step], "tm", [(i, i ^ step) for i in range(count)])
    return out


def pass_along(attitude):
    count = lax.axis_size("sky")
    part = attitude.shape[0] // CHUNKS
    right = [attitude[index * part:(index + 1) * part] for index in range(CHUNKS)]
    left = list(right)
    chunks = [[] for _ in range(CHUNKS)]
    for hop in range(1, count):
        for index in range(CHUNKS):
            right[index] = lax.ppermute(right[index], "sky", [(i, i + 1) for i in range(hop - 1, count - 1)])
            left[index] = lax.ppermute(left[index], "sky", [(i, i - 1) for i in range(1, count - hop + 1)])
            chunks[index] += [right[index], left[index]]
    return attitude, chunks


def on_device(residuals, seg_counts, attitude, sched_seg, sched_slot, periods):
    tm_count = lax.axis_size("tm")
    sched_dev, obs = sched_seg.shape
    seg_dev, slots, width = residuals.shape
    column_blocks = width // SRC_GROUP
    capacity = 2 * sched_dev * obs // tm_count
    pieces = pass_along(attitude)
    tables, times, wanted = make_lists(
        sched_seg, sched_slot, seg_dev, slots, column_blocks, tm_count, capacity
    )
    asked = lax.all_to_all(wanted.reshape(tm_count, capacity), "tm", split_axis=0, concat_axis=0, tiled=True)
    cnt = jnp.sum((asked < seg_dev * slots * column_blocks).astype(jnp.int32), axis=1)
    part = sched_dev // BASIS_CALLS
    parts, norms = zip(
        *[make_basis(times[index * part:(index + 1) * part], periods) for index in range(BASIS_CALLS)]
    )
    norms = jnp.concatenate(norms)
    where = jnp.stack([lax.axis_index("tm"), lax.axis_index("sky")])
    scalars = (asked.reshape(-1), cnt, seg_counts, where)

    current, returned = residuals, None
    for iteration in range(ITERS):
        current, picked = owner_step(scalars, norms, current, pieces, returned)
        models, score = fit_plans(tables, exchange(picked), parts, norms)
        returned = exchange(models)
    current, _ = owner_step(scalars, norms, current, None, returned)
    return (current, score.reshape(sched_dev, SRC_GROUP))


def solution(mesh):
    in_specs = (
        P("tm", None, "sky"),
        P("tm"),
        P("tm", "sky", None),
        P(("tm", "sky"), None),
        P(("tm", "sky"), None),
        P(),
    )
    out_specs = (P("tm", None, "sky"), P(("tm", "sky"), None))
    return jax.shard_map(
        on_device, mesh=mesh, in_specs=in_specs, out_specs=out_specs, check_vma=False
    )
```

time: 191 us -> 186 us (0.974)
  Pallas kernels: 75.5 us -> 52.6 us
  starting transfers between devices: 53.6 us -> 61.7 us
  local copies, waits for them, and re-layouts: 5.27 us -> 10.6 us
  waiting for transfers between devices: 44 us -> 48.5 us
    pallas_call x5, Pallas kernels: 56.7 us -> 35.8 us  [the longest x3 19.2 us: owner_step(): pl.pallas_call(functools.partial(owner_kernel, tm_count, counts, placing)...]
    ppermute x6 -> x12, starting transfers between devices: 9.95 us -> 21.2 us  [the longest x6 13.5 us: pass_along(): lax.ppermute(right[index], 'sky', [(i, i + 1) for i in range(hop - 1, cou...]
    ppermute x35 -> x28, starting transfers between devices: 43.6 us -> 34.8 us  [exchange(): lax.ppermute(blocks[step], 'tm', [(i, i ^ step) for i in range(count)])]
    all_to_all x0 -> x1, starting transfers between devices: none -> 5.67 us  [on_device(): lax.all_to_all(wanted.reshape(tm_count, capacity), 'tm', split_axis=0, co...]
    unnamed x87 -> x35, local copies, waits for them, and re-layouts: 3.95 us -> 8.3 us
    ppermute x35 -> x28, waiting for transfers between devices: 28.8 us -> 32.3 us  [exchange(): lax.ppermute(blocks[step], 'tm', [(i, i ^ step) for i in range(count)])]
    pallas_call x1 -> x4, Pallas kernels: 18.8 us -> 16.8 us  [make_basis(): pl.pallas_call(basis_kernel, grid=(sched_dev,), in_specs=[pl.BlockSpec((o...]
    ppermute x6 -> x12, waiting for transfers between devices: 15.2 us -> 16.2 us  [the longest x6 16.2 us: pass_along(): lax.ppermute(left[index], 'sky', [(i, i - 1) for i in range(1, count - ho...]
  transfers between devices with their start and end apart: 41 -> 41, of which waited for: 13 -> 14; matrix products, arithmetic and copies ran while one was open for 6% -> 6% of each run, Pallas kernels for 10% -> 9%
where the time goes in v3:
time: 186 us; the launch traced here: 185 us
  starting transfers between devices  61.7 us (33%)
  Pallas kernels  52.6 us (28%)
  waiting for transfers between devices  48.5 us (26%)
  local copies, waits for them, and re-layouts  10.6 us (6%)
  other arithmetic  9.95 us (5%)
    ppermute x28, starting transfers between devices, exchange(): lax.ppermute(blocks[step], 'tm', [(i, i ^ step) for i in range(count)])  34.8 us
    ppermute x28, waiting for transfers between devices, exchange(): lax.ppermute(blocks[step], 'tm', [(i, i ^ step) for i in range(count)])  32.3 us
    pallas_call x3, Pallas kernels, owner_step(): pl.pallas_call(functools.partial(owner_kernel, tm_count, counts, placing)...  19.2 us
    pallas_call x4, Pallas kernels, make_basis(): pl.pallas_call(basis_kernel, grid=(sched_dev,), in_specs=[pl.BlockSpec((o...  16.8 us
    pallas_call x2, Pallas kernels, fit_plans(): pl.pallas_call(functools.partial(fit_kernel, tm_count), in_specs=[SMEM, S...  16.6 us
    ppermute x6, waiting for transfers between devices, pass_along(): lax.ppermute(left[index], 'sky', [(i, i - 1) for i in range(1, count - ho...  16.2 us
    ppermute x6, starting transfers between devices, pass_along(): lax.ppermute(right[index], 'sky', [(i, i + 1) for i in range(hop - 1, cou...  13.5 us
    unnamed x35, local copies, waits for them, and re-layouts  8.3 us
  transfers between devices with their start and end apart: 41, of which 14 were waited for; matrix products, arithmetic and copies ran while one was open for 6% of the time, Pallas kernels for 9%

profile of v3, /device:TPU:1, one launch (start us, length us, event | category | flops | bytes accessed | tf_op | source)
XLA Modules:
  0.0 184.5 jit_solution(16085531591686445809)
XLA Ops:
  0.6 1.8 fusion.19
  3.7 4.7 %collective-permute-start.6 = (bf16[2,128,512]{2,1,0:T(8,128)(2,1)S(1)}, bf16[2,128,512]{2,1,0:T(8,128)(2,1)S(1)}, u32[]{:S(2)}, u32[]{:S(2)}) collective-permute-start(bf16[2,128,512]{2,1,0:T(8,128)(2,1)S(1)} %get-tuple-element.93), channel_id=1, source_target_pairs={{0,1},{1,2},{2,3},{4,5},{5,6},{6,7},{8,9},{9,10},{10,11},{12,13},{... | collective-permute-start | bytes 786440 | tf_op jit(solution)/shard_map/ppermute | solution.py:443
  8.4 1.3 collective-permute-start.1
  9.7 4.0 %collective-permute-start = (bf16[2,128,512]{2,1,0:T(8,128)(2,1)}, bf16[2,128,512]{2,1,0:T(8,128)(2,1)S(1)}, u32[]{:S(2)}, u32[]{:S(2)}) collective-permute-start(bf16[2,128,512]{2,1,0:T(8,128)(2,1)} %get-tuple-element.94), channel_id=1, source_target_pairs={{0,1},{1,2},{2,3},{4,5},{5,6},{6,7},{8,9},{9,10},{10,11},{12,13},{... | collective-permute-start | bytes 786440 | tf_op jit(solution)/shard_map/ppermute | solution.py:443
  16.8 3.4 %select_reduce_fusion = s32[4096]{0:T(1024)S(1)} fusion(s32[2048]{0:T(1024)S(1)} %bitcast.40, s32[2048]{0:T(1024)S(1)} %bitcast.39), kind=kLoop, calls=%fused_computation | loop fusion | flops 25161728 | bytes 32768 | tf_op jit(solution)/shard_map/reduce_sum | solution.py:406
  20.8 5.7 %all-to-all-start = ((s32[8,1,512]{2,1,0:T(1,128)}), s32[8,1,512]{2,1,0:T(1,128)S(1)}, u32[]{:S(2)}, u32[]{:S(2)}) async-start(s32[8,1,512]{2,1,0:T(1,128)} %bitcast), calls=%async_computation | async-start | bytes 32768 | tf_op jit(solution)/shard_map/all_to_all | solution.py:459
  28.5 4.2 %shard_map.80 = (bf16[2,256,2048]{2,1,0:T(8,128)(2,1)S(1)}, f32[2,1,2048]{2,1,0:T(1,128)S(1)}) custom-call(f32[512,128]{1,0:T(8,128)S(1)} %broadcast_in_dim.57.time_ref, f32[1,1024]{1,0:T(1,128)S(1)} %bitcast.31, f32[1,1024]{1,0:T(1,128)S(1)} %bitcast.27), custom_call_target="tpu_custom_call" | custom-call | flops 5242880000 | bytes 2097152 | tf_op jit(solution)/shard_map/pallas_call | solution.py:77
  32.7 1.4 copy-done.5
  34.2 4.2 %shard_map.79 = (bf16[2,256,2048]{2,1,0:T(8,128)(2,1)S(1)}, f32[2,1,2048]{2,1,0:T(1,128)S(1)}) custom-call(f32[512,128]{1,0:T(8,128)S(1)} %broadcast_in_dim.55.time_ref, f32[1,1024]{1,0:T(1,128)S(1)} %bitcast.32, f32[1,1024]{1,0:T(1,128)S(1)} %bitcast.28), custom_call_target="tpu_custom_call" | custom-call | flops 5242880000 | bytes 2097152 | tf_op jit(solution)/shard_map/pallas_call | solution.py:77
  38.4 1.3 copy-done.7
  39.8 4.2 %shard_map.78 = (bf16[2,256,2048]{2,1,0:T(8,128)(2,1)S(1)}, f32[2,1,2048]{2,1,0:T(1,128)S(1)}) custom-call(f32[512,128]{1,0:T(8,128)S(1)} %broadcast_in_dim.53.time_ref, f32[1,1024]{1,0:T(1,128)S(1)} %bitcast.33, f32[1,1024]{1,0:T(1,128)S(1)} %bitcast.29), custom_call_target="tpu_custom_call" | custom-call | flops 5242880000 | bytes 2097152 | tf_op jit(solution)/shard_map/pallas_call | solution.py:77
  44.1 1.3 copy-done.9
  45.6 4.2 %shard_map.77 = (bf16[2,256,2048]{2,1,0:T(8,128)(2,1)S(1)}, f32[2,1,2048]{2,1,0:T(1,128)S(1)}) custom-call(f32[512,128]{1,0:T(8,128)S(1)} %broadcast_in_dim.50.time_ref, f32[1,1024]{1,0:T(1,128)S(1)} %bitcast.34, f32[1,1024]{1,0:T(1,128)S(1)} %bitcast.30), custom_call_target="tpu_custom_call" | custom-call | flops 5242880000 | bytes 2097152 | tf_op jit(solution)/shard_map/pallas_call | solution.py:77
  49.8 1.3 copy-done.11
  51.1 1.3 collective-permute-start.9
  53.1 1.3 collective-permute-start.3
  54.4 1.4 collective-permute-start.2
  55.8 5.1 %collective-permute-done.9.refs_16_ = bf16[2,128,512]{2,1,0:T(8,128)(2,1)S(1)} collective-permute-done((bf16[2,128,512]{2,1,0:T(8,128)(2,1)S(1)}, bf16[2,128,512]{2,1,0:T(8,128)(2,1)S(1)}, u32[]{:S(2)}, u32[]{:S(2)}) %collective-permute-start.9) | collective-permute-done | bytes 262176 | tf_op jit(solution)/shard_map/ppermute | solution.py:444
  62.3 1.4 collective-permute-start.10
  63.6 3.0 %collective-permute-done.3.refs_10_ = bf16[2,128,512]{2,1,0:T(8,128)(2,1)S(1)} collective-permute-done((bf16[2,128,512]{2,1,0:T(8,128)(2,1)S(1)}, bf16[2,128,512]{2,1,0:T(8,128)(2,1)S(1)}, u32[]{:S(2)}, u32[]{:S(2)}) %collective-permute-start.3) | collective-permute-done | bytes 262176 | tf_op jit(solution)/shard_map/ppermute | solution.py:444
  67.9 1.4 collective-permute-start.4
  69.5 2.5 %collective-permute-done.11.refs_18_ = bf16[2,128,512]{2,1,0:T(8,128)(2,1)} collective-permute-done((bf16[2,128,512]{2,1,0:T(8,128)(2,1)S(1)}, bf16[2,128,512]{2,1,0:T(8,128)(2,1)}, u32[]{:S(2)}, u32[]{:S(2)}) %collective-permute-start.11) | collective-permute-done | bytes 262176 | tf_op jit(solution)/shard_map/ppermute | solution.py:444
  72.0 5.6 %collective-permute-done.5.refs_12_ = bf16[2,128,512]{2,1,0:T(8,128)(2,1)} collective-permute-done((bf16[2,128,512]{2,1,0:T(8,128)(2,1)S(1)}, bf16[2,128,512]{2,1,0:T(8,128)(2,1)}, u32[]{:S(2)}, u32[]{:S(2)}) %collective-permute-start.5) | collective-permute-done | bytes 262176 | tf_op jit(solution)/shard_map/ppermute | solution.py:444
  77.6 5.5 %shard_map.81 = (bf16[512,128]{1,0:T(8,128)(2,1)S(1)}, bf16[512,128]{1,0:T(8,128)(2,1)S(1)}, bf16[512,128]{1,0:T(8,128)(2,1)S(1)}, bf16[512,128]{1,0:T(8,128)(2,...) custom-call(s32[4096]{0:T(1024)S(1)} %bitcast.24, ...), custom_call_target="tpu_custom_call" | custom-call | flops 4294967296 | bytes 16777216 | tf_op jit(solution)/shard_map/pallas_call | solution.py:365
  83.2 1.5 collective-permute-start.12
  84.6 2.4 %collective-permute-start.13 = (bf16[512,128]{1,0:T(8,128)(2,1)S(1)}, bf16[512,128]{1,0:T(8,128)(2,1)S(1)}, u32[]{:S(2)}, u32[]{:S(2)}) collective-permute-start(bf16[512,128]{1,0:T(8,128)(2,1)S(1)} %get-tuple-element.50), channel_id=1, source_target_pairs={{0,8},{4,12},{8,0},{12,4},{16,24},{20,28},{24,16},{28,20},{1,9},{5... | collective-permute-start | bytes 393224 | tf_op jit(solution)/shard_map/ppermute | solution.py:431
  87.6 1.6 collective-permute-start.16
  90.8 2.1 %collective-permute-start.18 = (bf16[512,128]{1,0:T(8,128)(2,1)S(1)}, bf16[512,128]{1,0:T(8,128)(2,1)S(1)}, u32[]{:S(2)}, u32[]{:S(2)}) collective-permute-start(bf16[512,128]{1,0:T(8,128)(2,1)S(1)} %get-tuple-element.55), channel_id=1, source_target_pairs={{0,28},{4,24},{8,20},{12,16},{16,12},{20,8},{24,4},{28,0},{1,29},{... | collective-permute-start | bytes 393224 | tf_op jit(solution)/shard_map/ppermute | solution.py:431
  94.1 6.8 %collective-permute-done.16.refs_5_ = bf16[512,128]{1,0:T(8,128)(2,1)S(1)} collective-permute-done((bf16[512,128]{1,0:T(8,128)(2,1)S(1)}, bf16[512,128]{1,0:T(8,128)(2,1)S(1)}, u32[]{:S(2)}, u32[]{:S(2)}) %collective-permute-start.16) | collective-permute-done | bytes 131104 | tf_op jit(solution)/shard_map/ppermute | solution.py:431
  101.0 8.7 %shard_map.82 = (bf16[512,128]{1,0:T(8,128)(2,1)S(1)}, bf16[512,128]{1,0:T(8,128)(2,1)S(1)}, bf16[512,128]{1,0:T(8,128)(2,1)S(1)}, bf16[512,128]{1,0:T(8,128)(2,...) custom-call(s32[8,24]{1,0:T(8,128)S(1)} %get-tuple-element.106.src_r, ...), custom_call_target="tpu_custom_call" | custom-call | flops 10737418240 | bytes 8388608 | tf_op jit(solution)/shard_map/pallas_call | solution.py:200
  109.7 1.7 collective-permute-start.20
  112.2 1.5 collective-permute-start.23
  114.9 2.9 %collective-permute-start.25 = (bf16[512,128]{1,0:T(8,128)(2,1)S(1)}, bf16[512,128]{1,0:T(8,128)(2,1)S(1)}, u32[]{:S(2)}, u32[]{:S(2)}) collective-permute-start(bf16[512,128]{1,0:T(8,128)(2,1)S(1)} %get-tuple-element.67), channel_id=1, source_target_pairs={{0,28},{4,24},{8,20},{12,16},{16,12},{20,8},{24,4},{28,0},{1,29},{... | collective-permute-start | bytes 393224 | tf_op jit(solution)/shard_map/ppermute | solution.py:431
  118.9 6.5 %collective-permute-done.23.refs_24_ = bf16[512,128]{1,0:T(8,128)(2,1)S(1)} collective-permute-done((bf16[512,128]{1,0:T(8,128)(2,1)S(1)}, bf16[512,128]{1,0:T(8,128)(2,1)S(1)}, u32[]{:S(2)}, u32[]{:S(2)}) %collective-permute-start.23) | collective-permute-done | bytes 131104 | tf_op jit(solution)/shard_map/ppermute | solution.py:431
  125.5 7.8 %shard_map.83 = (f32[4,512,256]{2,1,0:T(8,128)S(1)}, bf16[512,128]{1,0:T(8,128)(2,1)S(1)}, bf16[512,128]{1,0:T(8,128)(2,1)S(1)}, bf16[512,128]{1,0:T(8,128)(2,1)...) custom-call(s32[4096]{0:T(1024)S(1)} %bitcast.25, ...), custom_call_target="tpu_custom_call" | custom-call | flops 4294967296 | bytes 16777216 | tf_op jit(solution)/shard_map/pallas_call | solution.py:365
  133.3 1.3 copy-done.3
  135.4 4.2 %collective-permute-start.27 = (bf16[512,128]{1,0:T(8,128)(2,1)S(1)}, bf16[512,128]{1,0:T(8,128)(2,1)S(1)}, u32[]{:S(2)}, u32[]{:S(2)}) collective-permute-start(bf16[512,128]{1,0:T(8,128)(2,1)S(1)} %get-tuple-element.71), channel_id=1, source_target_pairs={{0,8},{4,12},{8,0},{12,4},{16,24},{20,28},{24,16},{28,20},{1,9},{5... | collective-permute-start | bytes 393224 | tf_op jit(solution)/shard_map/ppermute | solution.py:431
  139.6 2.1 %collective-permute-start.30 = (bf16[512,128]{1,0:T(8,128)(2,1)S(1)}, bf16[512,128]{1,0:T(8,128)(2,1)S(1)}, u32[]{:S(2)}, u32[]{:S(2)}) collective-permute-start(bf16[512,128]{1,0:T(8,128)(2,1)S(1)} %get-tuple-element.74), channel_id=1, source_target_pairs={{0,20},{4,16},{8,28},{12,24},{16,4},{20,0},{24,12},{28,8},{1,21},{... | collective-permute-start | bytes 393224 | tf_op jit(solution)/shard_map/ppermute | solution.py:431
  143.4 1.7 collective-permute-start.32
  145.1 1.5 collective-permute-done.28.refs_3_
  146.6 6.6 %collective-permute-done.30.refs_5_ = bf16[512,128]{1,0:T(8,128)(2,1)S(1)} collective-permute-done((bf16[512,128]{1,0:T(8,128)(2,1)S(1)}, bf16[512,128]{1,0:T(8,128)(2,1)S(1)}, u32[]{:S(2)}, u32[]{:S(2)}) %collective-permute-start.30) | collective-permute-done | bytes 131104 | tf_op jit(solution)/shard_map/ppermute | solution.py:431
  153.2 7.9 %shard_map.84 = (bf16[512,128]{1,0:T(8,128)(2,1)S(1)}, bf16[512,128]{1,0:T(8,128)(2,1)S(1)}, bf16[512,128]{1,0:T(8,128)(2,1)S(1)}, bf16[512,128]{1,0:T(8,128)(2,...) custom-call(s32[8,24]{1,0:T(8,128)S(1)} %get-tuple-element.106.src_r, ...), custom_call_target="tpu_custom_call" | custom-call | flops 10737418240 | bytes 8388608 | tf_op jit(solution)/shard_map/pallas_call | solution.py:200
  161.3 1.7 collective-permute-start.34
  163.4 1.9 %collective-permute-start.37 = (bf16[512,128]{1,0:T(8,128)(2,1)S(1)}, bf16[512,128]{1,0:T(8,128)(2,1)S(1)}, u32[]{:S(2)}, u32[]{:S(2)}) collective-permute-start(bf16[512,128]{1,0:T(8,128)(2,1)S(1)} %get-tuple-element.82), channel_id=1, source_target_pairs={{0,20},{4,16},{8,28},{12,24},{16,4},{20,0},{24,12},{28,8},{1,21},{... | collective-permute-start | bytes 393224 | tf_op jit(solution)/shard_map/ppermute | solution.py:431
  166.5 2.9 %collective-permute-start.39 = (bf16[512,128]{1,0:T(8,128)(2,1)S(1)}, bf16[512,128]{1,0:T(8,128)(2,1)S(1)}, u32[]{:S(2)}, u32[]{:S(2)}) collective-permute-start(bf16[512,128]{1,0:T(8,128)(2,1)S(1)} %get-tuple-element.84), channel_id=1, source_target_pairs={{0,28},{4,24},{8,20},{12,16},{16,12},{20,8},{24,4},{28,0},{1,29},{... | collective-permute-start | bytes 393224 | tf_op jit(solution)/shard_map/ppermute | solution.py:431
  170.5 6.5 %collective-permute-done.37.refs_11_ = bf16[512,128]{1,0:T(8,128)(2,1)S(1)} collective-permute-done((bf16[512,128]{1,0:T(8,128)(2,1)S(1)}, bf16[512,128]{1,0:T(8,128)(2,1)S(1)}, u32[]{:S(2)}, u32[]{:S(2)}) %collective-permute-start.37) | collective-permute-done | bytes 131104 | tf_op jit(solution)/shard_map/ppermute | solution.py:431
  177.1 1.6 copy-done.4
  178.6 5.9 %shard_map.85 = f32[4,512,256]{2,1,0:T(8,128)} custom-call(s32[4096]{0:T(1024)S(1)} %bitcast.26, s32[8]{0:T(128)S(1)} %convert_reduce_fusion.2.refs_1_, s32[4]{0:T(128)S(1)} %copy-done.2, s32[2]{0:T(128)S(1)} %pad_add_fusion.refs_3_, f32[8,1,2048]{2,1,0:T(1,128)S(1)} %constant_dynamic-update-slice_fusion.refs_4_.refs_12_, f32[4,512,256]{2,1,0:T(8,128)S(1)} %copy-done.4, ...), custom_call_target="tpu_custom_call" | custom-call | flops 4294967296 | bytes 16777216 | tf_op jit(solution)/shard_map/pallas_call | solution.py:365
  (107 shorter events, 22.7 us)
Async XLA Ops:
  2.4 48.7 %collective-permute-start.7 = (bf16[2,128,512]{2,1,0:T(8,128)(2,1)S(1)}, bf16[2,128,512]{2,1,0:T(8,128)(2,1)S(1)}, u32[]{:S(2)}, u32[]{:S(2)}) collective-permute-start(bf16[2,128,512]{2,1,0:T(8,128)(2,1)S(1)} %get-tuple-element.93), channel_id=1, source_target_pairs={{1,0},{2,1},{3,2},{5,4},{6,5},{7,6},{9,8},{10,9},{11,10},{13,12},{... | collective-permute-start | bytes 786440 | tf_op jit(solution)/shard_map/ppermute | solution.py:444
  3.7 48.7 %collective-permute-start.6 = (bf16[2,128,512]{2,1,0:T(8,128)(2,1)S(1)}, bf16[2,128,512]{2,1,0:T(8,128)(2,1)S(1)}, u32[]{:S(2)}, u32[]{:S(2)}) collective-permute-start(bf16[2,128,512]{2,1,0:T(8,128)(2,1)S(1)} %get-tuple-element.93), channel_id=1, source_target_pairs={{0,1},{1,2},{2,3},{4,5},{5,6},{6,7},{8,9},{9,10},{10,11},{12,13},{... | collective-permute-start | bytes 786440 | tf_op jit(solution)/shard_map/ppermute | solution.py:443
  8.4 44.7 %collective-permute-start.1 = (bf16[2,128,512]{2,1,0:T(8,128)(2,1)}, bf16[2,128,512]{2,1,0:T(8,128)(2,1)S(1)}, u32[]{:S(2)}, u32[]{:S(2)}) collective-permute-start(bf16[2,128,512]{2,1,0:T(8,128)(2,1)} %get-tuple-element.94), channel_id=1, source_target_pairs={{1,0},{2,1},{3,2},{5,4},{6,5},{7,6},{9,8},{10,9},{11,10},{13,12},{... | collective-permute-start | bytes 786440 | tf_op jit(solution)/shard_map/ppermute | solution.py:444
  9.7 44.8 %collective-permute-start = (bf16[2,128,512]{2,1,0:T(8,128)(2,1)}, bf16[2,128,512]{2,1,0:T(8,128)(2,1)S(1)}, u32[]{:S(2)}, u32[]{:S(2)}) collective-permute-start(bf16[2,128,512]{2,1,0:T(8,128)(2,1)} %get-tuple-element.94), channel_id=1, source_target_pairs={{0,1},{1,2},{2,3},{4,5},{5,6},{6,7},{8,9},{9,10},{10,11},{12,13},{... | collective-permute-start | bytes 786440 | tf_op jit(solution)/shard_map/ppermute | solution.py:443
  20.8 48.6 %all-to-all-start = ((s32[8,1,512]{2,1,0:T(1,128)}), s32[8,1,512]{2,1,0:T(1,128)S(1)}, u32[]{:S(2)}, u32[]{:S(2)}) async-start(s32[8,1,512]{2,1,0:T(1,128)} %bitcast), calls=%async_computation | async-start | bytes 32768 | tf_op jit(solution)/shard_map/all_to_all | solution.py:459
  45.5 32.1 %copy-start = (bf16[4,128,512]{2,1,0:T(8,128)(2,1)S(1)}, bf16[4,128,512]{2,1,0:T(8,128)(2,1)}, u32[]{:S(2)}) copy-start(bf16[4,128,512]{2,1,0:T(8,128)(2,1)} %refs_6_.3) | copy-start | bytes 1572868
  45.5 32.0 %copy-start.1 = (bf16[4,512,256]{2,1,0:T(8,128)(2,1)S(1)}, bf16[4,512,256]{2,1,0:T(8,128)(2,1)}, u32[]{:S(2)}) copy-start(bf16[4,512,256]{2,1,0:T(8,128)(2,1)} %refs_5_.3) | copy-start | bytes 3145732
  45.6 32.0 %copy-start.2 = (s32[4]{0:T(128)S(1)}, s32[4]{0:T(128)}, u32[]{:S(2)}) copy-start(s32[4]{0:T(128)} %refs_2_.5) | copy-start | bytes 52
  51.1 9.8 %collective-permute-start.9 = (bf16[2,128,512]{2,1,0:T(8,128)(2,1)S(1)}, bf16[2,128,512]{2,1,0:T(8,128)(2,1)S(1)}, u32[]{:S(2)}, u32[]{:S(2)}) collective-permute-start(bf16[2,128,512]{2,1,0:T(8,128)(2,1)S(1)} %collective-permute-done.7.refs_14_), channel_id=1, source_target_pairs={{1,0},{2,1},{5,4},{6,5},{9,8},{10,9},{13,12},{14,13},{17,16},{18,1... | collective-permute-start | bytes 786440 | tf_op jit(solution)/shard_map/ppermute | solution.py:444
  52.4 9.8 %collective-permute-start.8 = (bf16[2,128,512]{2,1,0:T(8,128)(2,1)S(1)}, bf16[2,128,512]{2,1,0:T(8,128)(2,1)S(1)}, u32[]{:S(2)}, u32[]{:S(2)}) collective-permute-start(bf16[2,128,512]{2,1,0:T(8,128)(2,1)S(1)} %collective-permute-done.6.refs_13_), channel_id=1, source_target_pairs={{1,2},{2,3},{5,6},{6,7},{9,10},{10,11},{13,14},{14,15},{17,18},{18... | collective-permute-start | bytes 786440 | tf_op jit(solution)/shard_map/ppermute | solution.py:443
  53.1 13.4 %collective-permute-start.3 = (bf16[2,128,512]{2,1,0:T(8,128)(2,1)S(1)}, bf16[2,128,512]{2,1,0:T(8,128)(2,1)S(1)}, u32[]{:S(2)}, u32[]{:S(2)}) collective-permute-start(bf16[2,128,512]{2,1,0:T(8,128)(2,1)S(1)} %collective-permute-done.1.refs_8_), channel_id=1, source_target_pairs={{1,0},{2,1},{5,4},{6,5},{9,8},{10,9},{13,12},{14,13},{17,16},{18,1... | collective-permute-start | bytes 786440 | tf_op jit(solution)/shard_map/ppermute | solution.py:444
  54.4 13.4 %collective-permute-start.2 = (bf16[2,128,512]{2,1,0:T(8,128)(2,1)S(1)}, bf16[2,128,512]{2,1,0:T(8,128)(2,1)}, u32[]{:S(2)}, u32[]{:S(2)}) collective-permute-start(bf16[2,128,512]{2,1,0:T(8,128)(2,1)S(1)} %collective-permute-done.refs_7_), channel_id=1, source_target_pairs={{1,2},{2,3},{5,6},{6,7},{9,10},{10,11},{13,14},{14,15},{17,18},{18... | collective-permute-start | bytes 786440 | tf_op jit(solution)/shard_map/ppermute | solution.py:443
  61.0 11.0 %collective-permute-start.11 = (bf16[2,128,512]{2,1,0:T(8,128)(2,1)S(1)}, bf16[2,128,512]{2,1,0:T(8,128)(2,1)}, u32[]{:S(2)}, u32[]{:S(2)}) collective-permute-start(bf16[2,128,512]{2,1,0:T(8,128)(2,1)S(1)} %collective-permute-done.9.refs_16_), channel_id=1, source_target_pairs={{1,0},{5,4},{9,8},{13,12},{17,16},{21,20},{25,24},{29,28}} | collective-permute-start | bytes 786440 | tf_op jit(solution)/shard_map/ppermute | solution.py:444
  62.3 9.7 %collective-permute-start.10 = (bf16[2,128,512]{2,1,0:T(8,128)(2,1)S(1)}, bf16[2,128,512]{2,1,0:T(8,128)(2,1)}, u32[]{:S(2)}, u32[]{:S(2)}) collective-permute-start(bf16[2,128,512]{2,1,0:T(8,128)(2,1)S(1)} %collective-permute-done.8.refs_15_), channel_id=1, source_target_pairs={{2,3},{6,7},{10,11},{14,15},{18,19},{22,23},{26,27},{30,31}} | collective-permute-start | bytes 786440 | tf_op jit(solution)/shard_map/ppermute | solution.py:443
  66.6 11.0 %collective-permute-start.5 = (bf16[2,128,512]{2,1,0:T(8,128)(2,1)S(1)}, bf16[2,128,512]{2,1,0:T(8,128)(2,1)}, u32[]{:S(2)}, u32[]{:S(2)}) collective-permute-start(bf16[2,128,512]{2,1,0:T(8,128)(2,1)S(1)} %collective-permute-done.3.refs_10_), channel_id=1, source_target_pairs={{1,0},{5,4},{9,8},{13,12},{17,16},{21,20},{25,24},{29,28}} | collective-permute-start | bytes 786440 | tf_op jit(solution)/shard_map/ppermute | solution.py:444
  67.9 9.7 %collective-permute-start.4 = (bf16[2,128,512]{2,1,0:T(8,128)(2,1)}, bf16[2,128,512]{2,1,0:T(8,128)(2,1)}, u32[]{:S(2)}, u32[]{:S(2)}) collective-permute-start(bf16[2,128,512]{2,1,0:T(8,128)(2,1)} %collective-permute-done.2.refs_9_), channel_id=1, source_target_pairs={{2,3},{6,7},{10,11},{14,15},{18,19},{22,23},{26,27},{30,31}} | collective-permute-start | bytes 786440 | tf_op jit(solution)/shard_map/ppermute | solution.py:443
  77.6 23.3 %copy-start.6 = (bf16[2,256,2048]{2,1,0:T(8,128)(2,1)S(1)}, bf16[2,256,2048]{2,1,0:T(8,128)(2,1)}, u32[]{:S(2)}) copy-start(bf16[2,256,2048]{2,1,0:T(8,128)(2,1)} %copy-done.5) | copy-start | bytes 6291460
  77.6 23.3 %copy-start.8 = (bf16[2,256,2048]{2,1,0:T(8,128)(2,1)S(1)}, bf16[2,256,2048]{2,1,0:T(8,128)(2,1)}, u32[]{:S(2)}) copy-start(bf16[2,256,2048]{2,1,0:T(8,128)(2,1)} %copy-done.7) | copy-start | bytes 6291460
  77.6 23.3 %copy-start.10 = (bf16[2,256,2048]{2,1,0:T(8,128)(2,1)S(1)}, bf16[2,256,2048]{2,1,0:T(8,128)(2,1)}, u32[]{:S(2)}) copy-start(bf16[2,256,2048]{2,1,0:T(8,128)(2,1)} %copy-done.9) | copy-start | bytes 6291460
  77.6 23.3 %copy-start.12 = (bf16[2,256,2048]{2,1,0:T(8,128)(2,1)S(1)}, bf16[2,256,2048]{2,1,0:T(8,128)(2,1)}, u32[]{:S(2)}) copy-start(bf16[2,256,2048]{2,1,0:T(8,128)(2,1)} %copy-done.11) | copy-start | bytes 6291460
  83.2 6.1 %collective-permute-start.12 = (bf16[512,128]{1,0:T(8,128)(2,1)S(1)}, bf16[512,128]{1,0:T(8,128)(2,1)S(1)}, u32[]{:S(2)}, u32[]{:S(2)}) collective-permute-start(bf16[512,128]{1,0:T(8,128)(2,1)S(1)} %get-tuple-element.49), channel_id=1, source_target_pairs={{0,4},{4,0},{8,12},{12,8},{16,20},{20,16},{24,28},{28,24},{1,5},{5... | collective-permute-start | bytes 393224 | tf_op jit(solution)/shard_map/ppermute | solution.py:431
  84.6 6.1 %collective-permute-start.13 = (bf16[512,128]{1,0:T(8,128)(2,1)S(1)}, bf16[512,128]{1,0:T(8,128)(2,1)S(1)}, u32[]{:S(2)}, u32[]{:S(2)}) collective-permute-start(bf16[512,128]{1,0:T(8,128)(2,1)S(1)} %get-tuple-element.50), channel_id=1, source_target_pairs={{0,8},{4,12},{8,0},{12,4},{16,24},{20,28},{24,16},{28,20},{1,9},{5... | collective-permute-start | bytes 393224 | tf_op jit(solution)/shard_map/ppermute | solution.py:431
  87.1 7.0 %collective-permute-start.14 = (bf16[512,128]{1,0:T(8,128)(2,1)S(1)}, bf16[512,128]{1,0:T(8,128)(2,1)S(1)}, u32[]{:S(2)}, u32[]{:S(2)}) collective-permute-start(bf16[512,128]{1,0:T(8,128)(2,1)S(1)} %get-tuple-element.51), channel_id=1, source_target_pairs={{0,12},{4,8},{8,4},{12,0},{16,28},{20,24},{24,20},{28,16},{1,13},{... | collective-permute-start | bytes 393224 | tf_op jit(solution)/shard_map/ppermute | solution.py:431
  87.2 6.9 %collective-permute-start.15 = (bf16[512,128]{1,0:T(8,128)(2,1)S(1)}, bf16[512,128]{1,0:T(8,128)(2,1)S(1)}, u32[]{:S(2)}, u32[]{:S(2)}) collective-permute-start(bf16[512,128]{1,0:T(8,128)(2,1)S(1)} %get-tuple-element.52), channel_id=1, source_target_pairs={{0,16},{4,20},{8,24},{12,28},{16,0},{20,4},{24,8},{28,12},{1,17},{... | collective-permute-start | bytes 393224 | tf_op jit(solution)/shard_map/ppermute | solution.py:431
  87.6 13.3 %collective-permute-start.16 = (bf16[512,128]{1,0:T(8,128)(2,1)S(1)}, bf16[512,128]{1,0:T(8,128)(2,1)S(1)}, u32[]{:S(2)}, u32[]{:S(2)}) collective-permute-start(bf16[512,128]{1,0:T(8,128)(2,1)S(1)} %get-tuple-element.53), channel_id=1, source_target_pairs={{0,20},{4,16},{8,28},{12,24},{16,4},{20,0},{24,12},{28,8},{1,21},{... | collective-permute-start | bytes 393224 | tf_op jit(solution)/shard_map/ppermute | solution.py:431
  89.2 11.7 %collective-permute-start.17 = (bf16[512,128]{1,0:T(8,128)(2,1)S(1)}, bf16[512,128]{1,0:T(8,128)(2,1)S(1)}, u32[]{:S(2)}, u32[]{:S(2)}) collective-permute-start(bf16[512,128]{1,0:T(8,128)(2,1)S(1)} %get-tuple-element.54), channel_id=1, source_target_pairs={{0,24},{4,28},{8,16},{12,20},{16,8},{20,12},{24,0},{28,4},{1,25},{... | collective-permute-start | bytes 393224 | tf_op jit(solution)/shard_map/ppermute | solution.py:431
  90.8 10.1 %collective-permute-start.18 = (bf16[512,128]{1,0:T(8,128)(2,1)S(1)}, bf16[512,128]{1,0:T(8,128)(2,1)S(1)}, u32[]{:S(2)}, u32[]{:S(2)}) collective-permute-start(bf16[512,128]{1,0:T(8,128)(2,1)S(1)} %get-tuple-element.55), channel_id=1, source_target_pairs={{0,28},{4,24},{8,20},{12,16},{16,12},{20,8},{24,4},{28,0},{1,29},{... | collective-permute-start | bytes 393224 | tf_op jit(solution)/shard_map/ppermute | solution.py:431
  109.6 4.1 %collective-permute-start.19 = (bf16[512,128]{1,0:T(8,128)(2,1)S(1)}, bf16[512,128]{1,0:T(8,128)(2,1)S(1)}, u32[]{:S(2)}, u32[]{:S(2)}) collective-permute-start(bf16[512,128]{1,0:T(8,128)(2,1)S(1)} %get-tuple-element.61), channel_id=1, source_target_pairs={{0,4},{4,0},{8,12},{12,8},{16,20},{20,16},{24,28},{28,24},{1,5},{5... | collective-permute-start | bytes 393224 | tf_op jit(solution)/shard_map/ppermute | solution.py:431
  109.7 5.2 %collective-permute-start.20 = (bf16[512,128]{1,0:T(8,128)(2,1)S(1)}, bf16[512,128]{1,0:T(8,128)(2,1)S(1)}, u32[]{:S(2)}, u32[]{:S(2)}) collective-permute-start(bf16[512,128]{1,0:T(8,128)(2,1)S(1)} %get-tuple-element.62), channel_id=1, source_target_pairs={{0,8},{4,12},{8,0},{12,4},{16,24},{20,28},{24,16},{28,20},{1,9},{5... | collective-permute-start | bytes 393224 | tf_op jit(solution)/shard_map/ppermute | solution.py:431
  111.4 7.5 %collective-permute-start.21 = (bf16[512,128]{1,0:T(8,128)(2,1)S(1)}, bf16[512,128]{1,0:T(8,128)(2,1)S(1)}, u32[]{:S(2)}, u32[]{:S(2)}) collective-permute-start(bf16[512,128]{1,0:T(8,128)(2,1)S(1)} %get-tuple-element.63), channel_id=1, source_target_pairs={{0,12},{4,8},{8,4},{12,0},{16,28},{20,24},{24,20},{28,16},{1,13},{... | collective-permute-start | bytes 393224 | tf_op jit(solution)/shard_map/ppermute | solution.py:431
  111.8 7.1 %collective-permute-start.22 = (bf16[512,128]{1,0:T(8,128)(2,1)S(1)}, bf16[512,128]{1,0:T(8,128)(2,1)S(1)}, u32[]{:S(2)}, u32[]{:S(2)}) collective-permute-start(bf16[512,128]{1,0:T(8,128)(2,1)S(1)} %get-tuple-element.64), channel_id=1, source_target_pairs={{0,16},{4,20},{8,24},{12,28},{16,0},{20,4},{24,8},{28,12},{1,17},{... | collective-permute-start | bytes 393224 | tf_op jit(solution)/shard_map/ppermute | solution.py:431
  112.2 13.3 %collective-permute-start.23 = (bf16[512,128]{1,0:T(8,128)(2,1)S(1)}, bf16[512,128]{1,0:T(8,128)(2,1)S(1)}, u32[]{:S(2)}, u32[]{:S(2)}) collective-permute-start(bf16[512,128]{1,0:T(8,128)(2,1)S(1)} %get-tuple-element.65), channel_id=1, source_target_pairs={{0,20},{4,16},{8,28},{12,24},{16,4},{20,0},{24,12},{28,8},{1,21},{... | collective-permute-start | bytes 393224 | tf_op jit(solution)/shard_map/ppermute | solution.py:431
  113.8 11.7 %collective-permute-start.24 = (bf16[512,128]{1,0:T(8,128)(2,1)S(1)}, bf16[512,128]{1,0:T(8,128)(2,1)S(1)}, u32[]{:S(2)}, u32[]{:S(2)}) collective-permute-start(bf16[512,128]{1,0:T(8,128)(2,1)S(1)} %get-tuple-element.66), channel_id=1, source_target_pairs={{0,24},{4,28},{8,16},{12,20},{16,8},{20,12},{24,0},{28,4},{1,25},{... | collective-permute-start | bytes 393224 | tf_op jit(solution)/shard_map/ppermute | solution.py:431
  114.9 10.6 %collective-permute-start.25 = (bf16[512,128]{1,0:T(8,128)(2,1)S(1)}, bf16[512,128]{1,0:T(8,128)(2,1)S(1)}, u32[]{:S(2)}, u32[]{:S(2)}) collective-permute-start(bf16[512,128]{1,0:T(8,128)(2,1)S(1)} %get-tuple-element.67), channel_id=1, source_target_pairs={{0,28},{4,24},{8,20},{12,16},{16,12},{20,8},{24,4},{28,0},{1,29},{... | collective-permute-start | bytes 393224 | tf_op jit(solution)/shard_map/ppermute | solution.py:431
  134.6 7.0 %collective-permute-start.26 = (bf16[512,128]{1,0:T(8,128)(2,1)S(1)}, bf16[512,128]{1,0:T(8,128)(2,1)S(1)}, u32[]{:S(2)}, u32[]{:S(2)}) collective-permute-start(bf16[512,128]{1,0:T(8,128)(2,1)S(1)} %get-tuple-element.70), channel_id=1, source_target_pairs={{0,4},{4,0},{8,12},{12,8},{16,20},{20,16},{24,28},{28,24},{1,5},{5... | collective-permute-start | bytes 393224 | tf_op jit(solution)/shard_map/ppermute | solution.py:431
  135.4 8.1 %collective-permute-start.27 = (bf16[512,128]{1,0:T(8,128)(2,1)S(1)}, bf16[512,128]{1,0:T(8,128)(2,1)S(1)}, u32[]{:S(2)}, u32[]{:S(2)}) collective-permute-start(bf16[512,128]{1,0:T(8,128)(2,1)S(1)} %get-tuple-element.71), channel_id=1, source_target_pairs={{0,8},{4,12},{8,0},{12,4},{16,24},{20,28},{24,16},{28,20},{1,9},{5... | collective-permute-start | bytes 393224 | tf_op jit(solution)/shard_map/ppermute | solution.py:431
  139.6 7.0 %collective-permute-start.28 = (bf16[512,128]{1,0:T(8,128)(2,1)S(1)}, bf16[512,128]{1,0:T(8,128)(2,1)S(1)}, u32[]{:S(2)}, u32[]{:S(2)}) collective-permute-start(bf16[512,128]{1,0:T(8,128)(2,1)S(1)} %get-tuple-element.72), channel_id=1, source_target_pairs={{0,12},{4,8},{8,4},{12,0},{16,28},{20,24},{24,20},{28,16},{1,13},{... | collective-permute-start | bytes 393224 | tf_op jit(solution)/shard_map/ppermute | solution.py:431
  139.6 7.0 %collective-permute-start.29 = (bf16[512,128]{1,0:T(8,128)(2,1)S(1)}, bf16[512,128]{1,0:T(8,128)(2,1)S(1)}, u32[]{:S(2)}, u32[]{:S(2)}) collective-permute-start(bf16[512,128]{1,0:T(8,128)(2,1)S(1)} %get-tuple-element.73), channel_id=1, source_target_pairs={{0,16},{4,20},{8,24},{12,28},{16,0},{20,4},{24,8},{28,12},{1,17},{... | collective-permute-start | bytes 393224 | tf_op jit(solution)/shard_map/ppermute | solution.py:431
  139.6 13.6 %collective-permute-start.30 = (bf16[512,128]{1,0:T(8,128)(2,1)S(1)}, bf16[512,128]{1,0:T(8,128)(2,1)S(1)}, u32[]{:S(2)}, u32[]{:S(2)}) collective-permute-start(bf16[512,128]{1,0:T(8,128)(2,1)S(1)} %get-tuple-element.74), channel_id=1, source_target_pairs={{0,20},{4,16},{8,28},{12,24},{16,4},{20,0},{24,12},{28,8},{1,21},{... | collective-permute-start | bytes 393224 | tf_op jit(solution)/shard_map/ppermute | solution.py:431
  141.6 11.6 %collective-permute-start.31 = (bf16[512,128]{1,0:T(8,128)(2,1)S(1)}, bf16[512,128]{1,0:T(8,128)(2,1)S(1)}, u32[]{:S(2)}, u32[]{:S(2)}) collective-permute-start(bf16[512,128]{1,0:T(8,128)(2,1)S(1)} %get-tuple-element.75), channel_id=1, source_target_pairs={{0,24},{4,28},{8,16},{12,20},{16,8},{20,12},{24,0},{28,4},{1,25},{... | collective-permute-start | bytes 393224 | tf_op jit(solution)/shard_map/ppermute | solution.py:431
  143.4 9.8 %collective-permute-start.32 = (bf16[512,128]{1,0:T(8,128)(2,1)S(1)}, bf16[512,128]{1,0:T(8,128)(2,1)S(1)}, u32[]{:S(2)}, u32[]{:S(2)}) collective-permute-start(bf16[512,128]{1,0:T(8,128)(2,1)S(1)} %get-tuple-element.76), channel_id=1, source_target_pairs={{0,28},{4,24},{8,20},{12,16},{16,12},{20,8},{24,4},{28,0},{1,29},{... | collective-permute-start | bytes 393224 | tf_op jit(solution)/shard_map/ppermute | solution.py:431
  161.2 4.1 %collective-permute-start.33 = (bf16[512,128]{1,0:T(8,128)(2,1)S(1)}, bf16[512,128]{1,0:T(8,128)(2,1)S(1)}, u32[]{:S(2)}, u32[]{:S(2)}) collective-permute-start(bf16[512,128]{1,0:T(8,128)(2,1)S(1)} %get-tuple-element.78), channel_id=1, source_target_pairs={{0,4},{4,0},{8,12},{12,8},{16,20},{20,16},{24,28},{28,24},{1,5},{5... | collective-permute-start | bytes 393224 | tf_op jit(solution)/shard_map/ppermute | solution.py:431
  161.3 5.2 %collective-permute-start.34 = (bf16[512,128]{1,0:T(8,128)(2,1)S(1)}, bf16[512,128]{1,0:T(8,128)(2,1)S(1)}, u32[]{:S(2)}, u32[]{:S(2)}) collective-permute-start(bf16[512,128]{1,0:T(8,128)(2,1)S(1)} %get-tuple-element.79), channel_id=1, source_target_pairs={{0,8},{4,12},{8,0},{12,4},{16,24},{20,28},{24,16},{28,20},{1,9},{5... | collective-permute-start | bytes 393224 | tf_op jit(solution)/shard_map/ppermute | solution.py:431
  163.0 7.5 %collective-permute-start.35 = (bf16[512,128]{1,0:T(8,128)(2,1)S(1)}, bf16[512,128]{1,0:T(8,128)(2,1)S(1)}, u32[]{:S(2)}, u32[]{:S(2)}) collective-permute-start(bf16[512,128]{1,0:T(8,128)(2,1)S(1)} %get-tuple-element.80), channel_id=1, source_target_pairs={{0,12},{4,8},{8,4},{12,0},{16,28},{20,24},{24,20},{28,16},{1,13},{... | collective-permute-start | bytes 393224 | tf_op jit(solution)/shard_map/ppermute | solution.py:431
  163.4 7.1 %collective-permute-start.36 = (bf16[512,128]{1,0:T(8,128)(2,1)S(1)}, bf16[512,128]{1,0:T(8,128)(2,1)S(1)}, u32[]{:S(2)}, u32[]{:S(2)}) collective-permute-start(bf16[512,128]{1,0:T(8,128)(2,1)S(1)} %get-tuple-element.81), channel_id=1, source_target_pairs={{0,16},{4,20},{8,24},{12,28},{16,0},{20,4},{24,8},{28,12},{1,17},{... | collective-permute-start | bytes 393224 | tf_op jit(solution)/shard_map/ppermute | solution.py:431
  163.4 13.6 %collective-permute-start.37 = (bf16[512,128]{1,0:T(8,128)(2,1)S(1)}, bf16[512,128]{1,0:T(8,128)(2,1)S(1)}, u32[]{:S(2)}, u32[]{:S(2)}) collective-permute-start(bf16[512,128]{1,0:T(8,128)(2,1)S(1)} %get-tuple-element.82), channel_id=1, source_target_pairs={{0,20},{4,16},{8,28},{12,24},{16,4},{20,0},{24,12},{28,8},{1,21},{... | collective-permute-start | bytes 393224 | tf_op jit(solution)/shard_map/ppermute | solution.py:431
  165.3 11.7 %collective-permute-start.38 = (bf16[512,128]{1,0:T(8,128)(2,1)S(1)}, bf16[512,128]{1,0:T(8,128)(2,1)S(1)}, u32[]{:S(2)}, u32[]{:S(2)}) collective-permute-start(bf16[512,128]{1,0:T(8,128)(2,1)S(1)} %get-tuple-element.83), channel_id=1, source_target_pairs={{0,24},{4,28},{8,16},{12,20},{16,8},{20,12},{24,0},{28,4},{1,25},{... | collective-permute-start | bytes 393224 | tf_op jit(solution)/shard_map/ppermute | solution.py:431
  166.5 10.6 %collective-permute-start.39 = (bf16[512,128]{1,0:T(8,128)(2,1)S(1)}, bf16[512,128]{1,0:T(8,128)(2,1)S(1)}, u32[]{:S(2)}, u32[]{:S(2)}) collective-permute-start(bf16[512,128]{1,0:T(8,128)(2,1)S(1)} %get-tuple-element.84), channel_id=1, source_target_pairs={{0,28},{4,24},{8,20},{12,16},{16,12},{20,8},{24,4},{28,0},{1,29},{... | collective-permute-start | bytes 393224 | tf_op jit(solution)/shard_map/ppermute | solution.py:431
  (6 other events, 8.3 us)

commit v4 on v3

--- a/solution.py
+++ b/solution.py
@@ -13,9 +13,8 @@
 STEP = 16
 BETA = 2.0
 RIDGE = 1.0
-VMEM_LIMIT = 36 * 1024 * 1024
-BASIS_CALLS = 4
-CHUNKS = 2
+VMEM_LIMIT = 24 * 1024 * 1024
+BASIS_CALLS = 2
 UNROLL = 16
 
 COS_POLY = (1.0, -19.73920440673828, 64.9391098022461, -85.4500503540039, 60.16689682006836,
@@ -34,7 +33,8 @@
     return acc
 
 
-def basis_kernel(time_ref, period_ref, inverse_ref, basis_ref, norm_ref):
+def basis_kernel(after, time_ref, period_ref, inverse_ref, *refs):
+    basis_ref, norm_ref = refs[after:]
     obs = time_ref.shape[0]
     nper = period_ref.shape[1]
     rows = 32
@@ -67,7 +67,7 @@
         norm_ref[0, :, sines] = 1.0 / (jnp.sum(total_s, axis=0, keepdims=True) + RIDGE)
 
 
-def make_basis(times, periods):
+def make_basis(times, periods, after):
     sched_dev, obs = times.shape
     nper = periods.shape[0]
     wide = jnp.broadcast_to(
@@ -75,13 +75,13 @@
     )
     period = periods.astype(jnp.float32)[None, :]
     return pl.pallas_call(
-        basis_kernel,
+        functools.partial(basis_kernel, len(after)),
         grid=(sched_dev,),
         in_specs=[
             pl.BlockSpec((obs, SRC_GROUP), lambda j: (j, 0)),
             pl.BlockSpec((1, nper), lambda j: (0, 0)),
             pl.BlockSpec((1, nper), lambda j: (0, 0)),
-        ],
+        ] + [pl.BlockSpec(memory_space=pl.ANY)] * len(after),
         out_specs=[
             pl.BlockSpec((1, obs, 2 * nper), lambda j: (j, 0, 0)),
             pl.BlockSpec((1, 1, 2 * nper), lambda j: (j, 0, 0)),
@@ -94,7 +94,7 @@
         cost_estimate=pl.CostEstimate(
             flops=sched_dev * obs * nper * 10000, bytes_accessed=sched_dev * obs * nper * 4, transcendentals=0
         ),
-    )(wide, period, 1.0 / period)
+    )(wide, period, 1.0 / period, *after)
 
 
 def fit_kernel(tm_count, src_ref, dst_ref, *refs):
@@ -215,22 +215,19 @@
     return models, score
 
 
-def load_attitude(sky, own_ref, chunks, whole_ref, sems):
+def load_attitude(sky, own_ref, passed, whole_ref, sems):
     rows = own_ref.shape[1]
-    copies = [(None, sky, slice(None), own_ref)]
-    for index, passed in enumerate(chunks):
-        count = len(passed) // 2 + 1
-        segs = passed[0].shape[0]
-        held = pl.ds(index * segs, segs)
-        for hop in range(1, count):
-            copies.append((sky >= hop, sky - hop, held, passed[2 * hop - 2]))
-            copies.append((sky + hop < count, sky + hop, held, passed[2 * hop - 1]))
+    count = len(passed) // 2 + 1
+    copies = [(None, sky, own_ref)]
+    for hop in range(1, count):
+        copies.append((sky >= hop, sky - hop, passed[2 * hop - 2]))
+        copies.append((sky + hop < count, sky + hop, passed[2 * hop - 1]))
 
     def each(act):
-        for index, (valid, quarter, held, ref) in enumerate(copies):
-            def run(index=index, quarter=quarter, held=held, ref=ref):
+        for index, (valid, quarter, ref) in enumerate(copies):
+            def run(index=index, quarter=quarter, ref=ref):
                 at = pl.ds(pl.multiple_of(quarter * rows, rows), rows)
-                act(pltpu.make_async_copy(ref, whole_ref.at[held, at, :], sems.at[index]))
+                act(pltpu.make_async_copy(ref, whole_ref.at[:, at, :], sems.at[index]))
 
             if valid is None:
                 run()
@@ -300,7 +297,7 @@
             out_ref[seg, :, lanes] = current_ref[seg, :, lanes].astype(jnp.float32) - placed
 
 
-def owner_kernel(tm_count, chunk_counts, placing, *refs):
+def owner_kernel(tm_count, passed_count, placing, *refs):
     refs = list(refs)
 
     def take(count):
@@ -310,16 +307,16 @@
 
     asked_ref, cnt_ref, count_ref, where_ref, _, current_ref = take(6)
     me, sky = where_ref[0], where_ref[1]
-    picking = chunk_counts is not None
+    picking = passed_count > 0
     if picking:
         (own_ref,) = take(1)
-        chunks = [take(count) for count in chunk_counts]
+        passed = take(passed_count)
     returned = take(tm_count) if placing else None
     out_ref = take(1)[0] if placing else None
     picked = take(tm_count) if picking else None
     if picking:
         whole_ref, sems, white_ref = take(3)
-        wait = load_attitude(sky, own_ref, chunks, whole_ref, sems)
+        wait = load_attitude(sky, own_ref, passed, whole_ref, sems)
     (rows_ref,) = take(1)
     if placing:
         place_rows(me, asked_ref, cnt_ref, returned, current_ref, out_ref, rows_ref, refs)
@@ -343,15 +340,12 @@
     args = [asked, cnt, seg_counts, where, norms, current]
     out_shape = []
     scratch = []
-    counts = None
     if picking:
-        own, chunks = attitude
-        counts = [len(chunk) for chunk in chunks]
-        args += [own] + [piece for chunk in chunks for piece in chunk]
-        in_specs += [anywhere] * (1 + sum(counts))
+        args += attitude
+        in_specs += [anywhere] * len(attitude)
         scratch += [
             pltpu.VMEM((seg_dev, slots, slots), jnp.bfloat16),
-            pltpu.SemaphoreType.DMA((1 + sum(counts),)),
+            pltpu.SemaphoreType.DMA((len(attitude),)),
             table,
         ]
     scratch.append(pltpu.VMEM((tm_count * capacity, SRC_GROUP), jnp.float32))
@@ -363,7 +357,7 @@
     if picking:
         out_shape += [jax.ShapeDtypeStruct((capacity, SRC_GROUP), jnp.bfloat16)] * tm_count
     out = pl.pallas_call(
-        functools.partial(owner_kernel, tm_count, counts, placing),
+        functools.partial(owner_kernel, tm_count, len(attitude) - 1 if picking else 0, placing),
         in_specs=in_specs,
         out_specs=[VMEM] * len(out_shape),
         out_shape=out_shape,
@@ -432,18 +426,18 @@
     return out
 
 
-def pass_along(attitude):
+def pass_along(attitude, work):
     count = lax.axis_size("sky")
-    part = attitude.shape[0] // CHUNKS
-    right = [attitude[index * part:(index + 1) * part] for index in range(CHUNKS)]
-    left = list(right)
-    chunks = [[] for _ in range(CHUNKS)]
+    right = left = attitude
+    pieces = [attitude]
+    done = []
     for hop in range(1, count):
-        for index in range(CHUNKS):
-            right[index] = lax.ppermute(right[index], "sky", [(i, i + 1) for i in range(hop - 1, count - 1)])
-            left[index] = lax.ppermute(left[index], "sky", [(i, i - 1) for i in range(1, count - hop + 1)])
-            chunks[index] += [right[index], left[index]]
-    return attitude, chunks
+        right = lax.ppermute(right, "sky", [(i, i + 1) for i in range(hop - 1, count - 1)])
+        left = lax.ppermute(left, "sky", [(i, i - 1) for i in range(1, count - hop + 1)])
+        pieces += [right, left]
+        if hop < count - 1 and work:
+            done.append(work.pop(0)([right, left]))
+    return pieces, done
 
 
 def on_device(residuals, seg_counts, attitude, sched_seg, sched_slot, periods):
@@ -452,16 +446,18 @@
     seg_dev, slots, width = residuals.shape
     column_blocks = width // SRC_GROUP
     capacity = 2 * sched_dev * obs // tm_count
-    pieces = pass_along(attitude)
     tables, times, wanted = make_lists(
         sched_seg, sched_slot, seg_dev, slots, column_blocks, tm_count, capacity
     )
     asked = lax.all_to_all(wanted.reshape(tm_count, capacity), "tm", split_axis=0, concat_axis=0, tiled=True)
     cnt = jnp.sum((asked < seg_dev * slots * column_blocks).astype(jnp.int32), axis=1)
     part = sched_dev // BASIS_CALLS
-    parts, norms = zip(
-        *[make_basis(times[index * part:(index + 1) * part], periods) for index in range(BASIS_CALLS)]
-    )
+    work = [
+        functools.partial(make_basis, times[index * part:(index + 1) * part], periods)
+        for index in range(BASIS_CALLS)
+    ]
+    pieces, made = pass_along(attitude, work)
+    parts, norms = zip(*made)
     norms = jnp.concatenate(norms)
     where = jnp.stack([lax.axis_index("tm"), lax.axis_index("sky")])
     scalars = (asked.reshape(-1), cnt, seg_counts, where)

time: 186 us -> 159 us (0.85)
  starting transfers between devices: 61.7 us -> 50 us
  local copies, waits for them, and re-layouts: 10.6 us -> 3.33 us
  waiting for transfers between devices: 48.5 us -> 41.9 us
  Pallas kernels: 52.6 us -> 50.3 us
    ppermute x12 -> x6, starting transfers between devices: 21.2 us -> 9.95 us  [the longest x3 6.08 us: pass_along(): lax.ppermute(right, 'sky', [(i, i + 1) for i in range(hop - 1, count - 1)])]
    ppermute x12 -> x6, waiting for transfers between devices: 16.2 us -> 7.02 us  [the longest x3 7.01 us: pass_along(): lax.ppermute(left, 'sky', [(i, i - 1) for i in range(1, count - hop + 1)])]
    unnamed x35 -> x15, local copies, waits for them, and re-layouts: 8.3 us -> 2.94 us
    pallas_call x7 -> x5, Pallas kernels: 36 us -> 33.8 us  [the longest x3 17 us: owner_step(): pl.pallas_call(functools.partial(owner_kernel, tm_count, len(attitude) -...]
    all_to_all x1, waiting for transfers between devices: 0.01 us -> 2.11 us  [on_device(): lax.all_to_all(wanted.reshape(tm_count, capacity), 'tm', split_axis=0, co...]
  transfers between devices with their start and end apart: 41 -> 35, of which waited for: 14 -> 14; matrix products, arithmetic and copies ran while one was open for 6% -> 7% of each run, Pallas kernels for 9% -> 11%
where the time goes in v4:
time: 159 us; the launch traced here: 156 us
  Pallas kernels  50.3 us (32%)
  starting transfers between devices  50 us (31%)
  waiting for transfers between devices  41.9 us (26%)
  other arithmetic  9.96 us (6%)
  local copies, waits for them, and re-layouts  3.33 us (2%)
    ppermute x28, starting transfers between devices, exchange(): lax.ppermute(blocks[step], 'tm', [(i, i ^ step) for i in range(count)])  34.9 us
    ppermute x28, waiting for transfers between devices, exchange(): lax.ppermute(blocks[step], 'tm', [(i, i ^ step) for i in range(count)])  32.8 us
    pallas_call x3, Pallas kernels, owner_step(): pl.pallas_call(functools.partial(owner_kernel, tm_count, len(attitude) -...  17 us
    pallas_call x2, Pallas kernels, make_basis(): pl.pallas_call(functools.partial(basis_kernel, len(after)), grid=(sched_d...  16.8 us
    pallas_call x2, Pallas kernels, fit_plans(): pl.pallas_call(functools.partial(fit_kernel, tm_count), in_specs=[SMEM, S...  16.6 us
    ppermute x3, waiting for transfers between devices, pass_along(): lax.ppermute(left, 'sky', [(i, i - 1) for i in range(1, count - hop + 1)])  7.01 us
    ppermute x3, starting transfers between devices, pass_along(): lax.ppermute(right, 'sky', [(i, i + 1) for i in range(hop - 1, count - 1)])  6.08 us
    all_to_all x1, starting transfers between devices, on_device(): lax.all_to_all(wanted.reshape(tm_count, capacity), 'tm', split_axis=0, co...  5.11 us
  transfers between devices with their start and end apart: 35, of which 14 were waited for; matrix products, arithmetic and copies ran while one was open for 7% of the time, Pallas kernels for 11%

profile of v4, /device:TPU:1, one launch (start us, length us, event | category | flops | bytes accessed | tf_op | source)
XLA Modules:
  0.0 156.5 jit_solution(3289526842330146126)
XLA Ops:
  0.6 1.3 collective-permute-start.1
  1.9 4.7 %collective-permute-start = (bf16[4,128,512]{2,1,0:T(8,128)(2,1)}, bf16[4,128,512]{2,1,0:T(8,128)(2,1)S(1)}, u32[]{:S(2)}, u32[]{:S(2)}) collective-permute-start(bf16[4,128,512]{2,1,0:T(8,128)(2,1)} %refs_6_.3), channel_id=1, source_target_pairs={{0,1},{1,2},{2,3},{4,5},{5,6},{6,7},{8,9},{9,10},{10,11},{12,13},{... | collective-permute-start | bytes 1572872 | tf_op jit(solution)/shard_map/ppermute | solution.py:435
  6.7 0.7 broadcast_xor_fusion
  7.6 0.8 convert_reduce_fusion
  8.9 0.8 fusion.17
  9.7 3.4 %select_reduce_fusion = s32[4096]{0:T(1024)S(1)} fusion(s32[2048]{0:T(1024)S(1)} %bitcast.28, s32[2048]{0:T(1024)S(1)} %bitcast.27), kind=kLoop, calls=%fused_computation | loop fusion | flops 25161728 | bytes 32768 | tf_op jit(solution)/shard_map/reduce_sum | solution.py:400
  13.7 5.1 %all-to-all-start = ((s32[8,1,512]{2,1,0:T(1,128)}), s32[8,1,512]{2,1,0:T(1,128)S(1)}, u32[]{:S(2)}, u32[]{:S(2)}) async-start(s32[8,1,512]{2,1,0:T(1,128)} %bitcast), calls=%async_computation | async-start | bytes 32768 | tf_op jit(solution)/shard_map/all_to_all | solution.py:452
  20.8 2.1 %all-to-all-done = s32[8,1,512]{2,1,0:T(1,128)S(1)} async-done(((s32[8,1,512]{2,1,0:T(1,128)}), s32[8,1,512]{2,1,0:T(1,128)S(1)}, u32[]{:S(2)}, u32[]{:S(2)}) %all-to-all-start) | async-done | bytes 16416 | tf_op jit(solution)/shard_map/all_to_all | solution.py:452
  23.0 1.3 collective-permute-start.3
  24.3 0.7 collective-permute-start.2
  25.2 8.4 %shard_map.77 = (bf16[4,256,2048]{2,1,0:T(8,128)(2,1)S(1)}, f32[4,1,2048]{2,1,0:T(1,128)S(1)}) custom-call(f32[1024,128]{1,0:T(8,128)S(1)} %broadcast_in_dim.41.time_ref, f32[1,1024]{1,0:T(1,128)S(1)} %bitcast.23, f32[1,1024]{1,0:T(1,128)S(1)} %bitcast.21, bf16[4,128,512]{2,1,0:T(8,128)(2,1)S(1)} %collective-permute-done.refs_0_.refs_7_, ...), custom_call_target="tpu_custom_call" | custom-call | flops 10485760000 | bytes 4194304 | tf_op jit(solution)/shard_map/pallas_call | solution.py:77
  33.6 4.0 %collective-permute-done.3.refs_1_.refs_10_ = bf16[4,128,512]{2,1,0:T(8,128)(2,1)S(1)} collective-permute-done((bf16[4,128,512]{2,1,0:T(8,128)(2,1)S(1)}, bf16[4,128,512]{2,1,0:T(8,128)(2,1)S(1)}, u32[]{:S(2)}, u32[]{:S(2)}) %collective-permute-start.3) | collective-permute-done | bytes 524320 | tf_op jit(solution)/shard_map/ppermute | solution.py:436
  37.6 1.3 collective-permute-start.5
  39.8 8.4 %shard_map.78 = (bf16[4,256,2048]{2,1,0:T(8,128)(2,1)S(1)}, f32[4,1,2048]{2,1,0:T(1,128)S(1)}) custom-call(f32[1024,128]{1,0:T(8,128)S(1)} %broadcast_in_dim.44.time_ref, f32[1,1024]{1,0:T(1,128)S(1)} %bitcast.24, f32[1,1024]{1,0:T(1,128)S(1)} %bitcast.22, bf16[4,128,512]{2,1,0:T(8,128)(2,1)S(1)} %collective-permute-done.2.refs_0_.refs_9_, ...), custom_call_target="tpu_custom_call" | custom-call | flops 10485760000 | bytes 4194304 | tf_op jit(solution)/shard_map/pallas_call | solution.py:77
  48.3 3.0 %collective-permute-done.5.refs_12_ = bf16[4,128,512]{2,1,0:T(8,128)(2,1)S(1)} collective-permute-done((bf16[4,128,512]{2,1,0:T(8,128)(2,1)S(1)}, bf16[4,128,512]{2,1,0:T(8,128)(2,1)S(1)}, u32[]{:S(2)}, u32[]{:S(2)}) %collective-permute-start.5) | collective-permute-done | bytes 524320 | tf_op jit(solution)/shard_map/ppermute | solution.py:436
  51.3 3.7 %shard_map.79 = (bf16[512,128]{1,0:T(8,128)(2,1)S(1)}, bf16[512,128]{1,0:T(8,128)(2,1)S(1)}, bf16[512,128]{1,0:T(8,128)(2,1)S(1)}, bf16[512,128]{1,0:T(8,128)(2,...) custom-call(s32[4096]{0:T(1024)S(1)} %bitcast.18, ...), custom_call_target="tpu_custom_call" | custom-call | flops 4294967296 | bytes 16777216 | tf_op jit(solution)/shard_map/pallas_call | solution.py:359
  55.0 2.5 %collective-permute-start.6 = (bf16[512,128]{1,0:T(8,128)(2,1)S(1)}, bf16[512,128]{1,0:T(8,128)(2,1)S(1)}, u32[]{:S(2)}, u32[]{:S(2)}) collective-permute-start(bf16[512,128]{1,0:T(8,128)(2,1)S(1)} %get-tuple-element.43), channel_id=1, source_target_pairs={{0,4},{4,0},{8,12},{12,8},{16,20},{20,16},{24,28},{28,24},{1,5},{5... | collective-permute-start | bytes 393224 | tf_op jit(solution)/shard_map/ppermute | solution.py:425
  57.5 1.8 %collective-permute-start.7 = (bf16[512,128]{1,0:T(8,128)(2,1)S(1)}, bf16[512,128]{1,0:T(8,128)(2,1)S(1)}, u32[]{:S(2)}, u32[]{:S(2)}) collective-permute-start(bf16[512,128]{1,0:T(8,128)(2,1)S(1)} %get-tuple-element.44), channel_id=1, source_target_pairs={{0,8},{4,12},{8,0},{12,4},{16,24},{20,28},{24,16},{28,20},{1,9},{5... | collective-permute-start | bytes 393224 | tf_op jit(solution)/shard_map/ppermute | solution.py:425
  59.5 1.8 %collective-permute-start.9 = (bf16[512,128]{1,0:T(8,128)(2,1)S(1)}, bf16[512,128]{1,0:T(8,128)(2,1)S(1)}, u32[]{:S(2)}, u32[]{:S(2)}) collective-permute-start(bf16[512,128]{1,0:T(8,128)(2,1)S(1)} %get-tuple-element.46), channel_id=1, source_target_pairs={{0,16},{4,20},{8,24},{12,28},{16,0},{20,4},{24,8},{28,12},{1,17},{... | collective-permute-start | bytes 393224 | tf_op jit(solution)/shard_map/ppermute | solution.py:425
  61.5 1.3 collective-permute-start.11
  63.1 2.1 %collective-permute-start.12 = (bf16[512,128]{1,0:T(8,128)(2,1)S(1)}, bf16[512,128]{1,0:T(8,128)(2,1)S(1)}, u32[]{:S(2)}, u32[]{:S(2)}) collective-permute-start(bf16[512,128]{1,0:T(8,128)(2,1)S(1)} %get-tuple-element.49), channel_id=1, source_target_pairs={{0,28},{4,24},{8,20},{12,16},{16,12},{20,8},{24,4},{28,0},{1,29},{... | collective-permute-start | bytes 393224 | tf_op jit(solution)/shard_map/ppermute | solution.py:425
  65.1 1.2 collective-permute-done.8.refs_3_
  66.4 7.1 %collective-permute-done.10.refs_5_ = bf16[512,128]{1,0:T(8,128)(2,1)S(1)} collective-permute-done((bf16[512,128]{1,0:T(8,128)(2,1)S(1)}, bf16[512,128]{1,0:T(8,128)(2,1)S(1)}, u32[]{:S(2)}, u32[]{:S(2)}) %collective-permute-start.10) | collective-permute-done | bytes 131104 | tf_op jit(solution)/shard_map/ppermute | solution.py:425
  73.5 8.6 %shard_map.80 = (bf16[512,128]{1,0:T(8,128)(2,1)S(1)}, bf16[512,128]{1,0:T(8,128)(2,1)S(1)}, bf16[512,128]{1,0:T(8,128)(2,1)S(1)}, bf16[512,128]{1,0:T(8,128)(2,...) custom-call(s32[8,24]{1,0:T(8,128)S(1)} %get-tuple-element.94.src_re, ...), custom_call_target="tpu_custom_call" | custom-call | flops 10737418240 | bytes 8388608 | tf_op jit(solution)/shard_map/pallas_call | solution.py:200
  82.4 1.3 collective-permute-start.14
  84.3 1.5 collective-permute-start.16
  86.0 1.3 collective-permute-start.18
  87.2 2.7 %collective-permute-start.19 = (bf16[512,128]{1,0:T(8,128)(2,1)S(1)}, bf16[512,128]{1,0:T(8,128)(2,1)S(1)}, u32[]{:S(2)}, u32[]{:S(2)}) collective-permute-start(bf16[512,128]{1,0:T(8,128)(2,1)S(1)} %get-tuple-element.59), channel_id=1, source_target_pairs={{0,28},{4,24},{8,20},{12,16},{16,12},{20,8},{24,4},{28,0},{1,29},{... | collective-permute-start | bytes 393224 | tf_op jit(solution)/shard_map/ppermute | solution.py:425
  90.0 1.5 collective-permute-done.15.refs_16_
  91.4 6.5 %collective-permute-done.17.refs_18_ = bf16[512,128]{1,0:T(8,128)(2,1)S(1)} collective-permute-done((bf16[512,128]{1,0:T(8,128)(2,1)S(1)}, bf16[512,128]{1,0:T(8,128)(2,1)S(1)}, u32[]{:S(2)}, u32[]{:S(2)}) %collective-permute-start.17) | collective-permute-done | bytes 131104 | tf_op jit(solution)/shard_map/ppermute | solution.py:425
  98.0 7.5 %shard_map.81 = (f32[4,512,256]{2,1,0:T(8,128)S(1)}, bf16[512,128]{1,0:T(8,128)(2,1)S(1)}, bf16[512,128]{1,0:T(8,128)(2,1)S(1)}, bf16[512,128]{1,0:T(8,128)(2,1)...) custom-call(s32[4096]{0:T(1024)S(1)} %bitcast.19, ...), custom_call_target="tpu_custom_call" | custom-call | flops 4294967296 | bytes 16777216 | tf_op jit(solution)/shard_map/pallas_call | solution.py:359
  105.5 1.3 copy-done.3
  106.9 4.2 %collective-permute-start.21 = (bf16[512,128]{1,0:T(8,128)(2,1)S(1)}, bf16[512,128]{1,0:T(8,128)(2,1)S(1)}, u32[]{:S(2)}, u32[]{:S(2)}) collective-permute-start(bf16[512,128]{1,0:T(8,128)(2,1)S(1)} %get-tuple-element.63), channel_id=1, source_target_pairs={{0,8},{4,12},{8,0},{12,4},{16,24},{20,28},{24,16},{28,20},{1,9},{5... | collective-permute-start | bytes 393224 | tf_op jit(solution)/shard_map/ppermute | solution.py:425
  111.6 0.7 collective-permute-start.23
  112.3 1.3 collective-permute-start.24
  113.6 0.9 collective-permute-start.25
  114.5 1.8 %collective-permute-start.26 = (bf16[512,128]{1,0:T(8,128)(2,1)S(1)}, bf16[512,128]{1,0:T(8,128)(2,1)S(1)}, u32[]{:S(2)}, u32[]{:S(2)}) collective-permute-start(bf16[512,128]{1,0:T(8,128)(2,1)S(1)} %get-tuple-element.68), channel_id=1, source_target_pairs={{0,28},{4,24},{8,20},{12,16},{16,12},{20,8},{24,4},{28,0},{1,29},{... | collective-permute-start | bytes 393224 | tf_op jit(solution)/shard_map/ppermute | solution.py:425
  116.3 2.3 %collective-permute-done.22.refs_3_ = bf16[512,128]{1,0:T(8,128)(2,1)S(1)} collective-permute-done((bf16[512,128]{1,0:T(8,128)(2,1)S(1)}, bf16[512,128]{1,0:T(8,128)(2,1)S(1)}, u32[]{:S(2)}, u32[]{:S(2)}) %collective-permute-start.22) | collective-permute-done | bytes 131104 | tf_op jit(solution)/shard_map/ppermute | solution.py:425
  118.7 6.6 %collective-permute-done.24.refs_5_ = bf16[512,128]{1,0:T(8,128)(2,1)S(1)} collective-permute-done((bf16[512,128]{1,0:T(8,128)(2,1)S(1)}, bf16[512,128]{1,0:T(8,128)(2,1)S(1)}, u32[]{:S(2)}, u32[]{:S(2)}) %collective-permute-start.24) | collective-permute-done | bytes 131104 | tf_op jit(solution)/shard_map/ppermute | solution.py:425
  125.2 7.9 %shard_map.82 = (bf16[512,128]{1,0:T(8,128)(2,1)S(1)}, bf16[512,128]{1,0:T(8,128)(2,1)S(1)}, bf16[512,128]{1,0:T(8,128)(2,1)S(1)}, bf16[512,128]{1,0:T(8,128)(2,...) custom-call(s32[8,24]{1,0:T(8,128)S(1)} %get-tuple-element.94.src_re, ...), custom_call_target="tpu_custom_call" | custom-call | flops 10737418240 | bytes 8388608 | tf_op jit(solution)/shard_map/pallas_call | solution.py:200
  133.2 2.2 %collective-permute-start.28 = (bf16[512,128]{1,0:T(8,128)(2,1)S(1)}, bf16[512,128]{1,0:T(8,128)(2,1)S(1)}, u32[]{:S(2)}, u32[]{:S(2)}) collective-permute-start(bf16[512,128]{1,0:T(8,128)(2,1)S(1)} %get-tuple-element.71), channel_id=1, source_target_pairs={{0,8},{4,12},{8,0},{12,4},{16,24},{20,28},{24,16},{28,20},{1,9},{5... | collective-permute-start | bytes 393224 | tf_op jit(solution)/shard_map/ppermute | solution.py:425
  136.1 1.4 collective-permute-start.31
  137.5 1.3 collective-permute-start.32
  139.2 2.3 %collective-permute-start.33 = (bf16[512,128]{1,0:T(8,128)(2,1)S(1)}, bf16[512,128]{1,0:T(8,128)(2,1)S(1)}, u32[]{:S(2)}, u32[]{:S(2)}) collective-permute-start(bf16[512,128]{1,0:T(8,128)(2,1)S(1)} %get-tuple-element.76), channel_id=1, source_target_pairs={{0,28},{4,24},{8,20},{12,16},{16,12},{20,8},{24,4},{28,0},{1,29},{... | collective-permute-start | bytes 393224 | tf_op jit(solution)/shard_map/ppermute | solution.py:425
  141.5 0.8 reduce.1
  142.6 6.6 %collective-permute-done.31.refs_11_ = bf16[512,128]{1,0:T(8,128)(2,1)S(1)} collective-permute-done((bf16[512,128]{1,0:T(8,128)(2,1)S(1)}, bf16[512,128]{1,0:T(8,128)(2,1)S(1)}, u32[]{:S(2)}, u32[]{:S(2)}) %collective-permute-start.31) | collective-permute-done | bytes 131104 | tf_op jit(solution)/shard_map/ppermute | solution.py:425
  149.2 1.6 %copy-done.4 = f32[4,512,256]{2,1,0:T(8,128)S(1)} copy-done((f32[4,512,256]{2,1,0:T(8,128)S(1)}, f32[4,512,256]{2,1,0:T(8,128)}, u32[]{:S(2)}) %copy-start.4) | copy-done | bytes 2097176
  150.8 5.7 %shard_map.83 = f32[4,512,256]{2,1,0:T(8,128)} custom-call(s32[4096]{0:T(1024)S(1)} %bitcast.20, s32[8]{0:T(128)S(1)} %convert_reduce_fusion.2.refs_1_, s32[4]{0:T(128)S(1)} %copy-done.2, s32[2]{0:T(128)S(1)} %pad_add_fusion.refs_3_, f32[8,1,2048]{2,1,0:T(1,128)S(1)} %constant_dynamic-update-slice_fusion.refs_4_.refs_10_, f32[4,512,256]{2,1,0:T(8,128)S(1)} %copy-done.4, ...), custom_call_target="tpu_custom_call" | custom-call | flops 4294967296 | bytes 16777216 | tf_op jit(solution)/shard_map/pallas_call | solution.py:359
  (70 shorter events, 8.3 us)
Async XLA Ops:
  0.6 22.4 %collective-permute-start.1 = (bf16[4,128,512]{2,1,0:T(8,128)(2,1)}, bf16[4,128,512]{2,1,0:T(8,128)(2,1)S(1)}, u32[]{:S(2)}, u32[]{:S(2)}) collective-permute-start(bf16[4,128,512]{2,1,0:T(8,128)(2,1)} %refs_6_.3), channel_id=1, source_target_pairs={{1,0},{2,1},{3,2},{5,4},{6,5},{7,6},{9,8},{10,9},{11,10},{13,12},{... | collective-permute-start | bytes 1572872 | tf_op jit(solution)/shard_map/ppermute | solution.py:436
  1.9 22.4 %collective-permute-start = (bf16[4,128,512]{2,1,0:T(8,128)(2,1)}, bf16[4,128,512]{2,1,0:T(8,128)(2,1)S(1)}, u32[]{:S(2)}, u32[]{:S(2)}) collective-permute-start(bf16[4,128,512]{2,1,0:T(8,128)(2,1)} %refs_6_.3), channel_id=1, source_target_pairs={{0,1},{1,2},{2,3},{4,5},{5,6},{6,7},{8,9},{9,10},{10,11},{12,13},{... | collective-permute-start | bytes 1572872 | tf_op jit(solution)/shard_map/ppermute | solution.py:435
  13.7 9.1 %all-to-all-start = ((s32[8,1,512]{2,1,0:T(1,128)}), s32[8,1,512]{2,1,0:T(1,128)S(1)}, u32[]{:S(2)}, u32[]{:S(2)}) async-start(s32[8,1,512]{2,1,0:T(1,128)} %bitcast), calls=%async_computation | async-start | bytes 32768 | tf_op jit(solution)/shard_map/all_to_all | solution.py:452
  23.0 14.6 %collective-permute-start.3 = (bf16[4,128,512]{2,1,0:T(8,128)(2,1)S(1)}, bf16[4,128,512]{2,1,0:T(8,128)(2,1)S(1)}, u32[]{:S(2)}, u32[]{:S(2)}) collective-permute-start(bf16[4,128,512]{2,1,0:T(8,128)(2,1)S(1)} %collective-permute-done.1.refs_1_.refs_8_), channel_id=1, source_target_pairs={{1,0},{2,1},{5,4},{6,5},{9,8},{10,9},{13,12},{14,13},{17,16},{18,1... | collective-permute-start | bytes 1572872 | tf_op jit(solution)/shard_map/ppermute | solution.py:436
  24.3 14.6 %collective-permute-start.2 = (bf16[4,128,512]{2,1,0:T(8,128)(2,1)S(1)}, bf16[4,128,512]{2,1,0:T(8,128)(2,1)S(1)}, u32[]{:S(2)}, u32[]{:S(2)}) collective-permute-start(bf16[4,128,512]{2,1,0:T(8,128)(2,1)S(1)} %collective-permute-done.refs_0_.refs_7_), channel_id=1, source_target_pairs={{1,2},{2,3},{5,6},{6,7},{9,10},{10,11},{13,14},{14,15},{17,18},{18... | collective-permute-start | bytes 1572872 | tf_op jit(solution)/shard_map/ppermute | solution.py:435
  37.6 13.7 %collective-permute-start.5 = (bf16[4,128,512]{2,1,0:T(8,128)(2,1)S(1)}, bf16[4,128,512]{2,1,0:T(8,128)(2,1)S(1)}, u32[]{:S(2)}, u32[]{:S(2)}) collective-permute-start(bf16[4,128,512]{2,1,0:T(8,128)(2,1)S(1)} %collective-permute-done.3.refs_1_.refs_10_), channel_id=1, source_target_pairs={{1,0},{5,4},{9,8},{13,12},{17,16},{21,20},{25,24},{29,28}} | collective-permute-start | bytes 1572872 | tf_op jit(solution)/shard_map/ppermute | solution.py:436
  38.9 12.4 %collective-permute-start.4 = (bf16[4,128,512]{2,1,0:T(8,128)(2,1)S(1)}, bf16[4,128,512]{2,1,0:T(8,128)(2,1)S(1)}, u32[]{:S(2)}, u32[]{:S(2)}) collective-permute-start(bf16[4,128,512]{2,1,0:T(8,128)(2,1)S(1)} %collective-permute-done.2.refs_0_.refs_9_), channel_id=1, source_target_pairs={{2,3},{6,7},{10,11},{14,15},{18,19},{22,23},{26,27},{30,31}} | collective-permute-start | bytes 1572872 | tf_op jit(solution)/shard_map/ppermute | solution.py:435
  39.8 11.5 %copy-start = (bf16[4,512,256]{2,1,0:T(8,128)(2,1)S(1)}, bf16[4,512,256]{2,1,0:T(8,128)(2,1)}, u32[]{:S(2)}) copy-start(bf16[4,512,256]{2,1,0:T(8,128)(2,1)} %refs_5_.3) | copy-start | bytes 3145732
  39.8 11.5 %copy-start.1 = (bf16[4,128,512]{2,1,0:T(8,128)(2,1)S(1)}, bf16[4,128,512]{2,1,0:T(8,128)(2,1)}, u32[]{:S(2)}) copy-start(bf16[4,128,512]{2,1,0:T(8,128)(2,1)} %refs_6_.3) | copy-start | bytes 1572868
  39.8 11.5 %copy-start.2 = (s32[4]{0:T(128)S(1)}, s32[4]{0:T(128)}, u32[]{:S(2)}) copy-start(s32[4]{0:T(128)} %refs_2_.5) | copy-start | bytes 52
  55.0 6.5 %collective-permute-start.6 = (bf16[512,128]{1,0:T(8,128)(2,1)S(1)}, bf16[512,128]{1,0:T(8,128)(2,1)S(1)}, u32[]{:S(2)}, u32[]{:S(2)}) collective-permute-start(bf16[512,128]{1,0:T(8,128)(2,1)S(1)} %get-tuple-element.43), channel_id=1, source_target_pairs={{0,4},{4,0},{8,12},{12,8},{16,20},{20,16},{24,28},{28,24},{1,5},{5... | collective-permute-start | bytes 393224 | tf_op jit(solution)/shard_map/ppermute | solution.py:425
  57.5 5.5 %collective-permute-start.7 = (bf16[512,128]{1,0:T(8,128)(2,1)S(1)}, bf16[512,128]{1,0:T(8,128)(2,1)S(1)}, u32[]{:S(2)}, u32[]{:S(2)}) collective-permute-start(bf16[512,128]{1,0:T(8,128)(2,1)S(1)} %get-tuple-element.44), channel_id=1, source_target_pairs={{0,8},{4,12},{8,0},{12,4},{16,24},{20,28},{24,16},{28,20},{1,9},{5... | collective-permute-start | bytes 393224 | tf_op jit(solution)/shard_map/ppermute | solution.py:425
  59.4 7.0 %collective-permute-start.8 = (bf16[512,128]{1,0:T(8,128)(2,1)S(1)}, bf16[512,128]{1,0:T(8,128)(2,1)S(1)}, u32[]{:S(2)}, u32[]{:S(2)}) collective-permute-start(bf16[512,128]{1,0:T(8,128)(2,1)S(1)} %get-tuple-element.45), channel_id=1, source_target_pairs={{0,12},{4,8},{8,4},{12,0},{16,28},{20,24},{24,20},{28,16},{1,13},{... | collective-permute-start | bytes 393224 | tf_op jit(solution)/shard_map/ppermute | solution.py:425
  59.5 6.9 %collective-permute-start.9 = (bf16[512,128]{1,0:T(8,128)(2,1)S(1)}, bf16[512,128]{1,0:T(8,128)(2,1)S(1)}, u32[]{:S(2)}, u32[]{:S(2)}) collective-permute-start(bf16[512,128]{1,0:T(8,128)(2,1)S(1)} %get-tuple-element.46), channel_id=1, source_target_pairs={{0,16},{4,20},{8,24},{12,28},{16,0},{20,4},{24,8},{28,12},{1,17},{... | collective-permute-start | bytes 393224 | tf_op jit(solution)/shard_map/ppermute | solution.py:425
  61.3 12.2 %collective-permute-start.10 = (bf16[512,128]{1,0:T(8,128)(2,1)S(1)}, bf16[512,128]{1,0:T(8,128)(2,1)S(1)}, u32[]{:S(2)}, u32[]{:S(2)}) collective-permute-start(bf16[512,128]{1,0:T(8,128)(2,1)S(1)} %get-tuple-element.47), channel_id=1, source_target_pairs={{0,20},{4,16},{8,28},{12,24},{16,4},{20,0},{24,12},{28,8},{1,21},{... | collective-permute-start | bytes 393224 | tf_op jit(solution)/shard_map/ppermute | solution.py:425
  61.5 11.9 %collective-permute-start.11 = (bf16[512,128]{1,0:T(8,128)(2,1)S(1)}, bf16[512,128]{1,0:T(8,128)(2,1)S(1)}, u32[]{:S(2)}, u32[]{:S(2)}) collective-permute-start(bf16[512,128]{1,0:T(8,128)(2,1)S(1)} %get-tuple-element.48), channel_id=1, source_target_pairs={{0,24},{4,28},{8,16},{12,20},{16,8},{20,12},{24,0},{28,4},{1,25},{... | collective-permute-start | bytes 393224 | tf_op jit(solution)/shard_map/ppermute | solution.py:425
  63.1 10.4 %collective-permute-start.12 = (bf16[512,128]{1,0:T(8,128)(2,1)S(1)}, bf16[512,128]{1,0:T(8,128)(2,1)S(1)}, u32[]{:S(2)}, u32[]{:S(2)}) collective-permute-start(bf16[512,128]{1,0:T(8,128)(2,1)S(1)} %get-tuple-element.49), channel_id=1, source_target_pairs={{0,28},{4,24},{8,20},{12,16},{16,12},{20,8},{24,4},{28,0},{1,29},{... | collective-permute-start | bytes 393224 | tf_op jit(solution)/shard_map/ppermute | solution.py:425
  82.1 3.9 %collective-permute-start.13 = (bf16[512,128]{1,0:T(8,128)(2,1)S(1)}, bf16[512,128]{1,0:T(8,128)(2,1)S(1)}, u32[]{:S(2)}, u32[]{:S(2)}) collective-permute-start(bf16[512,128]{1,0:T(8,128)(2,1)S(1)} %get-tuple-element.53), channel_id=1, source_target_pairs={{0,4},{4,0},{8,12},{12,8},{16,20},{20,16},{24,28},{28,24},{1,5},{5... | collective-permute-start | bytes 393224 | tf_op jit(solution)/shard_map/ppermute | solution.py:425
  82.4 4.9 %collective-permute-start.14 = (bf16[512,128]{1,0:T(8,128)(2,1)S(1)}, bf16[512,128]{1,0:T(8,128)(2,1)S(1)}, u32[]{:S(2)}, u32[]{:S(2)}) collective-permute-start(bf16[512,128]{1,0:T(8,128)(2,1)S(1)} %get-tuple-element.54), channel_id=1, source_target_pairs={{0,8},{4,12},{8,0},{12,4},{16,24},{20,28},{24,16},{28,20},{1,9},{5... | collective-permute-start | bytes 393224 | tf_op jit(solution)/shard_map/ppermute | solution.py:425
  83.6 7.8 %collective-permute-start.15 = (bf16[512,128]{1,0:T(8,128)(2,1)S(1)}, bf16[512,128]{1,0:T(8,128)(2,1)S(1)}, u32[]{:S(2)}, u32[]{:S(2)}) collective-permute-start(bf16[512,128]{1,0:T(8,128)(2,1)S(1)} %get-tuple-element.55), channel_id=1, source_target_pairs={{0,12},{4,8},{8,4},{12,0},{16,28},{20,24},{24,20},{28,16},{1,13},{... | collective-permute-start | bytes 393224 | tf_op jit(solution)/shard_map/ppermute | solution.py:425
  84.3 7.1 %collective-permute-start.16 = (bf16[512,128]{1,0:T(8,128)(2,1)S(1)}, bf16[512,128]{1,0:T(8,128)(2,1)S(1)}, u32[]{:S(2)}, u32[]{:S(2)}) collective-permute-start(bf16[512,128]{1,0:T(8,128)(2,1)S(1)} %get-tuple-element.56), channel_id=1, source_target_pairs={{0,16},{4,20},{8,24},{12,28},{16,0},{20,4},{24,8},{28,12},{1,17},{... | collective-permute-start | bytes 393224 | tf_op jit(solution)/shard_map/ppermute | solution.py:425
  85.8 12.2 %collective-permute-start.17 = (bf16[512,128]{1,0:T(8,128)(2,1)S(1)}, bf16[512,128]{1,0:T(8,128)(2,1)S(1)}, u32[]{:S(2)}, u32[]{:S(2)}) collective-permute-start(bf16[512,128]{1,0:T(8,128)(2,1)S(1)} %get-tuple-element.57), channel_id=1, source_target_pairs={{0,20},{4,16},{8,28},{12,24},{16,4},{20,0},{24,12},{28,8},{1,21},{... | collective-permute-start | bytes 393224 | tf_op jit(solution)/shard_map/ppermute | solution.py:425
  86.0 12.0 %collective-permute-start.18 = (bf16[512,128]{1,0:T(8,128)(2,1)S(1)}, bf16[512,128]{1,0:T(8,128)(2,1)S(1)}, u32[]{:S(2)}, u32[]{:S(2)}) collective-permute-start(bf16[512,128]{1,0:T(8,128)(2,1)S(1)} %get-tuple-element.58), channel_id=1, source_target_pairs={{0,24},{4,28},{8,16},{12,20},{16,8},{20,12},{24,0},{28,4},{1,25},{... | collective-permute-start | bytes 393224 | tf_op jit(solution)/shard_map/ppermute | solution.py:425
  87.2 10.7 %collective-permute-start.19 = (bf16[512,128]{1,0:T(8,128)(2,1)S(1)}, bf16[512,128]{1,0:T(8,128)(2,1)S(1)}, u32[]{:S(2)}, u32[]{:S(2)}) collective-permute-start(bf16[512,128]{1,0:T(8,128)(2,1)S(1)} %get-tuple-element.59), channel_id=1, source_target_pairs={{0,28},{4,24},{8,20},{12,16},{16,12},{20,8},{24,4},{28,0},{1,29},{... | collective-permute-start | bytes 393224 | tf_op jit(solution)/shard_map/ppermute | solution.py:425
  105.5 1.3 copy-start.3
  106.8 6.7 %collective-permute-start.20 = (bf16[512,128]{1,0:T(8,128)(2,1)S(1)}, bf16[512,128]{1,0:T(8,128)(2,1)S(1)}, u32[]{:S(2)}, u32[]{:S(2)}) collective-permute-start(bf16[512,128]{1,0:T(8,128)(2,1)S(1)} %get-tuple-element.62), channel_id=1, source_target_pairs={{0,4},{4,0},{8,12},{12,8},{16,20},{20,16},{24,28},{28,24},{1,5},{5... | collective-permute-start | bytes 393224 | tf_op jit(solution)/shard_map/ppermute | solution.py:425
  106.9 7.6 %collective-permute-start.21 = (bf16[512,128]{1,0:T(8,128)(2,1)S(1)}, bf16[512,128]{1,0:T(8,128)(2,1)S(1)}, u32[]{:S(2)}, u32[]{:S(2)}) collective-permute-start(bf16[512,128]{1,0:T(8,128)(2,1)S(1)} %get-tuple-element.63), channel_id=1, source_target_pairs={{0,8},{4,12},{8,0},{12,4},{16,24},{20,28},{24,16},{28,20},{1,9},{5... | collective-permute-start | bytes 393224 | tf_op jit(solution)/shard_map/ppermute | solution.py:425
  111.1 7.5 %collective-permute-start.22 = (bf16[512,128]{1,0:T(8,128)(2,1)S(1)}, bf16[512,128]{1,0:T(8,128)(2,1)S(1)}, u32[]{:S(2)}, u32[]{:S(2)}) collective-permute-start(bf16[512,128]{1,0:T(8,128)(2,1)S(1)} %get-tuple-element.64), channel_id=1, source_target_pairs={{0,12},{4,8},{8,4},{12,0},{16,28},{20,24},{24,20},{28,16},{1,13},{... | collective-permute-start | bytes 393224 | tf_op jit(solution)/shard_map/ppermute | solution.py:425
  111.6 7.1 %collective-permute-start.23 = (bf16[512,128]{1,0:T(8,128)(2,1)S(1)}, bf16[512,128]{1,0:T(8,128)(2,1)S(1)}, u32[]{:S(2)}, u32[]{:S(2)}) collective-permute-start(bf16[512,128]{1,0:T(8,128)(2,1)S(1)} %get-tuple-element.65), channel_id=1, source_target_pairs={{0,16},{4,20},{8,24},{12,28},{16,0},{20,4},{24,8},{28,12},{1,17},{... | collective-permute-start | bytes 393224 | tf_op jit(solution)/shard_map/ppermute | solution.py:425
  112.3 12.9 %collective-permute-start.24 = (bf16[512,128]{1,0:T(8,128)(2,1)S(1)}, bf16[512,128]{1,0:T(8,128)(2,1)S(1)}, u32[]{:S(2)}, u32[]{:S(2)}) collective-permute-start(bf16[512,128]{1,0:T(8,128)(2,1)S(1)} %get-tuple-element.66), channel_id=1, source_target_pairs={{0,20},{4,16},{8,28},{12,24},{16,4},{20,0},{24,12},{28,8},{1,21},{... | collective-permute-start | bytes 393224 | tf_op jit(solution)/shard_map/ppermute | solution.py:425
  113.6 11.7 %collective-permute-start.25 = (bf16[512,128]{1,0:T(8,128)(2,1)S(1)}, bf16[512,128]{1,0:T(8,128)(2,1)S(1)}, u32[]{:S(2)}, u32[]{:S(2)}) collective-permute-start(bf16[512,128]{1,0:T(8,128)(2,1)S(1)} %get-tuple-element.67), channel_id=1, source_target_pairs={{0,24},{4,28},{8,16},{12,20},{16,8},{20,12},{24,0},{28,4},{1,25},{... | collective-permute-start | bytes 393224 | tf_op jit(solution)/shard_map/ppermute | solution.py:425
  114.5 10.7 %collective-permute-start.26 = (bf16[512,128]{1,0:T(8,128)(2,1)S(1)}, bf16[512,128]{1,0:T(8,128)(2,1)S(1)}, u32[]{:S(2)}, u32[]{:S(2)}) collective-permute-start(bf16[512,128]{1,0:T(8,128)(2,1)S(1)} %get-tuple-element.68), channel_id=1, source_target_pairs={{0,28},{4,24},{8,20},{12,16},{16,12},{20,8},{24,4},{28,0},{1,29},{... | collective-permute-start | bytes 393224 | tf_op jit(solution)/shard_map/ppermute | solution.py:425
  133.2 4.4 %collective-permute-start.27 = (bf16[512,128]{1,0:T(8,128)(2,1)S(1)}, bf16[512,128]{1,0:T(8,128)(2,1)S(1)}, u32[]{:S(2)}, u32[]{:S(2)}) collective-permute-start(bf16[512,128]{1,0:T(8,128)(2,1)S(1)} %get-tuple-element.70), channel_id=1, source_target_pairs={{0,4},{4,0},{8,12},{12,8},{16,20},{20,16},{24,28},{28,24},{1,5},{5... | collective-permute-start | bytes 393224 | tf_op jit(solution)/shard_map/ppermute | solution.py:425
  133.2 6.0 %collective-permute-start.28 = (bf16[512,128]{1,0:T(8,128)(2,1)S(1)}, bf16[512,128]{1,0:T(8,128)(2,1)S(1)}, u32[]{:S(2)}, u32[]{:S(2)}) collective-permute-start(bf16[512,128]{1,0:T(8,128)(2,1)S(1)} %get-tuple-element.71), channel_id=1, source_target_pairs={{0,8},{4,12},{8,0},{12,4},{16,24},{20,28},{24,16},{28,20},{1,9},{5... | collective-permute-start | bytes 393224 | tf_op jit(solution)/shard_map/ppermute | solution.py:425
  135.5 7.1 %collective-permute-start.29 = (bf16[512,128]{1,0:T(8,128)(2,1)S(1)}, bf16[512,128]{1,0:T(8,128)(2,1)S(1)}, u32[]{:S(2)}, u32[]{:S(2)}) collective-permute-start(bf16[512,128]{1,0:T(8,128)(2,1)S(1)} %get-tuple-element.72), channel_id=1, source_target_pairs={{0,12},{4,8},{8,4},{12,0},{16,28},{20,24},{24,20},{28,16},{1,13},{... | collective-permute-start | bytes 393224 | tf_op jit(solution)/shard_map/ppermute | solution.py:425
  135.5 7.1 %collective-permute-start.30 = (bf16[512,128]{1,0:T(8,128)(2,1)S(1)}, bf16[512,128]{1,0:T(8,128)(2,1)S(1)}, u32[]{:S(2)}, u32[]{:S(2)}) collective-permute-start(bf16[512,128]{1,0:T(8,128)(2,1)S(1)} %get-tuple-element.73), channel_id=1, source_target_pairs={{0,16},{4,20},{8,24},{12,28},{16,0},{20,4},{24,8},{28,12},{1,17},{... | collective-permute-start | bytes 393224 | tf_op jit(solution)/shard_map/ppermute | solution.py:425
  136.1 13.1 %collective-permute-start.31 = (bf16[512,128]{1,0:T(8,128)(2,1)S(1)}, bf16[512,128]{1,0:T(8,128)(2,1)S(1)}, u32[]{:S(2)}, u32[]{:S(2)}) collective-permute-start(bf16[512,128]{1,0:T(8,128)(2,1)S(1)} %get-tuple-element.74), channel_id=1, source_target_pairs={{0,20},{4,16},{8,28},{12,24},{16,4},{20,0},{24,12},{28,8},{1,21},{... | collective-permute-start | bytes 393224 | tf_op jit(solution)/shard_map/ppermute | solution.py:425
  137.5 11.6 %collective-permute-start.32 = (bf16[512,128]{1,0:T(8,128)(2,1)S(1)}, bf16[512,128]{1,0:T(8,128)(2,1)S(1)}, u32[]{:S(2)}, u32[]{:S(2)}) collective-permute-start(bf16[512,128]{1,0:T(8,128)(2,1)S(1)} %get-tuple-element.75), channel_id=1, source_target_pairs={{0,24},{4,28},{8,16},{12,20},{16,8},{20,12},{24,0},{28,4},{1,25},{... | collective-permute-start | bytes 393224 | tf_op jit(solution)/shard_map/ppermute | solution.py:425
  139.2 10.0 %collective-permute-start.33 = (bf16[512,128]{1,0:T(8,128)(2,1)S(1)}, bf16[512,128]{1,0:T(8,128)(2,1)S(1)}, u32[]{:S(2)}, u32[]{:S(2)}) collective-permute-start(bf16[512,128]{1,0:T(8,128)(2,1)S(1)} %get-tuple-element.76), channel_id=1, source_target_pairs={{0,28},{4,24},{8,20},{12,16},{16,12},{20,8},{24,4},{28,0},{1,29},{... | collective-permute-start | bytes 393224 | tf_op jit(solution)/shard_map/ppermute | solution.py:425
  149.2 1.6 %copy-start.4 = (f32[4,512,256]{2,1,0:T(8,128)S(1)}, f32[4,512,256]{2,1,0:T(8,128)}, u32[]{:S(2)}) copy-start(f32[4,512,256]{2,1,0:T(8,128)} %copy-done.3) | copy-start | bytes 6291460

commit v5 on v4

--- a/solution.py
+++ b/solution.py
@@ -10,12 +10,14 @@
 SRC_GROUP = 128
 ITERS = 2
 STREAMS = 4
+LATE_STREAMS = 2
 STEP = 16
 BETA = 2.0
 RIDGE = 1.0
 VMEM_LIMIT = 24 * 1024 * 1024
-BASIS_CALLS = 2
+BASIS_CALLS = 4
 UNROLL = 16
+COST_US = 10 ** 9
 
 COS_POLY = (1.0, -19.73920440673828, 64.9391098022461, -85.4500503540039, 60.16689682006836,
             -25.96480369567871, 6.52468729019165)
@@ -23,6 +25,8 @@
             41.33811950683594, -12.463061332702637)
 
 VMEM = pl.BlockSpec(memory_space=pltpu.VMEM)
+HBM = pl.BlockSpec(memory_space=pltpu.HBM)
+ANY = pl.BlockSpec(memory_space=pl.ANY)
 SMEM = pl.BlockSpec(memory_space=pltpu.SMEM)
 
 
@@ -81,7 +85,7 @@
             pl.BlockSpec((obs, SRC_GROUP), lambda j: (j, 0)),
             pl.BlockSpec((1, nper), lambda j: (0, 0)),
             pl.BlockSpec((1, nper), lambda j: (0, 0)),
-        ] + [pl.BlockSpec(memory_space=pl.ANY)] * len(after),
+        ] + [ANY] * len(after),
         out_specs=[
             pl.BlockSpec((1, obs, 2 * nper), lambda j: (j, 0, 0)),
             pl.BlockSpec((1, 1, 2 * nper), lambda j: (j, 0, 0)),
@@ -199,7 +203,7 @@
     ]
     *models, score = pl.pallas_call(
         functools.partial(fit_kernel, tm_count),
-        in_specs=[SMEM, SMEM] + [VMEM] * tm_count + [pl.BlockSpec(memory_space=pl.ANY)] * len(parts) + [VMEM],
+        in_specs=[SMEM, SMEM] + [VMEM] * tm_count + [ANY] * len(parts) + [VMEM],
         out_specs=[VMEM] * (tm_count + 1),
         out_shape=[jax.ShapeDtypeStruct((capacity, width), jnp.bfloat16)] * tm_count
         + [jax.ShapeDtypeStruct((sched_dev, width, 1), jnp.float32)],
@@ -263,16 +267,13 @@
         out_ref[...] = gather_ref[pl.ds(owner * capacity, capacity), :].astype(jnp.bfloat16)
 
 
-def place_rows(me, asked_ref, cnt_ref, returned, current_ref, out_ref, rows_ref, sums):
-    segs, slots, _ = current_ref.shape
-    capacity, width = returned[0].shape
-    blocks = current_ref.shape[2] // width
+def add_rows(me, asked_ref, cnt_ref, owners, returned, rows_ref, sums):
+    capacity = returned[0].shape[0]
     streams = len(sums)
     for total in sums:
         total[...] = jnp.zeros_like(total)
-    for owner, ref in enumerate(returned):
-        rows_ref[pl.ds(owner * capacity, capacity), :] = ref[...].astype(jnp.float32)
-
+    for number, (owner, ref) in enumerate(zip(owners, returned)):
+        rows_ref[pl.ds(number * capacity, capacity), :] = ref[...].astype(jnp.float32)
         asker = owner ^ me
 
         def step(index, carry):
@@ -281,7 +282,7 @@
                 lanes = [first + start + lane for lane in range(streams)]
                 places = [asked_ref[asker * capacity + lane] for lane in lanes]
                 values = [
-                    total[pl.ds(place, 1), :] + rows_ref[pl.ds(owner * capacity + lane, 1), :]
+                    total[pl.ds(place, 1), :] + rows_ref[pl.ds(number * capacity + lane, 1), :]
                     for total, place, lane in zip(sums, places, lanes)
                 ]
                 for total, place, value in zip(sums, places, values):
@@ -289,15 +290,86 @@
             return carry
 
         lax.fori_loop(0, (cnt_ref[asker] + UNROLL - 1) // UNROLL, step, 0)
-    for seg in range(segs):
-        for block in range(blocks):
+
+
+def placed_at(sums, at):
+    return functools.reduce(jnp.add, [total[at, :] for total in sums])
+
+
+def early_kernel(owners, table_base, asked_ref, cnt_ref, where_ref, base_ref, *refs):
+    refs = list(refs)
+    returned = [refs.pop(0) for _ in owners]
+    out_ref, rows_ref = refs.pop(0), refs.pop(0)
+    if table_base:
+        held_ref, sem = refs.pop(0), refs.pop(0)
+        copy = pltpu.make_async_copy(base_ref, held_ref, sem)
+        copy.start()
+    add_rows(where_ref[0], asked_ref, cnt_ref, owners, returned, rows_ref, refs)
+    if table_base:
+        copy.wait()
+        out_ref[...] = held_ref[...] - placed_at(refs, pl.ds(0, out_ref.shape[0]))
+        return
+    segs, slots, total_width = base_ref.shape
+    width = out_ref.shape[1]
+    for block in range(total_width // width):
+        for seg in range(segs):
             at = pl.ds((block * segs + seg) * slots, slots)
-            lanes = slice(block * width, (block + 1) * width)
-            placed = functools.reduce(jnp.add, [total[at, :] for total in sums])
-            out_ref[seg, :, lanes] = current_ref[seg, :, lanes].astype(jnp.float32) - placed
-
-
-def owner_kernel(tm_count, passed_count, placing, *refs):
+            base = base_ref[seg, :, block * width:(block + 1) * width].astype(jnp.float32)
+            out_ref[at, :] = base - placed_at(refs, at)
+
+
+def place_early(scalars, owners, base, returned, rows):
+    asked, cnt, _, where = scalars
+    table_base = base.ndim == 2
+    capacity = returned[0].shape[0]
+    sums = [pltpu.VMEM((rows + 8, SRC_GROUP), jnp.float32)] * STREAMS
+    held = [pltpu.VMEM((rows, SRC_GROUP), jnp.float32), pltpu.SemaphoreType.DMA(())] if table_base else []
+    return pl.pallas_call(
+        functools.partial(early_kernel, owners, table_base),
+        in_specs=[SMEM] * 3 + [HBM if table_base else VMEM] + [VMEM] * len(owners),
+        out_specs=VMEM,
+        out_shape=jax.ShapeDtypeStruct((rows, SRC_GROUP), jnp.float32),
+        scratch_shapes=[pltpu.VMEM((len(owners) * capacity, SRC_GROUP), jnp.float32)] + held + sums,
+        compiler_params=pltpu.CompilerParams(vmem_limit_bytes=VMEM_LIMIT),
+        cost_estimate=pl.CostEstimate(flops=6 * COST_US, bytes_accessed=1 << 20, transcendentals=0),
+    )(asked, cnt, where, base, *[returned[owner] for owner in owners])
+
+
+def pick_kernel(tm_count, passed_count, asked_ref, cnt_ref, count_ref, where_ref, base_ref, own_ref, *refs):
+    refs = list(refs)
+    passed = [refs.pop(0) for _ in range(passed_count)]
+    picked = [refs.pop(0) for _ in range(tm_count)]
+    whole_ref, sems, white_ref, gather_ref = refs
+    load_attitude(where_ref[1], own_ref, passed, whole_ref, sems)()
+    whiten_and_pick(
+        where_ref[0], asked_ref, cnt_ref, count_ref, whole_ref, lambda seg: base_ref[seg], picked, white_ref,
+        gather_ref,
+    )
+
+
+def pick_rows(scalars, base, attitude, rows):
+    asked, cnt, seg_counts, where = scalars
+    tm_count, = cnt.shape
+    seg_dev, slots, _ = base.shape
+    capacity = asked.shape[0] // tm_count
+    return pl.pallas_call(
+        functools.partial(pick_kernel, tm_count, len(attitude) - 1),
+        in_specs=[SMEM] * 4 + [VMEM] + [ANY] * len(attitude),
+        out_specs=[VMEM] * tm_count,
+        out_shape=[jax.ShapeDtypeStruct((capacity, SRC_GROUP), jnp.bfloat16)] * tm_count,
+        scratch_shapes=[
+            pltpu.VMEM((seg_dev, slots, slots), jnp.bfloat16),
+            pltpu.SemaphoreType.DMA((len(attitude),)),
+            pltpu.VMEM((rows + 8, SRC_GROUP), jnp.float32),
+            pltpu.VMEM((tm_count * capacity, SRC_GROUP), jnp.float32),
+        ],
+        compiler_params=pltpu.CompilerParams(vmem_limit_bytes=VMEM_LIMIT),
+        cost_estimate=pl.CostEstimate(flops=5 * COST_US, bytes_accessed=1 << 20, transcendentals=0),
+    )(asked, cnt, seg_counts, where, base, *attitude)
+
+
+def late_pick_kernel(tm_count, passed_count, owners, asked_ref, cnt_ref, count_ref, where_ref, part_ref, own_ref,
+                     *refs):
     refs = list(refs)
 
     def take(count):
@@ -305,71 +377,94 @@
         del refs[:count]
         return taken
 
-    asked_ref, cnt_ref, count_ref, where_ref, _, current_ref = take(6)
-    me, sky = where_ref[0], where_ref[1]
-    picking = passed_count > 0
-    if picking:
-        (own_ref,) = take(1)
-        passed = take(passed_count)
-    returned = take(tm_count) if placing else None
-    out_ref = take(1)[0] if placing else None
-    picked = take(tm_count) if picking else None
-    if picking:
-        whole_ref, sems, white_ref = take(3)
-        wait = load_attitude(sky, own_ref, passed, whole_ref, sems)
-    (rows_ref,) = take(1)
-    if placing:
-        place_rows(me, asked_ref, cnt_ref, returned, current_ref, out_ref, rows_ref, refs)
-    if picking:
-        wait()
-        source = out_ref if placing else current_ref
-        whiten_and_pick(
-            me, asked_ref, cnt_ref, count_ref, whole_ref, lambda seg: source[seg], picked, white_ref, rows_ref
+    passed = take(passed_count)
+    returned = take(len(owners))
+    (out_ref,) = take(1)
+    picked = take(tm_count)
+    whole_ref, sems, white_ref, gather_ref, table_ref, sem = take(6)
+    segs, slots, _ = whole_ref.shape
+    blocks = table_ref.shape[0] // (segs * slots)
+    wait = load_attitude(where_ref[1], own_ref, passed, whole_ref, sems)
+    add_rows(where_ref[0], asked_ref, cnt_ref, owners, returned, gather_ref, refs)
+    table_ref[...] = part_ref[...] - placed_at(refs, pl.ds(0, table_ref.shape[0]))
+    copy = pltpu.make_async_copy(table_ref, out_ref, sem)
+    copy.start()
+    wait()
+
+    def load(seg):
+        return jnp.concatenate(
+            [table_ref[pl.ds((block * segs + seg) * slots, slots), :] for block in range(blocks)], axis=1
         )
 
-
-def owner_step(scalars, norms, current, attitude, returned):
+    whiten_and_pick(
+        where_ref[0], asked_ref, cnt_ref, count_ref, whole_ref, load, picked, white_ref, gather_ref
+    )
+    copy.wait()
+
+
+def place_late_and_pick(scalars, owners, part, returned, attitude):
     asked, cnt, seg_counts, where = scalars
-    seg_dev, slots, width = current.shape
-    placing, picking = returned is not None, attitude is not None
-    tm_count = cnt.shape[0]
+    tm_count, = cnt.shape
+    seg_dev = seg_counts.shape[0]
+    slots = attitude[0].shape[2]
     capacity = asked.shape[0] // tm_count
-    table = pltpu.VMEM((seg_dev * slots * width // SRC_GROUP + 8, SRC_GROUP), jnp.float32)
-    anywhere = pl.BlockSpec(memory_space=pl.ANY)
-    in_specs = [SMEM] * 4 + [anywhere, VMEM]
-    args = [asked, cnt, seg_counts, where, norms, current]
-    out_shape = []
-    scratch = []
-    if picking:
-        args += attitude
-        in_specs += [anywhere] * len(attitude)
-        scratch += [
+    rows = part.shape[0]
+    table = pltpu.VMEM((rows + 8, SRC_GROUP), jnp.float32)
+    out = pl.pallas_call(
+        functools.partial(late_pick_kernel, tm_count, len(attitude) - 1, owners),
+        in_specs=[SMEM] * 4 + [VMEM] + [ANY] * len(attitude) + [VMEM] * len(owners),
+        out_specs=[HBM] + [VMEM] * tm_count,
+        out_shape=[jax.ShapeDtypeStruct(part.shape, jnp.float32)]
+        + [jax.ShapeDtypeStruct((capacity, SRC_GROUP), jnp.bfloat16)] * tm_count,
+        scratch_shapes=[
             pltpu.VMEM((seg_dev, slots, slots), jnp.bfloat16),
             pltpu.SemaphoreType.DMA((len(attitude),)),
             table,
-        ]
-    scratch.append(pltpu.VMEM((tm_count * capacity, SRC_GROUP), jnp.float32))
-    if placing:
-        in_specs += [VMEM] * tm_count
-        args += returned
-        out_shape.append(jax.ShapeDtypeStruct(current.shape, jnp.float32))
-        scratch += [table] * STREAMS
-    if picking:
-        out_shape += [jax.ShapeDtypeStruct((capacity, SRC_GROUP), jnp.bfloat16)] * tm_count
-    out = pl.pallas_call(
-        functools.partial(owner_kernel, tm_count, len(attitude) - 1 if picking else 0, placing),
-        in_specs=in_specs,
-        out_specs=[VMEM] * len(out_shape),
-        out_shape=out_shape,
-        scratch_shapes=scratch,
+            pltpu.VMEM((tm_count * capacity, SRC_GROUP), jnp.float32),
+            pltpu.VMEM((rows, SRC_GROUP), jnp.float32),
+            pltpu.SemaphoreType.DMA(()),
+        ] + [table] * LATE_STREAMS,
         compiler_params=pltpu.CompilerParams(vmem_limit_bytes=VMEM_LIMIT),
-        cost_estimate=pl.CostEstimate(
-            flops=16 * seg_dev * slots * slots * width, bytes_accessed=16 << 20, transcendentals=0
-        ),
-    )(*args)
-    if placing:
-        return out[0], list(out[1:])
-    return current, list(out)
+        cost_estimate=pl.CostEstimate(flops=7 * COST_US, bytes_accessed=1 << 20, transcendentals=0),
+    )(asked, cnt, seg_counts, where, part, *attitude, *[returned[owner] for owner in owners])
+    return out[0], list(out[1:])
+
+
+def late_kernel(owners, asked_ref, cnt_ref, where_ref, part_ref, *refs):
+    refs = list(refs)
+    returned = [refs.pop(0) for _ in owners]
+    out_ref, rows_ref, held_ref, sems = refs[:4]
+    sums = refs[4:]
+    segs, slots, total_width = out_ref.shape
+    width = part_ref.shape[1]
+    add_rows(where_ref[0], asked_ref, cnt_ref, owners, returned, rows_ref, sums)
+    copies = []
+    for seg in range(segs):
+        for block in range(total_width // width):
+            at = pl.ds((block * segs + seg) * slots, slots)
+            held_ref[seg, :, block * width:(block + 1) * width] = part_ref[at, :] - placed_at(sums, at)
+        copies.append(pltpu.make_async_copy(held_ref.at[seg], out_ref.at[seg], sems.at[seg]))
+        copies[-1].start()
+    for copy in copies:
+        copy.wait()
+
+
+def place_late(scalars, owners, part, returned, shape):
+    asked, cnt, _, where = scalars
+    capacity = returned[0].shape[0]
+    return pl.pallas_call(
+        functools.partial(late_kernel, owners),
+        in_specs=[SMEM] * 3 + [VMEM] * (1 + len(owners)),
+        out_specs=HBM,
+        out_shape=jax.ShapeDtypeStruct(shape, jnp.float32),
+        scratch_shapes=[
+            pltpu.VMEM((len(owners) * capacity, SRC_GROUP), jnp.float32),
+            pltpu.VMEM(shape, jnp.float32),
+            pltpu.SemaphoreType.DMA((shape[0],)),
+        ] + [pltpu.VMEM((part.shape[0] + 8, SRC_GROUP), jnp.float32)] * LATE_STREAMS,
+        compiler_params=pltpu.CompilerParams(vmem_limit_bytes=VMEM_LIMIT),
+        cost_estimate=pl.CostEstimate(flops=4 * COST_US, bytes_accessed=1 << 20, transcendentals=0),
+    )(asked, cnt, where, part, *[returned[owner] for owner in owners])
 
 
 def make_lists(sched_seg, sched_slot, seg_dev, slots, column_blocks, tm_count, capacity):
@@ -418,26 +513,29 @@
     return (step_src, step_dst), times, wanted
 
 
+def send_order(count):
+    return sorted(range(1, count), key=lambda step: (bin(step // 2).count("1"), step % 2, -step))
+
+
 def exchange(blocks):
     count = len(blocks)
     out = list(blocks)
-    for step in sorted(range(1, count), key=lambda step: -bin(step // 2).count("1")):
+    for step in send_order(count):
         out[step] = lax.ppermute(blocks[step], "tm", [(i, i ^ step) for i in range(count)])
     return out
 
 
-def pass_along(attitude, work):
+def pass_along(attitude, beside):
     count = lax.axis_size("sky")
     right = left = attitude
     pieces = [attitude]
-    done = []
     for hop in range(1, count):
         right = lax.ppermute(right, "sky", [(i, i + 1) for i in range(hop - 1, count - 1)])
         left = lax.ppermute(left, "sky", [(i, i - 1) for i in range(1, count - hop + 1)])
+        if hop in beside:
+            right, left = beside[hop](right, left)
         pieces += [right, left]
-        if hop < count - 1 and work:
-            done.append(work.pop(0)([right, left]))
-    return pieces, done
+    return pieces
 
 
 def on_device(residuals, seg_counts, attitude, sched_seg, sched_slot, periods):
@@ -449,26 +547,48 @@
     tables, times, wanted = make_lists(
         sched_seg, sched_slot, seg_dev, slots, column_blocks, tm_count, capacity
     )
-    asked = lax.all_to_all(wanted.reshape(tm_count, capacity), "tm", split_axis=0, concat_axis=0, tiled=True)
+    wanted = wanted.reshape(tm_count, capacity)
+    part = sched_dev // BASIS_CALLS
+    made = []
+    asked = None
+
+    def basis_part(after):
+        first = len(made) * part
+        made.append(make_basis(times[first:first + part], periods, after))
+
+    def first_hop(right, left):
+        nonlocal asked
+        held, right, left = lax.optimization_barrier((wanted, right, left))
+        asked = lax.all_to_all(held, "tm", split_axis=0, concat_axis=0, tiled=True)
+        basis_part([right, left])
+        return right, left
+
+    def second_hop(right, left):
+        basis_part([right, left])
+        basis_part([right, left])
+        return right, left
+
+    pieces = pass_along(attitude, {1: first_hop, 2: second_hop})
     cnt = jnp.sum((asked < seg_dev * slots * column_blocks).astype(jnp.int32), axis=1)
-    part = sched_dev // BASIS_CALLS
-    work = [
-        functools.partial(make_basis, times[index * part:(index + 1) * part], periods)
-        for index in range(BASIS_CALLS)
-    ]
-    pieces, made = pass_along(attitude, work)
+    where = jnp.stack([lax.axis_index("tm"), lax.axis_index("sky")])
+    scalars = (asked.reshape(-1), cnt, seg_counts, where)
+    rows = seg_dev * slots * column_blocks
+    order = [0] + send_order(tm_count)
+    near, far = order[:3 * tm_count // 4], order[3 * tm_count // 4:]
+
+    base = residuals
+    picked = pick_rows(scalars, base, pieces, rows)
+    basis_part([picked[0]])
     parts, norms = zip(*made)
     norms = jnp.concatenate(norms)
-    where = jnp.stack([lax.axis_index("tm"), lax.axis_index("sky")])
-    scalars = (asked.reshape(-1), cnt, seg_counts, where)
-
-    current, returned = residuals, None
     for iteration in range(ITERS):
-        current, picked = owner_step(scalars, norms, current, pieces, returned)
         models, score = fit_plans(tables, exchange(picked), parts, norms)
         returned = exchange(models)
-    current, _ = owner_step(scalars, norms, current, None, returned)
-    return (current, score.reshape(sched_dev, SRC_GROUP))
+        base = place_early(scalars, near, base, returned, rows)
+        if iteration < ITERS - 1:
+            base, picked = place_late_and_pick(scalars, far, base, returned, pieces)
+    cleaned = place_late(scalars, far, base, returned, residuals.shape)
+    return (cleaned, score.reshape(sched_dev, SRC_GROUP))
 
 
 def solution(mesh):

time: 159 us -> 158 us (level); the launches traced: 156 us -> 157 us
  Pallas kernels: 50.3 us -> 58.9 us
  starting transfers between devices: 50 us -> 45.1 us
  waiting for transfers between devices: 41.9 us -> 37.2 us
  local copies, waits for them, and re-layouts: 3.33 us -> 5.4 us
    ppermute x28, waiting for transfers between devices: 32.8 us -> 19.8 us  [exchange(): lax.ppermute(blocks[step], 'tm', [(i, i ^ step) for i in range(count)])]
    ppermute x3, waiting for transfers between devices: 7.01 us -> 16.5 us  [pass_along(): lax.ppermute(left, 'sky', [(i, i - 1) for i in range(1, count - hop + 1)])]
    pallas_call x3 -> x5, Pallas kernels: 17 us -> 25.5 us  [the longest x2 10 us: place_early(): pl.pallas_call(functools.partial(early_kernel, owners, table_base), in_sp...]
    ppermute x28, starting transfers between devices: 34.9 us -> 29.8 us  [exchange(): lax.ppermute(blocks[step], 'tm', [(i, i ^ step) for i in range(count)])]
    all_to_all x1, waiting for transfers between devices: 2.11 us -> 0.01 us  [first_hop(): asked = lax.all_to_all(held, 'tm', split_axis=0, concat_axis=0, tiled=True)]
    unnamed x15 -> x23, local copies, waits for them, and re-layouts: 2.94 us -> 4.29 us
    pallas_call x2 -> x4, Pallas kernels: 16.8 us -> 16.9 us  [make_basis(): pl.pallas_call(functools.partial(basis_kernel, len(after)), grid=(sched_d...]
  transfers between devices with their start and end apart: 35 -> 35, of which waited for: 14 -> 12; matrix products, arithmetic and copies ran while one was open for 7% -> 6% of each run, Pallas kernels for 11% -> 17%
where the time goes in v5:
time: 158 us; the launch traced here: 157 us
  Pallas kernels  58.9 us (37%)
  starting transfers between devices  45.1 us (29%)
  waiting for transfers between devices  37.2 us (24%)
  other arithmetic  9.48 us (6%)
  local copies, waits for them, and re-layouts  5.4 us (3%)
    ppermute x28, starting transfers between devices, exchange(): lax.ppermute(blocks[step], 'tm', [(i, i ^ step) for i in range(count)])  29.8 us
    ppermute x28, waiting for transfers between devices, exchange(): lax.ppermute(blocks[step], 'tm', [(i, i ^ step) for i in range(count)])  19.8 us
    pallas_call x4, Pallas kernels, make_basis(): pl.pallas_call(functools.partial(basis_kernel, len(after)), grid=(sched_d...  16.9 us
    pallas_call x2, Pallas kernels, fit_plans(): pl.pallas_call(functools.partial(fit_kernel, tm_count), in_specs=[SMEM, S...  16.6 us
    ppermute x3, waiting for transfers between devices, pass_along(): lax.ppermute(left, 'sky', [(i, i - 1) for i in range(1, count - hop + 1)])  16.5 us
    pallas_call x2, Pallas kernels, place_early(): pl.pallas_call(functools.partial(early_kernel, owners, table_base), in_sp...  10 us
    pallas_call x1, Pallas kernels, place_late_and_pick(): pl.pallas_call(functools.partial(late_pick_kernel, tm_count, len(attitude...  6.91 us
    ppermute x3, starting transfers between devices, pass_along(): lax.ppermute(right, 'sky', [(i, i + 1) for i in range(hop - 1, count - 1)])  6.07 us
  transfers between devices with their start and end apart: 35, of which 12 were waited for; matrix products, arithmetic and copies ran while one was open for 6% of the time, Pallas kernels for 17%

profile of v5, /device:TPU:1, one launch (start us, length us, event | category | flops | bytes accessed | tf_op | source)
XLA Modules:
  0.0 157.4 jit_solution(12077119521456782160)
XLA Ops:
  0.6 1.3 collective-permute-start.1
  1.9 4.7 %collective-permute-start = (bf16[4,128,512]{2,1,0:T(8,128)(2,1)}, bf16[4,128,512]{2,1,0:T(8,128)(2,1)S(1)}, u32[]{:S(2)}, u32[]{:S(2)}) collective-permute-start(bf16[4,128,512]{2,1,0:T(8,128)(2,1)} %own_ref.3), channel_id=1, source_target_pairs={{0,1},{1,2},{2,3},{4,5},{5,6},{6,7},{8,9},{9,10},{10,11},{12,13},{... | collective-permute-start | bytes 1572872 | tf_op jit(solution)/shard_map/ppermute | solution.py:533
  10.9 3.4 %select_reduce_fusion = s32[4096]{0:T(1024)S(1)} fusion(s32[2048]{0:T(1024)S(1)} %bitcast.41, s32[2048]{0:T(1024)S(1)} %bitcast.40), kind=kLoop, calls=%fused_computation | loop fusion | flops 25161728 | bytes 32768 | tf_op jit(solution)/shard_map/reduce_sum | solution.py:495
  15.2 1.3 collective-permute-done.1.refs_1_
  16.5 1.0 collective-permute-done.refs_0_
  18.1 5.4 %all-to-all-start = ((s32[8,1,512]{2,1,0:T(1,128)}), s32[8,1,512]{2,1,0:T(1,128)S(1)}, u32[]{:S(2)}, u32[]{:S(2)}) async-start(s32[8,1,512]{2,1,0:T(1,128)} %all_to_all.6), calls=%async_computation | async-start | bytes 32768 | tf_op jit(solution)/shard_map/all_to_all | solution.py:562
  24.2 1.3 collective-permute-start.3
  25.6 4.2 %shard_map.78 = (bf16[2,256,2048]{2,1,0:T(8,128)(2,1)S(1)}, f32[2,1,2048]{2,1,0:T(1,128)S(1)}) custom-call(f32[512,128]{1,0:T(8,128)S(1)} %broadcast_in_dim.50.time_ref, f32[1,1024]{1,0:T(1,128)S(1)} %bitcast.28, f32[1,1024]{1,0:T(1,128)S(1)} %bitcast.32, bf16[4,128,512]{2,1,0:T(8,128)(2,1)S(1)} %collective-permute-done.refs_0_, ...), custom_call_target="tpu_custom_call" | custom-call | flops 5242880000 | bytes 2097152 | tf_op jit(solution)/shard_map/pallas_call | solution.py:81
  29.9 1.3 copy-done.5
  32.1 10.7 %collective-permute-done.3.refs_3_.refs_1_ = bf16[4,128,512]{2,1,0:T(8,128)(2,1)S(1)} collective-permute-done((bf16[4,128,512]{2,1,0:T(8,128)(2,1)S(1)}, bf16[4,128,512]{2,1,0:T(8,128)(2,1)S(1)}, u32[]{:S(2)}, u32[]{:S(2)}) %collective-permute-start.3) | collective-permute-done | bytes 524320 | tf_op jit(solution)/shard_map/ppermute | solution.py:534
  42.8 1.3 collective-permute-start.5
  44.3 4.2 %shard_map.80 = (bf16[2,256,2048]{2,1,0:T(8,128)(2,1)S(1)}, f32[2,1,2048]{2,1,0:T(1,128)S(1)}) custom-call(f32[512,128]{1,0:T(8,128)S(1)} %broadcast_in_dim.55.time_ref, f32[1,1024]{1,0:T(1,128)S(1)} %bitcast.29, f32[1,1024]{1,0:T(1,128)S(1)} %bitcast.33, bf16[4,128,512]{2,1,0:T(8,128)(2,1)S(1)} %collective-permute-done.2.refs_2_.refs_0_, ...), custom_call_target="tpu_custom_call" | custom-call | flops 5242880000 | bytes 2097152 | tf_op jit(solution)/shard_map/pallas_call | solution.py:81
  48.6 4.2 %shard_map.79 = (bf16[2,256,2048]{2,1,0:T(8,128)(2,1)S(1)}, f32[2,1,2048]{2,1,0:T(1,128)S(1)}) custom-call(f32[512,128]{1,0:T(8,128)S(1)} %broadcast_in_dim.53.time_ref, f32[1,1024]{1,0:T(1,128)S(1)} %bitcast.30, f32[1,1024]{1,0:T(1,128)S(1)} %bitcast.34, bf16[4,128,512]{2,1,0:T(8,128)(2,1)S(1)} %collective-permute-done.2.refs_2_.refs_0_, ...), custom_call_target="tpu_custom_call" | custom-call | flops 5242880000 | bytes 2097152 | tf_op jit(solution)/shard_map/pallas_call | solution.py:81
  52.9 4.5 %collective-permute-done.5.refs_5_ = bf16[4,128,512]{2,1,0:T(8,128)(2,1)S(1)} collective-permute-done((bf16[4,128,512]{2,1,0:T(8,128)(2,1)S(1)}, bf16[4,128,512]{2,1,0:T(8,128)(2,1)S(1)}, u32[]{:S(2)}, u32[]{:S(2)}) %collective-permute-start.5) | collective-permute-done | bytes 524320 | tf_op jit(solution)/shard_map/ppermute | solution.py:534
  57.4 4.9 %shard_map.77 = (bf16[512,128]{1,0:T(8,128)(2,1)S(1)}, bf16[512,128]{1,0:T(8,128)(2,1)S(1)}, bf16[512,128]{1,0:T(8,128)(2,1)S(1)}, bf16[512,128]{1,0:T(8,128)(2,...) custom-call(s32[4096]{0:T(1024)S(1)} %bitcast.23, ...), custom_call_target="tpu_custom_call" | custom-call | flops 5000000000 | bytes 1048576 | tf_op jit(solution)/shard_map/pallas_call | solution.py:355
  62.3 1.0 collective-permute-start.6
  63.3 0.8 collective-permute-start.7
  64.2 0.9 collective-permute-start.8
  65.0 1.3 collective-permute-start.9
  67.0 4.2 %shard_map.81 = (bf16[2,256,2048]{2,1,0:T(8,128)(2,1)S(1)}, f32[2,1,2048]{2,1,0:T(1,128)S(1)}) custom-call(f32[512,128]{1,0:T(8,128)S(1)} %broadcast_in_dim.57.time_ref, f32[1,1024]{1,0:T(1,128)S(1)} %bitcast.31, f32[1,1024]{1,0:T(1,128)S(1)} %bitcast.35, bf16[512,128]{1,0:T(8,128)(2,1)S(1)} %get-tuple-element.50.refs_0_), custom_call_target="tpu_custom_call" | custom-call | flops 5242880000 | bytes 2097152 | tf_op jit(solution)/shard_map/pallas_call | solution.py:81
  71.2 2.7 %collective-permute-start.11 = (bf16[512,128]{1,0:T(8,128)(2,1)S(1)}, bf16[512,128]{1,0:T(8,128)(2,1)S(1)}, u32[]{:S(2)}, u32[]{:S(2)}) collective-permute-start(bf16[512,128]{1,0:T(8,128)(2,1)S(1)} %get-tuple-element.56), channel_id=1, source_target_pairs={{0,24},{4,28},{8,16},{12,20},{16,8},{20,12},{24,0},{28,4},{1,25},{... | collective-permute-start | bytes 393224 | tf_op jit(solution)/shard_map/ppermute | solution.py:524
  73.9 3.7 %collective-permute-done.11.refs_6_ = bf16[512,128]{1,0:T(8,128)(2,1)S(1)} collective-permute-done((bf16[512,128]{1,0:T(8,128)(2,1)S(1)}, bf16[512,128]{1,0:T(8,128)(2,1)S(1)}, u32[]{:S(2)}, u32[]{:S(2)}) %collective-permute-start.11) | collective-permute-done | bytes 131104 | tf_op jit(solution)/shard_map/ppermute | solution.py:524
  77.6 3.0 %collective-permute-done.12.refs_7_ = bf16[512,128]{1,0:T(8,128)(2,1)S(1)} collective-permute-done((bf16[512,128]{1,0:T(8,128)(2,1)S(1)}, bf16[512,128]{1,0:T(8,128)(2,1)S(1)}, u32[]{:S(2)}, u32[]{:S(2)}) %collective-permute-start.12) | collective-permute-done | bytes 131104 | tf_op jit(solution)/shard_map/ppermute | solution.py:524
  80.6 8.6 %shard_map.82 = (bf16[512,128]{1,0:T(8,128)(2,1)S(1)}, bf16[512,128]{1,0:T(8,128)(2,1)S(1)}, bf16[512,128]{1,0:T(8,128)(2,1)S(1)}, bf16[512,128]{1,0:T(8,128)(2,...) custom-call(s32[8,24]{1,0:T(8,128)S(1)} %get-tuple-element.110.src_r, ...), custom_call_target="tpu_custom_call" | custom-call | flops 10737418240 | bytes 8388608 | tf_op jit(solution)/shard_map/pallas_call | solution.py:204
  89.7 1.1 collective-permute-start.14
  90.8 1.3 collective-permute-start.15
  92.9 2.1 %collective-permute-start.18 = (bf16[512,128]{1,0:T(8,128)(2,1)S(1)}, bf16[512,128]{1,0:T(8,128)(2,1)S(1)}, u32[]{:S(2)}, u32[]{:S(2)}) collective-permute-start(bf16[512,128]{1,0:T(8,128)(2,1)S(1)} %get-tuple-element.72), channel_id=1, source_target_pairs={{0,24},{4,28},{8,16},{12,20},{16,8},{20,12},{24,0},{28,4},{1,25},{... | collective-permute-start | bytes 393224 | tf_op jit(solution)/shard_map/ppermute | solution.py:524
  95.0 3.2 %collective-permute-start.19 = (bf16[512,128]{1,0:T(8,128)(2,1)S(1)}, bf16[512,128]{1,0:T(8,128)(2,1)S(1)}, u32[]{:S(2)}, u32[]{:S(2)}) collective-permute-start(bf16[512,128]{1,0:T(8,128)(2,1)S(1)} %get-tuple-element.73), channel_id=1, source_target_pairs={{0,28},{4,24},{8,20},{12,16},{16,12},{20,8},{24,4},{28,0},{1,29},{... | collective-permute-start | bytes 393224 | tf_op jit(solution)/shard_map/ppermute | solution.py:524
  98.2 1.3 collective-permute-done.17.refs_5_
  99.6 5.0 %shard_map.83.part_ref = f32[4096,128]{1,0:T(8,128)S(1)} custom-call(s32[4096]{0:T(1024)S(1)} %bitcast.24, s32[8]{0:T(128)S(1)} %fusion.4.cnt_ref, s32[2]{0:T(128)S(1)} %pad_add_fusion.where_ref, bf16[4,512,256]{2,1,0:T(8,128)(2,1)S(1)} %copy-done, bf16[512,128]{1,0:T(8,128)(2,1)S(1)} %get-tuple-element.66.refs_0_, ...), custom_call_target="tpu_custom_call" | custom-call | flops 6000000000 | bytes 1048576 | tf_op jit(solution)/shard_map/pallas_call | solution.py:327
  104.6 6.9 %shard_map.84 = (f32[4096,128]{1,0:T(8,128)S(1)}, bf16[512,128]{1,0:T(8,128)(2,1)S(1)}, bf16[512,128]{1,0:T(8,128)(2,1)S(1)}, bf16[512,128]{1,0:T(8,128)(2,1)S(1...) custom-call(s32[4096]{0:T(1024)S(1)} %bitcast.25, ...), custom_call_target="tpu_custom_call" | custom-call | flops 7000000000 | bytes 1048576 | tf_op jit(solution)/shard_map/pallas_call | solution.py:413
  111.5 1.3 copy-done.3
  113.3 1.7 %collective-permute-start.22 = (bf16[512,128]{1,0:T(8,128)(2,1)S(1)}, bf16[512,128]{1,0:T(8,128)(2,1)S(1)}, u32[]{:S(2)}, u32[]{:S(2)}) collective-permute-start(bf16[512,128]{1,0:T(8,128)(2,1)S(1)} %get-tuple-element.78), channel_id=1, source_target_pairs={{0,12},{4,8},{8,4},{12,0},{16,28},{20,24},{24,20},{28,16},{1,13},{... | collective-permute-start | bytes 393224 | tf_op jit(solution)/shard_map/ppermute | solution.py:524
  114.9 0.9 collective-permute-start.23
  118.1 2.0 %collective-permute-start.26 = (bf16[512,128]{1,0:T(8,128)(2,1)S(1)}, bf16[512,128]{1,0:T(8,128)(2,1)S(1)}, u32[]{:S(2)}, u32[]{:S(2)}) collective-permute-start(bf16[512,128]{1,0:T(8,128)(2,1)S(1)} %get-tuple-element.82), channel_id=1, source_target_pairs={{0,28},{4,24},{8,20},{12,16},{16,12},{20,8},{24,4},{28,0},{1,29},{... | collective-permute-start | bytes 393224 | tf_op jit(solution)/shard_map/ppermute | solution.py:524
  120.1 1.9 %collective-permute-done.22.refs_3_ = bf16[512,128]{1,0:T(8,128)(2,1)S(1)} collective-permute-done((bf16[512,128]{1,0:T(8,128)(2,1)S(1)}, bf16[512,128]{1,0:T(8,128)(2,1)S(1)}, u32[]{:S(2)}, u32[]{:S(2)}) %collective-permute-start.22) | collective-permute-done | bytes 131104 | tf_op jit(solution)/shard_map/ppermute | solution.py:524
  122.0 6.5 %collective-permute-done.24.refs_5_ = bf16[512,128]{1,0:T(8,128)(2,1)S(1)} collective-permute-done((bf16[512,128]{1,0:T(8,128)(2,1)S(1)}, bf16[512,128]{1,0:T(8,128)(2,1)S(1)}, u32[]{:S(2)}, u32[]{:S(2)}) %collective-permute-start.24) | collective-permute-done | bytes 131104 | tf_op jit(solution)/shard_map/ppermute | solution.py:524
  128.6 7.9 %shard_map.85 = (bf16[512,128]{1,0:T(8,128)(2,1)S(1)}, bf16[512,128]{1,0:T(8,128)(2,1)S(1)}, bf16[512,128]{1,0:T(8,128)(2,1)S(1)}, bf16[512,128]{1,0:T(8,128)(2,...) custom-call(s32[8,24]{1,0:T(8,128)S(1)} %get-tuple-element.110.src_r, ...), custom_call_target="tpu_custom_call" | custom-call | flops 10737418240 | bytes 8388608 | tf_op jit(solution)/shard_map/pallas_call | solution.py:204
  136.8 1.2 collective-permute-start.28
  138.0 1.6 %collective-permute-start.30 = (bf16[512,128]{1,0:T(8,128)(2,1)S(1)}, bf16[512,128]{1,0:T(8,128)(2,1)S(1)}, u32[]{:S(2)}, u32[]{:S(2)}) collective-permute-start(bf16[512,128]{1,0:T(8,128)(2,1)S(1)} %get-tuple-element.87), channel_id=1, source_target_pairs={{0,20},{4,16},{8,28},{12,24},{16,4},{20,0},{24,12},{28,8},{1,21},{... | collective-permute-start | bytes 393224 | tf_op jit(solution)/shard_map/ppermute | solution.py:524
  140.1 0.8 reduce.1
  140.9 1.2 collective-permute-start.32
  142.1 2.2 %collective-permute-start.33 = (bf16[512,128]{1,0:T(8,128)(2,1)S(1)}, bf16[512,128]{1,0:T(8,128)(2,1)S(1)}, u32[]{:S(2)}, u32[]{:S(2)}) collective-permute-start(bf16[512,128]{1,0:T(8,128)(2,1)S(1)} %get-tuple-element.90), channel_id=1, source_target_pairs={{0,28},{4,24},{8,20},{12,16},{16,12},{20,8},{24,4},{28,0},{1,29},{... | collective-permute-start | bytes 393224 | tf_op jit(solution)/shard_map/ppermute | solution.py:524
  144.2 0.9 collective-permute-done.30.refs_4_
  145.2 1.7 %collective-permute-done.31.refs_5_ = bf16[512,128]{1,0:T(8,128)(2,1)S(1)} collective-permute-done((bf16[512,128]{1,0:T(8,128)(2,1)S(1)}, bf16[512,128]{1,0:T(8,128)(2,1)S(1)}, u32[]{:S(2)}, u32[]{:S(2)}) %collective-permute-start.31) | collective-permute-done | bytes 131104 | tf_op jit(solution)/shard_map/ppermute | solution.py:524
  146.9 1.6 %copy-done.4 = f32[4096,128]{1,0:T(8,128)S(1)} copy-done((f32[4096,128]{1,0:T(8,128)S(1)}, f32[4096,128]{1,0:T(8,128)}, u32[]{:S(2)}) %copy-start.4) | copy-done | bytes 2097176
  148.5 5.0 %shard_map.86.part_ref = f32[4096,128]{1,0:T(8,128)S(1)} custom-call(s32[4096]{0:T(1024)S(1)} %bitcast.26, s32[8]{0:T(128)S(1)} %fusion.4.cnt_ref, s32[2]{0:T(128)S(1)} %pad_add_fusion.where_ref, f32[4096,128]{1,0:T(8,128)S(1)} %copy-done.4, bf16[512,128]{1,0:T(8,128)(2,1)S(1)} %get-tuple-element.83.refs_0_, ...), custom_call_target="tpu_custom_call" | custom-call | flops 6000000000 | bytes 1048576 | tf_op jit(solution)/shard_map/pallas_call | solution.py:327
  153.6 3.7 %shard_map.87 = f32[4,512,256]{2,1,0:T(8,128)} custom-call(s32[4096]{0:T(1024)S(1)} %bitcast.27, s32[8]{0:T(128)S(1)} %fusion.4.cnt_ref, s32[2]{0:T(128)S(1)} %pad_add_fusion.where_ref, f32[4096,128]{1,0:T(8,128)S(1)} %shard_map.86.part_ref, bf16[512,128]{1,0:T(8,128)(2,1)S(1)} %collective-permute-done.32.refs_0_, ...), custom_call_target="tpu_custom_call" | custom-call | flops 4000000000 | bytes 1048576 | tf_op jit(solution)/shard_map/pallas_call | solution.py:455
  (86 shorter events, 13.3 us)
Async XLA Ops:
  0.6 15.9 %collective-permute-start.1 = (bf16[4,128,512]{2,1,0:T(8,128)(2,1)}, bf16[4,128,512]{2,1,0:T(8,128)(2,1)S(1)}, u32[]{:S(2)}, u32[]{:S(2)}) collective-permute-start(bf16[4,128,512]{2,1,0:T(8,128)(2,1)} %own_ref.3), channel_id=1, source_target_pairs={{1,0},{2,1},{3,2},{5,4},{6,5},{7,6},{9,8},{10,9},{11,10},{13,12},{... | collective-permute-start | bytes 1572872 | tf_op jit(solution)/shard_map/ppermute | solution.py:534
  1.9 15.6 %collective-permute-start = (bf16[4,128,512]{2,1,0:T(8,128)(2,1)}, bf16[4,128,512]{2,1,0:T(8,128)(2,1)S(1)}, u32[]{:S(2)}, u32[]{:S(2)}) collective-permute-start(bf16[4,128,512]{2,1,0:T(8,128)(2,1)} %own_ref.3), channel_id=1, source_target_pairs={{0,1},{1,2},{2,3},{4,5},{5,6},{6,7},{8,9},{9,10},{10,11},{12,13},{... | collective-permute-start | bytes 1572872 | tf_op jit(solution)/shard_map/ppermute | solution.py:533
  18.1 13.1 %all-to-all-start = ((s32[8,1,512]{2,1,0:T(1,128)}), s32[8,1,512]{2,1,0:T(1,128)S(1)}, u32[]{:S(2)}, u32[]{:S(2)}) async-start(s32[8,1,512]{2,1,0:T(1,128)} %all_to_all.6), calls=%async_computation | async-start | bytes 32768 | tf_op jit(solution)/shard_map/all_to_all | solution.py:562
  23.5 7.9 %collective-permute-start.2 = (bf16[4,128,512]{2,1,0:T(8,128)(2,1)S(1)}, bf16[4,128,512]{2,1,0:T(8,128)(2,1)S(1)}, u32[]{:S(2)}, u32[]{:S(2)}) collective-permute-start(bf16[4,128,512]{2,1,0:T(8,128)(2,1)S(1)} %collective-permute-done.refs_0_), channel_id=1, source_target_pairs={{1,2},{2,3},{5,6},{6,7},{9,10},{10,11},{13,14},{14,15},{17,18},{18... | collective-permute-start | bytes 1572872 | tf_op jit(solution)/shard_map/ppermute | solution.py:533
  24.2 18.6 %collective-permute-start.3 = (bf16[4,128,512]{2,1,0:T(8,128)(2,1)S(1)}, bf16[4,128,512]{2,1,0:T(8,128)(2,1)S(1)}, u32[]{:S(2)}, u32[]{:S(2)}) collective-permute-start(bf16[4,128,512]{2,1,0:T(8,128)(2,1)S(1)} %collective-permute-done.1.refs_1_), channel_id=1, source_target_pairs={{1,0},{2,1},{5,4},{6,5},{9,8},{10,9},{13,12},{14,13},{17,16},{18,1... | collective-permute-start | bytes 1572872 | tf_op jit(solution)/shard_map/ppermute | solution.py:534
  29.9 1.3 copy-start.5
  31.4 21.5 %collective-permute-start.4 = (bf16[4,128,512]{2,1,0:T(8,128)(2,1)S(1)}, bf16[4,128,512]{2,1,0:T(8,128)(2,1)S(1)}, u32[]{:S(2)}, u32[]{:S(2)}) collective-permute-start(bf16[4,128,512]{2,1,0:T(8,128)(2,1)S(1)} %collective-permute-done.2.refs_2_.refs_0_), channel_id=1, source_target_pairs={{2,3},{6,7},{10,11},{14,15},{18,19},{22,23},{26,27},{30,31}} | collective-permute-start | bytes 1572872 | tf_op jit(solution)/shard_map/ppermute | solution.py:533
  42.8 14.5 %collective-permute-start.5 = (bf16[4,128,512]{2,1,0:T(8,128)(2,1)S(1)}, bf16[4,128,512]{2,1,0:T(8,128)(2,1)S(1)}, u32[]{:S(2)}, u32[]{:S(2)}) collective-permute-start(bf16[4,128,512]{2,1,0:T(8,128)(2,1)S(1)} %collective-permute-done.3.refs_3_.refs_1_), channel_id=1, source_target_pairs={{1,0},{5,4},{9,8},{13,12},{17,16},{21,20},{25,24},{29,28}} | collective-permute-start | bytes 1572872 | tf_op jit(solution)/shard_map/ppermute | solution.py:534
  48.6 8.8 %copy-start = (bf16[4,512,256]{2,1,0:T(8,128)(2,1)S(1)}, bf16[4,512,256]{2,1,0:T(8,128)(2,1)}, u32[]{:S(2)}) copy-start(bf16[4,512,256]{2,1,0:T(8,128)(2,1)} %base_ref.3) | copy-start | bytes 3145732
  48.6 8.8 %copy-start.1 = (bf16[4,128,512]{2,1,0:T(8,128)(2,1)S(1)}, bf16[4,128,512]{2,1,0:T(8,128)(2,1)}, u32[]{:S(2)}) copy-start(bf16[4,128,512]{2,1,0:T(8,128)(2,1)} %own_ref.3) | copy-start | bytes 1572868
  48.6 8.8 %copy-start.2 = (s32[4]{0:T(128)S(1)}, s32[4]{0:T(128)}, u32[]{:S(2)}) copy-start(s32[4]{0:T(128)} %count_ref.3) | copy-start | bytes 52
  62.3 8.9 %collective-permute-start.6 = (bf16[512,128]{1,0:T(8,128)(2,1)S(1)}, bf16[512,128]{1,0:T(8,128)(2,1)S(1)}, u32[]{:S(2)}, u32[]{:S(2)}) collective-permute-start(bf16[512,128]{1,0:T(8,128)(2,1)S(1)} %get-tuple-element.51), channel_id=1, source_target_pairs={{0,4},{4,0},{8,12},{12,8},{16,20},{20,16},{24,28},{28,24},{1,5},{5... | collective-permute-start | bytes 393224 | tf_op jit(solution)/shard_map/ppermute | solution.py:524
  63.3 10.5 %collective-permute-start.7 = (bf16[512,128]{1,0:T(8,128)(2,1)S(1)}, bf16[512,128]{1,0:T(8,128)(2,1)S(1)}, u32[]{:S(2)}, u32[]{:S(2)}) collective-permute-start(bf16[512,128]{1,0:T(8,128)(2,1)S(1)} %get-tuple-element.52), channel_id=1, source_target_pairs={{0,8},{4,12},{8,0},{12,4},{16,24},{20,28},{24,16},{28,20},{1,9},{5... | collective-permute-start | bytes 393224 | tf_op jit(solution)/shard_map/ppermute | solution.py:524
  64.2 9.7 %collective-permute-start.8 = (bf16[512,128]{1,0:T(8,128)(2,1)S(1)}, bf16[512,128]{1,0:T(8,128)(2,1)S(1)}, u32[]{:S(2)}, u32[]{:S(2)}) collective-permute-start(bf16[512,128]{1,0:T(8,128)(2,1)S(1)} %get-tuple-element.53), channel_id=1, source_target_pairs={{0,12},{4,8},{8,4},{12,0},{16,28},{20,24},{24,20},{28,16},{1,13},{... | collective-permute-start | bytes 393224 | tf_op jit(solution)/shard_map/ppermute | solution.py:524
  65.0 8.9 %collective-permute-start.9 = (bf16[512,128]{1,0:T(8,128)(2,1)S(1)}, bf16[512,128]{1,0:T(8,128)(2,1)S(1)}, u32[]{:S(2)}, u32[]{:S(2)}) collective-permute-start(bf16[512,128]{1,0:T(8,128)(2,1)S(1)} %get-tuple-element.54), channel_id=1, source_target_pairs={{0,16},{4,20},{8,24},{12,28},{16,0},{20,4},{24,8},{28,12},{1,17},{... | collective-permute-start | bytes 393224 | tf_op jit(solution)/shard_map/ppermute | solution.py:524
  66.3 7.6 %collective-permute-start.10 = (bf16[512,128]{1,0:T(8,128)(2,1)S(1)}, bf16[512,128]{1,0:T(8,128)(2,1)S(1)}, u32[]{:S(2)}, u32[]{:S(2)}) collective-permute-start(bf16[512,128]{1,0:T(8,128)(2,1)S(1)} %get-tuple-element.55), channel_id=1, source_target_pairs={{0,20},{4,16},{8,28},{12,24},{16,4},{20,0},{24,12},{28,8},{1,21},{... | collective-permute-start | bytes 393224 | tf_op jit(solution)/shard_map/ppermute | solution.py:524
  67.0 13.6 %copy-start.6 = (bf16[2,256,2048]{2,1,0:T(8,128)(2,1)S(1)}, bf16[2,256,2048]{2,1,0:T(8,128)(2,1)}, u32[]{:S(2)}) copy-start(bf16[2,256,2048]{2,1,0:T(8,128)(2,1)} %copy-done.5) | copy-start | bytes 6291460
  71.2 6.4 %collective-permute-start.11 = (bf16[512,128]{1,0:T(8,128)(2,1)S(1)}, bf16[512,128]{1,0:T(8,128)(2,1)S(1)}, u32[]{:S(2)}, u32[]{:S(2)}) collective-permute-start(bf16[512,128]{1,0:T(8,128)(2,1)S(1)} %get-tuple-element.56), channel_id=1, source_target_pairs={{0,24},{4,28},{8,16},{12,20},{16,8},{20,12},{24,0},{28,4},{1,25},{... | collective-permute-start | bytes 393224 | tf_op jit(solution)/shard_map/ppermute | solution.py:524
  73.9 6.7 %collective-permute-start.12 = (bf16[512,128]{1,0:T(8,128)(2,1)S(1)}, bf16[512,128]{1,0:T(8,128)(2,1)S(1)}, u32[]{:S(2)}, u32[]{:S(2)}) collective-permute-start(bf16[512,128]{1,0:T(8,128)(2,1)S(1)} %get-tuple-element.57), channel_id=1, source_target_pairs={{0,28},{4,24},{8,20},{12,16},{16,12},{20,8},{24,4},{28,0},{1,29},{... | collective-permute-start | bytes 393224 | tf_op jit(solution)/shard_map/ppermute | solution.py:524
  89.2 3.7 %collective-permute-start.13 = (bf16[512,128]{1,0:T(8,128)(2,1)S(1)}, bf16[512,128]{1,0:T(8,128)(2,1)S(1)}, u32[]{:S(2)}, u32[]{:S(2)}) collective-permute-start(bf16[512,128]{1,0:T(8,128)(2,1)S(1)} %get-tuple-element.67), channel_id=1, source_target_pairs={{0,4},{4,0},{8,12},{12,8},{16,20},{20,16},{24,28},{28,24},{1,5},{5... | collective-permute-start | bytes 393224 | tf_op jit(solution)/shard_map/ppermute | solution.py:524
  89.7 5.3 %collective-permute-start.14 = (bf16[512,128]{1,0:T(8,128)(2,1)S(1)}, bf16[512,128]{1,0:T(8,128)(2,1)S(1)}, u32[]{:S(2)}, u32[]{:S(2)}) collective-permute-start(bf16[512,128]{1,0:T(8,128)(2,1)S(1)} %get-tuple-element.68), channel_id=1, source_target_pairs={{0,16},{4,20},{8,24},{12,28},{16,0},{20,4},{24,8},{28,12},{1,17},{... | collective-permute-start | bytes 393224 | tf_op jit(solution)/shard_map/ppermute | solution.py:524
  90.8 7.5 %collective-permute-start.15 = (bf16[512,128]{1,0:T(8,128)(2,1)S(1)}, bf16[512,128]{1,0:T(8,128)(2,1)S(1)}, u32[]{:S(2)}, u32[]{:S(2)}) collective-permute-start(bf16[512,128]{1,0:T(8,128)(2,1)S(1)} %get-tuple-element.69), channel_id=1, source_target_pairs={{0,8},{4,12},{8,0},{12,4},{16,24},{20,28},{24,16},{28,20},{1,9},{5... | collective-permute-start | bytes 393224 | tf_op jit(solution)/shard_map/ppermute | solution.py:524
  92.1 6.2 %collective-permute-start.16 = (bf16[512,128]{1,0:T(8,128)(2,1)S(1)}, bf16[512,128]{1,0:T(8,128)(2,1)S(1)}, u32[]{:S(2)}, u32[]{:S(2)}) collective-permute-start(bf16[512,128]{1,0:T(8,128)(2,1)S(1)} %get-tuple-element.70), channel_id=1, source_target_pairs={{0,20},{4,16},{8,28},{12,24},{16,4},{20,0},{24,12},{28,8},{1,21},{... | collective-permute-start | bytes 393224 | tf_op jit(solution)/shard_map/ppermute | solution.py:524
  92.5 7.1 %collective-permute-start.17 = (bf16[512,128]{1,0:T(8,128)(2,1)S(1)}, bf16[512,128]{1,0:T(8,128)(2,1)S(1)}, u32[]{:S(2)}, u32[]{:S(2)}) collective-permute-start(bf16[512,128]{1,0:T(8,128)(2,1)S(1)} %get-tuple-element.71), channel_id=1, source_target_pairs={{0,12},{4,8},{8,4},{12,0},{16,28},{20,24},{24,20},{28,16},{1,13},{... | collective-permute-start | bytes 393224 | tf_op jit(solution)/shard_map/ppermute | solution.py:524
  92.9 11.6 %collective-permute-start.18 = (bf16[512,128]{1,0:T(8,128)(2,1)S(1)}, bf16[512,128]{1,0:T(8,128)(2,1)S(1)}, u32[]{:S(2)}, u32[]{:S(2)}) collective-permute-start(bf16[512,128]{1,0:T(8,128)(2,1)S(1)} %get-tuple-element.72), channel_id=1, source_target_pairs={{0,24},{4,28},{8,16},{12,20},{16,8},{20,12},{24,0},{28,4},{1,25},{... | collective-permute-start | bytes 393224 | tf_op jit(solution)/shard_map/ppermute | solution.py:524
  95.0 9.6 %collective-permute-start.19 = (bf16[512,128]{1,0:T(8,128)(2,1)S(1)}, bf16[512,128]{1,0:T(8,128)(2,1)S(1)}, u32[]{:S(2)}, u32[]{:S(2)}) collective-permute-start(bf16[512,128]{1,0:T(8,128)(2,1)S(1)} %get-tuple-element.73), channel_id=1, source_target_pairs={{0,28},{4,24},{8,20},{12,16},{16,12},{20,8},{24,4},{28,0},{1,29},{... | collective-permute-start | bytes 393224 | tf_op jit(solution)/shard_map/ppermute | solution.py:524
  111.5 1.3 copy-start.3
  112.8 3.8 %collective-permute-start.20 = (bf16[512,128]{1,0:T(8,128)(2,1)S(1)}, bf16[512,128]{1,0:T(8,128)(2,1)S(1)}, u32[]{:S(2)}, u32[]{:S(2)}) collective-permute-start(bf16[512,128]{1,0:T(8,128)(2,1)S(1)} %get-tuple-element.76), channel_id=1, source_target_pairs={{0,4},{4,0},{8,12},{12,8},{16,20},{20,16},{24,28},{28,24},{1,5},{5... | collective-permute-start | bytes 393224 | tf_op jit(solution)/shard_map/ppermute | solution.py:524
  113.1 4.9 %collective-permute-start.21 = (bf16[512,128]{1,0:T(8,128)(2,1)S(1)}, bf16[512,128]{1,0:T(8,128)(2,1)S(1)}, u32[]{:S(2)}, u32[]{:S(2)}) collective-permute-start(bf16[512,128]{1,0:T(8,128)(2,1)S(1)} %get-tuple-element.77), channel_id=1, source_target_pairs={{0,8},{4,12},{8,0},{12,4},{16,24},{20,28},{24,16},{28,20},{1,9},{5... | collective-permute-start | bytes 393224 | tf_op jit(solution)/shard_map/ppermute | solution.py:524
  113.3 8.8 %collective-permute-start.22 = (bf16[512,128]{1,0:T(8,128)(2,1)S(1)}, bf16[512,128]{1,0:T(8,128)(2,1)S(1)}, u32[]{:S(2)}, u32[]{:S(2)}) collective-permute-start(bf16[512,128]{1,0:T(8,128)(2,1)S(1)} %get-tuple-element.78), channel_id=1, source_target_pairs={{0,12},{4,8},{8,4},{12,0},{16,28},{20,24},{24,20},{28,16},{1,13},{... | collective-permute-start | bytes 393224 | tf_op jit(solution)/shard_map/ppermute | solution.py:524
  114.9 7.1 %collective-permute-start.23 = (bf16[512,128]{1,0:T(8,128)(2,1)S(1)}, bf16[512,128]{1,0:T(8,128)(2,1)S(1)}, u32[]{:S(2)}, u32[]{:S(2)}) collective-permute-start(bf16[512,128]{1,0:T(8,128)(2,1)S(1)} %get-tuple-element.79), channel_id=1, source_target_pairs={{0,16},{4,20},{8,24},{12,28},{16,0},{20,4},{24,8},{28,12},{1,17},{... | collective-permute-start | bytes 393224 | tf_op jit(solution)/shard_map/ppermute | solution.py:524
  115.8 12.8 %collective-permute-start.24 = (bf16[512,128]{1,0:T(8,128)(2,1)S(1)}, bf16[512,128]{1,0:T(8,128)(2,1)S(1)}, u32[]{:S(2)}, u32[]{:S(2)}) collective-permute-start(bf16[512,128]{1,0:T(8,128)(2,1)S(1)} %get-tuple-element.80), channel_id=1, source_target_pairs={{0,20},{4,16},{8,28},{12,24},{16,4},{20,0},{24,12},{28,8},{1,21},{... | collective-permute-start | bytes 393224 | tf_op jit(solution)/shard_map/ppermute | solution.py:524
  116.6 11.9 %collective-permute-start.25 = (bf16[512,128]{1,0:T(8,128)(2,1)S(1)}, bf16[512,128]{1,0:T(8,128)(2,1)S(1)}, u32[]{:S(2)}, u32[]{:S(2)}) collective-permute-start(bf16[512,128]{1,0:T(8,128)(2,1)S(1)} %get-tuple-element.81), channel_id=1, source_target_pairs={{0,24},{4,28},{8,16},{12,20},{16,8},{20,12},{24,0},{28,4},{1,25},{... | collective-permute-start | bytes 393224 | tf_op jit(solution)/shard_map/ppermute | solution.py:524
  118.1 10.5 %collective-permute-start.26 = (bf16[512,128]{1,0:T(8,128)(2,1)S(1)}, bf16[512,128]{1,0:T(8,128)(2,1)S(1)}, u32[]{:S(2)}, u32[]{:S(2)}) collective-permute-start(bf16[512,128]{1,0:T(8,128)(2,1)S(1)} %get-tuple-element.82), channel_id=1, source_target_pairs={{0,28},{4,24},{8,20},{12,16},{16,12},{20,8},{24,4},{28,0},{1,29},{... | collective-permute-start | bytes 393224 | tf_op jit(solution)/shard_map/ppermute | solution.py:524
  136.6 4.3 %collective-permute-start.27 = (bf16[512,128]{1,0:T(8,128)(2,1)S(1)}, bf16[512,128]{1,0:T(8,128)(2,1)S(1)}, u32[]{:S(2)}, u32[]{:S(2)}) collective-permute-start(bf16[512,128]{1,0:T(8,128)(2,1)S(1)} %get-tuple-element.84), channel_id=1, source_target_pairs={{0,4},{4,0},{8,12},{12,8},{16,20},{20,16},{24,28},{28,24},{1,5},{5... | collective-permute-start | bytes 393224 | tf_op jit(solution)/shard_map/ppermute | solution.py:524
  136.8 5.2 %collective-permute-start.28 = (bf16[512,128]{1,0:T(8,128)(2,1)S(1)}, bf16[512,128]{1,0:T(8,128)(2,1)S(1)}, u32[]{:S(2)}, u32[]{:S(2)}) collective-permute-start(bf16[512,128]{1,0:T(8,128)(2,1)S(1)} %get-tuple-element.85), channel_id=1, source_target_pairs={{0,16},{4,20},{8,24},{12,28},{16,0},{20,4},{24,8},{28,12},{1,17},{... | collective-permute-start | bytes 393224 | tf_op jit(solution)/shard_map/ppermute | solution.py:524
  138.0 6.2 %collective-permute-start.29 = (bf16[512,128]{1,0:T(8,128)(2,1)S(1)}, bf16[512,128]{1,0:T(8,128)(2,1)S(1)}, u32[]{:S(2)}, u32[]{:S(2)}) collective-permute-start(bf16[512,128]{1,0:T(8,128)(2,1)S(1)} %get-tuple-element.86), channel_id=1, source_target_pairs={{0,8},{4,12},{8,0},{12,4},{16,24},{20,28},{24,16},{28,20},{1,9},{5... | collective-permute-start | bytes 393224 | tf_op jit(solution)/shard_map/ppermute | solution.py:524
  138.0 7.1 %collective-permute-start.30 = (bf16[512,128]{1,0:T(8,128)(2,1)S(1)}, bf16[512,128]{1,0:T(8,128)(2,1)S(1)}, u32[]{:S(2)}, u32[]{:S(2)}) collective-permute-start(bf16[512,128]{1,0:T(8,128)(2,1)S(1)} %get-tuple-element.87), channel_id=1, source_target_pairs={{0,20},{4,16},{8,28},{12,24},{16,4},{20,0},{24,12},{28,8},{1,21},{... | collective-permute-start | bytes 393224 | tf_op jit(solution)/shard_map/ppermute | solution.py:524
  139.6 7.3 %collective-permute-start.31 = (bf16[512,128]{1,0:T(8,128)(2,1)S(1)}, bf16[512,128]{1,0:T(8,128)(2,1)S(1)}, u32[]{:S(2)}, u32[]{:S(2)}) collective-permute-start(bf16[512,128]{1,0:T(8,128)(2,1)S(1)} %get-tuple-element.88), channel_id=1, source_target_pairs={{0,12},{4,8},{8,4},{12,0},{16,28},{20,24},{24,20},{28,16},{1,13},{... | collective-permute-start | bytes 393224 | tf_op jit(solution)/shard_map/ppermute | solution.py:524
  140.9 12.7 %collective-permute-start.32 = (bf16[512,128]{1,0:T(8,128)(2,1)S(1)}, bf16[512,128]{1,0:T(8,128)(2,1)S(1)}, u32[]{:S(2)}, u32[]{:S(2)}) collective-permute-start(bf16[512,128]{1,0:T(8,128)(2,1)S(1)} %get-tuple-element.89), channel_id=1, source_target_pairs={{0,24},{4,28},{8,16},{12,20},{16,8},{20,12},{24,0},{28,4},{1,25},{... | collective-permute-start | bytes 393224 | tf_op jit(solution)/shard_map/ppermute | solution.py:524
  142.1 11.5 %collective-permute-start.33 = (bf16[512,128]{1,0:T(8,128)(2,1)S(1)}, bf16[512,128]{1,0:T(8,128)(2,1)S(1)}, u32[]{:S(2)}, u32[]{:S(2)}) collective-permute-start(bf16[512,128]{1,0:T(8,128)(2,1)S(1)} %get-tuple-element.90), channel_id=1, source_target_pairs={{0,28},{4,24},{8,20},{12,16},{16,12},{20,8},{24,4},{28,0},{1,29},{... | collective-permute-start | bytes 393224 | tf_op jit(solution)/shard_map/ppermute | solution.py:524
  146.9 1.6 %copy-start.4 = (f32[4096,128]{1,0:T(8,128)S(1)}, f32[4096,128]{1,0:T(8,128)}, u32[]{:S(2)}) copy-start(f32[4096,128]{1,0:T(8,128)} %copy-done.3) | copy-start | bytes 6291460

commit v6 on v5

--- a/solution.py
+++ b/solution.py
@@ -14,7 +14,13 @@
 STEP = 16
 BETA = 2.0
 RIDGE = 1.0
-VMEM_LIMIT = 24 * 1024 * 1024
+MIB = 1024 * 1024
+BASIS_VMEM = 8 * MIB
+FIT_VMEM = 22 * MIB
+EARLY_VMEM = 20 * MIB
+PICK_VMEM = 12 * MIB
+LATE_PICK_VMEM = 18 * MIB
+LATE_VMEM = 12 * MIB
 BASIS_CALLS = 4
 UNROLL = 16
 COST_US = 10 ** 9
@@ -94,7 +100,7 @@
             jax.ShapeDtypeStruct((sched_dev, obs, 2 * nper), jnp.bfloat16),
             jax.ShapeDtypeStruct((sched_dev, 1, 2 * nper), jnp.float32),
         ],
-        compiler_params=pltpu.CompilerParams(vmem_limit_bytes=VMEM_LIMIT),
+        compiler_params=pltpu.CompilerParams(vmem_limit_bytes=BASIS_VMEM),
         cost_estimate=pl.CostEstimate(
             flops=sched_dev * obs * nper * 10000, bytes_accessed=sched_dev * obs * nper * 4, transcendentals=0
         ),
@@ -213,7 +219,7 @@
             pltpu.VMEM((spaced, width), jnp.float32),
             pltpu.VMEM((spaced, width), jnp.float32),
         ] + slot + slot,
-        compiler_params=pltpu.CompilerParams(vmem_limit_bytes=VMEM_LIMIT),
+        compiler_params=pltpu.CompilerParams(vmem_limit_bytes=FIT_VMEM),
         cost_estimate=pl.CostEstimate(flops=20 * work, bytes_accessed=sched_dev * obs * twice * 2, transcendentals=0),
     )(*tables, *arrived, *parts, norms)
     return models, score
@@ -330,7 +336,7 @@
         out_specs=VMEM,
         out_shape=jax.ShapeDtypeStruct((rows, SRC_GROUP), jnp.float32),
         scratch_shapes=[pltpu.VMEM((len(owners) * capacity, SRC_GROUP), jnp.float32)] + held + sums,
-        compiler_params=pltpu.CompilerParams(vmem_limit_bytes=VMEM_LIMIT),
+        compiler_params=pltpu.CompilerParams(vmem_limit_bytes=EARLY_VMEM),
         cost_estimate=pl.CostEstimate(flops=6 * COST_US, bytes_accessed=1 << 20, transcendentals=0),
     )(asked, cnt, where, base, *[returned[owner] for owner in owners])
 
@@ -363,7 +369,7 @@
             pltpu.VMEM((rows + 8, SRC_GROUP), jnp.float32),
             pltpu.VMEM((tm_count * capacity, SRC_GROUP), jnp.float32),
         ],
-        compiler_params=pltpu.CompilerParams(vmem_limit_bytes=VMEM_LIMIT),
+        compiler_params=pltpu.CompilerParams(vmem_limit_bytes=PICK_VMEM),
         cost_estimate=pl.CostEstimate(flops=5 * COST_US, bytes_accessed=1 << 20, transcendentals=0),
     )(asked, cnt, seg_counts, where, base, *attitude)
 
@@ -424,7 +430,7 @@
             pltpu.VMEM((rows, SRC_GROUP), jnp.float32),
             pltpu.SemaphoreType.DMA(()),
         ] + [table] * LATE_STREAMS,
-        compiler_params=pltpu.CompilerParams(vmem_limit_bytes=VMEM_LIMIT),
+        compiler_params=pltpu.CompilerParams(vmem_limit_bytes=LATE_PICK_VMEM),
         cost_estimate=pl.CostEstimate(flops=7 * COST_US, bytes_accessed=1 << 20, transcendentals=0),
     )(asked, cnt, seg_counts, where, part, *attitude, *[returned[owner] for owner in owners])
     return out[0], list(out[1:])
@@ -462,7 +468,7 @@
             pltpu.VMEM(shape, jnp.float32),
             pltpu.SemaphoreType.DMA((shape[0],)),
         ] + [pltpu.VMEM((part.shape[0] + 8, SRC_GROUP), jnp.float32)] * LATE_STREAMS,
-        compiler_params=pltpu.CompilerParams(vmem_limit_bytes=VMEM_LIMIT),
+        compiler_params=pltpu.CompilerParams(vmem_limit_bytes=LATE_VMEM),
         cost_estimate=pl.CostEstimate(flops=4 * COST_US, bytes_accessed=1 << 20, transcendentals=0),
     )(asked, cnt, where, part, *[returned[owner] for owner in owners])
 
@@ -558,9 +564,9 @@
 
     def first_hop(right, left):
         nonlocal asked
-        held, right, left = lax.optimization_barrier((wanted, right, left))
+        basis_part([right, left])
+        held, _ = lax.optimization_barrier((wanted, made[0][1]))
         asked = lax.all_to_all(held, "tm", split_axis=0, concat_axis=0, tiled=True)
-        basis_part([right, left])
         return right, left
 
     def second_hop(right, left):

time: 158 us -> 151 us (0.956)
  Pallas kernels: 58.9 us -> 51.9 us
  starting transfers between devices: 45.1 us -> 43 us
    ppermute x3, waiting for transfers between devices: 16.5 us -> 8.56 us  [pass_along(): lax.ppermute(left, 'sky', [(i, i - 1) for i in range(1, count - hop + 1)])]
    ppermute x28, waiting for transfers between devices: 19.8 us -> 26.1 us  [exchange(): lax.ppermute(blocks[step], 'tm', [(i, i ^ step) for i in range(count)])]
    all_to_all x1, waiting for transfers between devices: 0.01 us -> 4.02 us  [first_hop(): asked = lax.all_to_all(held, 'tm', split_axis=0, concat_axis=0, tiled=True)]
    pallas_call x2, Pallas kernels: 10 us -> 6.67 us  [place_early(): pl.pallas_call(functools.partial(early_kernel, owners, table_base), in_sp...]
    pallas_call x1, Pallas kernels: 6.91 us -> 4.96 us  [place_late_and_pick(): pl.pallas_call(functools.partial(late_pick_kernel, tm_count, len(attitude...]
    ppermute x28, starting transfers between devices: 29.8 us -> 28 us  [exchange(): lax.ppermute(blocks[step], 'tm', [(i, i ^ step) for i in range(count)])]
  transfers between devices with their start and end apart: 35 -> 35, of which waited for: 12 -> 16; matrix products, arithmetic and copies ran while one was open for 6% -> 7% of each run, Pallas kernels for 17% -> 16%
where the time goes in v6:
time: 151 us; the launch traced here: 150 us
  Pallas kernels  51.9 us (34%)
  starting transfers between devices  43 us (28%)
  waiting for transfers between devices  38.7 us (26%)
  other arithmetic  9.48 us (6%)
  local copies, waits for them, and re-layouts  5.4 us (4%)
    ppermute x28, starting transfers between devices, exchange(): lax.ppermute(blocks[step], 'tm', [(i, i ^ step) for i in range(count)])  28 us
    ppermute x28, waiting for transfers between devices, exchange(): lax.ppermute(blocks[step], 'tm', [(i, i ^ step) for i in range(count)])  26.1 us
    pallas_call x4, Pallas kernels, make_basis(): pl.pallas_call(functools.partial(basis_kernel, len(after)), grid=(sched_d...  16.8 us
    pallas_call x2, Pallas kernels, fit_plans(): pl.pallas_call(functools.partial(fit_kernel, tm_count), in_specs=[SMEM, S...  16.6 us
    ppermute x3, waiting for transfers between devices, pass_along(): lax.ppermute(left, 'sky', [(i, i - 1) for i in range(1, count - hop + 1)])  8.56 us
    pallas_call x2, Pallas kernels, place_early(): pl.pallas_call(functools.partial(early_kernel, owners, table_base), in_sp...  6.67 us
    ppermute x3, starting transfers between devices, pass_along(): lax.ppermute(right, 'sky', [(i, i + 1) for i in range(hop - 1, count - 1)])  6.08 us
    all_to_all x1, starting transfers between devices, first_hop(): asked = lax.all_to_all(held, 'tm', split_axis=0, concat_axis=0, tiled=True)  5.1 us
  transfers between devices with their start and end apart: 35, of which 16 were waited for; matrix products, arithmetic and copies ran while one was open for 7% of the time, Pallas kernels for 16%

profile of v6, /device:TPU:1, one launch (start us, length us, event | category | flops | bytes accessed | tf_op | source)
XLA Modules:
  0.0 149.8 jit_solution(5146862985666563725)
XLA Ops:
  0.6 1.3 collective-permute-start.1
  1.9 4.7 %collective-permute-start = (bf16[4,128,512]{2,1,0:T(8,128)(2,1)}, bf16[4,128,512]{2,1,0:T(8,128)(2,1)S(1)}, u32[]{:S(2)}, u32[]{:S(2)}) collective-permute-start(bf16[4,128,512]{2,1,0:T(8,128)(2,1)} %own_ref.3), channel_id=1, source_target_pairs={{0,1},{1,2},{2,3},{4,5},{5,6},{6,7},{8,9},{9,10},{10,11},{12,13},{... | collective-permute-start | bytes 1572872 | tf_op jit(solution)/shard_map/ppermute | solution.py:539
  10.9 3.4 %select_reduce_fusion = s32[4096]{0:T(1024)S(1)} fusion(s32[2048]{0:T(1024)S(1)} %bitcast.41, s32[2048]{0:T(1024)S(1)} %bitcast.40), kind=kLoop, calls=%fused_computation | loop fusion | flops 25161728 | bytes 32768 | tf_op jit(solution)/shard_map/reduce_sum | solution.py:501
  15.2 1.3 collective-permute-done.1.refs_1_
  16.5 1.3 collective-permute-start.3
  18.6 4.2 %shard_map.77 = (bf16[2,256,2048]{2,1,0:T(8,128)(2,1)S(1)}, f32[2,1,2048]{2,1,0:T(1,128)S(1)}) custom-call(f32[512,128]{1,0:T(8,128)S(1)} %broadcast_in_dim.50.time_ref, f32[1,1024]{1,0:T(1,128)S(1)} %bitcast.28, f32[1,1024]{1,0:T(1,128)S(1)} %bitcast.32, bf16[4,128,512]{2,1,0:T(8,128)(2,1)S(1)} %collective-permute-done.refs_0_, ...), custom_call_target="tpu_custom_call" | custom-call | flops 5242880000 | bytes 2097152 | tf_op jit(solution)/shard_map/pallas_call | solution.py:87
  22.9 1.3 copy-done.5
  24.8 5.1 %all-to-all-start = ((s32[8,1,512]{2,1,0:T(1,128)}), s32[8,1,512]{2,1,0:T(1,128)S(1)}, u32[]{:S(2)}, u32[]{:S(2)}) async-start(s32[8,1,512]{2,1,0:T(1,128)} %all_to_all.6), calls=%async_computation | async-start | bytes 32768 | tf_op jit(solution)/shard_map/all_to_all | solution.py:569
  29.9 4.0 %all-to-all-done = s32[8,1,512]{2,1,0:T(1,128)S(1)} async-done(((s32[8,1,512]{2,1,0:T(1,128)}), s32[8,1,512]{2,1,0:T(1,128)S(1)}, u32[]{:S(2)}, u32[]{:S(2)}) %all-to-all-start) | async-done | bytes 16416 | tf_op jit(solution)/shard_map/all_to_all | solution.py:569
  34.2 1.3 collective-permute-start.5
  36.3 4.2 %shard_map.80 = (bf16[2,256,2048]{2,1,0:T(8,128)(2,1)S(1)}, f32[2,1,2048]{2,1,0:T(1,128)S(1)}) custom-call(f32[512,128]{1,0:T(8,128)S(1)} %broadcast_in_dim.55.time_ref, f32[1,1024]{1,0:T(1,128)S(1)} %bitcast.29, f32[1,1024]{1,0:T(1,128)S(1)} %bitcast.33, bf16[4,128,512]{2,1,0:T(8,128)(2,1)S(1)} %collective-permute-done.2.refs_2_.refs_0_, ...), custom_call_target="tpu_custom_call" | custom-call | flops 5242880000 | bytes 2097152 | tf_op jit(solution)/shard_map/pallas_call | solution.py:87
  40.7 4.2 %shard_map.79 = (bf16[2,256,2048]{2,1,0:T(8,128)(2,1)S(1)}, f32[2,1,2048]{2,1,0:T(1,128)S(1)}) custom-call(f32[512,128]{1,0:T(8,128)S(1)} %broadcast_in_dim.53.time_ref, f32[1,1024]{1,0:T(1,128)S(1)} %bitcast.30, f32[1,1024]{1,0:T(1,128)S(1)} %bitcast.34, bf16[4,128,512]{2,1,0:T(8,128)(2,1)S(1)} %collective-permute-done.2.refs_2_.refs_0_, ...), custom_call_target="tpu_custom_call" | custom-call | flops 5242880000 | bytes 2097152 | tf_op jit(solution)/shard_map/pallas_call | solution.py:87
  45.0 7.3 %collective-permute-done.5.refs_5_ = bf16[4,128,512]{2,1,0:T(8,128)(2,1)S(1)} collective-permute-done((bf16[4,128,512]{2,1,0:T(8,128)(2,1)S(1)}, bf16[4,128,512]{2,1,0:T(8,128)(2,1)S(1)}, u32[]{:S(2)}, u32[]{:S(2)}) %collective-permute-start.5) | collective-permute-done | bytes 524320 | tf_op jit(solution)/shard_map/ppermute | solution.py:540
  52.3 3.5 %shard_map.78 = (bf16[512,128]{1,0:T(8,128)(2,1)S(1)}, bf16[512,128]{1,0:T(8,128)(2,1)S(1)}, bf16[512,128]{1,0:T(8,128)(2,1)S(1)}, bf16[512,128]{1,0:T(8,128)(2,...) custom-call(s32[4096]{0:T(1024)S(1)} %bitcast.23, ...), custom_call_target="tpu_custom_call" | custom-call | flops 5000000000 | bytes 1048576 | tf_op jit(solution)/shard_map/pallas_call | solution.py:361
  55.8 3.2 %collective-permute-start.6 = (bf16[512,128]{1,0:T(8,128)(2,1)S(1)}, bf16[512,128]{1,0:T(8,128)(2,1)S(1)}, u32[]{:S(2)}, u32[]{:S(2)}) collective-permute-start(bf16[512,128]{1,0:T(8,128)(2,1)S(1)} %get-tuple-element.48), channel_id=1, source_target_pairs={{0,4},{4,0},{8,12},{12,8},{16,20},{20,16},{24,28},{28,24},{1,5},{5... | collective-permute-start | bytes 393224 | tf_op jit(solution)/shard_map/ppermute | solution.py:530
  59.0 1.7 %collective-permute-start.8 = (bf16[512,128]{1,0:T(8,128)(2,1)S(1)}, bf16[512,128]{1,0:T(8,128)(2,1)S(1)}, u32[]{:S(2)}, u32[]{:S(2)}) collective-permute-start(bf16[512,128]{1,0:T(8,128)(2,1)S(1)} %get-tuple-element.50), channel_id=1, source_target_pairs={{0,12},{4,8},{8,4},{12,0},{16,28},{20,24},{24,20},{28,16},{1,13},{... | collective-permute-start | bytes 393224 | tf_op jit(solution)/shard_map/ppermute | solution.py:530
  60.6 1.8 %collective-permute-start.10 = (bf16[512,128]{1,0:T(8,128)(2,1)S(1)}, bf16[512,128]{1,0:T(8,128)(2,1)S(1)}, u32[]{:S(2)}, u32[]{:S(2)}) collective-permute-start(bf16[512,128]{1,0:T(8,128)(2,1)S(1)} %get-tuple-element.52), channel_id=1, source_target_pairs={{0,20},{4,16},{8,28},{12,24},{16,4},{20,0},{24,12},{28,8},{1,21},{... | collective-permute-start | bytes 393224 | tf_op jit(solution)/shard_map/ppermute | solution.py:530
  62.6 4.2 %shard_map.81 = (bf16[2,256,2048]{2,1,0:T(8,128)(2,1)S(1)}, f32[2,1,2048]{2,1,0:T(1,128)S(1)}) custom-call(f32[512,128]{1,0:T(8,128)S(1)} %broadcast_in_dim.57.time_ref, f32[1,1024]{1,0:T(1,128)S(1)} %bitcast.31, f32[1,1024]{1,0:T(1,128)S(1)} %bitcast.35, bf16[512,128]{1,0:T(8,128)(2,1)S(1)} %get-tuple-element.47.refs_0_), custom_call_target="tpu_custom_call" | custom-call | flops 5242880000 | bytes 2097152 | tf_op jit(solution)/shard_map/pallas_call | solution.py:87
  66.9 2.6 %collective-permute-start.12 = (bf16[512,128]{1,0:T(8,128)(2,1)S(1)}, bf16[512,128]{1,0:T(8,128)(2,1)S(1)}, u32[]{:S(2)}, u32[]{:S(2)}) collective-permute-start(bf16[512,128]{1,0:T(8,128)(2,1)S(1)} %get-tuple-element.54), channel_id=1, source_target_pairs={{0,28},{4,24},{8,20},{12,16},{16,12},{20,8},{24,4},{28,0},{1,29},{... | collective-permute-start | bytes 393224 | tf_op jit(solution)/shard_map/ppermute | solution.py:530
  69.5 3.4 %collective-permute-done.11.refs_6_ = bf16[512,128]{1,0:T(8,128)(2,1)S(1)} collective-permute-done((bf16[512,128]{1,0:T(8,128)(2,1)S(1)}, bf16[512,128]{1,0:T(8,128)(2,1)S(1)}, u32[]{:S(2)}, u32[]{:S(2)}) %collective-permute-start.11) | collective-permute-done | bytes 131104 | tf_op jit(solution)/shard_map/ppermute | solution.py:530
  72.9 3.0 %collective-permute-done.12.refs_7_ = bf16[512,128]{1,0:T(8,128)(2,1)S(1)} collective-permute-done((bf16[512,128]{1,0:T(8,128)(2,1)S(1)}, bf16[512,128]{1,0:T(8,128)(2,1)S(1)}, u32[]{:S(2)}, u32[]{:S(2)}) %collective-permute-start.12) | collective-permute-done | bytes 131104 | tf_op jit(solution)/shard_map/ppermute | solution.py:530
  75.8 8.6 %shard_map.82 = (bf16[512,128]{1,0:T(8,128)(2,1)S(1)}, bf16[512,128]{1,0:T(8,128)(2,1)S(1)}, bf16[512,128]{1,0:T(8,128)(2,1)S(1)}, bf16[512,128]{1,0:T(8,128)(2,...) custom-call(s32[8,24]{1,0:T(8,128)S(1)} %get-tuple-element.106.src_r, ...), custom_call_target="tpu_custom_call" | custom-call | flops 10737418240 | bytes 8388608 | tf_op jit(solution)/shard_map/pallas_call | solution.py:210
  85.3 1.6 %collective-permute-start.16 = (bf16[512,128]{1,0:T(8,128)(2,1)S(1)}, bf16[512,128]{1,0:T(8,128)(2,1)S(1)}, u32[]{:S(2)}, u32[]{:S(2)}) collective-permute-start(bf16[512,128]{1,0:T(8,128)(2,1)S(1)} %get-tuple-element.66), channel_id=1, source_target_pairs={{0,20},{4,16},{8,28},{12,24},{16,4},{20,0},{24,12},{28,8},{1,21},{... | collective-permute-start | bytes 393224 | tf_op jit(solution)/shard_map/ppermute | solution.py:530
  87.0 1.0 collective-permute-start.17
  88.3 1.4 collective-permute-done.14.refs_2_
  89.6 1.7 %collective-permute-start.19 = (bf16[512,128]{1,0:T(8,128)(2,1)S(1)}, bf16[512,128]{1,0:T(8,128)(2,1)S(1)}, u32[]{:S(2)}, u32[]{:S(2)}) collective-permute-start(bf16[512,128]{1,0:T(8,128)(2,1)S(1)} %get-tuple-element.69), channel_id=1, source_target_pairs={{0,28},{4,24},{8,20},{12,16},{16,12},{20,8},{24,4},{28,0},{1,29},{... | collective-permute-start | bytes 393224 | tf_op jit(solution)/shard_map/ppermute | solution.py:530
  91.4 1.5 collective-permute-done.16.refs_4_
  93.4 3.3 %shard_map.83.part_ref = f32[4096,128]{1,0:T(8,128)S(1)} custom-call(s32[4096]{0:T(1024)S(1)} %bitcast.24, s32[8]{0:T(128)S(1)} %fusion.4.cnt_ref, s32[2]{0:T(128)S(1)} %pad_add_fusion.where_ref, bf16[4,512,256]{2,1,0:T(8,128)(2,1)S(1)} %copy-done, bf16[512,128]{1,0:T(8,128)(2,1)S(1)} %get-tuple-element.62.refs_0_, ...), custom_call_target="tpu_custom_call" | custom-call | flops 6000000000 | bytes 1048576 | tf_op jit(solution)/shard_map/pallas_call | solution.py:333
  96.8 2.9 %collective-permute-done.19.refs_7_ = bf16[512,128]{1,0:T(8,128)(2,1)S(1)} collective-permute-done((bf16[512,128]{1,0:T(8,128)(2,1)S(1)}, bf16[512,128]{1,0:T(8,128)(2,1)S(1)}, u32[]{:S(2)}, u32[]{:S(2)}) %collective-permute-start.19) | collective-permute-done | bytes 131104 | tf_op jit(solution)/shard_map/ppermute | solution.py:530
  99.6 5.0 %shard_map.84 = (f32[4096,128]{1,0:T(8,128)S(1)}, bf16[512,128]{1,0:T(8,128)(2,1)S(1)}, bf16[512,128]{1,0:T(8,128)(2,1)S(1)}, bf16[512,128]{1,0:T(8,128)(2,1)S(1...) custom-call(s32[4096]{0:T(1024)S(1)} %bitcast.25, ...), custom_call_target="tpu_custom_call" | custom-call | flops 7000000000 | bytes 1048576 | tf_op jit(solution)/shard_map/pallas_call | solution.py:419
  104.6 1.3 copy-done.3
  105.9 2.1 %collective-permute-start.20 = (bf16[512,128]{1,0:T(8,128)(2,1)S(1)}, bf16[512,128]{1,0:T(8,128)(2,1)S(1)}, u32[]{:S(2)}, u32[]{:S(2)}) collective-permute-start(bf16[512,128]{1,0:T(8,128)(2,1)S(1)} %get-tuple-element.72), channel_id=1, source_target_pairs={{0,4},{4,0},{8,12},{12,8},{16,20},{20,16},{24,28},{28,24},{1,5},{5... | collective-permute-start | bytes 393224 | tf_op jit(solution)/shard_map/ppermute | solution.py:530
  108.0 1.6 %collective-permute-start.22 = (bf16[512,128]{1,0:T(8,128)(2,1)S(1)}, bf16[512,128]{1,0:T(8,128)(2,1)S(1)}, u32[]{:S(2)}, u32[]{:S(2)}) collective-permute-start(bf16[512,128]{1,0:T(8,128)(2,1)S(1)} %get-tuple-element.74), channel_id=1, source_target_pairs={{0,12},{4,8},{8,4},{12,0},{16,28},{20,24},{24,20},{28,16},{1,13},{... | collective-permute-start | bytes 393224 | tf_op jit(solution)/shard_map/ppermute | solution.py:530
  109.6 1.9 %collective-permute-start.24 = (bf16[512,128]{1,0:T(8,128)(2,1)S(1)}, bf16[512,128]{1,0:T(8,128)(2,1)S(1)}, u32[]{:S(2)}, u32[]{:S(2)}) collective-permute-start(bf16[512,128]{1,0:T(8,128)(2,1)S(1)} %get-tuple-element.76), channel_id=1, source_target_pairs={{0,20},{4,16},{8,28},{12,24},{16,4},{20,0},{24,12},{28,8},{1,21},{... | collective-permute-start | bytes 393224 | tf_op jit(solution)/shard_map/ppermute | solution.py:530
  111.5 1.6 %collective-permute-done.21.refs_2_ = bf16[512,128]{1,0:T(8,128)(2,1)S(1)} collective-permute-done((bf16[512,128]{1,0:T(8,128)(2,1)S(1)}, bf16[512,128]{1,0:T(8,128)(2,1)S(1)}, u32[]{:S(2)}, u32[]{:S(2)}) %collective-permute-start.21) | collective-permute-done | bytes 131104 | tf_op jit(solution)/shard_map/ppermute | solution.py:530
  113.1 0.9 collective-permute-start.26
  114.0 2.7 %collective-permute-done.22.refs_3_ = bf16[512,128]{1,0:T(8,128)(2,1)S(1)} collective-permute-done((bf16[512,128]{1,0:T(8,128)(2,1)S(1)}, bf16[512,128]{1,0:T(8,128)(2,1)S(1)}, u32[]{:S(2)}, u32[]{:S(2)}) %collective-permute-start.22) | collective-permute-done | bytes 131104 | tf_op jit(solution)/shard_map/ppermute | solution.py:530
  116.7 6.6 %collective-permute-done.24.refs_5_ = bf16[512,128]{1,0:T(8,128)(2,1)S(1)} collective-permute-done((bf16[512,128]{1,0:T(8,128)(2,1)S(1)}, bf16[512,128]{1,0:T(8,128)(2,1)S(1)}, u32[]{:S(2)}, u32[]{:S(2)}) %collective-permute-start.24) | collective-permute-done | bytes 131104 | tf_op jit(solution)/shard_map/ppermute | solution.py:530
  123.3 7.9 %shard_map.85 = (bf16[512,128]{1,0:T(8,128)(2,1)S(1)}, bf16[512,128]{1,0:T(8,128)(2,1)S(1)}, bf16[512,128]{1,0:T(8,128)(2,1)S(1)}, bf16[512,128]{1,0:T(8,128)(2,...) custom-call(s32[8,24]{1,0:T(8,128)S(1)} %get-tuple-element.106.src_r, ...), custom_call_target="tpu_custom_call" | custom-call | flops 10737418240 | bytes 8388608 | tf_op jit(solution)/shard_map/pallas_call | solution.py:210
  131.7 1.9 %collective-permute-start.30 = (bf16[512,128]{1,0:T(8,128)(2,1)S(1)}, bf16[512,128]{1,0:T(8,128)(2,1)S(1)}, u32[]{:S(2)}, u32[]{:S(2)}) collective-permute-start(bf16[512,128]{1,0:T(8,128)(2,1)S(1)} %get-tuple-element.83), channel_id=1, source_target_pairs={{0,20},{4,16},{8,28},{12,24},{16,4},{20,0},{24,12},{28,8},{1,21},{... | collective-permute-start | bytes 393224 | tf_op jit(solution)/shard_map/ppermute | solution.py:530
  133.6 1.0 collective-permute-start.31
  134.6 0.8 reduce.1
  136.0 2.9 %collective-permute-start.33 = (bf16[512,128]{1,0:T(8,128)(2,1)S(1)}, bf16[512,128]{1,0:T(8,128)(2,1)S(1)}, u32[]{:S(2)}, u32[]{:S(2)}) collective-permute-start(bf16[512,128]{1,0:T(8,128)(2,1)S(1)} %get-tuple-element.86), channel_id=1, source_target_pairs={{0,28},{4,24},{8,20},{12,16},{16,12},{20,8},{24,4},{28,0},{1,29},{... | collective-permute-start | bytes 393224 | tf_op jit(solution)/shard_map/ppermute | solution.py:530
  139.4 1.0 collective-permute-done.31.refs_5_
  140.4 1.6 %copy-done.4 = f32[4096,128]{1,0:T(8,128)S(1)} copy-done((f32[4096,128]{1,0:T(8,128)S(1)}, f32[4096,128]{1,0:T(8,128)}, u32[]{:S(2)}) %copy-start.4) | copy-done | bytes 2097176
  142.0 3.4 %shard_map.86.part_ref = f32[4096,128]{1,0:T(8,128)S(1)} custom-call(s32[4096]{0:T(1024)S(1)} %bitcast.26, s32[8]{0:T(128)S(1)} %fusion.4.cnt_ref, s32[2]{0:T(128)S(1)} %pad_add_fusion.where_ref, f32[4096,128]{1,0:T(8,128)S(1)} %copy-done.4, bf16[512,128]{1,0:T(8,128)(2,1)S(1)} %get-tuple-element.79.refs_0_, ...), custom_call_target="tpu_custom_call" | custom-call | flops 6000000000 | bytes 1048576 | tf_op jit(solution)/shard_map/pallas_call | solution.py:333
  145.4 0.8 collective-permute-done.33.refs_1_
  146.2 3.4 %shard_map.87 = f32[4,512,256]{2,1,0:T(8,128)} custom-call(s32[4096]{0:T(1024)S(1)} %bitcast.27, s32[8]{0:T(128)S(1)} %fusion.4.cnt_ref, s32[2]{0:T(128)S(1)} %pad_add_fusion.where_ref, f32[4096,128]{1,0:T(8,128)S(1)} %shard_map.86.part_ref, bf16[512,128]{1,0:T(8,128)(2,1)S(1)} %collective-permute-done.32.refs_0_, ...), custom_call_target="tpu_custom_call" | custom-call | flops 4000000000 | bytes 1048576 | tf_op jit(solution)/shard_map/pallas_call | solution.py:461
  (86 shorter events, 11.3 us)
Async XLA Ops:
  0.6 15.9 %collective-permute-start.1 = (bf16[4,128,512]{2,1,0:T(8,128)(2,1)}, bf16[4,128,512]{2,1,0:T(8,128)(2,1)S(1)}, u32[]{:S(2)}, u32[]{:S(2)}) collective-permute-start(bf16[4,128,512]{2,1,0:T(8,128)(2,1)} %own_ref.3), channel_id=1, source_target_pairs={{1,0},{2,1},{3,2},{5,4},{6,5},{7,6},{9,8},{10,9},{11,10},{13,12},{... | collective-permute-start | bytes 1572872 | tf_op jit(solution)/shard_map/ppermute | solution.py:540
  1.9 15.9 %collective-permute-start = (bf16[4,128,512]{2,1,0:T(8,128)(2,1)}, bf16[4,128,512]{2,1,0:T(8,128)(2,1)S(1)}, u32[]{:S(2)}, u32[]{:S(2)}) collective-permute-start(bf16[4,128,512]{2,1,0:T(8,128)(2,1)} %own_ref.3), channel_id=1, source_target_pairs={{0,1},{1,2},{2,3},{4,5},{5,6},{6,7},{8,9},{9,10},{10,11},{12,13},{... | collective-permute-start | bytes 1572872 | tf_op jit(solution)/shard_map/ppermute | solution.py:539
  16.5 17.7 %collective-permute-start.3 = (bf16[4,128,512]{2,1,0:T(8,128)(2,1)S(1)}, bf16[4,128,512]{2,1,0:T(8,128)(2,1)S(1)}, u32[]{:S(2)}, u32[]{:S(2)}) collective-permute-start(bf16[4,128,512]{2,1,0:T(8,128)(2,1)S(1)} %collective-permute-done.1.refs_1_), channel_id=1, source_target_pairs={{1,0},{2,1},{5,4},{6,5},{9,8},{10,9},{13,12},{14,13},{17,16},{18,1... | collective-permute-start | bytes 1572872 | tf_op jit(solution)/shard_map/ppermute | solution.py:540
  17.8 17.7 %collective-permute-start.2 = (bf16[4,128,512]{2,1,0:T(8,128)(2,1)S(1)}, bf16[4,128,512]{2,1,0:T(8,128)(2,1)S(1)}, u32[]{:S(2)}, u32[]{:S(2)}) collective-permute-start(bf16[4,128,512]{2,1,0:T(8,128)(2,1)S(1)} %collective-permute-done.refs_0_), channel_id=1, source_target_pairs={{1,2},{2,3},{5,6},{6,7},{9,10},{10,11},{13,14},{14,15},{17,18},{18... | collective-permute-start | bytes 1572872 | tf_op jit(solution)/shard_map/ppermute | solution.py:539
  22.9 1.3 copy-start.5
  24.8 9.1 %all-to-all-start = ((s32[8,1,512]{2,1,0:T(1,128)}), s32[8,1,512]{2,1,0:T(1,128)S(1)}, u32[]{:S(2)}, u32[]{:S(2)}) async-start(s32[8,1,512]{2,1,0:T(1,128)} %all_to_all.6), calls=%async_computation | async-start | bytes 32768 | tf_op jit(solution)/shard_map/all_to_all | solution.py:569
  34.2 18.1 %collective-permute-start.5 = (bf16[4,128,512]{2,1,0:T(8,128)(2,1)S(1)}, bf16[4,128,512]{2,1,0:T(8,128)(2,1)S(1)}, u32[]{:S(2)}, u32[]{:S(2)}) collective-permute-start(bf16[4,128,512]{2,1,0:T(8,128)(2,1)S(1)} %collective-permute-done.3.refs_3_.refs_1_), channel_id=1, source_target_pairs={{1,0},{5,4},{9,8},{13,12},{17,16},{21,20},{25,24},{29,28}} | collective-permute-start | bytes 1572872 | tf_op jit(solution)/shard_map/ppermute | solution.py:540
  35.5 16.8 %collective-permute-start.4 = (bf16[4,128,512]{2,1,0:T(8,128)(2,1)S(1)}, bf16[4,128,512]{2,1,0:T(8,128)(2,1)S(1)}, u32[]{:S(2)}, u32[]{:S(2)}) collective-permute-start(bf16[4,128,512]{2,1,0:T(8,128)(2,1)S(1)} %collective-permute-done.2.refs_2_.refs_0_), channel_id=1, source_target_pairs={{2,3},{6,7},{10,11},{14,15},{18,19},{22,23},{26,27},{30,31}} | collective-permute-start | bytes 1572872 | tf_op jit(solution)/shard_map/ppermute | solution.py:539
  40.7 11.6 %copy-start = (bf16[4,512,256]{2,1,0:T(8,128)(2,1)S(1)}, bf16[4,512,256]{2,1,0:T(8,128)(2,1)}, u32[]{:S(2)}) copy-start(bf16[4,512,256]{2,1,0:T(8,128)(2,1)} %base_ref.3) | copy-start | bytes 3145732
  40.7 11.6 %copy-start.1 = (bf16[4,128,512]{2,1,0:T(8,128)(2,1)S(1)}, bf16[4,128,512]{2,1,0:T(8,128)(2,1)}, u32[]{:S(2)}) copy-start(bf16[4,128,512]{2,1,0:T(8,128)(2,1)} %own_ref.3) | copy-start | bytes 1572868
  40.7 11.6 %copy-start.2 = (s32[4]{0:T(128)S(1)}, s32[4]{0:T(128)}, u32[]{:S(2)}) copy-start(s32[4]{0:T(128)} %count_ref.3) | copy-start | bytes 52
  55.8 11.0 %collective-permute-start.6 = (bf16[512,128]{1,0:T(8,128)(2,1)S(1)}, bf16[512,128]{1,0:T(8,128)(2,1)S(1)}, u32[]{:S(2)}, u32[]{:S(2)}) collective-permute-start(bf16[512,128]{1,0:T(8,128)(2,1)S(1)} %get-tuple-element.48), channel_id=1, source_target_pairs={{0,4},{4,0},{8,12},{12,8},{16,20},{20,16},{24,28},{28,24},{1,5},{5... | collective-permute-start | bytes 393224 | tf_op jit(solution)/shard_map/ppermute | solution.py:530
  58.9 8.0 %collective-permute-start.7 = (bf16[512,128]{1,0:T(8,128)(2,1)S(1)}, bf16[512,128]{1,0:T(8,128)(2,1)S(1)}, u32[]{:S(2)}, u32[]{:S(2)}) collective-permute-start(bf16[512,128]{1,0:T(8,128)(2,1)S(1)} %get-tuple-element.49), channel_id=1, source_target_pairs={{0,8},{4,12},{8,0},{12,4},{16,24},{20,28},{24,16},{28,20},{1,9},{5... | collective-permute-start | bytes 393224 | tf_op jit(solution)/shard_map/ppermute | solution.py:530
  59.0 10.5 %collective-permute-start.8 = (bf16[512,128]{1,0:T(8,128)(2,1)S(1)}, bf16[512,128]{1,0:T(8,128)(2,1)S(1)}, u32[]{:S(2)}, u32[]{:S(2)}) collective-permute-start(bf16[512,128]{1,0:T(8,128)(2,1)S(1)} %get-tuple-element.50), channel_id=1, source_target_pairs={{0,12},{4,8},{8,4},{12,0},{16,28},{20,24},{24,20},{28,16},{1,13},{... | collective-permute-start | bytes 393224 | tf_op jit(solution)/shard_map/ppermute | solution.py:530
  60.6 8.8 %collective-permute-start.9 = (bf16[512,128]{1,0:T(8,128)(2,1)S(1)}, bf16[512,128]{1,0:T(8,128)(2,1)S(1)}, u32[]{:S(2)}, u32[]{:S(2)}) collective-permute-start(bf16[512,128]{1,0:T(8,128)(2,1)S(1)} %get-tuple-element.51), channel_id=1, source_target_pairs={{0,16},{4,20},{8,24},{12,28},{16,0},{20,4},{24,8},{28,12},{1,17},{... | collective-permute-start | bytes 393224 | tf_op jit(solution)/shard_map/ppermute | solution.py:530
  60.6 8.8 %collective-permute-start.10 = (bf16[512,128]{1,0:T(8,128)(2,1)S(1)}, bf16[512,128]{1,0:T(8,128)(2,1)S(1)}, u32[]{:S(2)}, u32[]{:S(2)}) collective-permute-start(bf16[512,128]{1,0:T(8,128)(2,1)S(1)} %get-tuple-element.52), channel_id=1, source_target_pairs={{0,20},{4,16},{8,28},{12,24},{16,4},{20,0},{24,12},{28,8},{1,21},{... | collective-permute-start | bytes 393224 | tf_op jit(solution)/shard_map/ppermute | solution.py:530
  62.6 13.2 %copy-start.6 = (bf16[2,256,2048]{2,1,0:T(8,128)(2,1)S(1)}, bf16[2,256,2048]{2,1,0:T(8,128)(2,1)}, u32[]{:S(2)}) copy-start(bf16[2,256,2048]{2,1,0:T(8,128)(2,1)} %copy-done.5) | copy-start | bytes 6291460
  66.8 6.0 %collective-permute-start.11 = (bf16[512,128]{1,0:T(8,128)(2,1)S(1)}, bf16[512,128]{1,0:T(8,128)(2,1)S(1)}, u32[]{:S(2)}, u32[]{:S(2)}) collective-permute-start(bf16[512,128]{1,0:T(8,128)(2,1)S(1)} %get-tuple-element.53), channel_id=1, source_target_pairs={{0,24},{4,28},{8,16},{12,20},{16,8},{20,12},{24,0},{28,4},{1,25},{... | collective-permute-start | bytes 393224 | tf_op jit(solution)/shard_map/ppermute | solution.py:530
  66.9 8.9 %collective-permute-start.12 = (bf16[512,128]{1,0:T(8,128)(2,1)S(1)}, bf16[512,128]{1,0:T(8,128)(2,1)S(1)}, u32[]{:S(2)}, u32[]{:S(2)}) collective-permute-start(bf16[512,128]{1,0:T(8,128)(2,1)S(1)} %get-tuple-element.54), channel_id=1, source_target_pairs={{0,28},{4,24},{8,20},{12,16},{16,12},{20,8},{24,4},{28,0},{1,29},{... | collective-permute-start | bytes 393224 | tf_op jit(solution)/shard_map/ppermute | solution.py:530
  84.5 3.5 %collective-permute-start.13 = (bf16[512,128]{1,0:T(8,128)(2,1)S(1)}, bf16[512,128]{1,0:T(8,128)(2,1)S(1)}, u32[]{:S(2)}, u32[]{:S(2)}) collective-permute-start(bf16[512,128]{1,0:T(8,128)(2,1)S(1)} %get-tuple-element.63), channel_id=1, source_target_pairs={{0,4},{4,0},{8,12},{12,8},{16,20},{20,16},{24,28},{28,24},{1,5},{5... | collective-permute-start | bytes 393224 | tf_op jit(solution)/shard_map/ppermute | solution.py:530
  84.8 4.8 %collective-permute-start.14 = (bf16[512,128]{1,0:T(8,128)(2,1)S(1)}, bf16[512,128]{1,0:T(8,128)(2,1)S(1)}, u32[]{:S(2)}, u32[]{:S(2)}) collective-permute-start(bf16[512,128]{1,0:T(8,128)(2,1)S(1)} %get-tuple-element.64), channel_id=1, source_target_pairs={{0,16},{4,20},{8,24},{12,28},{16,0},{20,4},{24,8},{28,12},{1,17},{... | collective-permute-start | bytes 393224 | tf_op jit(solution)/shard_map/ppermute | solution.py:530
  84.8 6.6 %collective-permute-start.15 = (bf16[512,128]{1,0:T(8,128)(2,1)S(1)}, bf16[512,128]{1,0:T(8,128)(2,1)S(1)}, u32[]{:S(2)}, u32[]{:S(2)}) collective-permute-start(bf16[512,128]{1,0:T(8,128)(2,1)S(1)} %get-tuple-element.65), channel_id=1, source_target_pairs={{0,8},{4,12},{8,0},{12,4},{16,24},{20,28},{24,16},{28,20},{1,9},{5... | collective-permute-start | bytes 393224 | tf_op jit(solution)/shard_map/ppermute | solution.py:530
  85.3 7.5 %collective-permute-start.16 = (bf16[512,128]{1,0:T(8,128)(2,1)S(1)}, bf16[512,128]{1,0:T(8,128)(2,1)S(1)}, u32[]{:S(2)}, u32[]{:S(2)}) collective-permute-start(bf16[512,128]{1,0:T(8,128)(2,1)S(1)} %get-tuple-element.66), channel_id=1, source_target_pairs={{0,20},{4,16},{8,28},{12,24},{16,4},{20,0},{24,12},{28,8},{1,21},{... | collective-permute-start | bytes 393224 | tf_op jit(solution)/shard_map/ppermute | solution.py:530
  87.0 6.5 %collective-permute-start.17 = (bf16[512,128]{1,0:T(8,128)(2,1)S(1)}, bf16[512,128]{1,0:T(8,128)(2,1)S(1)}, u32[]{:S(2)}, u32[]{:S(2)}) collective-permute-start(bf16[512,128]{1,0:T(8,128)(2,1)S(1)} %get-tuple-element.67), channel_id=1, source_target_pairs={{0,12},{4,8},{8,4},{12,0},{16,28},{20,24},{24,20},{28,16},{1,13},{... | collective-permute-start | bytes 393224 | tf_op jit(solution)/shard_map/ppermute | solution.py:530
  88.0 8.7 %collective-permute-start.18 = (bf16[512,128]{1,0:T(8,128)(2,1)S(1)}, bf16[512,128]{1,0:T(8,128)(2,1)S(1)}, u32[]{:S(2)}, u32[]{:S(2)}) collective-permute-start(bf16[512,128]{1,0:T(8,128)(2,1)S(1)} %get-tuple-element.68), channel_id=1, source_target_pairs={{0,24},{4,28},{8,16},{12,20},{16,8},{20,12},{24,0},{28,4},{1,25},{... | collective-permute-start | bytes 393224 | tf_op jit(solution)/shard_map/ppermute | solution.py:530
  89.6 10.0 %collective-permute-start.19 = (bf16[512,128]{1,0:T(8,128)(2,1)S(1)}, bf16[512,128]{1,0:T(8,128)(2,1)S(1)}, u32[]{:S(2)}, u32[]{:S(2)}) collective-permute-start(bf16[512,128]{1,0:T(8,128)(2,1)S(1)} %get-tuple-element.69), channel_id=1, source_target_pairs={{0,28},{4,24},{8,20},{12,16},{16,12},{20,8},{24,4},{28,0},{1,29},{... | collective-permute-start | bytes 393224 | tf_op jit(solution)/shard_map/ppermute | solution.py:530
  104.6 1.3 copy-start.3
  105.9 5.6 %collective-permute-start.20 = (bf16[512,128]{1,0:T(8,128)(2,1)S(1)}, bf16[512,128]{1,0:T(8,128)(2,1)S(1)}, u32[]{:S(2)}, u32[]{:S(2)}) collective-permute-start(bf16[512,128]{1,0:T(8,128)(2,1)S(1)} %get-tuple-element.72), channel_id=1, source_target_pairs={{0,4},{4,0},{8,12},{12,8},{16,20},{20,16},{24,28},{28,24},{1,5},{5... | collective-permute-start | bytes 393224 | tf_op jit(solution)/shard_map/ppermute | solution.py:530
  108.0 5.1 %collective-permute-start.21 = (bf16[512,128]{1,0:T(8,128)(2,1)S(1)}, bf16[512,128]{1,0:T(8,128)(2,1)S(1)}, u32[]{:S(2)}, u32[]{:S(2)}) collective-permute-start(bf16[512,128]{1,0:T(8,128)(2,1)S(1)} %get-tuple-element.73), channel_id=1, source_target_pairs={{0,8},{4,12},{8,0},{12,4},{16,24},{20,28},{24,16},{28,20},{1,9},{5... | collective-permute-start | bytes 393224 | tf_op jit(solution)/shard_map/ppermute | solution.py:530
  108.0 8.7 %collective-permute-start.22 = (bf16[512,128]{1,0:T(8,128)(2,1)S(1)}, bf16[512,128]{1,0:T(8,128)(2,1)S(1)}, u32[]{:S(2)}, u32[]{:S(2)}) collective-permute-start(bf16[512,128]{1,0:T(8,128)(2,1)S(1)} %get-tuple-element.74), channel_id=1, source_target_pairs={{0,12},{4,8},{8,4},{12,0},{16,28},{20,24},{24,20},{28,16},{1,13},{... | collective-permute-start | bytes 393224 | tf_op jit(solution)/shard_map/ppermute | solution.py:530
  109.6 7.1 %collective-permute-start.23 = (bf16[512,128]{1,0:T(8,128)(2,1)S(1)}, bf16[512,128]{1,0:T(8,128)(2,1)S(1)}, u32[]{:S(2)}, u32[]{:S(2)}) collective-permute-start(bf16[512,128]{1,0:T(8,128)(2,1)S(1)} %get-tuple-element.75), channel_id=1, source_target_pairs={{0,16},{4,20},{8,24},{12,28},{16,0},{20,4},{24,8},{28,12},{1,17},{... | collective-permute-start | bytes 393224 | tf_op jit(solution)/shard_map/ppermute | solution.py:530
  109.6 13.6 %collective-permute-start.24 = (bf16[512,128]{1,0:T(8,128)(2,1)S(1)}, bf16[512,128]{1,0:T(8,128)(2,1)S(1)}, u32[]{:S(2)}, u32[]{:S(2)}) collective-permute-start(bf16[512,128]{1,0:T(8,128)(2,1)S(1)} %get-tuple-element.76), channel_id=1, source_target_pairs={{0,20},{4,16},{8,28},{12,24},{16,4},{20,0},{24,12},{28,8},{1,21},{... | collective-permute-start | bytes 393224 | tf_op jit(solution)/shard_map/ppermute | solution.py:530
  111.5 11.8 %collective-permute-start.25 = (bf16[512,128]{1,0:T(8,128)(2,1)S(1)}, bf16[512,128]{1,0:T(8,128)(2,1)S(1)}, u32[]{:S(2)}, u32[]{:S(2)}) collective-permute-start(bf16[512,128]{1,0:T(8,128)(2,1)S(1)} %get-tuple-element.77), channel_id=1, source_target_pairs={{0,24},{4,28},{8,16},{12,20},{16,8},{20,12},{24,0},{28,4},{1,25},{... | collective-permute-start | bytes 393224 | tf_op jit(solution)/shard_map/ppermute | solution.py:530
  113.1 10.2 %collective-permute-start.26 = (bf16[512,128]{1,0:T(8,128)(2,1)S(1)}, bf16[512,128]{1,0:T(8,128)(2,1)S(1)}, u32[]{:S(2)}, u32[]{:S(2)}) collective-permute-start(bf16[512,128]{1,0:T(8,128)(2,1)S(1)} %get-tuple-element.78), channel_id=1, source_target_pairs={{0,28},{4,24},{8,20},{12,16},{16,12},{20,8},{24,4},{28,0},{1,29},{... | collective-permute-start | bytes 393224 | tf_op jit(solution)/shard_map/ppermute | solution.py:530
  131.2 4.2 %collective-permute-start.27 = (bf16[512,128]{1,0:T(8,128)(2,1)S(1)}, bf16[512,128]{1,0:T(8,128)(2,1)S(1)}, u32[]{:S(2)}, u32[]{:S(2)}) collective-permute-start(bf16[512,128]{1,0:T(8,128)(2,1)S(1)} %get-tuple-element.80), channel_id=1, source_target_pairs={{0,4},{4,0},{8,12},{12,8},{16,20},{20,16},{24,28},{28,24},{1,5},{5... | collective-permute-start | bytes 393224 | tf_op jit(solution)/shard_map/ppermute | solution.py:530
  131.3 4.7 %collective-permute-start.28 = (bf16[512,128]{1,0:T(8,128)(2,1)S(1)}, bf16[512,128]{1,0:T(8,128)(2,1)S(1)}, u32[]{:S(2)}, u32[]{:S(2)}) collective-permute-start(bf16[512,128]{1,0:T(8,128)(2,1)S(1)} %get-tuple-element.81), channel_id=1, source_target_pairs={{0,16},{4,20},{8,24},{12,28},{16,0},{20,4},{24,8},{28,12},{1,17},{... | collective-permute-start | bytes 393224 | tf_op jit(solution)/shard_map/ppermute | solution.py:530
  131.7 7.3 %collective-permute-start.29 = (bf16[512,128]{1,0:T(8,128)(2,1)S(1)}, bf16[512,128]{1,0:T(8,128)(2,1)S(1)}, u32[]{:S(2)}, u32[]{:S(2)}) collective-permute-start(bf16[512,128]{1,0:T(8,128)(2,1)S(1)} %get-tuple-element.82), channel_id=1, source_target_pairs={{0,8},{4,12},{8,0},{12,4},{16,24},{20,28},{24,16},{28,20},{1,9},{5... | collective-permute-start | bytes 393224 | tf_op jit(solution)/shard_map/ppermute | solution.py:530
  131.7 7.8 %collective-permute-start.30 = (bf16[512,128]{1,0:T(8,128)(2,1)S(1)}, bf16[512,128]{1,0:T(8,128)(2,1)S(1)}, u32[]{:S(2)}, u32[]{:S(2)}) collective-permute-start(bf16[512,128]{1,0:T(8,128)(2,1)S(1)} %get-tuple-element.83), channel_id=1, source_target_pairs={{0,20},{4,16},{8,28},{12,24},{16,4},{20,0},{24,12},{28,8},{1,21},{... | collective-permute-start | bytes 393224 | tf_op jit(solution)/shard_map/ppermute | solution.py:530
  133.6 6.8 %collective-permute-start.31 = (bf16[512,128]{1,0:T(8,128)(2,1)S(1)}, bf16[512,128]{1,0:T(8,128)(2,1)S(1)}, u32[]{:S(2)}, u32[]{:S(2)}) collective-permute-start(bf16[512,128]{1,0:T(8,128)(2,1)S(1)} %get-tuple-element.84), channel_id=1, source_target_pairs={{0,12},{4,8},{8,4},{12,0},{16,28},{20,24},{24,20},{28,16},{1,13},{... | collective-permute-start | bytes 393224 | tf_op jit(solution)/shard_map/ppermute | solution.py:530
  135.4 10.0 %collective-permute-start.32 = (bf16[512,128]{1,0:T(8,128)(2,1)S(1)}, bf16[512,128]{1,0:T(8,128)(2,1)S(1)}, u32[]{:S(2)}, u32[]{:S(2)}) collective-permute-start(bf16[512,128]{1,0:T(8,128)(2,1)S(1)} %get-tuple-element.85), channel_id=1, source_target_pairs={{0,24},{4,28},{8,16},{12,20},{16,8},{20,12},{24,0},{28,4},{1,25},{... | collective-permute-start | bytes 393224 | tf_op jit(solution)/shard_map/ppermute | solution.py:530
  136.0 10.2 %collective-permute-start.33 = (bf16[512,128]{1,0:T(8,128)(2,1)S(1)}, bf16[512,128]{1,0:T(8,128)(2,1)S(1)}, u32[]{:S(2)}, u32[]{:S(2)}) collective-permute-start(bf16[512,128]{1,0:T(8,128)(2,1)S(1)} %get-tuple-element.86), channel_id=1, source_target_pairs={{0,28},{4,24},{8,20},{12,16},{16,12},{20,8},{24,4},{28,0},{1,29},{... | collective-permute-start | bytes 393224 | tf_op jit(solution)/shard_map/ppermute | solution.py:530
  140.4 1.6 %copy-start.4 = (f32[4096,128]{1,0:T(8,128)S(1)}, f32[4096,128]{1,0:T(8,128)}, u32[]{:S(2)}) copy-start(f32[4096,128]{1,0:T(8,128)} %copy-done.3) | copy-start | bytes 6291460

commit v7 on v6

--- a/solution.py
+++ b/solution.py
@@ -22,7 +22,9 @@
 LATE_PICK_VMEM = 18 * MIB
 LATE_VMEM = 12 * MIB
 BASIS_CALLS = 4
-UNROLL = 16
+UNROLL = 32
+SUB = 8
+HBM_SPARE = 32
 COST_US = 10 ** 9
 
 COS_POLY = (1.0, -19.73920440673828, 64.9391098022461, -85.4500503540039, 60.16689682006836,
@@ -107,7 +109,7 @@
     )(wide, period, 1.0 / period, *after)
 
 
-def fit_kernel(tm_count, src_ref, dst_ref, *refs):
+def fit_kernel(order, src_ref, dst_ref, *refs):
     refs = list(refs)
 
     def take(count):
@@ -115,7 +117,8 @@
         del refs[:count]
         return taken
 
-    arrived = take(tm_count)
+    tm_count = len(order)
+    arrived = dict(zip(order, take(tm_count)))
     parts = take(BASIS_CALLS)
     (norm_ref,) = take(1)
     outs = take(tm_count)
@@ -196,6 +199,7 @@
 
 def fit_plans(tables, arrived, parts, norms):
     tm_count = len(arrived)
+    order = [0] + ask_order(tm_count)
     each, obs, twice = parts[0].shape
     sched_dev = each * len(parts)
     capacity, width = arrived[0].shape
@@ -208,7 +212,7 @@
         pltpu.VMEM((obs + STEP, width), jnp.float32),
     ]
     *models, score = pl.pallas_call(
-        functools.partial(fit_kernel, tm_count),
+        functools.partial(fit_kernel, order),
         in_specs=[SMEM, SMEM] + [VMEM] * tm_count + [ANY] * len(parts) + [VMEM],
         out_specs=[VMEM] * (tm_count + 1),
         out_shape=[jax.ShapeDtypeStruct((capacity, width), jnp.bfloat16)] * tm_count
@@ -221,7 +225,7 @@
         ] + slot + slot,
         compiler_params=pltpu.CompilerParams(vmem_limit_bytes=FIT_VMEM),
         cost_estimate=pl.CostEstimate(flops=20 * work, bytes_accessed=sched_dev * obs * twice * 2, transcendentals=0),
-    )(*tables, *arrived, *parts, norms)
+    )(*tables, *[arrived[owner] for owner in order], *parts, norms)
     return models, score
 
 
@@ -233,27 +237,29 @@
         copies.append((sky >= hop, sky - hop, passed[2 * hop - 2]))
         copies.append((sky + hop < count, sky + hop, passed[2 * hop - 1]))
 
-    def each(act):
+    def each(act, segs):
         for index, (valid, quarter, ref) in enumerate(copies):
             def run(index=index, quarter=quarter, ref=ref):
                 at = pl.ds(pl.multiple_of(quarter * rows, rows), rows)
-                act(pltpu.make_async_copy(ref, whole_ref.at[:, at, :], sems.at[index]))
+                for seg in segs:
+                    act(pltpu.make_async_copy(ref.at[seg], whole_ref.at[seg, at, :], sems.at[index, seg]))
 
             if valid is None:
                 run()
             else:
                 pl.when(valid)(run)
 
-    each(lambda copy: copy.start())
-    return lambda: each(lambda copy: copy.wait())
-
-
-def whiten_and_pick(me, asked_ref, cnt_ref, count_ref, whole_ref, load, picked, white_ref, gather_ref):
+    each(lambda copy: copy.start(), range(own_ref.shape[0]))
+    return lambda seg: each(lambda copy: copy.wait(), [seg])
+
+
+def whiten_and_pick(me, asked_ref, cnt_ref, count_ref, whole_ref, wait, load, picked, white_ref, gather_ref):
     segs, slots, _ = whole_ref.shape
     capacity, width = picked[0].shape
     blocks = white_ref.shape[0] // (segs * slots)
     row = lax.broadcasted_iota(jnp.int32, (slots, width * blocks), 0)
     for seg in range(segs):
+        wait(seg)
         masked = jnp.where(row < count_ref[seg], load(seg).astype(jnp.float32), 0.0).astype(jnp.bfloat16)
         white = jnp.dot(whole_ref[seg], masked, preferred_element_type=jnp.float32)
         for block in range(blocks):
@@ -262,15 +268,17 @@
         asker = owner ^ me
 
         def step(index, carry):
-            first = index * UNROLL
+            first = asker * capacity + index * UNROLL
+            tile = (owner * capacity) // SUB + index * (UNROLL // SUB)
             for lane in range(UNROLL):
-                gather_ref[pl.ds(owner * capacity + first + lane, 1), :] = white_ref[
-                    pl.ds(asked_ref[asker * capacity + first + lane], 1), :
+                gather_ref[tile + lane // SUB, pl.ds(lane % SUB, 1), :] = white_ref[
+                    pl.ds(asked_ref[first + lane], 1), :
                 ]
             return carry
 
         lax.fori_loop(0, (cnt_ref[asker] + UNROLL - 1) // UNROLL, step, 0)
-        out_ref[...] = gather_ref[pl.ds(owner * capacity, capacity), :].astype(jnp.bfloat16)
+        block = gather_ref[pl.ds(owner * capacity // SUB, capacity // SUB)]
+        out_ref[...] = block.reshape(capacity, width).astype(jnp.bfloat16)
 
 
 def add_rows(me, asked_ref, cnt_ref, owners, returned, rows_ref, sums):
@@ -279,16 +287,18 @@
     for total in sums:
         total[...] = jnp.zeros_like(total)
     for number, (owner, ref) in enumerate(zip(owners, returned)):
-        rows_ref[pl.ds(number * capacity, capacity), :] = ref[...].astype(jnp.float32)
+        tiles = capacity // SUB
+        rows_ref[pl.ds(number * tiles, tiles)] = ref[...].astype(jnp.float32).reshape(tiles, SUB, -1)
         asker = owner ^ me
 
         def step(index, carry):
-            first = index * UNROLL
+            first = asker * capacity + index * UNROLL
+            tile = number * tiles + index * (UNROLL // SUB)
             for start in range(0, UNROLL, streams):
-                lanes = [first + start + lane for lane in range(streams)]
-                places = [asked_ref[asker * capacity + lane] for lane in lanes]
+                lanes = [start + lane for lane in range(streams)]
+                places = [asked_ref[first + lane] for lane in lanes]
                 values = [
-                    total[pl.ds(place, 1), :] + rows_ref[pl.ds(number * capacity + lane, 1), :]
+                    total[pl.ds(place, 1), :] + rows_ref[tile + lane // SUB, pl.ds(lane % SUB, 1), :]
                     for total, place, lane in zip(sums, places, lanes)
                 ]
                 for total, place, value in zip(sums, places, values):
@@ -308,7 +318,7 @@
     out_ref, rows_ref = refs.pop(0), refs.pop(0)
     if table_base:
         held_ref, sem = refs.pop(0), refs.pop(0)
-        copy = pltpu.make_async_copy(base_ref, held_ref, sem)
+        copy = pltpu.make_async_copy(base_ref.at[pl.ds(0, held_ref.shape[0]), :], held_ref, sem)
         copy.start()
     add_rows(where_ref[0], asked_ref, cnt_ref, owners, returned, rows_ref, refs)
     if table_base:
@@ -335,7 +345,7 @@
         in_specs=[SMEM] * 3 + [HBM if table_base else VMEM] + [VMEM] * len(owners),
         out_specs=VMEM,
         out_shape=jax.ShapeDtypeStruct((rows, SRC_GROUP), jnp.float32),
-        scratch_shapes=[pltpu.VMEM((len(owners) * capacity, SRC_GROUP), jnp.float32)] + held + sums,
+        scratch_shapes=[pltpu.VMEM((len(owners) * capacity // SUB, SUB, SRC_GROUP), jnp.float32)] + held + sums,
         compiler_params=pltpu.CompilerParams(vmem_limit_bytes=EARLY_VMEM),
         cost_estimate=pl.CostEstimate(flops=6 * COST_US, bytes_accessed=1 << 20, transcendentals=0),
     )(asked, cnt, where, base, *[returned[owner] for owner in owners])
@@ -346,9 +356,9 @@
     passed = [refs.pop(0) for _ in range(passed_count)]
     picked = [refs.pop(0) for _ in range(tm_count)]
     whole_ref, sems, white_ref, gather_ref = refs
-    load_attitude(where_ref[1], own_ref, passed, whole_ref, sems)()
+    wait = load_attitude(where_ref[1], own_ref, passed, whole_ref, sems)
     whiten_and_pick(
-        where_ref[0], asked_ref, cnt_ref, count_ref, whole_ref, lambda seg: base_ref[seg], picked, white_ref,
+        where_ref[0], asked_ref, cnt_ref, count_ref, whole_ref, wait, lambda seg: base_ref[seg], picked, white_ref,
         gather_ref,
     )
 
@@ -365,9 +375,9 @@
         out_shape=[jax.ShapeDtypeStruct((capacity, SRC_GROUP), jnp.bfloat16)] * tm_count,
         scratch_shapes=[
             pltpu.VMEM((seg_dev, slots, slots), jnp.bfloat16),
-            pltpu.SemaphoreType.DMA((len(attitude),)),
+            pltpu.SemaphoreType.DMA((len(attitude), seg_dev)),
             pltpu.VMEM((rows + 8, SRC_GROUP), jnp.float32),
-            pltpu.VMEM((tm_count * capacity, SRC_GROUP), jnp.float32),
+            pltpu.VMEM((tm_count * capacity // SUB, SUB, SRC_GROUP), jnp.float32),
         ],
         compiler_params=pltpu.CompilerParams(vmem_limit_bytes=PICK_VMEM),
         cost_estimate=pl.CostEstimate(flops=5 * COST_US, bytes_accessed=1 << 20, transcendentals=0),
@@ -393,9 +403,8 @@
     wait = load_attitude(where_ref[1], own_ref, passed, whole_ref, sems)
     add_rows(where_ref[0], asked_ref, cnt_ref, owners, returned, gather_ref, refs)
     table_ref[...] = part_ref[...] - placed_at(refs, pl.ds(0, table_ref.shape[0]))
-    copy = pltpu.make_async_copy(table_ref, out_ref, sem)
+    copy = pltpu.make_async_copy(table_ref, out_ref.at[pl.ds(0, table_ref.shape[0]), :], sem)
     copy.start()
-    wait()
 
     def load(seg):
         return jnp.concatenate(
@@ -403,7 +412,7 @@
         )
 
     whiten_and_pick(
-        where_ref[0], asked_ref, cnt_ref, count_ref, whole_ref, load, picked, white_ref, gather_ref
+        where_ref[0], asked_ref, cnt_ref, count_ref, whole_ref, wait, load, picked, white_ref, gather_ref
     )
     copy.wait()
 
@@ -420,13 +429,13 @@
         functools.partial(late_pick_kernel, tm_count, len(attitude) - 1, owners),
         in_specs=[SMEM] * 4 + [VMEM] + [ANY] * len(attitude) + [VMEM] * len(owners),
         out_specs=[HBM] + [VMEM] * tm_count,
-        out_shape=[jax.ShapeDtypeStruct(part.shape, jnp.float32)]
+        out_shape=[jax.ShapeDtypeStruct((HBM_SPARE * rows, SRC_GROUP), jnp.float32)]
         + [jax.ShapeDtypeStruct((capacity, SRC_GROUP), jnp.bfloat16)] * tm_count,
         scratch_shapes=[
             pltpu.VMEM((seg_dev, slots, slots), jnp.bfloat16),
-            pltpu.SemaphoreType.DMA((len(attitude),)),
+            pltpu.SemaphoreType.DMA((len(attitude), seg_dev)),
             table,
-            pltpu.VMEM((tm_count * capacity, SRC_GROUP), jnp.float32),
+            pltpu.VMEM((tm_count * capacity // SUB, SUB, SRC_GROUP), jnp.float32),
             pltpu.VMEM((rows, SRC_GROUP), jnp.float32),
             pltpu.SemaphoreType.DMA(()),
         ] + [table] * LATE_STREAMS,
@@ -464,7 +473,7 @@
         out_specs=HBM,
         out_shape=jax.ShapeDtypeStruct(shape, jnp.float32),
         scratch_shapes=[
-            pltpu.VMEM((len(owners) * capacity, SRC_GROUP), jnp.float32),
+            pltpu.VMEM((len(owners) * capacity // SUB, SUB, SRC_GROUP), jnp.float32),
             pltpu.VMEM(shape, jnp.float32),
             pltpu.SemaphoreType.DMA((shape[0],)),
         ] + [pltpu.VMEM((part.shape[0] + 8, SRC_GROUP), jnp.float32)] * LATE_STREAMS,
@@ -523,10 +532,17 @@
     return sorted(range(1, count), key=lambda step: (bin(step // 2).count("1"), step % 2, -step))
 
 
+def ask_order(count):
+    first = [1, count // 2]
+    return first + sorted(
+        (step for step in range(2, count) if step not in first), key=lambda step: -bin(step // 2).count("1")
+    )
+
+
 def exchange(blocks):
     count = len(blocks)
     out = list(blocks)
-    for step in send_order(count):
+    for step in range(1, count):
         out[step] = lax.ppermute(blocks[step], "tm", [(i, i ^ step) for i in range(count)])
     return out
 
@@ -563,15 +579,15 @@
         made.append(make_basis(times[first:first + part], periods, after))
 
     def first_hop(right, left):
+        basis_part([right, left])
+        basis_part([right, left])
+        return right, left
+
+    def second_hop(right, left):
         nonlocal asked
         basis_part([right, left])
-        held, _ = lax.optimization_barrier((wanted, made[0][1]))
+        held, _ = lax.optimization_barrier((wanted, made[-1][1]))
         asked = lax.all_to_all(held, "tm", split_axis=0, concat_axis=0, tiled=True)
-        return right, left
-
-    def second_hop(right, left):
-        basis_part([right, left])
-        basis_part([right, left])
         return right, left
 
     pieces = pass_along(attitude, {1: first_hop, 2: second_hop})

time: 151 us -> 159 us (1.053)
  the two profiles are of different devices: /device:TPU:1 before, /device:TPU:9 now
where the time goes in v7:
time: 159 us; the launch traced here: 158 us
  Pallas kernels  60.5 us (38%)
  starting transfers between devices  45.5 us (29%)
  waiting for transfers between devices  36.3 us (23%)
  other arithmetic  9.48 us (6%)
  local copies, waits for them, and re-layouts  5.12 us (3%)
    ppermute x28, waiting for transfers between devices, exchange(): lax.ppermute(blocks[step], 'tm', [(i, i ^ step) for i in range(count)])  31.3 us
    ppermute x28, starting transfers between devices, exchange(): lax.ppermute(blocks[step], 'tm', [(i, i ^ step) for i in range(count)])  23.9 us
    pallas_call x4, Pallas kernels, make_basis(): pl.pallas_call(functools.partial(basis_kernel, len(after)), grid=(sched_d...  16.8 us
    pallas_call x2, Pallas kernels, fit_plans(): pl.pallas_call(functools.partial(fit_kernel, order), in_specs=[SMEM, SMEM...  16.6 us
    ppermute x3, starting transfers between devices, pass_along(): lax.ppermute(right, 'sky', [(i, i + 1) for i in range(hop - 1, count - 1)])  9.46 us
    pallas_call x1, Pallas kernels, place_late_and_pick(): pl.pallas_call(functools.partial(late_pick_kernel, tm_count, len(attitude...  8.67 us
    pallas_call x1, Pallas kernels, pick_rows(): pl.pallas_call(functools.partial(pick_kernel, tm_count, len(attitude) - 1...  7.61 us
    pallas_call x2, Pallas kernels, place_early(): pl.pallas_call(functools.partial(early_kernel, owners, table_base), in_sp...  6.95 us
  transfers between devices with their start and end apart: 35, of which 18 were waited for; matrix products, arithmetic and copies ran while one was open for 6% of the time, Pallas kernels for 15%

profile of v7, /device:TPU:9, one launch (start us, length us, event | category | flops | bytes accessed | tf_op | source)
XLA Modules:
  0.0 158.1 jit_solution(3565386246416366652)
XLA Ops:
  0.6 1.9 %collective-permute-start.2 = (bf16[4,128,512]{2,1,0:T(8,128)(2,1)}, bf16[4,128,512]{2,1,0:T(8,128)(2,1)S(1)}, u32[]{:S(2)}, u32[]{:S(2)}) collective-permute-start(bf16[4,128,512]{2,1,0:T(8,128)(2,1)} %own_ref.3), channel_id=1, source_target_pairs={{1,0},{2,1},{3,2},{5,4},{6,5},{7,6},{9,8},{10,9},{11,10},{13,12},{... | collective-permute-start | bytes 1572872 | tf_op jit(solution)/shard_map/ppermute | solution.py:556
  2.6 3.4 %collective-permute-start = (bf16[4,128,512]{2,1,0:T(8,128)(2,1)}, bf16[4,128,512]{2,1,0:T(8,128)(2,1)S(1)}, u32[]{:S(2)}, u32[]{:S(2)}) collective-permute-start(bf16[4,128,512]{2,1,0:T(8,128)(2,1)} %own_ref.3), channel_id=1, source_target_pairs={{0,1},{1,2},{2,3},{4,5},{5,6},{6,7},{8,9},{9,10},{10,11},{12,13},{... | collective-permute-start | bytes 1572872 | tf_op jit(solution)/shard_map/ppermute | solution.py:555
  10.2 3.4 %select_reduce_fusion = s32[4096]{0:T(1024)S(1)} fusion(s32[2048]{0:T(1024)S(1)} %bitcast.41, s32[2048]{0:T(1024)S(1)} %bitcast.40), kind=kLoop, calls=%fused_computation | loop fusion | flops 25161728 | bytes 32768 | tf_op jit(solution)/shard_map/reduce_sum | solution.py:510
  14.5 1.0 collective-permute-done.2.refs_1_
  15.5 2.2 %collective-permute-start.3 = (bf16[4,128,512]{2,1,0:T(8,128)(2,1)S(1)}, bf16[4,128,512]{2,1,0:T(8,128)(2,1)}, u32[]{:S(2)}, u32[]{:S(2)}) collective-permute-start(bf16[4,128,512]{2,1,0:T(8,128)(2,1)S(1)} %collective-permute-done.2.refs_1_), channel_id=1, source_target_pairs={{1,0},{2,1},{5,4},{6,5},{9,8},{10,9},{13,12},{14,13},{17,16},{18,1... | collective-permute-start | bytes 1572872 | tf_op jit(solution)/shard_map/ppermute | solution.py:556
  17.8 4.6 %collective-permute-start.1 = (bf16[4,128,512]{2,1,0:T(8,128)(2,1)S(1)}, bf16[4,128,512]{2,1,0:T(8,128)(2,1)}, u32[]{:S(2)}, u32[]{:S(2)}) collective-permute-start(bf16[4,128,512]{2,1,0:T(8,128)(2,1)S(1)} %collective-permute-done.refs_0_), channel_id=1, source_target_pairs={{1,2},{2,3},{5,6},{6,7},{9,10},{10,11},{13,14},{14,15},{17,18},{18... | collective-permute-start | bytes 1572872 | tf_op jit(solution)/shard_map/ppermute | solution.py:555
  22.5 4.2 %shard_map.80 = (bf16[2,256,2048]{2,1,0:T(8,128)(2,1)S(1)}, f32[2,1,2048]{2,1,0:T(1,128)S(1)}) custom-call(f32[512,128]{1,0:T(8,128)S(1)} %broadcast_in_dim.55.time_ref, f32[1,1024]{1,0:T(1,128)S(1)} %bitcast.28, f32[1,1024]{1,0:T(1,128)S(1)} %bitcast.32, bf16[4,128,512]{2,1,0:T(8,128)(2,1)S(1)} %collective-permute-done.refs_0_, ...), custom_call_target="tpu_custom_call" | custom-call | flops 5242880000 | bytes 2097152 | tf_op jit(solution)/shard_map/pallas_call | solution.py:89
  26.8 1.3 copy-done.3
  28.2 4.2 %shard_map.79 = (bf16[2,256,2048]{2,1,0:T(8,128)(2,1)S(1)}, f32[2,1,2048]{2,1,0:T(1,128)S(1)}) custom-call(f32[512,128]{1,0:T(8,128)S(1)} %broadcast_in_dim.53.time_ref, f32[1,1024]{1,0:T(1,128)S(1)} %bitcast.29, f32[1,1024]{1,0:T(1,128)S(1)} %bitcast.33, bf16[4,128,512]{2,1,0:T(8,128)(2,1)S(1)} %collective-permute-done.refs_0_, ...), custom_call_target="tpu_custom_call" | custom-call | flops 5242880000 | bytes 2097152 | tf_op jit(solution)/shard_map/pallas_call | solution.py:89
  32.5 1.3 copy-done.5
  33.8 2.1 %collective-permute-start.5 = (bf16[4,128,512]{2,1,0:T(8,128)(2,1)}, bf16[4,128,512]{2,1,0:T(8,128)(2,1)}, u32[]{:S(2)}, u32[]{:S(2)}) collective-permute-start(bf16[4,128,512]{2,1,0:T(8,128)(2,1)} %collective-permute-done.3.refs_1_.refs_3_), channel_id=1, source_target_pairs={{1,0},{5,4},{9,8},{13,12},{17,16},{21,20},{25,24},{29,28}} | collective-permute-start | bytes 1572872 | tf_op jit(solution)/shard_map/ppermute | solution.py:556
  35.9 1.5 collective-permute-start.4
  37.5 4.2 %shard_map.77 = (bf16[2,256,2048]{2,1,0:T(8,128)(2,1)S(1)}, f32[2,1,2048]{2,1,0:T(1,128)S(1)}) custom-call(f32[512,128]{1,0:T(8,128)S(1)} %broadcast_in_dim.50.time_ref, f32[1,1024]{1,0:T(1,128)S(1)} %bitcast.30, f32[1,1024]{1,0:T(1,128)S(1)} %bitcast.34, bf16[4,128,512]{2,1,0:T(8,128)(2,1)} %collective-permute-done.1.refs_0_.refs_2_, ...), custom_call_target="tpu_custom_call" | custom-call | flops 5242880000 | bytes 2097152 | tf_op jit(solution)/shard_map/pallas_call | solution.py:89
  41.7 1.3 copy-done.7
  43.7 5.8 %all-to-all-start = ((s32[8,1,512]{2,1,0:T(1,128)}), s32[8,1,512]{2,1,0:T(1,128)S(1)}, u32[]{:S(2)}, u32[]{:S(2)}) async-start(s32[8,1,512]{2,1,0:T(1,128)} %all_to_all.6), calls=%async_computation | async-start | bytes 32768 | tf_op jit(solution)/shard_map/all_to_all | solution.py:590
  49.5 4.0 %all-to-all-done = s32[8,1,512]{2,1,0:T(1,128)S(1)} async-done(((s32[8,1,512]{2,1,0:T(1,128)}), s32[8,1,512]{2,1,0:T(1,128)S(1)}, u32[]{:S(2)}, u32[]{:S(2)}) %all-to-all-start) | async-done | bytes 16416 | tf_op jit(solution)/shard_map/all_to_all | solution.py:590
  53.8 7.6 %shard_map.78 = (bf16[512,128]{1,0:T(8,128)(2,1)S(1)}, bf16[512,128]{1,0:T(8,128)(2,1)S(1)}, bf16[512,128]{1,0:T(8,128)(2,1)S(1)}, bf16[512,128]{1,0:T(8,128)(2,...) custom-call(s32[4096]{0:T(1024)S(1)} %bitcast.23, ...), custom_call_target="tpu_custom_call" | custom-call | flops 5000000000 | bytes 1048576 | tf_op jit(solution)/shard_map/pallas_call | solution.py:371
  61.4 1.4 collective-permute-start.6
  62.8 1.3 collective-permute-start.8
  64.2 1.9 %collective-permute-start.9 = (bf16[512,128]{1,0:T(8,128)(2,1)S(1)}, bf16[512,128]{1,0:T(8,128)(2,1)S(1)}, u32[]{:S(2)}, u32[]{:S(2)}) collective-permute-start(bf16[512,128]{1,0:T(8,128)(2,1)S(1)} %get-tuple-element.51), channel_id=1, source_target_pairs={{0,28},{4,24},{8,20},{12,16},{16,12},{20,8},{24,4},{28,0},{1,29},{... | collective-permute-start | bytes 393224 | tf_op jit(solution)/shard_map/ppermute | solution.py:546
  66.5 4.2 %shard_map.81 = (bf16[2,256,2048]{2,1,0:T(8,128)(2,1)S(1)}, f32[2,1,2048]{2,1,0:T(1,128)S(1)}) custom-call(f32[512,128]{1,0:T(8,128)S(1)} %broadcast_in_dim.57.time_ref, f32[1,1024]{1,0:T(1,128)S(1)} %bitcast.31, f32[1,1024]{1,0:T(1,128)S(1)} %bitcast.35, bf16[512,128]{1,0:T(8,128)(2,1)S(1)} %get-tuple-element.47.refs_0_), custom_call_target="tpu_custom_call" | custom-call | flops 5242880000 | bytes 2097152 | tf_op jit(solution)/shard_map/pallas_call | solution.py:89
  70.8 0.9 collective-permute-start.11
  71.7 1.8 %collective-permute-done.7.refs_2_ = bf16[512,128]{1,0:T(8,128)(2,1)S(1)} collective-permute-done((bf16[512,128]{1,0:T(8,128)(2,1)S(1)}, bf16[512,128]{1,0:T(8,128)(2,1)S(1)}, u32[]{:S(2)}, u32[]{:S(2)}) %collective-permute-start.7) | collective-permute-done | bytes 131104 | tf_op jit(solution)/shard_map/ppermute | solution.py:546
  74.4 3.6 %collective-permute-done.11.refs_6_ = bf16[512,128]{1,0:T(8,128)(2,1)S(1)} collective-permute-done((bf16[512,128]{1,0:T(8,128)(2,1)S(1)}, bf16[512,128]{1,0:T(8,128)(2,1)S(1)}, u32[]{:S(2)}, u32[]{:S(2)}) %collective-permute-start.11) | collective-permute-done | bytes 131104 | tf_op jit(solution)/shard_map/ppermute | solution.py:546
  78.0 1.4 collective-permute-done.12.refs_7_
  79.4 8.7 %shard_map.82 = (bf16[512,128]{1,0:T(8,128)(2,1)S(1)}, bf16[512,128]{1,0:T(8,128)(2,1)S(1)}, bf16[512,128]{1,0:T(8,128)(2,1)S(1)}, bf16[512,128]{1,0:T(8,128)(2,...) custom-call(s32[8,24]{1,0:T(8,128)S(1)} %get-tuple-element.106.src_r, ...), custom_call_target="tpu_custom_call" | custom-call | flops 10737418240 | bytes 8388608 | tf_op jit(solution)/shard_map/pallas_call | solution.py:214
  88.7 1.7 %collective-permute-start.16 = (bf16[512,128]{1,0:T(8,128)(2,1)S(1)}, bf16[512,128]{1,0:T(8,128)(2,1)S(1)}, u32[]{:S(2)}, u32[]{:S(2)}) collective-permute-start(bf16[512,128]{1,0:T(8,128)(2,1)S(1)} %get-tuple-element.66), channel_id=1, source_target_pairs={{0,20},{4,16},{8,28},{12,24},{16,4},{20,0},{24,12},{28,8},{1,21},{... | collective-permute-start | bytes 393224 | tf_op jit(solution)/shard_map/ppermute | solution.py:546
  90.5 1.5 collective-permute-start.17
  92.0 1.8 %collective-permute-done.14.refs_2_ = bf16[512,128]{1,0:T(8,128)(2,1)S(1)} collective-permute-done((bf16[512,128]{1,0:T(8,128)(2,1)S(1)}, bf16[512,128]{1,0:T(8,128)(2,1)S(1)}, u32[]{:S(2)}, u32[]{:S(2)}) %collective-permute-start.14) | collective-permute-done | bytes 131104 | tf_op jit(solution)/shard_map/ppermute | solution.py:546
  93.8 1.3 collective-permute-start.19
  95.1 1.7 %collective-permute-done.16.refs_4_ = bf16[512,128]{1,0:T(8,128)(2,1)S(1)} collective-permute-done((bf16[512,128]{1,0:T(8,128)(2,1)S(1)}, bf16[512,128]{1,0:T(8,128)(2,1)S(1)}, u32[]{:S(2)}, u32[]{:S(2)}) %collective-permute-start.16) | collective-permute-done | bytes 131104 | tf_op jit(solution)/shard_map/ppermute | solution.py:546
  97.3 3.5 %shard_map.83.part_ref = f32[4096,128]{1,0:T(8,128)S(1)} custom-call(s32[4096]{0:T(1024)S(1)} %bitcast.24, s32[8]{0:T(128)S(1)} %fusion.4.cnt_ref, s32[2]{0:T(128)S(1)} %pad_add_fusion.where_ref, bf16[4,512,256]{2,1,0:T(8,128)(2,1)S(1)} %copy-done, bf16[512,128]{1,0:T(8,128)(2,1)S(1)} %get-tuple-element.62.refs_0_, ...), custom_call_target="tpu_custom_call" | custom-call | flops 6000000000 | bytes 1048576 | tf_op jit(solution)/shard_map/pallas_call | solution.py:343
  100.9 2.7 %collective-permute-done.19.refs_7_ = bf16[512,128]{1,0:T(8,128)(2,1)S(1)} collective-permute-done((bf16[512,128]{1,0:T(8,128)(2,1)S(1)}, bf16[512,128]{1,0:T(8,128)(2,1)S(1)}, u32[]{:S(2)}, u32[]{:S(2)}) %collective-permute-start.19) | collective-permute-done | bytes 131104 | tf_op jit(solution)/shard_map/ppermute | solution.py:546
  103.6 8.7 %shard_map.84 = (f32[131072,128]{1,0:T(8,128)}, bf16[512,128]{1,0:T(8,128)(2,1)S(1)}, bf16[512,128]{1,0:T(8,128)(2,1)S(1)}, bf16[512,128]{1,0:T(8,128)(2,1)S(1)}...) custom-call(s32[4096]{0:T(1024)S(1)} %bitcast.25, ...), custom_call_target="tpu_custom_call" | custom-call | flops 7000000000 | bytes 1048576 | tf_op jit(solution)/shard_map/pallas_call | solution.py:428
  112.3 1.8 %collective-permute-start.20 = (bf16[512,128]{1,0:T(8,128)(2,1)S(1)}, bf16[512,128]{1,0:T(8,128)(2,1)S(1)}, u32[]{:S(2)}, u32[]{:S(2)}) collective-permute-start(bf16[512,128]{1,0:T(8,128)(2,1)S(1)} %get-tuple-element.72), channel_id=1, source_target_pairs={{0,4},{4,0},{8,12},{12,8},{16,20},{20,16},{24,28},{28,24},{1,5},{5... | collective-permute-start | bytes 393224 | tf_op jit(solution)/shard_map/ppermute | solution.py:546
  114.8 2.2 %collective-permute-start.23 = (bf16[512,128]{1,0:T(8,128)(2,1)S(1)}, bf16[512,128]{1,0:T(8,128)(2,1)S(1)}, u32[]{:S(2)}, u32[]{:S(2)}) collective-permute-start(bf16[512,128]{1,0:T(8,128)(2,1)S(1)} %get-tuple-element.75), channel_id=1, source_target_pairs={{0,28},{4,24},{8,20},{12,16},{16,12},{20,8},{24,4},{28,0},{1,29},{... | collective-permute-start | bytes 393224 | tf_op jit(solution)/shard_map/ppermute | solution.py:546
  117.1 1.4 collective-permute-start.25
  118.5 6.3 %collective-permute-done.21.refs_2_ = bf16[512,128]{1,0:T(8,128)(2,1)S(1)} collective-permute-done((bf16[512,128]{1,0:T(8,128)(2,1)S(1)}, bf16[512,128]{1,0:T(8,128)(2,1)S(1)}, u32[]{:S(2)}, u32[]{:S(2)}) %collective-permute-start.21) | collective-permute-done | bytes 131104 | tf_op jit(solution)/shard_map/ppermute | solution.py:546
  125.7 3.6 %collective-permute-done.25.refs_6_ = bf16[512,128]{1,0:T(8,128)(2,1)S(1)} collective-permute-done((bf16[512,128]{1,0:T(8,128)(2,1)S(1)}, bf16[512,128]{1,0:T(8,128)(2,1)S(1)}, u32[]{:S(2)}, u32[]{:S(2)}) %collective-permute-start.25) | collective-permute-done | bytes 131104 | tf_op jit(solution)/shard_map/ppermute | solution.py:546
  129.3 1.4 collective-permute-done.26.refs_7_
  130.7 7.9 %shard_map.85 = (bf16[512,128]{1,0:T(8,128)(2,1)S(1)}, bf16[512,128]{1,0:T(8,128)(2,1)S(1)}, bf16[512,128]{1,0:T(8,128)(2,1)S(1)}, bf16[512,128]{1,0:T(8,128)(2,...) custom-call(s32[8,24]{1,0:T(8,128)S(1)} %get-tuple-element.106.src_r, ...), custom_call_target="tpu_custom_call" | custom-call | flops 10737418240 | bytes 8388608 | tf_op jit(solution)/shard_map/pallas_call | solution.py:214
  139.3 1.7 %collective-permute-start.30 = (bf16[512,128]{1,0:T(8,128)(2,1)S(1)}, bf16[512,128]{1,0:T(8,128)(2,1)S(1)}, u32[]{:S(2)}, u32[]{:S(2)}) collective-permute-start(bf16[512,128]{1,0:T(8,128)(2,1)S(1)} %get-tuple-element.83), channel_id=1, source_target_pairs={{0,20},{4,16},{8,28},{12,24},{16,4},{20,0},{24,12},{28,8},{1,21},{... | collective-permute-start | bytes 393224 | tf_op jit(solution)/shard_map/ppermute | solution.py:546
  141.0 1.5 collective-permute-start.31
  143.3 1.0 collective-permute-done.28.refs_2_
  144.4 2.1 %collective-permute-start.33 = (bf16[512,128]{1,0:T(8,128)(2,1)S(1)}, bf16[512,128]{1,0:T(8,128)(2,1)S(1)}, u32[]{:S(2)}, u32[]{:S(2)}) collective-permute-start(bf16[512,128]{1,0:T(8,128)(2,1)S(1)} %get-tuple-element.86), channel_id=1, source_target_pairs={{0,28},{4,24},{8,20},{12,16},{16,12},{20,8},{24,4},{28,0},{1,29},{... | collective-permute-start | bytes 393224 | tf_op jit(solution)/shard_map/ppermute | solution.py:546
  147.9 3.4 %shard_map.86.part_ref = f32[4096,128]{1,0:T(8,128)S(1)} custom-call(s32[4096]{0:T(1024)S(1)} %bitcast.26, s32[8]{0:T(128)S(1)} %fusion.4.cnt_ref, s32[2]{0:T(128)S(1)} %pad_add_fusion.where_ref, f32[131072,128]{1,0:T(8,128)} %get-tuple-element.70.base_ref, bf16[512,128]{1,0:T(8,128)(2,1)S(1)} %get-tuple-element.79.refs_0_, ...), custom_call_target="tpu_custom_call" | custom-call | flops 6000000000 | bytes 1048576 | tf_op jit(solution)/shard_map/pallas_call | solution.py:343
  151.3 2.8 %collective-permute-done.33.refs_1_ = bf16[512,128]{1,0:T(8,128)(2,1)S(1)} collective-permute-done((bf16[512,128]{1,0:T(8,128)(2,1)S(1)}, bf16[512,128]{1,0:T(8,128)(2,1)S(1)}, u32[]{:S(2)}, u32[]{:S(2)}) %collective-permute-start.33) | collective-permute-done | bytes 131104 | tf_op jit(solution)/shard_map/ppermute | solution.py:546
  154.1 3.8 %shard_map.87 = f32[4,512,256]{2,1,0:T(8,128)} custom-call(s32[4096]{0:T(1024)S(1)} %bitcast.27, s32[8]{0:T(128)S(1)} %fusion.4.cnt_ref, s32[2]{0:T(128)S(1)} %pad_add_fusion.where_ref, f32[4096,128]{1,0:T(8,128)S(1)} %shard_map.86.part_ref, bf16[512,128]{1,0:T(8,128)(2,1)S(1)} %collective-permute-done.32.refs_0_, ...), custom_call_target="tpu_custom_call" | custom-call | flops 4000000000 | bytes 1048576 | tf_op jit(solution)/shard_map/pallas_call | solution.py:470
  (90 shorter events, 13.4 us)
Async XLA Ops:
  0.6 14.9 %collective-permute-start.2 = (bf16[4,128,512]{2,1,0:T(8,128)(2,1)}, bf16[4,128,512]{2,1,0:T(8,128)(2,1)S(1)}, u32[]{:S(2)}, u32[]{:S(2)}) collective-permute-start(bf16[4,128,512]{2,1,0:T(8,128)(2,1)} %own_ref.3), channel_id=1, source_target_pairs={{1,0},{2,1},{3,2},{5,4},{6,5},{7,6},{9,8},{10,9},{11,10},{13,12},{... | collective-permute-start | bytes 1572872 | tf_op jit(solution)/shard_map/ppermute | solution.py:556
  2.6 15.2 %collective-permute-start = (bf16[4,128,512]{2,1,0:T(8,128)(2,1)}, bf16[4,128,512]{2,1,0:T(8,128)(2,1)S(1)}, u32[]{:S(2)}, u32[]{:S(2)}) collective-permute-start(bf16[4,128,512]{2,1,0:T(8,128)(2,1)} %own_ref.3), channel_id=1, source_target_pairs={{0,1},{1,2},{2,3},{4,5},{5,6},{6,7},{8,9},{9,10},{10,11},{12,13},{... | collective-permute-start | bytes 1572872 | tf_op jit(solution)/shard_map/ppermute | solution.py:555
  15.5 18.2 %collective-permute-start.3 = (bf16[4,128,512]{2,1,0:T(8,128)(2,1)S(1)}, bf16[4,128,512]{2,1,0:T(8,128)(2,1)}, u32[]{:S(2)}, u32[]{:S(2)}) collective-permute-start(bf16[4,128,512]{2,1,0:T(8,128)(2,1)S(1)} %collective-permute-done.2.refs_1_), channel_id=1, source_target_pairs={{1,0},{2,1},{5,4},{6,5},{9,8},{10,9},{13,12},{14,13},{17,16},{18,1... | collective-permute-start | bytes 1572872 | tf_op jit(solution)/shard_map/ppermute | solution.py:556
  17.8 18.1 %collective-permute-start.1 = (bf16[4,128,512]{2,1,0:T(8,128)(2,1)S(1)}, bf16[4,128,512]{2,1,0:T(8,128)(2,1)}, u32[]{:S(2)}, u32[]{:S(2)}) collective-permute-start(bf16[4,128,512]{2,1,0:T(8,128)(2,1)S(1)} %collective-permute-done.refs_0_), channel_id=1, source_target_pairs={{1,2},{2,3},{5,6},{6,7},{9,10},{10,11},{13,14},{14,15},{17,18},{18... | collective-permute-start | bytes 1572872 | tf_op jit(solution)/shard_map/ppermute | solution.py:555
  26.8 1.3 copy-start.3
  32.4 1.3 copy-start.5
  33.8 20.0 %collective-permute-start.5 = (bf16[4,128,512]{2,1,0:T(8,128)(2,1)}, bf16[4,128,512]{2,1,0:T(8,128)(2,1)}, u32[]{:S(2)}, u32[]{:S(2)}) collective-permute-start(bf16[4,128,512]{2,1,0:T(8,128)(2,1)} %collective-permute-done.3.refs_1_.refs_3_), channel_id=1, source_target_pairs={{1,0},{5,4},{9,8},{13,12},{17,16},{21,20},{25,24},{29,28}} | collective-permute-start | bytes 1572872 | tf_op jit(solution)/shard_map/ppermute | solution.py:556
  35.9 17.9 %collective-permute-start.4 = (bf16[4,128,512]{2,1,0:T(8,128)(2,1)}, bf16[4,128,512]{2,1,0:T(8,128)(2,1)}, u32[]{:S(2)}, u32[]{:S(2)}) collective-permute-start(bf16[4,128,512]{2,1,0:T(8,128)(2,1)} %collective-permute-done.1.refs_0_.refs_2_), channel_id=1, source_target_pairs={{2,3},{6,7},{10,11},{14,15},{18,19},{22,23},{26,27},{30,31}} | collective-permute-start | bytes 1572872 | tf_op jit(solution)/shard_map/ppermute | solution.py:555
  37.5 16.3 %copy-start = (bf16[4,512,256]{2,1,0:T(8,128)(2,1)S(1)}, bf16[4,512,256]{2,1,0:T(8,128)(2,1)}, u32[]{:S(2)}) copy-start(bf16[4,512,256]{2,1,0:T(8,128)(2,1)} %base_ref.3) | copy-start | bytes 3145732
  37.5 16.3 %copy-start.1 = (bf16[4,128,512]{2,1,0:T(8,128)(2,1)S(1)}, bf16[4,128,512]{2,1,0:T(8,128)(2,1)}, u32[]{:S(2)}) copy-start(bf16[4,128,512]{2,1,0:T(8,128)(2,1)} %own_ref.3) | copy-start | bytes 1572868
  37.5 16.3 %copy-start.2 = (s32[4]{0:T(128)S(1)}, s32[4]{0:T(128)}, u32[]{:S(2)}) copy-start(s32[4]{0:T(128)} %count_ref.3) | copy-start | bytes 52
  41.7 1.3 copy-start.7
  43.7 9.9 %all-to-all-start = ((s32[8,1,512]{2,1,0:T(1,128)}), s32[8,1,512]{2,1,0:T(1,128)S(1)}, u32[]{:S(2)}, u32[]{:S(2)}) async-start(s32[8,1,512]{2,1,0:T(1,128)} %all_to_all.6), calls=%async_computation | async-start | bytes 32768 | tf_op jit(solution)/shard_map/all_to_all | solution.py:590
  61.4 9.4 %collective-permute-start.6 = (bf16[512,128]{1,0:T(8,128)(2,1)S(1)}, bf16[512,128]{1,0:T(8,128)(2,1)S(1)}, u32[]{:S(2)}, u32[]{:S(2)}) collective-permute-start(bf16[512,128]{1,0:T(8,128)(2,1)S(1)} %get-tuple-element.48), channel_id=1, source_target_pairs={{0,4},{4,0},{8,12},{12,8},{16,20},{20,16},{24,28},{28,24},{1,5},{5... | collective-permute-start | bytes 393224 | tf_op jit(solution)/shard_map/ppermute | solution.py:546
  62.8 10.7 %collective-permute-start.7 = (bf16[512,128]{1,0:T(8,128)(2,1)S(1)}, bf16[512,128]{1,0:T(8,128)(2,1)S(1)}, u32[]{:S(2)}, u32[]{:S(2)}) collective-permute-start(bf16[512,128]{1,0:T(8,128)(2,1)S(1)} %get-tuple-element.49), channel_id=1, source_target_pairs={{0,16},{4,20},{8,24},{12,28},{16,0},{20,4},{24,8},{28,12},{1,17},{... | collective-permute-start | bytes 393224 | tf_op jit(solution)/shard_map/ppermute | solution.py:546
  62.8 11.1 %collective-permute-start.8 = (bf16[512,128]{1,0:T(8,128)(2,1)S(1)}, bf16[512,128]{1,0:T(8,128)(2,1)S(1)}, u32[]{:S(2)}, u32[]{:S(2)}) collective-permute-start(bf16[512,128]{1,0:T(8,128)(2,1)S(1)} %get-tuple-element.50), channel_id=1, source_target_pairs={{0,24},{4,28},{8,16},{12,20},{16,8},{20,12},{24,0},{28,4},{1,25},{... | collective-permute-start | bytes 393224 | tf_op jit(solution)/shard_map/ppermute | solution.py:546
  64.2 9.7 %collective-permute-start.9 = (bf16[512,128]{1,0:T(8,128)(2,1)S(1)}, bf16[512,128]{1,0:T(8,128)(2,1)S(1)}, u32[]{:S(2)}, u32[]{:S(2)}) collective-permute-start(bf16[512,128]{1,0:T(8,128)(2,1)S(1)} %get-tuple-element.51), channel_id=1, source_target_pairs={{0,28},{4,24},{8,20},{12,16},{16,12},{20,8},{24,4},{28,0},{1,29},{... | collective-permute-start | bytes 393224 | tf_op jit(solution)/shard_map/ppermute | solution.py:546
  66.1 8.3 %collective-permute-start.10 = (bf16[512,128]{1,0:T(8,128)(2,1)S(1)}, bf16[512,128]{1,0:T(8,128)(2,1)S(1)}, u32[]{:S(2)}, u32[]{:S(2)}) collective-permute-start(bf16[512,128]{1,0:T(8,128)(2,1)S(1)} %get-tuple-element.52), channel_id=1, source_target_pairs={{0,8},{4,12},{8,0},{12,4},{16,24},{20,28},{24,16},{28,20},{1,9},{5... | collective-permute-start | bytes 393224 | tf_op jit(solution)/shard_map/ppermute | solution.py:546
  66.5 12.9 %copy-start.4 = (bf16[2,256,2048]{2,1,0:T(8,128)(2,1)S(1)}, bf16[2,256,2048]{2,1,0:T(8,128)(2,1)}, u32[]{:S(2)}) copy-start(bf16[2,256,2048]{2,1,0:T(8,128)(2,1)} %copy-done.3) | copy-start | bytes 6291460
  66.5 12.9 %copy-start.6 = (bf16[2,256,2048]{2,1,0:T(8,128)(2,1)S(1)}, bf16[2,256,2048]{2,1,0:T(8,128)(2,1)}, u32[]{:S(2)}) copy-start(bf16[2,256,2048]{2,1,0:T(8,128)(2,1)} %copy-done.5) | copy-start | bytes 6291460
  66.5 12.9 %copy-start.8 = (bf16[2,256,2048]{2,1,0:T(8,128)(2,1)S(1)}, bf16[2,256,2048]{2,1,0:T(8,128)(2,1)}, u32[]{:S(2)}) copy-start(bf16[2,256,2048]{2,1,0:T(8,128)(2,1)} %copy-done.7) | copy-start | bytes 6291460
  70.8 7.2 %collective-permute-start.11 = (bf16[512,128]{1,0:T(8,128)(2,1)S(1)}, bf16[512,128]{1,0:T(8,128)(2,1)S(1)}, u32[]{:S(2)}, u32[]{:S(2)}) collective-permute-start(bf16[512,128]{1,0:T(8,128)(2,1)S(1)} %get-tuple-element.53), channel_id=1, source_target_pairs={{0,12},{4,8},{8,4},{12,0},{16,28},{20,24},{24,20},{28,16},{1,13},{... | collective-permute-start | bytes 393224 | tf_op jit(solution)/shard_map/ppermute | solution.py:546
  73.5 5.9 %collective-permute-start.12 = (bf16[512,128]{1,0:T(8,128)(2,1)S(1)}, bf16[512,128]{1,0:T(8,128)(2,1)S(1)}, u32[]{:S(2)}, u32[]{:S(2)}) collective-permute-start(bf16[512,128]{1,0:T(8,128)(2,1)S(1)} %get-tuple-element.54), channel_id=1, source_target_pairs={{0,20},{4,16},{8,28},{12,24},{16,4},{20,0},{24,12},{28,8},{1,21},{... | collective-permute-start | bytes 393224 | tf_op jit(solution)/shard_map/ppermute | solution.py:546
  88.1 3.8 %collective-permute-start.13 = (bf16[512,128]{1,0:T(8,128)(2,1)S(1)}, bf16[512,128]{1,0:T(8,128)(2,1)S(1)}, u32[]{:S(2)}, u32[]{:S(2)}) collective-permute-start(bf16[512,128]{1,0:T(8,128)(2,1)S(1)} %get-tuple-element.63), channel_id=1, source_target_pairs={{0,4},{4,0},{8,12},{12,8},{16,20},{20,16},{24,28},{28,24},{1,5},{5... | collective-permute-start | bytes 393224 | tf_op jit(solution)/shard_map/ppermute | solution.py:546
  88.7 5.1 %collective-permute-start.14 = (bf16[512,128]{1,0:T(8,128)(2,1)S(1)}, bf16[512,128]{1,0:T(8,128)(2,1)S(1)}, u32[]{:S(2)}, u32[]{:S(2)}) collective-permute-start(bf16[512,128]{1,0:T(8,128)(2,1)S(1)} %get-tuple-element.64), channel_id=1, source_target_pairs={{0,16},{4,20},{8,24},{12,28},{16,0},{20,4},{24,8},{28,12},{1,17},{... | collective-permute-start | bytes 393224 | tf_op jit(solution)/shard_map/ppermute | solution.py:546
  88.7 6.4 %collective-permute-start.15 = (bf16[512,128]{1,0:T(8,128)(2,1)S(1)}, bf16[512,128]{1,0:T(8,128)(2,1)S(1)}, u32[]{:S(2)}, u32[]{:S(2)}) collective-permute-start(bf16[512,128]{1,0:T(8,128)(2,1)S(1)} %get-tuple-element.65), channel_id=1, source_target_pairs={{0,8},{4,12},{8,0},{12,4},{16,24},{20,28},{24,16},{28,20},{1,9},{5... | collective-permute-start | bytes 393224 | tf_op jit(solution)/shard_map/ppermute | solution.py:546
  88.7 8.0 %collective-permute-start.16 = (bf16[512,128]{1,0:T(8,128)(2,1)S(1)}, bf16[512,128]{1,0:T(8,128)(2,1)S(1)}, u32[]{:S(2)}, u32[]{:S(2)}) collective-permute-start(bf16[512,128]{1,0:T(8,128)(2,1)S(1)} %get-tuple-element.66), channel_id=1, source_target_pairs={{0,20},{4,16},{8,28},{12,24},{16,4},{20,0},{24,12},{28,8},{1,21},{... | collective-permute-start | bytes 393224 | tf_op jit(solution)/shard_map/ppermute | solution.py:546
  90.5 6.9 %collective-permute-start.17 = (bf16[512,128]{1,0:T(8,128)(2,1)S(1)}, bf16[512,128]{1,0:T(8,128)(2,1)S(1)}, u32[]{:S(2)}, u32[]{:S(2)}) collective-permute-start(bf16[512,128]{1,0:T(8,128)(2,1)S(1)} %get-tuple-element.67), channel_id=1, source_target_pairs={{0,12},{4,8},{8,4},{12,0},{16,28},{20,24},{24,20},{28,16},{1,13},{... | collective-permute-start | bytes 393224 | tf_op jit(solution)/shard_map/ppermute | solution.py:546
  92.0 8.9 %collective-permute-start.18 = (bf16[512,128]{1,0:T(8,128)(2,1)S(1)}, bf16[512,128]{1,0:T(8,128)(2,1)S(1)}, u32[]{:S(2)}, u32[]{:S(2)}) collective-permute-start(bf16[512,128]{1,0:T(8,128)(2,1)S(1)} %get-tuple-element.68), channel_id=1, source_target_pairs={{0,24},{4,28},{8,16},{12,20},{16,8},{20,12},{24,0},{28,4},{1,25},{... | collective-permute-start | bytes 393224 | tf_op jit(solution)/shard_map/ppermute | solution.py:546
  93.8 9.8 %collective-permute-start.19 = (bf16[512,128]{1,0:T(8,128)(2,1)S(1)}, bf16[512,128]{1,0:T(8,128)(2,1)S(1)}, u32[]{:S(2)}, u32[]{:S(2)}) collective-permute-start(bf16[512,128]{1,0:T(8,128)(2,1)S(1)} %get-tuple-element.69), channel_id=1, source_target_pairs={{0,28},{4,24},{8,20},{12,16},{16,12},{20,8},{24,4},{28,0},{1,29},{... | collective-permute-start | bytes 393224 | tf_op jit(solution)/shard_map/ppermute | solution.py:546
  112.3 4.8 %collective-permute-start.20 = (bf16[512,128]{1,0:T(8,128)(2,1)S(1)}, bf16[512,128]{1,0:T(8,128)(2,1)S(1)}, u32[]{:S(2)}, u32[]{:S(2)}) collective-permute-start(bf16[512,128]{1,0:T(8,128)(2,1)S(1)} %get-tuple-element.72), channel_id=1, source_target_pairs={{0,4},{4,0},{8,12},{12,8},{16,20},{20,16},{24,28},{28,24},{1,5},{5... | collective-permute-start | bytes 393224 | tf_op jit(solution)/shard_map/ppermute | solution.py:546
  114.1 10.7 %collective-permute-start.21 = (bf16[512,128]{1,0:T(8,128)(2,1)S(1)}, bf16[512,128]{1,0:T(8,128)(2,1)S(1)}, u32[]{:S(2)}, u32[]{:S(2)}) collective-permute-start(bf16[512,128]{1,0:T(8,128)(2,1)S(1)} %get-tuple-element.73), channel_id=1, source_target_pairs={{0,16},{4,20},{8,24},{12,28},{16,0},{20,4},{24,8},{28,12},{1,17},{... | collective-permute-start | bytes 393224 | tf_op jit(solution)/shard_map/ppermute | solution.py:546
  114.1 11.0 %collective-permute-start.22 = (bf16[512,128]{1,0:T(8,128)(2,1)S(1)}, bf16[512,128]{1,0:T(8,128)(2,1)S(1)}, u32[]{:S(2)}, u32[]{:S(2)}) collective-permute-start(bf16[512,128]{1,0:T(8,128)(2,1)S(1)} %get-tuple-element.74), channel_id=1, source_target_pairs={{0,24},{4,28},{8,16},{12,20},{16,8},{20,12},{24,0},{28,4},{1,25},{... | collective-permute-start | bytes 393224 | tf_op jit(solution)/shard_map/ppermute | solution.py:546
  114.8 10.4 %collective-permute-start.23 = (bf16[512,128]{1,0:T(8,128)(2,1)S(1)}, bf16[512,128]{1,0:T(8,128)(2,1)S(1)}, u32[]{:S(2)}, u32[]{:S(2)}) collective-permute-start(bf16[512,128]{1,0:T(8,128)(2,1)S(1)} %get-tuple-element.75), channel_id=1, source_target_pairs={{0,28},{4,24},{8,20},{12,16},{16,12},{20,8},{24,4},{28,0},{1,29},{... | collective-permute-start | bytes 393224 | tf_op jit(solution)/shard_map/ppermute | solution.py:546
  117.0 8.7 %collective-permute-start.24 = (bf16[512,128]{1,0:T(8,128)(2,1)S(1)}, bf16[512,128]{1,0:T(8,128)(2,1)S(1)}, u32[]{:S(2)}, u32[]{:S(2)}) collective-permute-start(bf16[512,128]{1,0:T(8,128)(2,1)S(1)} %get-tuple-element.76), channel_id=1, source_target_pairs={{0,8},{4,12},{8,0},{12,4},{16,24},{20,28},{24,16},{28,20},{1,9},{5... | collective-permute-start | bytes 393224 | tf_op jit(solution)/shard_map/ppermute | solution.py:546
  117.1 12.2 %collective-permute-start.25 = (bf16[512,128]{1,0:T(8,128)(2,1)S(1)}, bf16[512,128]{1,0:T(8,128)(2,1)S(1)}, u32[]{:S(2)}, u32[]{:S(2)}) collective-permute-start(bf16[512,128]{1,0:T(8,128)(2,1)S(1)} %get-tuple-element.77), channel_id=1, source_target_pairs={{0,12},{4,8},{8,4},{12,0},{16,28},{20,24},{24,20},{28,16},{1,13},{... | collective-permute-start | bytes 393224 | tf_op jit(solution)/shard_map/ppermute | solution.py:546
  124.8 5.9 %collective-permute-start.26 = (bf16[512,128]{1,0:T(8,128)(2,1)S(1)}, bf16[512,128]{1,0:T(8,128)(2,1)S(1)}, u32[]{:S(2)}, u32[]{:S(2)}) collective-permute-start(bf16[512,128]{1,0:T(8,128)(2,1)S(1)} %get-tuple-element.78), channel_id=1, source_target_pairs={{0,20},{4,16},{8,28},{12,24},{16,4},{20,0},{24,12},{28,8},{1,21},{... | collective-permute-start | bytes 393224 | tf_op jit(solution)/shard_map/ppermute | solution.py:546
  138.7 4.7 %collective-permute-start.27 = (bf16[512,128]{1,0:T(8,128)(2,1)S(1)}, bf16[512,128]{1,0:T(8,128)(2,1)S(1)}, u32[]{:S(2)}, u32[]{:S(2)}) collective-permute-start(bf16[512,128]{1,0:T(8,128)(2,1)S(1)} %get-tuple-element.80), channel_id=1, source_target_pairs={{0,4},{4,0},{8,12},{12,8},{16,20},{20,16},{24,28},{28,24},{1,5},{5... | collective-permute-start | bytes 393224 | tf_op jit(solution)/shard_map/ppermute | solution.py:546
  139.3 5.1 %collective-permute-start.28 = (bf16[512,128]{1,0:T(8,128)(2,1)S(1)}, bf16[512,128]{1,0:T(8,128)(2,1)S(1)}, u32[]{:S(2)}, u32[]{:S(2)}) collective-permute-start(bf16[512,128]{1,0:T(8,128)(2,1)S(1)} %get-tuple-element.81), channel_id=1, source_target_pairs={{0,16},{4,20},{8,24},{12,28},{16,0},{20,4},{24,8},{28,12},{1,17},{... | collective-permute-start | bytes 393224 | tf_op jit(solution)/shard_map/ppermute | solution.py:546
  139.3 7.2 %collective-permute-start.29 = (bf16[512,128]{1,0:T(8,128)(2,1)S(1)}, bf16[512,128]{1,0:T(8,128)(2,1)S(1)}, u32[]{:S(2)}, u32[]{:S(2)}) collective-permute-start(bf16[512,128]{1,0:T(8,128)(2,1)S(1)} %get-tuple-element.82), channel_id=1, source_target_pairs={{0,8},{4,12},{8,0},{12,4},{16,24},{20,28},{24,16},{28,20},{1,9},{5... | collective-permute-start | bytes 393224 | tf_op jit(solution)/shard_map/ppermute | solution.py:546
  139.3 8.0 %collective-permute-start.30 = (bf16[512,128]{1,0:T(8,128)(2,1)S(1)}, bf16[512,128]{1,0:T(8,128)(2,1)S(1)}, u32[]{:S(2)}, u32[]{:S(2)}) collective-permute-start(bf16[512,128]{1,0:T(8,128)(2,1)S(1)} %get-tuple-element.83), channel_id=1, source_target_pairs={{0,20},{4,16},{8,28},{12,24},{16,4},{20,0},{24,12},{28,8},{1,21},{... | collective-permute-start | bytes 393224 | tf_op jit(solution)/shard_map/ppermute | solution.py:546
  141.0 6.9 %collective-permute-start.31 = (bf16[512,128]{1,0:T(8,128)(2,1)S(1)}, bf16[512,128]{1,0:T(8,128)(2,1)S(1)}, u32[]{:S(2)}, u32[]{:S(2)}) collective-permute-start(bf16[512,128]{1,0:T(8,128)(2,1)S(1)} %get-tuple-element.84), channel_id=1, source_target_pairs={{0,12},{4,8},{8,4},{12,0},{16,28},{20,24},{24,20},{28,16},{1,13},{... | collective-permute-start | bytes 393224 | tf_op jit(solution)/shard_map/ppermute | solution.py:546
  143.3 8.0 %collective-permute-start.32 = (bf16[512,128]{1,0:T(8,128)(2,1)S(1)}, bf16[512,128]{1,0:T(8,128)(2,1)S(1)}, u32[]{:S(2)}, u32[]{:S(2)}) collective-permute-start(bf16[512,128]{1,0:T(8,128)(2,1)S(1)} %get-tuple-element.85), channel_id=1, source_target_pairs={{0,24},{4,28},{8,16},{12,20},{16,8},{20,12},{24,0},{28,4},{1,25},{... | collective-permute-start | bytes 393224 | tf_op jit(solution)/shard_map/ppermute | solution.py:546
  144.4 9.8 %collective-permute-start.33 = (bf16[512,128]{1,0:T(8,128)(2,1)S(1)}, bf16[512,128]{1,0:T(8,128)(2,1)S(1)}, u32[]{:S(2)}, u32[]{:S(2)}) collective-permute-start(bf16[512,128]{1,0:T(8,128)(2,1)S(1)} %get-tuple-element.86), channel_id=1, source_target_pairs={{0,28},{4,24},{8,20},{12,16},{16,12},{20,8},{24,4},{28,0},{1,29},{... | collective-permute-start | bytes 393224 | tf_op jit(solution)/shard_map/ppermute | solution.py:546

commit v8 on v7

--- a/solution.py
+++ b/solution.py
@@ -21,10 +21,12 @@
 PICK_VMEM = 12 * MIB
 LATE_PICK_VMEM = 18 * MIB
 LATE_VMEM = 12 * MIB
-BASIS_CALLS = 4
+BASIS_CALLS = (1, 2, 3, 2)
 UNROLL = 32
+PICK_UNROLL = 16
 SUB = 8
-HBM_SPARE = 32
+HBM_ROWS = 24 * 1024 * 1024 // 512
+HBM_PLANS = 48
 COST_US = 10 ** 9
 
 COS_POLY = (1.0, -19.73920440673828, 64.9391098022461, -85.4500503540039, 60.16689682006836,
@@ -45,8 +47,8 @@
     return acc
 
 
-def basis_kernel(after, time_ref, period_ref, inverse_ref, *refs):
-    basis_ref, norm_ref = refs[after:]
+def basis_kernel(time_ref, period_ref, inverse_ref, *refs):
+    basis_ref, norm_ref = refs[-2:]
     obs = time_ref.shape[0]
     nper = period_ref.shape[1]
     rows = 32
@@ -79,34 +81,36 @@
         norm_ref[0, :, sines] = 1.0 / (jnp.sum(total_s, axis=0, keepdims=True) + RIDGE)
 
 
-def make_basis(times, periods, after):
+def make_basis(times, periods, first, count, held, after):
     sched_dev, obs = times.shape
     nper = periods.shape[0]
     wide = jnp.broadcast_to(
-        times.astype(jnp.float32).reshape(-1, 1), (sched_dev * obs, SRC_GROUP)
+        times[first:first + count].astype(jnp.float32).reshape(-1, 1), (count * obs, SRC_GROUP)
     )
     period = periods.astype(jnp.float32)[None, :]
+    others = after + ([] if held is None else [held])
     return pl.pallas_call(
-        functools.partial(basis_kernel, len(after)),
-        grid=(sched_dev,),
+        basis_kernel,
+        grid=(count,),
         in_specs=[
             pl.BlockSpec((obs, SRC_GROUP), lambda j: (j, 0)),
             pl.BlockSpec((1, nper), lambda j: (0, 0)),
             pl.BlockSpec((1, nper), lambda j: (0, 0)),
-        ] + [ANY] * len(after),
+        ] + [ANY] * len(others),
         out_specs=[
-            pl.BlockSpec((1, obs, 2 * nper), lambda j: (j, 0, 0)),
+            pl.BlockSpec((1, obs, 2 * nper), lambda j: (first + j, 0, 0)),
             pl.BlockSpec((1, 1, 2 * nper), lambda j: (j, 0, 0)),
         ],
         out_shape=[
-            jax.ShapeDtypeStruct((sched_dev, obs, 2 * nper), jnp.bfloat16),
-            jax.ShapeDtypeStruct((sched_dev, 1, 2 * nper), jnp.float32),
+            jax.ShapeDtypeStruct((max(HBM_PLANS, sched_dev), obs, 2 * nper), jnp.bfloat16),
+            jax.ShapeDtypeStruct((count, 1, 2 * nper), jnp.float32),
         ],
+        input_output_aliases={} if held is None else {2 + len(others): 0},
         compiler_params=pltpu.CompilerParams(vmem_limit_bytes=BASIS_VMEM),
         cost_estimate=pl.CostEstimate(
-            flops=sched_dev * obs * nper * 10000, bytes_accessed=sched_dev * obs * nper * 4, transcendentals=0
+            flops=count * obs * nper * 2500, bytes_accessed=count * obs * nper * 4, transcendentals=0
         ),
-    )(wide, period, 1.0 / period, *after)
+    )(wide, period, 1.0 / period, *others)
 
 
 def fit_kernel(order, src_ref, dst_ref, *refs):
@@ -119,8 +123,7 @@
 
     tm_count = len(order)
     arrived = dict(zip(order, take(tm_count)))
-    parts = take(BASIS_CALLS)
-    (norm_ref,) = take(1)
+    all_ref, norm_ref = take(2)
     outs = take(tm_count)
     score_ref, basis_ref, sems, rows_ref, back_ref = take(5)
     slots = [take(4), take(4)]
@@ -129,10 +132,9 @@
     capacity, width = arrived[0].shape
     spaced = capacity + STEP
     steps = src_ref.shape[1]
-    each = plans // len(parts)
 
     def basis_copy(plan):
-        return pltpu.make_async_copy(parts[plan // each].at[plan % each], basis_ref.at[plan], sems.at[plan])
+        return pltpu.make_async_copy(all_ref.at[plan], basis_ref.at[plan], sems.at[plan])
 
     for plan in range(plans):
         basis_copy(plan).start()
@@ -197,11 +199,11 @@
         outs[owner][...] = back_ref[pl.ds(owner * spaced, capacity), :].astype(jnp.bfloat16)
 
 
-def fit_plans(tables, arrived, parts, norms):
+def fit_plans(tables, arrived, basis, norms):
     tm_count = len(arrived)
     order = [0] + ask_order(tm_count)
-    each, obs, twice = parts[0].shape
-    sched_dev = each * len(parts)
+    _, obs, twice = basis.shape
+    sched_dev = norms.shape[0]
     capacity, width = arrived[0].shape
     work = sched_dev * obs * twice * width
     spaced = tm_count * (capacity + STEP) + STEP
@@ -213,7 +215,7 @@
     ]
     *models, score = pl.pallas_call(
         functools.partial(fit_kernel, order),
-        in_specs=[SMEM, SMEM] + [VMEM] * tm_count + [ANY] * len(parts) + [VMEM],
+        in_specs=[SMEM, SMEM] + [VMEM] * tm_count + [ANY, VMEM],
         out_specs=[VMEM] * (tm_count + 1),
         out_shape=[jax.ShapeDtypeStruct((capacity, width), jnp.bfloat16)] * tm_count
         + [jax.ShapeDtypeStruct((sched_dev, width, 1), jnp.float32)],
@@ -225,7 +227,7 @@
         ] + slot + slot,
         compiler_params=pltpu.CompilerParams(vmem_limit_bytes=FIT_VMEM),
         cost_estimate=pl.CostEstimate(flops=20 * work, bytes_accessed=sched_dev * obs * twice * 2, transcendentals=0),
-    )(*tables, *[arrived[owner] for owner in order], *parts, norms)
+    )(*tables, *[arrived[owner] for owner in order], basis, norms)
     return models, score
 
 
@@ -237,20 +239,19 @@
         copies.append((sky >= hop, sky - hop, passed[2 * hop - 2]))
         copies.append((sky + hop < count, sky + hop, passed[2 * hop - 1]))
 
-    def each(act, segs):
+    def each(act):
         for index, (valid, quarter, ref) in enumerate(copies):
             def run(index=index, quarter=quarter, ref=ref):
                 at = pl.ds(pl.multiple_of(quarter * rows, rows), rows)
-                for seg in segs:
-                    act(pltpu.make_async_copy(ref.at[seg], whole_ref.at[seg, at, :], sems.at[index, seg]))
+                act(pltpu.make_async_copy(ref, whole_ref.at[:, at, :], sems.at[index]))
 
             if valid is None:
                 run()
             else:
                 pl.when(valid)(run)
 
-    each(lambda copy: copy.start(), range(own_ref.shape[0]))
-    return lambda seg: each(lambda copy: copy.wait(), [seg])
+    each(lambda copy: copy.start())
+    return lambda: each(lambda copy: copy.wait())
 
 
 def whiten_and_pick(me, asked_ref, cnt_ref, count_ref, whole_ref, wait, load, picked, white_ref, gather_ref):
@@ -258,8 +259,8 @@
     capacity, width = picked[0].shape
     blocks = white_ref.shape[0] // (segs * slots)
     row = lax.broadcasted_iota(jnp.int32, (slots, width * blocks), 0)
+    wait()
     for seg in range(segs):
-        wait(seg)
         masked = jnp.where(row < count_ref[seg], load(seg).astype(jnp.float32), 0.0).astype(jnp.bfloat16)
         white = jnp.dot(whole_ref[seg], masked, preferred_element_type=jnp.float32)
         for block in range(blocks):
@@ -268,37 +269,43 @@
         asker = owner ^ me
 
         def step(index, carry):
-            first = asker * capacity + index * UNROLL
-            tile = (owner * capacity) // SUB + index * (UNROLL // SUB)
-            for lane in range(UNROLL):
-                gather_ref[tile + lane // SUB, pl.ds(lane % SUB, 1), :] = white_ref[
-                    pl.ds(asked_ref[first + lane], 1), :
+            first = index * PICK_UNROLL
+            for lane in range(PICK_UNROLL):
+                gather_ref[pl.ds(owner * capacity + first + lane, 1), :] = white_ref[
+                    pl.ds(asked_ref[asker * capacity + first + lane], 1), :
                 ]
             return carry
 
-        lax.fori_loop(0, (cnt_ref[asker] + UNROLL - 1) // UNROLL, step, 0)
-        block = gather_ref[pl.ds(owner * capacity // SUB, capacity // SUB)]
-        out_ref[...] = block.reshape(capacity, width).astype(jnp.bfloat16)
-
-
-def add_rows(me, asked_ref, cnt_ref, owners, returned, rows_ref, sums):
+        lax.fori_loop(0, (cnt_ref[asker] + PICK_UNROLL - 1) // PICK_UNROLL, step, 0)
+        out_ref[...] = gather_ref[pl.ds(owner * capacity, capacity), :].astype(jnp.bfloat16)
+
+
+def add_rows(me, asked_ref, cnt_ref, owners, returned, rows_ref, sums, tiled):
     capacity = returned[0].shape[0]
     streams = len(sums)
     for total in sums:
         total[...] = jnp.zeros_like(total)
     for number, (owner, ref) in enumerate(zip(owners, returned)):
         tiles = capacity // SUB
-        rows_ref[pl.ds(number * tiles, tiles)] = ref[...].astype(jnp.float32).reshape(tiles, SUB, -1)
+        block = ref[...].astype(jnp.float32)
+        if tiled:
+            rows_ref[pl.ds(number * tiles, tiles)] = block.reshape(tiles, SUB, -1)
+        else:
+            rows_ref[pl.ds(number * capacity, capacity), :] = block
         asker = owner ^ me
+
+        def row_at(index, lane):
+            if tiled:
+                return rows_ref[number * tiles + index * (UNROLL // SUB) + lane // SUB, pl.ds(lane % SUB, 1), :]
+            return rows_ref[pl.ds(number * capacity + index * UNROLL + lane, 1), :]
 
         def step(index, carry):
             first = asker * capacity + index * UNROLL
-            tile = number * tiles + index * (UNROLL // SUB)
             for start in range(0, UNROLL, streams):
                 lanes = [start + lane for lane in range(streams)]
                 places = [asked_ref[first + lane] for lane in lanes]
                 values = [
-                    total[pl.ds(place, 1), :] + rows_ref[tile + lane // SUB, pl.ds(lane % SUB, 1), :]
+                    total[pl.ds(place, 1), :] + row_at(index, lane)
                     for total, place, lane in zip(sums, places, lanes)
                 ]
                 for total, place, value in zip(sums, places, values):
@@ -320,7 +327,7 @@
         held_ref, sem = refs.pop(0), refs.pop(0)
         copy = pltpu.make_async_copy(base_ref.at[pl.ds(0, held_ref.shape[0]), :], held_ref, sem)
         copy.start()
-    add_rows(where_ref[0], asked_ref, cnt_ref, owners, returned, rows_ref, refs)
+    add_rows(where_ref[0], asked_ref, cnt_ref, owners, returned, rows_ref, refs, not table_base)
     if table_base:
         copy.wait()
         out_ref[...] = held_ref[...] - placed_at(refs, pl.ds(0, out_ref.shape[0]))
@@ -339,13 +346,16 @@
     table_base = base.ndim == 2
     capacity = returned[0].shape[0]
     sums = [pltpu.VMEM((rows + 8, SRC_GROUP), jnp.float32)] * STREAMS
+    shape = (len(owners) * capacity, SRC_GROUP)
+    if not table_base:
+        shape = (shape[0] // SUB, SUB, SRC_GROUP)
     held = [pltpu.VMEM((rows, SRC_GROUP), jnp.float32), pltpu.SemaphoreType.DMA(())] if table_base else []
     return pl.pallas_call(
         functools.partial(early_kernel, owners, table_base),
         in_specs=[SMEM] * 3 + [HBM if table_base else VMEM] + [VMEM] * len(owners),
         out_specs=VMEM,
         out_shape=jax.ShapeDtypeStruct((rows, SRC_GROUP), jnp.float32),
-        scratch_shapes=[pltpu.VMEM((len(owners) * capacity // SUB, SUB, SRC_GROUP), jnp.float32)] + held + sums,
+        scratch_shapes=[pltpu.VMEM(shape, jnp.float32)] + held + sums,
         compiler_params=pltpu.CompilerParams(vmem_limit_bytes=EARLY_VMEM),
         cost_estimate=pl.CostEstimate(flops=6 * COST_US, bytes_accessed=1 << 20, transcendentals=0),
     )(asked, cnt, where, base, *[returned[owner] for owner in owners])
@@ -375,9 +385,9 @@
         out_shape=[jax.ShapeDtypeStruct((capacity, SRC_GROUP), jnp.bfloat16)] * tm_count,
         scratch_shapes=[
             pltpu.VMEM((seg_dev, slots, slots), jnp.bfloat16),
-            pltpu.SemaphoreType.DMA((len(attitude), seg_dev)),
+            pltpu.SemaphoreType.DMA((len(attitude),)),
             pltpu.VMEM((rows + 8, SRC_GROUP), jnp.float32),
-            pltpu.VMEM((tm_count * capacity // SUB, SUB, SRC_GROUP), jnp.float32),
+            pltpu.VMEM((tm_count * capacity, SRC_GROUP), jnp.float32),
         ],
         compiler_params=pltpu.CompilerParams(vmem_limit_bytes=PICK_VMEM),
         cost_estimate=pl.CostEstimate(flops=5 * COST_US, bytes_accessed=1 << 20, transcendentals=0),
@@ -401,7 +411,7 @@
     segs, slots, _ = whole_ref.shape
     blocks = table_ref.shape[0] // (segs * slots)
     wait = load_attitude(where_ref[1], own_ref, passed, whole_ref, sems)
-    add_rows(where_ref[0], asked_ref, cnt_ref, owners, returned, gather_ref, refs)
+    add_rows(where_ref[0], asked_ref, cnt_ref, owners, returned, gather_ref, refs, False)
     table_ref[...] = part_ref[...] - placed_at(refs, pl.ds(0, table_ref.shape[0]))
     copy = pltpu.make_async_copy(table_ref, out_ref.at[pl.ds(0, table_ref.shape[0]), :], sem)
     copy.start()
@@ -429,13 +439,13 @@
         functools.partial(late_pick_kernel, tm_count, len(attitude) - 1, owners),
         in_specs=[SMEM] * 4 + [VMEM] + [ANY] * len(attitude) + [VMEM] * len(owners),
         out_specs=[HBM] + [VMEM] * tm_count,
-        out_shape=[jax.ShapeDtypeStruct((HBM_SPARE * rows, SRC_GROUP), jnp.float32)]
+        out_shape=[jax.ShapeDtypeStruct((max(HBM_ROWS, rows), SRC_GROUP), jnp.float32)]
         + [jax.ShapeDtypeStruct((capacity, SRC_GROUP), jnp.bfloat16)] * tm_count,
         scratch_shapes=[
             pltpu.VMEM((seg_dev, slots, slots), jnp.bfloat16),
-            pltpu.SemaphoreType.DMA((len(attitude), seg_dev)),
+            pltpu.SemaphoreType.DMA((len(attitude),)),
             table,
-            pltpu.VMEM((tm_count * capacity // SUB, SUB, SRC_GROUP), jnp.float32),
+            pltpu.VMEM((tm_count * capacity, SRC_GROUP), jnp.float32),
             pltpu.VMEM((rows, SRC_GROUP), jnp.float32),
             pltpu.SemaphoreType.DMA(()),
         ] + [table] * LATE_STREAMS,
@@ -452,7 +462,7 @@
     sums = refs[4:]
     segs, slots, total_width = out_ref.shape
     width = part_ref.shape[1]
-    add_rows(where_ref[0], asked_ref, cnt_ref, owners, returned, rows_ref, sums)
+    add_rows(where_ref[0], asked_ref, cnt_ref, owners, returned, rows_ref, sums, False)
     copies = []
     for seg in range(segs):
         for block in range(total_width // width):
@@ -473,7 +483,7 @@
         out_specs=HBM,
         out_shape=jax.ShapeDtypeStruct(shape, jnp.float32),
         scratch_shapes=[
-            pltpu.VMEM((len(owners) * capacity // SUB, SUB, SRC_GROUP), jnp.float32),
+            pltpu.VMEM((len(owners) * capacity, SRC_GROUP), jnp.float32),
             pltpu.VMEM(shape, jnp.float32),
             pltpu.SemaphoreType.DMA((shape[0],)),
         ] + [pltpu.VMEM((part.shape[0] + 8, SRC_GROUP), jnp.float32)] * LATE_STREAMS,
@@ -570,24 +580,26 @@
         sched_seg, sched_slot, seg_dev, slots, column_blocks, tm_count, capacity
     )
     wanted = wanted.reshape(tm_count, capacity)
-    part = sched_dev // BASIS_CALLS
-    made = []
+    basis, norms = None, []
     asked = None
 
     def basis_part(after):
-        first = len(made) * part
-        made.append(make_basis(times[first:first + part], periods, after))
+        nonlocal basis
+        first, count = sum(BASIS_CALLS[:len(norms)]), BASIS_CALLS[len(norms)]
+        basis, norm = make_basis(times, periods, first, count, basis, after)
+        norms.append(norm)
 
     def first_hop(right, left):
+        nonlocal asked
+        held, right, left = lax.optimization_barrier((wanted, right, left))
         basis_part([right, left])
+        held, _ = lax.optimization_barrier((held, norms[0]))
+        asked = lax.all_to_all(held, "tm", split_axis=0, concat_axis=0, tiled=True)
+        basis_part([])
+        return right, left
+
+    def second_hop(right, left):
         basis_part([right, left])
-        return right, left
-
-    def second_hop(right, left):
-        nonlocal asked
-        basis_part([right, left])
-        held, _ = lax.optimization_barrier((wanted, made[-1][1]))
-        asked = lax.all_to_all(held, "tm", split_axis=0, concat_axis=0, tiled=True)
         return right, left
 
     pieces = pass_along(attitude, {1: first_hop, 2: second_hop})
@@ -601,10 +613,9 @@
     base = residuals
     picked = pick_rows(scalars, base, pieces, rows)
     basis_part([picked[0]])
-    parts, norms = zip(*made)
     norms = jnp.concatenate(norms)
     for iteration in range(ITERS):
-        models, score = fit_plans(tables, exchange(picked), parts, norms)
+        models, score = fit_plans(tables, exchange(picked), basis, norms)
         returned = exchange(models)
         base = place_early(scalars, near, base, returned, rows)
         if iteration < ITERS - 1:

time: 159 us -> 168 us (1.057)
  the two profiles are of different devices: /device:TPU:9 before, /device:TPU:1 now
where the time goes in v8:
time: 168 us; the launch traced here: 165 us
  Pallas kernels  57 us (34%)
  starting transfers between devices  53.6 us (32%)
  waiting for transfers between devices  26.5 us (16%)
  local copies, waits for them, and re-layouts  17.6 us (10%)
  other arithmetic  9.49 us (6%)
    ppermute x28, starting transfers between devices, exchange(): lax.ppermute(blocks[step], 'tm', [(i, i ^ step) for i in range(count)])  38.2 us
    pallas_call x4, Pallas kernels, make_basis(): pl.pallas_call(basis_kernel, grid=(count,), in_specs=[pl.BlockSpec((obs,...  20.8 us
    ppermute x28, waiting for transfers between devices, exchange(): lax.ppermute(blocks[step], 'tm', [(i, i ^ step) for i in range(count)])  19 us
    pallas_call x2, Pallas kernels, fit_plans(): pl.pallas_call(functools.partial(fit_kernel, order), in_specs=[SMEM, SMEM...  18.1 us
    unnamed x17, local copies, waits for them, and re-layouts  16.5 us
    pallas_call x2, Pallas kernels, place_early(): pl.pallas_call(functools.partial(early_kernel, owners, table_base), in_sp...  6.75 us
    ppermute x3, waiting for transfers between devices, pass_along(): lax.ppermute(left, 'sky', [(i, i - 1) for i in range(1, count - hop + 1)])  6.53 us
    ppermute x3, starting transfers between devices, pass_along(): lax.ppermute(right, 'sky', [(i, i + 1) for i in range(hop - 1, count - 1)])  6.07 us
  transfers between devices with their start and end apart: 35, of which 14 were waited for; matrix products, arithmetic and copies ran while one was open for 6% of the time, Pallas kernels for 17%

profile of v8, /device:TPU:1, one launch (start us, length us, event | category | flops | bytes accessed | tf_op | source)
XLA Modules:
  0.0 165.4 jit_solution(17755234289025760606)
XLA Ops:
  0.6 1.3 collective-permute-start.1
  1.9 4.7 %collective-permute-start = (bf16[4,128,512]{2,1,0:T(8,128)(2,1)}, bf16[4,128,512]{2,1,0:T(8,128)(2,1)S(1)}, u32[]{:S(2)}, u32[]{:S(2)}) collective-permute-start(bf16[4,128,512]{2,1,0:T(8,128)(2,1)} %own_ref.3), channel_id=1, source_target_pairs={{0,1},{1,2},{2,3},{4,5},{5,6},{6,7},{8,9},{9,10},{10,11},{12,13},{... | collective-permute-start | bytes 1572872 | tf_op jit(solution)/shard_map/ppermute | solution.py:565
  10.9 3.4 %select_reduce_fusion = s32[4096]{0:T(1024)S(1)} fusion(s32[2048]{0:T(1024)S(1)} %bitcast.34, s32[2048]{0:T(1024)S(1)} %bitcast.33), kind=kLoop, calls=%fused_computation | loop fusion | flops 25161728 | bytes 32768 | tf_op jit(solution)/shard_map/reduce_sum | solution.py:520
  14.5 2.1 %collective-permute-done.1.refs_1_ = bf16[4,128,512]{2,1,0:T(8,128)(2,1)S(1)} collective-permute-done((bf16[4,128,512]{2,1,0:T(8,128)(2,1)}, bf16[4,128,512]{2,1,0:T(8,128)(2,1)S(1)}, u32[]{:S(2)}, u32[]{:S(2)}) %collective-permute-start.1) | collective-permute-done | bytes 524320 | tf_op jit(solution)/shard_map/ppermute | solution.py:566
  16.5 1.0 collective-permute-done.refs_0_
  18.2 1.3 collective-permute-start.3
  20.4 3.1 %shard_map.77 = (bf16[48,256,2048]{2,1,0:T(8,128)(2,1)}, f32[1,1,2048]{2,1,0:T(1,128)S(1)}) custom-call(f32[256,128]{1,0:T(8,128)S(1)} %broadcast_in_dim.50.time_ref, f32[1,1024]{1,0:T(1,128)S(1)} %bitcast.27, f32[1,1024]{1,0:T(1,128)S(1)} %bitcast.23, bf16[4,128,512]{2,1,0:T(8,128)(2,1)S(1)} %collective-permute-done.refs_0_, ...), custom_call_target="tpu_custom_call" | custom-call | flops 655360000 | bytes 1048576 | tf_op jit(solution)/shard_map/pallas_call | solution.py:92
  24.0 5.4 %all-to-all-start = ((s32[8,1,512]{2,1,0:T(1,128)}), s32[8,1,512]{2,1,0:T(1,128)S(1)}, u32[]{:S(2)}, u32[]{:S(2)}) async-start(s32[8,1,512]{2,1,0:T(1,128)} %all_to_all.6), calls=%async_computation | async-start | bytes 32768 | tf_op jit(solution)/shard_map/all_to_all | solution.py:597
  30.2 4.5 %collective-permute-done.3.refs_3_.refs_1_ = bf16[4,128,512]{2,1,0:T(8,128)(2,1)S(1)} collective-permute-done((bf16[4,128,512]{2,1,0:T(8,128)(2,1)S(1)}, bf16[4,128,512]{2,1,0:T(8,128)(2,1)S(1)}, u32[]{:S(2)}, u32[]{:S(2)}) %collective-permute-start.3) | collective-permute-done | bytes 524320 | tf_op jit(solution)/shard_map/ppermute | solution.py:566
  34.6 1.3 collective-permute-start.5
  36.1 5.2 %shard_map.79 = (bf16[48,256,2048]{2,1,0:T(8,128)(2,1)}, f32[2,1,2048]{2,1,0:T(1,128)S(1)}) custom-call(f32[512,128]{1,0:T(8,128)S(1)} %broadcast_in_dim.57.time_ref, f32[1,1024]{1,0:T(1,128)S(1)} %bitcast.28, f32[1,1024]{1,0:T(1,128)S(1)} %bitcast.24, bf16[48,256,2048]{2,1,0:T(8,128)(2,1)} %get-tuple-element.61.refs_0_), custom_call_target="tpu_custom_call", output_to_operand_aliasing={{0}: (3, {})} | custom-call | flops 1310720000 | bytes 2097152 | tf_op jit(solution)/shard_map/pallas_call | solution.py:92
  41.7 7.3 %shard_map.80 = (bf16[48,256,2048]{2,1,0:T(8,128)(2,1)}, f32[3,1,2048]{2,1,0:T(1,128)S(1)}) custom-call(f32[768,128]{1,0:T(8,128)S(1)} %broadcast_in_dim.55.time_ref, f32[1,1024]{1,0:T(1,128)S(1)} %bitcast.29, f32[1,1024]{1,0:T(1,128)S(1)} %bitcast.25, ...), custom_call_target="tpu_custom_call", output_to_operand_aliasing={{0}: (5, {})} | custom-call | flops 1966080000 | bytes 3145728 | tf_op jit(solution)/shard_map/pallas_call | solution.py:92
  49.1 3.5 %shard_map.78 = (bf16[512,128]{1,0:T(8,128)(2,1)S(1)}, bf16[512,128]{1,0:T(8,128)(2,1)S(1)}, bf16[512,128]{1,0:T(8,128)(2,1)S(1)}, bf16[512,128]{1,0:T(8,128)(2,...) custom-call(s32[4096]{0:T(1024)S(1)} %bitcast.18, ...), custom_call_target="tpu_custom_call" | custom-call | flops 5000000000 | bytes 1048576 | tf_op jit(solution)/shard_map/pallas_call | solution.py:381
  52.6 3.1 %collective-permute-start.6 = (bf16[512,128]{1,0:T(8,128)(2,1)S(1)}, bf16[512,128]{1,0:T(8,128)(2,1)S(1)}, u32[]{:S(2)}, u32[]{:S(2)}) collective-permute-start(bf16[512,128]{1,0:T(8,128)(2,1)S(1)} %get-tuple-element.54), channel_id=1, source_target_pairs={{0,4},{4,0},{8,12},{12,8},{16,20},{20,16},{24,28},{28,24},{1,5},{5... | collective-permute-start | bytes 393224 | tf_op jit(solution)/shard_map/ppermute | solution.py:556
  55.7 2.6 %collective-permute-start.7 = (bf16[512,128]{1,0:T(8,128)(2,1)S(1)}, bf16[512,128]{1,0:T(8,128)(2,1)S(1)}, u32[]{:S(2)}, u32[]{:S(2)}) collective-permute-start(bf16[512,128]{1,0:T(8,128)(2,1)S(1)} %get-tuple-element.55), channel_id=1, source_target_pairs={{0,16},{4,20},{8,24},{12,28},{16,0},{20,4},{24,8},{28,12},{1,17},{... | collective-permute-start | bytes 393224 | tf_op jit(solution)/shard_map/ppermute | solution.py:556
  58.6 2.6 %collective-permute-start.9 = (bf16[512,128]{1,0:T(8,128)(2,1)S(1)}, bf16[512,128]{1,0:T(8,128)(2,1)S(1)}, u32[]{:S(2)}, u32[]{:S(2)}) collective-permute-start(bf16[512,128]{1,0:T(8,128)(2,1)S(1)} %get-tuple-element.57), channel_id=1, source_target_pairs={{0,28},{4,24},{8,20},{12,16},{16,12},{20,8},{24,4},{28,0},{1,29},{... | collective-permute-start | bytes 393224 | tf_op jit(solution)/shard_map/ppermute | solution.py:556
  61.9 5.3 %shard_map.81 = (bf16[48,256,2048]{2,1,0:T(8,128)(2,1)}, f32[2,1,2048]{2,1,0:T(1,128)S(1)}) custom-call(f32[512,128]{1,0:T(8,128)S(1)} %broadcast_in_dim.53.time_ref, f32[1,1024]{1,0:T(1,128)S(1)} %bitcast.30, f32[1,1024]{1,0:T(1,128)S(1)} %bitcast.26, bf16[512,128]{1,0:T(8,128)(2,1)S(1)} %get-tuple-element.53.refs_0_, ...), custom_call_target="tpu_custom_call", output_to_operand_aliasing={{0}: (4, {})} | custom-call | flops 1310720000 | bytes 2097152 | tf_op jit(solution)/shard_map/pallas_call | solution.py:92
  67.1 1.0 collective-permute-start.11
  68.1 1.6 collective-permute-start.12
  69.8 2.9 %collective-permute-done.11.refs_6_ = bf16[512,128]{1,0:T(8,128)(2,1)S(1)} collective-permute-done((bf16[512,128]{1,0:T(8,128)(2,1)S(1)}, bf16[512,128]{1,0:T(8,128)(2,1)S(1)}, u32[]{:S(2)}, u32[]{:S(2)}) %collective-permute-start.11) | collective-permute-done | bytes 131104 | tf_op jit(solution)/shard_map/ppermute | solution.py:556
  72.7 0.9 collective-permute-done.12.refs_7_
  73.6 9.4 %shard_map.82 = (bf16[512,128]{1,0:T(8,128)(2,1)S(1)}, bf16[512,128]{1,0:T(8,128)(2,1)S(1)}, bf16[512,128]{1,0:T(8,128)(2,1)S(1)}, bf16[512,128]{1,0:T(8,128)(2,...) custom-call(s32[8,24]{1,0:T(8,128)S(1)} %get-tuple-element.110.src_r, ...), custom_call_target="tpu_custom_call" | custom-call | flops 10737418240 | bytes 8388608 | tf_op jit(solution)/shard_map/pallas_call | solution.py:216
  83.4 1.6 collective-permute-start.14
  86.0 1.0 collective-permute-start.17
  87.0 1.5 collective-permute-start.18
  88.6 2.9 %collective-permute-start.19 = (bf16[512,128]{1,0:T(8,128)(2,1)S(1)}, bf16[512,128]{1,0:T(8,128)(2,1)S(1)}, u32[]{:S(2)}, u32[]{:S(2)}) collective-permute-start(bf16[512,128]{1,0:T(8,128)(2,1)S(1)} %get-tuple-element.75), channel_id=1, source_target_pairs={{0,28},{4,24},{8,20},{12,16},{16,12},{20,8},{24,4},{28,0},{1,29},{... | collective-permute-start | bytes 393224 | tf_op jit(solution)/shard_map/ppermute | solution.py:556
  91.9 2.3 %collective-permute-done.17.refs_5_ = bf16[512,128]{1,0:T(8,128)(2,1)S(1)} collective-permute-done((bf16[512,128]{1,0:T(8,128)(2,1)S(1)}, bf16[512,128]{1,0:T(8,128)(2,1)S(1)}, u32[]{:S(2)}, u32[]{:S(2)}) %collective-permute-start.17) | collective-permute-done | bytes 131104 | tf_op jit(solution)/shard_map/ppermute | solution.py:556
  94.1 3.4 %shard_map.83.part_ref = f32[4096,128]{1,0:T(8,128)S(1)} custom-call(s32[4096]{0:T(1024)S(1)} %bitcast.19, s32[8]{0:T(128)S(1)} %fusion.4.cnt_ref, s32[2]{0:T(128)S(1)} %pad_add_fusion.where_ref, bf16[4,512,256]{2,1,0:T(8,128)(2,1)S(1)} %copy-done.2, bf16[512,128]{1,0:T(8,128)(2,1)S(1)} %get-tuple-element.68.refs_0_, ...), custom_call_target="tpu_custom_call" | custom-call | flops 6000000000 | bytes 1048576 | tf_op jit(solution)/shard_map/pallas_call | solution.py:353
  97.5 0.9 collective-permute-done.19.refs_7_
  98.4 4.7 %shard_map.84 = (f32[49152,128]{1,0:T(8,128)S(1)}, bf16[512,128]{1,0:T(8,128)(2,1)S(1)}, bf16[512,128]{1,0:T(8,128)(2,1)S(1)}, bf16[512,128]{1,0:T(8,128)(2,1)S(...) custom-call(s32[4096]{0:T(1024)S(1)} %bitcast.20, ...), custom_call_target="tpu_custom_call" | custom-call | flops 7000000000 | bytes 1048576 | tf_op jit(solution)/shard_map/pallas_call | solution.py:438
  103.1 8.3 %copy-done = f32[49152,128]{1,0:T(8,128)} copy-done((f32[49152,128]{1,0:T(8,128)}, f32[49152,128]{1,0:T(8,128)S(1)}, u32[]{:S(2)}) %copy-start) | copy-done | bytes 25165848
  112.2 3.2 %collective-permute-start.21 = (bf16[512,128]{1,0:T(8,128)(2,1)S(1)}, bf16[512,128]{1,0:T(8,128)(2,1)S(1)}, u32[]{:S(2)}, u32[]{:S(2)}) collective-permute-start(bf16[512,128]{1,0:T(8,128)(2,1)S(1)} %get-tuple-element.79), channel_id=1, source_target_pairs={{0,16},{4,20},{8,24},{12,28},{16,0},{20,4},{24,8},{28,12},{1,17},{... | collective-permute-start | bytes 393224 | tf_op jit(solution)/shard_map/ppermute | solution.py:556
  115.8 2.3 %collective-permute-start.23 = (bf16[512,128]{1,0:T(8,128)(2,1)S(1)}, bf16[512,128]{1,0:T(8,128)(2,1)S(1)}, u32[]{:S(2)}, u32[]{:S(2)}) collective-permute-start(bf16[512,128]{1,0:T(8,128)(2,1)S(1)} %get-tuple-element.81), channel_id=1, source_target_pairs={{0,28},{4,24},{8,20},{12,16},{16,12},{20,8},{24,4},{28,0},{1,29},{... | collective-permute-start | bytes 393224 | tf_op jit(solution)/shard_map/ppermute | solution.py:556
  118.2 0.8 collective-permute-start.24
  119.8 4.6 %collective-permute-done.21.refs_2_ = bf16[512,128]{1,0:T(8,128)(2,1)S(1)} collective-permute-done((bf16[512,128]{1,0:T(8,128)(2,1)S(1)}, bf16[512,128]{1,0:T(8,128)(2,1)S(1)}, u32[]{:S(2)}, u32[]{:S(2)}) %collective-permute-start.21) | collective-permute-done | bytes 131104 | tf_op jit(solution)/shard_map/ppermute | solution.py:556
  124.3 2.4 %collective-permute-start.26 = (bf16[512,128]{1,0:T(8,128)(2,1)S(1)}, bf16[512,128]{1,0:T(8,128)(2,1)S(1)}, u32[]{:S(2)}, u32[]{:S(2)}) collective-permute-start(bf16[512,128]{1,0:T(8,128)(2,1)S(1)} %get-tuple-element.84), channel_id=1, source_target_pairs={{0,20},{4,16},{8,28},{12,24},{16,4},{20,0},{24,12},{28,8},{1,21},{... | collective-permute-start | bytes 393224 | tf_op jit(solution)/shard_map/ppermute | solution.py:556
  126.8 2.3 %collective-permute-done.25.refs_6_ = bf16[512,128]{1,0:T(8,128)(2,1)S(1)} collective-permute-done((bf16[512,128]{1,0:T(8,128)(2,1)S(1)}, bf16[512,128]{1,0:T(8,128)(2,1)S(1)}, u32[]{:S(2)}, u32[]{:S(2)}) %collective-permute-start.25) | collective-permute-done | bytes 131104 | tf_op jit(solution)/shard_map/ppermute | solution.py:556
  129.1 1.2 collective-permute-done.26.refs_7_
  130.2 8.7 %shard_map.85 = (bf16[512,128]{1,0:T(8,128)(2,1)S(1)}, bf16[512,128]{1,0:T(8,128)(2,1)S(1)}, bf16[512,128]{1,0:T(8,128)(2,1)S(1)}, bf16[512,128]{1,0:T(8,128)(2,...) custom-call(s32[8,24]{1,0:T(8,128)S(1)} %get-tuple-element.110.src_r, ...), custom_call_target="tpu_custom_call" | custom-call | flops 10737418240 | bytes 8388608 | tf_op jit(solution)/shard_map/pallas_call | solution.py:216
  139.2 2.2 %collective-permute-start.28 = (bf16[512,128]{1,0:T(8,128)(2,1)S(1)}, bf16[512,128]{1,0:T(8,128)(2,1)S(1)}, u32[]{:S(2)}, u32[]{:S(2)}) collective-permute-start(bf16[512,128]{1,0:T(8,128)(2,1)S(1)} %get-tuple-element.87), channel_id=1, source_target_pairs={{0,16},{4,20},{8,24},{12,28},{16,0},{20,4},{24,8},{28,12},{1,17},{... | collective-permute-start | bytes 393224 | tf_op jit(solution)/shard_map/ppermute | solution.py:556
  142.1 1.3 collective-permute-start.31
  144.2 1.2 collective-permute-start.32
  145.4 1.7 %collective-permute-start.33 = (bf16[512,128]{1,0:T(8,128)(2,1)S(1)}, bf16[512,128]{1,0:T(8,128)(2,1)S(1)}, u32[]{:S(2)}, u32[]{:S(2)}) collective-permute-start(bf16[512,128]{1,0:T(8,128)(2,1)S(1)} %get-tuple-element.92), channel_id=1, source_target_pairs={{0,28},{4,24},{8,20},{12,16},{16,12},{20,8},{24,4},{28,0},{1,29},{... | collective-permute-start | bytes 393224 | tf_op jit(solution)/shard_map/ppermute | solution.py:556
  147.1 1.2 collective-permute-done.30.refs_4_
  148.2 2.3 %collective-permute-done.31.refs_5_ = bf16[512,128]{1,0:T(8,128)(2,1)S(1)} collective-permute-done((bf16[512,128]{1,0:T(8,128)(2,1)S(1)}, bf16[512,128]{1,0:T(8,128)(2,1)S(1)}, u32[]{:S(2)}, u32[]{:S(2)}) %collective-permute-start.31) | collective-permute-done | bytes 131104 | tf_op jit(solution)/shard_map/ppermute | solution.py:556
  150.5 8.2 %copy-done.1 = f32[49152,128]{1,0:T(8,128)S(1)} copy-done((f32[49152,128]{1,0:T(8,128)S(1)}, f32[49152,128]{1,0:T(8,128)}, u32[]{:S(2)}) %copy-start.1) | copy-done | bytes 25165848
  158.7 3.4 %shard_map.86.part_ref = f32[4096,128]{1,0:T(8,128)S(1)} custom-call(s32[4096]{0:T(1024)S(1)} %bitcast.21, s32[8]{0:T(128)S(1)} %fusion.4.cnt_ref, s32[2]{0:T(128)S(1)} %pad_add_fusion.where_ref, f32[49152,128]{1,0:T(8,128)S(1)} %copy-done.1, bf16[512,128]{1,0:T(8,128)(2,1)S(1)} %get-tuple-element.85.refs_0_, ...), custom_call_target="tpu_custom_call" | custom-call | flops 6000000000 | bytes 1048576 | tf_op jit(solution)/shard_map/pallas_call | solution.py:353
  162.1 3.2 %shard_map.87 = f32[4,512,256]{2,1,0:T(8,128)} custom-call(s32[4096]{0:T(1024)S(1)} %bitcast.22, s32[8]{0:T(128)S(1)} %fusion.4.cnt_ref, s32[2]{0:T(128)S(1)} %pad_add_fusion.where_ref, f32[4096,128]{1,0:T(8,128)S(1)} %shard_map.86.part_ref, bf16[512,128]{1,0:T(8,128)(2,1)S(1)} %collective-permute-done.32.refs_0_, ...), custom_call_target="tpu_custom_call" | custom-call | flops 4000000000 | bytes 1048576 | tf_op jit(solution)/shard_map/pallas_call | solution.py:480
  (83 shorter events, 14.4 us)
Async XLA Ops:
  0.6 15.9 %collective-permute-start.1 = (bf16[4,128,512]{2,1,0:T(8,128)(2,1)}, bf16[4,128,512]{2,1,0:T(8,128)(2,1)S(1)}, u32[]{:S(2)}, u32[]{:S(2)}) collective-permute-start(bf16[4,128,512]{2,1,0:T(8,128)(2,1)} %own_ref.3), channel_id=1, source_target_pairs={{1,0},{2,1},{3,2},{5,4},{6,5},{7,6},{9,8},{10,9},{11,10},{13,12},{... | collective-permute-start | bytes 1572872 | tf_op jit(solution)/shard_map/ppermute | solution.py:566
  1.9 15.6 %collective-permute-start = (bf16[4,128,512]{2,1,0:T(8,128)(2,1)}, bf16[4,128,512]{2,1,0:T(8,128)(2,1)S(1)}, u32[]{:S(2)}, u32[]{:S(2)}) collective-permute-start(bf16[4,128,512]{2,1,0:T(8,128)(2,1)} %own_ref.3), channel_id=1, source_target_pairs={{0,1},{1,2},{2,3},{4,5},{5,6},{6,7},{8,9},{9,10},{10,11},{12,13},{... | collective-permute-start | bytes 1572872 | tf_op jit(solution)/shard_map/ppermute | solution.py:565
  17.5 12.0 %collective-permute-start.2 = (bf16[4,128,512]{2,1,0:T(8,128)(2,1)S(1)}, bf16[4,128,512]{2,1,0:T(8,128)(2,1)S(1)}, u32[]{:S(2)}, u32[]{:S(2)}) collective-permute-start(bf16[4,128,512]{2,1,0:T(8,128)(2,1)S(1)} %collective-permute-done.refs_0_), channel_id=1, source_target_pairs={{1,2},{2,3},{5,6},{6,7},{9,10},{10,11},{13,14},{14,15},{17,18},{18... | collective-permute-start | bytes 1572872 | tf_op jit(solution)/shard_map/ppermute | solution.py:565
  18.2 16.5 %collective-permute-start.3 = (bf16[4,128,512]{2,1,0:T(8,128)(2,1)S(1)}, bf16[4,128,512]{2,1,0:T(8,128)(2,1)S(1)}, u32[]{:S(2)}, u32[]{:S(2)}) collective-permute-start(bf16[4,128,512]{2,1,0:T(8,128)(2,1)S(1)} %collective-permute-done.1.refs_1_), channel_id=1, source_target_pairs={{1,0},{2,1},{5,4},{6,5},{9,8},{10,9},{13,12},{14,13},{17,16},{18,1... | collective-permute-start | bytes 1572872 | tf_op jit(solution)/shard_map/ppermute | solution.py:566
  24.0 17.2 %all-to-all-start = ((s32[8,1,512]{2,1,0:T(1,128)}), s32[8,1,512]{2,1,0:T(1,128)S(1)}, u32[]{:S(2)}, u32[]{:S(2)}) async-start(s32[8,1,512]{2,1,0:T(1,128)} %all_to_all.6), calls=%async_computation | async-start | bytes 32768 | tf_op jit(solution)/shard_map/all_to_all | solution.py:597
  29.5 19.6 %collective-permute-start.4 = (bf16[4,128,512]{2,1,0:T(8,128)(2,1)S(1)}, bf16[4,128,512]{2,1,0:T(8,128)(2,1)S(1)}, u32[]{:S(2)}, u32[]{:S(2)}) collective-permute-start(bf16[4,128,512]{2,1,0:T(8,128)(2,1)S(1)} %collective-permute-done.2.refs_2_.refs_0_), channel_id=1, source_target_pairs={{2,3},{6,7},{10,11},{14,15},{18,19},{22,23},{26,27},{30,31}} | collective-permute-start | bytes 1572872 | tf_op jit(solution)/shard_map/ppermute | solution.py:565
  34.6 14.4 %collective-permute-start.5 = (bf16[4,128,512]{2,1,0:T(8,128)(2,1)S(1)}, bf16[4,128,512]{2,1,0:T(8,128)(2,1)S(1)}, u32[]{:S(2)}, u32[]{:S(2)}) collective-permute-start(bf16[4,128,512]{2,1,0:T(8,128)(2,1)S(1)} %collective-permute-done.3.refs_3_.refs_1_), channel_id=1, source_target_pairs={{1,0},{5,4},{9,8},{13,12},{17,16},{21,20},{25,24},{29,28}} | collective-permute-start | bytes 1572872 | tf_op jit(solution)/shard_map/ppermute | solution.py:566
  41.7 7.4 %copy-start.2 = (bf16[4,512,256]{2,1,0:T(8,128)(2,1)S(1)}, bf16[4,512,256]{2,1,0:T(8,128)(2,1)}, u32[]{:S(2)}) copy-start(bf16[4,512,256]{2,1,0:T(8,128)(2,1)} %base_ref.3) | copy-start | bytes 3145732
  41.7 7.4 %copy-start.3 = (bf16[4,128,512]{2,1,0:T(8,128)(2,1)S(1)}, bf16[4,128,512]{2,1,0:T(8,128)(2,1)}, u32[]{:S(2)}) copy-start(bf16[4,128,512]{2,1,0:T(8,128)(2,1)} %own_ref.3) | copy-start | bytes 1572868
  41.7 7.4 %copy-start.4 = (s32[4]{0:T(128)S(1)}, s32[4]{0:T(128)}, u32[]{:S(2)}) copy-start(s32[4]{0:T(128)} %count_ref.3) | copy-start | bytes 52
  52.6 14.6 %collective-permute-start.6 = (bf16[512,128]{1,0:T(8,128)(2,1)S(1)}, bf16[512,128]{1,0:T(8,128)(2,1)S(1)}, u32[]{:S(2)}, u32[]{:S(2)}) collective-permute-start(bf16[512,128]{1,0:T(8,128)(2,1)S(1)} %get-tuple-element.54), channel_id=1, source_target_pairs={{0,4},{4,0},{8,12},{12,8},{16,20},{20,16},{24,28},{28,24},{1,5},{5... | collective-permute-start | bytes 393224 | tf_op jit(solution)/shard_map/ppermute | solution.py:556
  55.7 12.4 %collective-permute-start.7 = (bf16[512,128]{1,0:T(8,128)(2,1)S(1)}, bf16[512,128]{1,0:T(8,128)(2,1)S(1)}, u32[]{:S(2)}, u32[]{:S(2)}) collective-permute-start(bf16[512,128]{1,0:T(8,128)(2,1)S(1)} %get-tuple-element.55), channel_id=1, source_target_pairs={{0,16},{4,20},{8,24},{12,28},{16,0},{20,4},{24,8},{28,12},{1,17},{... | collective-permute-start | bytes 393224 | tf_op jit(solution)/shard_map/ppermute | solution.py:556
  58.3 11.4 %collective-permute-start.8 = (bf16[512,128]{1,0:T(8,128)(2,1)S(1)}, bf16[512,128]{1,0:T(8,128)(2,1)S(1)}, u32[]{:S(2)}, u32[]{:S(2)}) collective-permute-start(bf16[512,128]{1,0:T(8,128)(2,1)S(1)} %get-tuple-element.56), channel_id=1, source_target_pairs={{0,24},{4,28},{8,16},{12,20},{16,8},{20,12},{24,0},{28,4},{1,25},{... | collective-permute-start | bytes 393224 | tf_op jit(solution)/shard_map/ppermute | solution.py:556
  58.6 11.1 %collective-permute-start.9 = (bf16[512,128]{1,0:T(8,128)(2,1)S(1)}, bf16[512,128]{1,0:T(8,128)(2,1)S(1)}, u32[]{:S(2)}, u32[]{:S(2)}) collective-permute-start(bf16[512,128]{1,0:T(8,128)(2,1)S(1)} %get-tuple-element.57), channel_id=1, source_target_pairs={{0,28},{4,24},{8,20},{12,16},{16,12},{20,8},{24,4},{28,0},{1,29},{... | collective-permute-start | bytes 393224 | tf_op jit(solution)/shard_map/ppermute | solution.py:556
  61.2 8.5 %collective-permute-start.10 = (bf16[512,128]{1,0:T(8,128)(2,1)S(1)}, bf16[512,128]{1,0:T(8,128)(2,1)S(1)}, u32[]{:S(2)}, u32[]{:S(2)}) collective-permute-start(bf16[512,128]{1,0:T(8,128)(2,1)S(1)} %get-tuple-element.58), channel_id=1, source_target_pairs={{0,8},{4,12},{8,0},{12,4},{16,24},{20,28},{24,16},{28,20},{1,9},{5... | collective-permute-start | bytes 393224 | tf_op jit(solution)/shard_map/ppermute | solution.py:556
  67.1 5.6 %collective-permute-start.11 = (bf16[512,128]{1,0:T(8,128)(2,1)S(1)}, bf16[512,128]{1,0:T(8,128)(2,1)S(1)}, u32[]{:S(2)}, u32[]{:S(2)}) collective-permute-start(bf16[512,128]{1,0:T(8,128)(2,1)S(1)} %get-tuple-element.59), channel_id=1, source_target_pairs={{0,12},{4,8},{8,4},{12,0},{16,28},{20,24},{24,20},{28,16},{1,13},{... | collective-permute-start | bytes 393224 | tf_op jit(solution)/shard_map/ppermute | solution.py:556
  68.1 5.5 %collective-permute-start.12 = (bf16[512,128]{1,0:T(8,128)(2,1)S(1)}, bf16[512,128]{1,0:T(8,128)(2,1)S(1)}, u32[]{:S(2)}, u32[]{:S(2)}) collective-permute-start(bf16[512,128]{1,0:T(8,128)(2,1)S(1)} %get-tuple-element.60), channel_id=1, source_target_pairs={{0,20},{4,16},{8,28},{12,24},{16,4},{20,0},{24,12},{28,8},{1,21},{... | collective-permute-start | bytes 393224 | tf_op jit(solution)/shard_map/ppermute | solution.py:556
  83.0 4.0 %collective-permute-start.13 = (bf16[512,128]{1,0:T(8,128)(2,1)S(1)}, bf16[512,128]{1,0:T(8,128)(2,1)S(1)}, u32[]{:S(2)}, u32[]{:S(2)}) collective-permute-start(bf16[512,128]{1,0:T(8,128)(2,1)S(1)} %get-tuple-element.69), channel_id=1, source_target_pairs={{0,4},{4,0},{8,12},{12,8},{16,20},{20,16},{24,28},{28,24},{1,5},{5... | collective-permute-start | bytes 393224 | tf_op jit(solution)/shard_map/ppermute | solution.py:556
  83.4 5.2 %collective-permute-start.14 = (bf16[512,128]{1,0:T(8,128)(2,1)S(1)}, bf16[512,128]{1,0:T(8,128)(2,1)S(1)}, u32[]{:S(2)}, u32[]{:S(2)}) collective-permute-start(bf16[512,128]{1,0:T(8,128)(2,1)S(1)} %get-tuple-element.70), channel_id=1, source_target_pairs={{0,16},{4,20},{8,24},{12,28},{16,0},{20,4},{24,8},{28,12},{1,17},{... | collective-permute-start | bytes 393224 | tf_op jit(solution)/shard_map/ppermute | solution.py:556
  85.0 6.5 %collective-permute-start.15 = (bf16[512,128]{1,0:T(8,128)(2,1)S(1)}, bf16[512,128]{1,0:T(8,128)(2,1)S(1)}, u32[]{:S(2)}, u32[]{:S(2)}) collective-permute-start(bf16[512,128]{1,0:T(8,128)(2,1)S(1)} %get-tuple-element.71), channel_id=1, source_target_pairs={{0,8},{4,12},{8,0},{12,4},{16,24},{20,28},{24,16},{28,20},{1,9},{5... | collective-permute-start | bytes 393224 | tf_op jit(solution)/shard_map/ppermute | solution.py:556
  85.5 6.3 %collective-permute-start.16 = (bf16[512,128]{1,0:T(8,128)(2,1)S(1)}, bf16[512,128]{1,0:T(8,128)(2,1)S(1)}, u32[]{:S(2)}, u32[]{:S(2)}) collective-permute-start(bf16[512,128]{1,0:T(8,128)(2,1)S(1)} %get-tuple-element.72), channel_id=1, source_target_pairs={{0,20},{4,16},{8,28},{12,24},{16,4},{20,0},{24,12},{28,8},{1,21},{... | collective-permute-start | bytes 393224 | tf_op jit(solution)/shard_map/ppermute | solution.py:556
  86.0 8.1 %collective-permute-start.17 = (bf16[512,128]{1,0:T(8,128)(2,1)S(1)}, bf16[512,128]{1,0:T(8,128)(2,1)S(1)}, u32[]{:S(2)}, u32[]{:S(2)}) collective-permute-start(bf16[512,128]{1,0:T(8,128)(2,1)S(1)} %get-tuple-element.73), channel_id=1, source_target_pairs={{0,12},{4,8},{8,4},{12,0},{16,28},{20,24},{24,20},{28,16},{1,13},{... | collective-permute-start | bytes 393224 | tf_op jit(solution)/shard_map/ppermute | solution.py:556
  87.0 10.5 %collective-permute-start.18 = (bf16[512,128]{1,0:T(8,128)(2,1)S(1)}, bf16[512,128]{1,0:T(8,128)(2,1)S(1)}, u32[]{:S(2)}, u32[]{:S(2)}) collective-permute-start(bf16[512,128]{1,0:T(8,128)(2,1)S(1)} %get-tuple-element.74), channel_id=1, source_target_pairs={{0,24},{4,28},{8,16},{12,20},{16,8},{20,12},{24,0},{28,4},{1,25},{... | collective-permute-start | bytes 393224 | tf_op jit(solution)/shard_map/ppermute | solution.py:556
  88.6 9.8 %collective-permute-start.19 = (bf16[512,128]{1,0:T(8,128)(2,1)S(1)}, bf16[512,128]{1,0:T(8,128)(2,1)S(1)}, u32[]{:S(2)}, u32[]{:S(2)}) collective-permute-start(bf16[512,128]{1,0:T(8,128)(2,1)S(1)} %get-tuple-element.75), channel_id=1, source_target_pairs={{0,28},{4,24},{8,20},{12,16},{16,12},{20,8},{24,4},{28,0},{1,29},{... | collective-permute-start | bytes 393224 | tf_op jit(solution)/shard_map/ppermute | solution.py:556
  103.1 8.3 %copy-start = (f32[49152,128]{1,0:T(8,128)}, f32[49152,128]{1,0:T(8,128)S(1)}, u32[]{:S(2)}) copy-start(f32[49152,128]{1,0:T(8,128)S(1)} %get-tuple-element.76.base_ref) | copy-start | bytes 75497472
  111.4 7.6 %collective-permute-start.20 = (bf16[512,128]{1,0:T(8,128)(2,1)S(1)}, bf16[512,128]{1,0:T(8,128)(2,1)S(1)}, u32[]{:S(2)}, u32[]{:S(2)}) collective-permute-start(bf16[512,128]{1,0:T(8,128)(2,1)S(1)} %get-tuple-element.78), channel_id=1, source_target_pairs={{0,4},{4,0},{8,12},{12,8},{16,20},{20,16},{24,28},{28,24},{1,5},{5... | collective-permute-start | bytes 393224 | tf_op jit(solution)/shard_map/ppermute | solution.py:556
  112.2 12.2 %collective-permute-start.21 = (bf16[512,128]{1,0:T(8,128)(2,1)S(1)}, bf16[512,128]{1,0:T(8,128)(2,1)S(1)}, u32[]{:S(2)}, u32[]{:S(2)}) collective-permute-start(bf16[512,128]{1,0:T(8,128)(2,1)S(1)} %get-tuple-element.79), channel_id=1, source_target_pairs={{0,16},{4,20},{8,24},{12,28},{16,0},{20,4},{24,8},{28,12},{1,17},{... | collective-permute-start | bytes 393224 | tf_op jit(solution)/shard_map/ppermute | solution.py:556
  115.4 11.4 %collective-permute-start.22 = (bf16[512,128]{1,0:T(8,128)(2,1)S(1)}, bf16[512,128]{1,0:T(8,128)(2,1)S(1)}, u32[]{:S(2)}, u32[]{:S(2)}) collective-permute-start(bf16[512,128]{1,0:T(8,128)(2,1)S(1)} %get-tuple-element.80), channel_id=1, source_target_pairs={{0,24},{4,28},{8,16},{12,20},{16,8},{20,12},{24,0},{28,4},{1,25},{... | collective-permute-start | bytes 393224 | tf_op jit(solution)/shard_map/ppermute | solution.py:556
  115.8 10.9 %collective-permute-start.23 = (bf16[512,128]{1,0:T(8,128)(2,1)S(1)}, bf16[512,128]{1,0:T(8,128)(2,1)S(1)}, u32[]{:S(2)}, u32[]{:S(2)}) collective-permute-start(bf16[512,128]{1,0:T(8,128)(2,1)S(1)} %get-tuple-element.81), channel_id=1, source_target_pairs={{0,28},{4,24},{8,20},{12,16},{16,12},{20,8},{24,4},{28,0},{1,29},{... | collective-permute-start | bytes 393224 | tf_op jit(solution)/shard_map/ppermute | solution.py:556
  118.2 8.6 %collective-permute-start.24 = (bf16[512,128]{1,0:T(8,128)(2,1)S(1)}, bf16[512,128]{1,0:T(8,128)(2,1)S(1)}, u32[]{:S(2)}, u32[]{:S(2)}) collective-permute-start(bf16[512,128]{1,0:T(8,128)(2,1)S(1)} %get-tuple-element.82), channel_id=1, source_target_pairs={{0,8},{4,12},{8,0},{12,4},{16,24},{20,28},{24,16},{28,20},{1,9},{5... | collective-permute-start | bytes 393224 | tf_op jit(solution)/shard_map/ppermute | solution.py:556
  119.0 10.1 %collective-permute-start.25 = (bf16[512,128]{1,0:T(8,128)(2,1)S(1)}, bf16[512,128]{1,0:T(8,128)(2,1)S(1)}, u32[]{:S(2)}, u32[]{:S(2)}) collective-permute-start(bf16[512,128]{1,0:T(8,128)(2,1)S(1)} %get-tuple-element.83), channel_id=1, source_target_pairs={{0,12},{4,8},{8,4},{12,0},{16,28},{20,24},{24,20},{28,16},{1,13},{... | collective-permute-start | bytes 393224 | tf_op jit(solution)/shard_map/ppermute | solution.py:556
  124.3 5.9 %collective-permute-start.26 = (bf16[512,128]{1,0:T(8,128)(2,1)S(1)}, bf16[512,128]{1,0:T(8,128)(2,1)S(1)}, u32[]{:S(2)}, u32[]{:S(2)}) collective-permute-start(bf16[512,128]{1,0:T(8,128)(2,1)S(1)} %get-tuple-element.84), channel_id=1, source_target_pairs={{0,20},{4,16},{8,28},{12,24},{16,4},{20,0},{24,12},{28,8},{1,21},{... | collective-permute-start | bytes 393224 | tf_op jit(solution)/shard_map/ppermute | solution.py:556
  138.9 5.2 %collective-permute-start.27 = (bf16[512,128]{1,0:T(8,128)(2,1)S(1)}, bf16[512,128]{1,0:T(8,128)(2,1)S(1)}, u32[]{:S(2)}, u32[]{:S(2)}) collective-permute-start(bf16[512,128]{1,0:T(8,128)(2,1)S(1)} %get-tuple-element.86), channel_id=1, source_target_pairs={{0,4},{4,0},{8,12},{12,8},{16,20},{20,16},{24,28},{28,24},{1,5},{5... | collective-permute-start | bytes 393224 | tf_op jit(solution)/shard_map/ppermute | solution.py:556
  139.2 6.2 %collective-permute-start.28 = (bf16[512,128]{1,0:T(8,128)(2,1)S(1)}, bf16[512,128]{1,0:T(8,128)(2,1)S(1)}, u32[]{:S(2)}, u32[]{:S(2)}) collective-permute-start(bf16[512,128]{1,0:T(8,128)(2,1)S(1)} %get-tuple-element.87), channel_id=1, source_target_pairs={{0,16},{4,20},{8,24},{12,28},{16,0},{20,4},{24,8},{28,12},{1,17},{... | collective-permute-start | bytes 393224 | tf_op jit(solution)/shard_map/ppermute | solution.py:556
  141.4 5.7 %collective-permute-start.29 = (bf16[512,128]{1,0:T(8,128)(2,1)S(1)}, bf16[512,128]{1,0:T(8,128)(2,1)S(1)}, u32[]{:S(2)}, u32[]{:S(2)}) collective-permute-start(bf16[512,128]{1,0:T(8,128)(2,1)S(1)} %get-tuple-element.88), channel_id=1, source_target_pairs={{0,8},{4,12},{8,0},{12,4},{16,24},{20,28},{24,16},{28,20},{1,9},{5... | collective-permute-start | bytes 393224 | tf_op jit(solution)/shard_map/ppermute | solution.py:556
  141.4 6.8 %collective-permute-start.30 = (bf16[512,128]{1,0:T(8,128)(2,1)S(1)}, bf16[512,128]{1,0:T(8,128)(2,1)S(1)}, u32[]{:S(2)}, u32[]{:S(2)}) collective-permute-start(bf16[512,128]{1,0:T(8,128)(2,1)S(1)} %get-tuple-element.89), channel_id=1, source_target_pairs={{0,20},{4,16},{8,28},{12,24},{16,4},{20,0},{24,12},{28,8},{1,21},{... | collective-permute-start | bytes 393224 | tf_op jit(solution)/shard_map/ppermute | solution.py:556
  142.1 8.4 %collective-permute-start.31 = (bf16[512,128]{1,0:T(8,128)(2,1)S(1)}, bf16[512,128]{1,0:T(8,128)(2,1)S(1)}, u32[]{:S(2)}, u32[]{:S(2)}) collective-permute-start(bf16[512,128]{1,0:T(8,128)(2,1)S(1)} %get-tuple-element.90), channel_id=1, source_target_pairs={{0,12},{4,8},{8,4},{12,0},{16,28},{20,24},{24,20},{28,16},{1,13},{... | collective-permute-start | bytes 393224 | tf_op jit(solution)/shard_map/ppermute | solution.py:556
  144.2 17.9 %collective-permute-start.32 = (bf16[512,128]{1,0:T(8,128)(2,1)S(1)}, bf16[512,128]{1,0:T(8,128)(2,1)S(1)}, u32[]{:S(2)}, u32[]{:S(2)}) collective-permute-start(bf16[512,128]{1,0:T(8,128)(2,1)S(1)} %get-tuple-element.91), channel_id=1, source_target_pairs={{0,24},{4,28},{8,16},{12,20},{16,8},{20,12},{24,0},{28,4},{1,25},{... | collective-permute-start | bytes 393224 | tf_op jit(solution)/shard_map/ppermute | solution.py:556
  145.4 16.7 %collective-permute-start.33 = (bf16[512,128]{1,0:T(8,128)(2,1)S(1)}, bf16[512,128]{1,0:T(8,128)(2,1)S(1)}, u32[]{:S(2)}, u32[]{:S(2)}) collective-permute-start(bf16[512,128]{1,0:T(8,128)(2,1)S(1)} %get-tuple-element.92), channel_id=1, source_target_pairs={{0,28},{4,24},{8,20},{12,16},{16,12},{20,8},{24,4},{28,0},{1,29},{... | collective-permute-start | bytes 393224 | tf_op jit(solution)/shard_map/ppermute | solution.py:556
  150.5 8.2 %copy-start.1 = (f32[49152,128]{1,0:T(8,128)S(1)}, f32[49152,128]{1,0:T(8,128)}, u32[]{:S(2)}) copy-start(f32[49152,128]{1,0:T(8,128)} %copy-done) | copy-start | bytes 75497472

commit v9 on v8

--- a/solution.py
+++ b/solution.py
@@ -13,6 +13,7 @@
 LATE_STREAMS = 2
 STEP = 16
 BETA = 2.0
+ROUND = 1.5 * 2.0 ** 23
 RIDGE = 1.0
 MIB = 1024 * 1024
 BASIS_VMEM = 8 * MIB
@@ -21,12 +22,11 @@
 PICK_VMEM = 12 * MIB
 LATE_PICK_VMEM = 18 * MIB
 LATE_VMEM = 12 * MIB
-BASIS_CALLS = (1, 2, 3, 2)
+BASIS_CALLS = (1, 2, 2, 3)
 UNROLL = 32
 PICK_UNROLL = 16
 SUB = 8
-HBM_ROWS = 24 * 1024 * 1024 // 512
-HBM_PLANS = 48
+HBM_SPARE = 32
 COST_US = 10 ** 9
 
 COS_POLY = (1.0, -19.73920440673828, 64.9391098022461, -85.4500503540039, 60.16689682006836,
@@ -47,11 +47,11 @@
     return acc
 
 
-def basis_kernel(time_ref, period_ref, inverse_ref, *refs):
-    basis_ref, norm_ref = refs[-2:]
+def basis_kernel(after, time_ref, period_ref, inverse_ref, *refs):
+    basis_ref, norm_ref = refs[after:]
     obs = time_ref.shape[0]
     nper = period_ref.shape[1]
-    rows = 32
+    rows = 64
     for chunk in range(nper // 128):
         lanes = pl.ds(chunk * 128, 128)
         sines = pl.ds(nper + chunk * 128, 128)
@@ -61,7 +61,7 @@
         def step(index, sums):
             at = pl.ds(pl.multiple_of(index * rows, rows), rows)
             time = time_ref[at, :]
-            turns = jnp.round(time * inverse)
+            turns = (time * inverse + ROUND) - ROUND
             part = (time - turns * period) * inverse
             square = part * part
             cosine = horner(COS_POLY, square).astype(jnp.bfloat16)
@@ -81,36 +81,34 @@
         norm_ref[0, :, sines] = 1.0 / (jnp.sum(total_s, axis=0, keepdims=True) + RIDGE)
 
 
-def make_basis(times, periods, first, count, held, after):
+def make_basis(times, periods, after):
     sched_dev, obs = times.shape
     nper = periods.shape[0]
     wide = jnp.broadcast_to(
-        times[first:first + count].astype(jnp.float32).reshape(-1, 1), (count * obs, SRC_GROUP)
+        times.astype(jnp.float32).reshape(-1, 1), (sched_dev * obs, SRC_GROUP)
     )
     period = periods.astype(jnp.float32)[None, :]
-    others = after + ([] if held is None else [held])
     return pl.pallas_call(
-        basis_kernel,
-        grid=(count,),
+        functools.partial(basis_kernel, len(after)),
+        grid=(sched_dev,),
         in_specs=[
             pl.BlockSpec((obs, SRC_GROUP), lambda j: (j, 0)),
             pl.BlockSpec((1, nper), lambda j: (0, 0)),
             pl.BlockSpec((1, nper), lambda j: (0, 0)),
-        ] + [ANY] * len(others),
+        ] + [ANY] * len(after),
         out_specs=[
-            pl.BlockSpec((1, obs, 2 * nper), lambda j: (first + j, 0, 0)),
+            pl.BlockSpec((1, obs, 2 * nper), lambda j: (j, 0, 0)),
             pl.BlockSpec((1, 1, 2 * nper), lambda j: (j, 0, 0)),
         ],
         out_shape=[
-            jax.ShapeDtypeStruct((max(HBM_PLANS, sched_dev), obs, 2 * nper), jnp.bfloat16),
-            jax.ShapeDtypeStruct((count, 1, 2 * nper), jnp.float32),
+            jax.ShapeDtypeStruct((sched_dev, obs, 2 * nper), jnp.bfloat16),
+            jax.ShapeDtypeStruct((sched_dev, 1, 2 * nper), jnp.float32),
         ],
-        input_output_aliases={} if held is None else {2 + len(others): 0},
         compiler_params=pltpu.CompilerParams(vmem_limit_bytes=BASIS_VMEM),
         cost_estimate=pl.CostEstimate(
-            flops=count * obs * nper * 2500, bytes_accessed=count * obs * nper * 4, transcendentals=0
+            flops=sched_dev * obs * nper * 8000, bytes_accessed=sched_dev * obs * nper * 4, transcendentals=0
         ),
-    )(wide, period, 1.0 / period, *others)
+    )(wide, period, 1.0 / period, *after)
 
 
 def fit_kernel(order, src_ref, dst_ref, *refs):
@@ -123,7 +121,8 @@
 
     tm_count = len(order)
     arrived = dict(zip(order, take(tm_count)))
-    all_ref, norm_ref = take(2)
+    parts = take(len(BASIS_CALLS))
+    (norm_ref,) = take(1)
     outs = take(tm_count)
     score_ref, basis_ref, sems, rows_ref, back_ref = take(5)
     slots = [take(4), take(4)]
@@ -132,9 +131,11 @@
     capacity, width = arrived[0].shape
     spaced = capacity + STEP
     steps = src_ref.shape[1]
+    held = [(part, plan) for part, count in zip(parts, BASIS_CALLS) for plan in range(count)]
 
     def basis_copy(plan):
-        return pltpu.make_async_copy(all_ref.at[plan], basis_ref.at[plan], sems.at[plan])
+        part, index = held[plan]
+        return pltpu.make_async_copy(part.at[index], basis_ref.at[plan], sems.at[plan])
 
     for plan in range(plans):
         basis_copy(plan).start()
@@ -199,10 +200,10 @@
         outs[owner][...] = back_ref[pl.ds(owner * spaced, capacity), :].astype(jnp.bfloat16)
 
 
-def fit_plans(tables, arrived, basis, norms):
+def fit_plans(tables, arrived, parts, norms):
     tm_count = len(arrived)
     order = [0] + ask_order(tm_count)
-    _, obs, twice = basis.shape
+    _, obs, twice = parts[0].shape
     sched_dev = norms.shape[0]
     capacity, width = arrived[0].shape
     work = sched_dev * obs * twice * width
@@ -215,7 +216,7 @@
     ]
     *models, score = pl.pallas_call(
         functools.partial(fit_kernel, order),
-        in_specs=[SMEM, SMEM] + [VMEM] * tm_count + [ANY, VMEM],
+        in_specs=[SMEM, SMEM] + [VMEM] * tm_count + [ANY] * len(parts) + [VMEM],
         out_specs=[VMEM] * (tm_count + 1),
         out_shape=[jax.ShapeDtypeStruct((capacity, width), jnp.bfloat16)] * tm_count
         + [jax.ShapeDtypeStruct((sched_dev, width, 1), jnp.float32)],
@@ -227,7 +228,7 @@
         ] + slot + slot,
         compiler_params=pltpu.CompilerParams(vmem_limit_bytes=FIT_VMEM),
         cost_estimate=pl.CostEstimate(flops=20 * work, bytes_accessed=sched_dev * obs * twice * 2, transcendentals=0),
-    )(*tables, *[arrived[owner] for owner in order], basis, norms)
+    )(*tables, *[arrived[owner] for owner in order], *parts, norms)
     return models, score
 
 
@@ -327,7 +328,7 @@
         held_ref, sem = refs.pop(0), refs.pop(0)
         copy = pltpu.make_async_copy(base_ref.at[pl.ds(0, held_ref.shape[0]), :], held_ref, sem)
         copy.start()
-    add_rows(where_ref[0], asked_ref, cnt_ref, owners, returned, rows_ref, refs, not table_base)
+    add_rows(where_ref[0], asked_ref, cnt_ref, owners, returned, rows_ref, refs, True)
     if table_base:
         copy.wait()
         out_ref[...] = held_ref[...] - placed_at(refs, pl.ds(0, out_ref.shape[0]))
@@ -346,16 +347,13 @@
     table_base = base.ndim == 2
     capacity = returned[0].shape[0]
     sums = [pltpu.VMEM((rows + 8, SRC_GROUP), jnp.float32)] * STREAMS
-    shape = (len(owners) * capacity, SRC_GROUP)
-    if not table_base:
-        shape = (shape[0] // SUB, SUB, SRC_GROUP)
     held = [pltpu.VMEM((rows, SRC_GROUP), jnp.float32), pltpu.SemaphoreType.DMA(())] if table_base else []
     return pl.pallas_call(
         functools.partial(early_kernel, owners, table_base),
         in_specs=[SMEM] * 3 + [HBM if table_base else VMEM] + [VMEM] * len(owners),
         out_specs=VMEM,
         out_shape=jax.ShapeDtypeStruct((rows, SRC_GROUP), jnp.float32),
-        scratch_shapes=[pltpu.VMEM(shape, jnp.float32)] + held + sums,
+        scratch_shapes=[pltpu.VMEM((len(owners) * capacity // SUB, SUB, SRC_GROUP), jnp.float32)] + held + sums,
         compiler_params=pltpu.CompilerParams(vmem_limit_bytes=EARLY_VMEM),
         cost_estimate=pl.CostEstimate(flops=6 * COST_US, bytes_accessed=1 << 20, transcendentals=0),
     )(asked, cnt, where, base, *[returned[owner] for owner in owners])
@@ -439,7 +437,7 @@
         functools.partial(late_pick_kernel, tm_count, len(attitude) - 1, owners),
         in_specs=[SMEM] * 4 + [VMEM] + [ANY] * len(attitude) + [VMEM] * len(owners),
         out_specs=[HBM] + [VMEM] * tm_count,
-        out_shape=[jax.ShapeDtypeStruct((max(HBM_ROWS, rows), SRC_GROUP), jnp.float32)]
+        out_shape=[jax.ShapeDtypeStruct((HBM_SPARE * rows, SRC_GROUP), jnp.float32)]
         + [jax.ShapeDtypeStruct((capacity, SRC_GROUP), jnp.bfloat16)] * tm_count,
         scratch_shapes=[
             pltpu.VMEM((seg_dev, slots, slots), jnp.bfloat16),
@@ -580,25 +578,22 @@
         sched_seg, sched_slot, seg_dev, slots, column_blocks, tm_count, capacity
     )
     wanted = wanted.reshape(tm_count, capacity)
-    basis, norms = None, []
+    made = []
     asked = None
 
     def basis_part(after):
-        nonlocal basis
-        first, count = sum(BASIS_CALLS[:len(norms)]), BASIS_CALLS[len(norms)]
-        basis, norm = make_basis(times, periods, first, count, basis, after)
-        norms.append(norm)
+        first, count = sum(BASIS_CALLS[:len(made)]), BASIS_CALLS[len(made)]
+        made.append(make_basis(times[first:first + count], periods, after))
 
     def first_hop(right, left):
         nonlocal asked
-        held, right, left = lax.optimization_barrier((wanted, right, left))
         basis_part([right, left])
-        held, _ = lax.optimization_barrier((held, norms[0]))
+        held, _ = lax.optimization_barrier((wanted, made[0][1]))
         asked = lax.all_to_all(held, "tm", split_axis=0, concat_axis=0, tiled=True)
-        basis_part([])
         return right, left
 
     def second_hop(right, left):
+        basis_part([right, left])
         basis_part([right, left])
         return right, left
 
@@ -613,9 +608,10 @@
     base = residuals
     picked = pick_rows(scalars, base, pieces, rows)
     basis_part([picked[0]])
+    parts, norms = zip(*made)
     norms = jnp.concatenate(norms)
     for iteration in range(ITERS):
-        models, score = fit_plans(tables, exchange(picked), basis, norms)
+        models, score = fit_plans(tables, exchange(picked), parts, norms)
         returned = exchange(models)
         base = place_early(scalars, near, base, returned, rows)
         if iteration < ITERS - 1:

time: 168 us -> 147 us (0.88)
  local copies, waits for them, and re-layouts: 17.6 us -> 2.14 us
  waiting for transfers between devices: 26.5 us -> 33 us
  Pallas kernels: 57 us -> 51.2 us
  starting transfers between devices: 53.6 us -> 48.9 us
    unnamed x17, local copies, waits for them, and re-layouts: 16.5 us -> 1.03 us
    pallas_call x4, Pallas kernels: 20.8 us -> 14.3 us  [make_basis(): pl.pallas_call(functools.partial(basis_kernel, len(after)), grid=(sched_d...]
    ppermute x28, starting transfers between devices: 38.2 us -> 33.8 us  [exchange(): lax.ppermute(blocks[step], 'tm', [(i, i ^ step) for i in range(count)])]
    all_to_all x1, waiting for transfers between devices: 0.01 us -> 4.02 us  [first_hop(): asked = lax.all_to_all(held, 'tm', split_axis=0, concat_axis=0, tiled=True)]
    ppermute x3, waiting for transfers between devices: 6.53 us -> 9.85 us  [pass_along(): lax.ppermute(left, 'sky', [(i, i - 1) for i in range(1, count - hop + 1)])]
  transfers between devices with their start and end apart: 35 -> 35, of which waited for: 14 -> 15; matrix products, arithmetic and copies ran while one was open for 6% -> 7% of each run, Pallas kernels for 17% -> 15%
where the time goes in v9:
time: 147 us; the launch traced here: 146 us
  Pallas kernels  51.2 us (35%)
  starting transfers between devices  48.9 us (33%)
  waiting for transfers between devices  33 us (22%)
  other arithmetic  9.49 us (6%)
  local copies, waits for them, and re-layouts  2.14 us (1%)
    ppermute x28, starting transfers between devices, exchange(): lax.ppermute(blocks[step], 'tm', [(i, i ^ step) for i in range(count)])  33.8 us
    ppermute x28, waiting for transfers between devices, exchange(): lax.ppermute(blocks[step], 'tm', [(i, i ^ step) for i in range(count)])  19.1 us
    pallas_call x2, Pallas kernels, fit_plans(): pl.pallas_call(functools.partial(fit_kernel, order), in_specs=[SMEM, SMEM...  16.7 us
    pallas_call x4, Pallas kernels, make_basis(): pl.pallas_call(functools.partial(basis_kernel, len(after)), grid=(sched_d...  14.3 us
    ppermute x3, waiting for transfers between devices, pass_along(): lax.ppermute(left, 'sky', [(i, i - 1) for i in range(1, count - hop + 1)])  9.85 us
    pallas_call x2, Pallas kernels, place_early(): pl.pallas_call(functools.partial(early_kernel, owners, table_base), in_sp...  7.94 us
    ppermute x3, starting transfers between devices, pass_along(): lax.ppermute(right, 'sky', [(i, i + 1) for i in range(hop - 1, count - 1)])  6.08 us
    all_to_all x1, starting transfers between devices, first_hop(): asked = lax.all_to_all(held, 'tm', split_axis=0, concat_axis=0, tiled=True)  5.1 us
  transfers between devices with their start and end apart: 35, of which 15 were waited for; matrix products, arithmetic and copies ran while one was open for 7% of the time, Pallas kernels for 15%

profile of v9, /device:TPU:1, one launch (start us, length us, event | category | flops | bytes accessed | tf_op | source)
XLA Modules:
  0.0 145.9 jit_solution(11039920264914790691)
XLA Ops:
  0.6 1.3 collective-permute-start.1
  1.9 4.7 %collective-permute-start = (bf16[4,128,512]{2,1,0:T(8,128)(2,1)}, bf16[4,128,512]{2,1,0:T(8,128)(2,1)S(1)}, u32[]{:S(2)}, u32[]{:S(2)}) collective-permute-start(bf16[4,128,512]{2,1,0:T(8,128)(2,1)} %own_ref.3), channel_id=1, source_target_pairs={{0,1},{1,2},{2,3},{4,5},{5,6},{6,7},{8,9},{9,10},{10,11},{12,13},{... | collective-permute-start | bytes 1572872 | tf_op jit(solution)/shard_map/ppermute | solution.py:563
  10.3 0.8 fusion.18
  11.6 3.4 %select_reduce_fusion = s32[4096]{0:T(1024)S(1)} fusion(s32[2048]{0:T(1024)S(1)} %bitcast.34, s32[2048]{0:T(1024)S(1)} %bitcast.33), kind=kLoop, calls=%fused_computation | loop fusion | flops 25161728 | bytes 32768 | tf_op jit(solution)/shard_map/reduce_sum | solution.py:518
  15.2 1.3 collective-permute-done.1.refs_1_
  16.5 1.3 collective-permute-start.3
  18.6 1.8 %shard_map.77 = (bf16[1,256,2048]{2,1,0:T(8,128)(2,1)S(1)}, f32[1,1,2048]{2,1,0:T(1,128)S(1)}) custom-call(f32[256,128]{1,0:T(8,128)S(1)} %broadcast_in_dim.50.time_ref, f32[1,1024]{1,0:T(1,128)S(1)} %bitcast.27, f32[1,1024]{1,0:T(1,128)S(1)} %bitcast.23, bf16[4,128,512]{2,1,0:T(8,128)(2,1)S(1)} %collective-permute-done.refs_0_, ...), custom_call_target="tpu_custom_call" | custom-call | flops 2097152000 | bytes 1048576 | tf_op jit(solution)/shard_map/pallas_call | solution.py:91
  20.4 1.0 copy-done.3
  22.0 5.1 %all-to-all-start = ((s32[8,1,512]{2,1,0:T(1,128)}), s32[8,1,512]{2,1,0:T(1,128)S(1)}, u32[]{:S(2)}, u32[]{:S(2)}) async-start(s32[8,1,512]{2,1,0:T(1,128)} %all_to_all.6), calls=%async_computation | async-start | bytes 32768 | tf_op jit(solution)/shard_map/all_to_all | solution.py:592
  27.1 4.0 %all-to-all-done = s32[8,1,512]{2,1,0:T(1,128)S(1)} async-done(((s32[8,1,512]{2,1,0:T(1,128)}), s32[8,1,512]{2,1,0:T(1,128)S(1)}, u32[]{:S(2)}, u32[]{:S(2)}) %all-to-all-start) | async-done | bytes 16416 | tf_op jit(solution)/shard_map/all_to_all | solution.py:592
  31.4 1.3 collective-permute-start.5
  33.5 3.6 %shard_map.80 = (bf16[2,256,2048]{2,1,0:T(8,128)(2,1)S(1)}, f32[2,1,2048]{2,1,0:T(1,128)S(1)}) custom-call(f32[512,128]{1,0:T(8,128)S(1)} %broadcast_in_dim.55.time_ref, f32[1,1024]{1,0:T(1,128)S(1)} %bitcast.28, f32[1,1024]{1,0:T(1,128)S(1)} %bitcast.24, bf16[4,128,512]{2,1,0:T(8,128)(2,1)S(1)} %collective-permute-done.2.refs_2_.refs_0_, ...), custom_call_target="tpu_custom_call" | custom-call | flops 4194304000 | bytes 2097152 | tf_op jit(solution)/shard_map/pallas_call | solution.py:91
  37.2 3.6 %shard_map.79 = (bf16[2,256,2048]{2,1,0:T(8,128)(2,1)S(1)}, f32[2,1,2048]{2,1,0:T(1,128)S(1)}) custom-call(f32[512,128]{1,0:T(8,128)S(1)} %broadcast_in_dim.53.time_ref, f32[1,1024]{1,0:T(1,128)S(1)} %bitcast.29, f32[1,1024]{1,0:T(1,128)S(1)} %bitcast.25, bf16[4,128,512]{2,1,0:T(8,128)(2,1)S(1)} %collective-permute-done.2.refs_2_.refs_0_, ...), custom_call_target="tpu_custom_call" | custom-call | flops 4194304000 | bytes 2097152 | tf_op jit(solution)/shard_map/pallas_call | solution.py:91
  40.8 8.6 %collective-permute-done.5.refs_5_ = bf16[4,128,512]{2,1,0:T(8,128)(2,1)S(1)} collective-permute-done((bf16[4,128,512]{2,1,0:T(8,128)(2,1)S(1)}, bf16[4,128,512]{2,1,0:T(8,128)(2,1)S(1)}, u32[]{:S(2)}, u32[]{:S(2)}) %collective-permute-start.5) | collective-permute-done | bytes 524320 | tf_op jit(solution)/shard_map/ppermute | solution.py:564
  49.4 4.1 %shard_map.78 = (bf16[512,128]{1,0:T(8,128)(2,1)S(1)}, bf16[512,128]{1,0:T(8,128)(2,1)S(1)}, bf16[512,128]{1,0:T(8,128)(2,1)S(1)}, bf16[512,128]{1,0:T(8,128)(2,...) custom-call(s32[4096]{0:T(1024)S(1)} %bitcast.18, ...), custom_call_target="tpu_custom_call" | custom-call | flops 5000000000 | bytes 1048576 | tf_op jit(solution)/shard_map/pallas_call | solution.py:379
  53.5 1.2 collective-permute-start.6
  54.7 1.2 collective-permute-start.7
  56.5 2.7 %collective-permute-start.9 = (bf16[512,128]{1,0:T(8,128)(2,1)S(1)}, bf16[512,128]{1,0:T(8,128)(2,1)S(1)}, u32[]{:S(2)}, u32[]{:S(2)}) collective-permute-start(bf16[512,128]{1,0:T(8,128)(2,1)S(1)} %get-tuple-element.51), channel_id=1, source_target_pairs={{0,28},{4,24},{8,20},{12,16},{16,12},{20,8},{24,4},{28,0},{1,29},{... | collective-permute-start | bytes 393224 | tf_op jit(solution)/shard_map/ppermute | solution.py:554
  59.6 5.3 %shard_map.81 = (bf16[3,256,2048]{2,1,0:T(8,128)(2,1)S(1)}, f32[3,1,2048]{2,1,0:T(1,128)S(1)}) custom-call(f32[768,128]{1,0:T(8,128)S(1)} %broadcast_in_dim.57.time_ref, f32[1,1024]{1,0:T(1,128)S(1)} %bitcast.30, f32[1,1024]{1,0:T(1,128)S(1)} %bitcast.26, bf16[512,128]{1,0:T(8,128)(2,1)S(1)} %get-tuple-element.47.refs_0_), custom_call_target="tpu_custom_call" | custom-call | flops 6291456000 | bytes 3145728 | tf_op jit(solution)/shard_map/pallas_call | solution.py:91
  65.0 0.9 collective-permute-start.11
  65.9 1.4 collective-permute-start.12
  67.4 3.3 %collective-permute-done.11.refs_6_ = bf16[512,128]{1,0:T(8,128)(2,1)S(1)} collective-permute-done((bf16[512,128]{1,0:T(8,128)(2,1)S(1)}, bf16[512,128]{1,0:T(8,128)(2,1)S(1)}, u32[]{:S(2)}, u32[]{:S(2)}) %collective-permute-start.11) | collective-permute-done | bytes 131104 | tf_op jit(solution)/shard_map/ppermute | solution.py:554
  70.6 1.3 collective-permute-done.12.refs_7_
  72.0 8.7 %shard_map.82 = (bf16[512,128]{1,0:T(8,128)(2,1)S(1)}, bf16[512,128]{1,0:T(8,128)(2,1)S(1)}, bf16[512,128]{1,0:T(8,128)(2,1)S(1)}, bf16[512,128]{1,0:T(8,128)(2,...) custom-call(s32[8,24]{1,0:T(8,128)S(1)} %get-tuple-element.104.src_r, ...), custom_call_target="tpu_custom_call" | custom-call | flops 10737418240 | bytes 8388608 | tf_op jit(solution)/shard_map/pallas_call | solution.py:217
  81.5 1.0 collective-permute-start.15
  83.2 1.2 collective-permute-start.17
  84.4 1.1 collective-permute-start.18
  86.2 2.3 %collective-permute-start.19 = (bf16[512,128]{1,0:T(8,128)(2,1)S(1)}, bf16[512,128]{1,0:T(8,128)(2,1)S(1)}, u32[]{:S(2)}, u32[]{:S(2)}) collective-permute-start(bf16[512,128]{1,0:T(8,128)(2,1)S(1)} %get-tuple-element.69), channel_id=1, source_target_pairs={{0,28},{4,24},{8,20},{12,16},{16,12},{20,8},{24,4},{28,0},{1,29},{... | collective-permute-start | bytes 393224 | tf_op jit(solution)/shard_map/ppermute | solution.py:554
  89.2 1.1 collective-permute-done.17.refs_5_
  90.3 4.0 %shard_map.83.part_ref = f32[4096,128]{1,0:T(8,128)S(1)} custom-call(s32[4096]{0:T(1024)S(1)} %bitcast.19, s32[8]{0:T(128)S(1)} %fusion.4.cnt_ref, s32[2]{0:T(128)S(1)} %pad_add_fusion.where_ref, bf16[4,512,256]{2,1,0:T(8,128)(2,1)S(1)} %copy-done, bf16[512,128]{1,0:T(8,128)(2,1)S(1)} %get-tuple-element.62.refs_0_, ...), custom_call_target="tpu_custom_call" | custom-call | flops 6000000000 | bytes 1048576 | tf_op jit(solution)/shard_map/pallas_call | solution.py:351
  94.4 1.6 %collective-permute-done.19.refs_7_ = bf16[512,128]{1,0:T(8,128)(2,1)S(1)} collective-permute-done((bf16[512,128]{1,0:T(8,128)(2,1)S(1)}, bf16[512,128]{1,0:T(8,128)(2,1)S(1)}, u32[]{:S(2)}, u32[]{:S(2)}) %collective-permute-start.19) | collective-permute-done | bytes 131104 | tf_op jit(solution)/shard_map/ppermute | solution.py:554
  96.0 5.1 %shard_map.84 = (f32[131072,128]{1,0:T(8,128)}, bf16[512,128]{1,0:T(8,128)(2,1)S(1)}, bf16[512,128]{1,0:T(8,128)(2,1)S(1)}, bf16[512,128]{1,0:T(8,128)(2,1)S(1)}...) custom-call(s32[4096]{0:T(1024)S(1)} %bitcast.20, ...), custom_call_target="tpu_custom_call" | custom-call | flops 7000000000 | bytes 1048576 | tf_op jit(solution)/shard_map/pallas_call | solution.py:436
  101.2 3.1 %collective-permute-start.21 = (bf16[512,128]{1,0:T(8,128)(2,1)S(1)}, bf16[512,128]{1,0:T(8,128)(2,1)S(1)}, u32[]{:S(2)}, u32[]{:S(2)}) collective-permute-start(bf16[512,128]{1,0:T(8,128)(2,1)S(1)} %get-tuple-element.73), channel_id=1, source_target_pairs={{0,16},{4,20},{8,24},{12,28},{16,0},{20,4},{24,8},{28,12},{1,17},{... | collective-permute-start | bytes 393224 | tf_op jit(solution)/shard_map/ppermute | solution.py:554
  104.4 3.2 %collective-permute-start.23 = (bf16[512,128]{1,0:T(8,128)(2,1)S(1)}, bf16[512,128]{1,0:T(8,128)(2,1)S(1)}, u32[]{:S(2)}, u32[]{:S(2)}) collective-permute-start(bf16[512,128]{1,0:T(8,128)(2,1)S(1)} %get-tuple-element.75), channel_id=1, source_target_pairs={{0,28},{4,24},{8,20},{12,16},{16,12},{20,8},{24,4},{28,0},{1,29},{... | collective-permute-start | bytes 393224 | tf_op jit(solution)/shard_map/ppermute | solution.py:554
  107.6 1.1 collective-permute-start.25
  108.8 3.3 %collective-permute-done.21.refs_2_ = bf16[512,128]{1,0:T(8,128)(2,1)S(1)} collective-permute-done((bf16[512,128]{1,0:T(8,128)(2,1)S(1)}, bf16[512,128]{1,0:T(8,128)(2,1)S(1)}, u32[]{:S(2)}, u32[]{:S(2)}) %collective-permute-start.21) | collective-permute-done | bytes 131104 | tf_op jit(solution)/shard_map/ppermute | solution.py:554
  112.1 3.7 %collective-permute-start.26 = (bf16[512,128]{1,0:T(8,128)(2,1)S(1)}, bf16[512,128]{1,0:T(8,128)(2,1)S(1)}, u32[]{:S(2)}, u32[]{:S(2)}) collective-permute-start(bf16[512,128]{1,0:T(8,128)(2,1)S(1)} %get-tuple-element.78), channel_id=1, source_target_pairs={{0,20},{4,16},{8,28},{12,24},{16,4},{20,0},{24,12},{28,8},{1,21},{... | collective-permute-start | bytes 393224 | tf_op jit(solution)/shard_map/ppermute | solution.py:554
  115.8 2.3 %collective-permute-done.25.refs_6_ = bf16[512,128]{1,0:T(8,128)(2,1)S(1)} collective-permute-done((bf16[512,128]{1,0:T(8,128)(2,1)S(1)}, bf16[512,128]{1,0:T(8,128)(2,1)S(1)}, u32[]{:S(2)}, u32[]{:S(2)}) %collective-permute-start.25) | collective-permute-done | bytes 131104 | tf_op jit(solution)/shard_map/ppermute | solution.py:554
  118.8 8.0 %shard_map.85 = (bf16[512,128]{1,0:T(8,128)(2,1)S(1)}, bf16[512,128]{1,0:T(8,128)(2,1)S(1)}, bf16[512,128]{1,0:T(8,128)(2,1)S(1)}, bf16[512,128]{1,0:T(8,128)(2,...) custom-call(s32[8,24]{1,0:T(8,128)S(1)} %get-tuple-element.104.src_r, ...), custom_call_target="tpu_custom_call" | custom-call | flops 10737418240 | bytes 8388608 | tf_op jit(solution)/shard_map/pallas_call | solution.py:217
  126.9 2.3 %collective-permute-start.28 = (bf16[512,128]{1,0:T(8,128)(2,1)S(1)}, bf16[512,128]{1,0:T(8,128)(2,1)S(1)}, u32[]{:S(2)}, u32[]{:S(2)}) collective-permute-start(bf16[512,128]{1,0:T(8,128)(2,1)S(1)} %get-tuple-element.81), channel_id=1, source_target_pairs={{0,16},{4,20},{8,24},{12,28},{16,0},{20,4},{24,8},{28,12},{1,17},{... | collective-permute-start | bytes 393224 | tf_op jit(solution)/shard_map/ppermute | solution.py:554
  129.8 1.4 collective-permute-start.31
  131.2 0.8 reduce.1
  132.0 1.2 collective-permute-start.32
  133.2 1.5 %collective-permute-start.33 = (bf16[512,128]{1,0:T(8,128)(2,1)S(1)}, bf16[512,128]{1,0:T(8,128)(2,1)S(1)}, u32[]{:S(2)}, u32[]{:S(2)}) collective-permute-start(bf16[512,128]{1,0:T(8,128)(2,1)S(1)} %get-tuple-element.86), channel_id=1, source_target_pairs={{0,28},{4,24},{8,20},{12,16},{16,12},{20,8},{24,4},{28,0},{1,29},{... | collective-permute-start | bytes 393224 | tf_op jit(solution)/shard_map/ppermute | solution.py:554
  134.7 1.3 collective-permute-done.30.refs_4_
  136.1 2.3 %collective-permute-done.31.refs_5_ = bf16[512,128]{1,0:T(8,128)(2,1)S(1)} collective-permute-done((bf16[512,128]{1,0:T(8,128)(2,1)S(1)}, bf16[512,128]{1,0:T(8,128)(2,1)S(1)}, u32[]{:S(2)}, u32[]{:S(2)}) %collective-permute-start.31) | collective-permute-done | bytes 131104 | tf_op jit(solution)/shard_map/ppermute | solution.py:554
  138.3 3.9 %shard_map.86.part_ref = f32[4096,128]{1,0:T(8,128)S(1)} custom-call(s32[4096]{0:T(1024)S(1)} %bitcast.21, s32[8]{0:T(128)S(1)} %fusion.4.cnt_ref, s32[2]{0:T(128)S(1)} %pad_add_fusion.where_ref, f32[131072,128]{1,0:T(8,128)} %get-tuple-element.70.base_ref, bf16[512,128]{1,0:T(8,128)(2,1)S(1)} %get-tuple-element.79.refs_0_, ...), custom_call_target="tpu_custom_call" | custom-call | flops 6000000000 | bytes 1048576 | tf_op jit(solution)/shard_map/pallas_call | solution.py:351
  142.6 3.2 %shard_map.87 = f32[4,512,256]{2,1,0:T(8,128)} custom-call(s32[4096]{0:T(1024)S(1)} %bitcast.22, s32[8]{0:T(128)S(1)} %fusion.4.cnt_ref, s32[2]{0:T(128)S(1)} %pad_add_fusion.where_ref, f32[4096,128]{1,0:T(8,128)S(1)} %shard_map.86.part_ref, bf16[512,128]{1,0:T(8,128)(2,1)S(1)} %collective-permute-done.32.refs_0_, ...), custom_call_target="tpu_custom_call" | custom-call | flops 4000000000 | bytes 1048576 | tf_op jit(solution)/shard_map/pallas_call | solution.py:478
  (83 shorter events, 12.9 us)
Async XLA Ops:
  0.6 15.9 %collective-permute-start.1 = (bf16[4,128,512]{2,1,0:T(8,128)(2,1)}, bf16[4,128,512]{2,1,0:T(8,128)(2,1)S(1)}, u32[]{:S(2)}, u32[]{:S(2)}) collective-permute-start(bf16[4,128,512]{2,1,0:T(8,128)(2,1)} %own_ref.3), channel_id=1, source_target_pairs={{1,0},{2,1},{3,2},{5,4},{6,5},{7,6},{9,8},{10,9},{11,10},{13,12},{... | collective-permute-start | bytes 1572872 | tf_op jit(solution)/shard_map/ppermute | solution.py:564
  1.9 15.9 %collective-permute-start = (bf16[4,128,512]{2,1,0:T(8,128)(2,1)}, bf16[4,128,512]{2,1,0:T(8,128)(2,1)S(1)}, u32[]{:S(2)}, u32[]{:S(2)}) collective-permute-start(bf16[4,128,512]{2,1,0:T(8,128)(2,1)} %own_ref.3), channel_id=1, source_target_pairs={{0,1},{1,2},{2,3},{4,5},{5,6},{6,7},{8,9},{9,10},{10,11},{12,13},{... | collective-permute-start | bytes 1572872 | tf_op jit(solution)/shard_map/ppermute | solution.py:563
  16.5 14.8 %collective-permute-start.3 = (bf16[4,128,512]{2,1,0:T(8,128)(2,1)S(1)}, bf16[4,128,512]{2,1,0:T(8,128)(2,1)S(1)}, u32[]{:S(2)}, u32[]{:S(2)}) collective-permute-start(bf16[4,128,512]{2,1,0:T(8,128)(2,1)S(1)} %collective-permute-done.1.refs_1_), channel_id=1, source_target_pairs={{1,0},{2,1},{5,4},{6,5},{9,8},{10,9},{13,12},{14,13},{17,16},{18,1... | collective-permute-start | bytes 1572872 | tf_op jit(solution)/shard_map/ppermute | solution.py:564
  17.8 14.8 %collective-permute-start.2 = (bf16[4,128,512]{2,1,0:T(8,128)(2,1)S(1)}, bf16[4,128,512]{2,1,0:T(8,128)(2,1)S(1)}, u32[]{:S(2)}, u32[]{:S(2)}) collective-permute-start(bf16[4,128,512]{2,1,0:T(8,128)(2,1)S(1)} %collective-permute-done.refs_0_), channel_id=1, source_target_pairs={{1,2},{2,3},{5,6},{6,7},{9,10},{10,11},{13,14},{14,15},{17,18},{18... | collective-permute-start | bytes 1572872 | tf_op jit(solution)/shard_map/ppermute | solution.py:563
  20.4 1.0 copy-start.3
  22.0 9.1 %all-to-all-start = ((s32[8,1,512]{2,1,0:T(1,128)}), s32[8,1,512]{2,1,0:T(1,128)S(1)}, u32[]{:S(2)}, u32[]{:S(2)}) async-start(s32[8,1,512]{2,1,0:T(1,128)} %all_to_all.6), calls=%async_computation | async-start | bytes 32768 | tf_op jit(solution)/shard_map/all_to_all | solution.py:592
  31.4 18.1 %collective-permute-start.5 = (bf16[4,128,512]{2,1,0:T(8,128)(2,1)S(1)}, bf16[4,128,512]{2,1,0:T(8,128)(2,1)S(1)}, u32[]{:S(2)}, u32[]{:S(2)}) collective-permute-start(bf16[4,128,512]{2,1,0:T(8,128)(2,1)S(1)} %collective-permute-done.3.refs_3_.refs_1_), channel_id=1, source_target_pairs={{1,0},{5,4},{9,8},{13,12},{17,16},{21,20},{25,24},{29,28}} | collective-permute-start | bytes 1572872 | tf_op jit(solution)/shard_map/ppermute | solution.py:564
  32.7 16.8 %collective-permute-start.4 = (bf16[4,128,512]{2,1,0:T(8,128)(2,1)S(1)}, bf16[4,128,512]{2,1,0:T(8,128)(2,1)S(1)}, u32[]{:S(2)}, u32[]{:S(2)}) collective-permute-start(bf16[4,128,512]{2,1,0:T(8,128)(2,1)S(1)} %collective-permute-done.2.refs_2_.refs_0_), channel_id=1, source_target_pairs={{2,3},{6,7},{10,11},{14,15},{18,19},{22,23},{26,27},{30,31}} | collective-permute-start | bytes 1572872 | tf_op jit(solution)/shard_map/ppermute | solution.py:563
  37.2 12.2 %copy-start = (bf16[4,512,256]{2,1,0:T(8,128)(2,1)S(1)}, bf16[4,512,256]{2,1,0:T(8,128)(2,1)}, u32[]{:S(2)}) copy-start(bf16[4,512,256]{2,1,0:T(8,128)(2,1)} %base_ref.3) | copy-start | bytes 3145732
  37.2 12.2 %copy-start.1 = (bf16[4,128,512]{2,1,0:T(8,128)(2,1)S(1)}, bf16[4,128,512]{2,1,0:T(8,128)(2,1)}, u32[]{:S(2)}) copy-start(bf16[4,128,512]{2,1,0:T(8,128)(2,1)} %own_ref.3) | copy-start | bytes 1572868
  37.2 12.2 %copy-start.2 = (s32[4]{0:T(128)S(1)}, s32[4]{0:T(128)}, u32[]{:S(2)}) copy-start(s32[4]{0:T(128)} %count_ref.3) | copy-start | bytes 52
  53.5 11.5 %collective-permute-start.6 = (bf16[512,128]{1,0:T(8,128)(2,1)S(1)}, bf16[512,128]{1,0:T(8,128)(2,1)S(1)}, u32[]{:S(2)}, u32[]{:S(2)}) collective-permute-start(bf16[512,128]{1,0:T(8,128)(2,1)S(1)} %get-tuple-element.48), channel_id=1, source_target_pairs={{0,4},{4,0},{8,12},{12,8},{16,20},{20,16},{24,28},{28,24},{1,5},{5... | collective-permute-start | bytes 393224 | tf_op jit(solution)/shard_map/ppermute | solution.py:554
  54.7 11.2 %collective-permute-start.7 = (bf16[512,128]{1,0:T(8,128)(2,1)S(1)}, bf16[512,128]{1,0:T(8,128)(2,1)S(1)}, u32[]{:S(2)}, u32[]{:S(2)}) collective-permute-start(bf16[512,128]{1,0:T(8,128)(2,1)S(1)} %get-tuple-element.49), channel_id=1, source_target_pairs={{0,16},{4,20},{8,24},{12,28},{16,0},{20,4},{24,8},{28,12},{1,17},{... | collective-permute-start | bytes 393224 | tf_op jit(solution)/shard_map/ppermute | solution.py:554
  55.9 11.4 %collective-permute-start.8 = (bf16[512,128]{1,0:T(8,128)(2,1)S(1)}, bf16[512,128]{1,0:T(8,128)(2,1)S(1)}, u32[]{:S(2)}, u32[]{:S(2)}) collective-permute-start(bf16[512,128]{1,0:T(8,128)(2,1)S(1)} %get-tuple-element.50), channel_id=1, source_target_pairs={{0,24},{4,28},{8,16},{12,20},{16,8},{20,12},{24,0},{28,4},{1,25},{... | collective-permute-start | bytes 393224 | tf_op jit(solution)/shard_map/ppermute | solution.py:554
  56.5 10.9 %collective-permute-start.9 = (bf16[512,128]{1,0:T(8,128)(2,1)S(1)}, bf16[512,128]{1,0:T(8,128)(2,1)S(1)}, u32[]{:S(2)}, u32[]{:S(2)}) collective-permute-start(bf16[512,128]{1,0:T(8,128)(2,1)S(1)} %get-tuple-element.51), channel_id=1, source_target_pairs={{0,28},{4,24},{8,20},{12,16},{16,12},{20,8},{24,4},{28,0},{1,29},{... | collective-permute-start | bytes 393224 | tf_op jit(solution)/shard_map/ppermute | solution.py:554
  59.2 8.2 %collective-permute-start.10 = (bf16[512,128]{1,0:T(8,128)(2,1)S(1)}, bf16[512,128]{1,0:T(8,128)(2,1)S(1)}, u32[]{:S(2)}, u32[]{:S(2)}) collective-permute-start(bf16[512,128]{1,0:T(8,128)(2,1)S(1)} %get-tuple-element.52), channel_id=1, source_target_pairs={{0,8},{4,12},{8,0},{12,4},{16,24},{20,28},{24,16},{28,20},{1,9},{5... | collective-permute-start | bytes 393224 | tf_op jit(solution)/shard_map/ppermute | solution.py:554
  59.6 12.4 %copy-start.4 = (bf16[1,256,2048]{2,1,0:T(8,128)(2,1)S(1)}, bf16[1,256,2048]{2,1,0:T(8,128)(2,1)}, u32[]{:S(2)}) copy-start(bf16[1,256,2048]{2,1,0:T(8,128)(2,1)} %copy-done.3) | copy-start | bytes 3145732
  65.0 5.6 %collective-permute-start.11 = (bf16[512,128]{1,0:T(8,128)(2,1)S(1)}, bf16[512,128]{1,0:T(8,128)(2,1)S(1)}, u32[]{:S(2)}, u32[]{:S(2)}) collective-permute-start(bf16[512,128]{1,0:T(8,128)(2,1)S(1)} %get-tuple-element.53), channel_id=1, source_target_pairs={{0,12},{4,8},{8,4},{12,0},{16,28},{20,24},{24,20},{28,16},{1,13},{... | collective-permute-start | bytes 393224 | tf_op jit(solution)/shard_map/ppermute | solution.py:554
  65.9 6.1 %collective-permute-start.12 = (bf16[512,128]{1,0:T(8,128)(2,1)S(1)}, bf16[512,128]{1,0:T(8,128)(2,1)S(1)}, u32[]{:S(2)}, u32[]{:S(2)}) collective-permute-start(bf16[512,128]{1,0:T(8,128)(2,1)S(1)} %get-tuple-element.54), channel_id=1, source_target_pairs={{0,20},{4,16},{8,28},{12,24},{16,4},{20,0},{24,12},{28,8},{1,21},{... | collective-permute-start | bytes 393224 | tf_op jit(solution)/shard_map/ppermute | solution.py:554
  80.7 3.7 %collective-permute-start.13 = (bf16[512,128]{1,0:T(8,128)(2,1)S(1)}, bf16[512,128]{1,0:T(8,128)(2,1)S(1)}, u32[]{:S(2)}, u32[]{:S(2)}) collective-permute-start(bf16[512,128]{1,0:T(8,128)(2,1)S(1)} %get-tuple-element.63), channel_id=1, source_target_pairs={{0,4},{4,0},{8,12},{12,8},{16,20},{20,16},{24,28},{28,24},{1,5},{5... | collective-permute-start | bytes 393224 | tf_op jit(solution)/shard_map/ppermute | solution.py:554
  81.2 5.1 %collective-permute-start.14 = (bf16[512,128]{1,0:T(8,128)(2,1)S(1)}, bf16[512,128]{1,0:T(8,128)(2,1)S(1)}, u32[]{:S(2)}, u32[]{:S(2)}) collective-permute-start(bf16[512,128]{1,0:T(8,128)(2,1)S(1)} %get-tuple-element.64), channel_id=1, source_target_pairs={{0,16},{4,20},{8,24},{12,28},{16,0},{20,4},{24,8},{28,12},{1,17},{... | collective-permute-start | bytes 393224 | tf_op jit(solution)/shard_map/ppermute | solution.py:554
  81.5 7.0 %collective-permute-start.15 = (bf16[512,128]{1,0:T(8,128)(2,1)S(1)}, bf16[512,128]{1,0:T(8,128)(2,1)S(1)}, u32[]{:S(2)}, u32[]{:S(2)}) collective-permute-start(bf16[512,128]{1,0:T(8,128)(2,1)S(1)} %get-tuple-element.65), channel_id=1, source_target_pairs={{0,8},{4,12},{8,0},{12,4},{16,24},{20,28},{24,16},{28,20},{1,9},{5... | collective-permute-start | bytes 393224 | tf_op jit(solution)/shard_map/ppermute | solution.py:554
  82.5 6.7 %collective-permute-start.16 = (bf16[512,128]{1,0:T(8,128)(2,1)S(1)}, bf16[512,128]{1,0:T(8,128)(2,1)S(1)}, u32[]{:S(2)}, u32[]{:S(2)}) collective-permute-start(bf16[512,128]{1,0:T(8,128)(2,1)S(1)} %get-tuple-element.66), channel_id=1, source_target_pairs={{0,20},{4,16},{8,28},{12,24},{16,4},{20,0},{24,12},{28,8},{1,21},{... | collective-permute-start | bytes 393224 | tf_op jit(solution)/shard_map/ppermute | solution.py:554
  83.2 7.1 %collective-permute-start.17 = (bf16[512,128]{1,0:T(8,128)(2,1)S(1)}, bf16[512,128]{1,0:T(8,128)(2,1)S(1)}, u32[]{:S(2)}, u32[]{:S(2)}) collective-permute-start(bf16[512,128]{1,0:T(8,128)(2,1)S(1)} %get-tuple-element.67), channel_id=1, source_target_pairs={{0,12},{4,8},{8,4},{12,0},{16,28},{20,24},{24,20},{28,16},{1,13},{... | collective-permute-start | bytes 393224 | tf_op jit(solution)/shard_map/ppermute | solution.py:554
  84.4 10.0 %collective-permute-start.18 = (bf16[512,128]{1,0:T(8,128)(2,1)S(1)}, bf16[512,128]{1,0:T(8,128)(2,1)S(1)}, u32[]{:S(2)}, u32[]{:S(2)}) collective-permute-start(bf16[512,128]{1,0:T(8,128)(2,1)S(1)} %get-tuple-element.68), channel_id=1, source_target_pairs={{0,24},{4,28},{8,16},{12,20},{16,8},{20,12},{24,0},{28,4},{1,25},{... | collective-permute-start | bytes 393224 | tf_op jit(solution)/shard_map/ppermute | solution.py:554
  86.2 9.8 %collective-permute-start.19 = (bf16[512,128]{1,0:T(8,128)(2,1)S(1)}, bf16[512,128]{1,0:T(8,128)(2,1)S(1)}, u32[]{:S(2)}, u32[]{:S(2)}) collective-permute-start(bf16[512,128]{1,0:T(8,128)(2,1)S(1)} %get-tuple-element.69), channel_id=1, source_target_pairs={{0,28},{4,24},{8,20},{12,16},{16,12},{20,8},{24,4},{28,0},{1,29},{... | collective-permute-start | bytes 393224 | tf_op jit(solution)/shard_map/ppermute | solution.py:554
  101.1 6.5 %collective-permute-start.20 = (bf16[512,128]{1,0:T(8,128)(2,1)S(1)}, bf16[512,128]{1,0:T(8,128)(2,1)S(1)}, u32[]{:S(2)}, u32[]{:S(2)}) collective-permute-start(bf16[512,128]{1,0:T(8,128)(2,1)S(1)} %get-tuple-element.72), channel_id=1, source_target_pairs={{0,4},{4,0},{8,12},{12,8},{16,20},{20,16},{24,28},{28,24},{1,5},{5... | collective-permute-start | bytes 393224 | tf_op jit(solution)/shard_map/ppermute | solution.py:554
  101.2 10.8 %collective-permute-start.21 = (bf16[512,128]{1,0:T(8,128)(2,1)S(1)}, bf16[512,128]{1,0:T(8,128)(2,1)S(1)}, u32[]{:S(2)}, u32[]{:S(2)}) collective-permute-start(bf16[512,128]{1,0:T(8,128)(2,1)S(1)} %get-tuple-element.73), channel_id=1, source_target_pairs={{0,16},{4,20},{8,24},{12,28},{16,0},{20,4},{24,8},{28,12},{1,17},{... | collective-permute-start | bytes 393224 | tf_op jit(solution)/shard_map/ppermute | solution.py:554
  104.4 11.4 %collective-permute-start.22 = (bf16[512,128]{1,0:T(8,128)(2,1)S(1)}, bf16[512,128]{1,0:T(8,128)(2,1)S(1)}, u32[]{:S(2)}, u32[]{:S(2)}) collective-permute-start(bf16[512,128]{1,0:T(8,128)(2,1)S(1)} %get-tuple-element.74), channel_id=1, source_target_pairs={{0,24},{4,28},{8,16},{12,20},{16,8},{20,12},{24,0},{28,4},{1,25},{... | collective-permute-start | bytes 393224 | tf_op jit(solution)/shard_map/ppermute | solution.py:554
  104.4 11.4 %collective-permute-start.23 = (bf16[512,128]{1,0:T(8,128)(2,1)S(1)}, bf16[512,128]{1,0:T(8,128)(2,1)S(1)}, u32[]{:S(2)}, u32[]{:S(2)}) collective-permute-start(bf16[512,128]{1,0:T(8,128)(2,1)S(1)} %get-tuple-element.75), channel_id=1, source_target_pairs={{0,28},{4,24},{8,20},{12,16},{16,12},{20,8},{24,4},{28,0},{1,29},{... | collective-permute-start | bytes 393224 | tf_op jit(solution)/shard_map/ppermute | solution.py:554
  107.6 8.2 %collective-permute-start.24 = (bf16[512,128]{1,0:T(8,128)(2,1)S(1)}, bf16[512,128]{1,0:T(8,128)(2,1)S(1)}, u32[]{:S(2)}, u32[]{:S(2)}) collective-permute-start(bf16[512,128]{1,0:T(8,128)(2,1)S(1)} %get-tuple-element.76), channel_id=1, source_target_pairs={{0,8},{4,12},{8,0},{12,4},{16,24},{20,28},{24,16},{28,20},{1,9},{5... | collective-permute-start | bytes 393224 | tf_op jit(solution)/shard_map/ppermute | solution.py:554
  107.6 10.4 %collective-permute-start.25 = (bf16[512,128]{1,0:T(8,128)(2,1)S(1)}, bf16[512,128]{1,0:T(8,128)(2,1)S(1)}, u32[]{:S(2)}, u32[]{:S(2)}) collective-permute-start(bf16[512,128]{1,0:T(8,128)(2,1)S(1)} %get-tuple-element.77), channel_id=1, source_target_pairs={{0,12},{4,8},{8,4},{12,0},{16,28},{20,24},{24,20},{28,16},{1,13},{... | collective-permute-start | bytes 393224 | tf_op jit(solution)/shard_map/ppermute | solution.py:554
  112.1 6.8 %collective-permute-start.26 = (bf16[512,128]{1,0:T(8,128)(2,1)S(1)}, bf16[512,128]{1,0:T(8,128)(2,1)S(1)}, u32[]{:S(2)}, u32[]{:S(2)}) collective-permute-start(bf16[512,128]{1,0:T(8,128)(2,1)S(1)} %get-tuple-element.78), channel_id=1, source_target_pairs={{0,20},{4,16},{8,28},{12,24},{16,4},{20,0},{24,12},{28,8},{1,21},{... | collective-permute-start | bytes 393224 | tf_op jit(solution)/shard_map/ppermute | solution.py:554
  126.8 5.2 %collective-permute-start.27 = (bf16[512,128]{1,0:T(8,128)(2,1)S(1)}, bf16[512,128]{1,0:T(8,128)(2,1)S(1)}, u32[]{:S(2)}, u32[]{:S(2)}) collective-permute-start(bf16[512,128]{1,0:T(8,128)(2,1)S(1)} %get-tuple-element.80), channel_id=1, source_target_pairs={{0,4},{4,0},{8,12},{12,8},{16,20},{20,16},{24,28},{28,24},{1,5},{5... | collective-permute-start | bytes 393224 | tf_op jit(solution)/shard_map/ppermute | solution.py:554
  126.9 6.3 %collective-permute-start.28 = (bf16[512,128]{1,0:T(8,128)(2,1)S(1)}, bf16[512,128]{1,0:T(8,128)(2,1)S(1)}, u32[]{:S(2)}, u32[]{:S(2)}) collective-permute-start(bf16[512,128]{1,0:T(8,128)(2,1)S(1)} %get-tuple-element.81), channel_id=1, source_target_pairs={{0,16},{4,20},{8,24},{12,28},{16,0},{20,4},{24,8},{28,12},{1,17},{... | collective-permute-start | bytes 393224 | tf_op jit(solution)/shard_map/ppermute | solution.py:554
  129.2 5.5 %collective-permute-start.29 = (bf16[512,128]{1,0:T(8,128)(2,1)S(1)}, bf16[512,128]{1,0:T(8,128)(2,1)S(1)}, u32[]{:S(2)}, u32[]{:S(2)}) collective-permute-start(bf16[512,128]{1,0:T(8,128)(2,1)S(1)} %get-tuple-element.82), channel_id=1, source_target_pairs={{0,8},{4,12},{8,0},{12,4},{16,24},{20,28},{24,16},{28,20},{1,9},{5... | collective-permute-start | bytes 393224 | tf_op jit(solution)/shard_map/ppermute | solution.py:554
  129.2 6.8 %collective-permute-start.30 = (bf16[512,128]{1,0:T(8,128)(2,1)S(1)}, bf16[512,128]{1,0:T(8,128)(2,1)S(1)}, u32[]{:S(2)}, u32[]{:S(2)}) collective-permute-start(bf16[512,128]{1,0:T(8,128)(2,1)S(1)} %get-tuple-element.83), channel_id=1, source_target_pairs={{0,20},{4,16},{8,28},{12,24},{16,4},{20,0},{24,12},{28,8},{1,21},{... | collective-permute-start | bytes 393224 | tf_op jit(solution)/shard_map/ppermute | solution.py:554
  129.8 8.5 %collective-permute-start.31 = (bf16[512,128]{1,0:T(8,128)(2,1)S(1)}, bf16[512,128]{1,0:T(8,128)(2,1)S(1)}, u32[]{:S(2)}, u32[]{:S(2)}) collective-permute-start(bf16[512,128]{1,0:T(8,128)(2,1)S(1)} %get-tuple-element.84), channel_id=1, source_target_pairs={{0,12},{4,8},{8,4},{12,0},{16,28},{20,24},{24,20},{28,16},{1,13},{... | collective-permute-start | bytes 393224 | tf_op jit(solution)/shard_map/ppermute | solution.py:554
  132.0 10.2 %collective-permute-start.32 = (bf16[512,128]{1,0:T(8,128)(2,1)S(1)}, bf16[512,128]{1,0:T(8,128)(2,1)S(1)}, u32[]{:S(2)}, u32[]{:S(2)}) collective-permute-start(bf16[512,128]{1,0:T(8,128)(2,1)S(1)} %get-tuple-element.85), channel_id=1, source_target_pairs={{0,24},{4,28},{8,16},{12,20},{16,8},{20,12},{24,0},{28,4},{1,25},{... | collective-permute-start | bytes 393224 | tf_op jit(solution)/shard_map/ppermute | solution.py:554
  133.2 9.3 %collective-permute-start.33 = (bf16[512,128]{1,0:T(8,128)(2,1)S(1)}, bf16[512,128]{1,0:T(8,128)(2,1)S(1)}, u32[]{:S(2)}, u32[]{:S(2)}) collective-permute-start(bf16[512,128]{1,0:T(8,128)(2,1)S(1)} %get-tuple-element.86), channel_id=1, source_target_pairs={{0,28},{4,24},{8,20},{12,16},{16,12},{20,8},{24,4},{28,0},{1,29},{... | collective-permute-start | bytes 393224 | tf_op jit(solution)/shard_map/ppermute | solution.py:554

commit v10 on v9

--- a/solution.py
+++ b/solution.py
@@ -22,7 +22,7 @@
 PICK_VMEM = 12 * MIB
 LATE_PICK_VMEM = 18 * MIB
 LATE_VMEM = 12 * MIB
-BASIS_CALLS = (1, 2, 2, 3)
+BASIS_CALLS = (1, 2, 3, 2)
 UNROLL = 32
 PICK_UNROLL = 16
 SUB = 8
@@ -106,7 +106,7 @@
         ],
         compiler_params=pltpu.CompilerParams(vmem_limit_bytes=BASIS_VMEM),
         cost_estimate=pl.CostEstimate(
-            flops=sched_dev * obs * nper * 8000, bytes_accessed=sched_dev * obs * nper * 4, transcendentals=0
+            flops=sched_dev * obs * nper * 2500, bytes_accessed=sched_dev * obs * nper * 4, transcendentals=0
         ),
     )(wide, period, 1.0 / period, *after)
 
@@ -140,7 +140,7 @@
     for plan in range(plans):
         basis_copy(plan).start()
     for owner in range(tm_count):
-        rows_ref[pl.ds(owner * spaced, capacity), :] = arrived[owner][...].astype(jnp.float32)
+        rows_ref[pl.ds(owner * spaced, capacity), :] = own_half(arrived, owner, capacity)[...].astype(jnp.float32)
 
     def correlate(plan, obs_ref, corr_ref):
         for step in range(steps):
@@ -258,6 +258,8 @@
 def whiten_and_pick(me, asked_ref, cnt_ref, count_ref, whole_ref, wait, load, picked, white_ref, gather_ref):
     segs, slots, _ = whole_ref.shape
     capacity, width = picked[0].shape
+    picked = by_step(picked)
+    picked[3] = picked[2]
     blocks = white_ref.shape[0] // (segs * slots)
     row = lax.broadcasted_iota(jnp.int32, (slots, width * blocks), 0)
     wait()
@@ -266,7 +268,7 @@
         white = jnp.dot(whole_ref[seg], masked, preferred_element_type=jnp.float32)
         for block in range(blocks):
             white_ref[pl.ds((block * segs + seg) * slots, slots), :] = white[:, block * width:(block + 1) * width]
-    for owner, out_ref in enumerate(picked):
+    for owner in range(len(picked)):
         asker = owner ^ me
 
         def step(index, carry):
@@ -278,17 +280,19 @@
             return carry
 
         lax.fori_loop(0, (cnt_ref[asker] + PICK_UNROLL - 1) // PICK_UNROLL, step, 0)
-        out_ref[...] = gather_ref[pl.ds(owner * capacity, capacity), :].astype(jnp.bfloat16)
+        block = gather_ref[pl.ds(owner * capacity, capacity), :]
+        own_half(picked, owner, capacity)[...] = block.astype(jnp.bfloat16)
 
 
 def add_rows(me, asked_ref, cnt_ref, owners, returned, rows_ref, sums, tiled):
-    capacity = returned[0].shape[0]
+    returned = dict(zip(owners, returned))
+    capacity = asked_ref.shape[0] // cnt_ref.shape[0]
     streams = len(sums)
     for total in sums:
         total[...] = jnp.zeros_like(total)
-    for number, (owner, ref) in enumerate(zip(owners, returned)):
+    for number, owner in enumerate(owners):
         tiles = capacity // SUB
-        block = ref[...].astype(jnp.float32)
+        block = returned[owner][...].astype(jnp.float32)
         if tiled:
             rows_ref[pl.ds(number * tiles, tiles)] = block.reshape(tiles, SUB, -1)
         else:
@@ -362,7 +366,7 @@
 def pick_kernel(tm_count, passed_count, asked_ref, cnt_ref, count_ref, where_ref, base_ref, own_ref, *refs):
     refs = list(refs)
     passed = [refs.pop(0) for _ in range(passed_count)]
-    picked = [refs.pop(0) for _ in range(tm_count)]
+    picked = [refs.pop(0) for _ in range(tm_count - 1)]
     whole_ref, sems, white_ref, gather_ref = refs
     wait = load_attitude(where_ref[1], own_ref, passed, whole_ref, sems)
     whiten_and_pick(
@@ -376,11 +380,11 @@
     tm_count, = cnt.shape
     seg_dev, slots, _ = base.shape
     capacity = asked.shape[0] // tm_count
-    return pl.pallas_call(
+    return by_step(pl.pallas_call(
         functools.partial(pick_kernel, tm_count, len(attitude) - 1),
         in_specs=[SMEM] * 4 + [VMEM] + [ANY] * len(attitude),
-        out_specs=[VMEM] * tm_count,
-        out_shape=[jax.ShapeDtypeStruct((capacity, SRC_GROUP), jnp.bfloat16)] * tm_count,
+        out_specs=[VMEM] * (tm_count - 1),
+        out_shape=block_shapes(tm_count, capacity),
         scratch_shapes=[
             pltpu.VMEM((seg_dev, slots, slots), jnp.bfloat16),
             pltpu.SemaphoreType.DMA((len(attitude),)),
@@ -389,7 +393,7 @@
         ],
         compiler_params=pltpu.CompilerParams(vmem_limit_bytes=PICK_VMEM),
         cost_estimate=pl.CostEstimate(flops=5 * COST_US, bytes_accessed=1 << 20, transcendentals=0),
-    )(asked, cnt, seg_counts, where, base, *attitude)
+    )(asked, cnt, seg_counts, where, base, *attitude))
 
 
 def late_pick_kernel(tm_count, passed_count, owners, asked_ref, cnt_ref, count_ref, where_ref, part_ref, own_ref,
@@ -404,7 +408,7 @@
     passed = take(passed_count)
     returned = take(len(owners))
     (out_ref,) = take(1)
-    picked = take(tm_count)
+    picked = take(tm_count - 1)
     whole_ref, sems, white_ref, gather_ref, table_ref, sem = take(6)
     segs, slots, _ = whole_ref.shape
     blocks = table_ref.shape[0] // (segs * slots)
@@ -436,9 +440,9 @@
     out = pl.pallas_call(
         functools.partial(late_pick_kernel, tm_count, len(attitude) - 1, owners),
         in_specs=[SMEM] * 4 + [VMEM] + [ANY] * len(attitude) + [VMEM] * len(owners),
-        out_specs=[HBM] + [VMEM] * tm_count,
+        out_specs=[HBM] + [VMEM] * (tm_count - 1),
         out_shape=[jax.ShapeDtypeStruct((HBM_SPARE * rows, SRC_GROUP), jnp.float32)]
-        + [jax.ShapeDtypeStruct((capacity, SRC_GROUP), jnp.bfloat16)] * tm_count,
+        + block_shapes(tm_count, capacity),
         scratch_shapes=[
             pltpu.VMEM((seg_dev, slots, slots), jnp.bfloat16),
             pltpu.SemaphoreType.DMA((len(attitude),)),
@@ -450,7 +454,7 @@
         compiler_params=pltpu.CompilerParams(vmem_limit_bytes=LATE_PICK_VMEM),
         cost_estimate=pl.CostEstimate(flops=7 * COST_US, bytes_accessed=1 << 20, transcendentals=0),
     )(asked, cnt, seg_counts, where, part, *attitude, *[returned[owner] for owner in owners])
-    return out[0], list(out[1:])
+    return out[0], by_step(out[1:])
 
 
 def late_kernel(owners, asked_ref, cnt_ref, where_ref, part_ref, *refs):
@@ -541,18 +545,42 @@
 
 
 def ask_order(count):
-    first = [1, count // 2]
-    return first + sorted(
-        (step for step in range(2, count) if step not in first), key=lambda step: -bin(step // 2).count("1")
-    )
+    first = [1, 2, count // 2]
+    rest = (step for step in range(4, count) if step not in first)
+    return first + sorted(rest, key=lambda step: -bin(step // 2).count("1")) + [3]
+
+
+def block_shapes(count, capacity):
+    return [
+        jax.ShapeDtypeStruct((2 * capacity if step == 2 else capacity, SRC_GROUP), jnp.bfloat16)
+        for step in range(count)
+        if step != 3
+    ]
+
+
+def own_half(refs, step, capacity):
+    if step == 3:
+        return refs[step].at[pl.ds(capacity, capacity), :]
+    return refs[step].at[pl.ds(0, capacity), :]
+
+
+def by_step(blocks):
+    return dict(zip([step for step in range(len(blocks) + 1) if step != 3], blocks))
+
+
+def send_on(block, step):
+    return lax.ppermute(block, "tm", [(i, i ^ step) for i in range(lax.axis_size("tm"))])
+
+
+def ask_exchange(blocks):
+    out = {step: send_on(block, step) if step else block for step, block in blocks.items()}
+    both, *_ = lax.optimization_barrier([out[step] for step in out if step > 1])
+    out[3] = send_on(both, 1)
+    return out, both
 
 
 def exchange(blocks):
-    count = len(blocks)
-    out = list(blocks)
-    for step in range(1, count):
-        out[step] = lax.ppermute(blocks[step], "tm", [(i, i ^ step) for i in range(count)])
-    return out
+    return [send_on(block, step) if step else block for step, block in enumerate(blocks)]
 
 
 def pass_along(attitude, beside):
@@ -587,19 +615,21 @@
 
     def first_hop(right, left):
         nonlocal asked
+        held, right, left = lax.optimization_barrier((wanted, right, left))
         basis_part([right, left])
-        held, _ = lax.optimization_barrier((wanted, made[0][1]))
+        held, _ = lax.optimization_barrier((held, made[0][1]))
         asked = lax.all_to_all(held, "tm", split_axis=0, concat_axis=0, tiled=True)
+        basis_part([made[0][1]])
         return right, left
 
     def second_hop(right, left):
-        basis_part([right, left])
         basis_part([right, left])
         return right, left
 
     pieces = pass_along(attitude, {1: first_hop, 2: second_hop})
     cnt = jnp.sum((asked < seg_dev * slots * column_blocks).astype(jnp.int32), axis=1)
     where = jnp.stack([lax.axis_index("tm"), lax.axis_index("sky")])
+    where, _ = lax.optimization_barrier((where, made[-1][1]))
     scalars = (asked.reshape(-1), cnt, seg_counts, where)
     rows = seg_dev * slots * column_blocks
     order = [0] + send_order(tm_count)
@@ -607,11 +637,13 @@
 
     base = residuals
     picked = pick_rows(scalars, base, pieces, rows)
-    basis_part([picked[0]])
-    parts, norms = zip(*made)
-    norms = jnp.concatenate(norms)
     for iteration in range(ITERS):
-        models, score = fit_plans(tables, exchange(picked), parts, norms)
+        arrived, both = ask_exchange(picked)
+        if iteration == 0:
+            basis_part([both])
+            parts, norms = zip(*made)
+            norms = jnp.concatenate(norms)
+        models, score = fit_plans(tables, arrived, parts, norms)
         returned = exchange(models)
         base = place_early(scalars, near, base, returned, rows)
         if iteration < ITERS - 1:

time: 147 us -> 155 us (1.054)
  waiting for transfers between devices: 33 us -> 41.4 us
  starting transfers between devices: 48.9 us -> 42.3 us
  Pallas kernels: 51.2 us -> 56.7 us
    ppermute x28, waiting for transfers between devices: 19.1 us -> 28.3 us  [send_on(): lax.ppermute(block, 'tm', [(i, i ^ step) for i in range(lax.axis_size('tm...]
    ppermute x28, starting transfers between devices: 33.8 us -> 25.1 us  [send_on(): lax.ppermute(block, 'tm', [(i, i ^ step) for i in range(lax.axis_size('tm...]
    all_to_all x1, waiting for transfers between devices: 4.02 us -> 0.01 us  [first_hop(): asked = lax.all_to_all(held, 'tm', split_axis=0, concat_axis=0, tiled=True)]
    ppermute x3, waiting for transfers between devices: 9.85 us -> 12.1 us  [pass_along(): lax.ppermute(left, 'sky', [(i, i - 1) for i in range(1, count - hop + 1)])]
    pallas_call x1, Pallas kernels: 4.05 us -> 5.87 us  [pick_rows(): pl.pallas_call(functools.partial(pick_kernel, tm_count, len(attitude) - 1...]
    pallas_call x1, Pallas kernels: 5.07 us -> 6.8 us  [place_late_and_pick(): pl.pallas_call(functools.partial(late_pick_kernel, tm_count, len(attitude...]
  transfers between devices with their start and end apart: 35 -> 35, of which waited for: 15 -> 19; matrix products, arithmetic and copies ran while one was open for 7% -> 6% of each run, Pallas kernels for 15% -> 15%
where the time goes in v10:
time: 155 us
  Pallas kernels  56.7 us (37%)
  starting transfers between devices  42.3 us (27%)
  waiting for transfers between devices  41.4 us (27%)
  other arithmetic  9.5 us (6%)
  local copies, waits for them, and re-layouts  3.48 us (2%)
    ppermute x28, waiting for transfers between devices, send_on(): lax.ppermute(block, 'tm', [(i, i ^ step) for i in range(lax.axis_size('tm...  28.3 us
    ppermute x28, starting transfers between devices, send_on(): lax.ppermute(block, 'tm', [(i, i ^ step) for i in range(lax.axis_size('tm...  25.1 us
    pallas_call x2, Pallas kernels, fit_plans(): pl.pallas_call(functools.partial(fit_kernel, order), in_specs=[SMEM, SMEM...  16.7 us
    pallas_call x4, Pallas kernels, make_basis(): pl.pallas_call(functools.partial(basis_kernel, len(after)), grid=(sched_d...  14.3 us
    ppermute x3, waiting for transfers between devices, pass_along(): lax.ppermute(left, 'sky', [(i, i - 1) for i in range(1, count - hop + 1)])  12.1 us
    pallas_call x2, Pallas kernels, place_early(): pl.pallas_call(functools.partial(early_kernel, owners, table_base), in_sp...  8.94 us
    ppermute x3, starting transfers between devices, pass_along(): lax.ppermute(right, 'sky', [(i, i + 1) for i in range(hop - 1, count - 1)])  6.84 us
    pallas_call x1, Pallas kernels, place_late_and_pick(): pl.pallas_call(functools.partial(late_pick_kernel, tm_count, len(attitude...  6.8 us
  transfers between devices with their start and end apart: 35, of which 19 were waited for; matrix products, arithmetic and copies ran while one was open for 6% of the time, Pallas kernels for 15%

profile of v10, /device:TPU:1, one launch (start us, length us, event | category | flops | bytes accessed | tf_op | source)
XLA Modules:
  0.0 154.6 jit_solution(11170231126925678121)
XLA Ops:
  0.6 1.3 collective-permute-start.1
  1.9 4.7 %collective-permute-start = (bf16[4,128,512]{2,1,0:T(8,128)(2,1)}, bf16[4,128,512]{2,1,0:T(8,128)(2,1)S(1)}, u32[]{:S(2)}, u32[]{:S(2)}) collective-permute-start(bf16[4,128,512]{2,1,0:T(8,128)(2,1)} %own_ref.3), channel_id=1, source_target_pairs={{0,1},{1,2},{2,3},{4,5},{5,6},{6,7},{8,9},{9,10},{10,11},{12,13},{... | collective-permute-start | bytes 1572872 | tf_op jit(solution)/shard_map/ppermute | solution.py:591
  10.4 3.4 %select_reduce_fusion = s32[4096]{0:T(1024)S(1)} fusion(s32[2048]{0:T(1024)S(1)} %bitcast.34, s32[2048]{0:T(1024)S(1)} %bitcast.33), kind=kLoop, calls=%fused_computation | loop fusion | flops 25161728 | bytes 32768 | tf_op jit(solution)/shard_map/reduce_sum | solution.py:522
  14.4 2.1 %collective-permute-done.1.refs_1_ = bf16[4,128,512]{2,1,0:T(8,128)(2,1)S(1)} collective-permute-done((bf16[4,128,512]{2,1,0:T(8,128)(2,1)}, bf16[4,128,512]{2,1,0:T(8,128)(2,1)S(1)}, u32[]{:S(2)}, u32[]{:S(2)}) %collective-permute-start.1) | collective-permute-done | bytes 524320 | tf_op jit(solution)/shard_map/ppermute | solution.py:592
  16.5 1.0 collective-permute-done.refs_0_
  18.2 1.3 collective-permute-start.3
  20.4 1.8 %shard_map.77 = (bf16[1,256,2048]{2,1,0:T(8,128)(2,1)S(1)}, f32[1,1,2048]{2,1,0:T(1,128)S(1)}) custom-call(f32[256,128]{1,0:T(8,128)S(1)} %broadcast_in_dim.50.time_ref, f32[1,1024]{1,0:T(1,128)S(1)} %bitcast.27, f32[1,1024]{1,0:T(1,128)S(1)} %bitcast.23, bf16[4,128,512]{2,1,0:T(8,128)(2,1)S(1)} %collective-permute-done.refs_0_, ...), custom_call_target="tpu_custom_call" | custom-call | flops 655360000 | bytes 1048576 | tf_op jit(solution)/shard_map/pallas_call | solution.py:91
  22.2 1.0 copy-done.3
  23.1 1.5 collective-permute-start.4
  24.6 10.0 %collective-permute-done.3.refs_1_.refs_3_ = bf16[4,128,512]{2,1,0:T(8,128)(2,1)S(1)} collective-permute-done((bf16[4,128,512]{2,1,0:T(8,128)(2,1)S(1)}, bf16[4,128,512]{2,1,0:T(8,128)(2,1)S(1)}, u32[]{:S(2)}, u32[]{:S(2)}) %collective-permute-start.3) | collective-permute-done | bytes 524320 | tf_op jit(solution)/shard_map/ppermute | solution.py:592
  34.6 1.3 collective-permute-start.5
  36.6 6.5 %all-to-all-start = ((s32[8,1,512]{2,1,0:T(1,128)}), s32[8,1,512]{2,1,0:T(1,128)S(1)}, u32[]{:S(2)}, u32[]{:S(2)}) async-start(s32[8,1,512]{2,1,0:T(1,128)} %all_to_all.6), calls=%async_computation | async-start | bytes 32768 | tf_op jit(solution)/shard_map/all_to_all | solution.py:621
  43.2 3.6 %shard_map.80 = (bf16[2,256,2048]{2,1,0:T(8,128)(2,1)S(1)}, f32[2,1,2048]{2,1,0:T(1,128)S(1)}) custom-call(f32[512,128]{1,0:T(8,128)S(1)} %broadcast_in_dim.55.time_ref, f32[1,1024]{1,0:T(1,128)S(1)} %bitcast.28, f32[1,1024]{1,0:T(1,128)S(1)} %bitcast.24, f32[1,1,2048]{2,1,0:T(1,128)S(1)} %get-tuple-element.52.refs_0_), custom_call_target="tpu_custom_call" | custom-call | flops 1310720000 | bytes 2097152 | tf_op jit(solution)/shard_map/pallas_call | solution.py:91
  46.8 1.3 copy-done.5
  48.5 5.3 %shard_map.78 = (bf16[3,256,2048]{2,1,0:T(8,128)(2,1)S(1)}, f32[3,1,2048]{2,1,0:T(1,128)S(1)}) custom-call(f32[768,128]{1,0:T(8,128)S(1)} %broadcast_in_dim.53.time_ref, f32[1,1024]{1,0:T(1,128)S(1)} %bitcast.29, f32[1,1024]{1,0:T(1,128)S(1)} %bitcast.25, bf16[4,128,512]{2,1,0:T(8,128)(2,1)S(1)} %collective-permute-done.2.refs_0_.refs_2_, ...), custom_call_target="tpu_custom_call" | custom-call | flops 1966080000 | bytes 3145728 | tf_op jit(solution)/shard_map/pallas_call | solution.py:91
  53.9 5.9 %shard_map.79 = (bf16[512,128]{1,0:T(8,128)(2,1)S(1)}, bf16[512,128]{1,0:T(8,128)(2,1)S(1)}, bf16[1024,128]{1,0:T(8,128)(2,1)S(1)}, bf16[512,128]{1,0:T(8,128)(2...) custom-call(s32[4096]{0:T(1024)S(1)} %bitcast.18, ...), custom_call_target="tpu_custom_call" | custom-call | flops 5000000000 | bytes 1048576 | tf_op jit(solution)/shard_map/pallas_call | solution.py:383
  59.8 1.2 collective-permute-start.7
  61.0 1.3 collective-permute-start.8
  62.5 2.5 %collective-permute-start.10 = (bf16[512,128]{1,0:T(8,128)(2,1)S(1)}, bf16[512,128]{1,0:T(8,128)(2,1)S(1)}, u32[]{:S(2)}, u32[]{:S(2)}) collective-permute-start(bf16[512,128]{1,0:T(8,128)(2,1)S(1)} %get-tuple-element.61), channel_id=1, source_target_pairs={{0,28},{4,24},{8,20},{12,16},{16,12},{20,8},{24,4},{28,0},{1,29},{... | collective-permute-start | bytes 393224 | tf_op jit(solution)/shard_map/ppermute | solution.py:572
  66.9 3.5 %collective-permute-done.9.refs_4_ = bf16[512,128]{1,0:T(8,128)(2,1)S(1)} collective-permute-done((bf16[512,128]{1,0:T(8,128)(2,1)S(1)}, bf16[512,128]{1,0:T(8,128)(2,1)S(1)}, u32[]{:S(2)}, u32[]{:S(2)}) %collective-permute-start.9) | collective-permute-done | bytes 131104 | tf_op jit(solution)/shard_map/ppermute | solution.py:572
  70.4 3.9 %collective-permute-done.10.refs_5_ = bf16[512,128]{1,0:T(8,128)(2,1)S(1)} collective-permute-done((bf16[512,128]{1,0:T(8,128)(2,1)S(1)}, bf16[512,128]{1,0:T(8,128)(2,1)S(1)}, u32[]{:S(2)}, u32[]{:S(2)}) %collective-permute-start.10) | collective-permute-done | bytes 131104 | tf_op jit(solution)/shard_map/ppermute | solution.py:572
  74.3 1.5 collective-permute-done.11.refs_6_
  76.3 3.6 %shard_map.81 = (bf16[2,256,2048]{2,1,0:T(8,128)(2,1)S(1)}, f32[2,1,2048]{2,1,0:T(1,128)S(1)}) custom-call(f32[512,128]{1,0:T(8,128)S(1)} %broadcast_in_dim.57.time_ref, f32[1,1024]{1,0:T(1,128)S(1)} %bitcast.30, f32[1,1024]{1,0:T(1,128)S(1)} %bitcast.26, bf16[1024,128]{1,0:T(8,128)(2,1)S(1)} %collective-permute-done.7.refs_0_.refs_2_), custom_call_target="tpu_custom_call" | custom-call | flops 1310720000 | bytes 2097152 | tf_op jit(solution)/shard_map/pallas_call | solution.py:91
  79.9 8.7 %shard_map.82 = (bf16[512,128]{1,0:T(8,128)(2,1)S(1)}, bf16[512,128]{1,0:T(8,128)(2,1)S(1)}, bf16[512,128]{1,0:T(8,128)(2,1)S(1)}, bf16[512,128]{1,0:T(8,128)(2,...) custom-call(s32[8,24]{1,0:T(8,128)S(1)} %get-tuple-element.112.src_r, ...), custom_call_target="tpu_custom_call" | custom-call | flops 10737418240 | bytes 8388608 | tf_op jit(solution)/shard_map/pallas_call | solution.py:217
  89.1 1.1 collective-permute-start.15
  90.1 1.2 collective-permute-start.16
  92.1 1.0 collective-permute-start.18
  93.6 2.3 %collective-permute-start.19 = (bf16[512,128]{1,0:T(8,128)(2,1)S(1)}, bf16[512,128]{1,0:T(8,128)(2,1)S(1)}, u32[]{:S(2)}, u32[]{:S(2)}) collective-permute-start(bf16[512,128]{1,0:T(8,128)(2,1)S(1)} %get-tuple-element.77), channel_id=1, source_target_pairs={{0,28},{4,24},{8,20},{12,16},{16,12},{20,8},{24,4},{28,0},{1,29},{... | collective-permute-start | bytes 393224 | tf_op jit(solution)/shard_map/ppermute | solution.py:572
  95.9 1.0 collective-permute-done.16.refs_4_
  97.8 4.5 %shard_map.83.part_ref = f32[4096,128]{1,0:T(8,128)S(1)} custom-call(s32[4096]{0:T(1024)S(1)} %bitcast.19, s32[8]{0:T(128)S(1)} %fusion.4.cnt_ref, s32[2]{0:T(128)S(1)} %pad_add_fusion.where_ref, bf16[4,512,256]{2,1,0:T(8,128)(2,1)S(1)} %copy-done, bf16[512,128]{1,0:T(8,128)(2,1)S(1)} %get-tuple-element.70.refs_0_, ...), custom_call_target="tpu_custom_call" | custom-call | flops 6000000000 | bytes 1048576 | tf_op jit(solution)/shard_map/pallas_call | solution.py:355
  102.4 1.3 collective-permute-done.19.refs_7_
  103.7 6.8 %shard_map.84 = (f32[131072,128]{1,0:T(8,128)}, bf16[512,128]{1,0:T(8,128)(2,1)S(1)}, bf16[512,128]{1,0:T(8,128)(2,1)S(1)}, bf16[1024,128]{1,0:T(8,128)(2,1)S(1)...) custom-call(s32[4096]{0:T(1024)S(1)} %bitcast.20, ...), custom_call_target="tpu_custom_call" | custom-call | flops 7000000000 | bytes 1048576 | tf_op jit(solution)/shard_map/pallas_call | solution.py:440
  110.6 1.1 collective-permute-start.22
  111.7 1.5 collective-permute-start.23
  113.6 1.1 collective-permute-start.25
  114.8 1.1 collective-permute-done.22.refs_3_
  115.9 4.2 %collective-permute-done.23.refs_4_ = bf16[512,128]{1,0:T(8,128)(2,1)S(1)} collective-permute-done((bf16[512,128]{1,0:T(8,128)(2,1)S(1)}, bf16[512,128]{1,0:T(8,128)(2,1)S(1)}, u32[]{:S(2)}, u32[]{:S(2)}) %collective-permute-start.23) | collective-permute-done | bytes 131104 | tf_op jit(solution)/shard_map/ppermute | solution.py:572
  120.1 3.6 %collective-permute-done.24.refs_5_ = bf16[512,128]{1,0:T(8,128)(2,1)S(1)} collective-permute-done((bf16[512,128]{1,0:T(8,128)(2,1)S(1)}, bf16[512,128]{1,0:T(8,128)(2,1)S(1)}, u32[]{:S(2)}, u32[]{:S(2)}) %collective-permute-start.24) | collective-permute-done | bytes 131104 | tf_op jit(solution)/shard_map/ppermute | solution.py:572
  123.7 1.5 collective-permute-done.25.refs_6_
  125.8 1.3 collective-permute-done.20.refs_1_
  127.1 8.0 %shard_map.85 = (bf16[512,128]{1,0:T(8,128)(2,1)S(1)}, bf16[512,128]{1,0:T(8,128)(2,1)S(1)}, bf16[512,128]{1,0:T(8,128)(2,1)S(1)}, bf16[512,128]{1,0:T(8,128)(2,...) custom-call(s32[8,24]{1,0:T(8,128)S(1)} %get-tuple-element.112.src_r, ...), custom_call_target="tpu_custom_call" | custom-call | flops 10737418240 | bytes 8388608 | tf_op jit(solution)/shard_map/pallas_call | solution.py:217
  135.6 1.4 collective-permute-start.29
  137.8 1.0 collective-permute-start.31
  139.6 1.1 collective-permute-start.32
  140.7 2.3 %collective-permute-start.33 = (bf16[512,128]{1,0:T(8,128)(2,1)S(1)}, bf16[512,128]{1,0:T(8,128)(2,1)S(1)}, u32[]{:S(2)}, u32[]{:S(2)}) collective-permute-start(bf16[512,128]{1,0:T(8,128)(2,1)S(1)} %get-tuple-element.94), channel_id=1, source_target_pairs={{0,28},{4,24},{8,20},{12,16},{16,12},{20,8},{24,4},{28,0},{1,29},{... | collective-permute-start | bytes 393224 | tf_op jit(solution)/shard_map/ppermute | solution.py:572
  144.3 4.4 %shard_map.86.part_ref = f32[4096,128]{1,0:T(8,128)S(1)} custom-call(s32[4096]{0:T(1024)S(1)} %bitcast.21, s32[8]{0:T(128)S(1)} %fusion.4.cnt_ref, s32[2]{0:T(128)S(1)} %pad_add_fusion.where_ref, f32[131072,128]{1,0:T(8,128)} %get-tuple-element.78.base_ref, bf16[512,128]{1,0:T(8,128)(2,1)S(1)} %get-tuple-element.87.refs_0_, ...), custom_call_target="tpu_custom_call" | custom-call | flops 6000000000 | bytes 1048576 | tf_op jit(solution)/shard_map/pallas_call | solution.py:355
  148.7 1.7 %collective-permute-done.33.refs_1_ = bf16[512,128]{1,0:T(8,128)(2,1)S(1)} collective-permute-done((bf16[512,128]{1,0:T(8,128)(2,1)S(1)}, bf16[512,128]{1,0:T(8,128)(2,1)S(1)}, u32[]{:S(2)}, u32[]{:S(2)}) %collective-permute-start.33) | collective-permute-done | bytes 131104 | tf_op jit(solution)/shard_map/ppermute | solution.py:572
  150.4 4.1 %shard_map.87 = f32[4,512,256]{2,1,0:T(8,128)} custom-call(s32[4096]{0:T(1024)S(1)} %bitcast.22, s32[8]{0:T(128)S(1)} %fusion.4.cnt_ref, s32[2]{0:T(128)S(1)} %pad_add_fusion.where_ref, f32[4096,128]{1,0:T(8,128)S(1)} %shard_map.86.part_ref, bf16[512,128]{1,0:T(8,128)(2,1)S(1)} %collective-permute-done.32.refs_0_, ...), custom_call_target="tpu_custom_call" | custom-call | flops 4000000000 | bytes 1048576 | tf_op jit(solution)/shard_map/pallas_call | solution.py:482
  (87 shorter events, 16.6 us)
Async XLA Ops:
  0.6 15.9 %collective-permute-start.1 = (bf16[4,128,512]{2,1,0:T(8,128)(2,1)}, bf16[4,128,512]{2,1,0:T(8,128)(2,1)S(1)}, u32[]{:S(2)}, u32[]{:S(2)}) collective-permute-start(bf16[4,128,512]{2,1,0:T(8,128)(2,1)} %own_ref.3), channel_id=1, source_target_pairs={{1,0},{2,1},{3,2},{5,4},{6,5},{7,6},{9,8},{10,9},{11,10},{13,12},{... | collective-permute-start | bytes 1572872 | tf_op jit(solution)/shard_map/ppermute | solution.py:592
  1.9 15.6 %collective-permute-start = (bf16[4,128,512]{2,1,0:T(8,128)(2,1)}, bf16[4,128,512]{2,1,0:T(8,128)(2,1)S(1)}, u32[]{:S(2)}, u32[]{:S(2)}) collective-permute-start(bf16[4,128,512]{2,1,0:T(8,128)(2,1)} %own_ref.3), channel_id=1, source_target_pairs={{0,1},{1,2},{2,3},{4,5},{5,6},{6,7},{8,9},{9,10},{10,11},{12,13},{... | collective-permute-start | bytes 1572872 | tf_op jit(solution)/shard_map/ppermute | solution.py:591
  17.5 5.7 %collective-permute-start.2 = (bf16[4,128,512]{2,1,0:T(8,128)(2,1)S(1)}, bf16[4,128,512]{2,1,0:T(8,128)(2,1)S(1)}, u32[]{:S(2)}, u32[]{:S(2)}) collective-permute-start(bf16[4,128,512]{2,1,0:T(8,128)(2,1)S(1)} %collective-permute-done.refs_0_), channel_id=1, source_target_pairs={{1,2},{2,3},{5,6},{6,7},{9,10},{10,11},{13,14},{14,15},{17,18},{18... | collective-permute-start | bytes 1572872 | tf_op jit(solution)/shard_map/ppermute | solution.py:591
  18.2 16.5 %collective-permute-start.3 = (bf16[4,128,512]{2,1,0:T(8,128)(2,1)S(1)}, bf16[4,128,512]{2,1,0:T(8,128)(2,1)S(1)}, u32[]{:S(2)}, u32[]{:S(2)}) collective-permute-start(bf16[4,128,512]{2,1,0:T(8,128)(2,1)S(1)} %collective-permute-done.1.refs_1_), channel_id=1, source_target_pairs={{1,0},{2,1},{5,4},{6,5},{9,8},{10,9},{13,12},{14,13},{17,16},{18,1... | collective-permute-start | bytes 1572872 | tf_op jit(solution)/shard_map/ppermute | solution.py:592
  22.2 1.0 copy-start.3
  23.1 30.8 %collective-permute-start.4 = (bf16[4,128,512]{2,1,0:T(8,128)(2,1)S(1)}, bf16[4,128,512]{2,1,0:T(8,128)(2,1)}, u32[]{:S(2)}, u32[]{:S(2)}) collective-permute-start(bf16[4,128,512]{2,1,0:T(8,128)(2,1)S(1)} %collective-permute-done.2.refs_0_.refs_2_), channel_id=1, source_target_pairs={{2,3},{6,7},{10,11},{14,15},{18,19},{22,23},{26,27},{30,31}} | collective-permute-start | bytes 1572872 | tf_op jit(solution)/shard_map/ppermute | solution.py:591
  34.6 19.3 %collective-permute-start.5 = (bf16[4,128,512]{2,1,0:T(8,128)(2,1)S(1)}, bf16[4,128,512]{2,1,0:T(8,128)(2,1)}, u32[]{:S(2)}, u32[]{:S(2)}) collective-permute-start(bf16[4,128,512]{2,1,0:T(8,128)(2,1)S(1)} %collective-permute-done.3.refs_1_.refs_3_), channel_id=1, source_target_pairs={{1,0},{5,4},{9,8},{13,12},{17,16},{21,20},{25,24},{29,28}} | collective-permute-start | bytes 1572872 | tf_op jit(solution)/shard_map/ppermute | solution.py:592
  36.6 11.5 %all-to-all-start = ((s32[8,1,512]{2,1,0:T(1,128)}), s32[8,1,512]{2,1,0:T(1,128)S(1)}, u32[]{:S(2)}, u32[]{:S(2)}) async-start(s32[8,1,512]{2,1,0:T(1,128)} %all_to_all.6), calls=%async_computation | async-start | bytes 32768 | tf_op jit(solution)/shard_map/all_to_all | solution.py:621
  46.8 1.3 copy-start.5
  48.5 5.4 %copy-start = (bf16[4,512,256]{2,1,0:T(8,128)(2,1)S(1)}, bf16[4,512,256]{2,1,0:T(8,128)(2,1)}, u32[]{:S(2)}) copy-start(bf16[4,512,256]{2,1,0:T(8,128)(2,1)} %base_ref.3) | copy-start | bytes 3145732
  48.5 5.4 %copy-start.1 = (bf16[4,128,512]{2,1,0:T(8,128)(2,1)S(1)}, bf16[4,128,512]{2,1,0:T(8,128)(2,1)}, u32[]{:S(2)}) copy-start(bf16[4,128,512]{2,1,0:T(8,128)(2,1)} %own_ref.3) | copy-start | bytes 1572868
  48.5 5.4 %copy-start.2 = (s32[4]{0:T(128)S(1)}, s32[4]{0:T(128)}, u32[]{:S(2)}) copy-start(s32[4]{0:T(128)} %count_ref.3) | copy-start | bytes 52
  59.8 16.0 %collective-permute-start.7 = (bf16[1024,128]{1,0:T(8,128)(2,1)S(1)}, bf16[1024,128]{1,0:T(8,128)(2,1)S(1)}, u32[]{:S(2)}, u32[]{:S(2)}) collective-permute-start(bf16[1024,128]{1,0:T(8,128)(2,1)S(1)} %get-tuple-element.58), channel_id=1, source_target_pairs={{0,8},{4,12},{8,0},{12,4},{16,24},{20,28},{24,16},{28,20},{1,9},{5... | collective-permute-start | bytes 786440 | tf_op jit(solution)/shard_map/ppermute | solution.py:572
  61.0 5.1 %collective-permute-start.8 = (bf16[512,128]{1,0:T(8,128)(2,1)S(1)}, bf16[512,128]{1,0:T(8,128)(2,1)S(1)}, u32[]{:S(2)}, u32[]{:S(2)}) collective-permute-start(bf16[512,128]{1,0:T(8,128)(2,1)S(1)} %get-tuple-element.59), channel_id=1, source_target_pairs={{0,16},{4,20},{8,24},{12,28},{16,0},{20,4},{24,8},{28,12},{1,17},{... | collective-permute-start | bytes 393224 | tf_op jit(solution)/shard_map/ppermute | solution.py:572
  62.3 8.1 %collective-permute-start.9 = (bf16[512,128]{1,0:T(8,128)(2,1)S(1)}, bf16[512,128]{1,0:T(8,128)(2,1)S(1)}, u32[]{:S(2)}, u32[]{:S(2)}) collective-permute-start(bf16[512,128]{1,0:T(8,128)(2,1)S(1)} %get-tuple-element.60), channel_id=1, source_target_pairs={{0,24},{4,28},{8,16},{12,20},{16,8},{20,12},{24,0},{28,4},{1,25},{... | collective-permute-start | bytes 393224 | tf_op jit(solution)/shard_map/ppermute | solution.py:572
  62.5 11.8 %collective-permute-start.10 = (bf16[512,128]{1,0:T(8,128)(2,1)S(1)}, bf16[512,128]{1,0:T(8,128)(2,1)S(1)}, u32[]{:S(2)}, u32[]{:S(2)}) collective-permute-start(bf16[512,128]{1,0:T(8,128)(2,1)S(1)} %get-tuple-element.61), channel_id=1, source_target_pairs={{0,28},{4,24},{8,20},{12,16},{16,12},{20,8},{24,4},{28,0},{1,29},{... | collective-permute-start | bytes 393224 | tf_op jit(solution)/shard_map/ppermute | solution.py:572
  65.1 10.7 %collective-permute-start.11 = (bf16[512,128]{1,0:T(8,128)(2,1)S(1)}, bf16[512,128]{1,0:T(8,128)(2,1)S(1)}, u32[]{:S(2)}, u32[]{:S(2)}) collective-permute-start(bf16[512,128]{1,0:T(8,128)(2,1)S(1)} %get-tuple-element.62), channel_id=1, source_target_pairs={{0,20},{4,16},{8,28},{12,24},{16,4},{20,0},{24,12},{28,8},{1,21},{... | collective-permute-start | bytes 393224 | tf_op jit(solution)/shard_map/ppermute | solution.py:572
  66.1 13.8 %collective-permute-start.6 = (bf16[512,128]{1,0:T(8,128)(2,1)S(1)}, bf16[512,128]{1,0:T(8,128)(2,1)S(1)}, u32[]{:S(2)}, u32[]{:S(2)}) collective-permute-start(bf16[512,128]{1,0:T(8,128)(2,1)S(1)} %get-tuple-element.57), channel_id=1, source_target_pairs={{0,4},{4,0},{8,12},{12,8},{16,20},{20,16},{24,28},{28,24},{1,5},{5... | collective-permute-start | bytes 393224 | tf_op jit(solution)/shard_map/ppermute | solution.py:572
  75.8 4.1 %collective-permute-start.12 = (bf16[1024,128]{1,0:T(8,128)(2,1)S(1)}, bf16[1024,128]{1,0:T(8,128)(2,1)S(1)}, u32[]{:S(2)}, u32[]{:S(2)}) collective-permute-start(bf16[1024,128]{1,0:T(8,128)(2,1)S(1)} %collective-permute-done.7.refs_0_.refs_2_), channel_id=1, source_target_pairs={{0,4},{4,0},{8,12},{12,8},{16,20},{20,16},{24,28},{28,24},{1,5},{5... | collective-permute-start | bytes 786440 | tf_op jit(solution)/shard_map/ppermute | solution.py:572
  76.3 3.6 %copy-start.4 = (bf16[1,256,2048]{2,1,0:T(8,128)(2,1)S(1)}, bf16[1,256,2048]{2,1,0:T(8,128)(2,1)}, u32[]{:S(2)}) copy-start(bf16[1,256,2048]{2,1,0:T(8,128)(2,1)} %copy-done.3) | copy-start | bytes 3145732
  76.3 3.6 %copy-start.6 = (bf16[2,256,2048]{2,1,0:T(8,128)(2,1)S(1)}, bf16[2,256,2048]{2,1,0:T(8,128)(2,1)}, u32[]{:S(2)}) copy-start(bf16[2,256,2048]{2,1,0:T(8,128)(2,1)} %copy-done.5) | copy-start | bytes 6291460
  88.7 3.5 %collective-permute-start.13 = (bf16[512,128]{1,0:T(8,128)(2,1)S(1)}, bf16[512,128]{1,0:T(8,128)(2,1)S(1)}, u32[]{:S(2)}, u32[]{:S(2)}) collective-permute-start(bf16[512,128]{1,0:T(8,128)(2,1)S(1)} %get-tuple-element.71), channel_id=1, source_target_pairs={{0,4},{4,0},{8,12},{12,8},{16,20},{20,16},{24,28},{28,24},{1,5},{5... | collective-permute-start | bytes 393224 | tf_op jit(solution)/shard_map/ppermute | solution.py:572
  88.9 4.7 %collective-permute-start.14 = (bf16[512,128]{1,0:T(8,128)(2,1)S(1)}, bf16[512,128]{1,0:T(8,128)(2,1)S(1)}, u32[]{:S(2)}, u32[]{:S(2)}) collective-permute-start(bf16[512,128]{1,0:T(8,128)(2,1)S(1)} %get-tuple-element.72), channel_id=1, source_target_pairs={{0,16},{4,20},{8,24},{12,28},{16,0},{20,4},{24,8},{28,12},{1,17},{... | collective-permute-start | bytes 393224 | tf_op jit(solution)/shard_map/ppermute | solution.py:572
  89.1 6.8 %collective-permute-start.15 = (bf16[512,128]{1,0:T(8,128)(2,1)S(1)}, bf16[512,128]{1,0:T(8,128)(2,1)S(1)}, u32[]{:S(2)}, u32[]{:S(2)}) collective-permute-start(bf16[512,128]{1,0:T(8,128)(2,1)S(1)} %get-tuple-element.73), channel_id=1, source_target_pairs={{0,8},{4,12},{8,0},{12,4},{16,24},{20,28},{24,16},{28,20},{1,9},{5... | collective-permute-start | bytes 393224 | tf_op jit(solution)/shard_map/ppermute | solution.py:572
  90.1 6.8 %collective-permute-start.16 = (bf16[512,128]{1,0:T(8,128)(2,1)S(1)}, bf16[512,128]{1,0:T(8,128)(2,1)S(1)}, u32[]{:S(2)}, u32[]{:S(2)}) collective-permute-start(bf16[512,128]{1,0:T(8,128)(2,1)S(1)} %get-tuple-element.74), channel_id=1, source_target_pairs={{0,20},{4,16},{8,28},{12,24},{16,4},{20,0},{24,12},{28,8},{1,21},{... | collective-permute-start | bytes 393224 | tf_op jit(solution)/shard_map/ppermute | solution.py:572
  91.4 6.5 %collective-permute-start.17 = (bf16[512,128]{1,0:T(8,128)(2,1)S(1)}, bf16[512,128]{1,0:T(8,128)(2,1)S(1)}, u32[]{:S(2)}, u32[]{:S(2)}) collective-permute-start(bf16[512,128]{1,0:T(8,128)(2,1)S(1)} %get-tuple-element.75), channel_id=1, source_target_pairs={{0,12},{4,8},{8,4},{12,0},{16,28},{20,24},{24,20},{28,16},{1,13},{... | collective-permute-start | bytes 393224 | tf_op jit(solution)/shard_map/ppermute | solution.py:572
  92.1 10.3 %collective-permute-start.18 = (bf16[512,128]{1,0:T(8,128)(2,1)S(1)}, bf16[512,128]{1,0:T(8,128)(2,1)S(1)}, u32[]{:S(2)}, u32[]{:S(2)}) collective-permute-start(bf16[512,128]{1,0:T(8,128)(2,1)S(1)} %get-tuple-element.76), channel_id=1, source_target_pairs={{0,24},{4,28},{8,16},{12,20},{16,8},{20,12},{24,0},{28,4},{1,25},{... | collective-permute-start | bytes 393224 | tf_op jit(solution)/shard_map/ppermute | solution.py:572
  93.6 10.1 %collective-permute-start.19 = (bf16[512,128]{1,0:T(8,128)(2,1)S(1)}, bf16[512,128]{1,0:T(8,128)(2,1)S(1)}, u32[]{:S(2)}, u32[]{:S(2)}) collective-permute-start(bf16[512,128]{1,0:T(8,128)(2,1)S(1)} %get-tuple-element.77), channel_id=1, source_target_pairs={{0,28},{4,24},{8,20},{12,16},{16,12},{20,8},{24,4},{28,0},{1,29},{... | collective-permute-start | bytes 393224 | tf_op jit(solution)/shard_map/ppermute | solution.py:572
  110.5 14.7 %collective-permute-start.21 = (bf16[1024,128]{1,0:T(8,128)(2,1)S(1)}, bf16[1024,128]{1,0:T(8,128)(2,1)S(1)}, u32[]{:S(2)}, u32[]{:S(2)}) collective-permute-start(bf16[1024,128]{1,0:T(8,128)(2,1)S(1)} %get-tuple-element.81), channel_id=1, source_target_pairs={{0,8},{4,12},{8,0},{12,4},{16,24},{20,28},{24,16},{28,20},{1,9},{5... | collective-permute-start | bytes 786440 | tf_op jit(solution)/shard_map/ppermute | solution.py:572
  110.6 5.3 %collective-permute-start.22 = (bf16[512,128]{1,0:T(8,128)(2,1)S(1)}, bf16[512,128]{1,0:T(8,128)(2,1)S(1)}, u32[]{:S(2)}, u32[]{:S(2)}) collective-permute-start(bf16[512,128]{1,0:T(8,128)(2,1)S(1)} %get-tuple-element.82), channel_id=1, source_target_pairs={{0,16},{4,20},{8,24},{12,28},{16,0},{20,4},{24,8},{28,12},{1,17},{... | collective-permute-start | bytes 393224 | tf_op jit(solution)/shard_map/ppermute | solution.py:572
  111.7 8.4 %collective-permute-start.23 = (bf16[512,128]{1,0:T(8,128)(2,1)S(1)}, bf16[512,128]{1,0:T(8,128)(2,1)S(1)}, u32[]{:S(2)}, u32[]{:S(2)}) collective-permute-start(bf16[512,128]{1,0:T(8,128)(2,1)S(1)} %get-tuple-element.83), channel_id=1, source_target_pairs={{0,24},{4,28},{8,16},{12,20},{16,8},{20,12},{24,0},{28,4},{1,25},{... | collective-permute-start | bytes 393224 | tf_op jit(solution)/shard_map/ppermute | solution.py:572
  113.2 10.5 %collective-permute-start.24 = (bf16[512,128]{1,0:T(8,128)(2,1)S(1)}, bf16[512,128]{1,0:T(8,128)(2,1)S(1)}, u32[]{:S(2)}, u32[]{:S(2)}) collective-permute-start(bf16[512,128]{1,0:T(8,128)(2,1)S(1)} %get-tuple-element.84), channel_id=1, source_target_pairs={{0,28},{4,24},{8,20},{12,16},{16,12},{20,8},{24,4},{28,0},{1,29},{... | collective-permute-start | bytes 393224 | tf_op jit(solution)/shard_map/ppermute | solution.py:572
  113.6 11.6 %collective-permute-start.25 = (bf16[512,128]{1,0:T(8,128)(2,1)S(1)}, bf16[512,128]{1,0:T(8,128)(2,1)S(1)}, u32[]{:S(2)}, u32[]{:S(2)}) collective-permute-start(bf16[512,128]{1,0:T(8,128)(2,1)S(1)} %get-tuple-element.85), channel_id=1, source_target_pairs={{0,20},{4,16},{8,28},{12,24},{16,4},{20,0},{24,12},{28,8},{1,21},{... | collective-permute-start | bytes 393224 | tf_op jit(solution)/shard_map/ppermute | solution.py:572
  125.2 1.9 %collective-permute-start.26 = (bf16[1024,128]{1,0:T(8,128)(2,1)S(1)}, bf16[1024,128]{1,0:T(8,128)(2,1)S(1)}, u32[]{:S(2)}, u32[]{:S(2)}) collective-permute-start(bf16[1024,128]{1,0:T(8,128)(2,1)S(1)} %collective-permute-done.21.refs_2_), channel_id=1, source_target_pairs={{0,4},{4,0},{8,12},{12,8},{16,20},{20,16},{24,28},{28,24},{1,5},{5... | collective-permute-start | bytes 786440 | tf_op jit(solution)/shard_map/ppermute | solution.py:572
  125.8 1.3 collective-permute-start.20
  135.1 4.5 %collective-permute-start.27 = (bf16[512,128]{1,0:T(8,128)(2,1)S(1)}, bf16[512,128]{1,0:T(8,128)(2,1)S(1)}, u32[]{:S(2)}, u32[]{:S(2)}) collective-permute-start(bf16[512,128]{1,0:T(8,128)(2,1)S(1)} %get-tuple-element.88), channel_id=1, source_target_pairs={{0,4},{4,0},{8,12},{12,8},{16,20},{20,16},{24,28},{28,24},{1,5},{5... | collective-permute-start | bytes 393224 | tf_op jit(solution)/shard_map/ppermute | solution.py:572
  135.6 5.1 %collective-permute-start.28 = (bf16[512,128]{1,0:T(8,128)(2,1)S(1)}, bf16[512,128]{1,0:T(8,128)(2,1)S(1)}, u32[]{:S(2)}, u32[]{:S(2)}) collective-permute-start(bf16[512,128]{1,0:T(8,128)(2,1)S(1)} %get-tuple-element.89), channel_id=1, source_target_pairs={{0,16},{4,20},{8,24},{12,28},{16,0},{20,4},{24,8},{28,12},{1,17},{... | collective-permute-start | bytes 393224 | tf_op jit(solution)/shard_map/ppermute | solution.py:572
  135.6 7.5 %collective-permute-start.29 = (bf16[512,128]{1,0:T(8,128)(2,1)S(1)}, bf16[512,128]{1,0:T(8,128)(2,1)S(1)}, u32[]{:S(2)}, u32[]{:S(2)}) collective-permute-start(bf16[512,128]{1,0:T(8,128)(2,1)S(1)} %get-tuple-element.90), channel_id=1, source_target_pairs={{0,8},{4,12},{8,0},{12,4},{16,24},{20,28},{24,16},{28,20},{1,9},{5... | collective-permute-start | bytes 393224 | tf_op jit(solution)/shard_map/ppermute | solution.py:572
  137.0 6.6 %collective-permute-start.30 = (bf16[512,128]{1,0:T(8,128)(2,1)S(1)}, bf16[512,128]{1,0:T(8,128)(2,1)S(1)}, u32[]{:S(2)}, u32[]{:S(2)}) collective-permute-start(bf16[512,128]{1,0:T(8,128)(2,1)S(1)} %get-tuple-element.91), channel_id=1, source_target_pairs={{0,20},{4,16},{8,28},{12,24},{16,4},{20,0},{24,12},{28,8},{1,21},{... | collective-permute-start | bytes 393224 | tf_op jit(solution)/shard_map/ppermute | solution.py:572
  137.8 6.5 %collective-permute-start.31 = (bf16[512,128]{1,0:T(8,128)(2,1)S(1)}, bf16[512,128]{1,0:T(8,128)(2,1)S(1)}, u32[]{:S(2)}, u32[]{:S(2)}) collective-permute-start(bf16[512,128]{1,0:T(8,128)(2,1)S(1)} %get-tuple-element.92), channel_id=1, source_target_pairs={{0,12},{4,8},{8,4},{12,0},{16,28},{20,24},{24,20},{28,16},{1,13},{... | collective-permute-start | bytes 393224 | tf_op jit(solution)/shard_map/ppermute | solution.py:572
  139.6 9.1 %collective-permute-start.32 = (bf16[512,128]{1,0:T(8,128)(2,1)S(1)}, bf16[512,128]{1,0:T(8,128)(2,1)S(1)}, u32[]{:S(2)}, u32[]{:S(2)}) collective-permute-start(bf16[512,128]{1,0:T(8,128)(2,1)S(1)} %get-tuple-element.93), channel_id=1, source_target_pairs={{0,24},{4,28},{8,16},{12,20},{16,8},{20,12},{24,0},{28,4},{1,25},{... | collective-permute-start | bytes 393224 | tf_op jit(solution)/shard_map/ppermute | solution.py:572
  140.7 9.7 %collective-permute-start.33 = (bf16[512,128]{1,0:T(8,128)(2,1)S(1)}, bf16[512,128]{1,0:T(8,128)(2,1)S(1)}, u32[]{:S(2)}, u32[]{:S(2)}) collective-permute-start(bf16[512,128]{1,0:T(8,128)(2,1)S(1)} %get-tuple-element.94), channel_id=1, source_target_pairs={{0,28},{4,24},{8,20},{12,16},{16,12},{20,8},{24,4},{28,0},{1,29},{... | collective-permute-start | bytes 393224 | tf_op jit(solution)/shard_map/ppermute | solution.py:572

commit v11 on v9

--- a/solution.py
+++ b/solution.py
@@ -22,7 +22,7 @@
 PICK_VMEM = 12 * MIB
 LATE_PICK_VMEM = 18 * MIB
 LATE_VMEM = 12 * MIB
-BASIS_CALLS = (1, 2, 2, 3)
+BASIS_CALLS = (1, 2, 3, 2)
 UNROLL = 32
 PICK_UNROLL = 16
 SUB = 8
@@ -202,7 +202,7 @@
 
 def fit_plans(tables, arrived, parts, norms):
     tm_count = len(arrived)
-    order = [0] + ask_order(tm_count)
+    order = [0] + send_order(tm_count)
     _, obs, twice = parts[0].shape
     sched_dev = norms.shape[0]
     capacity, width = arrived[0].shape
@@ -540,13 +540,6 @@
     return sorted(range(1, count), key=lambda step: (bin(step // 2).count("1"), step % 2, -step))
 
 
-def ask_order(count):
-    first = [1, count // 2]
-    return first + sorted(
-        (step for step in range(2, count) if step not in first), key=lambda step: -bin(step // 2).count("1")
-    )
-
-
 def exchange(blocks):
     count = len(blocks)
     out = list(blocks)

time: 147 us -> 144 us (0.980)
  starting transfers between devices: 48.9 us -> 46.1 us
    ppermute x28, waiting for transfers between devices: 19.1 us -> 22.3 us  [exchange(): lax.ppermute(blocks[step], 'tm', [(i, i ^ step) for i in range(count)])]
    ppermute x28, starting transfers between devices: 33.8 us -> 31 us  [exchange(): lax.ppermute(blocks[step], 'tm', [(i, i ^ step) for i in range(count)])]
    ppermute x3, waiting for transfers between devices: 9.85 us -> 8.04 us  [pass_along(): lax.ppermute(left, 'sky', [(i, i - 1) for i in range(1, count - hop + 1)])]
  transfers between devices with their start and end apart: 35 -> 35, of which waited for: 15 -> 16; matrix products, arithmetic and copies ran while one was open for 7% -> 7% of each run, Pallas kernels for 15% -> 15%
where the time goes in v11:
time: 144 us; the launch traced here: 143 us
  Pallas kernels  50 us (35%)
  starting transfers between devices  46.1 us (32%)
  waiting for transfers between devices  34.4 us (24%)
  other arithmetic  9.49 us (7%)
  local copies, waits for them, and re-layouts  2.14 us (1%)
    ppermute x28, starting transfers between devices, exchange(): lax.ppermute(blocks[step], 'tm', [(i, i ^ step) for i in range(count)])  31 us
    ppermute x28, waiting for transfers between devices, exchange(): lax.ppermute(blocks[step], 'tm', [(i, i ^ step) for i in range(count)])  22.3 us
    pallas_call x2, Pallas kernels, fit_plans(): pl.pallas_call(functools.partial(fit_kernel, order), in_specs=[SMEM, SMEM...  16.7 us
    pallas_call x4, Pallas kernels, make_basis(): pl.pallas_call(functools.partial(basis_kernel, len(after)), grid=(sched_d...  14.3 us
    ppermute x3, waiting for transfers between devices, pass_along(): lax.ppermute(left, 'sky', [(i, i - 1) for i in range(1, count - hop + 1)])  8.04 us
    pallas_call x2, Pallas kernels, place_early(): pl.pallas_call(functools.partial(early_kernel, owners, table_base), in_sp...  7.28 us
    ppermute x3, starting transfers between devices, pass_along(): lax.ppermute(right, 'sky', [(i, i + 1) for i in range(hop - 1, count - 1)])  6.08 us
    all_to_all x1, starting transfers between devices, first_hop(): asked = lax.all_to_all(held, 'tm', split_axis=0, concat_axis=0, tiled=True)  5.1 us
  transfers between devices with their start and end apart: 35, of which 16 were waited for; matrix products, arithmetic and copies ran while one was open for 7% of the time, Pallas kernels for 15%

profile of v11, /device:TPU:1, one launch (start us, length us, event | category | flops | bytes accessed | tf_op | source)
XLA Modules:
  0.0 143.3 jit_solution(18092583464474908156)
XLA Ops:
  0.6 1.3 collective-permute-start.1
  1.9 4.7 %collective-permute-start = (bf16[4,128,512]{2,1,0:T(8,128)(2,1)}, bf16[4,128,512]{2,1,0:T(8,128)(2,1)S(1)}, u32[]{:S(2)}, u32[]{:S(2)}) collective-permute-start(bf16[4,128,512]{2,1,0:T(8,128)(2,1)} %own_ref.3), channel_id=1, source_target_pairs={{0,1},{1,2},{2,3},{4,5},{5,6},{6,7},{8,9},{9,10},{10,11},{12,13},{... | collective-permute-start | bytes 1572872 | tf_op jit(solution)/shard_map/ppermute | solution.py:556
  11.6 3.4 %select_reduce_fusion = s32[4096]{0:T(1024)S(1)} fusion(s32[2048]{0:T(1024)S(1)} %bitcast.34, s32[2048]{0:T(1024)S(1)} %bitcast.33), kind=kLoop, calls=%fused_computation | loop fusion | flops 25161728 | bytes 32768 | tf_op jit(solution)/shard_map/reduce_sum | solution.py:518
  15.2 1.3 collective-permute-done.1.refs_1_
  16.5 1.3 collective-permute-start.3
  18.6 1.8 %shard_map.77 = (bf16[1,256,2048]{2,1,0:T(8,128)(2,1)S(1)}, f32[1,1,2048]{2,1,0:T(1,128)S(1)}) custom-call(f32[256,128]{1,0:T(8,128)S(1)} %broadcast_in_dim.50.time_ref, f32[1,1024]{1,0:T(1,128)S(1)} %bitcast.27, f32[1,1024]{1,0:T(1,128)S(1)} %bitcast.23, bf16[4,128,512]{2,1,0:T(8,128)(2,1)S(1)} %collective-permute-done.refs_0_, ...), custom_call_target="tpu_custom_call" | custom-call | flops 2097152000 | bytes 1048576 | tf_op jit(solution)/shard_map/pallas_call | solution.py:91
  20.4 1.0 copy-done.3
  22.0 5.1 %all-to-all-start = ((s32[8,1,512]{2,1,0:T(1,128)}), s32[8,1,512]{2,1,0:T(1,128)S(1)}, u32[]{:S(2)}, u32[]{:S(2)}) async-start(s32[8,1,512]{2,1,0:T(1,128)} %all_to_all.6), calls=%async_computation | async-start | bytes 32768 | tf_op jit(solution)/shard_map/all_to_all | solution.py:585
  27.1 4.0 %all-to-all-done = s32[8,1,512]{2,1,0:T(1,128)S(1)} async-done(((s32[8,1,512]{2,1,0:T(1,128)}), s32[8,1,512]{2,1,0:T(1,128)S(1)}, u32[]{:S(2)}, u32[]{:S(2)}) %all-to-all-start) | async-done | bytes 16416 | tf_op jit(solution)/shard_map/all_to_all | solution.py:585
  31.4 1.3 collective-permute-start.5
  33.5 5.3 %shard_map.80 = (bf16[3,256,2048]{2,1,0:T(8,128)(2,1)S(1)}, f32[3,1,2048]{2,1,0:T(1,128)S(1)}) custom-call(f32[768,128]{1,0:T(8,128)S(1)} %broadcast_in_dim.55.time_ref, f32[1,1024]{1,0:T(1,128)S(1)} %bitcast.28, f32[1,1024]{1,0:T(1,128)S(1)} %bitcast.24, bf16[4,128,512]{2,1,0:T(8,128)(2,1)S(1)} %collective-permute-done.2.refs_2_.refs_0_, ...), custom_call_target="tpu_custom_call" | custom-call | flops 6291456000 | bytes 3145728 | tf_op jit(solution)/shard_map/pallas_call | solution.py:91
  39.0 3.6 %shard_map.79 = (bf16[2,256,2048]{2,1,0:T(8,128)(2,1)S(1)}, f32[2,1,2048]{2,1,0:T(1,128)S(1)}) custom-call(f32[512,128]{1,0:T(8,128)S(1)} %broadcast_in_dim.53.time_ref, f32[1,1024]{1,0:T(1,128)S(1)} %bitcast.29, f32[1,1024]{1,0:T(1,128)S(1)} %bitcast.25, bf16[4,128,512]{2,1,0:T(8,128)(2,1)S(1)} %collective-permute-done.2.refs_2_.refs_0_, ...), custom_call_target="tpu_custom_call" | custom-call | flops 4194304000 | bytes 2097152 | tf_op jit(solution)/shard_map/pallas_call | solution.py:91
  42.7 6.8 %collective-permute-done.5.refs_5_ = bf16[4,128,512]{2,1,0:T(8,128)(2,1)S(1)} collective-permute-done((bf16[4,128,512]{2,1,0:T(8,128)(2,1)S(1)}, bf16[4,128,512]{2,1,0:T(8,128)(2,1)S(1)}, u32[]{:S(2)}, u32[]{:S(2)}) %collective-permute-start.5) | collective-permute-done | bytes 524320 | tf_op jit(solution)/shard_map/ppermute | solution.py:557
  49.4 3.8 %shard_map.78 = (bf16[512,128]{1,0:T(8,128)(2,1)S(1)}, bf16[512,128]{1,0:T(8,128)(2,1)S(1)}, bf16[512,128]{1,0:T(8,128)(2,1)S(1)}, bf16[512,128]{1,0:T(8,128)(2,...) custom-call(s32[4096]{0:T(1024)S(1)} %bitcast.18, ...), custom_call_target="tpu_custom_call" | custom-call | flops 5000000000 | bytes 1048576 | tf_op jit(solution)/shard_map/pallas_call | solution.py:379
  53.2 2.1 %collective-permute-start.6 = (bf16[512,128]{1,0:T(8,128)(2,1)S(1)}, bf16[512,128]{1,0:T(8,128)(2,1)S(1)}, u32[]{:S(2)}, u32[]{:S(2)}) collective-permute-start(bf16[512,128]{1,0:T(8,128)(2,1)S(1)} %get-tuple-element.48), channel_id=1, source_target_pairs={{0,4},{4,0},{8,12},{12,8},{16,20},{20,16},{24,28},{28,24},{1,5},{5... | collective-permute-start | bytes 393224 | tf_op jit(solution)/shard_map/ppermute | solution.py:547
  56.2 1.6 %collective-permute-start.9 = (bf16[512,128]{1,0:T(8,128)(2,1)S(1)}, bf16[512,128]{1,0:T(8,128)(2,1)S(1)}, u32[]{:S(2)}, u32[]{:S(2)}) collective-permute-start(bf16[512,128]{1,0:T(8,128)(2,1)S(1)} %get-tuple-element.51), channel_id=1, source_target_pairs={{0,20},{4,16},{8,28},{12,24},{16,4},{20,0},{24,12},{28,8},{1,21},{... | collective-permute-start | bytes 393224 | tf_op jit(solution)/shard_map/ppermute | solution.py:547
  58.6 3.6 %shard_map.81 = (bf16[2,256,2048]{2,1,0:T(8,128)(2,1)S(1)}, f32[2,1,2048]{2,1,0:T(1,128)S(1)}) custom-call(f32[512,128]{1,0:T(8,128)S(1)} %broadcast_in_dim.57.time_ref, f32[1,1024]{1,0:T(1,128)S(1)} %bitcast.30, f32[1,1024]{1,0:T(1,128)S(1)} %bitcast.26, bf16[512,128]{1,0:T(8,128)(2,1)S(1)} %get-tuple-element.47.refs_0_), custom_call_target="tpu_custom_call" | custom-call | flops 4194304000 | bytes 2097152 | tf_op jit(solution)/shard_map/pallas_call | solution.py:91
  63.0 2.5 %collective-permute-start.12 = (bf16[512,128]{1,0:T(8,128)(2,1)S(1)}, bf16[512,128]{1,0:T(8,128)(2,1)S(1)}, u32[]{:S(2)}, u32[]{:S(2)}) collective-permute-start(bf16[512,128]{1,0:T(8,128)(2,1)S(1)} %get-tuple-element.54), channel_id=1, source_target_pairs={{0,28},{4,24},{8,20},{12,16},{16,12},{20,8},{24,4},{28,0},{1,29},{... | collective-permute-start | bytes 393224 | tf_op jit(solution)/shard_map/ppermute | solution.py:547
  65.5 2.1 %collective-permute-done.11.refs_6_ = bf16[512,128]{1,0:T(8,128)(2,1)S(1)} collective-permute-done((bf16[512,128]{1,0:T(8,128)(2,1)S(1)}, bf16[512,128]{1,0:T(8,128)(2,1)S(1)}, u32[]{:S(2)}, u32[]{:S(2)}) %collective-permute-start.11) | collective-permute-done | bytes 131104 | tf_op jit(solution)/shard_map/ppermute | solution.py:547
  67.6 3.6 %collective-permute-done.12.refs_7_ = bf16[512,128]{1,0:T(8,128)(2,1)S(1)} collective-permute-done((bf16[512,128]{1,0:T(8,128)(2,1)S(1)}, bf16[512,128]{1,0:T(8,128)(2,1)S(1)}, u32[]{:S(2)}, u32[]{:S(2)}) %collective-permute-start.12) | collective-permute-done | bytes 131104 | tf_op jit(solution)/shard_map/ppermute | solution.py:547
  71.2 8.7 %shard_map.82 = (bf16[512,128]{1,0:T(8,128)(2,1)S(1)}, bf16[512,128]{1,0:T(8,128)(2,1)S(1)}, bf16[512,128]{1,0:T(8,128)(2,1)S(1)}, bf16[512,128]{1,0:T(8,128)(2,...) custom-call(s32[8,24]{1,0:T(8,128)S(1)} %get-tuple-element.104.src_r, ...), custom_call_target="tpu_custom_call" | custom-call | flops 10737418240 | bytes 8388608 | tf_op jit(solution)/shard_map/pallas_call | solution.py:217
  80.5 1.0 collective-permute-start.15
  81.4 1.4 %collective-permute-start.16 = (bf16[512,128]{1,0:T(8,128)(2,1)S(1)}, bf16[512,128]{1,0:T(8,128)(2,1)S(1)}, u32[]{:S(2)}, u32[]{:S(2)}) collective-permute-start(bf16[512,128]{1,0:T(8,128)(2,1)S(1)} %get-tuple-element.66), channel_id=1, source_target_pairs={{0,20},{4,16},{8,28},{12,24},{16,4},{20,0},{24,12},{28,8},{1,21},{... | collective-permute-start | bytes 393224 | tf_op jit(solution)/shard_map/ppermute | solution.py:547
  83.3 1.1 collective-permute-start.18
  84.7 2.5 %collective-permute-start.19 = (bf16[512,128]{1,0:T(8,128)(2,1)S(1)}, bf16[512,128]{1,0:T(8,128)(2,1)S(1)}, u32[]{:S(2)}, u32[]{:S(2)}) collective-permute-start(bf16[512,128]{1,0:T(8,128)(2,1)S(1)} %get-tuple-element.69), channel_id=1, source_target_pairs={{0,28},{4,24},{8,20},{12,16},{16,12},{20,8},{24,4},{28,0},{1,29},{... | collective-permute-start | bytes 393224 | tf_op jit(solution)/shard_map/ppermute | solution.py:547
  87.2 0.9 collective-permute-done.16.refs_4_
  88.1 1.3 collective-permute-done.17.refs_5_
  89.4 3.7 %shard_map.83.part_ref = f32[4096,128]{1,0:T(8,128)S(1)} custom-call(s32[4096]{0:T(1024)S(1)} %bitcast.19, s32[8]{0:T(128)S(1)} %fusion.4.cnt_ref, s32[2]{0:T(128)S(1)} %pad_add_fusion.where_ref, bf16[4,512,256]{2,1,0:T(8,128)(2,1)S(1)} %copy-done, bf16[512,128]{1,0:T(8,128)(2,1)S(1)} %get-tuple-element.62.refs_0_, ...), custom_call_target="tpu_custom_call" | custom-call | flops 6000000000 | bytes 1048576 | tf_op jit(solution)/shard_map/pallas_call | solution.py:351
  93.1 1.8 %collective-permute-done.19.refs_7_ = bf16[512,128]{1,0:T(8,128)(2,1)S(1)} collective-permute-done((bf16[512,128]{1,0:T(8,128)(2,1)S(1)}, bf16[512,128]{1,0:T(8,128)(2,1)S(1)}, u32[]{:S(2)}, u32[]{:S(2)}) %collective-permute-start.19) | collective-permute-done | bytes 131104 | tf_op jit(solution)/shard_map/ppermute | solution.py:547
  94.9 4.8 %shard_map.84 = (f32[131072,128]{1,0:T(8,128)}, bf16[512,128]{1,0:T(8,128)(2,1)S(1)}, bf16[512,128]{1,0:T(8,128)(2,1)S(1)}, bf16[512,128]{1,0:T(8,128)(2,1)S(1)}...) custom-call(s32[4096]{0:T(1024)S(1)} %bitcast.20, ...), custom_call_target="tpu_custom_call" | custom-call | flops 7000000000 | bytes 1048576 | tf_op jit(solution)/shard_map/pallas_call | solution.py:436
  100.3 3.1 %collective-permute-start.21 = (bf16[512,128]{1,0:T(8,128)(2,1)S(1)}, bf16[512,128]{1,0:T(8,128)(2,1)S(1)}, u32[]{:S(2)}, u32[]{:S(2)}) collective-permute-start(bf16[512,128]{1,0:T(8,128)(2,1)S(1)} %get-tuple-element.73), channel_id=1, source_target_pairs={{0,16},{4,20},{8,24},{12,28},{16,0},{20,4},{24,8},{28,12},{1,17},{... | collective-permute-start | bytes 393224 | tf_op jit(solution)/shard_map/ppermute | solution.py:547
  103.7 2.0 %collective-permute-start.24 = (bf16[512,128]{1,0:T(8,128)(2,1)S(1)}, bf16[512,128]{1,0:T(8,128)(2,1)S(1)}, u32[]{:S(2)}, u32[]{:S(2)}) collective-permute-start(bf16[512,128]{1,0:T(8,128)(2,1)S(1)} %get-tuple-element.76), channel_id=1, source_target_pairs={{0,12},{4,8},{8,4},{12,0},{16,28},{20,24},{24,20},{28,16},{1,13},{... | collective-permute-start | bytes 393224 | tf_op jit(solution)/shard_map/ppermute | solution.py:547
  105.7 1.2 collective-permute-start.25
  106.9 1.4 collective-permute-start.26
  108.4 1.9 %collective-permute-done.23.refs_4_ = bf16[512,128]{1,0:T(8,128)(2,1)S(1)} collective-permute-done((bf16[512,128]{1,0:T(8,128)(2,1)S(1)}, bf16[512,128]{1,0:T(8,128)(2,1)S(1)}, u32[]{:S(2)}, u32[]{:S(2)}) %collective-permute-start.23) | collective-permute-done | bytes 131104 | tf_op jit(solution)/shard_map/ppermute | solution.py:547
  110.2 2.7 %collective-permute-done.24.refs_5_ = bf16[512,128]{1,0:T(8,128)(2,1)S(1)} collective-permute-done((bf16[512,128]{1,0:T(8,128)(2,1)S(1)}, bf16[512,128]{1,0:T(8,128)(2,1)S(1)}, u32[]{:S(2)}, u32[]{:S(2)}) %collective-permute-start.24) | collective-permute-done | bytes 131104 | tf_op jit(solution)/shard_map/ppermute | solution.py:547
  112.9 0.9 collective-permute-done.25.refs_6_
  113.8 3.0 %collective-permute-done.26.refs_7_ = bf16[512,128]{1,0:T(8,128)(2,1)S(1)} collective-permute-done((bf16[512,128]{1,0:T(8,128)(2,1)S(1)}, bf16[512,128]{1,0:T(8,128)(2,1)S(1)}, u32[]{:S(2)}, u32[]{:S(2)}) %collective-permute-start.26) | collective-permute-done | bytes 131104 | tf_op jit(solution)/shard_map/ppermute | solution.py:547
  116.8 8.0 %shard_map.85 = (bf16[512,128]{1,0:T(8,128)(2,1)S(1)}, bf16[512,128]{1,0:T(8,128)(2,1)S(1)}, bf16[512,128]{1,0:T(8,128)(2,1)S(1)}, bf16[512,128]{1,0:T(8,128)(2,...) custom-call(s32[8,24]{1,0:T(8,128)S(1)} %get-tuple-element.104.src_r, ...), custom_call_target="tpu_custom_call" | custom-call | flops 10737418240 | bytes 8388608 | tf_op jit(solution)/shard_map/pallas_call | solution.py:217
  125.1 1.3 collective-permute-start.28
  126.6 1.1 collective-permute-start.30
  127.7 1.1 collective-permute-start.31
  128.7 0.8 reduce.1
  129.5 1.2 collective-permute-start.32
  130.7 1.9 %collective-permute-start.33 = (bf16[512,128]{1,0:T(8,128)(2,1)S(1)}, bf16[512,128]{1,0:T(8,128)(2,1)S(1)}, u32[]{:S(2)}, u32[]{:S(2)}) collective-permute-start(bf16[512,128]{1,0:T(8,128)(2,1)S(1)} %get-tuple-element.86), channel_id=1, source_target_pairs={{0,28},{4,24},{8,20},{12,16},{16,12},{20,8},{24,4},{28,0},{1,29},{... | collective-permute-start | bytes 393224 | tf_op jit(solution)/shard_map/ppermute | solution.py:547
  133.4 2.5 %collective-permute-done.31.refs_5_ = bf16[512,128]{1,0:T(8,128)(2,1)S(1)} collective-permute-done((bf16[512,128]{1,0:T(8,128)(2,1)S(1)}, bf16[512,128]{1,0:T(8,128)(2,1)S(1)}, u32[]{:S(2)}, u32[]{:S(2)}) %collective-permute-start.31) | collective-permute-done | bytes 131104 | tf_op jit(solution)/shard_map/ppermute | solution.py:547
  135.9 3.6 %shard_map.86.part_ref = f32[4096,128]{1,0:T(8,128)S(1)} custom-call(s32[4096]{0:T(1024)S(1)} %bitcast.21, s32[8]{0:T(128)S(1)} %fusion.4.cnt_ref, s32[2]{0:T(128)S(1)} %pad_add_fusion.where_ref, f32[131072,128]{1,0:T(8,128)} %get-tuple-element.70.base_ref, bf16[512,128]{1,0:T(8,128)(2,1)S(1)} %get-tuple-element.79.refs_0_, ...), custom_call_target="tpu_custom_call" | custom-call | flops 6000000000 | bytes 1048576 | tf_op jit(solution)/shard_map/pallas_call | solution.py:351
  140.0 3.2 %shard_map.87 = f32[4,512,256]{2,1,0:T(8,128)} custom-call(s32[4096]{0:T(1024)S(1)} %bitcast.22, s32[8]{0:T(128)S(1)} %fusion.4.cnt_ref, s32[2]{0:T(128)S(1)} %pad_add_fusion.where_ref, f32[4096,128]{1,0:T(8,128)S(1)} %shard_map.86.part_ref, bf16[512,128]{1,0:T(8,128)(2,1)S(1)} %collective-permute-done.32.refs_0_, ...), custom_call_target="tpu_custom_call" | custom-call | flops 4000000000 | bytes 1048576 | tf_op jit(solution)/shard_map/pallas_call | solution.py:478
  (83 shorter events, 14.3 us)
Async XLA Ops:
  0.6 15.9 %collective-permute-start.1 = (bf16[4,128,512]{2,1,0:T(8,128)(2,1)}, bf16[4,128,512]{2,1,0:T(8,128)(2,1)S(1)}, u32[]{:S(2)}, u32[]{:S(2)}) collective-permute-start(bf16[4,128,512]{2,1,0:T(8,128)(2,1)} %own_ref.3), channel_id=1, source_target_pairs={{1,0},{2,1},{3,2},{5,4},{6,5},{7,6},{9,8},{10,9},{11,10},{13,12},{... | collective-permute-start | bytes 1572872 | tf_op jit(solution)/shard_map/ppermute | solution.py:557
  1.9 15.9 %collective-permute-start = (bf16[4,128,512]{2,1,0:T(8,128)(2,1)}, bf16[4,128,512]{2,1,0:T(8,128)(2,1)S(1)}, u32[]{:S(2)}, u32[]{:S(2)}) collective-permute-start(bf16[4,128,512]{2,1,0:T(8,128)(2,1)} %own_ref.3), channel_id=1, source_target_pairs={{0,1},{1,2},{2,3},{4,5},{5,6},{6,7},{8,9},{9,10},{10,11},{12,13},{... | collective-permute-start | bytes 1572872 | tf_op jit(solution)/shard_map/ppermute | solution.py:556
  16.5 14.8 %collective-permute-start.3 = (bf16[4,128,512]{2,1,0:T(8,128)(2,1)S(1)}, bf16[4,128,512]{2,1,0:T(8,128)(2,1)S(1)}, u32[]{:S(2)}, u32[]{:S(2)}) collective-permute-start(bf16[4,128,512]{2,1,0:T(8,128)(2,1)S(1)} %collective-permute-done.1.refs_1_), channel_id=1, source_target_pairs={{1,0},{2,1},{5,4},{6,5},{9,8},{10,9},{13,12},{14,13},{17,16},{18,1... | collective-permute-start | bytes 1572872 | tf_op jit(solution)/shard_map/ppermute | solution.py:557
  17.8 14.8 %collective-permute-start.2 = (bf16[4,128,512]{2,1,0:T(8,128)(2,1)S(1)}, bf16[4,128,512]{2,1,0:T(8,128)(2,1)S(1)}, u32[]{:S(2)}, u32[]{:S(2)}) collective-permute-start(bf16[4,128,512]{2,1,0:T(8,128)(2,1)S(1)} %collective-permute-done.refs_0_), channel_id=1, source_target_pairs={{1,2},{2,3},{5,6},{6,7},{9,10},{10,11},{13,14},{14,15},{17,18},{18... | collective-permute-start | bytes 1572872 | tf_op jit(solution)/shard_map/ppermute | solution.py:556
  20.4 1.0 copy-start.3
  22.0 9.1 %all-to-all-start = ((s32[8,1,512]{2,1,0:T(1,128)}), s32[8,1,512]{2,1,0:T(1,128)S(1)}, u32[]{:S(2)}, u32[]{:S(2)}) async-start(s32[8,1,512]{2,1,0:T(1,128)} %all_to_all.6), calls=%async_computation | async-start | bytes 32768 | tf_op jit(solution)/shard_map/all_to_all | solution.py:585
  31.4 18.1 %collective-permute-start.5 = (bf16[4,128,512]{2,1,0:T(8,128)(2,1)S(1)}, bf16[4,128,512]{2,1,0:T(8,128)(2,1)S(1)}, u32[]{:S(2)}, u32[]{:S(2)}) collective-permute-start(bf16[4,128,512]{2,1,0:T(8,128)(2,1)S(1)} %collective-permute-done.3.refs_3_.refs_1_), channel_id=1, source_target_pairs={{1,0},{5,4},{9,8},{13,12},{17,16},{21,20},{25,24},{29,28}} | collective-permute-start | bytes 1572872 | tf_op jit(solution)/shard_map/ppermute | solution.py:557
  32.7 16.8 %collective-permute-start.4 = (bf16[4,128,512]{2,1,0:T(8,128)(2,1)S(1)}, bf16[4,128,512]{2,1,0:T(8,128)(2,1)S(1)}, u32[]{:S(2)}, u32[]{:S(2)}) collective-permute-start(bf16[4,128,512]{2,1,0:T(8,128)(2,1)S(1)} %collective-permute-done.2.refs_2_.refs_0_), channel_id=1, source_target_pairs={{2,3},{6,7},{10,11},{14,15},{18,19},{22,23},{26,27},{30,31}} | collective-permute-start | bytes 1572872 | tf_op jit(solution)/shard_map/ppermute | solution.py:556
  39.0 10.4 %copy-start = (bf16[4,512,256]{2,1,0:T(8,128)(2,1)S(1)}, bf16[4,512,256]{2,1,0:T(8,128)(2,1)}, u32[]{:S(2)}) copy-start(bf16[4,512,256]{2,1,0:T(8,128)(2,1)} %base_ref.3) | copy-start | bytes 3145732
  39.0 10.4 %copy-start.1 = (bf16[4,128,512]{2,1,0:T(8,128)(2,1)S(1)}, bf16[4,128,512]{2,1,0:T(8,128)(2,1)}, u32[]{:S(2)}) copy-start(bf16[4,128,512]{2,1,0:T(8,128)(2,1)} %own_ref.3) | copy-start | bytes 1572868
  39.0 10.4 %copy-start.2 = (s32[4]{0:T(128)S(1)}, s32[4]{0:T(128)}, u32[]{:S(2)}) copy-start(s32[4]{0:T(128)} %count_ref.3) | copy-start | bytes 52
  53.2 9.0 %collective-permute-start.6 = (bf16[512,128]{1,0:T(8,128)(2,1)S(1)}, bf16[512,128]{1,0:T(8,128)(2,1)S(1)}, u32[]{:S(2)}, u32[]{:S(2)}) collective-permute-start(bf16[512,128]{1,0:T(8,128)(2,1)S(1)} %get-tuple-element.48), channel_id=1, source_target_pairs={{0,4},{4,0},{8,12},{12,8},{16,20},{20,16},{24,28},{28,24},{1,5},{5... | collective-permute-start | bytes 393224 | tf_op jit(solution)/shard_map/ppermute | solution.py:547
  55.3 7.7 %collective-permute-start.7 = (bf16[512,128]{1,0:T(8,128)(2,1)S(1)}, bf16[512,128]{1,0:T(8,128)(2,1)S(1)}, u32[]{:S(2)}, u32[]{:S(2)}) collective-permute-start(bf16[512,128]{1,0:T(8,128)(2,1)S(1)} %get-tuple-element.49), channel_id=1, source_target_pairs={{0,16},{4,20},{8,24},{12,28},{16,0},{20,4},{24,8},{28,12},{1,17},{... | collective-permute-start | bytes 393224 | tf_op jit(solution)/shard_map/ppermute | solution.py:547
  55.6 9.8 %collective-permute-start.8 = (bf16[512,128]{1,0:T(8,128)(2,1)S(1)}, bf16[512,128]{1,0:T(8,128)(2,1)S(1)}, u32[]{:S(2)}, u32[]{:S(2)}) collective-permute-start(bf16[512,128]{1,0:T(8,128)(2,1)S(1)} %get-tuple-element.50), channel_id=1, source_target_pairs={{0,8},{4,12},{8,0},{12,4},{16,24},{20,28},{24,16},{28,20},{1,9},{5... | collective-permute-start | bytes 393224 | tf_op jit(solution)/shard_map/ppermute | solution.py:547
  56.2 9.3 %collective-permute-start.9 = (bf16[512,128]{1,0:T(8,128)(2,1)S(1)}, bf16[512,128]{1,0:T(8,128)(2,1)S(1)}, u32[]{:S(2)}, u32[]{:S(2)}) collective-permute-start(bf16[512,128]{1,0:T(8,128)(2,1)S(1)} %get-tuple-element.51), channel_id=1, source_target_pairs={{0,20},{4,16},{8,28},{12,24},{16,4},{20,0},{24,12},{28,8},{1,21},{... | collective-permute-start | bytes 393224 | tf_op jit(solution)/shard_map/ppermute | solution.py:547
  57.7 7.8 %collective-permute-start.10 = (bf16[512,128]{1,0:T(8,128)(2,1)S(1)}, bf16[512,128]{1,0:T(8,128)(2,1)S(1)}, u32[]{:S(2)}, u32[]{:S(2)}) collective-permute-start(bf16[512,128]{1,0:T(8,128)(2,1)S(1)} %get-tuple-element.52), channel_id=1, source_target_pairs={{0,12},{4,8},{8,4},{12,0},{16,28},{20,24},{24,20},{28,16},{1,13},{... | collective-permute-start | bytes 393224 | tf_op jit(solution)/shard_map/ppermute | solution.py:547
  58.6 12.6 %copy-start.4 = (bf16[1,256,2048]{2,1,0:T(8,128)(2,1)S(1)}, bf16[1,256,2048]{2,1,0:T(8,128)(2,1)}, u32[]{:S(2)}) copy-start(bf16[1,256,2048]{2,1,0:T(8,128)(2,1)} %copy-done.3) | copy-start | bytes 3145732
  62.2 5.4 %collective-permute-start.11 = (bf16[512,128]{1,0:T(8,128)(2,1)S(1)}, bf16[512,128]{1,0:T(8,128)(2,1)S(1)}, u32[]{:S(2)}, u32[]{:S(2)}) collective-permute-start(bf16[512,128]{1,0:T(8,128)(2,1)S(1)} %get-tuple-element.53), channel_id=1, source_target_pairs={{0,24},{4,28},{8,16},{12,20},{16,8},{20,12},{24,0},{28,4},{1,25},{... | collective-permute-start | bytes 393224 | tf_op jit(solution)/shard_map/ppermute | solution.py:547
  63.0 8.3 %collective-permute-start.12 = (bf16[512,128]{1,0:T(8,128)(2,1)S(1)}, bf16[512,128]{1,0:T(8,128)(2,1)S(1)}, u32[]{:S(2)}, u32[]{:S(2)}) collective-permute-start(bf16[512,128]{1,0:T(8,128)(2,1)S(1)} %get-tuple-element.54), channel_id=1, source_target_pairs={{0,28},{4,24},{8,20},{12,16},{16,12},{20,8},{24,4},{28,0},{1,29},{... | collective-permute-start | bytes 393224 | tf_op jit(solution)/shard_map/ppermute | solution.py:547
  79.9 3.4 %collective-permute-start.13 = (bf16[512,128]{1,0:T(8,128)(2,1)S(1)}, bf16[512,128]{1,0:T(8,128)(2,1)S(1)}, u32[]{:S(2)}, u32[]{:S(2)}) collective-permute-start(bf16[512,128]{1,0:T(8,128)(2,1)S(1)} %get-tuple-element.63), channel_id=1, source_target_pairs={{0,4},{4,0},{8,12},{12,8},{16,20},{20,16},{24,28},{28,24},{1,5},{5... | collective-permute-start | bytes 393224 | tf_op jit(solution)/shard_map/ppermute | solution.py:547
  80.0 4.7 %collective-permute-start.14 = (bf16[512,128]{1,0:T(8,128)(2,1)S(1)}, bf16[512,128]{1,0:T(8,128)(2,1)S(1)}, u32[]{:S(2)}, u32[]{:S(2)}) collective-permute-start(bf16[512,128]{1,0:T(8,128)(2,1)S(1)} %get-tuple-element.64), channel_id=1, source_target_pairs={{0,16},{4,20},{8,24},{12,28},{16,0},{20,4},{24,8},{28,12},{1,17},{... | collective-permute-start | bytes 393224 | tf_op jit(solution)/shard_map/ppermute | solution.py:547
  80.5 6.7 %collective-permute-start.15 = (bf16[512,128]{1,0:T(8,128)(2,1)S(1)}, bf16[512,128]{1,0:T(8,128)(2,1)S(1)}, u32[]{:S(2)}, u32[]{:S(2)}) collective-permute-start(bf16[512,128]{1,0:T(8,128)(2,1)S(1)} %get-tuple-element.65), channel_id=1, source_target_pairs={{0,8},{4,12},{8,0},{12,4},{16,24},{20,28},{24,16},{28,20},{1,9},{5... | collective-permute-start | bytes 393224 | tf_op jit(solution)/shard_map/ppermute | solution.py:547
  81.4 6.7 %collective-permute-start.16 = (bf16[512,128]{1,0:T(8,128)(2,1)S(1)}, bf16[512,128]{1,0:T(8,128)(2,1)S(1)}, u32[]{:S(2)}, u32[]{:S(2)}) collective-permute-start(bf16[512,128]{1,0:T(8,128)(2,1)S(1)} %get-tuple-element.66), channel_id=1, source_target_pairs={{0,20},{4,16},{8,28},{12,24},{16,4},{20,0},{24,12},{28,8},{1,21},{... | collective-permute-start | bytes 393224 | tf_op jit(solution)/shard_map/ppermute | solution.py:547
  82.9 6.5 %collective-permute-start.17 = (bf16[512,128]{1,0:T(8,128)(2,1)S(1)}, bf16[512,128]{1,0:T(8,128)(2,1)S(1)}, u32[]{:S(2)}, u32[]{:S(2)}) collective-permute-start(bf16[512,128]{1,0:T(8,128)(2,1)S(1)} %get-tuple-element.67), channel_id=1, source_target_pairs={{0,12},{4,8},{8,4},{12,0},{16,28},{20,24},{24,20},{28,16},{1,13},{... | collective-permute-start | bytes 393224 | tf_op jit(solution)/shard_map/ppermute | solution.py:547
  83.3 9.8 %collective-permute-start.18 = (bf16[512,128]{1,0:T(8,128)(2,1)S(1)}, bf16[512,128]{1,0:T(8,128)(2,1)S(1)}, u32[]{:S(2)}, u32[]{:S(2)}) collective-permute-start(bf16[512,128]{1,0:T(8,128)(2,1)S(1)} %get-tuple-element.68), channel_id=1, source_target_pairs={{0,24},{4,28},{8,16},{12,20},{16,8},{20,12},{24,0},{28,4},{1,25},{... | collective-permute-start | bytes 393224 | tf_op jit(solution)/shard_map/ppermute | solution.py:547
  84.7 10.2 %collective-permute-start.19 = (bf16[512,128]{1,0:T(8,128)(2,1)S(1)}, bf16[512,128]{1,0:T(8,128)(2,1)S(1)}, u32[]{:S(2)}, u32[]{:S(2)}) collective-permute-start(bf16[512,128]{1,0:T(8,128)(2,1)S(1)} %get-tuple-element.69), channel_id=1, source_target_pairs={{0,28},{4,24},{8,20},{12,16},{16,12},{20,8},{24,4},{28,0},{1,29},{... | collective-permute-start | bytes 393224 | tf_op jit(solution)/shard_map/ppermute | solution.py:547
  99.7 6.0 %collective-permute-start.20 = (bf16[512,128]{1,0:T(8,128)(2,1)S(1)}, bf16[512,128]{1,0:T(8,128)(2,1)S(1)}, u32[]{:S(2)}, u32[]{:S(2)}) collective-permute-start(bf16[512,128]{1,0:T(8,128)(2,1)S(1)} %get-tuple-element.72), channel_id=1, source_target_pairs={{0,4},{4,0},{8,12},{12,8},{16,20},{20,16},{24,28},{28,24},{1,5},{5... | collective-permute-start | bytes 393224 | tf_op jit(solution)/shard_map/ppermute | solution.py:547
  100.3 6.7 %collective-permute-start.21 = (bf16[512,128]{1,0:T(8,128)(2,1)S(1)}, bf16[512,128]{1,0:T(8,128)(2,1)S(1)}, u32[]{:S(2)}, u32[]{:S(2)}) collective-permute-start(bf16[512,128]{1,0:T(8,128)(2,1)S(1)} %get-tuple-element.73), channel_id=1, source_target_pairs={{0,16},{4,20},{8,24},{12,28},{16,0},{20,4},{24,8},{28,12},{1,17},{... | collective-permute-start | bytes 393224 | tf_op jit(solution)/shard_map/ppermute | solution.py:547
  103.4 5.0 %collective-permute-start.22 = (bf16[512,128]{1,0:T(8,128)(2,1)S(1)}, bf16[512,128]{1,0:T(8,128)(2,1)S(1)}, u32[]{:S(2)}, u32[]{:S(2)}) collective-permute-start(bf16[512,128]{1,0:T(8,128)(2,1)S(1)} %get-tuple-element.74), channel_id=1, source_target_pairs={{0,8},{4,12},{8,0},{12,4},{16,24},{20,28},{24,16},{28,20},{1,9},{5... | collective-permute-start | bytes 393224 | tf_op jit(solution)/shard_map/ppermute | solution.py:547
  103.4 6.9 %collective-permute-start.23 = (bf16[512,128]{1,0:T(8,128)(2,1)S(1)}, bf16[512,128]{1,0:T(8,128)(2,1)S(1)}, u32[]{:S(2)}, u32[]{:S(2)}) collective-permute-start(bf16[512,128]{1,0:T(8,128)(2,1)S(1)} %get-tuple-element.75), channel_id=1, source_target_pairs={{0,20},{4,16},{8,28},{12,24},{16,4},{20,0},{24,12},{28,8},{1,21},{... | collective-permute-start | bytes 393224 | tf_op jit(solution)/shard_map/ppermute | solution.py:547
  103.7 9.2 %collective-permute-start.24 = (bf16[512,128]{1,0:T(8,128)(2,1)S(1)}, bf16[512,128]{1,0:T(8,128)(2,1)S(1)}, u32[]{:S(2)}, u32[]{:S(2)}) collective-permute-start(bf16[512,128]{1,0:T(8,128)(2,1)S(1)} %get-tuple-element.76), channel_id=1, source_target_pairs={{0,12},{4,8},{8,4},{12,0},{16,28},{20,24},{24,20},{28,16},{1,13},{... | collective-permute-start | bytes 393224 | tf_op jit(solution)/shard_map/ppermute | solution.py:547
  105.7 8.1 %collective-permute-start.25 = (bf16[512,128]{1,0:T(8,128)(2,1)S(1)}, bf16[512,128]{1,0:T(8,128)(2,1)S(1)}, u32[]{:S(2)}, u32[]{:S(2)}) collective-permute-start(bf16[512,128]{1,0:T(8,128)(2,1)S(1)} %get-tuple-element.77), channel_id=1, source_target_pairs={{0,24},{4,28},{8,16},{12,20},{16,8},{20,12},{24,0},{28,4},{1,25},{... | collective-permute-start | bytes 393224 | tf_op jit(solution)/shard_map/ppermute | solution.py:547
  106.9 9.9 %collective-permute-start.26 = (bf16[512,128]{1,0:T(8,128)(2,1)S(1)}, bf16[512,128]{1,0:T(8,128)(2,1)S(1)}, u32[]{:S(2)}, u32[]{:S(2)}) collective-permute-start(bf16[512,128]{1,0:T(8,128)(2,1)S(1)} %get-tuple-element.78), channel_id=1, source_target_pairs={{0,28},{4,24},{8,20},{12,16},{16,12},{20,8},{24,4},{28,0},{1,29},{... | collective-permute-start | bytes 393224 | tf_op jit(solution)/shard_map/ppermute | solution.py:547
  124.8 4.7 %collective-permute-start.27 = (bf16[512,128]{1,0:T(8,128)(2,1)S(1)}, bf16[512,128]{1,0:T(8,128)(2,1)S(1)}, u32[]{:S(2)}, u32[]{:S(2)}) collective-permute-start(bf16[512,128]{1,0:T(8,128)(2,1)S(1)} %get-tuple-element.80), channel_id=1, source_target_pairs={{0,4},{4,0},{8,12},{12,8},{16,20},{20,16},{24,28},{28,24},{1,5},{5... | collective-permute-start | bytes 393224 | tf_op jit(solution)/shard_map/ppermute | solution.py:547
  125.1 5.6 %collective-permute-start.28 = (bf16[512,128]{1,0:T(8,128)(2,1)S(1)}, bf16[512,128]{1,0:T(8,128)(2,1)S(1)}, u32[]{:S(2)}, u32[]{:S(2)}) collective-permute-start(bf16[512,128]{1,0:T(8,128)(2,1)S(1)} %get-tuple-element.81), channel_id=1, source_target_pairs={{0,16},{4,20},{8,24},{12,28},{16,0},{20,4},{24,8},{28,12},{1,17},{... | collective-permute-start | bytes 393224 | tf_op jit(solution)/shard_map/ppermute | solution.py:547
  126.4 6.3 %collective-permute-start.29 = (bf16[512,128]{1,0:T(8,128)(2,1)S(1)}, bf16[512,128]{1,0:T(8,128)(2,1)S(1)}, u32[]{:S(2)}, u32[]{:S(2)}) collective-permute-start(bf16[512,128]{1,0:T(8,128)(2,1)S(1)} %get-tuple-element.82), channel_id=1, source_target_pairs={{0,8},{4,12},{8,0},{12,4},{16,24},{20,28},{24,16},{28,20},{1,9},{5... | collective-permute-start | bytes 393224 | tf_op jit(solution)/shard_map/ppermute | solution.py:547
  126.6 6.8 %collective-permute-start.30 = (bf16[512,128]{1,0:T(8,128)(2,1)S(1)}, bf16[512,128]{1,0:T(8,128)(2,1)S(1)}, u32[]{:S(2)}, u32[]{:S(2)}) collective-permute-start(bf16[512,128]{1,0:T(8,128)(2,1)S(1)} %get-tuple-element.83), channel_id=1, source_target_pairs={{0,20},{4,16},{8,28},{12,24},{16,4},{20,0},{24,12},{28,8},{1,21},{... | collective-permute-start | bytes 393224 | tf_op jit(solution)/shard_map/ppermute | solution.py:547
  127.7 8.2 %collective-permute-start.31 = (bf16[512,128]{1,0:T(8,128)(2,1)S(1)}, bf16[512,128]{1,0:T(8,128)(2,1)S(1)}, u32[]{:S(2)}, u32[]{:S(2)}) collective-permute-start(bf16[512,128]{1,0:T(8,128)(2,1)S(1)} %get-tuple-element.84), channel_id=1, source_target_pairs={{0,12},{4,8},{8,4},{12,0},{16,28},{20,24},{24,20},{28,16},{1,13},{... | collective-permute-start | bytes 393224 | tf_op jit(solution)/shard_map/ppermute | solution.py:547
  129.5 10.0 %collective-permute-start.32 = (bf16[512,128]{1,0:T(8,128)(2,1)S(1)}, bf16[512,128]{1,0:T(8,128)(2,1)S(1)}, u32[]{:S(2)}, u32[]{:S(2)}) collective-permute-start(bf16[512,128]{1,0:T(8,128)(2,1)S(1)} %get-tuple-element.85), channel_id=1, source_target_pairs={{0,24},{4,28},{8,16},{12,20},{16,8},{20,12},{24,0},{28,4},{1,25},{... | collective-permute-start | bytes 393224 | tf_op jit(solution)/shard_map/ppermute | solution.py:547
  130.7 9.2 %collective-permute-start.33 = (bf16[512,128]{1,0:T(8,128)(2,1)S(1)}, bf16[512,128]{1,0:T(8,128)(2,1)S(1)}, u32[]{:S(2)}, u32[]{:S(2)}) collective-permute-start(bf16[512,128]{1,0:T(8,128)(2,1)S(1)} %get-tuple-element.86), channel_id=1, source_target_pairs={{0,28},{4,24},{8,20},{12,16},{16,12},{20,8},{24,4},{28,0},{1,29},{... | collective-permute-start | bytes 393224 | tf_op jit(solution)/shard_map/ppermute | solution.py:547

commit v12 on v11

--- a/solution.py
+++ b/solution.py
@@ -175,9 +175,9 @@
                 coeff_ref[at, lanes] = (share * (corr_ref[at, lanes] * norm_ref[plan, :, lanes])).astype(jnp.bfloat16)
                 coeff_ref[at, sines] = (share * (corr_ref[at, sines] * norm_ref[plan, :, sines])).astype(jnp.bfloat16)
             score_ref[plan, at, :] = BETA * highest + jnp.log(total)
-        model_ref[:obs, :] = lax.dot_general(
-            basis_ref[plan], coeff_ref[...], (((1,), (1,)), ((), ())), preferred_element_type=jnp.float32
-        )
+            model_ref[:obs, :] = lax.dot_general(
+            coeff_ref[...], basis_ref[plan], (((1,), (1,)), ((), ())), preferred_element_type=jnp.float32
+        ).T
         for step in range(steps):
             back_ref[pl.ds(src_ref[plan, step], STEP), :] = model_ref[pl.ds(dst_ref[plan, step], STEP), :]
 
@@ -234,11 +234,14 @@
 
 def load_attitude(sky, own_ref, passed, whole_ref, sems):
     rows = own_ref.shape[1]
-    count = len(passed) // 2 + 1
+    count = whole_ref.shape[1] // rows
     copies = [(None, sky, own_ref)]
-    for hop in range(1, count):
+    for hop in range(1, 2 if count == 4 else count):
         copies.append((sky >= hop, sky - hop, passed[2 * hop - 2]))
         copies.append((sky + hop < count, sky + hop, passed[2 * hop - 1]))
+    if count == 4:
+        copies.append((None, sky ^ 2, passed[2]))
+        copies.append(((sky == 0) | (sky == 3), 3 - sky, passed[3]))
 
     def each(act):
         for index, (valid, quarter, ref) in enumerate(copies):
@@ -550,6 +553,14 @@
 
 def pass_along(attitude, beside):
     count = lax.axis_size("sky")
+    if count == 4:
+        right = lax.ppermute(attitude, "sky", [(0, 1), (1, 2), (2, 3)])
+        left = lax.ppermute(attitude, "sky", [(1, 0), (2, 1), (3, 2)])
+        across = lax.ppermute(attitude, "sky", [(0, 2), (1, 3), (2, 0), (3, 1)])
+        across, _ = beside[1](across, across)
+        last = lax.ppermute(across, "sky", [(2, 3), (1, 0)])
+        across, _ = beside[2](across, across)
+        return [attitude, right, left, across, last]
     right = left = attitude
     pieces = [attitude]
     for hop in range(1, count):
@@ -580,9 +591,9 @@
 
     def first_hop(right, left):
         nonlocal asked
-        basis_part([right, left])
-        held, _ = lax.optimization_barrier((wanted, made[0][1]))
-        asked = lax.all_to_all(held, "tm", split_axis=0, concat_axis=0, tiled=True)
+        asked = lax.all_to_all(wanted, "tm", split_axis=0, concat_axis=0, tiled=True)
+        basis_part([])
+        right, left, *_ = lax.optimization_barrier((right, left, asked, made[0][1]))
         return right, left
 
     def second_hop(right, left):
@@ -593,6 +604,7 @@
     pieces = pass_along(attitude, {1: first_hop, 2: second_hop})
     cnt = jnp.sum((asked < seg_dev * slots * column_blocks).astype(jnp.int32), axis=1)
     where = jnp.stack([lax.axis_index("tm"), lax.axis_index("sky")])
+    where, _ = lax.optimization_barrier((where, made[-1][1]))
     scalars = (asked.reshape(-1), cnt, seg_counts, where)
     rows = seg_dev * slots * column_blocks
     order = [0] + send_order(tm_count)

time: 144 us -> 189 us (1.31)
  Pallas kernels: 50 us -> 90 us
  waiting for transfers between devices: 34.4 us -> 38.4 us
    pallas_call x2, Pallas kernels: 16.7 us -> 55 us  [fit_plans(): pl.pallas_call(functools.partial(fit_kernel, order), in_specs=[SMEM, SMEM...]
    ppermute x6 -> x4, waiting for transfers between devices: 8.05 us -> 16.5 us  [the longest x1 13.3 us: pass_along(): across = lax.ppermute(attitude, 'sky', [(0, 2), (1, 3), (2, 0), (3, 1)])]
    all_to_all x1, waiting for transfers between devices: 4.02 us -> 0.01 us  [first_hop(): lax.all_to_all(wanted, 'tm', split_axis=0, concat_axis=0, tiled=True)]
    ppermute x6 -> x4, starting transfers between devices: 9.95 us -> 9.8 us  [the longest x1 4.7 us: pass_along(): right = lax.ppermute(attitude, 'sky', [(0, 1), (1, 2), (2, 3)])]
  transfers between devices with their start and end apart: 35 -> 33, of which waited for: 16 -> 15; matrix products, arithmetic and copies ran while one was open for 7% -> 6% of each run, Pallas kernels for 15% -> 12%
where the time goes in v12:
time: 189 us; the launch traced here: 188 us
  Pallas kernels  90 us (48%)
  starting transfers between devices  47.1 us (25%)
  waiting for transfers between devices  38.4 us (20%)
  other arithmetic  9.96 us (5%)
    pallas_call x2, Pallas kernels, fit_plans(): pl.pallas_call(functools.partial(fit_kernel, order), in_specs=[SMEM, SMEM...  55 us
    ppermute x28, starting transfers between devices, exchange(): lax.ppermute(blocks[step], 'tm', [(i, i ^ step) for i in range(count)])  32 us
    ppermute x28, waiting for transfers between devices, exchange(): lax.ppermute(blocks[step], 'tm', [(i, i ^ step) for i in range(count)])  22 us
    pallas_call x4, Pallas kernels, make_basis(): pl.pallas_call(functools.partial(basis_kernel, len(after)), grid=(sched_d...  14.3 us
    ppermute x1, waiting for transfers between devices, pass_along(): across = lax.ppermute(attitude, 'sky', [(0, 2), (1, 3), (2, 0), (3, 1)])  13.3 us
    pallas_call x2, Pallas kernels, place_early(): pl.pallas_call(functools.partial(early_kernel, owners, table_base), in_sp...  7.62 us
    pallas_call x1, Pallas kernels, place_late_and_pick(): pl.pallas_call(functools.partial(late_pick_kernel, tm_count, len(attitude...  5.58 us
    all_to_all x1, starting transfers between devices, first_hop(): lax.all_to_all(wanted, 'tm', split_axis=0, concat_axis=0, tiled=True)  5.23 us
  transfers between devices with their start and end apart: 33, of which 15 were waited for; matrix products, arithmetic and copies ran while one was open for 6% of the time, Pallas kernels for 12%

profile of v12, /device:TPU:1, one launch (start us, length us, event | category | flops | bytes accessed | tf_op | source)
XLA Modules:
  0.0 188.1 jit_solution(13355110273896298966)
XLA Ops:
  0.6 1.3 collective-permute-start.2
  1.9 4.7 %collective-permute-start.1 = (bf16[4,128,512]{2,1,0:T(8,128)(2,1)}, bf16[4,128,512]{2,1,0:T(8,128)(2,1)S(1)}, u32[]{:S(2)}, u32[]{:S(2)}) collective-permute-start(bf16[4,128,512]{2,1,0:T(8,128)(2,1)} %own_ref.3), channel_id=1, source_target_pairs={{0,1},{1,2},{2,3},{4,5},{5,6},{6,7},{8,9},{9,10},{10,11},{12,13},{... | collective-permute-start | bytes 1572872 | tf_op jit(solution)/shard_map/ppermute | solution.py:557
  6.6 2.5 %collective-permute-start = (bf16[4,128,512]{2,1,0:T(8,128)(2,1)}, bf16[4,128,512]{2,1,0:T(8,128)(2,1)S(1)}, u32[]{:S(2)}, u32[]{:S(2)}) collective-permute-start(bf16[4,128,512]{2,1,0:T(8,128)(2,1)} %own_ref.3), channel_id=1, source_target_pairs={{0,2},{1,3},{2,0},{3,1},{4,6},{5,7},{6,4},{7,5},{8,10},{9,11},{10,... | collective-permute-start | bytes 1572872 | tf_op jit(solution)/shard_map/ppermute | solution.py:559
  12.2 3.4 %select_reduce_fusion = s32[4096]{0:T(1024)S(1)} fusion(s32[2048]{0:T(1024)S(1)} %bitcast.39, s32[2048]{0:T(1024)S(1)} %bitcast.38), kind=kLoop, calls=%fused_computation | loop fusion | flops 25161728 | bytes 32768 | tf_op jit(solution)/shard_map/reduce_sum | solution.py:521
  16.2 5.2 %all-to-all-start = ((s32[8,1,512]{2,1,0:T(1,128)}), s32[8,1,512]{2,1,0:T(1,128)S(1)}, u32[]{:S(2)}, u32[]{:S(2)}) async-start(s32[8,1,512]{2,1,0:T(1,128)} %bitcast), calls=%async_computation | async-start | bytes 32768 | tf_op jit(solution)/shard_map/all_to_all | solution.py:594
  23.4 1.8 shard_map.77
  25.2 1.0 copy-done.3
  26.5 13.3 %collective-permute-done.refs_0_.refs_1_.refs_2_ = bf16[4,128,512]{2,1,0:T(8,128)(2,1)S(1)} collective-permute-done((bf16[4,128,512]{2,1,0:T(8,128)(2,1)}, bf16[4,128,512]{2,1,0:T(8,128)(2,1)S(1)}, u32[]{:S(2)}, u32[]{:S(2)}) %collective-permute-start) | collective-permute-done | bytes 524320 | tf_op jit(solution)/shard_map/ppermute | solution.py:559
  39.8 1.3 collective-permute-start.3
  41.3 5.3 %shard_map.78 = (bf16[3,256,2048]{2,1,0:T(8,128)(2,1)S(1)}, f32[3,1,2048]{2,1,0:T(1,128)S(1)}) custom-call(f32[768,128]{1,0:T(8,128)S(1)} %broadcast_in_dim.50.time_ref, f32[1,1024]{1,0:T(1,128)S(1)} %bitcast.33, f32[1,1024]{1,0:T(1,128)S(1)} %bitcast.29, bf16[4,128,512]{2,1,0:T(8,128)(2,1)S(1)} %collective-permute-done.refs_0_.refs_1_.refs_2_, ...), custom_call_target="tpu_custom_call" | custom-call | flops 6291456000 | bytes 3145728 | tf_op jit(solution)/shard_map/pallas_call | solution.py:91
  46.8 3.6 %shard_map.80 = (bf16[2,256,2048]{2,1,0:T(8,128)(2,1)S(1)}, f32[2,1,2048]{2,1,0:T(1,128)S(1)}) custom-call(f32[512,128]{1,0:T(8,128)S(1)} %broadcast_in_dim.55.time_ref, f32[1,1024]{1,0:T(1,128)S(1)} %bitcast.34, f32[1,1024]{1,0:T(1,128)S(1)} %bitcast.30, bf16[4,128,512]{2,1,0:T(8,128)(2,1)S(1)} %collective-permute-done.refs_0_.refs_1_.refs_2_, ...), custom_call_target="tpu_custom_call" | custom-call | flops 4194304000 | bytes 2097152 | tf_op jit(solution)/shard_map/pallas_call | solution.py:91
  50.4 3.2 %collective-permute-done.3.refs_3_ = bf16[4,128,512]{2,1,0:T(8,128)(2,1)S(1)} collective-permute-done((bf16[4,128,512]{2,1,0:T(8,128)(2,1)S(1)}, bf16[4,128,512]{2,1,0:T(8,128)(2,1)S(1)}, u32[]{:S(2)}, u32[]{:S(2)}) %collective-permute-start.3) | collective-permute-done | bytes 524320 | tf_op jit(solution)/shard_map/ppermute | solution.py:561
  53.6 4.0 %shard_map.79 = (bf16[512,128]{1,0:T(8,128)(2,1)S(1)}, bf16[512,128]{1,0:T(8,128)(2,1)S(1)}, bf16[512,128]{1,0:T(8,128)(2,1)S(1)}, bf16[512,128]{1,0:T(8,128)(2,...) custom-call(s32[4096]{0:T(1024)S(1)} %bitcast.23, ...), custom_call_target="tpu_custom_call" | custom-call | flops 5000000000 | bytes 1048576 | tf_op jit(solution)/shard_map/pallas_call | solution.py:382
  57.6 3.5 %collective-permute-start.4 = (bf16[512,128]{1,0:T(8,128)(2,1)S(1)}, bf16[512,128]{1,0:T(8,128)(2,1)S(1)}, u32[]{:S(2)}, u32[]{:S(2)}) collective-permute-start(bf16[512,128]{1,0:T(8,128)(2,1)S(1)} %get-tuple-element.51), channel_id=1, source_target_pairs={{0,4},{4,0},{8,12},{12,8},{16,20},{20,16},{24,28},{28,24},{1,5},{5... | collective-permute-start | bytes 393224 | tf_op jit(solution)/shard_map/ppermute | solution.py:550
  61.1 1.3 collective-permute-start.5
  63.1 1.3 collective-permute-start.8
  64.5 3.6 %shard_map.81 = (bf16[2,256,2048]{2,1,0:T(8,128)(2,1)S(1)}, f32[2,1,2048]{2,1,0:T(1,128)S(1)}) custom-call(f32[512,128]{1,0:T(8,128)S(1)} %broadcast_in_dim.57.time_ref, f32[1,1024]{1,0:T(1,128)S(1)} %bitcast.35, f32[1,1024]{1,0:T(1,128)S(1)} %bitcast.31, bf16[512,128]{1,0:T(8,128)(2,1)S(1)} %get-tuple-element.50.refs_0_), custom_call_target="tpu_custom_call" | custom-call | flops 4194304000 | bytes 2097152 | tf_op jit(solution)/shard_map/pallas_call | solution.py:91
  68.1 1.3 collective-permute-start.9
  69.4 2.0 %collective-permute-start.10 = (bf16[512,128]{1,0:T(8,128)(2,1)S(1)}, bf16[512,128]{1,0:T(8,128)(2,1)S(1)}, u32[]{:S(2)}, u32[]{:S(2)}) collective-permute-start(bf16[512,128]{1,0:T(8,128)(2,1)S(1)} %get-tuple-element.57), channel_id=1, source_target_pairs={{0,28},{4,24},{8,20},{12,16},{16,12},{20,8},{24,4},{28,0},{1,29},{... | collective-permute-start | bytes 393224 | tf_op jit(solution)/shard_map/ppermute | solution.py:550
  71.3 2.1 %collective-permute-done.9.refs_6_ = bf16[512,128]{1,0:T(8,128)(2,1)S(1)} collective-permute-done((bf16[512,128]{1,0:T(8,128)(2,1)S(1)}, bf16[512,128]{1,0:T(8,128)(2,1)S(1)}, u32[]{:S(2)}, u32[]{:S(2)}) %collective-permute-start.9) | collective-permute-done | bytes 131104 | tf_op jit(solution)/shard_map/ppermute | solution.py:550
  73.5 3.6 %collective-permute-done.10.refs_7_ = bf16[512,128]{1,0:T(8,128)(2,1)S(1)} collective-permute-done((bf16[512,128]{1,0:T(8,128)(2,1)S(1)}, bf16[512,128]{1,0:T(8,128)(2,1)S(1)}, u32[]{:S(2)}, u32[]{:S(2)}) %collective-permute-start.10) | collective-permute-done | bytes 131104 | tf_op jit(solution)/shard_map/ppermute | solution.py:550
  77.1 27.9 %shard_map.82 = (bf16[512,128]{1,0:T(8,128)(2,1)S(1)}, bf16[512,128]{1,0:T(8,128)(2,1)S(1)}, bf16[512,128]{1,0:T(8,128)(2,1)S(1)}, bf16[512,128]{1,0:T(8,128)(2,...) custom-call(s32[8,24]{1,0:T(8,128)S(1)} %get-tuple-element.106.src_r, ...), custom_call_target="tpu_custom_call" | custom-call | flops 10737418240 | bytes 8388608 | tf_op jit(solution)/shard_map/pallas_call | solution.py:217
  105.1 1.3 collective-permute-start.12
  106.6 1.4 collective-permute-start.14
  108.7 1.2 collective-permute-start.16
  109.9 2.7 %collective-permute-start.17 = (bf16[512,128]{1,0:T(8,128)(2,1)S(1)}, bf16[512,128]{1,0:T(8,128)(2,1)S(1)}, u32[]{:S(2)}, u32[]{:S(2)}) collective-permute-start(bf16[512,128]{1,0:T(8,128)(2,1)S(1)} %get-tuple-element.71), channel_id=1, source_target_pairs={{0,28},{4,24},{8,20},{12,16},{16,12},{20,8},{24,4},{28,0},{1,29},{... | collective-permute-start | bytes 393224 | tf_op jit(solution)/shard_map/ppermute | solution.py:550
  112.5 0.9 collective-permute-done.14.refs_4_
  113.5 2.4 %collective-permute-done.15.refs_5_ = bf16[512,128]{1,0:T(8,128)(2,1)S(1)} collective-permute-done((bf16[512,128]{1,0:T(8,128)(2,1)S(1)}, bf16[512,128]{1,0:T(8,128)(2,1)S(1)}, u32[]{:S(2)}, u32[]{:S(2)}) %collective-permute-start.15) | collective-permute-done | bytes 131104 | tf_op jit(solution)/shard_map/ppermute | solution.py:550
  115.9 3.9 %shard_map.83.part_ref = f32[4096,128]{1,0:T(8,128)S(1)} custom-call(s32[4096]{0:T(1024)S(1)} %bitcast.24, s32[8]{0:T(128)S(1)} %convert_reduce_fusion.2.cnt_ref, s32[2]{0:T(128)S(1)} %pad_add_fusion.where_ref, bf16[4,512,256]{2,1,0:T(8,128)(2,1)S(1)} %copy-done, bf16[512,128]{1,0:T(8,128)(2,1)S(1)} %get-tuple-element.64.refs_0_, ...), custom_call_target="tpu_custom_call" | custom-call | flops 6000000000 | bytes 1048576 | tf_op jit(solution)/shard_map/pallas_call | solution.py:354
  120.0 5.6 %shard_map.84 = (f32[131072,128]{1,0:T(8,128)}, bf16[512,128]{1,0:T(8,128)(2,1)S(1)}, bf16[512,128]{1,0:T(8,128)(2,1)S(1)}, bf16[512,128]{1,0:T(8,128)(2,1)S(1)}...) custom-call(s32[4096]{0:T(1024)S(1)} %bitcast.25, ...), custom_call_target="tpu_custom_call" | custom-call | flops 7000000000 | bytes 1048576 | tf_op jit(solution)/shard_map/pallas_call | solution.py:439
  126.2 2.7 %collective-permute-start.19 = (bf16[512,128]{1,0:T(8,128)(2,1)S(1)}, bf16[512,128]{1,0:T(8,128)(2,1)S(1)}, u32[]{:S(2)}, u32[]{:S(2)}) collective-permute-start(bf16[512,128]{1,0:T(8,128)(2,1)S(1)} %get-tuple-element.75), channel_id=1, source_target_pairs={{0,16},{4,20},{8,24},{12,28},{16,0},{20,4},{24,8},{28,12},{1,17},{... | collective-permute-start | bytes 393224 | tf_op jit(solution)/shard_map/ppermute | solution.py:550
  128.9 0.9 collective-permute-start.21
  129.8 1.1 collective-permute-start.22
  130.9 1.2 collective-permute-start.23
  132.7 0.9 collective-permute-start.24
  133.6 2.1 %collective-permute-done.21.refs_4_ = bf16[512,128]{1,0:T(8,128)(2,1)S(1)} collective-permute-done((bf16[512,128]{1,0:T(8,128)(2,1)S(1)}, bf16[512,128]{1,0:T(8,128)(2,1)S(1)}, u32[]{:S(2)}, u32[]{:S(2)}) %collective-permute-start.21) | collective-permute-done | bytes 131104 | tf_op jit(solution)/shard_map/ppermute | solution.py:550
  135.7 2.3 %collective-permute-done.22.refs_5_ = bf16[512,128]{1,0:T(8,128)(2,1)S(1)} collective-permute-done((bf16[512,128]{1,0:T(8,128)(2,1)S(1)}, bf16[512,128]{1,0:T(8,128)(2,1)S(1)}, u32[]{:S(2)}, u32[]{:S(2)}) %collective-permute-start.22) | collective-permute-done | bytes 131104 | tf_op jit(solution)/shard_map/ppermute | solution.py:550
  138.0 1.2 collective-permute-done.23.refs_6_
  139.2 3.1 %collective-permute-done.24.refs_7_ = bf16[512,128]{1,0:T(8,128)(2,1)S(1)} collective-permute-done((bf16[512,128]{1,0:T(8,128)(2,1)S(1)}, bf16[512,128]{1,0:T(8,128)(2,1)S(1)}, u32[]{:S(2)}, u32[]{:S(2)}) %collective-permute-start.24) | collective-permute-done | bytes 131104 | tf_op jit(solution)/shard_map/ppermute | solution.py:550
  142.2 27.1 %shard_map.85 = (bf16[512,128]{1,0:T(8,128)(2,1)S(1)}, bf16[512,128]{1,0:T(8,128)(2,1)S(1)}, bf16[512,128]{1,0:T(8,128)(2,1)S(1)}, bf16[512,128]{1,0:T(8,128)(2,...) custom-call(s32[8,24]{1,0:T(8,128)S(1)} %get-tuple-element.106.src_r, ...), custom_call_target="tpu_custom_call" | custom-call | flops 10737418240 | bytes 8388608 | tf_op jit(solution)/shard_map/pallas_call | solution.py:217
  169.6 1.4 collective-permute-start.26
  171.2 1.1 collective-permute-start.28
  172.3 1.1 collective-permute-start.29
  174.2 1.2 collective-permute-start.30
  175.4 1.9 %collective-permute-start.31 = (bf16[512,128]{1,0:T(8,128)(2,1)S(1)}, bf16[512,128]{1,0:T(8,128)(2,1)S(1)}, u32[]{:S(2)}, u32[]{:S(2)}) collective-permute-start(bf16[512,128]{1,0:T(8,128)(2,1)S(1)} %get-tuple-element.88), channel_id=1, source_target_pairs={{0,28},{4,24},{8,20},{12,16},{16,12},{20,8},{24,4},{28,0},{1,29},{... | collective-permute-start | bytes 393224 | tf_op jit(solution)/shard_map/ppermute | solution.py:550
  177.9 2.6 %collective-permute-done.29.refs_5_ = bf16[512,128]{1,0:T(8,128)(2,1)S(1)} collective-permute-done((bf16[512,128]{1,0:T(8,128)(2,1)S(1)}, bf16[512,128]{1,0:T(8,128)(2,1)S(1)}, u32[]{:S(2)}, u32[]{:S(2)}) %collective-permute-start.29) | collective-permute-done | bytes 131104 | tf_op jit(solution)/shard_map/ppermute | solution.py:550
  180.5 3.8 %shard_map.86.part_ref = f32[4096,128]{1,0:T(8,128)S(1)} custom-call(s32[4096]{0:T(1024)S(1)} %bitcast.26, s32[8]{0:T(128)S(1)} %convert_reduce_fusion.2.cnt_ref, s32[2]{0:T(128)S(1)} %pad_add_fusion.where_ref, f32[131072,128]{1,0:T(8,128)} %get-tuple-element.72.base_ref, bf16[512,128]{1,0:T(8,128)(2,1)S(1)} %get-tuple-element.81.refs_0_, ...), custom_call_target="tpu_custom_call" | custom-call | flops 6000000000 | bytes 1048576 | tf_op jit(solution)/shard_map/pallas_call | solution.py:354
  184.5 3.5 %shard_map.87 = f32[4,512,256]{2,1,0:T(8,128)} custom-call(s32[4096]{0:T(1024)S(1)} %bitcast.27, s32[8]{0:T(128)S(1)} %convert_reduce_fusion.2.cnt_ref, s32[2]{0:T(128)S(1)} %pad_add_fusion.where_ref, f32[4096,128]{1,0:T(8,128)S(1)} %shard_map.86.part_ref, bf16[512,128]{1,0:T(8,128)(2,1)S(1)} %collective-permute-done.30.refs_0_, ...), custom_call_target="tpu_custom_call" | custom-call | flops 4000000000 | bytes 1048576 | tf_op jit(solution)/shard_map/pallas_call | solution.py:481
  (77 shorter events, 11.6 us)
Async XLA Ops:
  0.6 49.8 %collective-permute-start.2 = (bf16[4,128,512]{2,1,0:T(8,128)(2,1)}, bf16[4,128,512]{2,1,0:T(8,128)(2,1)S(1)}, u32[]{:S(2)}, u32[]{:S(2)}) collective-permute-start(bf16[4,128,512]{2,1,0:T(8,128)(2,1)} %own_ref.3), channel_id=1, source_target_pairs={{1,0},{2,1},{3,2},{5,4},{6,5},{7,6},{9,8},{10,9},{11,10},{13,12},{... | collective-permute-start | bytes 1572872 | tf_op jit(solution)/shard_map/ppermute | solution.py:558
  1.9 48.5 %collective-permute-start.1 = (bf16[4,128,512]{2,1,0:T(8,128)(2,1)}, bf16[4,128,512]{2,1,0:T(8,128)(2,1)S(1)}, u32[]{:S(2)}, u32[]{:S(2)}) collective-permute-start(bf16[4,128,512]{2,1,0:T(8,128)(2,1)} %own_ref.3), channel_id=1, source_target_pairs={{0,1},{1,2},{2,3},{4,5},{5,6},{6,7},{8,9},{9,10},{10,11},{12,13},{... | collective-permute-start | bytes 1572872 | tf_op jit(solution)/shard_map/ppermute | solution.py:557
  6.6 33.2 %collective-permute-start = (bf16[4,128,512]{2,1,0:T(8,128)(2,1)}, bf16[4,128,512]{2,1,0:T(8,128)(2,1)S(1)}, u32[]{:S(2)}, u32[]{:S(2)}) collective-permute-start(bf16[4,128,512]{2,1,0:T(8,128)(2,1)} %own_ref.3), channel_id=1, source_target_pairs={{0,2},{1,3},{2,0},{3,1},{4,6},{5,7},{6,4},{7,5},{8,10},{9,11},{10,... | collective-permute-start | bytes 1572872 | tf_op jit(solution)/shard_map/ppermute | solution.py:559
  16.2 10.2 %all-to-all-start = ((s32[8,1,512]{2,1,0:T(1,128)}), s32[8,1,512]{2,1,0:T(1,128)S(1)}, u32[]{:S(2)}, u32[]{:S(2)}) async-start(s32[8,1,512]{2,1,0:T(1,128)} %bitcast), calls=%async_computation | async-start | bytes 32768 | tf_op jit(solution)/shard_map/all_to_all | solution.py:594
  25.2 1.0 copy-start.3
  39.8 13.8 %collective-permute-start.3 = (bf16[4,128,512]{2,1,0:T(8,128)(2,1)S(1)}, bf16[4,128,512]{2,1,0:T(8,128)(2,1)S(1)}, u32[]{:S(2)}, u32[]{:S(2)}) collective-permute-start(bf16[4,128,512]{2,1,0:T(8,128)(2,1)S(1)} %collective-permute-done.refs_0_.refs_1_.refs_2_), channel_id=1, source_target_pairs={{2,3},{1,0},{6,7},{5,4},{10,11},{9,8},{14,15},{13,12},{18,19},{17,... | collective-permute-start | bytes 1572872 | tf_op jit(solution)/shard_map/ppermute | solution.py:561
  46.8 6.8 %copy-start = (bf16[4,512,256]{2,1,0:T(8,128)(2,1)S(1)}, bf16[4,512,256]{2,1,0:T(8,128)(2,1)}, u32[]{:S(2)}) copy-start(bf16[4,512,256]{2,1,0:T(8,128)(2,1)} %base_ref.3) | copy-start | bytes 3145732
  46.8 6.8 %copy-start.1 = (bf16[4,128,512]{2,1,0:T(8,128)(2,1)S(1)}, bf16[4,128,512]{2,1,0:T(8,128)(2,1)}, u32[]{:S(2)}) copy-start(bf16[4,128,512]{2,1,0:T(8,128)(2,1)} %own_ref.3) | copy-start | bytes 1572868
  46.8 6.8 %copy-start.2 = (s32[4]{0:T(128)S(1)}, s32[4]{0:T(128)}, u32[]{:S(2)}) copy-start(s32[4]{0:T(128)} %count_ref.3) | copy-start | bytes 52
  57.6 10.5 %collective-permute-start.4 = (bf16[512,128]{1,0:T(8,128)(2,1)S(1)}, bf16[512,128]{1,0:T(8,128)(2,1)S(1)}, u32[]{:S(2)}, u32[]{:S(2)}) collective-permute-start(bf16[512,128]{1,0:T(8,128)(2,1)S(1)} %get-tuple-element.51), channel_id=1, source_target_pairs={{0,4},{4,0},{8,12},{12,8},{16,20},{20,16},{24,28},{28,24},{1,5},{5... | collective-permute-start | bytes 393224 | tf_op jit(solution)/shard_map/ppermute | solution.py:550
  61.1 8.2 %collective-permute-start.5 = (bf16[512,128]{1,0:T(8,128)(2,1)S(1)}, bf16[512,128]{1,0:T(8,128)(2,1)S(1)}, u32[]{:S(2)}, u32[]{:S(2)}) collective-permute-start(bf16[512,128]{1,0:T(8,128)(2,1)S(1)} %get-tuple-element.52), channel_id=1, source_target_pairs={{0,16},{4,20},{8,24},{12,28},{16,0},{20,4},{24,8},{28,12},{1,17},{... | collective-permute-start | bytes 393224 | tf_op jit(solution)/shard_map/ppermute | solution.py:550
  62.4 8.9 %collective-permute-start.6 = (bf16[512,128]{1,0:T(8,128)(2,1)S(1)}, bf16[512,128]{1,0:T(8,128)(2,1)S(1)}, u32[]{:S(2)}, u32[]{:S(2)}) collective-permute-start(bf16[512,128]{1,0:T(8,128)(2,1)S(1)} %get-tuple-element.53), channel_id=1, source_target_pairs={{0,8},{4,12},{8,0},{12,4},{16,24},{20,28},{24,16},{28,20},{1,9},{5... | collective-permute-start | bytes 393224 | tf_op jit(solution)/shard_map/ppermute | solution.py:550
  62.6 8.7 %collective-permute-start.7 = (bf16[512,128]{1,0:T(8,128)(2,1)S(1)}, bf16[512,128]{1,0:T(8,128)(2,1)S(1)}, u32[]{:S(2)}, u32[]{:S(2)}) collective-permute-start(bf16[512,128]{1,0:T(8,128)(2,1)S(1)} %get-tuple-element.54), channel_id=1, source_target_pairs={{0,20},{4,16},{8,28},{12,24},{16,4},{20,0},{24,12},{28,8},{1,21},{... | collective-permute-start | bytes 393224 | tf_op jit(solution)/shard_map/ppermute | solution.py:550
  63.1 8.2 %collective-permute-start.8 = (bf16[512,128]{1,0:T(8,128)(2,1)S(1)}, bf16[512,128]{1,0:T(8,128)(2,1)S(1)}, u32[]{:S(2)}, u32[]{:S(2)}) collective-permute-start(bf16[512,128]{1,0:T(8,128)(2,1)S(1)} %get-tuple-element.55), channel_id=1, source_target_pairs={{0,12},{4,8},{8,4},{12,0},{16,28},{20,24},{24,20},{28,16},{1,13},{... | collective-permute-start | bytes 393224 | tf_op jit(solution)/shard_map/ppermute | solution.py:550
  64.5 12.6 %copy-start.4 = (bf16[1,256,2048]{2,1,0:T(8,128)(2,1)S(1)}, bf16[1,256,2048]{2,1,0:T(8,128)(2,1)}, u32[]{:S(2)}) copy-start(bf16[1,256,2048]{2,1,0:T(8,128)(2,1)} %copy-done.3) | copy-start | bytes 3145732
  68.1 5.4 %collective-permute-start.9 = (bf16[512,128]{1,0:T(8,128)(2,1)S(1)}, bf16[512,128]{1,0:T(8,128)(2,1)S(1)}, u32[]{:S(2)}, u32[]{:S(2)}) collective-permute-start(bf16[512,128]{1,0:T(8,128)(2,1)S(1)} %get-tuple-element.56), channel_id=1, source_target_pairs={{0,24},{4,28},{8,16},{12,20},{16,8},{20,12},{24,0},{28,4},{1,25},{... | collective-permute-start | bytes 393224 | tf_op jit(solution)/shard_map/ppermute | solution.py:550
  69.4 7.7 %collective-permute-start.10 = (bf16[512,128]{1,0:T(8,128)(2,1)S(1)}, bf16[512,128]{1,0:T(8,128)(2,1)S(1)}, u32[]{:S(2)}, u32[]{:S(2)}) collective-permute-start(bf16[512,128]{1,0:T(8,128)(2,1)S(1)} %get-tuple-element.57), channel_id=1, source_target_pairs={{0,28},{4,24},{8,20},{12,16},{16,12},{20,8},{24,4},{28,0},{1,29},{... | collective-permute-start | bytes 393224 | tf_op jit(solution)/shard_map/ppermute | solution.py:550
  105.0 3.7 %collective-permute-start.11 = (bf16[512,128]{1,0:T(8,128)(2,1)S(1)}, bf16[512,128]{1,0:T(8,128)(2,1)S(1)}, u32[]{:S(2)}, u32[]{:S(2)}) collective-permute-start(bf16[512,128]{1,0:T(8,128)(2,1)S(1)} %get-tuple-element.65), channel_id=1, source_target_pairs={{0,4},{4,0},{8,12},{12,8},{16,20},{20,16},{24,28},{28,24},{1,5},{5... | collective-permute-start | bytes 393224 | tf_op jit(solution)/shard_map/ppermute | solution.py:550
  105.1 4.8 %collective-permute-start.12 = (bf16[512,128]{1,0:T(8,128)(2,1)S(1)}, bf16[512,128]{1,0:T(8,128)(2,1)S(1)}, u32[]{:S(2)}, u32[]{:S(2)}) collective-permute-start(bf16[512,128]{1,0:T(8,128)(2,1)S(1)} %get-tuple-element.66), channel_id=1, source_target_pairs={{0,16},{4,20},{8,24},{12,28},{16,0},{20,4},{24,8},{28,12},{1,17},{... | collective-permute-start | bytes 393224 | tf_op jit(solution)/shard_map/ppermute | solution.py:550
  106.3 6.2 %collective-permute-start.13 = (bf16[512,128]{1,0:T(8,128)(2,1)S(1)}, bf16[512,128]{1,0:T(8,128)(2,1)S(1)}, u32[]{:S(2)}, u32[]{:S(2)}) collective-permute-start(bf16[512,128]{1,0:T(8,128)(2,1)S(1)} %get-tuple-element.67), channel_id=1, source_target_pairs={{0,8},{4,12},{8,0},{12,4},{16,24},{20,28},{24,16},{28,20},{1,9},{5... | collective-permute-start | bytes 393224 | tf_op jit(solution)/shard_map/ppermute | solution.py:550
  106.6 6.8 %collective-permute-start.14 = (bf16[512,128]{1,0:T(8,128)(2,1)S(1)}, bf16[512,128]{1,0:T(8,128)(2,1)S(1)}, u32[]{:S(2)}, u32[]{:S(2)}) collective-permute-start(bf16[512,128]{1,0:T(8,128)(2,1)S(1)} %get-tuple-element.68), channel_id=1, source_target_pairs={{0,20},{4,16},{8,28},{12,24},{16,4},{20,0},{24,12},{28,8},{1,21},{... | collective-permute-start | bytes 393224 | tf_op jit(solution)/shard_map/ppermute | solution.py:550
  108.0 7.9 %collective-permute-start.15 = (bf16[512,128]{1,0:T(8,128)(2,1)S(1)}, bf16[512,128]{1,0:T(8,128)(2,1)S(1)}, u32[]{:S(2)}, u32[]{:S(2)}) collective-permute-start(bf16[512,128]{1,0:T(8,128)(2,1)S(1)} %get-tuple-element.69), channel_id=1, source_target_pairs={{0,12},{4,8},{8,4},{12,0},{16,28},{20,24},{24,20},{28,16},{1,13},{... | collective-permute-start | bytes 393224 | tf_op jit(solution)/shard_map/ppermute | solution.py:550
  108.7 11.0 %collective-permute-start.16 = (bf16[512,128]{1,0:T(8,128)(2,1)S(1)}, bf16[512,128]{1,0:T(8,128)(2,1)S(1)}, u32[]{:S(2)}, u32[]{:S(2)}) collective-permute-start(bf16[512,128]{1,0:T(8,128)(2,1)S(1)} %get-tuple-element.70), channel_id=1, source_target_pairs={{0,24},{4,28},{8,16},{12,20},{16,8},{20,12},{24,0},{28,4},{1,25},{... | collective-permute-start | bytes 393224 | tf_op jit(solution)/shard_map/ppermute | solution.py:550
  109.9 10.1 %collective-permute-start.17 = (bf16[512,128]{1,0:T(8,128)(2,1)S(1)}, bf16[512,128]{1,0:T(8,128)(2,1)S(1)}, u32[]{:S(2)}, u32[]{:S(2)}) collective-permute-start(bf16[512,128]{1,0:T(8,128)(2,1)S(1)} %get-tuple-element.71), channel_id=1, source_target_pairs={{0,28},{4,24},{8,20},{12,16},{16,12},{20,8},{24,4},{28,0},{1,29},{... | collective-permute-start | bytes 393224 | tf_op jit(solution)/shard_map/ppermute | solution.py:550
  125.6 5.3 %collective-permute-start.18 = (bf16[512,128]{1,0:T(8,128)(2,1)S(1)}, bf16[512,128]{1,0:T(8,128)(2,1)S(1)}, u32[]{:S(2)}, u32[]{:S(2)}) collective-permute-start(bf16[512,128]{1,0:T(8,128)(2,1)S(1)} %get-tuple-element.74), channel_id=1, source_target_pairs={{0,4},{4,0},{8,12},{12,8},{16,20},{20,16},{24,28},{28,24},{1,5},{5... | collective-permute-start | bytes 393224 | tf_op jit(solution)/shard_map/ppermute | solution.py:550
  126.2 6.4 %collective-permute-start.19 = (bf16[512,128]{1,0:T(8,128)(2,1)S(1)}, bf16[512,128]{1,0:T(8,128)(2,1)S(1)}, u32[]{:S(2)}, u32[]{:S(2)}) collective-permute-start(bf16[512,128]{1,0:T(8,128)(2,1)S(1)} %get-tuple-element.75), channel_id=1, source_target_pairs={{0,16},{4,20},{8,24},{12,28},{16,0},{20,4},{24,8},{28,12},{1,17},{... | collective-permute-start | bytes 393224 | tf_op jit(solution)/shard_map/ppermute | solution.py:550
  128.9 4.7 %collective-permute-start.20 = (bf16[512,128]{1,0:T(8,128)(2,1)S(1)}, bf16[512,128]{1,0:T(8,128)(2,1)S(1)}, u32[]{:S(2)}, u32[]{:S(2)}) collective-permute-start(bf16[512,128]{1,0:T(8,128)(2,1)S(1)} %get-tuple-element.76), channel_id=1, source_target_pairs={{0,8},{4,12},{8,0},{12,4},{16,24},{20,28},{24,16},{28,20},{1,9},{5... | collective-permute-start | bytes 393224 | tf_op jit(solution)/shard_map/ppermute | solution.py:550
  128.9 6.8 %collective-permute-start.21 = (bf16[512,128]{1,0:T(8,128)(2,1)S(1)}, bf16[512,128]{1,0:T(8,128)(2,1)S(1)}, u32[]{:S(2)}, u32[]{:S(2)}) collective-permute-start(bf16[512,128]{1,0:T(8,128)(2,1)S(1)} %get-tuple-element.77), channel_id=1, source_target_pairs={{0,20},{4,16},{8,28},{12,24},{16,4},{20,0},{24,12},{28,8},{1,21},{... | collective-permute-start | bytes 393224 | tf_op jit(solution)/shard_map/ppermute | solution.py:550
  129.8 8.2 %collective-permute-start.22 = (bf16[512,128]{1,0:T(8,128)(2,1)S(1)}, bf16[512,128]{1,0:T(8,128)(2,1)S(1)}, u32[]{:S(2)}, u32[]{:S(2)}) collective-permute-start(bf16[512,128]{1,0:T(8,128)(2,1)S(1)} %get-tuple-element.78), channel_id=1, source_target_pairs={{0,12},{4,8},{8,4},{12,0},{16,28},{20,24},{24,20},{28,16},{1,13},{... | collective-permute-start | bytes 393224 | tf_op jit(solution)/shard_map/ppermute | solution.py:550
  130.9 8.3 %collective-permute-start.23 = (bf16[512,128]{1,0:T(8,128)(2,1)S(1)}, bf16[512,128]{1,0:T(8,128)(2,1)S(1)}, u32[]{:S(2)}, u32[]{:S(2)}) collective-permute-start(bf16[512,128]{1,0:T(8,128)(2,1)S(1)} %get-tuple-element.79), channel_id=1, source_target_pairs={{0,24},{4,28},{8,16},{12,20},{16,8},{20,12},{24,0},{28,4},{1,25},{... | collective-permute-start | bytes 393224 | tf_op jit(solution)/shard_map/ppermute | solution.py:550
  132.7 9.6 %collective-permute-start.24 = (bf16[512,128]{1,0:T(8,128)(2,1)S(1)}, bf16[512,128]{1,0:T(8,128)(2,1)S(1)}, u32[]{:S(2)}, u32[]{:S(2)}) collective-permute-start(bf16[512,128]{1,0:T(8,128)(2,1)S(1)} %get-tuple-element.80), channel_id=1, source_target_pairs={{0,28},{4,24},{8,20},{12,16},{16,12},{20,8},{24,4},{28,0},{1,29},{... | collective-permute-start | bytes 393224 | tf_op jit(solution)/shard_map/ppermute | solution.py:550
  169.4 4.8 %collective-permute-start.25 = (bf16[512,128]{1,0:T(8,128)(2,1)S(1)}, bf16[512,128]{1,0:T(8,128)(2,1)S(1)}, u32[]{:S(2)}, u32[]{:S(2)}) collective-permute-start(bf16[512,128]{1,0:T(8,128)(2,1)S(1)} %get-tuple-element.82), channel_id=1, source_target_pairs={{0,4},{4,0},{8,12},{12,8},{16,20},{20,16},{24,28},{28,24},{1,5},{5... | collective-permute-start | bytes 393224 | tf_op jit(solution)/shard_map/ppermute | solution.py:550
  169.6 5.7 %collective-permute-start.26 = (bf16[512,128]{1,0:T(8,128)(2,1)S(1)}, bf16[512,128]{1,0:T(8,128)(2,1)S(1)}, u32[]{:S(2)}, u32[]{:S(2)}) collective-permute-start(bf16[512,128]{1,0:T(8,128)(2,1)S(1)} %get-tuple-element.83), channel_id=1, source_target_pairs={{0,16},{4,20},{8,24},{12,28},{16,0},{20,4},{24,8},{28,12},{1,17},{... | collective-permute-start | bytes 393224 | tf_op jit(solution)/shard_map/ppermute | solution.py:550
  171.0 6.3 %collective-permute-start.27 = (bf16[512,128]{1,0:T(8,128)(2,1)S(1)}, bf16[512,128]{1,0:T(8,128)(2,1)S(1)}, u32[]{:S(2)}, u32[]{:S(2)}) collective-permute-start(bf16[512,128]{1,0:T(8,128)(2,1)S(1)} %get-tuple-element.84), channel_id=1, source_target_pairs={{0,8},{4,12},{8,0},{12,4},{16,24},{20,28},{24,16},{28,20},{1,9},{5... | collective-permute-start | bytes 393224 | tf_op jit(solution)/shard_map/ppermute | solution.py:550
  171.2 6.7 %collective-permute-start.28 = (bf16[512,128]{1,0:T(8,128)(2,1)S(1)}, bf16[512,128]{1,0:T(8,128)(2,1)S(1)}, u32[]{:S(2)}, u32[]{:S(2)}) collective-permute-start(bf16[512,128]{1,0:T(8,128)(2,1)S(1)} %get-tuple-element.85), channel_id=1, source_target_pairs={{0,20},{4,16},{8,28},{12,24},{16,4},{20,0},{24,12},{28,8},{1,21},{... | collective-permute-start | bytes 393224 | tf_op jit(solution)/shard_map/ppermute | solution.py:550
  172.3 8.2 %collective-permute-start.29 = (bf16[512,128]{1,0:T(8,128)(2,1)S(1)}, bf16[512,128]{1,0:T(8,128)(2,1)S(1)}, u32[]{:S(2)}, u32[]{:S(2)}) collective-permute-start(bf16[512,128]{1,0:T(8,128)(2,1)S(1)} %get-tuple-element.86), channel_id=1, source_target_pairs={{0,12},{4,8},{8,4},{12,0},{16,28},{20,24},{24,20},{28,16},{1,13},{... | collective-permute-start | bytes 393224 | tf_op jit(solution)/shard_map/ppermute | solution.py:550
  174.2 10.1 %collective-permute-start.30 = (bf16[512,128]{1,0:T(8,128)(2,1)S(1)}, bf16[512,128]{1,0:T(8,128)(2,1)S(1)}, u32[]{:S(2)}, u32[]{:S(2)}) collective-permute-start(bf16[512,128]{1,0:T(8,128)(2,1)S(1)} %get-tuple-element.87), channel_id=1, source_target_pairs={{0,24},{4,28},{8,16},{12,20},{16,8},{20,12},{24,0},{28,4},{1,25},{... | collective-permute-start | bytes 393224 | tf_op jit(solution)/shard_map/ppermute | solution.py:550
  175.4 9.1 %collective-permute-start.31 = (bf16[512,128]{1,0:T(8,128)(2,1)S(1)}, bf16[512,128]{1,0:T(8,128)(2,1)S(1)}, u32[]{:S(2)}, u32[]{:S(2)}) collective-permute-start(bf16[512,128]{1,0:T(8,128)(2,1)S(1)} %get-tuple-element.88), channel_id=1, source_target_pairs={{0,28},{4,24},{8,20},{12,16},{16,12},{20,8},{24,4},{28,0},{1,29},{... | collective-permute-start | bytes 393224 | tf_op jit(solution)/shard_map/ppermute | solution.py:550

commit v13 on v11

--- a/solution.py
+++ b/solution.py
@@ -13,6 +13,7 @@
 LATE_STREAMS = 2
 STEP = 16
 BETA = 2.0
+LOG2_E = 1.4426950408889634
 ROUND = 1.5 * 2.0 ** 23
 RIDGE = 1.0
 MIB = 1024 * 1024
@@ -24,7 +25,7 @@
 LATE_VMEM = 12 * MIB
 BASIS_CALLS = (1, 2, 3, 2)
 UNROLL = 32
-PICK_UNROLL = 16
+PICK_UNROLL = 32
 SUB = 8
 HBM_SPARE = 32
 COST_US = 10 ** 9
@@ -165,7 +166,7 @@
                 )
             highest = functools.reduce(jnp.maximum, power)
             highest = jnp.max(highest, axis=1, keepdims=True)
-            expo = [jnp.exp(BETA * (value - highest)) for value in power]
+            expo = [jnp.exp2((value - highest) * (BETA * LOG2_E)) for value in power]
             total = jnp.sum(functools.reduce(jnp.add, expo), axis=1, keepdims=True)
             scale = 1.0 / total
             for chunk in range(nper // 128):

time: 144 us -> 144 us (level); the launches traced: 143 us -> 141 us
  waiting for transfers between devices: 34.4 us -> 31.4 us
    ppermute x28, waiting for transfers between devices: 22.3 us -> 19.3 us  [exchange(): lax.ppermute(blocks[step], 'tm', [(i, i ^ step) for i in range(count)])]
  transfers between devices with their start and end apart: 35 -> 35, of which waited for: 16 -> 14; matrix products, arithmetic and copies ran while one was open for 7% -> 7% of each run, Pallas kernels for 15% -> 16%
where the time goes in v13:
time: 144 us; the launch traced here: 141 us
  Pallas kernels  51.1 us (35%)
  starting transfers between devices  46.1 us (32%)
  waiting for transfers between devices  31.4 us (22%)
  other arithmetic  9.49 us (7%)
  local copies, waits for them, and re-layouts  2.15 us (1%)
    ppermute x28, starting transfers between devices, exchange(): lax.ppermute(blocks[step], 'tm', [(i, i ^ step) for i in range(count)])  31.1 us
    ppermute x28, waiting for transfers between devices, exchange(): lax.ppermute(blocks[step], 'tm', [(i, i ^ step) for i in range(count)])  19.3 us
    pallas_call x2, Pallas kernels, fit_plans(): pl.pallas_call(functools.partial(fit_kernel, order), in_specs=[SMEM, SMEM...  16.5 us
    pallas_call x4, Pallas kernels, make_basis(): pl.pallas_call(functools.partial(basis_kernel, len(after)), grid=(sched_d...  14.3 us
    pallas_call x2, Pallas kernels, place_early(): pl.pallas_call(functools.partial(early_kernel, owners, table_base), in_sp...  8.28 us
    ppermute x3, waiting for transfers between devices, pass_along(): lax.ppermute(left, 'sky', [(i, i - 1) for i in range(1, count - hop + 1)])  8.04 us
    ppermute x3, starting transfers between devices, pass_along(): lax.ppermute(right, 'sky', [(i, i + 1) for i in range(hop - 1, count - 1)])  6.08 us
    all_to_all x1, starting transfers between devices, first_hop(): asked = lax.all_to_all(held, 'tm', split_axis=0, concat_axis=0, tiled=True)  5.1 us
  transfers between devices with their start and end apart: 35, of which 14 were waited for; matrix products, arithmetic and copies ran while one was open for 7% of the time, Pallas kernels for 16%

profile of v13, /device:TPU:1, one launch (start us, length us, event | category | flops | bytes accessed | tf_op | source)
XLA Modules:
  0.0 141.5 jit_solution(9180657100362805651)
XLA Ops:
  0.6 1.3 collective-permute-start.1
  1.9 4.7 %collective-permute-start = (bf16[4,128,512]{2,1,0:T(8,128)(2,1)}, bf16[4,128,512]{2,1,0:T(8,128)(2,1)S(1)}, u32[]{:S(2)}, u32[]{:S(2)}) collective-permute-start(bf16[4,128,512]{2,1,0:T(8,128)(2,1)} %own_ref.3), channel_id=1, source_target_pairs={{0,1},{1,2},{2,3},{4,5},{5,6},{6,7},{8,9},{9,10},{10,11},{12,13},{... | collective-permute-start | bytes 1572872 | tf_op jit(solution)/shard_map/ppermute | solution.py:557
  10.3 0.8 fusion.18
  11.6 3.4 %select_reduce_fusion = s32[4096]{0:T(1024)S(1)} fusion(s32[2048]{0:T(1024)S(1)} %bitcast.34, s32[2048]{0:T(1024)S(1)} %bitcast.33), kind=kLoop, calls=%fused_computation | loop fusion | flops 25161728 | bytes 32768 | tf_op jit(solution)/shard_map/reduce_sum | solution.py:519
  15.2 1.3 collective-permute-done.1.refs_1_
  16.5 1.3 collective-permute-start.3
  18.6 1.8 %shard_map.77 = (bf16[1,256,2048]{2,1,0:T(8,128)(2,1)S(1)}, f32[1,1,2048]{2,1,0:T(1,128)S(1)}) custom-call(f32[256,128]{1,0:T(8,128)S(1)} %broadcast_in_dim.50.time_ref, f32[1,1024]{1,0:T(1,128)S(1)} %bitcast.27, f32[1,1024]{1,0:T(1,128)S(1)} %bitcast.23, bf16[4,128,512]{2,1,0:T(8,128)(2,1)S(1)} %collective-permute-done.refs_0_, ...), custom_call_target="tpu_custom_call" | custom-call | flops 2097152000 | bytes 1048576 | tf_op jit(solution)/shard_map/pallas_call | solution.py:92
  20.4 1.0 copy-done.3
  22.0 5.1 %all-to-all-start = ((s32[8,1,512]{2,1,0:T(1,128)}), s32[8,1,512]{2,1,0:T(1,128)S(1)}, u32[]{:S(2)}, u32[]{:S(2)}) async-start(s32[8,1,512]{2,1,0:T(1,128)} %all_to_all.6), calls=%async_computation | async-start | bytes 32768 | tf_op jit(solution)/shard_map/all_to_all | solution.py:586
  27.1 4.0 %all-to-all-done = s32[8,1,512]{2,1,0:T(1,128)S(1)} async-done(((s32[8,1,512]{2,1,0:T(1,128)}), s32[8,1,512]{2,1,0:T(1,128)S(1)}, u32[]{:S(2)}, u32[]{:S(2)}) %all-to-all-start) | async-done | bytes 16416 | tf_op jit(solution)/shard_map/all_to_all | solution.py:586
  31.4 1.3 collective-permute-start.5
  33.5 5.3 %shard_map.80 = (bf16[3,256,2048]{2,1,0:T(8,128)(2,1)S(1)}, f32[3,1,2048]{2,1,0:T(1,128)S(1)}) custom-call(f32[768,128]{1,0:T(8,128)S(1)} %broadcast_in_dim.55.time_ref, f32[1,1024]{1,0:T(1,128)S(1)} %bitcast.28, f32[1,1024]{1,0:T(1,128)S(1)} %bitcast.24, bf16[4,128,512]{2,1,0:T(8,128)(2,1)S(1)} %collective-permute-done.2.refs_2_.refs_0_, ...), custom_call_target="tpu_custom_call" | custom-call | flops 6291456000 | bytes 3145728 | tf_op jit(solution)/shard_map/pallas_call | solution.py:92
  39.0 3.6 %shard_map.79 = (bf16[2,256,2048]{2,1,0:T(8,128)(2,1)S(1)}, f32[2,1,2048]{2,1,0:T(1,128)S(1)}) custom-call(f32[512,128]{1,0:T(8,128)S(1)} %broadcast_in_dim.53.time_ref, f32[1,1024]{1,0:T(1,128)S(1)} %bitcast.29, f32[1,1024]{1,0:T(1,128)S(1)} %bitcast.25, bf16[4,128,512]{2,1,0:T(8,128)(2,1)S(1)} %collective-permute-done.2.refs_2_.refs_0_, ...), custom_call_target="tpu_custom_call" | custom-call | flops 4194304000 | bytes 2097152 | tf_op jit(solution)/shard_map/pallas_call | solution.py:92
  42.7 6.8 %collective-permute-done.5.refs_5_ = bf16[4,128,512]{2,1,0:T(8,128)(2,1)S(1)} collective-permute-done((bf16[4,128,512]{2,1,0:T(8,128)(2,1)S(1)}, bf16[4,128,512]{2,1,0:T(8,128)(2,1)S(1)}, u32[]{:S(2)}, u32[]{:S(2)}) %collective-permute-start.5) | collective-permute-done | bytes 524320 | tf_op jit(solution)/shard_map/ppermute | solution.py:558
  49.4 3.9 %shard_map.78 = (bf16[512,128]{1,0:T(8,128)(2,1)S(1)}, bf16[512,128]{1,0:T(8,128)(2,1)S(1)}, bf16[512,128]{1,0:T(8,128)(2,1)S(1)}, bf16[512,128]{1,0:T(8,128)(2,...) custom-call(s32[4096]{0:T(1024)S(1)} %bitcast.18, ...), custom_call_target="tpu_custom_call" | custom-call | flops 5000000000 | bytes 1048576 | tf_op jit(solution)/shard_map/pallas_call | solution.py:380
  53.4 1.0 collective-permute-start.6
  54.4 1.2 collective-permute-start.7
  56.0 2.0 %collective-permute-start.9 = (bf16[512,128]{1,0:T(8,128)(2,1)S(1)}, bf16[512,128]{1,0:T(8,128)(2,1)S(1)}, u32[]{:S(2)}, u32[]{:S(2)}) collective-permute-start(bf16[512,128]{1,0:T(8,128)(2,1)S(1)} %get-tuple-element.51), channel_id=1, source_target_pairs={{0,20},{4,16},{8,28},{12,24},{16,4},{20,0},{24,12},{28,8},{1,21},{... | collective-permute-start | bytes 393224 | tf_op jit(solution)/shard_map/ppermute | solution.py:548
  58.2 3.6 %shard_map.81 = (bf16[2,256,2048]{2,1,0:T(8,128)(2,1)S(1)}, f32[2,1,2048]{2,1,0:T(1,128)S(1)}) custom-call(f32[512,128]{1,0:T(8,128)S(1)} %broadcast_in_dim.57.time_ref, f32[1,1024]{1,0:T(1,128)S(1)} %bitcast.30, f32[1,1024]{1,0:T(1,128)S(1)} %bitcast.26, bf16[512,128]{1,0:T(8,128)(2,1)S(1)} %get-tuple-element.47.refs_0_), custom_call_target="tpu_custom_call" | custom-call | flops 4194304000 | bytes 2097152 | tf_op jit(solution)/shard_map/pallas_call | solution.py:92
  61.7 1.2 collective-permute-start.11
  63.0 1.6 %collective-permute-start.12 = (bf16[512,128]{1,0:T(8,128)(2,1)S(1)}, bf16[512,128]{1,0:T(8,128)(2,1)S(1)}, u32[]{:S(2)}, u32[]{:S(2)}) collective-permute-start(bf16[512,128]{1,0:T(8,128)(2,1)S(1)} %get-tuple-element.54), channel_id=1, source_target_pairs={{0,28},{4,24},{8,20},{12,16},{16,12},{20,8},{24,4},{28,0},{1,29},{... | collective-permute-start | bytes 393224 | tf_op jit(solution)/shard_map/ppermute | solution.py:548
  64.6 3.0 %collective-permute-done.11.refs_6_ = bf16[512,128]{1,0:T(8,128)(2,1)S(1)} collective-permute-done((bf16[512,128]{1,0:T(8,128)(2,1)S(1)}, bf16[512,128]{1,0:T(8,128)(2,1)S(1)}, u32[]{:S(2)}, u32[]{:S(2)}) %collective-permute-start.11) | collective-permute-done | bytes 131104 | tf_op jit(solution)/shard_map/ppermute | solution.py:548
  67.6 3.1 %collective-permute-done.12.refs_7_ = bf16[512,128]{1,0:T(8,128)(2,1)S(1)} collective-permute-done((bf16[512,128]{1,0:T(8,128)(2,1)S(1)}, bf16[512,128]{1,0:T(8,128)(2,1)S(1)}, u32[]{:S(2)}, u32[]{:S(2)}) %collective-permute-start.12) | collective-permute-done | bytes 131104 | tf_op jit(solution)/shard_map/ppermute | solution.py:548
  70.7 8.6 %shard_map.82 = (bf16[512,128]{1,0:T(8,128)(2,1)S(1)}, bf16[512,128]{1,0:T(8,128)(2,1)S(1)}, bf16[512,128]{1,0:T(8,128)(2,1)S(1)}, bf16[512,128]{1,0:T(8,128)(2,...) custom-call(s32[8,24]{1,0:T(8,128)S(1)} %get-tuple-element.104.src_r, ...), custom_call_target="tpu_custom_call" | custom-call | flops 10737418240 | bytes 8388608 | tf_op jit(solution)/shard_map/pallas_call | solution.py:218
  79.5 1.1 collective-permute-start.14
  81.0 2.1 %collective-permute-start.16 = (bf16[512,128]{1,0:T(8,128)(2,1)S(1)}, bf16[512,128]{1,0:T(8,128)(2,1)S(1)}, u32[]{:S(2)}, u32[]{:S(2)}) collective-permute-start(bf16[512,128]{1,0:T(8,128)(2,1)S(1)} %get-tuple-element.66), channel_id=1, source_target_pairs={{0,20},{4,16},{8,28},{12,24},{16,4},{20,0},{24,12},{28,8},{1,21},{... | collective-permute-start | bytes 393224 | tf_op jit(solution)/shard_map/ppermute | solution.py:548
  83.1 1.2 collective-permute-start.18
  84.3 2.6 %collective-permute-start.19 = (bf16[512,128]{1,0:T(8,128)(2,1)S(1)}, bf16[512,128]{1,0:T(8,128)(2,1)S(1)}, u32[]{:S(2)}, u32[]{:S(2)}) collective-permute-start(bf16[512,128]{1,0:T(8,128)(2,1)S(1)} %get-tuple-element.69), channel_id=1, source_target_pairs={{0,28},{4,24},{8,20},{12,16},{16,12},{20,8},{24,4},{28,0},{1,29},{... | collective-permute-start | bytes 393224 | tf_op jit(solution)/shard_map/ppermute | solution.py:548
  86.9 0.9 collective-permute-done.16.refs_4_
  87.8 1.9 %collective-permute-done.17.refs_5_ = bf16[512,128]{1,0:T(8,128)(2,1)S(1)} collective-permute-done((bf16[512,128]{1,0:T(8,128)(2,1)S(1)}, bf16[512,128]{1,0:T(8,128)(2,1)S(1)}, u32[]{:S(2)}, u32[]{:S(2)}) %collective-permute-start.17) | collective-permute-done | bytes 131104 | tf_op jit(solution)/shard_map/ppermute | solution.py:548
  89.8 4.2 %shard_map.83.part_ref = f32[4096,128]{1,0:T(8,128)S(1)} custom-call(s32[4096]{0:T(1024)S(1)} %bitcast.19, s32[8]{0:T(128)S(1)} %fusion.4.cnt_ref, s32[2]{0:T(128)S(1)} %pad_add_fusion.where_ref, bf16[4,512,256]{2,1,0:T(8,128)(2,1)S(1)} %copy-done, bf16[512,128]{1,0:T(8,128)(2,1)S(1)} %get-tuple-element.62.refs_0_, ...), custom_call_target="tpu_custom_call" | custom-call | flops 6000000000 | bytes 1048576 | tf_op jit(solution)/shard_map/pallas_call | solution.py:352
  94.3 4.9 %shard_map.84 = (f32[131072,128]{1,0:T(8,128)}, bf16[512,128]{1,0:T(8,128)(2,1)S(1)}, bf16[512,128]{1,0:T(8,128)(2,1)S(1)}, bf16[512,128]{1,0:T(8,128)(2,1)S(1)}...) custom-call(s32[4096]{0:T(1024)S(1)} %bitcast.20, ...), custom_call_target="tpu_custom_call" | custom-call | flops 7000000000 | bytes 1048576 | tf_op jit(solution)/shard_map/pallas_call | solution.py:437
  99.4 2.1 %collective-permute-start.21 = (bf16[512,128]{1,0:T(8,128)(2,1)S(1)}, bf16[512,128]{1,0:T(8,128)(2,1)S(1)}, u32[]{:S(2)}, u32[]{:S(2)}) collective-permute-start(bf16[512,128]{1,0:T(8,128)(2,1)S(1)} %get-tuple-element.73), channel_id=1, source_target_pairs={{0,16},{4,20},{8,24},{12,28},{16,0},{20,4},{24,8},{28,12},{1,17},{... | collective-permute-start | bytes 393224 | tf_op jit(solution)/shard_map/ppermute | solution.py:548
  101.9 1.8 %collective-permute-start.23 = (bf16[512,128]{1,0:T(8,128)(2,1)S(1)}, bf16[512,128]{1,0:T(8,128)(2,1)S(1)}, u32[]{:S(2)}, u32[]{:S(2)}) collective-permute-start(bf16[512,128]{1,0:T(8,128)(2,1)S(1)} %get-tuple-element.75), channel_id=1, source_target_pairs={{0,20},{4,16},{8,28},{12,24},{16,4},{20,0},{24,12},{28,8},{1,21},{... | collective-permute-start | bytes 393224 | tf_op jit(solution)/shard_map/ppermute | solution.py:548
  103.8 1.2 collective-permute-start.25
  105.0 3.3 %collective-permute-start.26 = (bf16[512,128]{1,0:T(8,128)(2,1)S(1)}, bf16[512,128]{1,0:T(8,128)(2,1)S(1)}, u32[]{:S(2)}, u32[]{:S(2)}) collective-permute-start(bf16[512,128]{1,0:T(8,128)(2,1)S(1)} %get-tuple-element.78), channel_id=1, source_target_pairs={{0,28},{4,24},{8,20},{12,16},{16,12},{20,8},{24,4},{28,0},{1,29},{... | collective-permute-start | bytes 393224 | tf_op jit(solution)/shard_map/ppermute | solution.py:548
  108.3 2.2 %collective-permute-done.24.refs_5_ = bf16[512,128]{1,0:T(8,128)(2,1)S(1)} collective-permute-done((bf16[512,128]{1,0:T(8,128)(2,1)S(1)}, bf16[512,128]{1,0:T(8,128)(2,1)S(1)}, u32[]{:S(2)}, u32[]{:S(2)}) %collective-permute-start.24) | collective-permute-done | bytes 131104 | tf_op jit(solution)/shard_map/ppermute | solution.py:548
  110.5 1.6 %collective-permute-done.25.refs_6_ = bf16[512,128]{1,0:T(8,128)(2,1)S(1)} collective-permute-done((bf16[512,128]{1,0:T(8,128)(2,1)S(1)}, bf16[512,128]{1,0:T(8,128)(2,1)S(1)}, u32[]{:S(2)}, u32[]{:S(2)}) %collective-permute-start.25) | collective-permute-done | bytes 131104 | tf_op jit(solution)/shard_map/ppermute | solution.py:548
  112.1 3.0 %collective-permute-done.26.refs_7_ = bf16[512,128]{1,0:T(8,128)(2,1)S(1)} collective-permute-done((bf16[512,128]{1,0:T(8,128)(2,1)S(1)}, bf16[512,128]{1,0:T(8,128)(2,1)S(1)}, u32[]{:S(2)}, u32[]{:S(2)}) %collective-permute-start.26) | collective-permute-done | bytes 131104 | tf_op jit(solution)/shard_map/ppermute | solution.py:548
  115.1 7.9 %shard_map.85 = (bf16[512,128]{1,0:T(8,128)(2,1)S(1)}, bf16[512,128]{1,0:T(8,128)(2,1)S(1)}, bf16[512,128]{1,0:T(8,128)(2,1)S(1)}, bf16[512,128]{1,0:T(8,128)(2,...) custom-call(s32[8,24]{1,0:T(8,128)S(1)} %get-tuple-element.104.src_r, ...), custom_call_target="tpu_custom_call" | custom-call | flops 10737418240 | bytes 8388608 | tf_op jit(solution)/shard_map/pallas_call | solution.py:218
  123.3 1.0 collective-permute-start.28
  124.8 2.2 %collective-permute-start.30 = (bf16[512,128]{1,0:T(8,128)(2,1)S(1)}, bf16[512,128]{1,0:T(8,128)(2,1)S(1)}, u32[]{:S(2)}, u32[]{:S(2)}) collective-permute-start(bf16[512,128]{1,0:T(8,128)(2,1)S(1)} %get-tuple-element.83), channel_id=1, source_target_pairs={{0,20},{4,16},{8,28},{12,24},{16,4},{20,0},{24,12},{28,8},{1,21},{... | collective-permute-start | bytes 393224 | tf_op jit(solution)/shard_map/ppermute | solution.py:548
  127.0 0.8 reduce.1
  127.8 1.2 collective-permute-start.32
  129.0 1.9 %collective-permute-start.33 = (bf16[512,128]{1,0:T(8,128)(2,1)S(1)}, bf16[512,128]{1,0:T(8,128)(2,1)S(1)}, u32[]{:S(2)}, u32[]{:S(2)}) collective-permute-start(bf16[512,128]{1,0:T(8,128)(2,1)S(1)} %get-tuple-element.86), channel_id=1, source_target_pairs={{0,28},{4,24},{8,20},{12,16},{16,12},{20,8},{24,4},{28,0},{1,29},{... | collective-permute-start | bytes 393224 | tf_op jit(solution)/shard_map/ppermute | solution.py:548
  131.6 1.8 %collective-permute-done.31.refs_5_ = bf16[512,128]{1,0:T(8,128)(2,1)S(1)} collective-permute-done((bf16[512,128]{1,0:T(8,128)(2,1)S(1)}, bf16[512,128]{1,0:T(8,128)(2,1)S(1)}, u32[]{:S(2)}, u32[]{:S(2)}) %collective-permute-start.31) | collective-permute-done | bytes 131104 | tf_op jit(solution)/shard_map/ppermute | solution.py:548
  133.4 4.1 %shard_map.86.part_ref = f32[4096,128]{1,0:T(8,128)S(1)} custom-call(s32[4096]{0:T(1024)S(1)} %bitcast.21, s32[8]{0:T(128)S(1)} %fusion.4.cnt_ref, s32[2]{0:T(128)S(1)} %pad_add_fusion.where_ref, f32[131072,128]{1,0:T(8,128)} %get-tuple-element.70.base_ref, bf16[512,128]{1,0:T(8,128)(2,1)S(1)} %get-tuple-element.79.refs_0_, ...), custom_call_target="tpu_custom_call" | custom-call | flops 6000000000 | bytes 1048576 | tf_op jit(solution)/shard_map/pallas_call | solution.py:352
  138.2 3.2 %shard_map.87 = f32[4,512,256]{2,1,0:T(8,128)} custom-call(s32[4096]{0:T(1024)S(1)} %bitcast.22, s32[8]{0:T(128)S(1)} %fusion.4.cnt_ref, s32[2]{0:T(128)S(1)} %pad_add_fusion.where_ref, f32[4096,128]{1,0:T(8,128)S(1)} %shard_map.86.part_ref, bf16[512,128]{1,0:T(8,128)(2,1)S(1)} %collective-permute-done.32.refs_0_, ...), custom_call_target="tpu_custom_call" | custom-call | flops 4000000000 | bytes 1048576 | tf_op jit(solution)/shard_map/pallas_call | solution.py:479
  (83 shorter events, 11.3 us)
Async XLA Ops:
  0.6 15.9 %collective-permute-start.1 = (bf16[4,128,512]{2,1,0:T(8,128)(2,1)}, bf16[4,128,512]{2,1,0:T(8,128)(2,1)S(1)}, u32[]{:S(2)}, u32[]{:S(2)}) collective-permute-start(bf16[4,128,512]{2,1,0:T(8,128)(2,1)} %own_ref.3), channel_id=1, source_target_pairs={{1,0},{2,1},{3,2},{5,4},{6,5},{7,6},{9,8},{10,9},{11,10},{13,12},{... | collective-permute-start | bytes 1572872 | tf_op jit(solution)/shard_map/ppermute | solution.py:558
  1.9 15.9 %collective-permute-start = (bf16[4,128,512]{2,1,0:T(8,128)(2,1)}, bf16[4,128,512]{2,1,0:T(8,128)(2,1)S(1)}, u32[]{:S(2)}, u32[]{:S(2)}) collective-permute-start(bf16[4,128,512]{2,1,0:T(8,128)(2,1)} %own_ref.3), channel_id=1, source_target_pairs={{0,1},{1,2},{2,3},{4,5},{5,6},{6,7},{8,9},{9,10},{10,11},{12,13},{... | collective-permute-start | bytes 1572872 | tf_op jit(solution)/shard_map/ppermute | solution.py:557
  16.5 14.8 %collective-permute-start.3 = (bf16[4,128,512]{2,1,0:T(8,128)(2,1)S(1)}, bf16[4,128,512]{2,1,0:T(8,128)(2,1)S(1)}, u32[]{:S(2)}, u32[]{:S(2)}) collective-permute-start(bf16[4,128,512]{2,1,0:T(8,128)(2,1)S(1)} %collective-permute-done.1.refs_1_), channel_id=1, source_target_pairs={{1,0},{2,1},{5,4},{6,5},{9,8},{10,9},{13,12},{14,13},{17,16},{18,1... | collective-permute-start | bytes 1572872 | tf_op jit(solution)/shard_map/ppermute | solution.py:558
  17.8 14.8 %collective-permute-start.2 = (bf16[4,128,512]{2,1,0:T(8,128)(2,1)S(1)}, bf16[4,128,512]{2,1,0:T(8,128)(2,1)S(1)}, u32[]{:S(2)}, u32[]{:S(2)}) collective-permute-start(bf16[4,128,512]{2,1,0:T(8,128)(2,1)S(1)} %collective-permute-done.refs_0_), channel_id=1, source_target_pairs={{1,2},{2,3},{5,6},{6,7},{9,10},{10,11},{13,14},{14,15},{17,18},{18... | collective-permute-start | bytes 1572872 | tf_op jit(solution)/shard_map/ppermute | solution.py:557
  20.4 1.0 copy-start.3
  22.0 9.1 %all-to-all-start = ((s32[8,1,512]{2,1,0:T(1,128)}), s32[8,1,512]{2,1,0:T(1,128)S(1)}, u32[]{:S(2)}, u32[]{:S(2)}) async-start(s32[8,1,512]{2,1,0:T(1,128)} %all_to_all.6), calls=%async_computation | async-start | bytes 32768 | tf_op jit(solution)/shard_map/all_to_all | solution.py:586
  31.4 18.1 %collective-permute-start.5 = (bf16[4,128,512]{2,1,0:T(8,128)(2,1)S(1)}, bf16[4,128,512]{2,1,0:T(8,128)(2,1)S(1)}, u32[]{:S(2)}, u32[]{:S(2)}) collective-permute-start(bf16[4,128,512]{2,1,0:T(8,128)(2,1)S(1)} %collective-permute-done.3.refs_3_.refs_1_), channel_id=1, source_target_pairs={{1,0},{5,4},{9,8},{13,12},{17,16},{21,20},{25,24},{29,28}} | collective-permute-start | bytes 1572872 | tf_op jit(solution)/shard_map/ppermute | solution.py:558
  32.7 16.8 %collective-permute-start.4 = (bf16[4,128,512]{2,1,0:T(8,128)(2,1)S(1)}, bf16[4,128,512]{2,1,0:T(8,128)(2,1)S(1)}, u32[]{:S(2)}, u32[]{:S(2)}) collective-permute-start(bf16[4,128,512]{2,1,0:T(8,128)(2,1)S(1)} %collective-permute-done.2.refs_2_.refs_0_), channel_id=1, source_target_pairs={{2,3},{6,7},{10,11},{14,15},{18,19},{22,23},{26,27},{30,31}} | collective-permute-start | bytes 1572872 | tf_op jit(solution)/shard_map/ppermute | solution.py:557
  39.0 10.4 %copy-start = (bf16[4,512,256]{2,1,0:T(8,128)(2,1)S(1)}, bf16[4,512,256]{2,1,0:T(8,128)(2,1)}, u32[]{:S(2)}) copy-start(bf16[4,512,256]{2,1,0:T(8,128)(2,1)} %base_ref.3) | copy-start | bytes 3145732
  39.0 10.4 %copy-start.1 = (bf16[4,128,512]{2,1,0:T(8,128)(2,1)S(1)}, bf16[4,128,512]{2,1,0:T(8,128)(2,1)}, u32[]{:S(2)}) copy-start(bf16[4,128,512]{2,1,0:T(8,128)(2,1)} %own_ref.3) | copy-start | bytes 1572868
  39.0 10.4 %copy-start.2 = (s32[4]{0:T(128)S(1)}, s32[4]{0:T(128)}, u32[]{:S(2)}) copy-start(s32[4]{0:T(128)} %count_ref.3) | copy-start | bytes 52
  53.4 8.4 %collective-permute-start.6 = (bf16[512,128]{1,0:T(8,128)(2,1)S(1)}, bf16[512,128]{1,0:T(8,128)(2,1)S(1)}, u32[]{:S(2)}, u32[]{:S(2)}) collective-permute-start(bf16[512,128]{1,0:T(8,128)(2,1)S(1)} %get-tuple-element.48), channel_id=1, source_target_pairs={{0,4},{4,0},{8,12},{12,8},{16,20},{20,16},{24,28},{28,24},{1,5},{5... | collective-permute-start | bytes 393224 | tf_op jit(solution)/shard_map/ppermute | solution.py:548
  54.4 8.6 %collective-permute-start.7 = (bf16[512,128]{1,0:T(8,128)(2,1)S(1)}, bf16[512,128]{1,0:T(8,128)(2,1)S(1)}, u32[]{:S(2)}, u32[]{:S(2)}) collective-permute-start(bf16[512,128]{1,0:T(8,128)(2,1)S(1)} %get-tuple-element.49), channel_id=1, source_target_pairs={{0,16},{4,20},{8,24},{12,28},{16,0},{20,4},{24,8},{28,12},{1,17},{... | collective-permute-start | bytes 393224 | tf_op jit(solution)/shard_map/ppermute | solution.py:548
  55.5 9.0 %collective-permute-start.8 = (bf16[512,128]{1,0:T(8,128)(2,1)S(1)}, bf16[512,128]{1,0:T(8,128)(2,1)S(1)}, u32[]{:S(2)}, u32[]{:S(2)}) collective-permute-start(bf16[512,128]{1,0:T(8,128)(2,1)S(1)} %get-tuple-element.50), channel_id=1, source_target_pairs={{0,8},{4,12},{8,0},{12,4},{16,24},{20,28},{24,16},{28,20},{1,9},{5... | collective-permute-start | bytes 393224 | tf_op jit(solution)/shard_map/ppermute | solution.py:548
  56.0 8.5 %collective-permute-start.9 = (bf16[512,128]{1,0:T(8,128)(2,1)S(1)}, bf16[512,128]{1,0:T(8,128)(2,1)S(1)}, u32[]{:S(2)}, u32[]{:S(2)}) collective-permute-start(bf16[512,128]{1,0:T(8,128)(2,1)S(1)} %get-tuple-element.51), channel_id=1, source_target_pairs={{0,20},{4,16},{8,28},{12,24},{16,4},{20,0},{24,12},{28,8},{1,21},{... | collective-permute-start | bytes 393224 | tf_op jit(solution)/shard_map/ppermute | solution.py:548
  58.0 6.6 %collective-permute-start.10 = (bf16[512,128]{1,0:T(8,128)(2,1)S(1)}, bf16[512,128]{1,0:T(8,128)(2,1)S(1)}, u32[]{:S(2)}, u32[]{:S(2)}) collective-permute-start(bf16[512,128]{1,0:T(8,128)(2,1)S(1)} %get-tuple-element.52), channel_id=1, source_target_pairs={{0,12},{4,8},{8,4},{12,0},{16,28},{20,24},{24,20},{28,16},{1,13},{... | collective-permute-start | bytes 393224 | tf_op jit(solution)/shard_map/ppermute | solution.py:548
  58.1 12.6 %copy-start.4 = (bf16[1,256,2048]{2,1,0:T(8,128)(2,1)S(1)}, bf16[1,256,2048]{2,1,0:T(8,128)(2,1)}, u32[]{:S(2)}) copy-start(bf16[1,256,2048]{2,1,0:T(8,128)(2,1)} %copy-done.3) | copy-start | bytes 3145732
  61.7 5.9 %collective-permute-start.11 = (bf16[512,128]{1,0:T(8,128)(2,1)S(1)}, bf16[512,128]{1,0:T(8,128)(2,1)S(1)}, u32[]{:S(2)}, u32[]{:S(2)}) collective-permute-start(bf16[512,128]{1,0:T(8,128)(2,1)S(1)} %get-tuple-element.53), channel_id=1, source_target_pairs={{0,24},{4,28},{8,16},{12,20},{16,8},{20,12},{24,0},{28,4},{1,25},{... | collective-permute-start | bytes 393224 | tf_op jit(solution)/shard_map/ppermute | solution.py:548
  63.0 7.7 %collective-permute-start.12 = (bf16[512,128]{1,0:T(8,128)(2,1)S(1)}, bf16[512,128]{1,0:T(8,128)(2,1)S(1)}, u32[]{:S(2)}, u32[]{:S(2)}) collective-permute-start(bf16[512,128]{1,0:T(8,128)(2,1)S(1)} %get-tuple-element.54), channel_id=1, source_target_pairs={{0,28},{4,24},{8,20},{12,16},{16,12},{20,8},{24,4},{28,0},{1,29},{... | collective-permute-start | bytes 393224 | tf_op jit(solution)/shard_map/ppermute | solution.py:548
  79.4 3.7 %collective-permute-start.13 = (bf16[512,128]{1,0:T(8,128)(2,1)S(1)}, bf16[512,128]{1,0:T(8,128)(2,1)S(1)}, u32[]{:S(2)}, u32[]{:S(2)}) collective-permute-start(bf16[512,128]{1,0:T(8,128)(2,1)S(1)} %get-tuple-element.63), channel_id=1, source_target_pairs={{0,4},{4,0},{8,12},{12,8},{16,20},{20,16},{24,28},{28,24},{1,5},{5... | collective-permute-start | bytes 393224 | tf_op jit(solution)/shard_map/ppermute | solution.py:548
  79.5 4.8 %collective-permute-start.14 = (bf16[512,128]{1,0:T(8,128)(2,1)S(1)}, bf16[512,128]{1,0:T(8,128)(2,1)S(1)}, u32[]{:S(2)}, u32[]{:S(2)}) collective-permute-start(bf16[512,128]{1,0:T(8,128)(2,1)S(1)} %get-tuple-element.64), channel_id=1, source_target_pairs={{0,16},{4,20},{8,24},{12,28},{16,0},{20,4},{24,8},{28,12},{1,17},{... | collective-permute-start | bytes 393224 | tf_op jit(solution)/shard_map/ppermute | solution.py:548
  80.6 6.4 %collective-permute-start.15 = (bf16[512,128]{1,0:T(8,128)(2,1)S(1)}, bf16[512,128]{1,0:T(8,128)(2,1)S(1)}, u32[]{:S(2)}, u32[]{:S(2)}) collective-permute-start(bf16[512,128]{1,0:T(8,128)(2,1)S(1)} %get-tuple-element.65), channel_id=1, source_target_pairs={{0,8},{4,12},{8,0},{12,4},{16,24},{20,28},{24,16},{28,20},{1,9},{5... | collective-permute-start | bytes 393224 | tf_op jit(solution)/shard_map/ppermute | solution.py:548
  81.0 6.8 %collective-permute-start.16 = (bf16[512,128]{1,0:T(8,128)(2,1)S(1)}, bf16[512,128]{1,0:T(8,128)(2,1)S(1)}, u32[]{:S(2)}, u32[]{:S(2)}) collective-permute-start(bf16[512,128]{1,0:T(8,128)(2,1)S(1)} %get-tuple-element.66), channel_id=1, source_target_pairs={{0,20},{4,16},{8,28},{12,24},{16,4},{20,0},{24,12},{28,8},{1,21},{... | collective-permute-start | bytes 393224 | tf_op jit(solution)/shard_map/ppermute | solution.py:548
  83.1 6.7 %collective-permute-start.17 = (bf16[512,128]{1,0:T(8,128)(2,1)S(1)}, bf16[512,128]{1,0:T(8,128)(2,1)S(1)}, u32[]{:S(2)}, u32[]{:S(2)}) collective-permute-start(bf16[512,128]{1,0:T(8,128)(2,1)S(1)} %get-tuple-element.67), channel_id=1, source_target_pairs={{0,12},{4,8},{8,4},{12,0},{16,28},{20,24},{24,20},{28,16},{1,13},{... | collective-permute-start | bytes 393224 | tf_op jit(solution)/shard_map/ppermute | solution.py:548
  83.1 10.9 %collective-permute-start.18 = (bf16[512,128]{1,0:T(8,128)(2,1)S(1)}, bf16[512,128]{1,0:T(8,128)(2,1)S(1)}, u32[]{:S(2)}, u32[]{:S(2)}) collective-permute-start(bf16[512,128]{1,0:T(8,128)(2,1)S(1)} %get-tuple-element.68), channel_id=1, source_target_pairs={{0,24},{4,28},{8,16},{12,20},{16,8},{20,12},{24,0},{28,4},{1,25},{... | collective-permute-start | bytes 393224 | tf_op jit(solution)/shard_map/ppermute | solution.py:548
  84.3 10.0 %collective-permute-start.19 = (bf16[512,128]{1,0:T(8,128)(2,1)S(1)}, bf16[512,128]{1,0:T(8,128)(2,1)S(1)}, u32[]{:S(2)}, u32[]{:S(2)}) collective-permute-start(bf16[512,128]{1,0:T(8,128)(2,1)S(1)} %get-tuple-element.69), channel_id=1, source_target_pairs={{0,28},{4,24},{8,20},{12,16},{16,12},{20,8},{24,4},{28,0},{1,29},{... | collective-permute-start | bytes 393224 | tf_op jit(solution)/shard_map/ppermute | solution.py:548
  99.3 4.5 %collective-permute-start.20 = (bf16[512,128]{1,0:T(8,128)(2,1)S(1)}, bf16[512,128]{1,0:T(8,128)(2,1)S(1)}, u32[]{:S(2)}, u32[]{:S(2)}) collective-permute-start(bf16[512,128]{1,0:T(8,128)(2,1)S(1)} %get-tuple-element.72), channel_id=1, source_target_pairs={{0,4},{4,0},{8,12},{12,8},{16,20},{20,16},{24,28},{28,24},{1,5},{5... | collective-permute-start | bytes 393224 | tf_op jit(solution)/shard_map/ppermute | solution.py:548
  99.4 5.6 %collective-permute-start.21 = (bf16[512,128]{1,0:T(8,128)(2,1)S(1)}, bf16[512,128]{1,0:T(8,128)(2,1)S(1)}, u32[]{:S(2)}, u32[]{:S(2)}) collective-permute-start(bf16[512,128]{1,0:T(8,128)(2,1)S(1)} %get-tuple-element.73), channel_id=1, source_target_pairs={{0,16},{4,20},{8,24},{12,28},{16,0},{20,4},{24,8},{28,12},{1,17},{... | collective-permute-start | bytes 393224 | tf_op jit(solution)/shard_map/ppermute | solution.py:548
  101.4 6.9 %collective-permute-start.22 = (bf16[512,128]{1,0:T(8,128)(2,1)S(1)}, bf16[512,128]{1,0:T(8,128)(2,1)S(1)}, u32[]{:S(2)}, u32[]{:S(2)}) collective-permute-start(bf16[512,128]{1,0:T(8,128)(2,1)S(1)} %get-tuple-element.74), channel_id=1, source_target_pairs={{0,8},{4,12},{8,0},{12,4},{16,24},{20,28},{24,16},{28,20},{1,9},{5... | collective-permute-start | bytes 393224 | tf_op jit(solution)/shard_map/ppermute | solution.py:548
  101.9 6.4 %collective-permute-start.23 = (bf16[512,128]{1,0:T(8,128)(2,1)S(1)}, bf16[512,128]{1,0:T(8,128)(2,1)S(1)}, u32[]{:S(2)}, u32[]{:S(2)}) collective-permute-start(bf16[512,128]{1,0:T(8,128)(2,1)S(1)} %get-tuple-element.75), channel_id=1, source_target_pairs={{0,20},{4,16},{8,28},{12,24},{16,4},{20,0},{24,12},{28,8},{1,21},{... | collective-permute-start | bytes 393224 | tf_op jit(solution)/shard_map/ppermute | solution.py:548
  103.7 6.8 %collective-permute-start.24 = (bf16[512,128]{1,0:T(8,128)(2,1)S(1)}, bf16[512,128]{1,0:T(8,128)(2,1)S(1)}, u32[]{:S(2)}, u32[]{:S(2)}) collective-permute-start(bf16[512,128]{1,0:T(8,128)(2,1)S(1)} %get-tuple-element.76), channel_id=1, source_target_pairs={{0,12},{4,8},{8,4},{12,0},{16,28},{20,24},{24,20},{28,16},{1,13},{... | collective-permute-start | bytes 393224 | tf_op jit(solution)/shard_map/ppermute | solution.py:548
  103.8 8.3 %collective-permute-start.25 = (bf16[512,128]{1,0:T(8,128)(2,1)S(1)}, bf16[512,128]{1,0:T(8,128)(2,1)S(1)}, u32[]{:S(2)}, u32[]{:S(2)}) collective-permute-start(bf16[512,128]{1,0:T(8,128)(2,1)S(1)} %get-tuple-element.77), channel_id=1, source_target_pairs={{0,24},{4,28},{8,16},{12,20},{16,8},{20,12},{24,0},{28,4},{1,25},{... | collective-permute-start | bytes 393224 | tf_op jit(solution)/shard_map/ppermute | solution.py:548
  105.0 10.2 %collective-permute-start.26 = (bf16[512,128]{1,0:T(8,128)(2,1)S(1)}, bf16[512,128]{1,0:T(8,128)(2,1)S(1)}, u32[]{:S(2)}, u32[]{:S(2)}) collective-permute-start(bf16[512,128]{1,0:T(8,128)(2,1)S(1)} %get-tuple-element.78), channel_id=1, source_target_pairs={{0,28},{4,24},{8,20},{12,16},{16,12},{20,8},{24,4},{28,0},{1,29},{... | collective-permute-start | bytes 393224 | tf_op jit(solution)/shard_map/ppermute | solution.py:548
  123.1 4.8 %collective-permute-start.27 = (bf16[512,128]{1,0:T(8,128)(2,1)S(1)}, bf16[512,128]{1,0:T(8,128)(2,1)S(1)}, u32[]{:S(2)}, u32[]{:S(2)}) collective-permute-start(bf16[512,128]{1,0:T(8,128)(2,1)S(1)} %get-tuple-element.80), channel_id=1, source_target_pairs={{0,4},{4,0},{8,12},{12,8},{16,20},{20,16},{24,28},{28,24},{1,5},{5... | collective-permute-start | bytes 393224 | tf_op jit(solution)/shard_map/ppermute | solution.py:548
  123.3 5.7 %collective-permute-start.28 = (bf16[512,128]{1,0:T(8,128)(2,1)S(1)}, bf16[512,128]{1,0:T(8,128)(2,1)S(1)}, u32[]{:S(2)}, u32[]{:S(2)}) collective-permute-start(bf16[512,128]{1,0:T(8,128)(2,1)S(1)} %get-tuple-element.81), channel_id=1, source_target_pairs={{0,16},{4,20},{8,24},{12,28},{16,0},{20,4},{24,8},{28,12},{1,17},{... | collective-permute-start | bytes 393224 | tf_op jit(solution)/shard_map/ppermute | solution.py:548
  124.3 6.6 %collective-permute-start.29 = (bf16[512,128]{1,0:T(8,128)(2,1)S(1)}, bf16[512,128]{1,0:T(8,128)(2,1)S(1)}, u32[]{:S(2)}, u32[]{:S(2)}) collective-permute-start(bf16[512,128]{1,0:T(8,128)(2,1)S(1)} %get-tuple-element.82), channel_id=1, source_target_pairs={{0,8},{4,12},{8,0},{12,4},{16,24},{20,28},{24,16},{28,20},{1,9},{5... | collective-permute-start | bytes 393224 | tf_op jit(solution)/shard_map/ppermute | solution.py:548
  124.8 6.8 %collective-permute-start.30 = (bf16[512,128]{1,0:T(8,128)(2,1)S(1)}, bf16[512,128]{1,0:T(8,128)(2,1)S(1)}, u32[]{:S(2)}, u32[]{:S(2)}) collective-permute-start(bf16[512,128]{1,0:T(8,128)(2,1)S(1)} %get-tuple-element.83), channel_id=1, source_target_pairs={{0,20},{4,16},{8,28},{12,24},{16,4},{20,0},{24,12},{28,8},{1,21},{... | collective-permute-start | bytes 393224 | tf_op jit(solution)/shard_map/ppermute | solution.py:548
  127.0 6.4 %collective-permute-start.31 = (bf16[512,128]{1,0:T(8,128)(2,1)S(1)}, bf16[512,128]{1,0:T(8,128)(2,1)S(1)}, u32[]{:S(2)}, u32[]{:S(2)}) collective-permute-start(bf16[512,128]{1,0:T(8,128)(2,1)S(1)} %get-tuple-element.84), channel_id=1, source_target_pairs={{0,12},{4,8},{8,4},{12,0},{16,28},{20,24},{24,20},{28,16},{1,13},{... | collective-permute-start | bytes 393224 | tf_op jit(solution)/shard_map/ppermute | solution.py:548
  127.8 9.7 %collective-permute-start.32 = (bf16[512,128]{1,0:T(8,128)(2,1)S(1)}, bf16[512,128]{1,0:T(8,128)(2,1)S(1)}, u32[]{:S(2)}, u32[]{:S(2)}) collective-permute-start(bf16[512,128]{1,0:T(8,128)(2,1)S(1)} %get-tuple-element.85), channel_id=1, source_target_pairs={{0,24},{4,28},{8,16},{12,20},{16,8},{20,12},{24,0},{28,4},{1,25},{... | collective-permute-start | bytes 393224 | tf_op jit(solution)/shard_map/ppermute | solution.py:548
  129.0 9.1 %collective-permute-start.33 = (bf16[512,128]{1,0:T(8,128)(2,1)S(1)}, bf16[512,128]{1,0:T(8,128)(2,1)S(1)}, u32[]{:S(2)}, u32[]{:S(2)}) collective-permute-start(bf16[512,128]{1,0:T(8,128)(2,1)S(1)} %get-tuple-element.86), channel_id=1, source_target_pairs={{0,28},{4,24},{8,20},{12,16},{16,12},{20,8},{24,4},{28,0},{1,29},{... | collective-permute-start | bytes 393224 | tf_op jit(solution)/shard_map/ppermute | solution.py:548

commit v14 on v13

--- a/solution.py
+++ b/solution.py
@@ -203,7 +203,7 @@
 
 def fit_plans(tables, arrived, parts, norms):
     tm_count = len(arrived)
-    order = [0] + send_order(tm_count)
+    order = [0] + send_order(tm_count)[1:] + [1]
     _, obs, twice = parts[0].shape
     sched_dev = norms.shape[0]
     capacity, width = arrived[0].shape

time: 144 us -> 142 us (0.986); the launches traced: 141 us -> 142 us
  transfers between devices with their start and end apart: 35 -> 35, of which waited for: 14 -> 16; matrix products, arithmetic and copies ran while one was open for 7% -> 7% of each run, Pallas kernels for 16% -> 15%
where the time goes in v14:
time: 142 us
  Pallas kernels  50.8 us (36%)
  starting transfers between devices  46 us (32%)
  waiting for transfers between devices  31.8 us (22%)
  other arithmetic  9.49 us (7%)
  local copies, waits for them, and re-layouts  2.14 us (2%)
    ppermute x28, starting transfers between devices, exchange(): lax.ppermute(blocks[step], 'tm', [(i, i ^ step) for i in range(count)])  31 us
    ppermute x28, waiting for transfers between devices, exchange(): lax.ppermute(blocks[step], 'tm', [(i, i ^ step) for i in range(count)])  19.7 us
    pallas_call x2, Pallas kernels, fit_plans(): pl.pallas_call(functools.partial(fit_kernel, order), in_specs=[SMEM, SMEM...  16.5 us
    pallas_call x4, Pallas kernels, make_basis(): pl.pallas_call(functools.partial(basis_kernel, len(after)), grid=(sched_d...  14.3 us
    ppermute x3, waiting for transfers between devices, pass_along(): lax.ppermute(left, 'sky', [(i, i - 1) for i in range(1, count - hop + 1)])  8.04 us
    pallas_call x2, Pallas kernels, place_early(): pl.pallas_call(functools.partial(early_kernel, owners, table_base), in_sp...  7.61 us
    ppermute x3, starting transfers between devices, pass_along(): lax.ppermute(right, 'sky', [(i, i + 1) for i in range(hop - 1, count - 1)])  6.08 us
    pallas_call x1, Pallas kernels, place_late_and_pick(): pl.pallas_call(functools.partial(late_pick_kernel, tm_count, len(attitude...  5.13 us
  transfers between devices with their start and end apart: 35, of which 16 were waited for; matrix products, arithmetic and copies ran while one was open for 7% of the time, Pallas kernels for 15%

profile of v14, /device:TPU:1, one launch (start us, length us, event | category | flops | bytes accessed | tf_op | source)
XLA Modules:
  0.0 141.5 jit_solution(3325430556369961048)
XLA Ops:
  0.6 1.3 collective-permute-start.1
  1.9 4.7 %collective-permute-start = (bf16[4,128,512]{2,1,0:T(8,128)(2,1)}, bf16[4,128,512]{2,1,0:T(8,128)(2,1)S(1)}, u32[]{:S(2)}, u32[]{:S(2)}) collective-permute-start(bf16[4,128,512]{2,1,0:T(8,128)(2,1)} %own_ref.3), channel_id=1, source_target_pairs={{0,1},{1,2},{2,3},{4,5},{5,6},{6,7},{8,9},{9,10},{10,11},{12,13},{... | collective-permute-start | bytes 1572872 | tf_op jit(solution)/shard_map/ppermute | solution.py:557
  11.6 3.4 %select_reduce_fusion = s32[4096]{0:T(1024)S(1)} fusion(s32[2048]{0:T(1024)S(1)} %bitcast.34, s32[2048]{0:T(1024)S(1)} %bitcast.33), kind=kLoop, calls=%fused_computation | loop fusion | flops 25161728 | bytes 32768 | tf_op jit(solution)/shard_map/reduce_sum | solution.py:519
  15.2 1.3 collective-permute-done.1.refs_1_
  16.5 1.3 collective-permute-start.3
  18.6 1.8 %shard_map.77 = (bf16[1,256,2048]{2,1,0:T(8,128)(2,1)S(1)}, f32[1,1,2048]{2,1,0:T(1,128)S(1)}) custom-call(f32[256,128]{1,0:T(8,128)S(1)} %broadcast_in_dim.50.time_ref, f32[1,1024]{1,0:T(1,128)S(1)} %bitcast.27, f32[1,1024]{1,0:T(1,128)S(1)} %bitcast.23, bf16[4,128,512]{2,1,0:T(8,128)(2,1)S(1)} %collective-permute-done.refs_0_, ...), custom_call_target="tpu_custom_call" | custom-call | flops 2097152000 | bytes 1048576 | tf_op jit(solution)/shard_map/pallas_call | solution.py:92
  20.4 1.0 copy-done.3
  22.0 5.1 %all-to-all-start = ((s32[8,1,512]{2,1,0:T(1,128)}), s32[8,1,512]{2,1,0:T(1,128)S(1)}, u32[]{:S(2)}, u32[]{:S(2)}) async-start(s32[8,1,512]{2,1,0:T(1,128)} %all_to_all.6), calls=%async_computation | async-start | bytes 32768 | tf_op jit(solution)/shard_map/all_to_all | solution.py:586
  27.1 4.0 %all-to-all-done = s32[8,1,512]{2,1,0:T(1,128)S(1)} async-done(((s32[8,1,512]{2,1,0:T(1,128)}), s32[8,1,512]{2,1,0:T(1,128)S(1)}, u32[]{:S(2)}, u32[]{:S(2)}) %all-to-all-start) | async-done | bytes 16416 | tf_op jit(solution)/shard_map/all_to_all | solution.py:586
  31.4 1.3 collective-permute-start.5
  33.5 5.3 %shard_map.80 = (bf16[3,256,2048]{2,1,0:T(8,128)(2,1)S(1)}, f32[3,1,2048]{2,1,0:T(1,128)S(1)}) custom-call(f32[768,128]{1,0:T(8,128)S(1)} %broadcast_in_dim.55.time_ref, f32[1,1024]{1,0:T(1,128)S(1)} %bitcast.28, f32[1,1024]{1,0:T(1,128)S(1)} %bitcast.24, bf16[4,128,512]{2,1,0:T(8,128)(2,1)S(1)} %collective-permute-done.2.refs_2_.refs_0_, ...), custom_call_target="tpu_custom_call" | custom-call | flops 6291456000 | bytes 3145728 | tf_op jit(solution)/shard_map/pallas_call | solution.py:92
  39.0 3.6 %shard_map.79 = (bf16[2,256,2048]{2,1,0:T(8,128)(2,1)S(1)}, f32[2,1,2048]{2,1,0:T(1,128)S(1)}) custom-call(f32[512,128]{1,0:T(8,128)S(1)} %broadcast_in_dim.53.time_ref, f32[1,1024]{1,0:T(1,128)S(1)} %bitcast.29, f32[1,1024]{1,0:T(1,128)S(1)} %bitcast.25, bf16[4,128,512]{2,1,0:T(8,128)(2,1)S(1)} %collective-permute-done.2.refs_2_.refs_0_, ...), custom_call_target="tpu_custom_call" | custom-call | flops 4194304000 | bytes 2097152 | tf_op jit(solution)/shard_map/pallas_call | solution.py:92
  42.7 6.8 %collective-permute-done.5.refs_5_ = bf16[4,128,512]{2,1,0:T(8,128)(2,1)S(1)} collective-permute-done((bf16[4,128,512]{2,1,0:T(8,128)(2,1)S(1)}, bf16[4,128,512]{2,1,0:T(8,128)(2,1)S(1)}, u32[]{:S(2)}, u32[]{:S(2)}) %collective-permute-start.5) | collective-permute-done | bytes 524320 | tf_op jit(solution)/shard_map/ppermute | solution.py:558
  49.4 3.8 %shard_map.78 = (bf16[512,128]{1,0:T(8,128)(2,1)S(1)}, bf16[512,128]{1,0:T(8,128)(2,1)S(1)}, bf16[512,128]{1,0:T(8,128)(2,1)S(1)}, bf16[512,128]{1,0:T(8,128)(2,...) custom-call(s32[4096]{0:T(1024)S(1)} %bitcast.18, ...), custom_call_target="tpu_custom_call" | custom-call | flops 5000000000 | bytes 1048576 | tf_op jit(solution)/shard_map/pallas_call | solution.py:380
  53.8 1.9 %collective-permute-start.7 = (bf16[512,128]{1,0:T(8,128)(2,1)S(1)}, bf16[512,128]{1,0:T(8,128)(2,1)S(1)}, u32[]{:S(2)}, u32[]{:S(2)}) collective-permute-start(bf16[512,128]{1,0:T(8,128)(2,1)S(1)} %get-tuple-element.49), channel_id=1, source_target_pairs={{0,8},{4,12},{8,0},{12,4},{16,24},{20,28},{24,16},{28,20},{1,9},{5... | collective-permute-start | bytes 393224 | tf_op jit(solution)/shard_map/ppermute | solution.py:548
  55.7 1.7 %collective-permute-start.8 = (bf16[512,128]{1,0:T(8,128)(2,1)S(1)}, bf16[512,128]{1,0:T(8,128)(2,1)S(1)}, u32[]{:S(2)}, u32[]{:S(2)}) collective-permute-start(bf16[512,128]{1,0:T(8,128)(2,1)S(1)} %get-tuple-element.50), channel_id=1, source_target_pairs={{0,20},{4,16},{8,28},{12,24},{16,4},{20,0},{24,12},{28,8},{1,21},{... | collective-permute-start | bytes 393224 | tf_op jit(solution)/shard_map/ppermute | solution.py:548
  57.5 1.2 collective-permute-start.10
  58.8 3.6 %shard_map.81 = (bf16[2,256,2048]{2,1,0:T(8,128)(2,1)S(1)}, f32[2,1,2048]{2,1,0:T(1,128)S(1)}) custom-call(f32[512,128]{1,0:T(8,128)S(1)} %broadcast_in_dim.57.time_ref, f32[1,1024]{1,0:T(1,128)S(1)} %bitcast.30, f32[1,1024]{1,0:T(1,128)S(1)} %bitcast.26, bf16[512,128]{1,0:T(8,128)(2,1)S(1)} %get-tuple-element.47.refs_0_), custom_call_target="tpu_custom_call" | custom-call | flops 4194304000 | bytes 2097152 | tf_op jit(solution)/shard_map/pallas_call | solution.py:92
  62.4 2.3 %collective-permute-start.11 = (bf16[512,128]{1,0:T(8,128)(2,1)S(1)}, bf16[512,128]{1,0:T(8,128)(2,1)S(1)}, u32[]{:S(2)}, u32[]{:S(2)}) collective-permute-start(bf16[512,128]{1,0:T(8,128)(2,1)S(1)} %get-tuple-element.53), channel_id=1, source_target_pairs={{0,28},{4,24},{8,20},{12,16},{16,12},{20,8},{24,4},{28,0},{1,29},{... | collective-permute-start | bytes 393224 | tf_op jit(solution)/shard_map/ppermute | solution.py:548
  65.4 3.9 %collective-permute-done.11.refs_6_ = bf16[512,128]{1,0:T(8,128)(2,1)S(1)} collective-permute-done((bf16[512,128]{1,0:T(8,128)(2,1)S(1)}, bf16[512,128]{1,0:T(8,128)(2,1)S(1)}, u32[]{:S(2)}, u32[]{:S(2)}) %collective-permute-start.11) | collective-permute-done | bytes 131104 | tf_op jit(solution)/shard_map/ppermute | solution.py:548
  69.4 8.6 %shard_map.82 = (bf16[512,128]{1,0:T(8,128)(2,1)S(1)}, bf16[512,128]{1,0:T(8,128)(2,1)S(1)}, bf16[512,128]{1,0:T(8,128)(2,1)S(1)}, bf16[512,128]{1,0:T(8,128)(2,...) custom-call(s32[8,24]{1,0:T(8,128)S(1)} %get-tuple-element.104.src_r, ...), custom_call_target="tpu_custom_call" | custom-call | flops 10737418240 | bytes 8388608 | tf_op jit(solution)/shard_map/pallas_call | solution.py:218
  78.5 0.8 collective-permute-start.14
  80.0 1.3 collective-permute-start.16
  81.7 1.2 collective-permute-start.18
  83.6 2.4 %collective-permute-start.19 = (bf16[512,128]{1,0:T(8,128)(2,1)S(1)}, bf16[512,128]{1,0:T(8,128)(2,1)S(1)}, u32[]{:S(2)}, u32[]{:S(2)}) collective-permute-start(bf16[512,128]{1,0:T(8,128)(2,1)S(1)} %get-tuple-element.69), channel_id=1, source_target_pairs={{0,28},{4,24},{8,20},{12,16},{16,12},{20,8},{24,4},{28,0},{1,29},{... | collective-permute-start | bytes 393224 | tf_op jit(solution)/shard_map/ppermute | solution.py:548
  86.0 0.9 collective-permute-done.16.refs_4_
  86.8 1.3 collective-permute-done.17.refs_5_
  88.1 3.9 %shard_map.83.part_ref = f32[4096,128]{1,0:T(8,128)S(1)} custom-call(s32[4096]{0:T(1024)S(1)} %bitcast.19, s32[8]{0:T(128)S(1)} %fusion.4.cnt_ref, s32[2]{0:T(128)S(1)} %pad_add_fusion.where_ref, bf16[4,512,256]{2,1,0:T(8,128)(2,1)S(1)} %copy-done, bf16[512,128]{1,0:T(8,128)(2,1)S(1)} %get-tuple-element.62.refs_0_, ...), custom_call_target="tpu_custom_call" | custom-call | flops 6000000000 | bytes 1048576 | tf_op jit(solution)/shard_map/pallas_call | solution.py:352
  92.0 1.3 collective-permute-done.19.refs_7_
  93.3 5.1 %shard_map.84 = (f32[131072,128]{1,0:T(8,128)}, bf16[512,128]{1,0:T(8,128)(2,1)S(1)}, bf16[512,128]{1,0:T(8,128)(2,1)S(1)}, bf16[512,128]{1,0:T(8,128)(2,1)S(1)}...) custom-call(s32[4096]{0:T(1024)S(1)} %bitcast.20, ...), custom_call_target="tpu_custom_call" | custom-call | flops 7000000000 | bytes 1048576 | tf_op jit(solution)/shard_map/pallas_call | solution.py:437
  98.5 0.8 collective-permute-start.20
  99.3 2.8 %collective-permute-start.21 = (bf16[512,128]{1,0:T(8,128)(2,1)S(1)}, bf16[512,128]{1,0:T(8,128)(2,1)S(1)}, u32[]{:S(2)}, u32[]{:S(2)}) collective-permute-start(bf16[512,128]{1,0:T(8,128)(2,1)S(1)} %get-tuple-element.73), channel_id=1, source_target_pairs={{0,8},{4,12},{8,0},{12,4},{16,24},{20,28},{24,16},{28,20},{1,9},{5... | collective-permute-start | bytes 393224 | tf_op jit(solution)/shard_map/ppermute | solution.py:548
  102.8 2.2 %collective-permute-start.24 = (bf16[512,128]{1,0:T(8,128)(2,1)S(1)}, bf16[512,128]{1,0:T(8,128)(2,1)S(1)}, u32[]{:S(2)}, u32[]{:S(2)}) collective-permute-start(bf16[512,128]{1,0:T(8,128)(2,1)S(1)} %get-tuple-element.76), channel_id=1, source_target_pairs={{0,24},{4,28},{8,16},{12,20},{16,8},{20,12},{24,0},{28,4},{1,25},{... | collective-permute-start | bytes 393224 | tf_op jit(solution)/shard_map/ppermute | solution.py:548
  105.5 1.3 collective-permute-start.26
  106.9 1.3 collective-permute-done.23.refs_4_
  108.1 3.5 %collective-permute-done.24.refs_5_ = bf16[512,128]{1,0:T(8,128)(2,1)S(1)} collective-permute-done((bf16[512,128]{1,0:T(8,128)(2,1)S(1)}, bf16[512,128]{1,0:T(8,128)(2,1)S(1)}, u32[]{:S(2)}, u32[]{:S(2)}) %collective-permute-start.24) | collective-permute-done | bytes 131104 | tf_op jit(solution)/shard_map/ppermute | solution.py:548
  111.6 2.3 %collective-permute-done.25.refs_6_ = bf16[512,128]{1,0:T(8,128)(2,1)S(1)} collective-permute-done((bf16[512,128]{1,0:T(8,128)(2,1)S(1)}, bf16[512,128]{1,0:T(8,128)(2,1)S(1)}, u32[]{:S(2)}, u32[]{:S(2)}) %collective-permute-start.25) | collective-permute-done | bytes 131104 | tf_op jit(solution)/shard_map/ppermute | solution.py:548
  113.9 7.9 %shard_map.85 = (bf16[512,128]{1,0:T(8,128)(2,1)S(1)}, bf16[512,128]{1,0:T(8,128)(2,1)S(1)}, bf16[512,128]{1,0:T(8,128)(2,1)S(1)}, bf16[512,128]{1,0:T(8,128)(2,...) custom-call(s32[8,24]{1,0:T(8,128)S(1)} %get-tuple-element.104.src_r, ...), custom_call_target="tpu_custom_call" | custom-call | flops 10737418240 | bytes 8388608 | tf_op jit(solution)/shard_map/pallas_call | solution.py:218
  121.9 0.8 collective-permute-start.27
  123.5 1.0 collective-permute-start.29
  124.5 2.0 %collective-permute-start.30 = (bf16[512,128]{1,0:T(8,128)(2,1)S(1)}, bf16[512,128]{1,0:T(8,128)(2,1)S(1)}, u32[]{:S(2)}, u32[]{:S(2)}) collective-permute-start(bf16[512,128]{1,0:T(8,128)(2,1)S(1)} %get-tuple-element.83), channel_id=1, source_target_pairs={{0,20},{4,16},{8,28},{12,24},{16,4},{20,0},{24,12},{28,8},{1,21},{... | collective-permute-start | bytes 393224 | tf_op jit(solution)/shard_map/ppermute | solution.py:548
  126.5 0.8 reduce.1
  127.3 1.2 collective-permute-start.32
  128.5 1.9 %collective-permute-start.33 = (bf16[512,128]{1,0:T(8,128)(2,1)S(1)}, bf16[512,128]{1,0:T(8,128)(2,1)S(1)}, u32[]{:S(2)}, u32[]{:S(2)}) collective-permute-start(bf16[512,128]{1,0:T(8,128)(2,1)S(1)} %get-tuple-element.86), channel_id=1, source_target_pairs={{0,28},{4,24},{8,20},{12,16},{16,12},{20,8},{24,4},{28,0},{1,29},{... | collective-permute-start | bytes 393224 | tf_op jit(solution)/shard_map/ppermute | solution.py:548
  131.1 1.2 collective-permute-done.31.refs_5_
  132.2 3.8 %shard_map.86.part_ref = f32[4096,128]{1,0:T(8,128)S(1)} custom-call(s32[4096]{0:T(1024)S(1)} %bitcast.21, s32[8]{0:T(128)S(1)} %fusion.4.cnt_ref, s32[2]{0:T(128)S(1)} %pad_add_fusion.where_ref, f32[131072,128]{1,0:T(8,128)} %get-tuple-element.70.base_ref, bf16[512,128]{1,0:T(8,128)(2,1)S(1)} %get-tuple-element.79.refs_0_, ...), custom_call_target="tpu_custom_call" | custom-call | flops 6000000000 | bytes 1048576 | tf_op jit(solution)/shard_map/pallas_call | solution.py:352
  136.0 1.9 %collective-permute-done.33.refs_1_ = bf16[512,128]{1,0:T(8,128)(2,1)S(1)} collective-permute-done((bf16[512,128]{1,0:T(8,128)(2,1)S(1)}, bf16[512,128]{1,0:T(8,128)(2,1)S(1)}, u32[]{:S(2)}, u32[]{:S(2)}) %collective-permute-start.33) | collective-permute-done | bytes 131104 | tf_op jit(solution)/shard_map/ppermute | solution.py:548
  137.9 3.5 %shard_map.87 = f32[4,512,256]{2,1,0:T(8,128)} custom-call(s32[4096]{0:T(1024)S(1)} %bitcast.22, s32[8]{0:T(128)S(1)} %fusion.4.cnt_ref, s32[2]{0:T(128)S(1)} %pad_add_fusion.where_ref, f32[4096,128]{1,0:T(8,128)S(1)} %shard_map.86.part_ref, bf16[512,128]{1,0:T(8,128)(2,1)S(1)} %collective-permute-done.32.refs_0_, ...), custom_call_target="tpu_custom_call" | custom-call | flops 4000000000 | bytes 1048576 | tf_op jit(solution)/shard_map/pallas_call | solution.py:479
  (83 shorter events, 14.1 us)
Async XLA Ops:
  0.6 15.9 %collective-permute-start.1 = (bf16[4,128,512]{2,1,0:T(8,128)(2,1)}, bf16[4,128,512]{2,1,0:T(8,128)(2,1)S(1)}, u32[]{:S(2)}, u32[]{:S(2)}) collective-permute-start(bf16[4,128,512]{2,1,0:T(8,128)(2,1)} %own_ref.3), channel_id=1, source_target_pairs={{1,0},{2,1},{3,2},{5,4},{6,5},{7,6},{9,8},{10,9},{11,10},{13,12},{... | collective-permute-start | bytes 1572872 | tf_op jit(solution)/shard_map/ppermute | solution.py:558
  1.9 15.9 %collective-permute-start = (bf16[4,128,512]{2,1,0:T(8,128)(2,1)}, bf16[4,128,512]{2,1,0:T(8,128)(2,1)S(1)}, u32[]{:S(2)}, u32[]{:S(2)}) collective-permute-start(bf16[4,128,512]{2,1,0:T(8,128)(2,1)} %own_ref.3), channel_id=1, source_target_pairs={{0,1},{1,2},{2,3},{4,5},{5,6},{6,7},{8,9},{9,10},{10,11},{12,13},{... | collective-permute-start | bytes 1572872 | tf_op jit(solution)/shard_map/ppermute | solution.py:557
  16.5 14.8 %collective-permute-start.3 = (bf16[4,128,512]{2,1,0:T(8,128)(2,1)S(1)}, bf16[4,128,512]{2,1,0:T(8,128)(2,1)S(1)}, u32[]{:S(2)}, u32[]{:S(2)}) collective-permute-start(bf16[4,128,512]{2,1,0:T(8,128)(2,1)S(1)} %collective-permute-done.1.refs_1_), channel_id=1, source_target_pairs={{1,0},{2,1},{5,4},{6,5},{9,8},{10,9},{13,12},{14,13},{17,16},{18,1... | collective-permute-start | bytes 1572872 | tf_op jit(solution)/shard_map/ppermute | solution.py:558
  17.8 14.8 %collective-permute-start.2 = (bf16[4,128,512]{2,1,0:T(8,128)(2,1)S(1)}, bf16[4,128,512]{2,1,0:T(8,128)(2,1)S(1)}, u32[]{:S(2)}, u32[]{:S(2)}) collective-permute-start(bf16[4,128,512]{2,1,0:T(8,128)(2,1)S(1)} %collective-permute-done.refs_0_), channel_id=1, source_target_pairs={{1,2},{2,3},{5,6},{6,7},{9,10},{10,11},{13,14},{14,15},{17,18},{18... | collective-permute-start | bytes 1572872 | tf_op jit(solution)/shard_map/ppermute | solution.py:557
  20.4 1.0 copy-start.3
  22.0 9.1 %all-to-all-start = ((s32[8,1,512]{2,1,0:T(1,128)}), s32[8,1,512]{2,1,0:T(1,128)S(1)}, u32[]{:S(2)}, u32[]{:S(2)}) async-start(s32[8,1,512]{2,1,0:T(1,128)} %all_to_all.6), calls=%async_computation | async-start | bytes 32768 | tf_op jit(solution)/shard_map/all_to_all | solution.py:586
  31.4 18.1 %collective-permute-start.5 = (bf16[4,128,512]{2,1,0:T(8,128)(2,1)S(1)}, bf16[4,128,512]{2,1,0:T(8,128)(2,1)S(1)}, u32[]{:S(2)}, u32[]{:S(2)}) collective-permute-start(bf16[4,128,512]{2,1,0:T(8,128)(2,1)S(1)} %collective-permute-done.3.refs_3_.refs_1_), channel_id=1, source_target_pairs={{1,0},{5,4},{9,8},{13,12},{17,16},{21,20},{25,24},{29,28}} | collective-permute-start | bytes 1572872 | tf_op jit(solution)/shard_map/ppermute | solution.py:558
  32.7 16.8 %collective-permute-start.4 = (bf16[4,128,512]{2,1,0:T(8,128)(2,1)S(1)}, bf16[4,128,512]{2,1,0:T(8,128)(2,1)S(1)}, u32[]{:S(2)}, u32[]{:S(2)}) collective-permute-start(bf16[4,128,512]{2,1,0:T(8,128)(2,1)S(1)} %collective-permute-done.2.refs_2_.refs_0_), channel_id=1, source_target_pairs={{2,3},{6,7},{10,11},{14,15},{18,19},{22,23},{26,27},{30,31}} | collective-permute-start | bytes 1572872 | tf_op jit(solution)/shard_map/ppermute | solution.py:557
  39.0 10.4 %copy-start = (bf16[4,512,256]{2,1,0:T(8,128)(2,1)S(1)}, bf16[4,512,256]{2,1,0:T(8,128)(2,1)}, u32[]{:S(2)}) copy-start(bf16[4,512,256]{2,1,0:T(8,128)(2,1)} %base_ref.3) | copy-start | bytes 3145732
  39.0 10.4 %copy-start.1 = (bf16[4,128,512]{2,1,0:T(8,128)(2,1)S(1)}, bf16[4,128,512]{2,1,0:T(8,128)(2,1)}, u32[]{:S(2)}) copy-start(bf16[4,128,512]{2,1,0:T(8,128)(2,1)} %own_ref.3) | copy-start | bytes 1572868
  39.0 10.4 %copy-start.2 = (s32[4]{0:T(128)S(1)}, s32[4]{0:T(128)}, u32[]{:S(2)}) copy-start(s32[4]{0:T(128)} %count_ref.3) | copy-start | bytes 52
  53.2 9.1 %collective-permute-start.6 = (bf16[512,128]{1,0:T(8,128)(2,1)S(1)}, bf16[512,128]{1,0:T(8,128)(2,1)S(1)}, u32[]{:S(2)}, u32[]{:S(2)}) collective-permute-start(bf16[512,128]{1,0:T(8,128)(2,1)S(1)} %get-tuple-element.48), channel_id=1, source_target_pairs={{0,16},{4,20},{8,24},{12,28},{16,0},{20,4},{24,8},{28,12},{1,17},{... | collective-permute-start | bytes 393224 | tf_op jit(solution)/shard_map/ppermute | solution.py:548
  53.8 10.9 %collective-permute-start.7 = (bf16[512,128]{1,0:T(8,128)(2,1)S(1)}, bf16[512,128]{1,0:T(8,128)(2,1)S(1)}, u32[]{:S(2)}, u32[]{:S(2)}) collective-permute-start(bf16[512,128]{1,0:T(8,128)(2,1)S(1)} %get-tuple-element.49), channel_id=1, source_target_pairs={{0,8},{4,12},{8,0},{12,4},{16,24},{20,28},{24,16},{28,20},{1,9},{5... | collective-permute-start | bytes 393224 | tf_op jit(solution)/shard_map/ppermute | solution.py:548
  55.7 9.0 %collective-permute-start.8 = (bf16[512,128]{1,0:T(8,128)(2,1)S(1)}, bf16[512,128]{1,0:T(8,128)(2,1)S(1)}, u32[]{:S(2)}, u32[]{:S(2)}) collective-permute-start(bf16[512,128]{1,0:T(8,128)(2,1)S(1)} %get-tuple-element.50), channel_id=1, source_target_pairs={{0,20},{4,16},{8,28},{12,24},{16,4},{20,0},{24,12},{28,8},{1,21},{... | collective-permute-start | bytes 393224 | tf_op jit(solution)/shard_map/ppermute | solution.py:548
  57.5 7.3 %collective-permute-start.9 = (bf16[512,128]{1,0:T(8,128)(2,1)S(1)}, bf16[512,128]{1,0:T(8,128)(2,1)S(1)}, u32[]{:S(2)}, u32[]{:S(2)}) collective-permute-start(bf16[512,128]{1,0:T(8,128)(2,1)S(1)} %get-tuple-element.51), channel_id=1, source_target_pairs={{0,12},{4,8},{8,4},{12,0},{16,28},{20,24},{24,20},{28,16},{1,13},{... | collective-permute-start | bytes 393224 | tf_op jit(solution)/shard_map/ppermute | solution.py:548
  57.5 8.0 %collective-permute-start.10 = (bf16[512,128]{1,0:T(8,128)(2,1)S(1)}, bf16[512,128]{1,0:T(8,128)(2,1)S(1)}, u32[]{:S(2)}, u32[]{:S(2)}) collective-permute-start(bf16[512,128]{1,0:T(8,128)(2,1)S(1)} %get-tuple-element.52), channel_id=1, source_target_pairs={{0,24},{4,28},{8,16},{12,20},{16,8},{20,12},{24,0},{28,4},{1,25},{... | collective-permute-start | bytes 393224 | tf_op jit(solution)/shard_map/ppermute | solution.py:548
  58.8 10.6 %copy-start.4 = (bf16[1,256,2048]{2,1,0:T(8,128)(2,1)S(1)}, bf16[1,256,2048]{2,1,0:T(8,128)(2,1)}, u32[]{:S(2)}) copy-start(bf16[1,256,2048]{2,1,0:T(8,128)(2,1)} %copy-done.3) | copy-start | bytes 3145732
  62.4 7.0 %collective-permute-start.11 = (bf16[512,128]{1,0:T(8,128)(2,1)S(1)}, bf16[512,128]{1,0:T(8,128)(2,1)S(1)}, u32[]{:S(2)}, u32[]{:S(2)}) collective-permute-start(bf16[512,128]{1,0:T(8,128)(2,1)S(1)} %get-tuple-element.53), channel_id=1, source_target_pairs={{0,28},{4,24},{8,20},{12,16},{16,12},{20,8},{24,4},{28,0},{1,29},{... | collective-permute-start | bytes 393224 | tf_op jit(solution)/shard_map/ppermute | solution.py:548
  64.7 4.7 %collective-permute-start.12 = (bf16[512,128]{1,0:T(8,128)(2,1)S(1)}, bf16[512,128]{1,0:T(8,128)(2,1)S(1)}, u32[]{:S(2)}, u32[]{:S(2)}) collective-permute-start(bf16[512,128]{1,0:T(8,128)(2,1)S(1)} %get-tuple-element.54), channel_id=1, source_target_pairs={{0,4},{4,0},{8,12},{12,8},{16,20},{20,16},{24,28},{28,24},{1,5},{5... | collective-permute-start | bytes 393224 | tf_op jit(solution)/shard_map/ppermute | solution.py:548
  78.0 3.7 %collective-permute-start.13 = (bf16[512,128]{1,0:T(8,128)(2,1)S(1)}, bf16[512,128]{1,0:T(8,128)(2,1)S(1)}, u32[]{:S(2)}, u32[]{:S(2)}) collective-permute-start(bf16[512,128]{1,0:T(8,128)(2,1)S(1)} %get-tuple-element.63), channel_id=1, source_target_pairs={{0,4},{4,0},{8,12},{12,8},{16,20},{20,16},{24,28},{28,24},{1,5},{5... | collective-permute-start | bytes 393224 | tf_op jit(solution)/shard_map/ppermute | solution.py:548
  78.5 5.1 %collective-permute-start.14 = (bf16[512,128]{1,0:T(8,128)(2,1)S(1)}, bf16[512,128]{1,0:T(8,128)(2,1)S(1)}, u32[]{:S(2)}, u32[]{:S(2)}) collective-permute-start(bf16[512,128]{1,0:T(8,128)(2,1)S(1)} %get-tuple-element.64), channel_id=1, source_target_pairs={{0,16},{4,20},{8,24},{12,28},{16,0},{20,4},{24,8},{28,12},{1,17},{... | collective-permute-start | bytes 393224 | tf_op jit(solution)/shard_map/ppermute | solution.py:548
  79.3 6.6 %collective-permute-start.15 = (bf16[512,128]{1,0:T(8,128)(2,1)S(1)}, bf16[512,128]{1,0:T(8,128)(2,1)S(1)}, u32[]{:S(2)}, u32[]{:S(2)}) collective-permute-start(bf16[512,128]{1,0:T(8,128)(2,1)S(1)} %get-tuple-element.65), channel_id=1, source_target_pairs={{0,8},{4,12},{8,0},{12,4},{16,24},{20,28},{24,16},{28,20},{1,9},{5... | collective-permute-start | bytes 393224 | tf_op jit(solution)/shard_map/ppermute | solution.py:548
  80.0 6.9 %collective-permute-start.16 = (bf16[512,128]{1,0:T(8,128)(2,1)S(1)}, bf16[512,128]{1,0:T(8,128)(2,1)S(1)}, u32[]{:S(2)}, u32[]{:S(2)}) collective-permute-start(bf16[512,128]{1,0:T(8,128)(2,1)S(1)} %get-tuple-element.66), channel_id=1, source_target_pairs={{0,20},{4,16},{8,28},{12,24},{16,4},{20,0},{24,12},{28,8},{1,21},{... | collective-permute-start | bytes 393224 | tf_op jit(solution)/shard_map/ppermute | solution.py:548
  81.3 6.9 %collective-permute-start.17 = (bf16[512,128]{1,0:T(8,128)(2,1)S(1)}, bf16[512,128]{1,0:T(8,128)(2,1)S(1)}, u32[]{:S(2)}, u32[]{:S(2)}) collective-permute-start(bf16[512,128]{1,0:T(8,128)(2,1)S(1)} %get-tuple-element.67), channel_id=1, source_target_pairs={{0,12},{4,8},{8,4},{12,0},{16,28},{20,24},{24,20},{28,16},{1,13},{... | collective-permute-start | bytes 393224 | tf_op jit(solution)/shard_map/ppermute | solution.py:548
  81.7 10.3 %collective-permute-start.18 = (bf16[512,128]{1,0:T(8,128)(2,1)S(1)}, bf16[512,128]{1,0:T(8,128)(2,1)S(1)}, u32[]{:S(2)}, u32[]{:S(2)}) collective-permute-start(bf16[512,128]{1,0:T(8,128)(2,1)S(1)} %get-tuple-element.68), channel_id=1, source_target_pairs={{0,24},{4,28},{8,16},{12,20},{16,8},{20,12},{24,0},{28,4},{1,25},{... | collective-permute-start | bytes 393224 | tf_op jit(solution)/shard_map/ppermute | solution.py:548
  83.6 9.8 %collective-permute-start.19 = (bf16[512,128]{1,0:T(8,128)(2,1)S(1)}, bf16[512,128]{1,0:T(8,128)(2,1)S(1)}, u32[]{:S(2)}, u32[]{:S(2)}) collective-permute-start(bf16[512,128]{1,0:T(8,128)(2,1)S(1)} %get-tuple-element.69), channel_id=1, source_target_pairs={{0,28},{4,24},{8,20},{12,16},{16,12},{20,8},{24,4},{28,0},{1,29},{... | collective-permute-start | bytes 393224 | tf_op jit(solution)/shard_map/ppermute | solution.py:548
  98.5 6.6 %collective-permute-start.20 = (bf16[512,128]{1,0:T(8,128)(2,1)S(1)}, bf16[512,128]{1,0:T(8,128)(2,1)S(1)}, u32[]{:S(2)}, u32[]{:S(2)}) collective-permute-start(bf16[512,128]{1,0:T(8,128)(2,1)S(1)} %get-tuple-element.72), channel_id=1, source_target_pairs={{0,16},{4,20},{8,24},{12,28},{16,0},{20,4},{24,8},{28,12},{1,17},{... | collective-permute-start | bytes 393224 | tf_op jit(solution)/shard_map/ppermute | solution.py:548
  99.3 6.2 %collective-permute-start.21 = (bf16[512,128]{1,0:T(8,128)(2,1)S(1)}, bf16[512,128]{1,0:T(8,128)(2,1)S(1)}, u32[]{:S(2)}, u32[]{:S(2)}) collective-permute-start(bf16[512,128]{1,0:T(8,128)(2,1)S(1)} %get-tuple-element.73), channel_id=1, source_target_pairs={{0,8},{4,12},{8,0},{12,4},{16,24},{20,28},{24,16},{28,20},{1,9},{5... | collective-permute-start | bytes 393224 | tf_op jit(solution)/shard_map/ppermute | solution.py:548
  102.2 4.7 %collective-permute-start.22 = (bf16[512,128]{1,0:T(8,128)(2,1)S(1)}, bf16[512,128]{1,0:T(8,128)(2,1)S(1)}, u32[]{:S(2)}, u32[]{:S(2)}) collective-permute-start(bf16[512,128]{1,0:T(8,128)(2,1)S(1)} %get-tuple-element.74), channel_id=1, source_target_pairs={{0,20},{4,16},{8,28},{12,24},{16,4},{20,0},{24,12},{28,8},{1,21},{... | collective-permute-start | bytes 393224 | tf_op jit(solution)/shard_map/ppermute | solution.py:548
  102.2 6.0 %collective-permute-start.23 = (bf16[512,128]{1,0:T(8,128)(2,1)S(1)}, bf16[512,128]{1,0:T(8,128)(2,1)S(1)}, u32[]{:S(2)}, u32[]{:S(2)}) collective-permute-start(bf16[512,128]{1,0:T(8,128)(2,1)S(1)} %get-tuple-element.75), channel_id=1, source_target_pairs={{0,12},{4,8},{8,4},{12,0},{16,28},{20,24},{24,20},{28,16},{1,13},{... | collective-permute-start | bytes 393224 | tf_op jit(solution)/shard_map/ppermute | solution.py:548
  102.8 8.8 %collective-permute-start.24 = (bf16[512,128]{1,0:T(8,128)(2,1)S(1)}, bf16[512,128]{1,0:T(8,128)(2,1)S(1)}, u32[]{:S(2)}, u32[]{:S(2)}) collective-permute-start(bf16[512,128]{1,0:T(8,128)(2,1)S(1)} %get-tuple-element.76), channel_id=1, source_target_pairs={{0,24},{4,28},{8,16},{12,20},{16,8},{20,12},{24,0},{28,4},{1,25},{... | collective-permute-start | bytes 393224 | tf_op jit(solution)/shard_map/ppermute | solution.py:548
  105.1 8.9 %collective-permute-start.25 = (bf16[512,128]{1,0:T(8,128)(2,1)S(1)}, bf16[512,128]{1,0:T(8,128)(2,1)S(1)}, u32[]{:S(2)}, u32[]{:S(2)}) collective-permute-start(bf16[512,128]{1,0:T(8,128)(2,1)S(1)} %get-tuple-element.77), channel_id=1, source_target_pairs={{0,28},{4,24},{8,20},{12,16},{16,12},{20,8},{24,4},{28,0},{1,29},{... | collective-permute-start | bytes 393224 | tf_op jit(solution)/shard_map/ppermute | solution.py:548
  105.5 8.4 %collective-permute-start.26 = (bf16[512,128]{1,0:T(8,128)(2,1)S(1)}, bf16[512,128]{1,0:T(8,128)(2,1)S(1)}, u32[]{:S(2)}, u32[]{:S(2)}) collective-permute-start(bf16[512,128]{1,0:T(8,128)(2,1)S(1)} %get-tuple-element.78), channel_id=1, source_target_pairs={{0,4},{4,0},{8,12},{12,8},{16,20},{20,16},{24,28},{28,24},{1,5},{5... | collective-permute-start | bytes 393224 | tf_op jit(solution)/shard_map/ppermute | solution.py:548
  121.9 5.4 %collective-permute-start.27 = (bf16[512,128]{1,0:T(8,128)(2,1)S(1)}, bf16[512,128]{1,0:T(8,128)(2,1)S(1)}, u32[]{:S(2)}, u32[]{:S(2)}) collective-permute-start(bf16[512,128]{1,0:T(8,128)(2,1)S(1)} %get-tuple-element.80), channel_id=1, source_target_pairs={{0,4},{4,0},{8,12},{12,8},{16,20},{20,16},{24,28},{28,24},{1,5},{5... | collective-permute-start | bytes 393224 | tf_op jit(solution)/shard_map/ppermute | solution.py:548
  122.7 5.7 %collective-permute-start.28 = (bf16[512,128]{1,0:T(8,128)(2,1)S(1)}, bf16[512,128]{1,0:T(8,128)(2,1)S(1)}, u32[]{:S(2)}, u32[]{:S(2)}) collective-permute-start(bf16[512,128]{1,0:T(8,128)(2,1)S(1)} %get-tuple-element.81), channel_id=1, source_target_pairs={{0,16},{4,20},{8,24},{12,28},{16,0},{20,4},{24,8},{28,12},{1,17},{... | collective-permute-start | bytes 393224 | tf_op jit(solution)/shard_map/ppermute | solution.py:548
  123.5 6.9 %collective-permute-start.29 = (bf16[512,128]{1,0:T(8,128)(2,1)S(1)}, bf16[512,128]{1,0:T(8,128)(2,1)S(1)}, u32[]{:S(2)}, u32[]{:S(2)}) collective-permute-start(bf16[512,128]{1,0:T(8,128)(2,1)S(1)} %get-tuple-element.82), channel_id=1, source_target_pairs={{0,8},{4,12},{8,0},{12,4},{16,24},{20,28},{24,16},{28,20},{1,9},{5... | collective-permute-start | bytes 393224 | tf_op jit(solution)/shard_map/ppermute | solution.py:548
  124.5 6.6 %collective-permute-start.30 = (bf16[512,128]{1,0:T(8,128)(2,1)S(1)}, bf16[512,128]{1,0:T(8,128)(2,1)S(1)}, u32[]{:S(2)}, u32[]{:S(2)}) collective-permute-start(bf16[512,128]{1,0:T(8,128)(2,1)S(1)} %get-tuple-element.83), channel_id=1, source_target_pairs={{0,20},{4,16},{8,28},{12,24},{16,4},{20,0},{24,12},{28,8},{1,21},{... | collective-permute-start | bytes 393224 | tf_op jit(solution)/shard_map/ppermute | solution.py:548
  126.5 5.8 %collective-permute-start.31 = (bf16[512,128]{1,0:T(8,128)(2,1)S(1)}, bf16[512,128]{1,0:T(8,128)(2,1)S(1)}, u32[]{:S(2)}, u32[]{:S(2)}) collective-permute-start(bf16[512,128]{1,0:T(8,128)(2,1)S(1)} %get-tuple-element.84), channel_id=1, source_target_pairs={{0,12},{4,8},{8,4},{12,0},{16,28},{20,24},{24,20},{28,16},{1,13},{... | collective-permute-start | bytes 393224 | tf_op jit(solution)/shard_map/ppermute | solution.py:548
  127.3 8.7 %collective-permute-start.32 = (bf16[512,128]{1,0:T(8,128)(2,1)S(1)}, bf16[512,128]{1,0:T(8,128)(2,1)S(1)}, u32[]{:S(2)}, u32[]{:S(2)}) collective-permute-start(bf16[512,128]{1,0:T(8,128)(2,1)S(1)} %get-tuple-element.85), channel_id=1, source_target_pairs={{0,24},{4,28},{8,16},{12,20},{16,8},{20,12},{24,0},{28,4},{1,25},{... | collective-permute-start | bytes 393224 | tf_op jit(solution)/shard_map/ppermute | solution.py:548
  128.5 9.4 %collective-permute-start.33 = (bf16[512,128]{1,0:T(8,128)(2,1)S(1)}, bf16[512,128]{1,0:T(8,128)(2,1)S(1)}, u32[]{:S(2)}, u32[]{:S(2)}) collective-permute-start(bf16[512,128]{1,0:T(8,128)(2,1)S(1)} %get-tuple-element.86), channel_id=1, source_target_pairs={{0,28},{4,24},{8,20},{12,16},{16,12},{20,8},{24,4},{28,0},{1,29},{... | collective-permute-start | bytes 393224 | tf_op jit(solution)/shard_map/ppermute | solution.py:548

commit v15 on v14

--- a/solution.py
+++ b/solution.py
@@ -192,11 +192,15 @@
                 pl.when(plan + ahead == known)(basis_copy(known).wait)
         correlate(plan + 1, slots[1][0], slots[1][1])
         finish(plan, *slots[0][1:])
-        correlate(jnp.minimum(plan + 2, plans - 1), slots[0][0], slots[0][1])
+        correlate(plan + 2, slots[0][0], slots[0][1])
         finish(plan + 1, *slots[1][1:])
         return carry
 
-    lax.fori_loop(0, plans // 2, pair, 0)
+    lax.fori_loop(0, plans // 2 - 1, pair, 0)
+    basis_copy(plans - 1).wait()
+    correlate(plans - 1, slots[1][0], slots[1][1])
+    finish(plans - 2, *slots[0][1:])
+    finish(plans - 1, *slots[1][1:])
     for owner in range(tm_count):
         outs[owner][...] = back_ref[pl.ds(owner * spaced, capacity), :].astype(jnp.bfloat16)
 

time: 142 us -> 144 us (1.014)
  Pallas kernels: 50.8 us -> 56.2 us
  starting transfers between devices: 46 us -> 42.9 us
    ppermute x28, starting transfers between devices: 31 us -> 27.9 us  [exchange(): lax.ppermute(blocks[step], 'tm', [(i, i ^ step) for i in range(count)])]
    pallas_call x1, Pallas kernels: 5.13 us -> 7.62 us  [place_late_and_pick(): pl.pallas_call(functools.partial(late_pick_kernel, tm_count, len(attitude...]
    pallas_call x1, Pallas kernels: 3.48 us -> 5 us  [place_late(): pl.pallas_call(functools.partial(late_kernel, owners), in_specs=[SMEM] *...]
  transfers between devices with their start and end apart: 35 -> 35, of which waited for: 16 -> 17; matrix products, arithmetic and copies ran while one was open for 7% -> 7% of each run, Pallas kernels for 15% -> 15%
where the time goes in v15:
time: 144 us
  Pallas kernels  56.2 us (39%)
  starting transfers between devices  42.9 us (30%)
  waiting for transfers between devices  31.9 us (22%)
  other arithmetic  9.49 us (7%)
  local copies, waits for them, and re-layouts  2.14 us (1%)
    ppermute x28, starting transfers between devices, exchange(): lax.ppermute(blocks[step], 'tm', [(i, i ^ step) for i in range(count)])  27.9 us
    ppermute x28, waiting for transfers between devices, exchange(): lax.ppermute(blocks[step], 'tm', [(i, i ^ step) for i in range(count)])  19.8 us
    pallas_call x2, Pallas kernels, fit_plans(): pl.pallas_call(functools.partial(fit_kernel, order), in_specs=[SMEM, SMEM...  16.8 us
    pallas_call x4, Pallas kernels, make_basis(): pl.pallas_call(functools.partial(basis_kernel, len(after)), grid=(sched_d...  14.3 us
    ppermute x3, waiting for transfers between devices, pass_along(): lax.ppermute(left, 'sky', [(i, i - 1) for i in range(1, count - hop + 1)])  8.04 us
    pallas_call x2, Pallas kernels, place_early(): pl.pallas_call(functools.partial(early_kernel, owners, table_base), in_sp...  7.96 us
    pallas_call x1, Pallas kernels, place_late_and_pick(): pl.pallas_call(functools.partial(late_pick_kernel, tm_count, len(attitude...  7.62 us
    ppermute x3, starting transfers between devices, pass_along(): lax.ppermute(right, 'sky', [(i, i + 1) for i in range(hop - 1, count - 1)])  6.08 us
  transfers between devices with their start and end apart: 35, of which 17 were waited for; matrix products, arithmetic and copies ran while one was open for 7% of the time, Pallas kernels for 15%

profile of v15, /device:TPU:1, one launch (start us, length us, event | category | flops | bytes accessed | tf_op | source)
XLA Modules:
  0.0 143.8 jit_solution(11854414943355542278)
XLA Ops:
  0.6 1.3 collective-permute-start.1
  1.9 4.7 %collective-permute-start = (bf16[4,128,512]{2,1,0:T(8,128)(2,1)}, bf16[4,128,512]{2,1,0:T(8,128)(2,1)S(1)}, u32[]{:S(2)}, u32[]{:S(2)}) collective-permute-start(bf16[4,128,512]{2,1,0:T(8,128)(2,1)} %own_ref.3), channel_id=1, source_target_pairs={{0,1},{1,2},{2,3},{4,5},{5,6},{6,7},{8,9},{9,10},{10,11},{12,13},{... | collective-permute-start | bytes 1572872 | tf_op jit(solution)/shard_map/ppermute | solution.py:561
  9.0 0.8 convert_reduce_fusion
  10.3 0.8 fusion.18
  11.6 3.4 %select_reduce_fusion = s32[4096]{0:T(1024)S(1)} fusion(s32[2048]{0:T(1024)S(1)} %bitcast.34, s32[2048]{0:T(1024)S(1)} %bitcast.33), kind=kLoop, calls=%fused_computation | loop fusion | flops 25161728 | bytes 32768 | tf_op jit(solution)/shard_map/reduce_sum | solution.py:523
  15.2 1.3 collective-permute-done.1.refs_1_
  16.5 1.3 collective-permute-start.3
  18.6 1.8 %shard_map.77 = (bf16[1,256,2048]{2,1,0:T(8,128)(2,1)S(1)}, f32[1,1,2048]{2,1,0:T(1,128)S(1)}) custom-call(f32[256,128]{1,0:T(8,128)S(1)} %broadcast_in_dim.50.time_ref, f32[1,1024]{1,0:T(1,128)S(1)} %bitcast.27, f32[1,1024]{1,0:T(1,128)S(1)} %bitcast.23, bf16[4,128,512]{2,1,0:T(8,128)(2,1)S(1)} %collective-permute-done.refs_0_, ...), custom_call_target="tpu_custom_call" | custom-call | flops 2097152000 | bytes 1048576 | tf_op jit(solution)/shard_map/pallas_call | solution.py:92
  20.4 1.0 copy-done.3
  22.0 5.1 %all-to-all-start = ((s32[8,1,512]{2,1,0:T(1,128)}), s32[8,1,512]{2,1,0:T(1,128)S(1)}, u32[]{:S(2)}, u32[]{:S(2)}) async-start(s32[8,1,512]{2,1,0:T(1,128)} %all_to_all.6), calls=%async_computation | async-start | bytes 32768 | tf_op jit(solution)/shard_map/all_to_all | solution.py:590
  27.1 4.0 %all-to-all-done = s32[8,1,512]{2,1,0:T(1,128)S(1)} async-done(((s32[8,1,512]{2,1,0:T(1,128)}), s32[8,1,512]{2,1,0:T(1,128)S(1)}, u32[]{:S(2)}, u32[]{:S(2)}) %all-to-all-start) | async-done | bytes 16416 | tf_op jit(solution)/shard_map/all_to_all | solution.py:590
  31.4 1.3 collective-permute-start.5
  33.5 5.3 %shard_map.80 = (bf16[3,256,2048]{2,1,0:T(8,128)(2,1)S(1)}, f32[3,1,2048]{2,1,0:T(1,128)S(1)}) custom-call(f32[768,128]{1,0:T(8,128)S(1)} %broadcast_in_dim.55.time_ref, f32[1,1024]{1,0:T(1,128)S(1)} %bitcast.28, f32[1,1024]{1,0:T(1,128)S(1)} %bitcast.24, bf16[4,128,512]{2,1,0:T(8,128)(2,1)S(1)} %collective-permute-done.2.refs_2_.refs_0_, ...), custom_call_target="tpu_custom_call" | custom-call | flops 6291456000 | bytes 3145728 | tf_op jit(solution)/shard_map/pallas_call | solution.py:92
  39.0 3.6 %shard_map.79 = (bf16[2,256,2048]{2,1,0:T(8,128)(2,1)S(1)}, f32[2,1,2048]{2,1,0:T(1,128)S(1)}) custom-call(f32[512,128]{1,0:T(8,128)S(1)} %broadcast_in_dim.53.time_ref, f32[1,1024]{1,0:T(1,128)S(1)} %bitcast.29, f32[1,1024]{1,0:T(1,128)S(1)} %bitcast.25, bf16[4,128,512]{2,1,0:T(8,128)(2,1)S(1)} %collective-permute-done.2.refs_2_.refs_0_, ...), custom_call_target="tpu_custom_call" | custom-call | flops 4194304000 | bytes 2097152 | tf_op jit(solution)/shard_map/pallas_call | solution.py:92
  42.7 6.8 %collective-permute-done.5.refs_5_ = bf16[4,128,512]{2,1,0:T(8,128)(2,1)S(1)} collective-permute-done((bf16[4,128,512]{2,1,0:T(8,128)(2,1)S(1)}, bf16[4,128,512]{2,1,0:T(8,128)(2,1)S(1)}, u32[]{:S(2)}, u32[]{:S(2)}) %collective-permute-start.5) | collective-permute-done | bytes 524320 | tf_op jit(solution)/shard_map/ppermute | solution.py:562
  49.4 4.5 %shard_map.78 = (bf16[512,128]{1,0:T(8,128)(2,1)S(1)}, bf16[512,128]{1,0:T(8,128)(2,1)S(1)}, bf16[512,128]{1,0:T(8,128)(2,1)S(1)}, bf16[512,128]{1,0:T(8,128)(2,...) custom-call(s32[4096]{0:T(1024)S(1)} %bitcast.18, ...), custom_call_target="tpu_custom_call" | custom-call | flops 5000000000 | bytes 1048576 | tf_op jit(solution)/shard_map/pallas_call | solution.py:384
  54.0 0.7 collective-permute-start.7
  54.8 2.9 %collective-permute-start.8 = (bf16[512,128]{1,0:T(8,128)(2,1)S(1)}, bf16[512,128]{1,0:T(8,128)(2,1)S(1)}, u32[]{:S(2)}, u32[]{:S(2)}) collective-permute-start(bf16[512,128]{1,0:T(8,128)(2,1)S(1)} %get-tuple-element.50), channel_id=1, source_target_pairs={{0,20},{4,16},{8,28},{12,24},{16,4},{20,0},{24,12},{28,8},{1,21},{... | collective-permute-start | bytes 393224 | tf_op jit(solution)/shard_map/ppermute | solution.py:552
  57.8 1.2 collective-permute-start.10
  59.2 3.6 %shard_map.81 = (bf16[2,256,2048]{2,1,0:T(8,128)(2,1)S(1)}, f32[2,1,2048]{2,1,0:T(1,128)S(1)}) custom-call(f32[512,128]{1,0:T(8,128)S(1)} %broadcast_in_dim.57.time_ref, f32[1,1024]{1,0:T(1,128)S(1)} %bitcast.30, f32[1,1024]{1,0:T(1,128)S(1)} %bitcast.26, bf16[512,128]{1,0:T(8,128)(2,1)S(1)} %get-tuple-element.47.refs_0_), custom_call_target="tpu_custom_call" | custom-call | flops 4194304000 | bytes 2097152 | tf_op jit(solution)/shard_map/pallas_call | solution.py:92
  62.7 1.6 %collective-permute-start.11 = (bf16[512,128]{1,0:T(8,128)(2,1)S(1)}, bf16[512,128]{1,0:T(8,128)(2,1)S(1)}, u32[]{:S(2)}, u32[]{:S(2)}) collective-permute-start(bf16[512,128]{1,0:T(8,128)(2,1)S(1)} %get-tuple-element.53), channel_id=1, source_target_pairs={{0,28},{4,24},{8,20},{12,16},{16,12},{20,8},{24,4},{28,0},{1,29},{... | collective-permute-start | bytes 393224 | tf_op jit(solution)/shard_map/ppermute | solution.py:552
  64.8 1.1 collective-permute-done.10.refs_5_
  65.9 3.3 %collective-permute-done.11.refs_6_ = bf16[512,128]{1,0:T(8,128)(2,1)S(1)} collective-permute-done((bf16[512,128]{1,0:T(8,128)(2,1)S(1)}, bf16[512,128]{1,0:T(8,128)(2,1)S(1)}, u32[]{:S(2)}, u32[]{:S(2)}) %collective-permute-start.11) | collective-permute-done | bytes 131104 | tf_op jit(solution)/shard_map/ppermute | solution.py:552
  69.2 8.8 %shard_map.82 = (bf16[512,128]{1,0:T(8,128)(2,1)S(1)}, bf16[512,128]{1,0:T(8,128)(2,1)S(1)}, bf16[512,128]{1,0:T(8,128)(2,1)S(1)}, bf16[512,128]{1,0:T(8,128)(2,...) custom-call(s32[8,24]{1,0:T(8,128)S(1)} %get-tuple-element.104.src_r, ...), custom_call_target="tpu_custom_call" | custom-call | flops 10737418240 | bytes 8388608 | tf_op jit(solution)/shard_map/pallas_call | solution.py:222
  78.4 1.2 collective-permute-start.14
  80.1 1.3 collective-permute-start.16
  81.6 1.5 %collective-permute-start.18 = (bf16[512,128]{1,0:T(8,128)(2,1)S(1)}, bf16[512,128]{1,0:T(8,128)(2,1)S(1)}, u32[]{:S(2)}, u32[]{:S(2)}) collective-permute-start(bf16[512,128]{1,0:T(8,128)(2,1)S(1)} %get-tuple-element.68), channel_id=1, source_target_pairs={{0,24},{4,28},{8,16},{12,20},{16,8},{20,12},{24,0},{28,4},{1,25},{... | collective-permute-start | bytes 393224 | tf_op jit(solution)/shard_map/ppermute | solution.py:552
  83.3 2.8 %collective-permute-start.19 = (bf16[512,128]{1,0:T(8,128)(2,1)S(1)}, bf16[512,128]{1,0:T(8,128)(2,1)S(1)}, u32[]{:S(2)}, u32[]{:S(2)}) collective-permute-start(bf16[512,128]{1,0:T(8,128)(2,1)S(1)} %get-tuple-element.69), channel_id=1, source_target_pairs={{0,28},{4,24},{8,20},{12,16},{16,12},{20,8},{24,4},{28,0},{1,29},{... | collective-permute-start | bytes 393224 | tf_op jit(solution)/shard_map/ppermute | solution.py:552
  86.7 2.0 %collective-permute-done.17.refs_5_ = bf16[512,128]{1,0:T(8,128)(2,1)S(1)} collective-permute-done((bf16[512,128]{1,0:T(8,128)(2,1)S(1)}, bf16[512,128]{1,0:T(8,128)(2,1)S(1)}, u32[]{:S(2)}, u32[]{:S(2)}) %collective-permute-start.17) | collective-permute-done | bytes 131104 | tf_op jit(solution)/shard_map/ppermute | solution.py:552
  88.7 4.0 %shard_map.83.part_ref = f32[4096,128]{1,0:T(8,128)S(1)} custom-call(s32[4096]{0:T(1024)S(1)} %bitcast.19, s32[8]{0:T(128)S(1)} %fusion.4.cnt_ref, s32[2]{0:T(128)S(1)} %pad_add_fusion.where_ref, bf16[4,512,256]{2,1,0:T(8,128)(2,1)S(1)} %copy-done, bf16[512,128]{1,0:T(8,128)(2,1)S(1)} %get-tuple-element.62.refs_0_, ...), custom_call_target="tpu_custom_call" | custom-call | flops 6000000000 | bytes 1048576 | tf_op jit(solution)/shard_map/pallas_call | solution.py:356
  93.2 7.6 %shard_map.84 = (f32[131072,128]{1,0:T(8,128)}, bf16[512,128]{1,0:T(8,128)(2,1)S(1)}, bf16[512,128]{1,0:T(8,128)(2,1)S(1)}, bf16[512,128]{1,0:T(8,128)(2,1)S(1)}...) custom-call(s32[4096]{0:T(1024)S(1)} %bitcast.20, ...), custom_call_target="tpu_custom_call" | custom-call | flops 7000000000 | bytes 1048576 | tf_op jit(solution)/shard_map/pallas_call | solution.py:441
  102.2 2.0 %collective-permute-start.23 = (bf16[512,128]{1,0:T(8,128)(2,1)S(1)}, bf16[512,128]{1,0:T(8,128)(2,1)S(1)}, u32[]{:S(2)}, u32[]{:S(2)}) collective-permute-start(bf16[512,128]{1,0:T(8,128)(2,1)S(1)} %get-tuple-element.75), channel_id=1, source_target_pairs={{0,12},{4,8},{8,4},{12,0},{16,28},{20,24},{24,20},{28,16},{1,13},{... | collective-permute-start | bytes 393224 | tf_op jit(solution)/shard_map/ppermute | solution.py:552
  104.5 1.3 collective-permute-done.20.refs_1_
  105.8 1.9 %collective-permute-start.26 = (bf16[512,128]{1,0:T(8,128)(2,1)S(1)}, bf16[512,128]{1,0:T(8,128)(2,1)S(1)}, u32[]{:S(2)}, u32[]{:S(2)}) collective-permute-start(bf16[512,128]{1,0:T(8,128)(2,1)S(1)} %get-tuple-element.78), channel_id=1, source_target_pairs={{0,4},{4,0},{8,12},{12,8},{16,20},{20,16},{24,28},{28,24},{1,5},{5... | collective-permute-start | bytes 393224 | tf_op jit(solution)/shard_map/ppermute | solution.py:552
  107.7 2.4 %collective-permute-done.23.refs_4_ = bf16[512,128]{1,0:T(8,128)(2,1)S(1)} collective-permute-done((bf16[512,128]{1,0:T(8,128)(2,1)S(1)}, bf16[512,128]{1,0:T(8,128)(2,1)S(1)}, u32[]{:S(2)}, u32[]{:S(2)}) %collective-permute-start.23) | collective-permute-done | bytes 131104 | tf_op jit(solution)/shard_map/ppermute | solution.py:552
  110.1 2.8 %collective-permute-done.24.refs_5_ = bf16[512,128]{1,0:T(8,128)(2,1)S(1)} collective-permute-done((bf16[512,128]{1,0:T(8,128)(2,1)S(1)}, bf16[512,128]{1,0:T(8,128)(2,1)S(1)}, u32[]{:S(2)}, u32[]{:S(2)}) %collective-permute-start.24) | collective-permute-done | bytes 131104 | tf_op jit(solution)/shard_map/ppermute | solution.py:552
  112.9 1.7 %collective-permute-done.25.refs_6_ = bf16[512,128]{1,0:T(8,128)(2,1)S(1)} collective-permute-done((bf16[512,128]{1,0:T(8,128)(2,1)S(1)}, bf16[512,128]{1,0:T(8,128)(2,1)S(1)}, u32[]{:S(2)}, u32[]{:S(2)}) %collective-permute-start.25) | collective-permute-done | bytes 131104 | tf_op jit(solution)/shard_map/ppermute | solution.py:552
  114.6 8.1 %shard_map.85 = (bf16[512,128]{1,0:T(8,128)(2,1)S(1)}, bf16[512,128]{1,0:T(8,128)(2,1)S(1)}, bf16[512,128]{1,0:T(8,128)(2,1)S(1)}, bf16[512,128]{1,0:T(8,128)(2,...) custom-call(s32[8,24]{1,0:T(8,128)S(1)} %get-tuple-element.104.src_r, ...), custom_call_target="tpu_custom_call" | custom-call | flops 10737418240 | bytes 8388608 | tf_op jit(solution)/shard_map/pallas_call | solution.py:222
  122.6 1.2 collective-permute-start.27
  124.0 1.2 collective-permute-start.29
  125.2 1.3 collective-permute-start.30
  127.0 0.8 reduce.1
  127.8 1.1 collective-permute-start.32
  129.0 2.2 %collective-permute-start.33 = (bf16[512,128]{1,0:T(8,128)(2,1)S(1)}, bf16[512,128]{1,0:T(8,128)(2,1)S(1)}, u32[]{:S(2)}, u32[]{:S(2)}) collective-permute-start(bf16[512,128]{1,0:T(8,128)(2,1)S(1)} %get-tuple-element.86), channel_id=1, source_target_pairs={{0,28},{4,24},{8,20},{12,16},{16,12},{20,8},{24,4},{28,0},{1,29},{... | collective-permute-start | bytes 393224 | tf_op jit(solution)/shard_map/ppermute | solution.py:552
  131.8 0.8 collective-permute-done.31.refs_5_
  132.6 3.9 %shard_map.86.part_ref = f32[4096,128]{1,0:T(8,128)S(1)} custom-call(s32[4096]{0:T(1024)S(1)} %bitcast.21, s32[8]{0:T(128)S(1)} %fusion.4.cnt_ref, s32[2]{0:T(128)S(1)} %pad_add_fusion.where_ref, f32[131072,128]{1,0:T(8,128)} %get-tuple-element.70.base_ref, bf16[512,128]{1,0:T(8,128)(2,1)S(1)} %get-tuple-element.79.refs_0_, ...), custom_call_target="tpu_custom_call" | custom-call | flops 6000000000 | bytes 1048576 | tf_op jit(solution)/shard_map/pallas_call | solution.py:356
  136.6 2.1 %collective-permute-done.33.refs_1_ = bf16[512,128]{1,0:T(8,128)(2,1)S(1)} collective-permute-done((bf16[512,128]{1,0:T(8,128)(2,1)S(1)}, bf16[512,128]{1,0:T(8,128)(2,1)S(1)}, u32[]{:S(2)}, u32[]{:S(2)}) %collective-permute-start.33) | collective-permute-done | bytes 131104 | tf_op jit(solution)/shard_map/ppermute | solution.py:552
  138.6 5.0 %shard_map.87 = f32[4,512,256]{2,1,0:T(8,128)} custom-call(s32[4096]{0:T(1024)S(1)} %bitcast.22, s32[8]{0:T(128)S(1)} %fusion.4.cnt_ref, s32[2]{0:T(128)S(1)} %pad_add_fusion.where_ref, f32[4096,128]{1,0:T(8,128)S(1)} %shard_map.86.part_ref, bf16[512,128]{1,0:T(8,128)(2,1)S(1)} %collective-permute-done.32.refs_0_, ...), custom_call_target="tpu_custom_call" | custom-call | flops 4000000000 | bytes 1048576 | tf_op jit(solution)/shard_map/pallas_call | solution.py:483
  (83 shorter events, 12.4 us)
Async XLA Ops:
  0.6 15.9 %collective-permute-start.1 = (bf16[4,128,512]{2,1,0:T(8,128)(2,1)}, bf16[4,128,512]{2,1,0:T(8,128)(2,1)S(1)}, u32[]{:S(2)}, u32[]{:S(2)}) collective-permute-start(bf16[4,128,512]{2,1,0:T(8,128)(2,1)} %own_ref.3), channel_id=1, source_target_pairs={{1,0},{2,1},{3,2},{5,4},{6,5},{7,6},{9,8},{10,9},{11,10},{13,12},{... | collective-permute-start | bytes 1572872 | tf_op jit(solution)/shard_map/ppermute | solution.py:562
  1.9 15.9 %collective-permute-start = (bf16[4,128,512]{2,1,0:T(8,128)(2,1)}, bf16[4,128,512]{2,1,0:T(8,128)(2,1)S(1)}, u32[]{:S(2)}, u32[]{:S(2)}) collective-permute-start(bf16[4,128,512]{2,1,0:T(8,128)(2,1)} %own_ref.3), channel_id=1, source_target_pairs={{0,1},{1,2},{2,3},{4,5},{5,6},{6,7},{8,9},{9,10},{10,11},{12,13},{... | collective-permute-start | bytes 1572872 | tf_op jit(solution)/shard_map/ppermute | solution.py:561
  16.5 14.8 %collective-permute-start.3 = (bf16[4,128,512]{2,1,0:T(8,128)(2,1)S(1)}, bf16[4,128,512]{2,1,0:T(8,128)(2,1)S(1)}, u32[]{:S(2)}, u32[]{:S(2)}) collective-permute-start(bf16[4,128,512]{2,1,0:T(8,128)(2,1)S(1)} %collective-permute-done.1.refs_1_), channel_id=1, source_target_pairs={{1,0},{2,1},{5,4},{6,5},{9,8},{10,9},{13,12},{14,13},{17,16},{18,1... | collective-permute-start | bytes 1572872 | tf_op jit(solution)/shard_map/ppermute | solution.py:562
  17.8 14.8 %collective-permute-start.2 = (bf16[4,128,512]{2,1,0:T(8,128)(2,1)S(1)}, bf16[4,128,512]{2,1,0:T(8,128)(2,1)S(1)}, u32[]{:S(2)}, u32[]{:S(2)}) collective-permute-start(bf16[4,128,512]{2,1,0:T(8,128)(2,1)S(1)} %collective-permute-done.refs_0_), channel_id=1, source_target_pairs={{1,2},{2,3},{5,6},{6,7},{9,10},{10,11},{13,14},{14,15},{17,18},{18... | collective-permute-start | bytes 1572872 | tf_op jit(solution)/shard_map/ppermute | solution.py:561
  20.4 1.0 copy-start.3
  22.0 9.1 %all-to-all-start = ((s32[8,1,512]{2,1,0:T(1,128)}), s32[8,1,512]{2,1,0:T(1,128)S(1)}, u32[]{:S(2)}, u32[]{:S(2)}) async-start(s32[8,1,512]{2,1,0:T(1,128)} %all_to_all.6), calls=%async_computation | async-start | bytes 32768 | tf_op jit(solution)/shard_map/all_to_all | solution.py:590
  31.4 18.1 %collective-permute-start.5 = (bf16[4,128,512]{2,1,0:T(8,128)(2,1)S(1)}, bf16[4,128,512]{2,1,0:T(8,128)(2,1)S(1)}, u32[]{:S(2)}, u32[]{:S(2)}) collective-permute-start(bf16[4,128,512]{2,1,0:T(8,128)(2,1)S(1)} %collective-permute-done.3.refs_3_.refs_1_), channel_id=1, source_target_pairs={{1,0},{5,4},{9,8},{13,12},{17,16},{21,20},{25,24},{29,28}} | collective-permute-start | bytes 1572872 | tf_op jit(solution)/shard_map/ppermute | solution.py:562
  32.7 16.8 %collective-permute-start.4 = (bf16[4,128,512]{2,1,0:T(8,128)(2,1)S(1)}, bf16[4,128,512]{2,1,0:T(8,128)(2,1)S(1)}, u32[]{:S(2)}, u32[]{:S(2)}) collective-permute-start(bf16[4,128,512]{2,1,0:T(8,128)(2,1)S(1)} %collective-permute-done.2.refs_2_.refs_0_), channel_id=1, source_target_pairs={{2,3},{6,7},{10,11},{14,15},{18,19},{22,23},{26,27},{30,31}} | collective-permute-start | bytes 1572872 | tf_op jit(solution)/shard_map/ppermute | solution.py:561
  39.0 10.4 %copy-start = (bf16[4,512,256]{2,1,0:T(8,128)(2,1)S(1)}, bf16[4,512,256]{2,1,0:T(8,128)(2,1)}, u32[]{:S(2)}) copy-start(bf16[4,512,256]{2,1,0:T(8,128)(2,1)} %base_ref.3) | copy-start | bytes 3145732
  39.0 10.4 %copy-start.1 = (bf16[4,128,512]{2,1,0:T(8,128)(2,1)S(1)}, bf16[4,128,512]{2,1,0:T(8,128)(2,1)}, u32[]{:S(2)}) copy-start(bf16[4,128,512]{2,1,0:T(8,128)(2,1)} %own_ref.3) | copy-start | bytes 1572868
  39.0 10.4 %copy-start.2 = (s32[4]{0:T(128)S(1)}, s32[4]{0:T(128)}, u32[]{:S(2)}) copy-start(s32[4]{0:T(128)} %count_ref.3) | copy-start | bytes 52
  54.0 8.8 %collective-permute-start.6 = (bf16[512,128]{1,0:T(8,128)(2,1)S(1)}, bf16[512,128]{1,0:T(8,128)(2,1)S(1)}, u32[]{:S(2)}, u32[]{:S(2)}) collective-permute-start(bf16[512,128]{1,0:T(8,128)(2,1)S(1)} %get-tuple-element.48), channel_id=1, source_target_pairs={{0,16},{4,20},{8,24},{12,28},{16,0},{20,4},{24,8},{28,12},{1,17},{... | collective-permute-start | bytes 393224 | tf_op jit(solution)/shard_map/ppermute | solution.py:552
  54.0 10.3 %collective-permute-start.7 = (bf16[512,128]{1,0:T(8,128)(2,1)S(1)}, bf16[512,128]{1,0:T(8,128)(2,1)S(1)}, u32[]{:S(2)}, u32[]{:S(2)}) collective-permute-start(bf16[512,128]{1,0:T(8,128)(2,1)S(1)} %get-tuple-element.49), channel_id=1, source_target_pairs={{0,8},{4,12},{8,0},{12,4},{16,24},{20,28},{24,16},{28,20},{1,9},{5... | collective-permute-start | bytes 393224 | tf_op jit(solution)/shard_map/ppermute | solution.py:552
  54.8 9.6 %collective-permute-start.8 = (bf16[512,128]{1,0:T(8,128)(2,1)S(1)}, bf16[512,128]{1,0:T(8,128)(2,1)S(1)}, u32[]{:S(2)}, u32[]{:S(2)}) collective-permute-start(bf16[512,128]{1,0:T(8,128)(2,1)S(1)} %get-tuple-element.50), channel_id=1, source_target_pairs={{0,20},{4,16},{8,28},{12,24},{16,4},{20,0},{24,12},{28,8},{1,21},{... | collective-permute-start | bytes 393224 | tf_op jit(solution)/shard_map/ppermute | solution.py:552
  57.7 7.1 %collective-permute-start.9 = (bf16[512,128]{1,0:T(8,128)(2,1)S(1)}, bf16[512,128]{1,0:T(8,128)(2,1)S(1)}, u32[]{:S(2)}, u32[]{:S(2)}) collective-permute-start(bf16[512,128]{1,0:T(8,128)(2,1)S(1)} %get-tuple-element.51), channel_id=1, source_target_pairs={{0,12},{4,8},{8,4},{12,0},{16,28},{20,24},{24,20},{28,16},{1,13},{... | collective-permute-start | bytes 393224 | tf_op jit(solution)/shard_map/ppermute | solution.py:552
  57.8 8.1 %collective-permute-start.10 = (bf16[512,128]{1,0:T(8,128)(2,1)S(1)}, bf16[512,128]{1,0:T(8,128)(2,1)S(1)}, u32[]{:S(2)}, u32[]{:S(2)}) collective-permute-start(bf16[512,128]{1,0:T(8,128)(2,1)S(1)} %get-tuple-element.52), channel_id=1, source_target_pairs={{0,24},{4,28},{8,16},{12,20},{16,8},{20,12},{24,0},{28,4},{1,25},{... | collective-permute-start | bytes 393224 | tf_op jit(solution)/shard_map/ppermute | solution.py:552
  59.1 10.0 %copy-start.4 = (bf16[1,256,2048]{2,1,0:T(8,128)(2,1)S(1)}, bf16[1,256,2048]{2,1,0:T(8,128)(2,1)}, u32[]{:S(2)}) copy-start(bf16[1,256,2048]{2,1,0:T(8,128)(2,1)} %copy-done.3) | copy-start | bytes 3145732
  62.7 6.4 %collective-permute-start.11 = (bf16[512,128]{1,0:T(8,128)(2,1)S(1)}, bf16[512,128]{1,0:T(8,128)(2,1)S(1)}, u32[]{:S(2)}, u32[]{:S(2)}) collective-permute-start(bf16[512,128]{1,0:T(8,128)(2,1)S(1)} %get-tuple-element.53), channel_id=1, source_target_pairs={{0,28},{4,24},{8,20},{12,16},{16,12},{20,8},{24,4},{28,0},{1,29},{... | collective-permute-start | bytes 393224 | tf_op jit(solution)/shard_map/ppermute | solution.py:552
  64.3 4.8 %collective-permute-start.12 = (bf16[512,128]{1,0:T(8,128)(2,1)S(1)}, bf16[512,128]{1,0:T(8,128)(2,1)S(1)}, u32[]{:S(2)}, u32[]{:S(2)}) collective-permute-start(bf16[512,128]{1,0:T(8,128)(2,1)S(1)} %get-tuple-element.54), channel_id=1, source_target_pairs={{0,4},{4,0},{8,12},{12,8},{16,20},{20,16},{24,28},{28,24},{1,5},{5... | collective-permute-start | bytes 393224 | tf_op jit(solution)/shard_map/ppermute | solution.py:552
  77.9 3.6 %collective-permute-start.13 = (bf16[512,128]{1,0:T(8,128)(2,1)S(1)}, bf16[512,128]{1,0:T(8,128)(2,1)S(1)}, u32[]{:S(2)}, u32[]{:S(2)}) collective-permute-start(bf16[512,128]{1,0:T(8,128)(2,1)S(1)} %get-tuple-element.63), channel_id=1, source_target_pairs={{0,4},{4,0},{8,12},{12,8},{16,20},{20,16},{24,28},{28,24},{1,5},{5... | collective-permute-start | bytes 393224 | tf_op jit(solution)/shard_map/ppermute | solution.py:552
  78.4 4.9 %collective-permute-start.14 = (bf16[512,128]{1,0:T(8,128)(2,1)S(1)}, bf16[512,128]{1,0:T(8,128)(2,1)S(1)}, u32[]{:S(2)}, u32[]{:S(2)}) collective-permute-start(bf16[512,128]{1,0:T(8,128)(2,1)S(1)} %get-tuple-element.64), channel_id=1, source_target_pairs={{0,16},{4,20},{8,24},{12,28},{16,0},{20,4},{24,8},{28,12},{1,17},{... | collective-permute-start | bytes 393224 | tf_op jit(solution)/shard_map/ppermute | solution.py:552
  79.6 6.5 %collective-permute-start.15 = (bf16[512,128]{1,0:T(8,128)(2,1)S(1)}, bf16[512,128]{1,0:T(8,128)(2,1)S(1)}, u32[]{:S(2)}, u32[]{:S(2)}) collective-permute-start(bf16[512,128]{1,0:T(8,128)(2,1)S(1)} %get-tuple-element.65), channel_id=1, source_target_pairs={{0,8},{4,12},{8,0},{12,4},{16,24},{20,28},{24,16},{28,20},{1,9},{5... | collective-permute-start | bytes 393224 | tf_op jit(solution)/shard_map/ppermute | solution.py:552
  80.1 6.6 %collective-permute-start.16 = (bf16[512,128]{1,0:T(8,128)(2,1)S(1)}, bf16[512,128]{1,0:T(8,128)(2,1)S(1)}, u32[]{:S(2)}, u32[]{:S(2)}) collective-permute-start(bf16[512,128]{1,0:T(8,128)(2,1)S(1)} %get-tuple-element.66), channel_id=1, source_target_pairs={{0,20},{4,16},{8,28},{12,24},{16,4},{20,0},{24,12},{28,8},{1,21},{... | collective-permute-start | bytes 393224 | tf_op jit(solution)/shard_map/ppermute | solution.py:552
  81.5 7.2 %collective-permute-start.17 = (bf16[512,128]{1,0:T(8,128)(2,1)S(1)}, bf16[512,128]{1,0:T(8,128)(2,1)S(1)}, u32[]{:S(2)}, u32[]{:S(2)}) collective-permute-start(bf16[512,128]{1,0:T(8,128)(2,1)S(1)} %get-tuple-element.67), channel_id=1, source_target_pairs={{0,12},{4,8},{8,4},{12,0},{16,28},{20,24},{24,20},{28,16},{1,13},{... | collective-permute-start | bytes 393224 | tf_op jit(solution)/shard_map/ppermute | solution.py:552
  81.6 11.1 %collective-permute-start.18 = (bf16[512,128]{1,0:T(8,128)(2,1)S(1)}, bf16[512,128]{1,0:T(8,128)(2,1)S(1)}, u32[]{:S(2)}, u32[]{:S(2)}) collective-permute-start(bf16[512,128]{1,0:T(8,128)(2,1)S(1)} %get-tuple-element.68), channel_id=1, source_target_pairs={{0,24},{4,28},{8,16},{12,20},{16,8},{20,12},{24,0},{28,4},{1,25},{... | collective-permute-start | bytes 393224 | tf_op jit(solution)/shard_map/ppermute | solution.py:552
  83.3 9.9 %collective-permute-start.19 = (bf16[512,128]{1,0:T(8,128)(2,1)S(1)}, bf16[512,128]{1,0:T(8,128)(2,1)S(1)}, u32[]{:S(2)}, u32[]{:S(2)}) collective-permute-start(bf16[512,128]{1,0:T(8,128)(2,1)S(1)} %get-tuple-element.69), channel_id=1, source_target_pairs={{0,28},{4,24},{8,20},{12,16},{16,12},{20,8},{24,4},{28,0},{1,29},{... | collective-permute-start | bytes 393224 | tf_op jit(solution)/shard_map/ppermute | solution.py:552
  100.8 4.9 %collective-permute-start.20 = (bf16[512,128]{1,0:T(8,128)(2,1)S(1)}, bf16[512,128]{1,0:T(8,128)(2,1)S(1)}, u32[]{:S(2)}, u32[]{:S(2)}) collective-permute-start(bf16[512,128]{1,0:T(8,128)(2,1)S(1)} %get-tuple-element.72), channel_id=1, source_target_pairs={{0,16},{4,20},{8,24},{12,28},{16,0},{20,4},{24,8},{28,12},{1,17},{... | collective-permute-start | bytes 393224 | tf_op jit(solution)/shard_map/ppermute | solution.py:552
  100.9 4.9 %collective-permute-start.21 = (bf16[512,128]{1,0:T(8,128)(2,1)S(1)}, bf16[512,128]{1,0:T(8,128)(2,1)S(1)}, u32[]{:S(2)}, u32[]{:S(2)}) collective-permute-start(bf16[512,128]{1,0:T(8,128)(2,1)S(1)} %get-tuple-element.73), channel_id=1, source_target_pairs={{0,8},{4,12},{8,0},{12,4},{16,24},{20,28},{24,16},{28,20},{1,9},{5... | collective-permute-start | bytes 393224 | tf_op jit(solution)/shard_map/ppermute | solution.py:552
  101.5 6.2 %collective-permute-start.22 = (bf16[512,128]{1,0:T(8,128)(2,1)S(1)}, bf16[512,128]{1,0:T(8,128)(2,1)S(1)}, u32[]{:S(2)}, u32[]{:S(2)}) collective-permute-start(bf16[512,128]{1,0:T(8,128)(2,1)S(1)} %get-tuple-element.74), channel_id=1, source_target_pairs={{0,20},{4,16},{8,28},{12,24},{16,4},{20,0},{24,12},{28,8},{1,21},{... | collective-permute-start | bytes 393224 | tf_op jit(solution)/shard_map/ppermute | solution.py:552
  102.2 8.0 %collective-permute-start.23 = (bf16[512,128]{1,0:T(8,128)(2,1)S(1)}, bf16[512,128]{1,0:T(8,128)(2,1)S(1)}, u32[]{:S(2)}, u32[]{:S(2)}) collective-permute-start(bf16[512,128]{1,0:T(8,128)(2,1)S(1)} %get-tuple-element.75), channel_id=1, source_target_pairs={{0,12},{4,8},{8,4},{12,0},{16,28},{20,24},{24,20},{28,16},{1,13},{... | collective-permute-start | bytes 393224 | tf_op jit(solution)/shard_map/ppermute | solution.py:552
  104.1 8.8 %collective-permute-start.24 = (bf16[512,128]{1,0:T(8,128)(2,1)S(1)}, bf16[512,128]{1,0:T(8,128)(2,1)S(1)}, u32[]{:S(2)}, u32[]{:S(2)}) collective-permute-start(bf16[512,128]{1,0:T(8,128)(2,1)S(1)} %get-tuple-element.76), channel_id=1, source_target_pairs={{0,24},{4,28},{8,16},{12,20},{16,8},{20,12},{24,0},{28,4},{1,25},{... | collective-permute-start | bytes 393224 | tf_op jit(solution)/shard_map/ppermute | solution.py:552
  105.8 8.8 %collective-permute-start.25 = (bf16[512,128]{1,0:T(8,128)(2,1)S(1)}, bf16[512,128]{1,0:T(8,128)(2,1)S(1)}, u32[]{:S(2)}, u32[]{:S(2)}) collective-permute-start(bf16[512,128]{1,0:T(8,128)(2,1)S(1)} %get-tuple-element.77), channel_id=1, source_target_pairs={{0,28},{4,24},{8,20},{12,16},{16,12},{20,8},{24,4},{28,0},{1,29},{... | collective-permute-start | bytes 393224 | tf_op jit(solution)/shard_map/ppermute | solution.py:552
  105.8 8.8 %collective-permute-start.26 = (bf16[512,128]{1,0:T(8,128)(2,1)S(1)}, bf16[512,128]{1,0:T(8,128)(2,1)S(1)}, u32[]{:S(2)}, u32[]{:S(2)}) collective-permute-start(bf16[512,128]{1,0:T(8,128)(2,1)S(1)} %get-tuple-element.78), channel_id=1, source_target_pairs={{0,4},{4,0},{8,12},{12,8},{16,20},{20,16},{24,28},{28,24},{1,5},{5... | collective-permute-start | bytes 393224 | tf_op jit(solution)/shard_map/ppermute | solution.py:552
  122.6 5.2 %collective-permute-start.27 = (bf16[512,128]{1,0:T(8,128)(2,1)S(1)}, bf16[512,128]{1,0:T(8,128)(2,1)S(1)}, u32[]{:S(2)}, u32[]{:S(2)}) collective-permute-start(bf16[512,128]{1,0:T(8,128)(2,1)S(1)} %get-tuple-element.80), channel_id=1, source_target_pairs={{0,4},{4,0},{8,12},{12,8},{16,20},{20,16},{24,28},{28,24},{1,5},{5... | collective-permute-start | bytes 393224 | tf_op jit(solution)/shard_map/ppermute | solution.py:552
  123.8 5.2 %collective-permute-start.28 = (bf16[512,128]{1,0:T(8,128)(2,1)S(1)}, bf16[512,128]{1,0:T(8,128)(2,1)S(1)}, u32[]{:S(2)}, u32[]{:S(2)}) collective-permute-start(bf16[512,128]{1,0:T(8,128)(2,1)S(1)} %get-tuple-element.81), channel_id=1, source_target_pairs={{0,16},{4,20},{8,24},{12,28},{16,0},{20,4},{24,8},{28,12},{1,17},{... | collective-permute-start | bytes 393224 | tf_op jit(solution)/shard_map/ppermute | solution.py:552
  124.0 7.2 %collective-permute-start.29 = (bf16[512,128]{1,0:T(8,128)(2,1)S(1)}, bf16[512,128]{1,0:T(8,128)(2,1)S(1)}, u32[]{:S(2)}, u32[]{:S(2)}) collective-permute-start(bf16[512,128]{1,0:T(8,128)(2,1)S(1)} %get-tuple-element.82), channel_id=1, source_target_pairs={{0,8},{4,12},{8,0},{12,4},{16,24},{20,28},{24,16},{28,20},{1,9},{5... | collective-permute-start | bytes 393224 | tf_op jit(solution)/shard_map/ppermute | solution.py:552
  125.2 6.6 %collective-permute-start.30 = (bf16[512,128]{1,0:T(8,128)(2,1)S(1)}, bf16[512,128]{1,0:T(8,128)(2,1)S(1)}, u32[]{:S(2)}, u32[]{:S(2)}) collective-permute-start(bf16[512,128]{1,0:T(8,128)(2,1)S(1)} %get-tuple-element.83), channel_id=1, source_target_pairs={{0,20},{4,16},{8,28},{12,24},{16,4},{20,0},{24,12},{28,8},{1,21},{... | collective-permute-start | bytes 393224 | tf_op jit(solution)/shard_map/ppermute | solution.py:552
  126.5 6.1 %collective-permute-start.31 = (bf16[512,128]{1,0:T(8,128)(2,1)S(1)}, bf16[512,128]{1,0:T(8,128)(2,1)S(1)}, u32[]{:S(2)}, u32[]{:S(2)}) collective-permute-start(bf16[512,128]{1,0:T(8,128)(2,1)S(1)} %get-tuple-element.84), channel_id=1, source_target_pairs={{0,12},{4,8},{8,4},{12,0},{16,28},{20,24},{24,20},{28,16},{1,13},{... | collective-permute-start | bytes 393224 | tf_op jit(solution)/shard_map/ppermute | solution.py:552
  127.8 8.7 %collective-permute-start.32 = (bf16[512,128]{1,0:T(8,128)(2,1)S(1)}, bf16[512,128]{1,0:T(8,128)(2,1)S(1)}, u32[]{:S(2)}, u32[]{:S(2)}) collective-permute-start(bf16[512,128]{1,0:T(8,128)(2,1)S(1)} %get-tuple-element.85), channel_id=1, source_target_pairs={{0,24},{4,28},{8,16},{12,20},{16,8},{20,12},{24,0},{28,4},{1,25},{... | collective-permute-start | bytes 393224 | tf_op jit(solution)/shard_map/ppermute | solution.py:552
  129.0 9.7 %collective-permute-start.33 = (bf16[512,128]{1,0:T(8,128)(2,1)S(1)}, bf16[512,128]{1,0:T(8,128)(2,1)S(1)}, u32[]{:S(2)}, u32[]{:S(2)}) collective-permute-start(bf16[512,128]{1,0:T(8,128)(2,1)S(1)} %get-tuple-element.86), channel_id=1, source_target_pairs={{0,28},{4,24},{8,20},{12,16},{16,12},{20,8},{24,4},{28,0},{1,29},{... | collective-permute-start | bytes 393224 | tf_op jit(solution)/shard_map/ppermute | solution.py:552
